TPU v7x, 32 devices: a whole 2x2x4 slice. The times are simulated.
32 devices in a mesh: slab: 16 (over z, y, core), chan: 2 (over x).
Axes of the slice: x: 2, y: 2, z: 4, core: 2. Of those that a mesh axis runs over, the one named last changes fastest.
Arguments:
- field: bfloat16 [32, 64, 48, 128], P('chan', 'slab'), may hold values from -6 to 6
- out_grad: bfloat16 [32, 64, 48, 128], P(None, 'slab'), may hold values from -6 to 6
- first_weight: bfloat16 [32, 27, 32], P('chan'), may hold values from -0.21875 to 0.21875
- second_weight: bfloat16 [32, 27, 32], P('chan'), may hold values from -0.21875 to 0.21875
Outputs:
- input_grad: bfloat16 [32, 64, 48, 128], P('chan', 'slab')
- first_grad: float32 [32, 27, 32], P('chan')
- second_grad: float32 [32, 27, 32], P('chan')
All inputs are finite; a program needn't handle non-finite values.
Results may differ from a plain program's by a relative error of at most 0.014.
Values may be sent and summed in bfloat16 or wider, within the bound.
No kernel may reach another device: no remote copies, remote signals or barrier semaphores. Data moves between devices by JAX's collectives and lax.ppermute only.
A program may use at most 320 MiB of HBM per device.

v0:
```python
import math

import jax
import jax.numpy as jnp
from jax import lax
from jax.sharding import PartitionSpec as P


def extended(cells, sides, width):
    for axis, dim in sides:
        count = lax.axis_size(axis)
        head = lax.slice_in_dim(cells, 0, width, axis=dim)
        tail = lax.slice_in_dim(cells, cells.shape[dim] - width, cells.shape[dim], axis=dim)
        cells = jnp.concatenate(
            [
                lax.ppermute(tail, axis, [(i, (i + 1) % count) for i in range(count)]),
                cells,
                lax.ppermute(head, axis, [((i + 1) % count, i) for i in range(count)]),
            ],
            axis=dim,
        )
    return cells


def tap_stack(padded, first, planes):
    base = padded[:, first : first + planes]
    return jnp.stack(
        [jnp.roll(base, (1 - b, 1 - e), axis=(2, 3)) for b in range(3) for e in range(3)]
    )


def forward_sum(padded, weight):
    planes = padded.shape[1] - 2
    total = jnp.zeros((weight.shape[2], planes) + padded.shape[2:], jnp.float32)
    for a in range(3):
        stack = tap_stack(padded, a, planes)
        total = total + jnp.einsum(
            "jixyz,ijo->oxyz",
            stack,
            weight[:, 9 * a : 9 * a + 9, :],
            preferred_element_type=jnp.float32,
        )
    return total


def weight_sum(padded, delta):
    planes = padded.shape[1] - 2
    parts = []
    for a in range(3):
        stack = tap_stack(padded, a, planes)
        parts.append(
            jnp.einsum("jixyz,oxyz->ijo", stack, delta, preferred_element_type=jnp.float32)
        )
    return jnp.concatenate(parts, axis=1)


def lifted_taps(weight, base, first):
    lifted = jnp.einsum(
        "ijo,oxyz->jixyz",
        weight[:, 9 * first : 9 * first + 9, :],
        base,
        preferred_element_type=jnp.float32,
    )
    total = jnp.zeros(lifted.shape[1:], jnp.float32)
    for j in range(9):
        b, e = (j // 3, j % 3)
        total = total + jnp.roll(lifted[j], (b - 1, e - 1), axis=(2, 3))
    return total


def spread_back(padded_delta, weight):
    planes = padded_delta.shape[1] - 2
    total = jnp.zeros((weight.shape[0], planes) + padded_delta.shape[2:], jnp.float32)
    for a in range(3):
        total = total + lifted_taps(weight, padded_delta[:, 2 - a : 2 - a + planes], a)
    return total


def silu_slope(values):
    sig = jax.nn.sigmoid(values)
    return sig * (1.0 + values * (1.0 - sig))


def body(field, out_grad, first_weight, second_weight):
    planes = field.shape[1]
    cells = planes * lax.axis_size("slab") * field.shape[2] * field.shape[3]
    factor = 1.0 / math.sqrt(cells)
    field_pad = extended(field, (("slab", 1),), 1)
    first_sum = lax.psum_scatter(
        forward_sum(field_pad, first_weight).astype(jnp.bfloat16),
        "chan",
        scatter_dimension=0,
        tiled=True,
    ).astype(jnp.float32)
    hidden = jax.nn.silu(first_sum).astype(jnp.bfloat16)
    hidden_pad = extended(hidden, (("slab", 1),), 1)
    second_sum = lax.psum(
        forward_sum(hidden_pad, second_weight).astype(jnp.bfloat16), "chan"
    ).astype(jnp.float32)
    second_delta = (out_grad.astype(jnp.float32) * silu_slope(second_sum)).astype(jnp.bfloat16)
    second_raw = weight_sum(hidden_pad, second_delta)
    delta_pad = extended(second_delta, (("slab", 1),), 1)
    hidden_back = spread_back(delta_pad, second_weight)
    first_delta = (hidden_back * silu_slope(first_sum)).astype(jnp.bfloat16)
    first_pad = extended(first_delta, (("slab", 1),), 1)
    piece = lax.all_gather(first_pad, "chan", axis=0, tiled=True)
    part = weight_sum(field_pad, piece[:, 1:-1])
    input_sum = spread_back(piece, first_weight)
    first_total, second_total = lax.psum((part, second_raw), "slab")
    return (input_sum.astype(jnp.bfloat16), first_total * factor, second_total * factor)


def solution(mesh):
    placed = (
        P("chan", "slab", None, None),
        P(None, "slab", None, None),
        P("chan", None, None),
        P("chan", None, None),
    )
    return jax.shard_map(
        body,
        mesh=mesh,
        in_specs=placed,
        out_specs=(P("chan", "slab", None, None), P("chan", None, None), P("chan", None, None)),
        check_vma=False,
    )
```

profile of v0, /device:TPU:0, one launch (start us, length us, event | category | flops | bytes accessed | tf_op | source)
XLA Modules:
  0.0 575.1 jit_solution(8807204771387383009)
XLA Ops:
  8.4 5.5 collective-permute-start.1
  25.5 1.8 copy-done.41
  42.5 1.8 copy-done.43
  44.9 2.9 copy-done.42
  47.7 2.3 fusion.121
  50.1 27.3 %reduce-scatter.2.cloned.1.call-done = bf16[16,4,48,128]{3,0,2,1:T(8,128)(2,1)} async-done(((bf16[32,4,48,128]{3,0,2,1:T(8,128)(2,1)}), bf16[16,4,48,128]{3,0,2,1:T(8,128)(2,1)}) %reduce-scatter.2.cloned.1.call-update) | async-done | bytes 786448 | tf_op jit(solution)/shard_map/reduce_scatter | solution.py:89
  79.0 4.9 collective-permute-start.3
  83.9 3.0 collective-permute-done.2
  112.4 1.7 copy-done.44
  115.9 1.8 copy-done.46
  122.9 2.3 fusion.23
  125.3 52.0 %all-reduce.4.cloned.1.call-done = bf16[32,4,48,128]{3,0,2,1:T(8,128)(2,1)} async-done(((bf16[32,4,48,128]{3,0,2,1:T(8,128)(2,1)}), bf16[32,4,48,128]{3,0,2,1:T(8,128)(2,1)}) %all-reduce.4.cloned.1.call-update) | async-done | bytes 1572880 | tf_op jit(solution)/shard_map/psum | solution.py:97
  177.3 3.0 fusion.12
  181.2 6.9 %convolution_bitcast_fusion.3 = f32[9,16,4,48,128]{4,1,3,2,0:T(8,128)} fusion(bf16[32,4,48,128]{3,0,2,1:T(8,128)(2,1)S(1)} %fusion.12, bf16[16,27,32]{2,0,1:T(8,128)(2,1)S(1)} %copy-done.83), kind=kOutput, calls=%fused_computation.3 | convolution fusion | flops 226492416 | bytes 15765504 | tf_op jit(solution)/shard_map/ijo,oxyz->jixyz/dot_general | solution.py:58
  188.1 8.0 %slice_bitcast_fusion.41 = (f32[16,4,48,128]{3,0,2,1:T(8,128)}, f32[16,4,48,128]{3,0,2,1:T(8,128)}, f32[16,4,48,128]{3,0,2,1:T(8,128)}, f32[16,4,48,128]{3,0,2,1...) fusion(f32[9,16,4,48,128]{4,1,3,2,0:T(8,128)} %convolution_bitc, ...), kind=kLoop, calls=%fused_computation.224 | loop fusion | bytes 25165824 | tf_op jit(solution)/shard_map/squeeze | solution.py:67
  198.7 2.4 copy-done.64
  201.2 1.8 copy-done.59
  203.2 1.8 copy-done.54
  208.2 3.7 collective-permute-start.4
  212.3 1.7 slice.1755
  214.0 1.6 slice.1751
  217.3 1.7 slice_maximum_fusion.18
  220.6 1.7 slice_maximum_fusion.16
  222.3 7.0 %convolution_bitcast_fusion.2 = f32[9,16,4,48,128]{4,1,3,2,0:T(8,128)} fusion(bf16[32,4,48,128]{3,0,2,1:T(8,128)(2,1)S(1)} %fusion.12, bf16[32,1,48,128]{3,0,2,1:T(8,128)(2,1)S(1)} %collective-permute-done.5, bf16[16,27,32]{2,0,1:T(8,128)(2,1)S(1)} %copy-done.83), kind=kOutput, calls=%fused_computation.2 | convolution fusion | flops 229638144 | bytes 16158720 | tf_op jit(solution)/shard_map/ijo,oxyz->jixyz/dot_general | solution.py:58
  229.3 8.9 %slice_bitcast_fusion.32 = (f32[16,4,48,128]{3,0,2,1:T(8,128)}, f32[16,4,48,128]{3,0,2,1:T(8,128)}, f32[16,4,48,128]{3,0,2,1:T(8,128)}, f32[16,4,48,128]{3,0,2,1...) fusion(f32[9,16,4,48,128]{4,1,3,2,0:T(8,128)} %convolution_bitc, ...), kind=kLoop, calls=%fused_computation.191 | loop fusion | bytes 25165824 | tf_op jit(solution)/shard_map/squeeze | solution.py:67
  239.1 2.6 slice.1801
  251.4 8.0 %convolution_bitcast_fusion.4 = f32[9,16,4,48,128]{4,1,3,2,0:T(8,128)} fusion(bf16[32,1,48,128]{3,0,2,1:T(8,128)(2,1)} %collective-permute-done.4, bf16[32,4,48,128]{3,0,2,1:T(8,128)(2,1)S(1)} %fusion.12, bf16[16,27,32]{2,0,1:T(8,128)(2,1)S(1)} %copy-done.83), kind=kOutput, calls=%fused_computation.4 | convolution fusion | flops 229638144 | bytes 16158720 | tf_op jit(solution)/shard_map/ijo,oxyz->jixyz/dot_general | solution.py:58
  259.4 9.2 %slice_bitcast_fusion.50 = (f32[16,4,48,128]{3,0,2,1:T(8,128)}, f32[16,4,48,128]{3,0,2,1:T(8,128)}, f32[16,4,48,128]{3,0,2,1:T(8,128)}, f32[16,4,48,128]{3,0,2,1...) fusion(f32[9,16,4,48,128]{4,1,3,2,0:T(8,128)} %convolution_bitc, ...), kind=kLoop, calls=%fused_computation.253 | loop fusion | bytes 25165824 | tf_op jit(solution)/shard_map/squeeze | solution.py:67
  271.2 2.4 copy-done.66
  273.7 1.8 copy-done.61
  275.6 1.8 copy-done.56
  290.5 1.8 slice_maximum_fusion.13
  292.3 1.7 slice_maximum_fusion.12
  294.0 1.7 slice_maximum_fusion.23
  295.6 1.7 slice_maximum_fusion.22
  301.5 19.9 %fusion.22 = bf16[16,4,48,128]{3,0,2,1:T(8,128)(2,1)} fusion(bf16[16,4,48,128]{3,0,2,1:T(8,128)(2,1)} %reduce-scatter.2.cloned.1.call-done, f32[16,4,47,128]{3,0,2,1:T(8,128)S(1)} %copy-done.33, f32[16,4,1,128]{3,0,2,1:T(8,128)S(1)} %slice.1800, f32[16,4,47,128]{3,0,2,1:T(8,128)} %slice.1793, f32[16,4,1,128]{3,0,2,1:T(8,128)S(1)} %slice.1792, ...), kind=kLoop, calls=%fused_computation.91 | loop fusion | flops 28311552 | bytes 53477376 | tf_op jit(solution)/shard_map/convert_element_type | solution.py:104
  322.5 4.5 collective-permute-start.7
  327.0 5.6 fusion.125
  333.9 5.1 fusion.128
  339.2 1.9 fusion.122
  341.9 26.1 %all-gather.2.cloned.1.call-done = bf16[32,6,48,128]{3,0,2,1:T(8,128)(2,1)} async-done(((bf16[16,6,48,128]{3,0,2,1:T(8,128)(2,1)}), bf16[32,6,48,128]{3,0,2,1:T(8,128)(2,1)}) %all-gather.2.cloned.1.call-update) | async-done | bytes 2359312 | tf_op jit(solution)/shard_map/all_gather | solution.py:106
  368.0 8.3 %convolution_bitcast_fusion = f32[9,16,4,48,128]{4,1,3,2,0:T(8,128)} fusion(bf16[32,6,48,128]{3,0,2,1:T(8,128)(2,1)} %all-gather.2.cloned.1.call-done, bf16[16,27,32]{2,0,1:T(8,128)(2,1)S(1)} %copy-done.85), kind=kOutput, calls=%fused_computation | convolution fusion | flops 226492416 | bytes 15765504 | tf_op jit(solution)/shard_map/ijo,oxyz->jixyz/dot_general | solution.py:58
  376.3 8.1 %slice_bitcast_fusion.1 = (f32[16,4,48,128]{3,0,2,1:T(8,128)S(1)}, f32[16,4,48,128]{3,0,2,1:T(8,128)}, f32[16,4,48,128]{3,0,2,1:T(8,128)}, f32[16,4,48,128]{3,0,...) fusion(f32[9,16,4,48,128]{4,1,3,2,0:T(8,128)} %convolution_bitc, ...), kind=kLoop, calls=%fused_computation.100 | loop fusion | bytes 25165824 | tf_op jit(solution)/shard_map/squeeze | solution.py:67
  385.3 2.7 slice.1905
  396.3 7.0 %convolution_bitcast_fusion.5 = f32[9,16,4,48,128]{4,1,0,3,2:T(8,128)} fusion(bf16[32,6,48,128]{3,0,2,1:T(8,128)(2,1)S(1)} %copy-done.1, bf16[16,27,32]{2,0,1:T(8,128)(2,1)S(1)} %copy-done.85), kind=kOutput, calls=%fused_computation.5 | convolution fusion | flops 226492416 | bytes 15765504 | tf_op jit(solution)/shard_map/ijo,oxyz->jixyz/dot_general | solution.py:58
  403.3 9.3 %slice_bitcast_fusion.21 = (f32[16,4,48,128]{3,0,2,1:T(8,128)}, f32[16,4,48,128]{3,0,2,1:T(8,128)}, f32[16,4,48,128]{3,0,2,1:T(8,128)}, f32[16,4,48,128]{3,0,2,1...) fusion(f32[9,16,4,48,128]{4,1,0,3,2:T(8,128)} %convolution_bitc, ...), kind=kLoop, calls=%fused_computation.160 | loop fusion | bytes 25165824 | tf_op jit(solution)/shard_map/squeeze | solution.py:67
  413.5 2.6 slice.1829
  425.8 7.0 %convolution_bitcast_fusion.1 = f32[9,16,4,48,128]{4,1,3,2,0:T(8,128)} fusion(bf16[32,6,48,128]{3,0,2,1:T(8,128)(2,1)S(1)} %copy-done.1, bf16[16,27,32]{2,0,1:T(8,128)(2,1)S(1)} %copy-done.85), kind=kOutput, calls=%fused_computation.1 | convolution fusion | flops 226492416 | bytes 15765504 | tf_op jit(solution)/shard_map/ijo,oxyz->jixyz/dot_general | solution.py:58
  432.8 9.2 %slice_bitcast_fusion.12 = (f32[16,4,48,128]{3,0,2,1:T(8,128)}, f32[16,4,48,128]{3,0,2,1:T(8,128)}, f32[16,4,48,128]{3,0,2,1:T(8,128)}, f32[16,4,48,128]{3,0,2,1...) fusion(f32[9,16,4,48,128]{4,1,3,2,0:T(8,128)} %convolution_bitc, ...), kind=kLoop, calls=%fused_computation.131 | loop fusion | bytes 25165824 | tf_op jit(solution)/shard_map/squeeze | solution.py:67
  442.9 2.8 slice.1871
  456.8 1.7 slice.1889
  458.4 1.7 slice.1825
  461.7 1.7 slice.1859
  465.0 5.1 fusion.131
  470.2 1.9 fusion.137
  472.1 1.9 fusion.134
  474.8 3.1 slice_maximum_fusion.3
  478.0 1.7 slice_maximum_fusion.2
  484.5 1.6 slice_maximum_fusion.11
  489.4 1.7 slice_maximum_fusion.7
  491.2 1.7 slice_maximum_fusion.6
  497.0 19.2 %fusion.27 = bf16[16,4,48,128]{3,0,2,1:T(8,128)(2,1)} fusion(f32[16,4,47,128]{3,0,2,1:T(8,128)S(1)} %copy-done.13, f32[16,4,1,128]{3,0,2,1:T(8,128)S(1)} %slice.1904, f32[16,4,47,128]{3,0,2,1:T(8,128)S(1)} %copy-done.14, f32[16,4,1,128]{3,0,2,1:T(8,128)S(1)} %slice.1896, f32[9,16,4,48,128]{4,1,3,2,0:T(8,128)} %convolution_bitcast_fusion, ...), kind=kLoop, calls=%fused_computation.97 | loop fusion | flops 24772608 | bytes 52690944 | tf_op jit(solution)/shard_map/convert_element_type | solution.py:110
  516.2 2.2 copy.60
  518.4 46.4 %all-reduce.6.cloned.1.call-done = (f32[16,27,32]{2,0,1:T(8,128)}, f32[16,27,32]{2,0,1:T(8,128)}) async-done(((f32[16,27,32]{2,0,1:T(8,128)}, f32[16,27,32]{2,0,1:T(8,128)}), (f32[16,27,32]{2,0,1:T(8,128)}, f32[16,27,32]{2,0,1:T(8,128)})) %all-reduce.6.cloned.1.call-update) | async-done | bytes 110608 | tf_op jit(solution)/shard_map/psum | solution.py:109
  (416 shorter events, 157.7 us)
Async XLA Ops:
  7.2 6.9 %copy-start = (bf16[16,4,48,128]{3,2,1,0:T(8,128)(2,1)S(1)}, bf16[16,4,48,128]{3,2,1,0:T(8,128)(2,1)}, u32[]{:S(2)}) copy-start(bf16[16,4,48,128]{3,2,1,0:T(8,128)(2,1)} %param.4) | copy-start | bytes 2359300
  7.2 70.2 %reduce-scatter.2.cloned.1.call-start = ((), (), s32[]{:S(2)}) async-start(), calls=%async_computation.1 | async-start | bytes 2359296 | tf_op jit(solution)/shard_map/reduce_scatter | solution.py:89
  8.4 19.6 %collective-permute-start.1 = (bf16[16,1,48,128]{3,0,2,1:T(8,128)(2,1)S(1)}, bf16[16,1,48,128]{3,0,2,1:T(8,128)(2,1)S(1)}, u32[]{:S(2)}, u32[]{:S(2)}) collective-permute-start(bf16[16,1,48,128]{3,0,2,1:T(8,128)(2,1)S(1)} %copy.134), channel_id=1, source_target_pairs={{2,0},{4,2},{6,4},{8,6},{10,8},{12,10},{14,12},{16,14},{18,16},{20... | collective-permute-start | bytes 589832 | tf_op jit(solution)/shard_map/ppermute | solution.py:18
  14.0 13.3 %collective-permute-start = (bf16[16,1,48,128]{3,0,2,1:T(8,128)(2,1)S(1)}, bf16[16,1,48,128]{3,0,2,1:T(8,128)(2,1)S(1)}, u32[]{:S(2)}, u32[]{:S(2)}) collective-permute-start(bf16[16,1,48,128]{3,0,2,1:T(8,128)(2,1)S(1)} %copy.143), channel_id=1, source_target_pairs={{0,2},{2,4},{4,6},{6,8},{8,10},{10,12},{12,14},{14,16},{16,18},{18... | collective-permute-start | bytes 589832 | tf_op jit(solution)/shard_map/ppermute | solution.py:16
  24.4 2.9 copy-start.41
  41.3 2.9 copy-start.43
  44.8 2.9 copy-start.42
  50.0 127.3 %all-reduce.4.cloned.1.call-start = ((), (), s32[]{:S(2)}) async-start(), calls=%async_computation.2 | async-start | bytes 3145728 | tf_op jit(solution)/shard_map/psum | solution.py:97
  79.0 8.0 %collective-permute-start.2 = (bf16[16,1,48,128]{3,0,2,1:T(8,128)(2,1)S(1)}, bf16[16,1,48,128]{3,0,2,1:T(8,128)(2,1)S(1)}, u32[]{:S(2)}, u32[]{:S(2)}) collective-permute-start(bf16[16,1,48,128]{3,0,2,1:T(8,128)(2,1)S(1)} %get-tuple-element.116), channel_id=1, source_target_pairs={{0,2},{2,4},{4,6},{6,8},{8,10},{10,12},{12,14},{14,16},{16,18},{18... | collective-permute-start | bytes 589832 | tf_op jit(solution)/shard_map/ppermute | solution.py:16
  79.0 8.0 %collective-permute-start.3 = (bf16[16,1,48,128]{3,0,2,1:T(8,128)(2,1)S(1)}, bf16[16,1,48,128]{3,0,2,1:T(8,128)(2,1)S(1)}, u32[]{:S(2)}, u32[]{:S(2)}) collective-permute-start(bf16[16,1,48,128]{3,0,2,1:T(8,128)(2,1)S(1)} %get-tuple-element.117), channel_id=1, source_target_pairs={{2,0},{4,2},{6,4},{8,6},{10,8},{12,10},{14,12},{16,14},{18,16},{20... | collective-permute-start | bytes 589832 | tf_op jit(solution)/shard_map/ppermute | solution.py:18
  111.3 2.8 copy-start.44
  114.8 2.9 copy-start.46
  119.9 3.0 copy-start.45
  125.2 52.1 %copy-start.82 = (bf16[32,4,48,128]{3,2,1,0:T(8,128)(2,1)S(1)}, bf16[32,4,48,128]{3,2,1,0:T(8,128)(2,1)}, u32[]{:S(2)}) copy-start(bf16[32,4,48,128]{3,2,1,0:T(8,128)(2,1)} %param.5) | copy-start | bytes 4718596
  125.2 242.8 %all-gather.2.cloned.1.call-start = ((), (), s32[]{:S(2)}) async-start(), calls=%async_computation.3 | async-start | bytes 3538944 | tf_op jit(solution)/shard_map/all_gather | solution.py:106
  196.1 2.4 copy-start.70
  198.5 22.1 %copy-start.15 = (f32[16,4,47,128]{3,0,2,1:T(8,128)}, f32[16,4,47,128]{3,0,2,1:T(8,128)S(1)}, u32[]{:S(2)}) copy-start(f32[16,4,47,128]{3,0,2,1:T(8,128)S(1)} %slice.1767) | copy-start | bytes 4620292
  198.5 2.5 copy-start.64
  198.7 20.3 %copy-start.18 = (f32[16,4,47,128]{3,0,2,1:T(8,128)}, f32[16,4,47,128]{3,0,2,1:T(8,128)S(1)}, u32[]{:S(2)}) copy-start(f32[16,4,47,128]{3,0,2,1:T(8,128)S(1)} %slice.1759) | copy-start | bytes 4620292
  201.2 16.1 %copy-start.21 = (f32[16,4,47,128]{3,0,2,1:T(8,128)}, f32[16,4,47,128]{3,0,2,1:T(8,128)S(1)}, u32[]{:S(2)}) copy-start(f32[16,4,47,128]{3,0,2,1:T(8,128)S(1)} %slice.1746) | copy-start | bytes 4620292
  203.2 12.5 %copy-start.23 = (f32[16,4,47,128]{3,0,2,1:T(8,128)}, f32[16,4,47,128]{3,0,2,1:T(8,128)S(1)}, u32[]{:S(2)}) copy-start(f32[16,4,47,128]{3,0,2,1:T(8,128)S(1)} %slice.1738) | copy-start | bytes 4620292
  206.3 5.6 copy-start.86
  208.2 43.3 %collective-permute-start.4 = (bf16[32,1,48,128]{3,0,2,1:T(8,128)(2,1)}, bf16[32,1,48,128]{3,0,2,1:T(8,128)(2,1)}, u32[]{:S(2)}, u32[]{:S(2)}) collective-permute-start(bf16[32,1,48,128]{3,0,2,1:T(8,128)(2,1)} %get-tuple-element.56), channel_id=1, source_target_pairs={{2,0},{4,2},{6,4},{8,6},{10,8},{12,10},{14,12},{16,14},{18,16},{20... | collective-permute-start | bytes 1179656 | tf_op jit(solution)/shard_map/ppermute | solution.py:18
  211.9 10.4 %collective-permute-start.5 = (bf16[32,1,48,128]{3,0,2,1:T(8,128)(2,1)S(1)}, bf16[32,1,48,128]{3,0,2,1:T(8,128)(2,1)S(1)}, u32[]{:S(2)}, u32[]{:S(2)}) collective-permute-start(bf16[32,1,48,128]{3,0,2,1:T(8,128)(2,1)S(1)} %copy-done.86), channel_id=1, source_target_pairs={{0,2},{2,4},{4,6},{6,8},{8,10},{10,12},{12,14},{14,16},{16,18},{18... | collective-permute-start | bytes 1179656 | tf_op jit(solution)/shard_map/ppermute | solution.py:16
  238.2 3.5 copy-start.71
  241.7 2.0 copy-start.65
  268.6 2.4 copy-start.72
  271.0 27.9 %copy-start.37 = (f32[16,4,47,128]{3,0,2,1:T(8,128)}, f32[16,4,47,128]{3,0,2,1:T(8,128)S(1)}, u32[]{:S(2)}) copy-start(f32[16,4,47,128]{3,0,2,1:T(8,128)S(1)} %slice.1734) | copy-start | bytes 4620292
  271.0 2.5 copy-start.66
  271.2 26.1 %copy-start.38 = (f32[16,4,47,128]{3,0,2,1:T(8,128)}, f32[16,4,47,128]{3,0,2,1:T(8,128)S(1)}, u32[]{:S(2)}) copy-start(f32[16,4,47,128]{3,0,2,1:T(8,128)S(1)} %slice.1726) | copy-start | bytes 4620292
  273.7 21.9 %copy-start.39 = (f32[16,4,47,128]{3,0,2,1:T(8,128)}, f32[16,4,47,128]{3,0,2,1:T(8,128)S(1)}, u32[]{:S(2)}) copy-start(f32[16,4,47,128]{3,0,2,1:T(8,128)S(1)} %slice.1713) | copy-start | bytes 4620292
  275.6 18.3 %copy-start.40 = (f32[16,4,47,128]{3,0,2,1:T(8,128)}, f32[16,4,47,128]{3,0,2,1:T(8,128)S(1)}, u32[]{:S(2)}) copy-start(f32[16,4,47,128]{3,0,2,1:T(8,128)S(1)} %slice.1705) | copy-start | bytes 4620292
  297.3 3.3 copy-start.22
  297.3 3.3 copy-start.24
  297.3 3.3 copy-start.94
  298.9 2.5 copy-start.19
  298.9 2.5 copy-start.89
  298.9 2.5 copy-start.93
  322.4 10.2 %collective-permute-start.6 = (bf16[16,1,48,128]{3,0,2,1:T(8,128)(2,1)S(1)}, bf16[16,1,48,128]{3,0,2,1:T(8,128)(2,1)S(1)}, u32[]{:S(2)}, u32[]{:S(2)}) collective-permute-start(bf16[16,1,48,128]{3,0,2,1:T(8,128)(2,1)S(1)} %get-tuple-element.90), channel_id=1, source_target_pairs={{0,2},{2,4},{4,6},{6,8},{8,10},{10,12},{12,14},{14,16},{16,18},{18... | collective-permute-start | bytes 589832 | tf_op jit(solution)/shard_map/ppermute | solution.py:16
  322.5 10.1 %copy-start.76 = (bf16[16,4,48,128]{3,0,2,1:T(8,128)(2,1)S(1)}, bf16[16,4,48,128]{3,0,2,1:T(8,128)(2,1)}, u32[]{:S(2)}) copy-start(bf16[16,4,48,128]{3,0,2,1:T(8,128)(2,1)} %fusion.22) | copy-start | bytes 2359300
  322.5 10.1 %collective-permute-start.7 = (bf16[16,1,48,128]{3,0,2,1:T(8,128)(2,1)S(1)}, bf16[16,1,48,128]{3,0,2,1:T(8,128)(2,1)S(1)}, u32[]{:S(2)}, u32[]{:S(2)}) collective-permute-start(bf16[16,1,48,128]{3,0,2,1:T(8,128)(2,1)S(1)} %get-tuple-element.91), channel_id=1, source_target_pairs={{2,0},{4,2},{6,4},{8,6},{10,8},{12,10},{14,12},{16,14},{18,16},{20... | collective-permute-start | bytes 589832 | tf_op jit(solution)/shard_map/ppermute | solution.py:18
  333.8 231.0 %all-reduce.6.cloned.1.call-start = ((), (), s32[]{:S(2)}) async-start(), calls=%async_computation.4 | async-start | bytes 884736 | tf_op jit(solution)/shard_map/psum | solution.py:109
  333.9 5.4 copy-start.47
  339.2 28.8 %copy-start.85 = (bf16[16,27,32]{2,0,1:T(8,128)(2,1)S(1)}, bf16[16,27,32]{2,0,1:T(8,128)(2,1)}, u32[]{:S(2)}) copy-start(bf16[16,27,32]{2,0,1:T(8,128)(2,1)} %param.6) | copy-start | bytes 82948
  384.4 3.6 copy-start.73
  387.9 2.0 copy-start.67
  412.7 3.5 copy-start.74
  442.0 3.6 copy-start.75
  453.9 16.3 %slice-start.2 = ((s8[7077888]{0:T(1024)(128)(4,1)}), s8[4194304]{0:T(1024)(128)(4,1)S(1)}, s32[]{:S(2)}) async-start(s8[7077888]{0:T(1024)(128)(4,1)} %bitcast.646), calls=%async_computation.7 | async-start | bytes 8388608
  461.7 8.4 %slice-start.3 = ((s8[7077888]{0:T(1024)(128)(4,1)}), s8[2883584]{0:T(1024)(128)(4,1)S(1)}, s32[]{:S(2)}) async-start(s8[7077888]{0:T(1024)(128)(4,1)} %bitcast.646), calls=%async_computation.8 | async-start | bytes 5767168
  465.0 7.1 %slice-start = ((s8[7077888]{0:T(1024)(128)(4,1)}), s8[4194304]{0:T(1024)(128)(4,1)S(1)}, s32[]{:S(2)}) async-start(s8[7077888]{0:T(1024)(128)(4,1)} %bitcast.644), calls=%async_computation.5 | async-start | bytes 8388608
  470.2 2.0 slice-start.1
  474.8 3.2 copy-start.17
  487.8 8.3 %copy-start.92 = (f32[16,4,1,128]{3,0,2,1:T(8,128)S(1)}, f32[16,4,1,128]{3,0,2,1:T(8,128)}, u32[]{:S(2)}) copy-start(f32[16,4,1,128]{3,0,2,1:T(8,128)} %slice.1867) | copy-start | bytes 98308
  489.4 3.4 copy-start.30
  489.4 6.6 %copy-start.90 = (f32[16,4,1,128]{3,0,2,1:T(8,128)S(1)}, f32[16,4,1,128]{3,0,2,1:T(8,128)}, u32[]{:S(2)}) copy-start(f32[16,4,1,128]{3,0,2,1:T(8,128)} %slice.1833) | copy-start | bytes 98308
  489.4 6.6 %copy-start.91 = (f32[16,4,1,128]{3,0,2,1:T(8,128)S(1)}, f32[16,4,1,128]{3,0,2,1:T(8,128)}, u32[]{:S(2)}) copy-start(f32[16,4,1,128]{3,0,2,1:T(8,128)} %slice.1814) | copy-start | bytes 98308
  491.1 3.3 copy-start.29
  491.1 4.9 copy-start.20
  491.1 4.9 copy-start.87
  491.1 4.9 copy-start.88
  492.8 3.3 copy-start.7
  492.8 3.3 copy-start.9
  494.4 2.6 copy-start.5
  (48 other events, 80.5 us)
Sparse Core Ops, SparseCore 0:
  50.1 27.1 reduce-scatter.1
  125.3 51.8 all-reduce.3
  333.9 34.0 all-gather.1
  475.0 89.8 all-reduce.5
where the time goes:
time: 585 us; the launch traced here: 575 us
  local copies, waits for them, and re-layouts  185 us (32%)
  waiting for transfers between devices  155 us (26%)
  other arithmetic  126 us (22%)
  matrix products  73.9 us (13%)
  starting transfers between devices  19.3 us (3%)
  between operations  15.6 us (3%)
    slice x84, local copies, waits for them, and re-layouts, lifted_taps(): total = total + jnp.roll(lifted[j], (b - 1, e - 1), axis=(2, 3))  76.1 us
    squeeze x6, local copies, waits for them, and re-layouts, lifted_taps(): total = total + jnp.roll(lifted[j], (b - 1, e - 1), axis=(2, 3))  52.7 us
    psum x1, waiting for transfers between devices, body(): lax.psum(forward_sum(hidden_pad, second_weight).astype(jnp.bfloat16), 'ch...  52 us
    psum x1, waiting for transfers between devices, body(): first_total, second_total = lax.psum((part, second_raw), 'slab')  46.4 us
    dot_general x6, matrix products, lifted_taps(): jnp.einsum('ijo,oxyz->jixyz', weight[:, 9 * first:9 * first + 9, :], base...  44.2 us
    unnamed x219, local copies, waits for them, and re-layouts  42.6 us
    concatenate x24, other arithmetic, lifted_taps(): total = total + jnp.roll(lifted[j], (b - 1, e - 1), axis=(2, 3))  41 us
    reduce_scatter x1, waiting for transfers between devices, body(): lax.psum_scatter(forward_sum(field_pad, first_weight).astype(jnp.bfloat16...  27.3 us
  transfers between devices with their start and end apart: 12, of which 6 were waited for; matrix products, arithmetic and copies ran while one was open for 18% of the time, Pallas kernels for 0%

commit v1 on v0

v1 whole, which is shorter than its diff:
```python
import functools
import math

import jax
import jax.numpy as jnp
from jax import lax
from jax.experimental import pallas as pl
from jax.experimental.pallas import tpu as pltpu
from jax.sharding import PartitionSpec as P

F32 = jnp.float32
BF16 = jnp.bfloat16
LIMIT = 48 * 1024 * 1024


def call(kernel, outs, args, scratch=(), flops=0, moved=0):
    whole = pl.BlockSpec(memory_space=pltpu.VMEM)
    return pl.pallas_call(
        kernel,
        out_shape=outs,
        in_specs=[whole] * len(args),
        out_specs=[whole] * len(outs),
        scratch_shapes=list(scratch),
        compiler_params=pltpu.CompilerParams(vmem_limit_bytes=LIMIT),
        cost_estimate=pl.CostEstimate(flops=flops, bytes_accessed=moved, transcendentals=0),
    )(*args)


def turn_kernel(extent, shifts, share, margin, x_ref, *refs):
    count, planes, rows = x_ref.shape[0], x_ref.shape[1], x_ref.shape[2]
    outs, wide = refs[:-1], refs[-1]
    pairs = planes // 2

    def widen(i, _):
        for x in range(planes):
            start = pl.multiple_of((i * planes + x) * rows, 8)
            wide[pl.ds(start, rows), :] = x_ref[i, x].astype(F32)
        return 0

    lax.fori_loop(0, count, widen, 0)
    me = lax.axis_index("chan")
    for s, shift in enumerate(shifts):
        base = lax.rem(me + shift, extent) * share - margin + rows

        def turn(f, _, base=base, s=s):
            y = lax.rem(base + f, rows)
            for x in range(planes):
                tile = wide[pl.ds(x * rows + y, count, stride=planes * rows), :]
                outs[s * pairs + x // 2][f, x % 2] = tile.astype(BF16)
            return 0

        lax.fori_loop(0, share + 2 * margin, turn, 0)


def turned(x, extent, shifts, margin):
    count, planes, rows, depth = x.shape
    share = rows // extent
    piece = jax.ShapeDtypeStruct((share + 2 * margin, 2, count, depth), BF16)
    return call(
        functools.partial(turn_kernel, extent, shifts, share, margin),
        [piece] * (len(shifts) * planes // 2),
        [x],
        [pltpu.VMEM((count * planes * rows, depth), F32)],
        moved=x.size * 4,
    )


def columns(refs, row):
    sides = []
    for q in range(2):
        parts = []
        for ref in refs:
            part = ref[pl.ds(row + q, 3)]
            parts.append(part.reshape(6 * part.shape[2], part.shape[3]))
        sides.append(jnp.concatenate(parts, axis=0) if len(parts) > 1 else parts[0])
    return jnp.concatenate(sides, axis=1)


def taps(weight, refs, row):
    lifted = jnp.dot(weight, columns(refs, row), preferred_element_type=F32)
    third = lifted.shape[0] // 3
    depth = lifted.shape[1] // 2
    sums = []
    for q in range(2):
        side = lifted[:, q * depth : (q + 1) * depth]
        sums.append(
            side[third : 2 * third]
            + pltpu.roll(side[:third], 1, 1)
            + pltpu.roll(side[2 * third :], depth - 1, 1)
        )
    return sums


def silu_parts(v):
    sig = jax.nn.sigmoid(v)
    return sig, sig * (1.0 + v * (1.0 - sig))


def forward_kernel(groups, pairs, *refs):
    refs = list(refs)
    fields = [[refs.pop(0) for _ in range(groups)] for _ in range(pairs + 2)]
    grads = [refs.pop(0) for _ in range(pairs)]
    first, second = refs.pop(0), refs.pop(0)
    hiddens = [refs.pop(0) for _ in range(pairs + 1)]
    slopes = [refs.pop(0) for _ in range(pairs + 1)]
    deltas = [refs.pop(0) for _ in range(pairs)]

    def one(r, _):
        row = 2 * r
        for p in range(pairs + 1):
            for q, v in enumerate(taps(first[...], fields[p] + fields[p + 1], row)):
                sig, slope = silu_parts(v)
                shape = hiddens[p].shape[1:]
                hiddens[p][row + q] = (v * sig).astype(BF16).reshape(shape)
                slopes[p][row + q] = slope.astype(BF16).reshape(shape)
        return 0

    lax.fori_loop(0, hiddens[0].shape[0] // 2, one, 0)

    def two(r, _):
        row = 2 * r
        for p in range(pairs):
            for q, v in enumerate(taps(second[...], hiddens[p : p + 2], row)):
                shape = deltas[p].shape[1:]
                out_grad = grads[p][row + q].astype(F32)
                slope = silu_parts(v)[1].reshape(shape)
                deltas[p][row + q] = (out_grad * slope).astype(BF16)
        return 0

    lax.fori_loop(0, deltas[0].shape[0] // 2, two, 0)


def planes_of(pairs):
    return [(refs, x) for refs in pairs for x in range(2)]


def weight_loop(total, pieces, first_row, deltas, delta_row, count):
    total[...] = jnp.zeros_like(total)

    def step(r, _):
        left, right = [], []
        for x, ((delta,), place) in enumerate(deltas):
            rows = []
            for refs, side in pieces[x : x + 3]:
                for ref in refs:
                    part = ref[pl.ds(first_row + 2 * r, 4), side]
                    rows.append(part.reshape(4 * part.shape[1], part.shape[2]))
            left.append(jnp.concatenate(rows, axis=0))
            rows = []
            for q in range(2):
                wide = delta[delta_row + 2 * r + q, place]
                plain = wide.astype(F32)
                depth = plain.shape[1]
                rows += [
                    pltpu.roll(plain, depth - 1, 1).astype(BF16),
                    wide,
                    pltpu.roll(plain, 1, 1).astype(BF16),
                    jnp.zeros_like(wide),
                ]
            right.append(jnp.concatenate(rows, axis=0))
        total[...] += lax.dot_general(
            jnp.concatenate(left, axis=1),
            jnp.concatenate(right, axis=1),
            (((1,), (1,)), ((), ())),
            preferred_element_type=F32,
        )
        return 0

    lax.fori_loop(0, count // 2, step, 0)


def weight_fold(total, raw, groups):
    size = raw.shape[2]
    lanes = raw.shape[3]
    for a in range(3):
        for j in range(groups):
            for b in range(3):
                start = ((a * groups + j) * 4 + b) * size
                raw[j, 3 * a + b] = (
                    total[start : start + size, :lanes]
                    + total[start + size : start + 2 * size, lanes:]
                )


def second_kernel(share, pairs, *refs):
    refs = list(refs)
    hiddens = [[refs.pop(0)] for _ in range(pairs + 1)]
    deltas = [refs.pop(0) for _ in range(pairs)]
    raw, total = refs
    weight_loop(total, planes_of(hiddens), 2, planes_of([[d] for d in deltas]), 2, share)
    weight_fold(total, raw, 1)


def back_kernel(share, groups, pairs, *refs):
    refs = list(refs)
    deltas = [refs.pop(0) for _ in range(pairs + 2)]
    slopes = [refs.pop(0) for _ in range(pairs + 1)]
    fields = [[refs.pop(0) for _ in range(groups)] for _ in range(pairs + 2)]
    weight = refs.pop(0)
    firsts = [refs.pop(0) for _ in range(pairs + 1)]
    raw, total = refs

    def one(r, _):
        row = 2 * r
        for p in range(pairs + 1):
            for q, v in enumerate(taps(weight[...], deltas[p : p + 2], row)):
                shape = firsts[p].shape[1:]
                slope = slopes[p][row + 2 + q].astype(F32)
                firsts[p][row + q] = (v.reshape(shape) * slope).astype(BF16)
        return 0

    lax.fori_loop(0, firsts[0].shape[0] // 2, one, 0)
    near = planes_of(fields)[1:-1]
    own = planes_of([[first] for first in firsts])[1:-1]
    weight_loop(total, near, 3, own, 1, share)
    weight_fold(total, raw, groups)


def last_kernel(pairs, *refs):
    refs = list(refs)
    firsts = [refs.pop(0) for _ in range(pairs + 1)]
    weight = refs.pop(0)
    outs = refs

    def one(r, _):
        row = 2 * r
        for p in range(pairs):
            for q, v in enumerate(taps(weight[...], firsts[p : p + 2], row)):
                size = outs[0].shape[2]
                channels = len(outs) * size
                for x in range(2):
                    for j, out in enumerate(outs):
                        low = x * channels + j * size
                        out[row + q, 2 * p + x] = v[low : low + size].astype(BF16)
        return 0

    lax.fori_loop(0, outs[0].shape[0] // 2, one, 0)


def merge_kernel(extent, *refs):
    pieces, out, wide = refs[:-2], refs[-2], refs[-1]
    share, planes, size = pieces[0].shape[:3]
    rows = out.shape[2]
    me = lax.axis_index("chan")
    for j, piece in enumerate(pieces):
        base = lax.rem(me + extent - j, extent) * share

        def widen(f, _, piece=piece, base=base):
            for x in range(planes):
                start = ((base + f) * planes + x) * size
                start = pl.multiple_of(start, 8) if size % 8 == 0 else start
                wide[pl.ds(start, size), :] = piece[f, x].astype(F32)
            return 0

        lax.fori_loop(0, share, widen, 0)

    def turn(i, _):
        for x in range(planes):
            tile = wide[pl.ds(x * size + i, rows, stride=planes * size), :]
            out[i, x] = tile.astype(BF16)
        return 0

    lax.fori_loop(0, size, turn, 0)


def paired(weight):
    shifted = [jnp.pad(weight, ((0, 0), (x, 1 - x), (0, 0), (0, 0), (0, 0))) for x in range(2)]
    return jnp.transpose(jnp.stack(shifted), (4, 0, 5, 2, 3, 1))


def wide_columns(paired_weight, groups):
    e, x, out, four, b, count = paired_weight.shape
    split = paired_weight.reshape(e, x, out, 2, 2, b, groups, count // groups)
    return jnp.transpose(split, (0, 1, 2, 3, 6, 5, 4, 7)).reshape(e * x * out, four * b * count)


def slab_sum(values, axis):
    count = lax.axis_size(axis)
    if count & (count - 1) != 0:
        return lax.psum(values, axis)
    stride = 1
    while stride < count:
        radix = 4 if count % (4 * stride) == 0 else 2
        got = [values] + [
            lax.ppermute(values, axis, [(i, i ^ (m * stride)) for i in range(count)])
            for m in range(1, radix)
        ]
        values = got[0] + got[1]
        if radix == 4:
            values = values + (got[2] + got[3])
        stride *= radix
    return values


def body(field, out_grad, first_weight, second_weight):
    extent = lax.axis_size("chan")
    slabs = lax.axis_size("slab")
    me = lax.axis_index("chan")
    size, planes, rows, depth = field.shape
    channels = size * extent
    pairs = planes // 2
    share = rows // extent
    factor = 1.0 / math.sqrt(planes * slabs * rows * depth)

    def to_chan(value, shift):
        return lax.ppermute(value, "chan", [(i, (i + shift) % extent) for i in range(extent)])

    def to_next(value):
        return lax.ppermute(value, "slab", [(i, (i + 1) % slabs) for i in range(slabs)])

    def to_prev(value):
        return lax.ppermute(value, "slab", [((i + 1) % slabs, i) for i in range(slabs)])

    sent = turned(field, extent, list(range(extent)), 4)
    weights = jnp.stack([first_weight, second_weight])
    weight_parts = [weights] + [to_chan(weights, j) for j in range(1, extent)]
    parts = [sent[:pairs]]
    for j in range(1, extent):
        parts.append([to_chan(piece, j) for piece in sent[j * pairs : (j + 1) * pairs]])
    by_pair = [[parts[j][p] for j in range(extent)] for p in range(pairs)]
    groups = extent
    if size % 16 != 0:
        by_pair = [[jnp.concatenate(pieces, axis=2)] for pieces in by_pair]
        groups = 1
    before = [to_next(piece) for piece in by_pair[-1]]
    after = [to_prev(piece) for piece in by_pair[0]]
    fields = [before] + by_pair + [after]

    own_order = jnp.concatenate([part[0] for part in weight_parts], axis=0)
    second_all = jnp.zeros((channels,) + second_weight.shape[1:], BF16)
    for j, part in enumerate(weight_parts):
        place = lax.rem(me + extent - j, extent) * size
        second_all = lax.dynamic_update_slice(second_all, part[1], (place, 0, 0))
    first_five = own_order.reshape(channels, 3, 3, 3, channels)
    second_five = second_all.reshape(channels, 3, 3, 3, channels)

    def backward(five):
        return jnp.transpose(five[:, ::-1, ::-1, ::-1], (4, 1, 2, 3, 0))

    first_wide = wide_columns(paired(first_five), groups)
    second_wide = wide_columns(paired(second_five), 1)
    second_back = wide_columns(paired(backward(second_five)), 1)
    first_back = wide_columns(paired(backward(first_five)), 1)

    grads = turned(out_grad, extent, [0], 2)

    def many(count, rows_each, dtype=BF16):
        return [jax.ShapeDtypeStruct((rows_each, 2, channels, depth), dtype)] * count

    flat_fields = [piece for pieces in fields for piece in pieces]
    work = 2 * 27 * channels * channels * depth
    made = call(
        functools.partial(forward_kernel, groups, pairs),
        many(pairs + 1, share + 6) * 2 + many(pairs, share + 4),
        flat_fields + list(grads) + [first_wide, second_wide],
        flops=work * 2 * planes * share,
        moved=8 * planes * share * channels * depth,
    )
    hiddens = made[: pairs + 1]
    slopes = made[pairs + 1 : 2 * pairs + 2]
    deltas = made[2 * pairs + 2 :]
    all_deltas = [to_next(deltas[-1])] + list(deltas) + [to_prev(deltas[0])]

    def raw_shape(count):
        return jax.ShapeDtypeStruct((count, 9, channels // count, 4 * channels), F32)

    total = pltpu.VMEM((12 * channels, 8 * channels), F32)
    (second_raw,) = call(
        functools.partial(second_kernel, share, pairs),
        [raw_shape(1)],
        list(hiddens) + list(deltas),
        [total],
        flops=work * planes * share,
        moved=8 * planes * share * channels * depth,
    )
    made = call(
        functools.partial(back_kernel, share, groups, pairs),
        many(pairs + 1, share + 2) + [raw_shape(groups)],
        all_deltas + list(slopes) + flat_fields + [second_back],
        [total],
        flops=work * 2 * planes * share,
        moved=8 * planes * share * channels * depth,
    )
    firsts, first_raw = made[:-1], made[-1]

    first_groups = first_raw.reshape(groups, 9, channels // groups, 4 * channels)
    if groups != extent:
        first_groups = jnp.transpose(
            first_groups.reshape(9, extent, size, 4 * channels), (1, 0, 2, 3)
        )
    second_groups = second_raw.reshape(9, channels, 4 * channels)
    mine = None
    for j in range(extent):
        place = lax.rem(me + extent - j, extent) * size
        piece = jnp.stack(
            [
                first_groups[j],
                lax.dynamic_slice_in_dim(second_groups, place, size, axis=1),
            ]
        )[..., : 3 * channels]
        piece = piece if j == 0 else to_chan(piece, extent - j)
        mine = piece if mine is None else mine + piece
    both = slab_sum(mine, "slab") * factor
    both = both.reshape(2, 3, 3, size, 3, channels)
    both = jnp.transpose(both, (0, 3, 1, 2, 4, 5)).reshape(2, size, 27, channels)

    out_piece = jax.ShapeDtypeStruct((share, planes, size, depth), BF16)
    made = call(
        functools.partial(last_kernel, pairs),
        [out_piece] * extent,
        list(firsts) + [first_back],
        flops=work * planes * share,
        moved=4 * planes * share * channels * depth,
    )
    pieces = [made[0]] + [None] * (extent - 1)
    for j in range(1, extent):
        pieces[extent - j] = to_chan(made[j], extent - j)
    (input_grad,) = call(
        functools.partial(merge_kernel, extent),
        [jax.ShapeDtypeStruct(field.shape, BF16)],
        pieces,
        [pltpu.VMEM((rows * planes * size, depth), F32)],
        moved=4 * field.size,
    )
    return input_grad, both[0], both[1]


def solution(mesh):
    placed = (
        P("chan", "slab", None, None),
        P(None, "slab", None, None),
        P("chan", None, None),
        P("chan", None, None),
    )
    return jax.shard_map(
        body,
        mesh=mesh,
        in_specs=placed,
        out_specs=(P("chan", "slab", None, None), P("chan", None, None), P("chan", None, None)),
        check_vma=False,
    )
```

time: 585 us -> 120 us (0.21); the launches traced: 575 us -> 119 us
  local copies, waits for them, and re-layouts: 185 us -> 32.7 us
  waiting for transfers between devices: 155 us -> 18.8 us
  other arithmetic: 126 us -> 3.2 us
  matrix products: 73.9 us -> 0 us
  Pallas kernels: 0 us -> 38.2 us
  between operations: 15.6 us -> 1.1 us
  starting transfers between devices: 19.3 us -> 25.2 us
    psum x2 -> x0, waiting for transfers between devices: 98.4 us -> none  [the longest x1 52 us: body(): lax.psum(forward_sum(hidden_pad, second_weight).astype(jnp.bfloat16), 'ch...]
    slice x109 -> x5, local copies, waits for them, and re-layouts: 89.1 us -> 2.46 us  [the longest x3 1.55 us: body(): return (input_grad, both[0], both[1])]
    dot_general x18 -> x0, matrix products: 73.9 us -> none  [the longest x6 44.2 us: lifted_taps(): jnp.einsum('ijo,oxyz->jixyz', weight[:, 9 * first:9 * first + 9, :], base...]
    squeeze x6 -> x0, local copies, waits for them, and re-layouts: 52.7 us -> none  [lifted_taps(): total = total + jnp.roll(lifted[j], (b - 1, e - 1), axis=(2, 3))]
    concatenate x43 -> x1, other arithmetic: 52.4 us -> 0.73 us  [body(): own_order = jnp.concatenate([part[0] for part in weight_parts], axis=0)]
    convert_element_type x5 -> x0, other arithmetic: 46 us -> none  [the longest x1 19.9 us: body(): first_delta = (hidden_back * silu_slope(first_sum)).astype(jnp.bfloat16)]
    pallas_call x0 -> x7, Pallas kernels: none -> 38.2 us  [call(): pl.pallas_call(kernel, out_shape=outs, in_specs=[whole] * len(args), out_...]
    unnamed x219 -> x62, local copies, waits for them, and re-layouts: 42.6 us -> 14.2 us
  transfers between devices with their start and end apart: 12 -> 17, of which waited for: 6 -> 4; matrix products, arithmetic and copies ran while one was open for 18% -> 17% of each run, Pallas kernels for 0% -> 11%
where the time goes in v1:
time: 120 us; the launch traced here: 119 us
  Pallas kernels  38.2 us (32%)
  local copies, waits for them, and re-layouts  32.7 us (27%)
  starting transfers between devices  25.2 us (21%)
  waiting for transfers between devices  18.8 us (16%)
  other arithmetic  3.2 us (3%)
    pallas_call x7, Pallas kernels, call(): pl.pallas_call(kernel, out_shape=outs, in_specs=[whole] * len(args), out_...  38.2 us
    unnamed x62, local copies, waits for them, and re-layouts  14.2 us
    ppermute x3, starting transfers between devices, to_prev(): lax.ppermute(value, 'slab', [((i + 1) % slabs, i) for i in range(slabs)])  13.3 us
    ppermute x5, waiting for transfers between devices, to_chan(): lax.ppermute(value, 'chan', [(i, (i + shift) % extent) for i in range(ext...  9.65 us
    ppermute x6, waiting for transfers between devices, slab_sum(): lax.ppermute(values, axis, [(i, i ^ m * stride) for i in range(count)])  9.15 us
    ppermute x6, starting transfers between devices, slab_sum(): lax.ppermute(values, axis, [(i, i ^ m * stride) for i in range(count)])  6.64 us
    ppermute x5, starting transfers between devices, to_chan(): lax.ppermute(value, 'chan', [(i, (i + shift) % extent) for i in range(ext...  5.16 us
    reshape x5, local copies, waits for them, and re-layouts, wide_columns(): jnp.transpose(split, (0, 1, 2, 3, 6, 5, 4, 7))  4.49 us
  transfers between devices with their start and end apart: 17, of which 4 were waited for; matrix products, arithmetic and copies ran while one was open for 17% of the time, Pallas kernels for 11%

profile of v1, /device:TPU:0, one launch (start us, length us, event | category | flops | bytes accessed | tf_op | source)
XLA Modules:
  0.0 119.2 jit_solution(13437891892334949675)
XLA Ops:
  0.6 1.8 %pad_maximum_fusion.1 = bf16[2,16,27,32]{3,1,2,0:T(8,128)(2,1)} fusion(bf16[1,16,27,32]{3,1,2,0:T(8,128)(2,1)} %bitcast.69, bf16[1,16,27,32]{3,1,2,0:T(8,128)(2,1)} %bitcast.67), kind=kLoop, calls=%fused_computation.12 | loop fusion | flops 27648 | bytes 110592 | tf_op jit(solution)/shard_map/stack | solution.py:315
  2.4 2.9 %collective-permute-start.6 = (bf16[2,16,27,32]{3,1,2,0:T(8,128)(2,1)}, bf16[2,16,27,32]{3,1,2,0:T(8,128)(2,1)}, u32[]{:S(2)}, u32[]{:S(2)}) collective-permute-start(bf16[2,16,27,32]{3,1,2,0:T(8,128)(2,1)} %pad_maximum_fusion.1), channel_id=1, source_target_pairs={{0,1},{1,0},{2,3},{3,2},{4,5},{5,4},{6,7},{7,6},{8,9},{9,8},{10,11... | collective-permute-start | bytes 165896 | tf_op jit(solution)/shard_map/ppermute | solution.py:306
  5.4 1.1 copy-done.1
  6.5 2.8 %shard_map.67 = (bf16[32,2,16,128]{3,2,1,0:T(8,128)(2,1)S(1)}, bf16[32,2,16,128]{3,2,1,0:T(8,128)(2,1)S(1)}, bf16[32,2,16,128]{3,2,1,0:T(8,128)(2,1)}, bf16[32,2,16,128]{3,2,1,0:T(8,128)(2,1)S(1)}) custom-call(bf16[16,4,48,128]{3,2,1,0:T(8,128)(2,1)S(1)} %copy-done.1), custom_call_target="tpu_custom_call" | custom-call | bytes 1572864 | tf_op jit(solution)/shard_map/pallas_call | solution.py:18
  9.3 2.0 %collective-permute-start.3 = (bf16[32,2,16,128]{3,2,1,0:T(8,128)(2,1)}, bf16[32,2,16,128]{3,2,1,0:T(8,128)(2,1)S(1)}, u32[]{:S(2)}, u32[]{:S(2)}) collective-permute-start(bf16[32,2,16,128]{3,2,1,0:T(8,128)(2,1)} %get-tuple-element.26), channel_id=1, source_target_pairs={{0,1},{1,0},{2,3},{3,2},{4,5},{5,4},{6,7},{7,6},{8,9},{9,8},{10,11... | collective-permute-start | bytes 786440 | tf_op jit(solution)/shard_map/ppermute | solution.py:306
  11.3 4.4 %collective-permute-start.4 = (bf16[32,2,16,128]{3,2,1,0:T(8,128)(2,1)S(1)}, bf16[32,2,16,128]{3,2,1,0:T(8,128)(2,1)S(1)}, u32[]{:S(2)}, u32[]{:S(2)}) collective-permute-start(bf16[32,2,16,128]{3,2,1,0:T(8,128)(2,1)S(1)} %get-tuple-element.25.refs_2_.refs_9_), channel_id=1, source_target_pairs={{2,0},{4,2},{6,4},{8,6},{10,8},{12,10},{14,12},{16,14},{18,16},{20... | collective-permute-start | bytes 786440 | tf_op jit(solution)/shard_map/ppermute | solution.py:312
  15.7 0.7 broadcast_in_dim.3
  16.5 1.6 %constant_dynamic-update-slice_fusion = bf16[32,27,32]{2,0,1:T(8,128)(2,1)} fusion(bf16[32,27,32]{2,0,1:T(8,128)(2,1)} %broadcast_in_dim.3, bf16[16,27,32]{2,0,1:T(8,128)(2,1)} %param.7, s32[]{:T(128)S(6)} %select_n.8), kind=kLoop, calls=%fused_computation.25 | loop fusion | bytes 221188 | tf_op jit(solution)/shard_map/dynamic_update_slice | solution.py:333
  18.0 1.7 %shard_map.68 = (bf16[28,2,32,128]{3,2,1,0:T(8,128)(2,1)S(1)}, bf16[28,2,32,128]{3,2,1,0:T(8,128)(2,1)S(1)}) custom-call(bf16[32,4,48,128]{3,2,1,0:T(8,128)(2,1)S(1)} %copy-done), custom_call_target="tpu_custom_call" | custom-call | bytes 3145728 | tf_op jit(solution)/shard_map/pallas_call | solution.py:18
  19.7 0.8 copy-done.25
  20.5 0.8 copy-done.27
  21.2 1.6 %fusion.1 = bf16[32,27,32]{2,0,1:T(8,128)(2,1)} fusion(bf16[32,27,32]{2,0,1:T(8,128)(2,1)} %constant_dynamic-update-slice_fusion, s32[]{:T(128)S(6)} %select_n.9, bf16[2,16,27,32]{3,1,2,0:T(8,128)(2,1)} %collective-permute-done.6), kind=kLoop, calls=%fused_computation.22 | loop fusion | bytes 221188 | tf_op jit(solution)/shard_map/dynamic_update_slice | solution.py:333
  22.8 0.9 slice.34
  23.8 1.1 pad_bitcast_fusion.5
  24.9 0.1 maximum_bitcast_fusion
  25.1 4.4 %collective-permute-start.5 = (bf16[32,2,16,128]{3,2,1,0:T(8,128)(2,1)S(1)}, bf16[32,2,16,128]{3,2,1,0:T(8,128)(2,1)S(1)}, u32[]{:S(2)}, u32[]{:S(2)}) collective-permute-start(bf16[32,2,16,128]{3,2,1,0:T(8,128)(2,1)S(1)} %collective-permute-done.3.refs_3_.refs_10_), channel_id=1, source_target_pairs={{2,0},{4,2},{6,4},{8,6},{10,8},{12,10},{14,12},{16,14},{18,16},{20... | collective-permute-start | bytes 786440 | tf_op jit(solution)/shard_map/ppermute | solution.py:312
  29.6 0.7 pad_maximum_fusion.2
  30.3 0.3 copy.20
  30.6 0.5 copy.21
  31.0 0.3 reshape.54.refs_11_
  31.4 1.1 pad_bitcast_fusion.7
  32.6 0.1 pad_maximum_fusion
  32.7 1.4 %copy.19 = bf16[3,2,32,2,2,3,2,16]{2,1,0,7,6,5,4,3:T(2,128)(2,1)} copy(bf16[3,2,32,2,2,3,2,16]{2,7,4,0,5,6,3,1:T(8,128)(2,1)S(1)} %bitcast.63) | data formatting | bytes 294912 | tf_op jit(solution)/shard_map/transpose | solution.py:274
  34.1 1.5 %reshape.51 = bf16[192,384]{0,1:T(8,128)(2,1)S(1)} reshape(bf16[3,2,32,2,2,3,2,16]{2,1,0,7,6,5,4,3:T(2,128)(2,1)} %copy.19) | data formatting | bytes 294912 | tf_op jit(solution)/shard_map/reshape | solution.py:274
  35.7 0.8 copy.22.refs_10_
  36.4 0.7 copy-done.12
  37.2 0.7 copy-done.15
  37.9 0.7 copy-done.18
  38.6 0.7 copy-done.21
  39.3 0.9 copy-done.7
  40.2 0.9 copy-done.10
  41.2 0.9 copy-done.13
  42.1 0.9 copy-done.16
  43.1 0.9 copy-done.19
  44.0 0.9 copy-done.22
  45.0 0.9 copy-done.24
  45.9 1.0 copy-done.26
  46.9 1.0 copy-done.28
  47.9 12.1 %shard_map.69 = (bf16[30,2,32,128]{3,2,1,0:T(8,128)(2,1)S(1)}, bf16[30,2,32,128]{3,2,1,0:T(8,128)(2,1)S(1)}, bf16[30,2,32,128]{3,2,1,0:T(8,128)(2,1)S(1)}, bf16[...) custom-call(bf16[32,2,16,128]{3,2,1,0:T(8,128)(2,1)S(1)} %copy-done., ...), custom_call_target="tpu_custom_call" | custom-call | flops 1358954496 | bytes 3145728 | tf_op jit(solution)/shard_map/pallas_call | solution.py:18
  60.0 4.4 %collective-permute-start.8 = (bf16[28,2,32,128]{3,2,1,0:T(8,128)(2,1)S(1)}, bf16[28,2,32,128]{3,2,1,0:T(8,128)(2,1)}, u32[]{:S(2)}, u32[]{:S(2)}) collective-permute-start(bf16[28,2,32,128]{3,2,1,0:T(8,128)(2,1)S(1)} %get-tuple-element.30.refs_1_.refs_3_), channel_id=1, source_target_pairs={{2,0},{4,2},{6,4},{8,6},{10,8},{12,10},{14,12},{16,14},{18,16},{20... | collective-permute-start | bytes 1376264 | tf_op jit(solution)/shard_map/ppermute | solution.py:312
  64.5 0.9 reverse_bitcast_fusion.1
  65.5 0.1 maximum_bitcast_fusion.1
  65.7 1.3 %copy.24 = bf16[3,2,32,2,1,3,2,32]{7,6,5,3,2,1,0,4:T(2,128)(2,1)} copy(bf16[3,2,32,2,1,3,2,32]{7,2,4,5,6,3,1,0:T(8,128)(2,1)S(1)} %bitcast.65) | data formatting | bytes 294912 | tf_op jit(solution)/shard_map/transpose | solution.py:274
  67.0 1.5 %reshape.56.refs_15_ = bf16[192,384]{1,0:T(8,128)(2,1)S(1)} reshape(bf16[3,2,32,2,1,3,2,32]{7,6,5,3,2,1,0,4:T(2,128)(2,1)} %copy.24) | data formatting | bytes 294912 | tf_op jit(solution)/shard_map/reshape | solution.py:274
  68.6 4.4 %shard_map.73 = f32[1,9,32,128]{3,2,1,0:T(8,128)S(1)} custom-call(bf16[30,2,32,128]{3,2,1,0:T(8,128)(2,1)S(1)} %get-tuple-element.40.refs_0_, bf16[30,2,32,128]{3,2,1,0:T(8,128)(2,1)S(1)} %get-tuple-element.41.refs_1_, bf16[30,2,32,128]{3,2,1,0:T(8,128)(2,1)S(1)} %get-tuple-element.42.refs_2_, ...), custom_call_target="tpu_custom_call" | custom-call | flops 679477248 | bytes 3145728 | tf_op jit(solution)/shard_map/pallas_call | solution.py:18
  73.1 10.8 %shard_map.70 = (bf16[26,2,32,128]{3,2,1,0:T(8,128)(2,1)S(1)}, bf16[26,2,32,128]{3,2,1,0:T(8,128)(2,1)S(1)}, bf16[26,2,32,128]{3,2,1,0:T(8,128)(2,1)S(1)}, f32[2,9,16,128]{3,2,1,0:T(8,128)S(1)}) custom-call(bf16[28,2,32,128]{3,2,1,0:T(8,128)(2,1)S(1)} %collective-permute-done.7.refs_0_, bf16[28,2,32,128]{3,2,1,0:T(8,128)(2,1)S(1)} %get-tuple-element.30.refs_1_.refs_3_, ...), custom_call_target="tpu_custom_call" | custom-call | flops 1358954496 | bytes 3145728 | tf_op jit(solution)/shard_map/pallas_call | solution.py:18
  84.0 0.1 collective-permute-start.10
  84.1 5.1 %collective-permute-done.10 = f32[2,9,16,96]{3,2,1,0:T(8,128)S(1)} collective-permute-done((f32[2,9,16,96]{3,2,1,0:T(8,128)S(1)}, f32[2,9,16,96]{3,2,1,0:T(8,128)S(1)}, u32[]{:S(2)}, u32[]{:S(2)}) %collective-permute-start.10) | collective-permute-done | bytes 110624 | tf_op jit(solution)/shard_map/ppermute | solution.py:306
  89.4 2.0 %collective-permute-start.11 = (f32[2,9,16,96]{3,2,1,0:T(8,128)S(1)}, f32[2,9,16,96]{3,2,1,0:T(8,128)S(1)}, u32[]{:S(2)}, u32[]{:S(2)}) collective-permute-start(f32[2,9,16,96]{3,2,1,0:T(8,128)S(1)} %fusion), channel_id=1, source_target_pairs={{0,2},{2,0},{4,6},{6,4},{8,10},{10,8},{12,14},{14,12},{16,18},{18,... | collective-permute-start | bytes 331784 | tf_op jit(solution)/shard_map/ppermute | solution.py:285
  91.5 4.0 %collective-permute-done.12 = f32[2,9,16,96]{3,2,1,0:T(8,128)S(1)} collective-permute-done((f32[2,9,16,96]{3,2,1,0:T(8,128)S(1)}, f32[2,9,16,96]{3,2,1,0:T(8,128)S(1)}, u32[]{:S(2)}, u32[]{:S(2)}) %collective-permute-start.12) | collective-permute-done | bytes 110624 | tf_op jit(solution)/shard_map/ppermute | solution.py:285
  95.6 3.0 %collective-permute-start.16 = (f32[2,9,16,96]{3,2,1,0:T(8,128)S(1)}, f32[2,9,16,96]{3,2,1,0:T(8,128)S(1)}, u32[]{:S(2)}, u32[]{:S(2)}) collective-permute-start(f32[2,9,16,96]{3,2,1,0:T(8,128)S(1)} %add_add_fusion), channel_id=1, source_target_pairs={{0,24},{2,26},{4,28},{6,30},{8,16},{10,18},{12,20},{14,22},{16,8},... | collective-permute-start | bytes 331784 | tf_op jit(solution)/shard_map/ppermute | solution.py:285
  98.6 1.5 %collective-permute-start.14 = (f32[2,9,16,96]{3,2,1,0:T(8,128)S(1)}, f32[2,9,16,96]{3,2,1,0:T(8,128)S(1)}, u32[]{:S(2)}, u32[]{:S(2)}) collective-permute-start(f32[2,9,16,96]{3,2,1,0:T(8,128)S(1)} %add_add_fusion), channel_id=1, source_target_pairs={{0,8},{2,10},{4,12},{6,14},{8,0},{10,2},{12,4},{14,6},{16,24},{18,... | collective-permute-start | bytes 331784 | tf_op jit(solution)/shard_map/ppermute | solution.py:285
  100.0 0.1 maximum_bitcast_fusion.2
  100.2 0.5 copy.26
  100.7 0.3 reshape.58.refs_3_
  101.0 4.3 %shard_map.71 = (bf16[24,4,16,128]{3,2,1,0:T(8,128)(2,1)S(1)}, bf16[24,4,16,128]{3,2,1,0:T(8,128)(2,1)S(1)}) custom-call(bf16[26,2,32,128]{3,2,1,0:T(8,128)(2,1)S(1)} %get-tuple-element.34.refs_0_, bf16[26,2,32,128]{3,2,1,0:T(8,128)(2,1)S(1)} %get-tuple-element.35.refs_1_, bf16[26,2,32,128]{3,2,1,0:T(8,128)(2,1)S(1)} %get-tuple-element.36.refs_2_, ...), custom_call_target="tpu_custom_call" | custom-call | flops 679477248 | bytes 1572864 | tf_op jit(solution)/shard_map/pallas_call | solution.py:18
  105.3 0.1 collective-permute-start.9
  105.4 5.1 %collective-permute-done.15 = f32[2,9,16,96]{3,2,1,0:T(8,128)S(1)} collective-permute-done((f32[2,9,16,96]{3,2,1,0:T(8,128)S(1)}, f32[2,9,16,96]{3,2,1,0:T(8,128)S(1)}, u32[]{:S(2)}, u32[]{:S(2)}) %collective-permute-start.15) | collective-permute-done | bytes 110624 | tf_op jit(solution)/shard_map/ppermute | solution.py:285
  110.6 0.2 reshape.59
  110.8 0.1 fusion.2
  111.0 0.7 copy.28
  111.7 0.7 copy.27
  112.4 4.6 %collective-permute-done.9.refs_1_ = bf16[24,4,16,128]{3,2,1,0:T(8,128)(2,1)S(1)} collective-permute-done((bf16[24,4,16,128]{3,2,1,0:T(8,128)(2,1)S(1)}, bf16[24,4,16,128]{3,2,1,0:T(8,128)(2,1)S(1)}, u32[]{:S(2)}, u32[]{:S(2)}) %collective-permute-start.9) | collective-permute-done | bytes 393248 | tf_op jit(solution)/shard_map/ppermute | solution.py:306
  116.9 2.2 %shard_map.72 = bf16[16,4,48,128]{3,2,1,0:T(8,128)(2,1)} custom-call(bf16[24,4,16,128]{3,2,1,0:T(8,128)(2,1)S(1)} %get-tuple-element.37.refs_0_, bf16[24,4,16,128]{3,2,1,0:T(8,128)(2,1)S(1)} %collective-permute-done.9.refs_1_), custom_call_target="tpu_custom_call" | custom-call | bytes 1572864 | tf_op jit(solution)/shard_map/pallas_call | solution.py:18
  (77 shorter events, 0.8 us)
Async XLA Ops:
  0.6 17.4 %copy-start = (bf16[32,4,48,128]{3,2,1,0:T(8,128)(2,1)S(1)}, bf16[32,4,48,128]{3,2,1,0:T(8,128)(2,1)}, u32[]{:S(2)}) copy-start(bf16[32,4,48,128]{3,2,1,0:T(8,128)(2,1)} %x_ref.3) | copy-start | bytes 4718596
  2.4 18.8 %collective-permute-start.6 = (bf16[2,16,27,32]{3,1,2,0:T(8,128)(2,1)}, bf16[2,16,27,32]{3,1,2,0:T(8,128)(2,1)}, u32[]{:S(2)}, u32[]{:S(2)}) collective-permute-start(bf16[2,16,27,32]{3,1,2,0:T(8,128)(2,1)} %pad_maximum_fusion.1), channel_id=1, source_target_pairs={{0,1},{1,0},{2,3},{3,2},{4,5},{5,4},{6,7},{7,6},{8,9},{9,8},{10,11... | collective-permute-start | bytes 165896 | tf_op jit(solution)/shard_map/ppermute | solution.py:306
  5.4 1.1 copy-start.1
  9.3 30.0 %copy-start.2 = (bf16[32,2,16,128]{3,2,1,0:T(8,128)(2,1)}, bf16[32,2,16,128]{3,2,1,0:T(8,128)(2,1)S(1)}, u32[]{:S(2)}) copy-start(bf16[32,2,16,128]{3,2,1,0:T(8,128)(2,1)S(1)} %get-tuple-element.25.refs_2_.refs_9_) | copy-start | bytes 786436
  9.3 30.0 %copy-start.4 = (bf16[32,2,16,128]{3,2,1,0:T(8,128)(2,1)}, bf16[32,2,16,128]{3,2,1,0:T(8,128)(2,1)S(1)}, u32[]{:S(2)}) copy-start(bf16[32,2,16,128]{3,2,1,0:T(8,128)(2,1)S(1)} %get-tuple-element.23.refs_4_.refs_11_) | copy-start | bytes 786436
  9.3 15.8 %collective-permute-start.1 = (bf16[32,2,16,128]{3,2,1,0:T(8,128)(2,1)S(1)}, bf16[32,2,16,128]{3,2,1,0:T(8,128)(2,1)S(1)}, u32[]{:S(2)}, u32[]{:S(2)}) collective-permute-start(bf16[32,2,16,128]{3,2,1,0:T(8,128)(2,1)S(1)} %get-tuple-element.24), channel_id=1, source_target_pairs={{0,1},{1,0},{2,3},{3,2},{4,5},{5,4},{6,7},{7,6},{8,9},{9,8},{10,11... | collective-permute-start | bytes 786440 | tf_op jit(solution)/shard_map/ppermute | solution.py:306
  9.3 15.8 %collective-permute-start.3 = (bf16[32,2,16,128]{3,2,1,0:T(8,128)(2,1)}, bf16[32,2,16,128]{3,2,1,0:T(8,128)(2,1)S(1)}, u32[]{:S(2)}, u32[]{:S(2)}) collective-permute-start(bf16[32,2,16,128]{3,2,1,0:T(8,128)(2,1)} %get-tuple-element.26), channel_id=1, source_target_pairs={{0,1},{1,0},{2,3},{3,2},{4,5},{5,4},{6,7},{7,6},{8,9},{9,8},{10,11... | collective-permute-start | bytes 786440 | tf_op jit(solution)/shard_map/ppermute | solution.py:306
  11.3 25.1 %collective-permute-start = (bf16[32,2,16,128]{3,2,1,0:T(8,128)(2,1)S(1)}, bf16[32,2,16,128]{3,2,1,0:T(8,128)(2,1)S(1)}, u32[]{:S(2)}, u32[]{:S(2)}) collective-permute-start(bf16[32,2,16,128]{3,2,1,0:T(8,128)(2,1)S(1)} %get-tuple-element.23.refs_4_.refs_11_), channel_id=1, source_target_pairs={{0,2},{2,4},{4,6},{6,8},{8,10},{10,12},{12,14},{14,16},{16,18},{18... | collective-permute-start | bytes 786440 | tf_op jit(solution)/shard_map/ppermute | solution.py:309
  11.3 25.9 %collective-permute-start.4 = (bf16[32,2,16,128]{3,2,1,0:T(8,128)(2,1)S(1)}, bf16[32,2,16,128]{3,2,1,0:T(8,128)(2,1)S(1)}, u32[]{:S(2)}, u32[]{:S(2)}) collective-permute-start(bf16[32,2,16,128]{3,2,1,0:T(8,128)(2,1)S(1)} %get-tuple-element.25.refs_2_.refs_9_), channel_id=1, source_target_pairs={{2,0},{4,2},{6,4},{8,6},{10,8},{12,10},{14,12},{16,14},{18,16},{20... | collective-permute-start | bytes 786440 | tf_op jit(solution)/shard_map/ppermute | solution.py:312
  19.7 0.8 copy-start.25
  20.5 0.8 copy-start.27
  21.2 8.3 %copy-start.30 = (bf16[16,27,32]{2,0,1:T(8,128)(2,1)S(1)}, bf16[16,27,32]{2,0,1:T(8,128)(2,1)}, u32[]{:S(2)}) copy-start(bf16[16,27,32]{2,0,1:T(8,128)(2,1)} %param.6) | copy-start | bytes 82948
  25.0 6.3 %copy-start.6 = (bf16[32,2,16,128]{3,2,1,0:T(8,128)(2,1)}, bf16[32,2,16,128]{3,2,1,0:T(8,128)(2,1)S(1)}, u32[]{:S(2)}) copy-start(bf16[32,2,16,128]{3,2,1,0:T(8,128)(2,1)S(1)} %collective-permute-done.1.refs_5_.refs_12_) | copy-start | bytes 786436
  25.1 12.8 %collective-permute-start.2 = (bf16[32,2,16,128]{3,2,1,0:T(8,128)(2,1)S(1)}, bf16[32,2,16,128]{3,2,1,0:T(8,128)(2,1)S(1)}, u32[]{:S(2)}, u32[]{:S(2)}) collective-permute-start(bf16[32,2,16,128]{3,2,1,0:T(8,128)(2,1)S(1)} %collective-permute-done.1.refs_5_.refs_12_), channel_id=1, source_target_pairs={{0,2},{2,4},{4,6},{6,8},{8,10},{10,12},{12,14},{14,16},{16,18},{18... | collective-permute-start | bytes 786440 | tf_op jit(solution)/shard_map/ppermute | solution.py:309
  25.1 6.3 %copy-start.9 = (bf16[32,2,16,128]{3,2,1,0:T(8,128)(2,1)}, bf16[32,2,16,128]{3,2,1,0:T(8,128)(2,1)S(1)}, u32[]{:S(2)}) copy-start(bf16[32,2,16,128]{3,2,1,0:T(8,128)(2,1)S(1)} %collective-permute-done.3.refs_3_.refs_10_) | copy-start | bytes 786436
  25.1 13.4 %collective-permute-start.5 = (bf16[32,2,16,128]{3,2,1,0:T(8,128)(2,1)S(1)}, bf16[32,2,16,128]{3,2,1,0:T(8,128)(2,1)S(1)}, u32[]{:S(2)}, u32[]{:S(2)}) collective-permute-start(bf16[32,2,16,128]{3,2,1,0:T(8,128)(2,1)S(1)} %collective-permute-done.3.refs_3_.refs_10_), channel_id=1, source_target_pairs={{2,0},{4,2},{6,4},{8,6},{10,8},{12,10},{14,12},{16,14},{18,16},{20... | collective-permute-start | bytes 786440 | tf_op jit(solution)/shard_map/ppermute | solution.py:312
  36.4 0.7 copy-start.12
  37.2 0.7 copy-start.15
  37.9 0.7 copy-start.18
  38.6 0.7 copy-start.21
  39.3 1.0 copy-start.7
  40.2 0.9 copy-start.10
  41.2 0.9 copy-start.13
  42.1 0.9 copy-start.16
  43.1 0.9 copy-start.19
  44.0 0.9 copy-start.22
  45.0 0.9 copy-start.24
  45.9 1.0 copy-start.26
  46.9 1.0 copy-start.28
  60.0 13.0 %collective-permute-start.7 = (bf16[28,2,32,128]{3,2,1,0:T(8,128)(2,1)S(1)}, bf16[28,2,32,128]{3,2,1,0:T(8,128)(2,1)S(1)}, u32[]{:S(2)}, u32[]{:S(2)}) collective-permute-start(bf16[28,2,32,128]{3,2,1,0:T(8,128)(2,1)S(1)} %get-tuple-element.29.refs_2_.refs_4_), channel_id=1, source_target_pairs={{0,2},{2,4},{4,6},{6,8},{8,10},{10,12},{12,14},{14,16},{16,18},{18... | collective-permute-start | bytes 1376264 | tf_op jit(solution)/shard_map/ppermute | solution.py:309
  60.0 13.0 %collective-permute-start.8 = (bf16[28,2,32,128]{3,2,1,0:T(8,128)(2,1)S(1)}, bf16[28,2,32,128]{3,2,1,0:T(8,128)(2,1)}, u32[]{:S(2)}, u32[]{:S(2)}) collective-permute-start(bf16[28,2,32,128]{3,2,1,0:T(8,128)(2,1)S(1)} %get-tuple-element.30.refs_1_.refs_3_), channel_id=1, source_target_pairs={{2,0},{4,2},{6,4},{8,6},{10,8},{12,10},{14,12},{16,14},{18,16},{20... | collective-permute-start | bytes 1376264 | tf_op jit(solution)/shard_map/ppermute | solution.py:312
  68.5 4.5 %copy-start.3 = (bf16[32,2,16,128]{3,2,1,0:T(8,128)(2,1)S(1)}, bf16[32,2,16,128]{3,2,1,0:T(8,128)(2,1)}, u32[]{:S(2)}) copy-start(bf16[32,2,16,128]{3,2,1,0:T(8,128)(2,1)} %copy-done.2) | copy-start | bytes 786436
  68.5 4.5 %copy-start.5 = (bf16[32,2,16,128]{3,2,1,0:T(8,128)(2,1)S(1)}, bf16[32,2,16,128]{3,2,1,0:T(8,128)(2,1)}, u32[]{:S(2)}) copy-start(bf16[32,2,16,128]{3,2,1,0:T(8,128)(2,1)} %copy-done.4) | copy-start | bytes 786436
  68.5 4.5 %copy-start.8 = (bf16[32,2,16,128]{3,2,1,0:T(8,128)(2,1)S(1)}, bf16[32,2,16,128]{3,2,1,0:T(8,128)(2,1)}, u32[]{:S(2)}) copy-start(bf16[32,2,16,128]{3,2,1,0:T(8,128)(2,1)} %copy-done.6) | copy-start | bytes 786436
  68.5 4.5 %copy-start.11 = (bf16[32,2,16,128]{3,2,1,0:T(8,128)(2,1)S(1)}, bf16[32,2,16,128]{3,2,1,0:T(8,128)(2,1)}, u32[]{:S(2)}) copy-start(bf16[32,2,16,128]{3,2,1,0:T(8,128)(2,1)} %copy-done.9) | copy-start | bytes 786436
  68.5 4.5 %copy-start.14 = (bf16[32,2,16,128]{3,2,1,0:T(8,128)(2,1)S(1)}, bf16[32,2,16,128]{3,2,1,0:T(8,128)(2,1)}, u32[]{:S(2)}) copy-start(bf16[32,2,16,128]{3,2,1,0:T(8,128)(2,1)} %copy-done.12) | copy-start | bytes 786436
  68.5 4.5 %copy-start.17 = (bf16[32,2,16,128]{3,2,1,0:T(8,128)(2,1)S(1)}, bf16[32,2,16,128]{3,2,1,0:T(8,128)(2,1)}, u32[]{:S(2)}) copy-start(bf16[32,2,16,128]{3,2,1,0:T(8,128)(2,1)} %copy-done.15) | copy-start | bytes 786436
  68.6 4.5 %copy-start.20 = (bf16[32,2,16,128]{3,2,1,0:T(8,128)(2,1)S(1)}, bf16[32,2,16,128]{3,2,1,0:T(8,128)(2,1)}, u32[]{:S(2)}) copy-start(bf16[32,2,16,128]{3,2,1,0:T(8,128)(2,1)} %copy-done.18) | copy-start | bytes 786436
  68.6 4.5 %copy-start.23 = (bf16[32,2,16,128]{3,2,1,0:T(8,128)(2,1)S(1)}, bf16[32,2,16,128]{3,2,1,0:T(8,128)(2,1)}, u32[]{:S(2)}) copy-start(bf16[32,2,16,128]{3,2,1,0:T(8,128)(2,1)} %copy-done.21) | copy-start | bytes 786436
  73.1 11.0 %copy-start.29 = (bf16[32,3,3,3,32]{4,0,3,2,1:T(8,128)(2,1)S(1)}, bf16[32,3,3,3,32]{4,0,3,2,1:T(8,128)(2,1)}, u32[]{:S(2)}) copy-start(bf16[32,3,3,3,32]{4,0,3,2,1:T(8,128)(2,1)} %pad_maximum_fusion.2) | copy-start | bytes 165892
  84.0 5.2 %collective-permute-start.10 = (f32[2,9,16,96]{3,2,1,0:T(8,128)S(1)}, f32[2,9,16,96]{3,2,1,0:T(8,128)S(1)}, u32[]{:S(2)}, u32[]{:S(2)}) collective-permute-start(f32[2,9,16,96]{3,2,1,0:T(8,128)S(1)} %pad_maximum_fusion.3), channel_id=1, source_target_pairs={{0,1},{1,0},{2,3},{3,2},{4,5},{5,4},{6,7},{7,6},{8,9},{9,8},{10,11... | collective-permute-start | bytes 331784 | tf_op jit(solution)/shard_map/ppermute | solution.py:306
  89.2 6.3 %collective-permute-start.12 = (f32[2,9,16,96]{3,2,1,0:T(8,128)S(1)}, f32[2,9,16,96]{3,2,1,0:T(8,128)S(1)}, u32[]{:S(2)}, u32[]{:S(2)}) collective-permute-start(f32[2,9,16,96]{3,2,1,0:T(8,128)S(1)} %fusion), channel_id=1, source_target_pairs={{0,4},{2,6},{4,0},{6,2},{8,12},{10,14},{12,8},{14,10},{16,20},{18,... | collective-permute-start | bytes 331784 | tf_op jit(solution)/shard_map/ppermute | solution.py:285
  89.3 6.2 %collective-permute-start.13 = (f32[2,9,16,96]{3,2,1,0:T(8,128)S(1)}, f32[2,9,16,96]{3,2,1,0:T(8,128)S(1)}, u32[]{:S(2)}, u32[]{:S(2)}) collective-permute-start(f32[2,9,16,96]{3,2,1,0:T(8,128)S(1)} %fusion), channel_id=1, source_target_pairs={{0,6},{2,4},{4,2},{6,0},{8,14},{10,12},{12,10},{14,8},{16,22},{18,... | collective-permute-start | bytes 331784 | tf_op jit(solution)/shard_map/ppermute | solution.py:285
  89.4 6.1 %collective-permute-start.11 = (f32[2,9,16,96]{3,2,1,0:T(8,128)S(1)}, f32[2,9,16,96]{3,2,1,0:T(8,128)S(1)}, u32[]{:S(2)}, u32[]{:S(2)}) collective-permute-start(f32[2,9,16,96]{3,2,1,0:T(8,128)S(1)} %fusion), channel_id=1, source_target_pairs={{0,2},{2,0},{4,6},{6,4},{8,10},{10,8},{12,14},{14,12},{16,18},{18,... | collective-permute-start | bytes 331784 | tf_op jit(solution)/shard_map/ppermute | solution.py:285
  95.6 9.8 %collective-permute-start.16 = (f32[2,9,16,96]{3,2,1,0:T(8,128)S(1)}, f32[2,9,16,96]{3,2,1,0:T(8,128)S(1)}, u32[]{:S(2)}, u32[]{:S(2)}) collective-permute-start(f32[2,9,16,96]{3,2,1,0:T(8,128)S(1)} %add_add_fusion), channel_id=1, source_target_pairs={{0,24},{2,26},{4,28},{6,30},{8,16},{10,18},{12,20},{14,22},{16,8},... | collective-permute-start | bytes 331784 | tf_op jit(solution)/shard_map/ppermute | solution.py:285
  98.5 12.0 %collective-permute-start.15 = (f32[2,9,16,96]{3,2,1,0:T(8,128)S(1)}, f32[2,9,16,96]{3,2,1,0:T(8,128)S(1)}, u32[]{:S(2)}, u32[]{:S(2)}) collective-permute-start(f32[2,9,16,96]{3,2,1,0:T(8,128)S(1)} %add_add_fusion), channel_id=1, source_target_pairs={{0,16},{2,18},{4,20},{6,22},{8,24},{10,26},{12,28},{14,30},{16,0},... | collective-permute-start | bytes 331784 | tf_op jit(solution)/shard_map/ppermute | solution.py:285
  98.6 12.0 %collective-permute-start.14 = (f32[2,9,16,96]{3,2,1,0:T(8,128)S(1)}, f32[2,9,16,96]{3,2,1,0:T(8,128)S(1)}, u32[]{:S(2)}, u32[]{:S(2)}) collective-permute-start(f32[2,9,16,96]{3,2,1,0:T(8,128)S(1)} %add_add_fusion), channel_id=1, source_target_pairs={{0,8},{2,10},{4,12},{6,14},{8,0},{10,2},{12,4},{14,6},{16,24},{18,... | collective-permute-start | bytes 331784 | tf_op jit(solution)/shard_map/ppermute | solution.py:285
  105.3 11.6 %collective-permute-start.9 = (bf16[24,4,16,128]{3,2,1,0:T(8,128)(2,1)S(1)}, bf16[24,4,16,128]{3,2,1,0:T(8,128)(2,1)S(1)}, u32[]{:S(2)}, u32[]{:S(2)}) collective-permute-start(bf16[24,4,16,128]{3,2,1,0:T(8,128)(2,1)S(1)} %get-tuple-element.38), channel_id=1, source_target_pairs={{0,1},{1,0},{2,3},{3,2},{4,5},{5,4},{6,7},{7,6},{8,9},{9,8},{10,11... | collective-permute-start | bytes 1179656 | tf_op jit(solution)/shard_map/ppermute | solution.py:306

commit v2 on v1

v2 whole, which is shorter than its diff:
```python
import functools
import math

import jax
import jax.numpy as jnp
from jax import lax
from jax.experimental import pallas as pl
from jax.experimental.pallas import tpu as pltpu
from jax.sharding import PartitionSpec as P

F32 = jnp.float32
BF16 = jnp.bfloat16
LIMIT = 16 * 1024 * 1024


def call(kernel, outs, args, scratch=(), flops=0, moved=0):
    whole = pl.BlockSpec(memory_space=pltpu.VMEM)
    return pl.pallas_call(
        kernel,
        out_shape=outs,
        in_specs=[whole] * len(args),
        out_specs=[whole] * len(outs),
        scratch_shapes=list(scratch),
        compiler_params=pltpu.CompilerParams(vmem_limit_bytes=LIMIT),
        cost_estimate=pl.CostEstimate(flops=flops, bytes_accessed=moved, transcendentals=0),
    )(*args)


def widened(x_ref, wide):
    count, planes, rows = x_ref.shape[:3]

    def widen(i, _):
        for x in range(planes):
            start = pl.multiple_of((i * planes + x) * rows, 8)
            wide[pl.ds(start, rows), :] = x_ref[i, x].astype(F32)
        return 0

    lax.fori_loop(0, count, widen, 0)


def turn(wide, outs, shape, base, length):
    count, planes, rows = shape

    def one(f, _):
        y = lax.rem(base + f, rows)
        for x in range(planes):
            tile = wide[pl.ds(x * rows + y, count, stride=planes * rows), :]
            outs[x // 2][f, x % 2] = tile.astype(BF16)
        return 0

    lax.fori_loop(0, length, one, 0)


def field_kernel(extent, margin, x_ref, first, second, *refs):
    outs, packed, wide = refs[:-2], refs[-2], refs[-1]
    count, planes, rows = x_ref.shape[:3]
    pairs = planes // 2
    share = rows // extent
    widened(x_ref, wide)
    me = lax.axis_index("chan")
    for s in range(extent):
        base = lax.rem(me + s, extent) * share - margin + rows
        turn(
            wide,
            outs[s * pairs : (s + 1) * pairs],
            (count, planes, rows),
            base,
            share + 2 * margin,
        )
    blank = jnp.zeros(first.shape[1:], F32)
    for h in range(packed.shape[0]):
        parts = []
        for ref in (first, second):
            for t in (2 * h, 2 * h + 1):
                parts.append(ref[t].astype(F32) if t < ref.shape[0] else blank)
        packed[h] = jnp.concatenate(parts, axis=1).astype(BF16)


def grad_kernel(extent, margin, x_ref, *refs):
    outs, wide = refs[:-1], refs[-1]
    count, planes, rows = x_ref.shape[:3]
    share = rows // extent
    widened(x_ref, wide)
    base = lax.axis_index("chan") * share - margin + rows
    turn(wide, outs, (count, planes, rows), base, share + 2 * margin)


def matrix_kernel(extent, *refs):
    packs, outs = refs[:extent], refs[extent:]
    me = lax.axis_index("chan")
    halves = packs[0].shape[0]
    quarter = packs[0].shape[2] // 4
    taps = []
    turned = []
    for h in range(halves):
        tiles = [pack[h].astype(F32) for pack in packs]
        own = jnp.concatenate(tiles, axis=0)
        fixed = []
        for g in range(extent):
            place = lax.rem(me + extent - g, extent)
            tile = tiles[0]
            for j in range(1, extent):
                tile = jnp.where(place == j, tiles[j], tile)
            fixed.append(tile)
        both = jnp.concatenate(
            [own[:, : 2 * quarter], jnp.concatenate(fixed, axis=0)[:, 2 * quarter :]], axis=1
        )
        across = both.T
        for side in range(2):
            taps.append(
                [both[:, k * quarter : (k + 1) * quarter] for k in (side, side + 2)]
            )
            turned.append(
                [across[k * quarter : (k + 1) * quarter] for k in (side, side + 2)]
            )
    channels = quarter
    blank = jnp.zeros((channels, channels), F32)
    for k in range(2):
        for out, blocks, flip in ((outs[k], turned, False), (outs[2 + k], taps, True)):
            for e in range(3):
                for x in range(2):
                    chunks = []
                    for pair in range(2):
                        for b in range(3):
                            for side in range(2):
                                a = 2 * pair + side - x
                                t = 9 * a + 3 * b + e
                                inside = 0 <= a <= 2
                                t = 26 - t if flip else t
                                chunks.append(blocks[t][k] if inside else blank)
                    low = (2 * e + x) * channels
                    out[low : low + channels, :] = jnp.concatenate(chunks, axis=1).astype(BF16)


def stacked(refs, row, count):
    if len(refs) == 1:
        part = refs[0][pl.ds(row, count)]
        return part.reshape(-1, part.shape[-1])
    parts = [ref[row + b, x] for b in range(count) for x in range(2) for ref in refs]
    return jnp.concatenate(parts, axis=0)


def taps(weight, pairs, row):
    sides = []
    for p in range(len(pairs) - 1):
        for q in range(2):
            above = stacked(pairs[p], row + q, 3)
            below = stacked(pairs[p + 1], row + q, 3)
            sides.append(jnp.concatenate([above, below], axis=0))
    lifted = jnp.dot(weight, jnp.concatenate(sides, axis=1), preferred_element_type=F32)
    third = lifted.shape[0] // 3
    depth = sides[0].shape[1]
    sums = []
    for k in range(len(sides)):
        side = lifted[:, k * depth : (k + 1) * depth]
        sums.append(
            side[third : 2 * third]
            + pltpu.roll(side[:third], 1, 1)
            + pltpu.roll(side[2 * third :], depth - 1, 1)
        )
    return [sums[2 * p : 2 * p + 2] for p in range(len(pairs) - 1)]


def silu_parts(v):
    sig = jax.nn.sigmoid(v)
    return sig, sig * (1.0 + v * (1.0 - sig))


def forward_kernel(groups, pairs, *refs):
    refs = list(refs)
    fields = [[refs.pop(0) for _ in range(groups)] for _ in range(pairs + 2)]
    grads = [refs.pop(0) for _ in range(pairs)]
    first, second = refs.pop(0), refs.pop(0)
    hiddens = [refs.pop(0) for _ in range(pairs + 1)]
    slopes = [refs.pop(0) for _ in range(pairs + 1)]
    deltas = [refs.pop(0) for _ in range(pairs)]

    def one(r, _):
        row = 2 * r
        for p, sums in enumerate(taps(first[...], fields, row)):
            for q, v in enumerate(sums):
                sig, slope = silu_parts(v)
                shape = hiddens[p].shape[1:]
                hiddens[p][row + q] = (v * sig).astype(BF16).reshape(shape)
                slopes[p][row + q] = slope.astype(BF16).reshape(shape)
        return 0

    lax.fori_loop(0, hiddens[0].shape[0] // 2, one, 0)

    def two(r, _):
        row = 2 * r
        for p, sums in enumerate(taps(second[...], [[ref] for ref in hiddens], row)):
            for q, v in enumerate(sums):
                shape = deltas[p].shape[1:]
                out_grad = grads[p][row + q].astype(F32)
                slope = silu_parts(v)[1].reshape(shape)
                deltas[p][row + q] = (out_grad * slope).astype(BF16)
        return 0

    lax.fori_loop(0, deltas[0].shape[0] // 2, two, 0)


def planes_of(pairs):
    return [(refs, x) for refs in pairs for x in range(2)]


def weight_loop(total, pieces, first_row, deltas, delta_row, count):
    total[...] = jnp.zeros_like(total)

    def step(r, _):
        left, right = [], []
        for x, ((delta,), place) in enumerate(deltas):
            rows = []
            for q in range(2):
                wide = delta[delta_row + 2 * r + q, place]
                plain = wide.astype(F32)
                depth = plain.shape[1]
                rows += [
                    pltpu.roll(plain, depth - 1, 1).astype(BF16),
                    wide,
                    pltpu.roll(plain, 1, 1).astype(BF16),
                ]
            left.append(jnp.concatenate(rows, axis=0))
            rows = []
            for refs, side in pieces[x : x + 3]:
                for b in range(4):
                    for ref in refs:
                        rows.append(ref[first_row + 2 * r + b, side])
            right.append(jnp.concatenate(rows, axis=0))
        total[...] += lax.dot_general(
            jnp.concatenate(left, axis=1),
            jnp.concatenate(right, axis=1),
            (((1,), (1,)), ((), ())),
            preferred_element_type=F32,
        )
        return 0

    lax.fori_loop(0, count // 2, step, 0)


def weight_fold(total, size):
    lanes = total.shape[0] // 2
    channels = total.shape[1] // 12
    upper, lower = total[:lanes, :].T, total[lanes:, :].T
    parts = []
    for g in range(channels // size):
        taps_of = []
        for a in range(3):
            for b in range(3):
                start = (4 * a + b) * channels + g * size
                taps_of.append(
                    upper[start : start + size]
                    + lower[start + channels : start + channels + size]
                )
        parts.append(taps_of)
    return parts


def second_kernel(share, pairs, *refs):
    refs = list(refs)
    hiddens = [[refs.pop(0)] for _ in range(pairs + 1)]
    deltas = [refs.pop(0) for _ in range(pairs)]
    raw, total = refs
    weight_loop(total, planes_of(hiddens), 2, planes_of([[d] for d in deltas]), 2, share)
    for g, taps_of in enumerate(weight_fold(total, raw.shape[2])):
        for t, part in enumerate(taps_of):
            raw[g, t] = part


def back_kernel(share, groups, pairs, *refs):
    refs = list(refs)
    deltas = [[refs.pop(0)] for _ in range(pairs + 2)]
    slopes = [refs.pop(0) for _ in range(pairs + 1)]
    fields = [[refs.pop(0) for _ in range(groups)] for _ in range(pairs + 2)]
    weight, second = refs.pop(0), refs.pop(0)
    firsts = [refs.pop(0) for _ in range(pairs + 1)]
    keep, send, total = refs

    def one(r, _):
        row = 2 * r
        for p, sums in enumerate(taps(weight[...], deltas, row)):
            for q, v in enumerate(sums):
                shape = firsts[p].shape[1:]
                slope = slopes[p][row + 2 + q].astype(F32)
                firsts[p][row + q] = (v.reshape(shape) * slope).astype(BF16)
        return 0

    lax.fori_loop(0, firsts[0].shape[0] // 2, one, 0)
    near = planes_of(fields)[1:-1]
    own = planes_of([[first] for first in firsts])[1:-1]
    weight_loop(total, near, 3, own, 1, share)
    parts = weight_fold(total, keep.shape[2])
    extent = keep.shape[0]
    me = lax.axis_index("chan")
    odd = lax.rem(lax.axis_index("slab"), 2)

    def place(ours, theirs):
        for g, taps_of in enumerate(parts):
            there = lax.rem(me + extent - g, extent)
            for t, part in enumerate(taps_of):
                ours[g, t] = part
                theirs[g, t] = second[there, t]

    @pl.when(odd == 0)
    def _():
        place(keep, send)

    @pl.when(odd == 1)
    def _():
        place(send, keep)


def last_kernel(pairs, *refs):
    refs = list(refs)
    firsts = [refs.pop(0) for _ in range(pairs + 1)]
    weight = refs.pop(0)
    outs = refs

    def one(r, _):
        row = 2 * r
        size = outs[0].shape[2]
        channels = len(outs) * size
        for p, sums in enumerate(taps(weight[...], [[first] for first in firsts], row)):
            for q, v in enumerate(sums):
                for x in range(2):
                    for j, out in enumerate(outs):
                        low = x * channels + j * size
                        out[row + q, 2 * p + x] = v[low : low + size].astype(BF16)
        return 0

    lax.fori_loop(0, outs[0].shape[0] // 2, one, 0)


def merge_kernel(extent, *refs):
    pieces, out, wide = refs[:-2], refs[-2], refs[-1]
    share, planes, size = pieces[0].shape[:3]
    rows = out.shape[2]
    me = lax.axis_index("chan")
    for j, piece in enumerate(pieces):
        base = lax.rem(me + extent - j, extent) * share

        def widen(f, _, piece=piece, base=base):
            for x in range(planes):
                start = ((base + f) * planes + x) * size
                start = pl.multiple_of(start, 8) if size % 8 == 0 else start
                wide[pl.ds(start, size), :] = piece[f, x].astype(F32)
            return 0

        lax.fori_loop(0, share, widen, 0)

    def turn(i, _):
        for x in range(planes):
            tile = wide[pl.ds(x * size + i, rows, stride=planes * size), :]
            out[i, x] = tile.astype(BF16)
        return 0

    lax.fori_loop(0, size, turn, 0)


def pair_sum(values, axis, stride):
    count = lax.axis_size(axis)
    return values + lax.ppermute(values, axis, [(i, i ^ stride) for i in range(count)])


def body(field, out_grad, first_weight, second_weight):
    extent = lax.axis_size("chan")
    slabs = lax.axis_size("slab")
    me = lax.axis_index("chan")
    size, planes, rows, depth = field.shape
    channels = size * extent
    pairs = planes // 2
    share = rows // extent
    factor = 1.0 / math.sqrt(planes * slabs * rows * depth)

    def to_chan(value, shift):
        return lax.ppermute(value, "chan", [(i, (i + shift) % extent) for i in range(extent)])

    def to_next(value):
        return lax.ppermute(value, "slab", [(i, (i + 1) % slabs) for i in range(slabs)])

    def to_prev(value):
        return lax.ppermute(value, "slab", [((i + 1) % slabs, i) for i in range(slabs)])

    piece = jax.ShapeDtypeStruct((share + 8, 2, size, depth), BF16)
    halves = 14
    made = call(
        functools.partial(field_kernel, extent, 4),
        [piece] * (extent * pairs) + [jax.ShapeDtypeStruct((halves, size, 4 * channels), BF16)],
        [field, jnp.transpose(first_weight, (1, 0, 2)), jnp.transpose(second_weight, (1, 0, 2))],
        [pltpu.VMEM((size * planes * rows, depth), F32)],
        moved=field.size * 6,
    )
    parts = [made[:pairs]]
    for j in range(1, extent):
        parts.append([to_chan(piece, j) for piece in made[j * pairs : (j + 1) * pairs]])
    packs = [made[-1]] + [to_chan(made[-1], j) for j in range(1, extent)]
    by_pair = [[parts[j][p] for j in range(extent)] for p in range(pairs)]
    groups = extent
    if size % 16 != 0:
        by_pair = [[jnp.concatenate(pieces, axis=2)] for pieces in by_pair]
        groups = 1
    before = [to_next(piece) for piece in by_pair[-1]]
    after = [to_prev(piece) for piece in by_pair[0]]
    fields = [before] + by_pair + [after]
    matrix = jax.ShapeDtypeStruct((6 * channels, 12 * channels), BF16)
    first_wide, second_wide, first_back, second_back = call(
        functools.partial(matrix_kernel, extent), [matrix] * 4, packs, moved=matrix.size * 8
    )
    grad_piece = jax.ShapeDtypeStruct((share + 4, 2, channels, depth), BF16)
    grads = call(
        functools.partial(grad_kernel, extent, 2),
        [grad_piece] * pairs,
        [out_grad],
        [pltpu.VMEM((channels * planes * rows, depth), F32)],
        moved=out_grad.size * 4,
    )

    def many(count, rows_each, dtype=BF16):
        return [jax.ShapeDtypeStruct((rows_each, 2, channels, depth), dtype)] * count

    flat_fields = [piece for pieces in fields for piece in pieces]
    work = 2 * 27 * channels * channels * depth
    made = call(
        functools.partial(forward_kernel, groups, pairs),
        many(pairs + 1, share + 6) * 2 + many(pairs, share + 4),
        flat_fields + list(grads) + [first_wide, second_wide],
        flops=work * 2 * planes * share,
        moved=8 * planes * share * channels * depth,
    )
    hiddens = made[: pairs + 1]
    slopes = made[pairs + 1 : 2 * pairs + 2]
    deltas = made[2 * pairs + 2 :]
    all_deltas = [to_next(deltas[-1])] + list(deltas) + [to_prev(deltas[0])]

    raw = jax.ShapeDtypeStruct((extent, 9, size, 3 * channels), F32)
    total = pltpu.VMEM((6 * channels, 12 * channels), F32)
    (second_raw,) = call(
        functools.partial(second_kernel, share, pairs),
        [raw],
        list(hiddens) + list(deltas),
        [total],
        flops=work * planes * share,
        moved=8 * planes * share * channels * depth,
    )
    made = call(
        functools.partial(back_kernel, share, groups, pairs),
        many(pairs + 1, share + 2) + [raw] * 2,
        all_deltas + list(slopes) + flat_fields + [second_back, second_raw],
        [total],
        flops=work * 2 * planes * share,
        moved=8 * planes * share * channels * depth,
    )
    firsts, keep, send = made[:-2], made[-2], made[-1]

    if slabs & (slabs - 1) == 0 and slabs > 1:
        keep = keep + lax.ppermute(send, "slab", [(i, i ^ 1) for i in range(slabs)])
        mine = keep[0]
        for j in range(1, extent):
            mine = mine + to_chan(keep[j], extent - j)
        stride = 2
        while stride < slabs:
            mine = pair_sum(mine, "slab", stride)
            stride *= 2
        mine = mine * factor
        other = lax.ppermute(mine, "slab", [(i, i ^ 1) for i in range(slabs)])
    else:
        mine, other = keep[0], send[0]
        for j in range(1, extent):
            mine, other = mine + to_chan(keep[j], extent - j), other + to_chan(send[j], extent - j)
        even = lax.rem(lax.axis_index("slab"), 2) == 0
        mine, other = jnp.where(even, mine, other), jnp.where(even, other, mine)
        mine, other = lax.psum((mine, other), "slab")
        mine, other = mine * factor, other * factor
        mine, other = jnp.where(even, mine, other), jnp.where(even, other, mine)
    even = lax.rem(lax.axis_index("slab"), 2) == 0

    def laid(value):
        taps_first = jnp.transpose(value.reshape(9, size, 3, channels), (0, 2, 1, 3))
        return jnp.transpose(taps_first.reshape(27, size, channels), (1, 0, 2))

    first_grad = laid(jnp.where(even, mine, other))
    second_grad = laid(jnp.where(even, other, mine))

    out_piece = jax.ShapeDtypeStruct((share, planes, size, depth), BF16)
    made = call(
        functools.partial(last_kernel, pairs),
        [out_piece] * extent,
        list(firsts) + [first_back],
        flops=work * planes * share,
        moved=4 * planes * share * channels * depth,
    )
    pieces = [made[0]] + [None] * (extent - 1)
    for j in range(1, extent):
        pieces[extent - j] = to_chan(made[j], extent - j)
    (input_grad,) = call(
        functools.partial(merge_kernel, extent),
        [jax.ShapeDtypeStruct(field.shape, BF16)],
        pieces,
        [pltpu.VMEM((rows * planes * size, depth), F32)],
        moved=4 * field.size,
    )
    return input_grad, first_grad, second_grad


def solution(mesh):
    placed = (
        P("chan", "slab", None, None),
        P(None, "slab", None, None),
        P("chan", None, None),
        P("chan", None, None),
    )
    return jax.shard_map(
        body,
        mesh=mesh,
        in_specs=placed,
        out_specs=(P("chan", "slab", None, None), P("chan", None, None), P("chan", None, None)),
        check_vma=False,
    )
```

time: 120 us -> 100 us (0.83)
  local copies, waits for them, and re-layouts: 32.7 us -> 4.47 us
  waiting for transfers between devices: 18.8 us -> 34.4 us
  Pallas kernels: 38.2 us -> 35.6 us
  starting transfers between devices: 25.2 us -> 23.4 us
  other arithmetic: 3.2 us -> 1.5 us
    unnamed x62 -> x8, local copies, waits for them, and re-layouts: 14.2 us -> 4.33 us
    ppermute x5, waiting for transfers between devices: 9.65 us -> 18.8 us  [to_chan(): lax.ppermute(value, 'chan', [(i, (i + shift) % extent) for i in range(ext...]
    transpose x9 -> x0, local copies, waits for them, and re-layouts: 4.95 us -> none  [the longest x4 3.6 us: wide_columns(): jnp.transpose(split, (0, 1, 2, 3, 6, 5, 4, 7))]
    reshape x6 -> x0, local copies, waits for them, and re-layouts: 4.74 us -> none  [the longest x5 4.49 us: wide_columns(): jnp.transpose(split, (0, 1, 2, 3, 6, 5, 4, 7))]
    ppermute x6 -> x5, waiting for transfers between devices: 9.15 us -> 13.4 us  [the longest x3 12.4 us: pair_sum(): lax.ppermute(values, axis, [(i, i ^ stride) for i in range(count)])]
    ppermute x6 -> x5, starting transfers between devices: 6.64 us -> 3.35 us  [the longest x3 2.59 us: pair_sum(): lax.ppermute(values, axis, [(i, i ^ stride) for i in range(count)])]
    dynamic_update_slice x2 -> x0, local copies, waits for them, and re-layouts: 3.16 us -> none  [body(): second_all = lax.dynamic_update_slice(second_all, part[1], (place, 0, 0))]
    pallas_call x7 -> x8, Pallas kernels: 38.2 us -> 35.6 us  [call(): pl.pallas_call(kernel, out_shape=outs, in_specs=[whole] * len(args), out_...]
  transfers between devices with their start and end apart: 17 -> 16, of which waited for: 4 -> 9; matrix products, arithmetic and copies ran while one was open for 17% -> 2% of each run, Pallas kernels for 11% -> 11%
where the time goes in v2:
time: 100 us
  Pallas kernels  35.6 us (36%)
  waiting for transfers between devices  34.4 us (34%)
  starting transfers between devices  23.4 us (23%)
  local copies, waits for them, and re-layouts  4.47 us (4%)
  other arithmetic  1.5 us (2%)
    pallas_call x8, Pallas kernels, call(): pl.pallas_call(kernel, out_shape=outs, in_specs=[whole] * len(args), out_...  35.6 us
    ppermute x5, waiting for transfers between devices, to_chan(): lax.ppermute(value, 'chan', [(i, (i + shift) % extent) for i in range(ext...  18.8 us
    ppermute x3, waiting for transfers between devices, pair_sum(): lax.ppermute(values, axis, [(i, i ^ stride) for i in range(count)])  12.4 us
    ppermute x3, starting transfers between devices, to_prev(): lax.ppermute(value, 'slab', [((i + 1) % slabs, i) for i in range(slabs)])  12.2 us
    ppermute x5, starting transfers between devices, to_chan(): lax.ppermute(value, 'chan', [(i, (i + shift) % extent) for i in range(ext...  7.75 us
    unnamed x8, local copies, waits for them, and re-layouts  4.33 us
    ppermute x3, starting transfers between devices, pair_sum(): lax.ppermute(values, axis, [(i, i ^ stride) for i in range(count)])  2.59 us
    ppermute x3, waiting for transfers between devices, to_next(): lax.ppermute(value, 'slab', [(i, (i + 1) % slabs) for i in range(slabs)])  2.15 us
  transfers between devices with their start and end apart: 16, of which 9 were waited for; matrix products, arithmetic and copies ran while one was open for 2% of the time, Pallas kernels for 11%

profile of v2, /device:TPU:0, one launch (start us, length us, event | category | flops | bytes accessed | tf_op | source)
XLA Modules:
  0.0 100.1 jit_solution(16781109552289575477)
XLA Ops:
  0.6 0.0 copy-start.1
  0.6 1.1 %copy-done.1 = bf16[16,4,48,128]{3,2,1,0:T(8,128)(2,1)S(1)} copy-done((bf16[16,4,48,128]{3,2,1,0:T(8,128)(2,1)S(1)}, bf16[16,4,48,128]{3,2,1,0:T(8,128)(2,1)}, u32[]{:S(2)}) %copy-start.1) | copy-done | bytes 786456
  1.8 0.0 copy-start.2
  1.8 0.9 copy-done.2
  2.7 0.0 copy-start.3
  2.7 0.9 copy-done.3
  3.6 2.2 %shard_map.67 = (bf16[32,2,16,128]{3,2,1,0:T(8,128)(2,1)S(1)}, bf16[32,2,16,128]{3,2,1,0:T(8,128)(2,1)S(1)}, bf16[32,2,16,128]{3,2,1,0:T(8,128)(2,1)S(1)}, bf16[...) custom-call(bf16[16,4,48,128]{3,2,1,0:T(8,128)(2,1)S(1)} %copy-done.1, bf16[27,16,32]{2,1,0:T(8,128)(2,1)S(1)} %bitcast.14, ...), custom_call_target="tpu_custom_call" | custom-call | bytes 2359296 | tf_op jit(solution)/shard_map/pallas_call | solution.py:18
  5.7 3.0 %collective-permute-start.1 = (bf16[32,2,16,128]{3,2,1,0:T(8,128)(2,1)S(1)}, bf16[32,2,16,128]{3,2,1,0:T(8,128)(2,1)S(1)}, u32[]{:S(2)}, u32[]{:S(2)}) collective-permute-start(bf16[32,2,16,128]{3,2,1,0:T(8,128)(2,1)S(1)} %get-tuple-element.30), channel_id=1, source_target_pairs={{0,1},{1,0},{2,3},{3,2},{4,5},{5,4},{6,7},{7,6},{8,9},{9,8},{10,11... | collective-permute-start | bytes 786440 | tf_op jit(solution)/shard_map/ppermute | solution.py:376
  8.7 0.1 collective-permute-start.3
  8.8 0.0 collective-permute-start
  8.8 4.4 %collective-permute-start.4 = (bf16[32,2,16,128]{3,2,1,0:T(8,128)(2,1)S(1)}, bf16[32,2,16,128]{3,2,1,0:T(8,128)(2,1)S(1)}, u32[]{:S(2)}, u32[]{:S(2)}) collective-permute-start(bf16[32,2,16,128]{3,2,1,0:T(8,128)(2,1)S(1)} %get-tuple-element.31.refs_2_.refs_9_), channel_id=1, source_target_pairs={{2,0},{4,2},{6,4},{8,6},{10,8},{12,10},{14,12},{16,14},{18,16},{20... | collective-permute-start | bytes 786440 | tf_op jit(solution)/shard_map/ppermute | solution.py:382
  13.3 2.6 %collective-permute-done.1.refs_5_.refs_12_ = bf16[32,2,16,128]{3,2,1,0:T(8,128)(2,1)S(1)} collective-permute-done((bf16[32,2,16,128]{3,2,1,0:T(8,128)(2,1)S(1)}, bf16[32,2,16,128]{3,2,1,0:T(8,128)(2,1)S(1)}, u32[]{:S(2)}, u32[]{:S(2)}) %collective-permute-start.1) | collective-permute-done | bytes 262176 | tf_op jit(solution)/shard_map/ppermute | solution.py:376
  15.9 0.0 collective-permute-start.2
  15.9 4.8 %collective-permute-done.3.refs_3_.refs_10_ = bf16[32,2,16,128]{3,2,1,0:T(8,128)(2,1)S(1)} collective-permute-done((bf16[32,2,16,128]{3,2,1,0:T(8,128)(2,1)S(1)}, bf16[32,2,16,128]{3,2,1,0:T(8,128)(2,1)S(1)}, u32[]{:S(2)}, u32[]{:S(2)}) %collective-permute-start.3) | collective-permute-done | bytes 262176 | tf_op jit(solution)/shard_map/ppermute | solution.py:376
  20.7 3.4 %collective-permute-start.5 = (bf16[32,2,16,128]{3,2,1,0:T(8,128)(2,1)S(1)}, bf16[32,2,16,128]{3,2,1,0:T(8,128)(2,1)S(1)}, u32[]{:S(2)}, u32[]{:S(2)}) collective-permute-start(bf16[32,2,16,128]{3,2,1,0:T(8,128)(2,1)S(1)} %collective-permute-done.3.refs_3_.refs_10_), channel_id=1, source_target_pairs={{2,0},{4,2},{6,4},{8,6},{10,8},{12,10},{14,12},{16,14},{18,16},{20... | collective-permute-start | bytes 786440 | tf_op jit(solution)/shard_map/ppermute | solution.py:382
  24.0 1.5 %collective-permute-start.6 = (bf16[14,16,128]{2,1,0:T(8,128)(2,1)S(1)}, bf16[14,16,128]{2,1,0:T(8,128)(2,1)S(1)}, u32[]{:S(2)}, u32[]{:S(2)}) collective-permute-start(bf16[14,16,128]{2,1,0:T(8,128)(2,1)S(1)} %get-tuple-element.35.refs_0_), channel_id=1, source_target_pairs={{0,1},{1,0},{2,3},{3,2},{4,5},{5,4},{6,7},{7,6},{8,9},{9,8},{10,11... | collective-permute-start | bytes 172040 | tf_op jit(solution)/shard_map/ppermute | solution.py:376
  25.5 0.0 copy-start
  25.5 1.4 %copy-done = bf16[32,4,48,128]{3,2,1,0:T(8,128)(2,1)S(1)} copy-done((bf16[32,4,48,128]{3,2,1,0:T(8,128)(2,1)S(1)}, bf16[32,4,48,128]{3,2,1,0:T(8,128)(2,1)}, u32[]{:S(2)}) %copy-start) | copy-done | bytes 1572888
  26.9 1.7 %shard_map.68 = (bf16[28,2,32,128]{3,2,1,0:T(8,128)(2,1)S(1)}, bf16[28,2,32,128]{3,2,1,0:T(8,128)(2,1)S(1)}) custom-call(bf16[32,4,48,128]{3,2,1,0:T(8,128)(2,1)S(1)} %copy-done), custom_call_target="tpu_custom_call" | custom-call | bytes 3145728 | tf_op jit(solution)/shard_map/pallas_call | solution.py:18
  28.6 0.0 collective-permute-done.6.refs_1_
  28.6 0.5 shard_map.69
  29.1 0.0 collective-permute-done.refs_0_.refs_7_
  29.2 0.0 collective-permute-done.4.refs_6_.refs_13_
  29.2 0.0 collective-permute-done.2.refs_1_.refs_8_
  29.2 0.0 collective-permute-done.5.refs_7_.refs_14_
  29.2 11.4 %shard_map.70 = (bf16[30,2,32,128]{3,2,1,0:T(8,128)(2,1)S(1)}, bf16[30,2,32,128]{3,2,1,0:T(8,128)(2,1)S(1)}, bf16[30,2,32,128]{3,2,1,0:T(8,128)(2,1)S(1)}, bf16[...) custom-call(bf16[32,2,16,128]{3,2,1,0:T(8,128)(2,1)S(1)} %collective, ...), custom_call_target="tpu_custom_call" | custom-call | flops 1358954496 | bytes 3145728 | tf_op jit(solution)/shard_map/pallas_call | solution.py:18
  40.6 0.1 collective-permute-start.7
  40.7 4.4 %collective-permute-start.8 = (bf16[28,2,32,128]{3,2,1,0:T(8,128)(2,1)S(1)}, bf16[28,2,32,128]{3,2,1,0:T(8,128)(2,1)S(1)}, u32[]{:S(2)}, u32[]{:S(2)}) collective-permute-start(bf16[28,2,32,128]{3,2,1,0:T(8,128)(2,1)S(1)} %get-tuple-element.39.refs_3_.refs_1_), channel_id=1, source_target_pairs={{2,0},{4,2},{6,4},{8,6},{10,8},{12,10},{14,12},{16,14},{18,16},{20... | collective-permute-start | bytes 1376264 | tf_op jit(solution)/shard_map/ppermute | solution.py:382
  45.1 4.1 %shard_map.71.refs_16_ = f32[2,9,16,96]{3,2,1,0:T(8,128)S(1)} custom-call(bf16[30,2,32,128]{3,2,1,0:T(8,128)(2,1)S(1)} %get-tuple-element.44.refs_0_, bf16[30,2,32,128]{3,2,1,0:T(8,128)(2,1)S(1)} %get-tuple-element.45.refs_1_, bf16[30,2,32,128]{3,2,1,0:T(8,128)(2,1)S(1)} %get-tuple-element.46.refs_2_, ...), custom_call_target="tpu_custom_call" | custom-call | flops 679477248 | bytes 3145728 | tf_op jit(solution)/shard_map/pallas_call | solution.py:18
  49.2 2.1 %collective-permute-done.7.refs_0_ = bf16[28,2,32,128]{3,2,1,0:T(8,128)(2,1)S(1)} collective-permute-done((bf16[28,2,32,128]{3,2,1,0:T(8,128)(2,1)S(1)}, bf16[28,2,32,128]{3,2,1,0:T(8,128)(2,1)S(1)}, u32[]{:S(2)}, u32[]{:S(2)}) %collective-permute-start.7) | collective-permute-done | bytes 458784 | tf_op jit(solution)/shard_map/ppermute | solution.py:379
  51.4 0.0 collective-permute-done.8.refs_3_
  51.4 9.2 %shard_map.72 = (bf16[26,2,32,128]{3,2,1,0:T(8,128)(2,1)S(1)}, bf16[26,2,32,128]{3,2,1,0:T(8,128)(2,1)S(1)}, bf16[26,2,32,128]{3,2,1,0:T(8,128)(2,1)S(1)}, f32[2...) custom-call(bf16[28,2,32,128]{3,2,1,0:T(8,128)(2,1)S(1)} %collective-permute-done.7.refs_0_, ...), custom_call_target="tpu_custom_call" | custom-call | flops 1358954496 | bytes 3145728 | tf_op jit(solution)/shard_map/pallas_call | solution.py:18
  60.6 0.7 collective-permute-start.10
  61.3 1.0 %collective-permute-done.10 = f32[2,9,16,96]{3,2,1,0:T(8,128)S(1)} collective-permute-done((f32[2,9,16,96]{3,2,1,0:T(8,128)S(1)}, f32[2,9,16,96]{3,2,1,0:T(8,128)S(1)}, u32[]{:S(2)}, u32[]{:S(2)}) %collective-permute-start.10) | collective-permute-done | bytes 110624 | tf_op jit(solution)/shard_map/ppermute | solution.py:456
  62.3 1.8 %collective-permute-start.11 = (f32[9,16,96]{2,1,0:T(8,128)S(1)}, f32[9,16,96]{2,1,0:T(8,128)S(1)}, u32[]{:S(2)}, u32[]{:S(2)}) collective-permute-start(f32[9,16,96]{2,1,0:T(8,128)S(1)} %slice_bitcast_fusion), channel_id=1, source_target_pairs={{0,1},{1,0},{2,3},{3,2},{4,5},{5,4},{6,7},{7,6},{8,9},{9,8},{10,11... | collective-permute-start | bytes 165896 | tf_op jit(solution)/shard_map/ppermute | solution.py:376
  64.1 2.8 %collective-permute-done.11 = f32[9,16,96]{2,1,0:T(8,128)S(1)} collective-permute-done((f32[9,16,96]{2,1,0:T(8,128)S(1)}, f32[9,16,96]{2,1,0:T(8,128)S(1)}, u32[]{:S(2)}, u32[]{:S(2)}) %collective-permute-start.11) | collective-permute-done | bytes 55328 | tf_op jit(solution)/shard_map/ppermute | solution.py:376
  66.9 0.1 collective-permute-start.12
  67.1 4.3 %collective-permute-done.12 = f32[9,16,96]{2,1,0:T(8,128)S(1)} collective-permute-done((f32[9,16,96]{2,1,0:T(8,128)S(1)}, f32[9,16,96]{2,1,0:T(8,128)S(1)}, u32[]{:S(2)}, u32[]{:S(2)}) %collective-permute-start.12) | collective-permute-done | bytes 55328 | tf_op jit(solution)/shard_map/ppermute | solution.py:362
  71.4 0.7 collective-permute-start.13
  72.1 3.7 %collective-permute-done.13 = f32[9,16,96]{2,1,0:T(8,128)S(1)} collective-permute-done((f32[9,16,96]{2,1,0:T(8,128)S(1)}, f32[9,16,96]{2,1,0:T(8,128)S(1)}, u32[]{:S(2)}, u32[]{:S(2)}) %collective-permute-start.13) | collective-permute-done | bytes 55328 | tf_op jit(solution)/shard_map/ppermute | solution.py:362
  75.8 1.7 %collective-permute-start.14 = (f32[9,16,96]{2,1,0:T(8,128)S(1)}, f32[9,16,96]{2,1,0:T(8,128)S(1)}, u32[]{:S(2)}, u32[]{:S(2)}) collective-permute-start(f32[9,16,96]{2,1,0:T(8,128)S(1)} %add.18), channel_id=1, source_target_pairs={{0,16},{2,18},{4,20},{6,22},{8,24},{10,26},{12,28},{14,30},{16,0},... | collective-permute-start | bytes 165896 | tf_op jit(solution)/shard_map/ppermute | solution.py:362
  77.6 4.4 %collective-permute-done.14 = f32[9,16,96]{2,1,0:T(8,128)S(1)} collective-permute-done((f32[9,16,96]{2,1,0:T(8,128)S(1)}, f32[9,16,96]{2,1,0:T(8,128)S(1)}, u32[]{:S(2)}, u32[]{:S(2)}) %collective-permute-start.14) | collective-permute-done | bytes 55328 | tf_op jit(solution)/shard_map/ppermute | solution.py:362
  81.9 0.1 collective-permute-start.15
  82.0 4.3 %shard_map.73 = (bf16[24,4,16,128]{3,2,1,0:T(8,128)(2,1)S(1)}, bf16[24,4,16,128]{3,2,1,0:T(8,128)(2,1)S(1)}) custom-call(bf16[26,2,32,128]{3,2,1,0:T(8,128)(2,1)S(1)} %get-tuple-element.47.refs_0_, bf16[26,2,32,128]{3,2,1,0:T(8,128)(2,1)S(1)} %get-tuple-element.48.refs_1_, bf16[26,2,32,128]{3,2,1,0:T(8,128)(2,1)S(1)} %get-tuple-element.49.refs_2_, ...), custom_call_target="tpu_custom_call" | custom-call | flops 679477248 | bytes 1572864 | tf_op jit(solution)/shard_map/pallas_call | solution.py:18
  86.3 1.4 %collective-permute-start.9 = (bf16[24,4,16,128]{3,2,1,0:T(8,128)(2,1)S(1)}, bf16[24,4,16,128]{3,2,1,0:T(8,128)(2,1)S(1)}, u32[]{:S(2)}, u32[]{:S(2)}) collective-permute-start(bf16[24,4,16,128]{3,2,1,0:T(8,128)(2,1)S(1)} %get-tuple-element.52), channel_id=1, source_target_pairs={{0,1},{1,0},{2,3},{3,2},{4,5},{5,4},{6,7},{7,6},{8,9},{9,8},{10,11... | collective-permute-start | bytes 1179656 | tf_op jit(solution)/shard_map/ppermute | solution.py:376
  87.7 0.0 collective-permute-done.15
  87.7 0.1 fusion.1
  87.8 0.7 pad_maximum_fusion.1
  88.5 0.7 pad_maximum_fusion
  89.2 8.6 %collective-permute-done.9.refs_1_ = bf16[24,4,16,128]{3,2,1,0:T(8,128)(2,1)S(1)} collective-permute-done((bf16[24,4,16,128]{3,2,1,0:T(8,128)(2,1)S(1)}, bf16[24,4,16,128]{3,2,1,0:T(8,128)(2,1)S(1)}, u32[]{:S(2)}, u32[]{:S(2)}) %collective-permute-start.9) | collective-permute-done | bytes 393248 | tf_op jit(solution)/shard_map/ppermute | solution.py:376
  97.9 2.2 %shard_map.74 = bf16[16,4,48,128]{3,2,1,0:T(8,128)(2,1)} custom-call(bf16[24,4,16,128]{3,2,1,0:T(8,128)(2,1)S(1)} %get-tuple-element.51.refs_0_, bf16[24,4,16,128]{3,2,1,0:T(8,128)(2,1)S(1)} %collective-permute-done.9.refs_1_), custom_call_target="tpu_custom_call" | custom-call | bytes 1572864 | tf_op jit(solution)/shard_map/pallas_call | solution.py:18
  (7 shorter events, 0.1 us)
Async XLA Ops:
  0.6 1.1 %copy-start.1 = (bf16[16,4,48,128]{3,2,1,0:T(8,128)(2,1)S(1)}, bf16[16,4,48,128]{3,2,1,0:T(8,128)(2,1)}, u32[]{:S(2)}) copy-start(bf16[16,4,48,128]{3,2,1,0:T(8,128)(2,1)} %x_ref.2) | copy-start | bytes 2359300
  1.8 0.9 copy-start.2
  2.7 0.9 copy-start.3
  5.7 10.1 %collective-permute-start.1 = (bf16[32,2,16,128]{3,2,1,0:T(8,128)(2,1)S(1)}, bf16[32,2,16,128]{3,2,1,0:T(8,128)(2,1)S(1)}, u32[]{:S(2)}, u32[]{:S(2)}) collective-permute-start(bf16[32,2,16,128]{3,2,1,0:T(8,128)(2,1)S(1)} %get-tuple-element.30), channel_id=1, source_target_pairs={{0,1},{1,0},{2,3},{3,2},{4,5},{5,4},{6,7},{7,6},{8,9},{9,8},{10,11... | collective-permute-start | bytes 786440 | tf_op jit(solution)/shard_map/ppermute | solution.py:376
  8.7 11.9 %collective-permute-start.3 = (bf16[32,2,16,128]{3,2,1,0:T(8,128)(2,1)S(1)}, bf16[32,2,16,128]{3,2,1,0:T(8,128)(2,1)S(1)}, u32[]{:S(2)}, u32[]{:S(2)}) collective-permute-start(bf16[32,2,16,128]{3,2,1,0:T(8,128)(2,1)S(1)} %get-tuple-element.32), channel_id=1, source_target_pairs={{0,1},{1,0},{2,3},{3,2},{4,5},{5,4},{6,7},{7,6},{8,9},{9,8},{10,11... | collective-permute-start | bytes 786440 | tf_op jit(solution)/shard_map/ppermute | solution.py:376
  8.8 20.3 %collective-permute-start = (bf16[32,2,16,128]{3,2,1,0:T(8,128)(2,1)S(1)}, bf16[32,2,16,128]{3,2,1,0:T(8,128)(2,1)S(1)}, u32[]{:S(2)}, u32[]{:S(2)}) collective-permute-start(bf16[32,2,16,128]{3,2,1,0:T(8,128)(2,1)S(1)} %get-tuple-element.29.refs_4_.refs_11_), channel_id=1, source_target_pairs={{0,2},{2,4},{4,6},{6,8},{8,10},{10,12},{12,14},{14,16},{16,18},{18... | collective-permute-start | bytes 786440 | tf_op jit(solution)/shard_map/ppermute | solution.py:379
  8.8 20.3 %collective-permute-start.4 = (bf16[32,2,16,128]{3,2,1,0:T(8,128)(2,1)S(1)}, bf16[32,2,16,128]{3,2,1,0:T(8,128)(2,1)S(1)}, u32[]{:S(2)}, u32[]{:S(2)}) collective-permute-start(bf16[32,2,16,128]{3,2,1,0:T(8,128)(2,1)S(1)} %get-tuple-element.31.refs_2_.refs_9_), channel_id=1, source_target_pairs={{2,0},{4,2},{6,4},{8,6},{10,8},{12,10},{14,12},{16,14},{18,16},{20... | collective-permute-start | bytes 786440 | tf_op jit(solution)/shard_map/ppermute | solution.py:382
  15.9 13.3 %collective-permute-start.2 = (bf16[32,2,16,128]{3,2,1,0:T(8,128)(2,1)S(1)}, bf16[32,2,16,128]{3,2,1,0:T(8,128)(2,1)S(1)}, u32[]{:S(2)}, u32[]{:S(2)}) collective-permute-start(bf16[32,2,16,128]{3,2,1,0:T(8,128)(2,1)S(1)} %collective-permute-done.1.refs_5_.refs_12_), channel_id=1, source_target_pairs={{0,2},{2,4},{4,6},{6,8},{8,10},{10,12},{12,14},{14,16},{16,18},{18... | collective-permute-start | bytes 786440 | tf_op jit(solution)/shard_map/ppermute | solution.py:379
  20.7 8.5 %collective-permute-start.5 = (bf16[32,2,16,128]{3,2,1,0:T(8,128)(2,1)S(1)}, bf16[32,2,16,128]{3,2,1,0:T(8,128)(2,1)S(1)}, u32[]{:S(2)}, u32[]{:S(2)}) collective-permute-start(bf16[32,2,16,128]{3,2,1,0:T(8,128)(2,1)S(1)} %collective-permute-done.3.refs_3_.refs_10_), channel_id=1, source_target_pairs={{2,0},{4,2},{6,4},{8,6},{10,8},{12,10},{14,12},{16,14},{18,16},{20... | collective-permute-start | bytes 786440 | tf_op jit(solution)/shard_map/ppermute | solution.py:382
  24.0 4.6 %collective-permute-start.6 = (bf16[14,16,128]{2,1,0:T(8,128)(2,1)S(1)}, bf16[14,16,128]{2,1,0:T(8,128)(2,1)S(1)}, u32[]{:S(2)}, u32[]{:S(2)}) collective-permute-start(bf16[14,16,128]{2,1,0:T(8,128)(2,1)S(1)} %get-tuple-element.35.refs_0_), channel_id=1, source_target_pairs={{0,1},{1,0},{2,3},{3,2},{4,5},{5,4},{6,7},{7,6},{8,9},{9,8},{10,11... | collective-permute-start | bytes 172040 | tf_op jit(solution)/shard_map/ppermute | solution.py:376
  25.5 1.4 %copy-start = (bf16[32,4,48,128]{3,2,1,0:T(8,128)(2,1)S(1)}, bf16[32,4,48,128]{3,2,1,0:T(8,128)(2,1)}, u32[]{:S(2)}) copy-start(bf16[32,4,48,128]{3,2,1,0:T(8,128)(2,1)} %x_ref.3) | copy-start | bytes 4718596
  40.6 10.8 %collective-permute-start.7 = (bf16[28,2,32,128]{3,2,1,0:T(8,128)(2,1)S(1)}, bf16[28,2,32,128]{3,2,1,0:T(8,128)(2,1)S(1)}, u32[]{:S(2)}, u32[]{:S(2)}) collective-permute-start(bf16[28,2,32,128]{3,2,1,0:T(8,128)(2,1)S(1)} %get-tuple-element.38.refs_4_.refs_2_), channel_id=1, source_target_pairs={{0,2},{2,4},{4,6},{6,8},{8,10},{10,12},{12,14},{14,16},{16,18},{18... | collective-permute-start | bytes 1376264 | tf_op jit(solution)/shard_map/ppermute | solution.py:379
  40.7 10.7 %collective-permute-start.8 = (bf16[28,2,32,128]{3,2,1,0:T(8,128)(2,1)S(1)}, bf16[28,2,32,128]{3,2,1,0:T(8,128)(2,1)S(1)}, u32[]{:S(2)}, u32[]{:S(2)}) collective-permute-start(bf16[28,2,32,128]{3,2,1,0:T(8,128)(2,1)S(1)} %get-tuple-element.39.refs_3_.refs_1_), channel_id=1, source_target_pairs={{2,0},{4,2},{6,4},{8,6},{10,8},{12,10},{14,12},{16,14},{18,16},{20... | collective-permute-start | bytes 1376264 | tf_op jit(solution)/shard_map/ppermute | solution.py:382
  60.6 1.7 %collective-permute-start.10 = (f32[2,9,16,96]{3,2,1,0:T(8,128)S(1)}, f32[2,9,16,96]{3,2,1,0:T(8,128)S(1)}, u32[]{:S(2)}, u32[]{:S(2)}) collective-permute-start(f32[2,9,16,96]{3,2,1,0:T(8,128)S(1)} %get-tuple-element.54), channel_id=1, source_target_pairs={{0,2},{2,0},{4,6},{6,4},{8,10},{10,8},{12,14},{14,12},{16,18},{18,... | collective-permute-start | bytes 331784 | tf_op jit(solution)/shard_map/ppermute | solution.py:456
  62.3 4.6 %collective-permute-start.11 = (f32[9,16,96]{2,1,0:T(8,128)S(1)}, f32[9,16,96]{2,1,0:T(8,128)S(1)}, u32[]{:S(2)}, u32[]{:S(2)}) collective-permute-start(f32[9,16,96]{2,1,0:T(8,128)S(1)} %slice_bitcast_fusion), channel_id=1, source_target_pairs={{0,1},{1,0},{2,3},{3,2},{4,5},{5,4},{6,7},{7,6},{8,9},{9,8},{10,11... | collective-permute-start | bytes 165896 | tf_op jit(solution)/shard_map/ppermute | solution.py:376
  66.9 4.4 %collective-permute-start.12 = (f32[9,16,96]{2,1,0:T(8,128)S(1)}, f32[9,16,96]{2,1,0:T(8,128)S(1)}, u32[]{:S(2)}, u32[]{:S(2)}) collective-permute-start(f32[9,16,96]{2,1,0:T(8,128)S(1)} %fusion), channel_id=1, source_target_pairs={{0,4},{2,6},{4,0},{6,2},{8,12},{10,14},{12,8},{14,10},{16,20},{18,... | collective-permute-start | bytes 165896 | tf_op jit(solution)/shard_map/ppermute | solution.py:362
  71.4 4.4 %collective-permute-start.13 = (f32[9,16,96]{2,1,0:T(8,128)S(1)}, f32[9,16,96]{2,1,0:T(8,128)S(1)}, u32[]{:S(2)}, u32[]{:S(2)}) collective-permute-start(f32[9,16,96]{2,1,0:T(8,128)S(1)} %add.17), channel_id=1, source_target_pairs={{0,8},{2,10},{4,12},{6,14},{8,0},{10,2},{12,4},{14,6},{16,24},{18,... | collective-permute-start | bytes 165896 | tf_op jit(solution)/shard_map/ppermute | solution.py:362
  75.8 6.1 %collective-permute-start.14 = (f32[9,16,96]{2,1,0:T(8,128)S(1)}, f32[9,16,96]{2,1,0:T(8,128)S(1)}, u32[]{:S(2)}, u32[]{:S(2)}) collective-permute-start(f32[9,16,96]{2,1,0:T(8,128)S(1)} %add.18), channel_id=1, source_target_pairs={{0,16},{2,18},{4,20},{6,22},{8,24},{10,26},{12,28},{14,30},{16,0},... | collective-permute-start | bytes 165896 | tf_op jit(solution)/shard_map/ppermute | solution.py:362
  81.9 5.7 %collective-permute-start.15 = (f32[9,16,96]{2,1,0:T(8,128)S(1)}, f32[9,16,96]{2,1,0:T(8,128)S(1)}, u32[]{:S(2)}, u32[]{:S(2)}) collective-permute-start(f32[9,16,96]{2,1,0:T(8,128)S(1)} %add_multiply_fusion), channel_id=1, source_target_pairs={{0,2},{2,0},{4,6},{6,4},{8,10},{10,8},{12,14},{14,12},{16,18},{18,... | collective-permute-start | bytes 165896 | tf_op jit(solution)/shard_map/ppermute | solution.py:465
  86.3 11.6 %collective-permute-start.9 = (bf16[24,4,16,128]{3,2,1,0:T(8,128)(2,1)S(1)}, bf16[24,4,16,128]{3,2,1,0:T(8,128)(2,1)S(1)}, u32[]{:S(2)}, u32[]{:S(2)}) collective-permute-start(bf16[24,4,16,128]{3,2,1,0:T(8,128)(2,1)S(1)} %get-tuple-element.52), channel_id=1, source_target_pairs={{0,1},{1,0},{2,3},{3,2},{4,5},{5,4},{6,7},{7,6},{8,9},{9,8},{10,11... | collective-permute-start | bytes 1179656 | tf_op jit(solution)/shard_map/ppermute | solution.py:376

commit v3 on v2

--- a/solution.py
+++ b/solution.py
@@ -13,12 +13,13 @@
 LIMIT = 16 * 1024 * 1024
 
 
-def call(kernel, outs, args, scratch=(), flops=0, moved=0):
+def call(kernel, outs, args, scratch=(), flops=0, moved=0, loose=0):
     whole = pl.BlockSpec(memory_space=pltpu.VMEM)
+    still = pl.BlockSpec(memory_space=pl.ANY)
     return pl.pallas_call(
         kernel,
         out_shape=outs,
-        in_specs=[whole] * len(args),
+        in_specs=[still] * loose + [whole] * (len(args) - loose),
         out_specs=[whole] * len(outs),
         scratch_shapes=list(scratch),
         compiler_params=pltpu.CompilerParams(vmem_limit_bytes=LIMIT),
@@ -26,33 +27,46 @@
     )(*args)
 
 
+def in_blocks(count, body):
+    block = max(k for k in range(1, 8) if count % k == 0)
+    if block < 4:
+        block = min(count, 15)
+
+    def several(r, _):
+        for k in range(block):
+            body(r * block + k)
+        return 0
+
+    lax.fori_loop(0, count // block, several, 0)
+    for k in range(count // block * block, count):
+        body(k)
+
+
 def widened(x_ref, wide):
     count, planes, rows = x_ref.shape[:3]
 
-    def widen(i, _):
+    def widen(i):
         for x in range(planes):
             start = pl.multiple_of((i * planes + x) * rows, 8)
             wide[pl.ds(start, rows), :] = x_ref[i, x].astype(F32)
-        return 0
-
-    lax.fori_loop(0, count, widen, 0)
+
+    in_blocks(count, widen)
 
 
 def turn(wide, outs, shape, base, length):
     count, planes, rows = shape
 
-    def one(f, _):
+    def one(f):
         y = lax.rem(base + f, rows)
         for x in range(planes):
             tile = wide[pl.ds(x * rows + y, count, stride=planes * rows), :]
             outs[x // 2][f, x % 2] = tile.astype(BF16)
-        return 0
-
-    lax.fori_loop(0, length, one, 0)
-
-
-def field_kernel(extent, margin, x_ref, first, second, *refs):
-    outs, packed, wide = refs[:-2], refs[-2], refs[-1]
+
+    in_blocks(length, one)
+
+
+def field_kernel(extent, margin, x_ref, *refs):
+    outs, wide = refs[:-1], refs[-1]
     count, planes, rows = x_ref.shape[:3]
     pairs = planes // 2
     share = rows // extent
@@ -67,6 +81,10 @@
             base,
             share + 2 * margin,
         )
+
+
+def pack_kernel(after, first, second, packed):
+    del after
     blank = jnp.zeros(first.shape[1:], F32)
     for h in range(packed.shape[0]):
         parts = []
@@ -175,7 +193,7 @@
     slopes = [refs.pop(0) for _ in range(pairs + 1)]
     deltas = [refs.pop(0) for _ in range(pairs)]
 
-    def one(r, _):
+    def one(r):
         row = 2 * r
         for p, sums in enumerate(taps(first[...], fields, row)):
             for q, v in enumerate(sums):
@@ -183,11 +201,10 @@
                 shape = hiddens[p].shape[1:]
                 hiddens[p][row + q] = (v * sig).astype(BF16).reshape(shape)
                 slopes[p][row + q] = slope.astype(BF16).reshape(shape)
-        return 0
-
-    lax.fori_loop(0, hiddens[0].shape[0] // 2, one, 0)
-
-    def two(r, _):
+
+    in_blocks(hiddens[0].shape[0] // 2, one)
+
+    def two(r):
         row = 2 * r
         for p, sums in enumerate(taps(second[...], [[ref] for ref in hiddens], row)):
             for q, v in enumerate(sums):
@@ -195,9 +212,8 @@
                 out_grad = grads[p][row + q].astype(F32)
                 slope = silu_parts(v)[1].reshape(shape)
                 deltas[p][row + q] = (out_grad * slope).astype(BF16)
-        return 0
-
-    lax.fori_loop(0, deltas[0].shape[0] // 2, two, 0)
+
+    in_blocks(deltas[0].shape[0] // 2, two)
 
 
 def planes_of(pairs):
@@ -207,26 +223,30 @@
 def weight_loop(total, pieces, first_row, deltas, delta_row, count):
     total[...] = jnp.zeros_like(total)
 
+    together = max(k for k in range(1, 4) if (count // 2) % k == 0)
+
     def step(r, _):
         left, right = [], []
-        for x, ((delta,), place) in enumerate(deltas):
-            rows = []
-            for q in range(2):
-                wide = delta[delta_row + 2 * r + q, place]
-                plain = wide.astype(F32)
-                depth = plain.shape[1]
-                rows += [
-                    pltpu.roll(plain, depth - 1, 1).astype(BF16),
-                    wide,
-                    pltpu.roll(plain, 1, 1).astype(BF16),
-                ]
-            left.append(jnp.concatenate(rows, axis=0))
-            rows = []
-            for refs, side in pieces[x : x + 3]:
-                for b in range(4):
-                    for ref in refs:
-                        rows.append(ref[first_row + 2 * r + b, side])
-            right.append(jnp.concatenate(rows, axis=0))
+        for k in range(together):
+            row = 2 * (r * together + k)
+            for x, ((delta,), place) in enumerate(deltas):
+                rows = []
+                for q in range(2):
+                    wide = delta[delta_row + row + q, place]
+                    plain = wide.astype(F32)
+                    depth = plain.shape[1]
+                    rows += [
+                        pltpu.roll(plain, depth - 1, 1).astype(BF16),
+                        wide,
+                        pltpu.roll(plain, 1, 1).astype(BF16),
+                    ]
+                left.append(jnp.concatenate(rows, axis=0))
+                rows = []
+                for refs, side in pieces[x : x + 3]:
+                    for b in range(4):
+                        for ref in refs:
+                            rows.append(ref[first_row + row + b, side])
+                right.append(jnp.concatenate(rows, axis=0))
         total[...] += lax.dot_general(
             jnp.concatenate(left, axis=1),
             jnp.concatenate(right, axis=1),
@@ -235,7 +255,7 @@
         )
         return 0
 
-    lax.fori_loop(0, count // 2, step, 0)
+    lax.fori_loop(0, count // 2 // together, step, 0)
 
 
 def weight_fold(total, size):
@@ -276,16 +296,15 @@
     firsts = [refs.pop(0) for _ in range(pairs + 1)]
     keep, send, total = refs
 
-    def one(r, _):
+    def one(r):
         row = 2 * r
         for p, sums in enumerate(taps(weight[...], deltas, row)):
             for q, v in enumerate(sums):
                 shape = firsts[p].shape[1:]
                 slope = slopes[p][row + 2 + q].astype(F32)
                 firsts[p][row + q] = (v.reshape(shape) * slope).astype(BF16)
-        return 0
-
-    lax.fori_loop(0, firsts[0].shape[0] // 2, one, 0)
+
+    in_blocks(firsts[0].shape[0] // 2, one)
     near = planes_of(fields)[1:-1]
     own = planes_of([[first] for first in firsts])[1:-1]
     weight_loop(total, near, 3, own, 1, share)
@@ -310,13 +329,19 @@
         place(send, keep)
 
 
-def last_kernel(pairs, *refs):
+def last_kernel(pairs, extent, *refs):
     refs = list(refs)
+    shares = [refs.pop(0) for _ in range(extent)]
+    added = refs.pop()
+    value = shares[0][0]
+    for j in range(1, extent):
+        value = value + shares[j][...]
+    added[...] = value
     firsts = [refs.pop(0) for _ in range(pairs + 1)]
     weight = refs.pop(0)
     outs = refs
 
-    def one(r, _):
+    def one(r):
         row = 2 * r
         size = outs[0].shape[2]
         channels = len(outs) * size
@@ -326,40 +351,33 @@
                     for j, out in enumerate(outs):
                         low = x * channels + j * size
                         out[row + q, 2 * p + x] = v[low : low + size].astype(BF16)
-        return 0
-
-    lax.fori_loop(0, outs[0].shape[0] // 2, one, 0)
-
-
-def merge_kernel(extent, *refs):
-    pieces, out, wide = refs[:-2], refs[-2], refs[-1]
+
+    in_blocks(outs[0].shape[0] // 2, one)
+
+
+def merge_kernel(extent, one, two, *refs):
+    pieces, out, added, wide = refs[:-3], refs[-3], refs[-2], refs[-1]
+    added[...] = one[...] + two[...]
     share, planes, size = pieces[0].shape[:3]
     rows = out.shape[2]
     me = lax.axis_index("chan")
     for j, piece in enumerate(pieces):
         base = lax.rem(me + extent - j, extent) * share
 
-        def widen(f, _, piece=piece, base=base):
+        def widen(f, piece=piece, base=base):
             for x in range(planes):
                 start = ((base + f) * planes + x) * size
                 start = pl.multiple_of(start, 8) if size % 8 == 0 else start
                 wide[pl.ds(start, size), :] = piece[f, x].astype(F32)
-            return 0
-
-        lax.fori_loop(0, share, widen, 0)
-
-    def turn(i, _):
+
+        in_blocks(share, widen)
+
+    def back(i):
         for x in range(planes):
             tile = wide[pl.ds(x * size + i, rows, stride=planes * size), :]
             out[i, x] = tile.astype(BF16)
-        return 0
-
-    lax.fori_loop(0, size, turn, 0)
-
-
-def pair_sum(values, axis, stride):
-    count = lax.axis_size(axis)
-    return values + lax.ppermute(values, axis, [(i, i ^ stride) for i in range(count)])
+
+    in_blocks(size, back)
 
 
 def body(field, out_grad, first_weight, second_weight):
@@ -385,15 +403,21 @@
     halves = 14
     made = call(
         functools.partial(field_kernel, extent, 4),
-        [piece] * (extent * pairs) + [jax.ShapeDtypeStruct((halves, size, 4 * channels), BF16)],
-        [field, jnp.transpose(first_weight, (1, 0, 2)), jnp.transpose(second_weight, (1, 0, 2))],
+        [piece] * (extent * pairs),
+        [field],
         [pltpu.VMEM((size * planes * rows, depth), F32)],
         moved=field.size * 6,
     )
     parts = [made[:pairs]]
     for j in range(1, extent):
         parts.append([to_chan(piece, j) for piece in made[j * pairs : (j + 1) * pairs]])
-    packs = [made[-1]] + [to_chan(made[-1], j) for j in range(1, extent)]
+    (pack,) = call(
+        pack_kernel,
+        [jax.ShapeDtypeStruct((halves, size, 4 * channels), BF16)],
+        [made[0], jnp.transpose(first_weight, (1, 0, 2)), jnp.transpose(second_weight, (1, 0, 2))],
+        loose=1,
+    )
+    packs = [pack] + [to_chan(pack, j) for j in range(1, extent)]
     by_pair = [[parts[j][p] for j in range(extent)] for p in range(pairs)]
     groups = extent
     if size % 16 != 0:
@@ -452,21 +476,50 @@
     )
     firsts, keep, send = made[:-2], made[-2], made[-1]
 
-    if slabs & (slabs - 1) == 0 and slabs > 1:
-        keep = keep + lax.ppermute(send, "slab", [(i, i ^ 1) for i in range(slabs)])
-        mine = keep[0]
+    def swapped(value, stride):
+        return lax.ppermute(value, "slab", [(i, i ^ stride) for i in range(slabs)])
+
+    plain = slabs & (slabs - 1) == 0 and slabs >= 4
+    if plain:
+        keep = keep + swapped(send, 1)
+    out_piece = jax.ShapeDtypeStruct((share, planes, size, depth), BF16)
+    portion = jax.ShapeDtypeStruct(keep.shape[1:], F32)
+    made = call(
+        functools.partial(last_kernel, pairs, extent),
+        [out_piece] * extent + [portion],
+        [keep]
+        + [to_chan(keep[j], extent - j) for j in range(1, extent)]
+        + list(firsts)
+        + [first_back],
+        flops=work * planes * share,
+        moved=4 * planes * share * channels * depth,
+    )
+    mine = made[-1]
+    pieces = [made[0]] + [None] * (extent - 1)
+    for j in range(1, extent):
+        pieces[extent - j] = to_chan(made[j], extent - j)
+    if plain:
+        stride = 2
+        while 2 * stride < slabs:
+            mine = mine + swapped(mine, stride)
+            stride *= 2
+        theirs = swapped(mine, stride)
+    else:
+        theirs = jnp.zeros_like(mine)
+    input_grad, mine = call(
+        functools.partial(merge_kernel, extent),
+        [jax.ShapeDtypeStruct(field.shape, BF16), portion],
+        [mine, theirs] + pieces,
+        [pltpu.VMEM((rows * planes * size, depth), F32)],
+        moved=4 * field.size,
+    )
+    if plain:
+        mine = mine * factor
+        other = swapped(mine, 1)
+    else:
+        other = send[0]
         for j in range(1, extent):
-            mine = mine + to_chan(keep[j], extent - j)
-        stride = 2
-        while stride < slabs:
-            mine = pair_sum(mine, "slab", stride)
-            stride *= 2
-        mine = mine * factor
-        other = lax.ppermute(mine, "slab", [(i, i ^ 1) for i in range(slabs)])
-    else:
-        mine, other = keep[0], send[0]
-        for j in range(1, extent):
-            mine, other = mine + to_chan(keep[j], extent - j), other + to_chan(send[j], extent - j)
+            other = other + to_chan(send[j], extent - j)
         even = lax.rem(lax.axis_index("slab"), 2) == 0
         mine, other = jnp.where(even, mine, other), jnp.where(even, other, mine)
         mine, other = lax.psum((mine, other), "slab")
@@ -480,25 +533,6 @@
 
     first_grad = laid(jnp.where(even, mine, other))
     second_grad = laid(jnp.where(even, other, mine))
-
-    out_piece = jax.ShapeDtypeStruct((share, planes, size, depth), BF16)
-    made = call(
-        functools.partial(last_kernel, pairs),
-        [out_piece] * extent,
-        list(firsts) + [first_back],
-        flops=work * planes * share,
-        moved=4 * planes * share * channels * depth,
-    )
-    pieces = [made[0]] + [None] * (extent - 1)
-    for j in range(1, extent):
-        pieces[extent - j] = to_chan(made[j], extent - j)
-    (input_grad,) = call(
-        functools.partial(merge_kernel, extent),
-        [jax.ShapeDtypeStruct(field.shape, BF16)],
-        pieces,
-        [pltpu.VMEM((rows * planes * size, depth), F32)],
-        moved=4 * field.size,
-    )
     return input_grad, first_grad, second_grad
 
 

time: 100 us -> 78.7 us (0.79)
  Pallas kernels: 35.6 us -> 19.4 us
  waiting for transfers between devices: 34.4 us -> 29.4 us
    pallas_call x8 -> x9, Pallas kernels: 35.6 us -> 19.4 us  [call(): pl.pallas_call(kernel, out_shape=outs, in_specs=[still] * loose + [whole]...]
    ppermute x5, waiting for transfers between devices: 18.8 us -> 11 us  [to_chan(): lax.ppermute(value, 'chan', [(i, (i + shift) % extent) for i in range(ext...]
    ppermute x3, waiting for transfers between devices: 2.15 us -> 3.82 us  [to_next(): lax.ppermute(value, 'slab', [(i, (i + 1) % slabs) for i in range(slabs)])]
    ppermute x5, waiting for transfers between devices: 13.4 us -> 14.6 us  [swapped(): return lax.ppermute(value, 'slab', [(i, i ^ stride) for i in range(slabs)])]
  transfers between devices with their start and end apart: 16 -> 16, of which waited for: 9 -> 9; matrix products, arithmetic and copies ran while one was open for 2% -> 0% of each run, Pallas kernels for 11% -> 6%
where the time goes in v3:
time: 78.7 us; the launch traced here: 78.5 us
  waiting for transfers between devices  29.4 us (37%)
  starting transfers between devices  22.9 us (29%)
  Pallas kernels  19.4 us (25%)
  local copies, waits for them, and re-layouts  4.47 us (6%)
  other arithmetic  1.47 us (2%)
  between operations  0.81 us (1%)
    pallas_call x9, Pallas kernels, call(): pl.pallas_call(kernel, out_shape=outs, in_specs=[still] * loose + [whole]...  19.4 us
    ppermute x5, waiting for transfers between devices, swapped(): return lax.ppermute(value, 'slab', [(i, i ^ stride) for i in range(slabs)])  14.6 us
    ppermute x3, starting transfers between devices, to_prev(): lax.ppermute(value, 'slab', [((i + 1) % slabs, i) for i in range(slabs)])  11.7 us
    ppermute x5, waiting for transfers between devices, to_chan(): lax.ppermute(value, 'chan', [(i, (i + shift) % extent) for i in range(ext...  11 us
    ppermute x5, starting transfers between devices, to_chan(): lax.ppermute(value, 'chan', [(i, (i + shift) % extent) for i in range(ext...  7.76 us
    unnamed x8, local copies, waits for them, and re-layouts  4.33 us
    ppermute x3, waiting for transfers between devices, to_next(): lax.ppermute(value, 'slab', [(i, (i + 1) % slabs) for i in range(slabs)])  3.82 us
    ppermute x5, starting transfers between devices, swapped(): return lax.ppermute(value, 'slab', [(i, i ^ stride) for i in range(slabs)])  3.39 us
  transfers between devices with their start and end apart: 16, of which 9 were waited for; matrix products, arithmetic and copies ran while one was open for 0% of the time, Pallas kernels for 6%

profile of v3, /device:TPU:0, one launch (start us, length us, event | category | flops | bytes accessed | tf_op | source)
XLA Modules:
  0.0 78.5 jit_solution(15571791736992635870)
XLA Ops:
  0.6 0.0 copy-start.1
  0.6 1.1 %copy-done.1 = bf16[16,4,48,128]{3,2,1,0:T(8,128)(2,1)S(1)} copy-done((bf16[16,4,48,128]{3,2,1,0:T(8,128)(2,1)S(1)}, bf16[16,4,48,128]{3,2,1,0:T(8,128)(2,1)}, u32[]{:S(2)}) %copy-start.1) | copy-done | bytes 786456
  1.8 1.5 %shard_map.67 = (bf16[32,2,16,128]{3,2,1,0:T(8,128)(2,1)S(1)}, bf16[32,2,16,128]{3,2,1,0:T(8,128)(2,1)S(1)}, bf16[32,2,16,128]{3,2,1,0:T(8,128)(2,1)S(1)}, bf16[32,2,16,128]{3,2,1,0:T(8,128)(2,1)S(1)}) custom-call(bf16[16,4,48,128]{3,2,1,0:T(8,128)(2,1)S(1)} %copy-done.1), custom_call_target="tpu_custom_call" | custom-call | bytes 2359296 | tf_op jit(solution)/shard_map/pallas_call | solution.py:19
  3.3 3.0 %collective-permute-start.1 = (bf16[32,2,16,128]{3,2,1,0:T(8,128)(2,1)S(1)}, bf16[32,2,16,128]{3,2,1,0:T(8,128)(2,1)S(1)}, u32[]{:S(2)}, u32[]{:S(2)}) collective-permute-start(bf16[32,2,16,128]{3,2,1,0:T(8,128)(2,1)S(1)} %get-tuple-element.32), channel_id=1, source_target_pairs={{0,1},{1,0},{2,3},{3,2},{4,5},{5,4},{6,7},{7,6},{8,9},{9,8},{10,11... | collective-permute-start | bytes 786440 | tf_op jit(solution)/shard_map/ppermute | solution.py:394
  6.3 0.1 collective-permute-start.3
  6.3 3.9 %collective-permute-start.4 = (bf16[32,2,16,128]{3,2,1,0:T(8,128)(2,1)S(1)}, bf16[32,2,16,128]{3,2,1,0:T(8,128)(2,1)S(1)}, u32[]{:S(2)}, u32[]{:S(2)}) collective-permute-start(bf16[32,2,16,128]{3,2,1,0:T(8,128)(2,1)S(1)} %get-tuple-element.33.after.refs_2_.refs_9_), channel_id=1, source_target_pairs={{2,0},{4,2},{6,4},{8,6},{10,8},{12,10},{14,12},{16,14},{18,16},{20... | collective-permute-start | bytes 786440 | tf_op jit(solution)/shard_map/ppermute | solution.py:400
  10.2 0.0 collective-permute-start
  10.2 3.2 %collective-permute-done.1.refs_5_.refs_12_ = bf16[32,2,16,128]{3,2,1,0:T(8,128)(2,1)S(1)} collective-permute-done((bf16[32,2,16,128]{3,2,1,0:T(8,128)(2,1)S(1)}, bf16[32,2,16,128]{3,2,1,0:T(8,128)(2,1)S(1)}, u32[]{:S(2)}, u32[]{:S(2)}) %collective-permute-start.1) | collective-permute-done | bytes 262176 | tf_op jit(solution)/shard_map/ppermute | solution.py:394
  13.4 0.0 collective-permute-start.2
  13.4 4.8 %collective-permute-done.3.refs_3_.refs_10_ = bf16[32,2,16,128]{3,2,1,0:T(8,128)(2,1)S(1)} collective-permute-done((bf16[32,2,16,128]{3,2,1,0:T(8,128)(2,1)S(1)}, bf16[32,2,16,128]{3,2,1,0:T(8,128)(2,1)S(1)}, u32[]{:S(2)}, u32[]{:S(2)}) %collective-permute-start.3) | collective-permute-done | bytes 262176 | tf_op jit(solution)/shard_map/ppermute | solution.py:394
  18.2 3.4 %collective-permute-start.5 = (bf16[32,2,16,128]{3,2,1,0:T(8,128)(2,1)S(1)}, bf16[32,2,16,128]{3,2,1,0:T(8,128)(2,1)S(1)}, u32[]{:S(2)}, u32[]{:S(2)}) collective-permute-start(bf16[32,2,16,128]{3,2,1,0:T(8,128)(2,1)S(1)} %collective-permute-done.3.refs_3_.refs_10_), channel_id=1, source_target_pairs={{2,0},{4,2},{6,4},{8,6},{10,8},{12,10},{14,12},{16,14},{18,16},{20... | collective-permute-start | bytes 786440 | tf_op jit(solution)/shard_map/ppermute | solution.py:400
  21.6 0.0 copy-start.2
  21.6 0.9 %copy-done.2 = bf16[16,27,32]{2,0,1:T(8,128)(2,1)S(1)} copy-done((bf16[16,27,32]{2,0,1:T(8,128)(2,1)S(1)}, bf16[16,27,32]{2,0,1:T(8,128)(2,1)}, u32[]{:S(2)}) %copy-start.2) | copy-done | bytes 27672
  22.5 0.0 copy-start.3
  22.5 0.9 %copy-done.3 = bf16[16,27,32]{2,0,1:T(8,128)(2,1)S(1)} copy-done((bf16[16,27,32]{2,0,1:T(8,128)(2,1)S(1)}, bf16[16,27,32]{2,0,1:T(8,128)(2,1)}, u32[]{:S(2)}) %copy-start.3) | copy-done | bytes 27672
  23.3 0.1 shard_map.69.refs_0_
  23.5 1.6 %collective-permute-start.6 = (bf16[14,16,128]{2,1,0:T(8,128)(2,1)S(1)}, bf16[14,16,128]{2,1,0:T(8,128)(2,1)S(1)}, u32[]{:S(2)}, u32[]{:S(2)}) collective-permute-start(bf16[14,16,128]{2,1,0:T(8,128)(2,1)S(1)} %shard_map.69.refs_0_), channel_id=1, source_target_pairs={{0,1},{1,0},{2,3},{3,2},{4,5},{5,4},{6,7},{7,6},{8,9},{9,8},{10,11... | collective-permute-start | bytes 172040 | tf_op jit(solution)/shard_map/ppermute | solution.py:394
  25.0 0.0 copy-start
  25.0 1.4 %copy-done = bf16[32,4,48,128]{3,2,1,0:T(8,128)(2,1)S(1)} copy-done((bf16[32,4,48,128]{3,2,1,0:T(8,128)(2,1)S(1)}, bf16[32,4,48,128]{3,2,1,0:T(8,128)(2,1)}, u32[]{:S(2)}) %copy-start) | copy-done | bytes 1572888
  26.4 1.3 %shard_map.68 = (bf16[28,2,32,128]{3,2,1,0:T(8,128)(2,1)S(1)}, bf16[28,2,32,128]{3,2,1,0:T(8,128)(2,1)S(1)}) custom-call(bf16[32,4,48,128]{3,2,1,0:T(8,128)(2,1)S(1)} %copy-done), custom_call_target="tpu_custom_call" | custom-call | bytes 3145728 | tf_op jit(solution)/shard_map/pallas_call | solution.py:19
  27.7 0.0 collective-permute-done.6.refs_1_
  27.7 0.5 shard_map.70
  28.3 0.0 collective-permute-done.4.refs_6_.refs_13_
  28.3 0.0 collective-permute-done.refs_0_.refs_7_
  28.3 0.0 collective-permute-done.2.refs_1_.refs_8_
  28.3 0.0 collective-permute-done.5.refs_7_.refs_14_
  28.3 5.1 %shard_map.71 = (bf16[30,2,32,128]{3,2,1,0:T(8,128)(2,1)S(1)}, bf16[30,2,32,128]{3,2,1,0:T(8,128)(2,1)S(1)}, bf16[30,2,32,128]{3,2,1,0:T(8,128)(2,1)S(1)}, bf16[...) custom-call(bf16[32,2,16,128]{3,2,1,0:T(8,128)(2,1)S(1)} %collective, ...), custom_call_target="tpu_custom_call" | custom-call | flops 1358954496 | bytes 3145728 | tf_op jit(solution)/shard_map/pallas_call | solution.py:19
  33.5 0.1 collective-permute-start.7
  33.5 4.4 %collective-permute-start.8 = (bf16[28,2,32,128]{3,2,1,0:T(8,128)(2,1)S(1)}, bf16[28,2,32,128]{3,2,1,0:T(8,128)(2,1)S(1)}, u32[]{:S(2)}, u32[]{:S(2)}) collective-permute-start(bf16[28,2,32,128]{3,2,1,0:T(8,128)(2,1)S(1)} %get-tuple-element.40.refs_3_.refs_1_), channel_id=1, source_target_pairs={{2,0},{4,2},{6,4},{8,6},{10,8},{12,10},{14,12},{16,14},{18,16},{20... | collective-permute-start | bytes 1376264 | tf_op jit(solution)/shard_map/ppermute | solution.py:400
  38.0 2.4 %shard_map.72.refs_16_ = f32[2,9,16,96]{3,2,1,0:T(8,128)S(1)} custom-call(bf16[30,2,32,128]{3,2,1,0:T(8,128)(2,1)S(1)} %get-tuple-element.45.refs_0_, bf16[30,2,32,128]{3,2,1,0:T(8,128)(2,1)S(1)} %get-tuple-element.46.refs_1_, bf16[30,2,32,128]{3,2,1,0:T(8,128)(2,1)S(1)} %get-tuple-element.47.refs_2_, ...), custom_call_target="tpu_custom_call" | custom-call | flops 679477248 | bytes 3145728 | tf_op jit(solution)/shard_map/pallas_call | solution.py:19
  40.4 3.8 %collective-permute-done.7.refs_0_ = bf16[28,2,32,128]{3,2,1,0:T(8,128)(2,1)S(1)} collective-permute-done((bf16[28,2,32,128]{3,2,1,0:T(8,128)(2,1)S(1)}, bf16[28,2,32,128]{3,2,1,0:T(8,128)(2,1)S(1)}, u32[]{:S(2)}, u32[]{:S(2)}) %collective-permute-start.7) | collective-permute-done | bytes 458784 | tf_op jit(solution)/shard_map/ppermute | solution.py:397
  44.2 0.0 collective-permute-done.8.refs_3_
  44.2 4.7 %shard_map.73 = (bf16[26,2,32,128]{3,2,1,0:T(8,128)(2,1)S(1)}, bf16[26,2,32,128]{3,2,1,0:T(8,128)(2,1)S(1)}, bf16[26,2,32,128]{3,2,1,0:T(8,128)(2,1)S(1)}, f32[2...) custom-call(bf16[28,2,32,128]{3,2,1,0:T(8,128)(2,1)S(1)} %collective-permute-done.7.refs_0_, ...), custom_call_target="tpu_custom_call" | custom-call | flops 1358954496 | bytes 3145728 | tf_op jit(solution)/shard_map/pallas_call | solution.py:19
  49.0 0.8 %collective-permute-start.9 = (f32[2,9,16,96]{3,2,1,0:T(8,128)S(1)}, f32[2,9,16,96]{3,2,1,0:T(8,128)S(1)}, u32[]{:S(2)}, u32[]{:S(2)}) collective-permute-start(f32[2,9,16,96]{3,2,1,0:T(8,128)S(1)} %get-tuple-element.49), channel_id=1, source_target_pairs={{0,2},{2,0},{4,6},{6,4},{8,10},{10,8},{12,14},{14,12},{16,18},{18,... | collective-permute-start | bytes 331784 | tf_op jit(solution)/shard_map/ppermute | solution.py:480
  49.8 1.0 %collective-permute-done.9 = f32[2,9,16,96]{3,2,1,0:T(8,128)S(1)} collective-permute-done((f32[2,9,16,96]{3,2,1,0:T(8,128)S(1)}, f32[2,9,16,96]{3,2,1,0:T(8,128)S(1)}, u32[]{:S(2)}, u32[]{:S(2)}) %collective-permute-start.9) | collective-permute-done | bytes 110624 | tf_op jit(solution)/shard_map/ppermute | solution.py:480
  50.8 1.6 %collective-permute-start.10 = (f32[9,16,96]{2,1,0:T(8,128)S(1)}, f32[9,16,96]{2,1,0:T(8,128)S(1)}, u32[]{:S(2)}, u32[]{:S(2)}) collective-permute-start(f32[9,16,96]{2,1,0:T(8,128)S(1)} %slice_bitcast_fusion), channel_id=1, source_target_pairs={{0,1},{1,0},{2,3},{3,2},{4,5},{5,4},{6,7},{7,6},{8,9},{9,8},{10,11... | collective-permute-start | bytes 165896 | tf_op jit(solution)/shard_map/ppermute | solution.py:394
  52.4 3.0 %collective-permute-done.10.refs_1_ = f32[9,16,96]{2,1,0:T(8,128)S(1)} collective-permute-done((f32[9,16,96]{2,1,0:T(8,128)S(1)}, f32[9,16,96]{2,1,0:T(8,128)S(1)}, u32[]{:S(2)}, u32[]{:S(2)}) %collective-permute-start.10) | collective-permute-done | bytes 55328 | tf_op jit(solution)/shard_map/ppermute | solution.py:394
  55.4 1.7 %shard_map.74 = (bf16[24,4,16,128]{3,2,1,0:T(8,128)(2,1)S(1)}, bf16[24,4,16,128]{3,2,1,0:T(8,128)(2,1)S(1)}, f32[9,16,96]{2,1,0:T(8,128)S(1)}) custom-call(f32[2,9,16,96]{3,2,1,0:T(8,128)S(1)} %add.9.refs_0_, f32[9,16,96]{2,1,0:T(8,128)S(1)} %collective-permute-done.10.refs_1_, bf16[26,2,32,128]{3,2,1,0:T(8,128)(2,1)S(1)} %get-tuple-element.50.refs_2_, ...), custom_call_target="tpu_custom_call" | custom-call | flops 679477248 | bytes 1572864 | tf_op jit(solution)/shard_map/pallas_call | solution.py:19
  57.2 1.6 %collective-permute-start.14 = (bf16[24,4,16,128]{3,2,1,0:T(8,128)(2,1)S(1)}, bf16[24,4,16,128]{3,2,1,0:T(8,128)(2,1)S(1)}, u32[]{:S(2)}, u32[]{:S(2)}) collective-permute-start(bf16[24,4,16,128]{3,2,1,0:T(8,128)(2,1)S(1)} %get-tuple-element.56), channel_id=1, source_target_pairs={{0,1},{1,0},{2,3},{3,2},{4,5},{5,4},{6,7},{7,6},{8,9},{9,8},{10,11... | collective-permute-start | bytes 1179656 | tf_op jit(solution)/shard_map/ppermute | solution.py:394
  58.7 0.1 collective-permute-start.11
  58.8 4.3 %collective-permute-done.11 = f32[9,16,96]{2,1,0:T(8,128)S(1)} collective-permute-done((f32[9,16,96]{2,1,0:T(8,128)S(1)}, f32[9,16,96]{2,1,0:T(8,128)S(1)}, u32[]{:S(2)}, u32[]{:S(2)}) %collective-permute-start.11) | collective-permute-done | bytes 55328 | tf_op jit(solution)/shard_map/ppermute | solution.py:480
  63.1 0.7 collective-permute-start.12
  63.8 3.7 %collective-permute-done.12 = f32[9,16,96]{2,1,0:T(8,128)S(1)} collective-permute-done((f32[9,16,96]{2,1,0:T(8,128)S(1)}, f32[9,16,96]{2,1,0:T(8,128)S(1)}, u32[]{:S(2)}, u32[]{:S(2)}) %collective-permute-start.12) | collective-permute-done | bytes 55328 | tf_op jit(solution)/shard_map/ppermute | solution.py:480
  67.5 1.7 %collective-permute-start.13 = (f32[9,16,96]{2,1,0:T(8,128)S(1)}, f32[9,16,96]{2,1,0:T(8,128)S(1)}, u32[]{:S(2)}, u32[]{:S(2)}) collective-permute-start(f32[9,16,96]{2,1,0:T(8,128)S(1)} %add.11.one), channel_id=1, source_target_pairs={{0,16},{2,18},{4,20},{6,22},{8,24},{10,26},{12,28},{14,30},{16,0},... | collective-permute-start | bytes 165896 | tf_op jit(solution)/shard_map/ppermute | solution.py:480
  69.3 4.4 %collective-permute-done.13.two = f32[9,16,96]{2,1,0:T(8,128)S(1)} collective-permute-done((f32[9,16,96]{2,1,0:T(8,128)S(1)}, f32[9,16,96]{2,1,0:T(8,128)S(1)}, u32[]{:S(2)}, u32[]{:S(2)}) %collective-permute-start.13) | collective-permute-done | bytes 55328 | tf_op jit(solution)/shard_map/ppermute | solution.py:480
  73.6 0.0 collective-permute-done.14.refs_1_
  73.6 1.9 %shard_map.75 = (bf16[16,4,48,128]{3,2,1,0:T(8,128)(2,1)}, f32[9,16,96]{2,1,0:T(8,128)S(1)}) custom-call(f32[9,16,96]{2,1,0:T(8,128)S(1)} %add.11.one, f32[9,16,96]{2,1,0:T(8,128)S(1)} %collective-permute-done.13.two, bf16[24,4,16,128]{3,2,1,0:T(8,128)(2,1)S(1)} %get-tuple-element.55.refs_0_, bf16[24,4,16,128]{3,2,1,0:T(8,128)(2,1)S(1)} %collective-permute-done.14.refs_1_), custom_call_target="tpu_custom_call" | custom-call | bytes 1572864 | tf_op jit(solution)/shard_map/pallas_call | solution.py:19
  75.6 0.1 collective-permute-start.15
  75.7 1.2 %collective-permute-done.15 = f32[9,16,96]{2,1,0:T(8,128)S(1)} collective-permute-done((f32[9,16,96]{2,1,0:T(8,128)S(1)}, f32[9,16,96]{2,1,0:T(8,128)S(1)}, u32[]{:S(2)}, u32[]{:S(2)}) %collective-permute-start.15) | collective-permute-done | bytes 55328 | tf_op jit(solution)/shard_map/ppermute | solution.py:480
  76.9 0.1 fusion
  77.1 0.7 pad_maximum_fusion.1
  77.8 0.7 pad_maximum_fusion
  (6 shorter events, 0.1 us)
Async XLA Ops:
  0.6 1.1 %copy-start.1 = (bf16[16,4,48,128]{3,2,1,0:T(8,128)(2,1)S(1)}, bf16[16,4,48,128]{3,2,1,0:T(8,128)(2,1)}, u32[]{:S(2)}) copy-start(bf16[16,4,48,128]{3,2,1,0:T(8,128)(2,1)} %x_ref.2) | copy-start | bytes 2359300
  3.3 10.1 %collective-permute-start.1 = (bf16[32,2,16,128]{3,2,1,0:T(8,128)(2,1)S(1)}, bf16[32,2,16,128]{3,2,1,0:T(8,128)(2,1)S(1)}, u32[]{:S(2)}, u32[]{:S(2)}) collective-permute-start(bf16[32,2,16,128]{3,2,1,0:T(8,128)(2,1)S(1)} %get-tuple-element.32), channel_id=1, source_target_pairs={{0,1},{1,0},{2,3},{3,2},{4,5},{5,4},{6,7},{7,6},{8,9},{9,8},{10,11... | collective-permute-start | bytes 786440 | tf_op jit(solution)/shard_map/ppermute | solution.py:394
  6.3 11.9 %collective-permute-start.3 = (bf16[32,2,16,128]{3,2,1,0:T(8,128)(2,1)S(1)}, bf16[32,2,16,128]{3,2,1,0:T(8,128)(2,1)S(1)}, u32[]{:S(2)}, u32[]{:S(2)}) collective-permute-start(bf16[32,2,16,128]{3,2,1,0:T(8,128)(2,1)S(1)} %get-tuple-element.34), channel_id=1, source_target_pairs={{0,1},{1,0},{2,3},{3,2},{4,5},{5,4},{6,7},{7,6},{8,9},{9,8},{10,11... | collective-permute-start | bytes 786440 | tf_op jit(solution)/shard_map/ppermute | solution.py:394
  6.3 22.0 %collective-permute-start.4 = (bf16[32,2,16,128]{3,2,1,0:T(8,128)(2,1)S(1)}, bf16[32,2,16,128]{3,2,1,0:T(8,128)(2,1)S(1)}, u32[]{:S(2)}, u32[]{:S(2)}) collective-permute-start(bf16[32,2,16,128]{3,2,1,0:T(8,128)(2,1)S(1)} %get-tuple-element.33.after.refs_2_.refs_9_), channel_id=1, source_target_pairs={{2,0},{4,2},{6,4},{8,6},{10,8},{12,10},{14,12},{16,14},{18,16},{20... | collective-permute-start | bytes 786440 | tf_op jit(solution)/shard_map/ppermute | solution.py:400
  10.2 18.1 %collective-permute-start = (bf16[32,2,16,128]{3,2,1,0:T(8,128)(2,1)S(1)}, bf16[32,2,16,128]{3,2,1,0:T(8,128)(2,1)S(1)}, u32[]{:S(2)}, u32[]{:S(2)}) collective-permute-start(bf16[32,2,16,128]{3,2,1,0:T(8,128)(2,1)S(1)} %get-tuple-element.31.refs_4_.refs_11_), channel_id=1, source_target_pairs={{0,2},{2,4},{4,6},{6,8},{8,10},{10,12},{12,14},{14,16},{16,18},{18... | collective-permute-start | bytes 786440 | tf_op jit(solution)/shard_map/ppermute | solution.py:397
  13.4 14.9 %collective-permute-start.2 = (bf16[32,2,16,128]{3,2,1,0:T(8,128)(2,1)S(1)}, bf16[32,2,16,128]{3,2,1,0:T(8,128)(2,1)S(1)}, u32[]{:S(2)}, u32[]{:S(2)}) collective-permute-start(bf16[32,2,16,128]{3,2,1,0:T(8,128)(2,1)S(1)} %collective-permute-done.1.refs_5_.refs_12_), channel_id=1, source_target_pairs={{0,2},{2,4},{4,6},{6,8},{8,10},{10,12},{12,14},{14,16},{16,18},{18... | collective-permute-start | bytes 786440 | tf_op jit(solution)/shard_map/ppermute | solution.py:397
  18.2 10.1 %collective-permute-start.5 = (bf16[32,2,16,128]{3,2,1,0:T(8,128)(2,1)S(1)}, bf16[32,2,16,128]{3,2,1,0:T(8,128)(2,1)S(1)}, u32[]{:S(2)}, u32[]{:S(2)}) collective-permute-start(bf16[32,2,16,128]{3,2,1,0:T(8,128)(2,1)S(1)} %collective-permute-done.3.refs_3_.refs_10_), channel_id=1, source_target_pairs={{2,0},{4,2},{6,4},{8,6},{10,8},{12,10},{14,12},{16,14},{18,16},{20... | collective-permute-start | bytes 786440 | tf_op jit(solution)/shard_map/ppermute | solution.py:400
  21.6 0.9 %copy-start.2 = (bf16[16,27,32]{2,0,1:T(8,128)(2,1)S(1)}, bf16[16,27,32]{2,0,1:T(8,128)(2,1)}, u32[]{:S(2)}) copy-start(bf16[16,27,32]{2,0,1:T(8,128)(2,1)} %param.6) | copy-start | bytes 82948
  22.5 0.9 %copy-start.3 = (bf16[16,27,32]{2,0,1:T(8,128)(2,1)S(1)}, bf16[16,27,32]{2,0,1:T(8,128)(2,1)}, u32[]{:S(2)}) copy-start(bf16[16,27,32]{2,0,1:T(8,128)(2,1)} %param.7) | copy-start | bytes 82948
  23.5 4.3 %collective-permute-start.6 = (bf16[14,16,128]{2,1,0:T(8,128)(2,1)S(1)}, bf16[14,16,128]{2,1,0:T(8,128)(2,1)S(1)}, u32[]{:S(2)}, u32[]{:S(2)}) collective-permute-start(bf16[14,16,128]{2,1,0:T(8,128)(2,1)S(1)} %shard_map.69.refs_0_), channel_id=1, source_target_pairs={{0,1},{1,0},{2,3},{3,2},{4,5},{5,4},{6,7},{7,6},{8,9},{9,8},{10,11... | collective-permute-start | bytes 172040 | tf_op jit(solution)/shard_map/ppermute | solution.py:394
  25.0 1.4 %copy-start = (bf16[32,4,48,128]{3,2,1,0:T(8,128)(2,1)S(1)}, bf16[32,4,48,128]{3,2,1,0:T(8,128)(2,1)}, u32[]{:S(2)}) copy-start(bf16[32,4,48,128]{3,2,1,0:T(8,128)(2,1)} %x_ref.3) | copy-start | bytes 4718596
  33.5 10.8 %collective-permute-start.7 = (bf16[28,2,32,128]{3,2,1,0:T(8,128)(2,1)S(1)}, bf16[28,2,32,128]{3,2,1,0:T(8,128)(2,1)S(1)}, u32[]{:S(2)}, u32[]{:S(2)}) collective-permute-start(bf16[28,2,32,128]{3,2,1,0:T(8,128)(2,1)S(1)} %get-tuple-element.39.refs_4_.refs_2_), channel_id=1, source_target_pairs={{0,2},{2,4},{4,6},{6,8},{8,10},{10,12},{12,14},{14,16},{16,18},{18... | collective-permute-start | bytes 1376264 | tf_op jit(solution)/shard_map/ppermute | solution.py:397
  33.5 10.7 %collective-permute-start.8 = (bf16[28,2,32,128]{3,2,1,0:T(8,128)(2,1)S(1)}, bf16[28,2,32,128]{3,2,1,0:T(8,128)(2,1)S(1)}, u32[]{:S(2)}, u32[]{:S(2)}) collective-permute-start(bf16[28,2,32,128]{3,2,1,0:T(8,128)(2,1)S(1)} %get-tuple-element.40.refs_3_.refs_1_), channel_id=1, source_target_pairs={{2,0},{4,2},{6,4},{8,6},{10,8},{12,10},{14,12},{16,14},{18,16},{20... | collective-permute-start | bytes 1376264 | tf_op jit(solution)/shard_map/ppermute | solution.py:400
  49.0 1.8 %collective-permute-start.9 = (f32[2,9,16,96]{3,2,1,0:T(8,128)S(1)}, f32[2,9,16,96]{3,2,1,0:T(8,128)S(1)}, u32[]{:S(2)}, u32[]{:S(2)}) collective-permute-start(f32[2,9,16,96]{3,2,1,0:T(8,128)S(1)} %get-tuple-element.49), channel_id=1, source_target_pairs={{0,2},{2,0},{4,6},{6,4},{8,10},{10,8},{12,14},{14,12},{16,18},{18,... | collective-permute-start | bytes 331784 | tf_op jit(solution)/shard_map/ppermute | solution.py:480
  50.8 4.6 %collective-permute-start.10 = (f32[9,16,96]{2,1,0:T(8,128)S(1)}, f32[9,16,96]{2,1,0:T(8,128)S(1)}, u32[]{:S(2)}, u32[]{:S(2)}) collective-permute-start(f32[9,16,96]{2,1,0:T(8,128)S(1)} %slice_bitcast_fusion), channel_id=1, source_target_pairs={{0,1},{1,0},{2,3},{3,2},{4,5},{5,4},{6,7},{7,6},{8,9},{9,8},{10,11... | collective-permute-start | bytes 165896 | tf_op jit(solution)/shard_map/ppermute | solution.py:394
  57.2 16.5 %collective-permute-start.14 = (bf16[24,4,16,128]{3,2,1,0:T(8,128)(2,1)S(1)}, bf16[24,4,16,128]{3,2,1,0:T(8,128)(2,1)S(1)}, u32[]{:S(2)}, u32[]{:S(2)}) collective-permute-start(bf16[24,4,16,128]{3,2,1,0:T(8,128)(2,1)S(1)} %get-tuple-element.56), channel_id=1, source_target_pairs={{0,1},{1,0},{2,3},{3,2},{4,5},{5,4},{6,7},{7,6},{8,9},{9,8},{10,11... | collective-permute-start | bytes 1179656 | tf_op jit(solution)/shard_map/ppermute | solution.py:394
  58.7 4.4 %collective-permute-start.11 = (f32[9,16,96]{2,1,0:T(8,128)S(1)}, f32[9,16,96]{2,1,0:T(8,128)S(1)}, u32[]{:S(2)}, u32[]{:S(2)}) collective-permute-start(f32[9,16,96]{2,1,0:T(8,128)S(1)} %get-tuple-element.54), channel_id=1, source_target_pairs={{0,4},{2,6},{4,0},{6,2},{8,12},{10,14},{12,8},{14,10},{16,20},{18,... | collective-permute-start | bytes 165896 | tf_op jit(solution)/shard_map/ppermute | solution.py:480
  63.1 4.4 %collective-permute-start.12 = (f32[9,16,96]{2,1,0:T(8,128)S(1)}, f32[9,16,96]{2,1,0:T(8,128)S(1)}, u32[]{:S(2)}, u32[]{:S(2)}) collective-permute-start(f32[9,16,96]{2,1,0:T(8,128)S(1)} %add.10), channel_id=1, source_target_pairs={{0,8},{2,10},{4,12},{6,14},{8,0},{10,2},{12,4},{14,6},{16,24},{18,... | collective-permute-start | bytes 165896 | tf_op jit(solution)/shard_map/ppermute | solution.py:480
  67.5 6.1 %collective-permute-start.13 = (f32[9,16,96]{2,1,0:T(8,128)S(1)}, f32[9,16,96]{2,1,0:T(8,128)S(1)}, u32[]{:S(2)}, u32[]{:S(2)}) collective-permute-start(f32[9,16,96]{2,1,0:T(8,128)S(1)} %add.11.one), channel_id=1, source_target_pairs={{0,16},{2,18},{4,20},{6,22},{8,24},{10,26},{12,28},{14,30},{16,0},... | collective-permute-start | bytes 165896 | tf_op jit(solution)/shard_map/ppermute | solution.py:480
  75.6 1.3 %collective-permute-start.15 = (f32[9,16,96]{2,1,0:T(8,128)S(1)}, f32[9,16,96]{2,1,0:T(8,128)S(1)}, u32[]{:S(2)}, u32[]{:S(2)}) collective-permute-start(f32[9,16,96]{2,1,0:T(8,128)S(1)} %broadcast_multiply_fusion), channel_id=1, source_target_pairs={{0,2},{2,0},{4,6},{6,4},{8,10},{10,8},{12,14},{14,12},{16,18},{18,... | collective-permute-start | bytes 165896 | tf_op jit(solution)/shard_map/ppermute | solution.py:480

commit v4 on v3

--- a/solution.py
+++ b/solution.py
@@ -13,14 +13,15 @@
 LIMIT = 16 * 1024 * 1024
 
 
-def call(kernel, outs, args, scratch=(), flops=0, moved=0, loose=0):
+def call(kernel, outs, args, scratch=(), flops=0, moved=0, loose=0, same=None):
     whole = pl.BlockSpec(memory_space=pltpu.VMEM)
     still = pl.BlockSpec(memory_space=pl.ANY)
     return pl.pallas_call(
         kernel,
         out_shape=outs,
         in_specs=[still] * loose + [whole] * (len(args) - loose),
-        out_specs=[whole] * len(outs),
+        out_specs=[whole if same is None else still] * len(outs),
+        input_output_aliases=same or {},
         scratch_shapes=list(scratch),
         compiler_params=pltpu.CompilerParams(vmem_limit_bytes=LIMIT),
         cost_estimate=pl.CostEstimate(flops=flops, bytes_accessed=moved, transcendentals=0),
@@ -262,18 +263,21 @@
     lanes = total.shape[0] // 2
     channels = total.shape[1] // 12
     upper, lower = total[:lanes, :].T, total[lanes:, :].T
-    parts = []
+    groups = []
     for g in range(channels // size):
         taps_of = []
         for a in range(3):
             for b in range(3):
                 start = (4 * a + b) * channels + g * size
-                taps_of.append(
+                part = (
                     upper[start : start + size]
                     + lower[start + channels : start + channels + size]
                 )
-        parts.append(taps_of)
-    return parts
+                taps_of += [part[:, e * channels : (e + 1) * channels] for e in range(3)]
+        blank = jnp.zeros((size, channels), F32)
+        taps_of += [blank] * 5
+        groups.append([jnp.concatenate(taps_of[4 * h : 4 * h + 4], axis=1) for h in range(8)])
+    return groups
 
 
 def second_kernel(share, pairs, *refs):
@@ -282,9 +286,9 @@
     deltas = [refs.pop(0) for _ in range(pairs)]
     raw, total = refs
     weight_loop(total, planes_of(hiddens), 2, planes_of([[d] for d in deltas]), 2, share)
-    for g, taps_of in enumerate(weight_fold(total, raw.shape[2])):
-        for t, part in enumerate(taps_of):
-            raw[g, t] = part
+    for g, tiles in enumerate(weight_fold(total, raw.shape[2])):
+        for h, tile in enumerate(tiles):
+            raw[g, h] = tile
 
 
 def back_kernel(share, groups, pairs, *refs):
@@ -294,7 +298,7 @@
     fields = [[refs.pop(0) for _ in range(groups)] for _ in range(pairs + 2)]
     weight, second = refs.pop(0), refs.pop(0)
     firsts = [refs.pop(0) for _ in range(pairs + 1)]
-    keep, send, total = refs
+    sent, total = refs
 
     def one(r):
         row = 2 * r
@@ -308,35 +312,17 @@
     near = planes_of(fields)[1:-1]
     own = planes_of([[first] for first in firsts])[1:-1]
     weight_loop(total, near, 3, own, 1, share)
-    parts = weight_fold(total, keep.shape[2])
-    extent = keep.shape[0]
+    extent, size = sent.shape[1:3]
     me = lax.axis_index("chan")
-    odd = lax.rem(lax.axis_index("slab"), 2)
-
-    def place(ours, theirs):
-        for g, taps_of in enumerate(parts):
-            there = lax.rem(me + extent - g, extent)
-            for t, part in enumerate(taps_of):
-                ours[g, t] = part
-                theirs[g, t] = second[there, t]
-
-    @pl.when(odd == 0)
-    def _():
-        place(keep, send)
-
-    @pl.when(odd == 1)
-    def _():
-        place(send, keep)
-
-
-def last_kernel(pairs, extent, *refs):
+    for g, tiles in enumerate(weight_fold(total, size)):
+        there = lax.rem(me + extent - g, extent)
+        for h, tile in enumerate(tiles):
+            sent[h, there] = tile
+            sent[8 + h, g] = second[g, h]
+
+
+def last_kernel(pairs, *refs):
     refs = list(refs)
-    shares = [refs.pop(0) for _ in range(extent)]
-    added = refs.pop()
-    value = shares[0][0]
-    for j in range(1, extent):
-        value = value + shares[j][...]
-    added[...] = value
     firsts = [refs.pop(0) for _ in range(pairs + 1)]
     weight = refs.pop(0)
     outs = refs
@@ -355,9 +341,20 @@
     in_blocks(outs[0].shape[0] // 2, one)
 
 
-def merge_kernel(extent, one, two, *refs):
-    pieces, out, added, wide = refs[:-3], refs[-3], refs[-2], refs[-1]
-    added[...] = one[...] + two[...]
+def finish_kernel(factor, sums, first, second):
+    channels = first.shape[2]
+    for k, out in enumerate((first, second)):
+        for t in range(27):
+            low = t % 4 * channels
+            out[t] = sums[8 * k + t // 4, :, low : low + channels] * factor
+
+
+def relay_kernel(*refs):
+    pass
+
+
+def merge_kernel(extent, *refs):
+    pieces, out, wide = refs[:-2], refs[-2], refs[-1]
     share, planes, size = pieces[0].shape[:3]
     rows = out.shape[2]
     me = lax.axis_index("chan")
@@ -418,6 +415,21 @@
         loose=1,
     )
     packs = [pack] + [to_chan(pack, j) for j in range(1, extent)]
+    matrix = jax.ShapeDtypeStruct((6 * channels, 12 * channels), BF16)
+    first_wide, second_wide, first_back, second_back = call(
+        functools.partial(matrix_kernel, extent), [matrix] * 4, packs, moved=matrix.size * 8
+    )
+    grad_piece = jax.ShapeDtypeStruct((share + 4, 2, channels, depth), BF16)
+    grads = call(
+        functools.partial(grad_kernel, extent, 2),
+        [grad_piece] * pairs,
+        [out_grad],
+        [pltpu.VMEM((channels * planes * rows, depth), F32)],
+        moved=out_grad.size * 4,
+    )
+    if extent > 1:
+        early = [parts[1][0], first_wide, grads[0]]
+        (parts[1][0],) = call(relay_kernel, [piece], early, loose=3, same={0: 0})
     by_pair = [[parts[j][p] for j in range(extent)] for p in range(pairs)]
     groups = extent
     if size % 16 != 0:
@@ -426,18 +438,6 @@
     before = [to_next(piece) for piece in by_pair[-1]]
     after = [to_prev(piece) for piece in by_pair[0]]
     fields = [before] + by_pair + [after]
-    matrix = jax.ShapeDtypeStruct((6 * channels, 12 * channels), BF16)
-    first_wide, second_wide, first_back, second_back = call(
-        functools.partial(matrix_kernel, extent), [matrix] * 4, packs, moved=matrix.size * 8
-    )
-    grad_piece = jax.ShapeDtypeStruct((share + 4, 2, channels, depth), BF16)
-    grads = call(
-        functools.partial(grad_kernel, extent, 2),
-        [grad_piece] * pairs,
-        [out_grad],
-        [pltpu.VMEM((channels * planes * rows, depth), F32)],
-        moved=out_grad.size * 4,
-    )
 
     def many(count, rows_each, dtype=BF16):
         return [jax.ShapeDtypeStruct((rows_each, 2, channels, depth), dtype)] * count
@@ -456,7 +456,8 @@
     deltas = made[2 * pairs + 2 :]
     all_deltas = [to_next(deltas[-1])] + list(deltas) + [to_prev(deltas[0])]
 
-    raw = jax.ShapeDtypeStruct((extent, 9, size, 3 * channels), F32)
+    raw = jax.ShapeDtypeStruct((extent, 8, size, 4 * channels), F32)
+    ready = jax.ShapeDtypeStruct((16, extent, size, 4 * channels), F32)
     total = pltpu.VMEM((6 * channels, 12 * channels), F32)
     (second_raw,) = call(
         functools.partial(second_kernel, share, pairs),
@@ -468,71 +469,54 @@
     )
     made = call(
         functools.partial(back_kernel, share, groups, pairs),
-        many(pairs + 1, share + 2) + [raw] * 2,
+        many(pairs + 1, share + 2) + [ready],
         all_deltas + list(slopes) + flat_fields + [second_back, second_raw],
         [total],
         flops=work * 2 * planes * share,
         moved=8 * planes * share * channels * depth,
     )
-    firsts, keep, send = made[:-2], made[-2], made[-1]
-
-    def swapped(value, stride):
-        return lax.ppermute(value, "slab", [(i, i ^ stride) for i in range(slabs)])
-
-    plain = slabs & (slabs - 1) == 0 and slabs >= 4
-    if plain:
-        keep = keep + swapped(send, 1)
+    firsts, sent = made[:-1], made[-1]
+
+    wide = 4 * channels
+    lines = 16 * size // slabs
+    if lines * slabs == 16 * size:
+        if lines != size:
+            sent = jnp.swapaxes(sent, 0, 1).reshape(extent, slabs, lines, wide)
+            sent = jnp.swapaxes(sent, 0, 1)
+        sent = sent.reshape(slabs * extent, lines, wide)
+        got = lax.all_to_all(sent, ("slab", "chan"), 0, 0, tiled=True)
+        own = jnp.sum(got, axis=0, keepdims=True)
+        sums = lax.all_to_all(
+            jnp.broadcast_to(own, (slabs, lines, wide)), "slab", 0, 0, tiled=True
+        )
+    else:
+        sums = lax.psum(sent, ("slab", "chan"))
+        sums = lax.dynamic_index_in_dim(sums, me, axis=1, keepdims=False)
+    sums = sums.reshape(16, size, wide)
+    by_tap = jax.ShapeDtypeStruct((27, size, channels), F32)
+    first_grad, second_grad = call(
+        functools.partial(finish_kernel, factor), [by_tap] * 2, [sums]
+    )
+    first_grad, second_grad = (jnp.transpose(g, (1, 0, 2)) for g in (first_grad, second_grad))
+
     out_piece = jax.ShapeDtypeStruct((share, planes, size, depth), BF16)
-    portion = jax.ShapeDtypeStruct(keep.shape[1:], F32)
     made = call(
-        functools.partial(last_kernel, pairs, extent),
-        [out_piece] * extent + [portion],
-        [keep]
-        + [to_chan(keep[j], extent - j) for j in range(1, extent)]
-        + list(firsts)
-        + [first_back],
+        functools.partial(last_kernel, pairs),
+        [out_piece] * extent,
+        list(firsts) + [first_back],
         flops=work * planes * share,
         moved=4 * planes * share * channels * depth,
     )
-    mine = made[-1]
     pieces = [made[0]] + [None] * (extent - 1)
     for j in range(1, extent):
         pieces[extent - j] = to_chan(made[j], extent - j)
-    if plain:
-        stride = 2
-        while 2 * stride < slabs:
-            mine = mine + swapped(mine, stride)
-            stride *= 2
-        theirs = swapped(mine, stride)
-    else:
-        theirs = jnp.zeros_like(mine)
-    input_grad, mine = call(
+    (input_grad,) = call(
         functools.partial(merge_kernel, extent),
-        [jax.ShapeDtypeStruct(field.shape, BF16), portion],
-        [mine, theirs] + pieces,
+        [jax.ShapeDtypeStruct(field.shape, BF16)],
+        pieces,
         [pltpu.VMEM((rows * planes * size, depth), F32)],
         moved=4 * field.size,
     )
-    if plain:
-        mine = mine * factor
-        other = swapped(mine, 1)
-    else:
-        other = send[0]
-        for j in range(1, extent):
-            other = other + to_chan(send[j], extent - j)
-        even = lax.rem(lax.axis_index("slab"), 2) == 0
-        mine, other = jnp.where(even, mine, other), jnp.where(even, other, mine)
-        mine, other = lax.psum((mine, other), "slab")
-        mine, other = mine * factor, other * factor
-        mine, other = jnp.where(even, mine, other), jnp.where(even, other, mine)
-    even = lax.rem(lax.axis_index("slab"), 2) == 0
-
-    def laid(value):
-        taps_first = jnp.transpose(value.reshape(9, size, 3, channels), (0, 2, 1, 3))
-        return jnp.transpose(taps_first.reshape(27, size, channels), (1, 0, 2))
-
-    first_grad = laid(jnp.where(even, mine, other))
-    second_grad = laid(jnp.where(even, other, mine))
     return input_grad, first_grad, second_grad
 
 

time: 78.7 us -> 81.3 us (1.033)
  starting transfers between devices: 22.9 us -> 29.9 us
  waiting for transfers between devices: 29.4 us -> 24.2 us
  Pallas kernels: 19.4 us -> 21 us
  other arithmetic: 1.47 us -> 0.04 us
    ppermute x5 -> x0, waiting for transfers between devices: 14.6 us -> none  [swapped(): return lax.ppermute(value, 'slab', [(i, i ^ stride) for i in range(slabs)])]
    all_to_all x0 -> x2, waiting for transfers between devices: none -> 13.1 us  [the longest x1 7.12 us: body(): got = lax.all_to_all(sent, ('slab', 'chan'), 0, 0, tiled=True)]
    all_to_all x0 -> x2, starting transfers between devices: none -> 10.8 us  [the longest x1 7.31 us: body(): got = lax.all_to_all(sent, ('slab', 'chan'), 0, 0, tiled=True)]
    ppermute x5 -> x4, waiting for transfers between devices: 11 us -> 3.28 us  [to_chan(): lax.ppermute(value, 'chan', [(i, (i + shift) % extent) for i in range(ext...]
    ppermute x3, waiting for transfers between devices: 3.82 us -> 7.88 us  [to_next(): lax.ppermute(value, 'slab', [(i, (i + 1) % slabs) for i in range(slabs)])]
    ppermute x5 -> x0, starting transfers between devices: 3.39 us -> none  [swapped(): return lax.ppermute(value, 'slab', [(i, i ^ stride) for i in range(slabs)])]
    ppermute x3, starting transfers between devices: 0.06 us -> 2 us  [to_next(): lax.ppermute(value, 'slab', [(i, (i + 1) % slabs) for i in range(slabs)])]
    pallas_call x9 -> x11, Pallas kernels: 19.4 us -> 21 us  [call(): pl.pallas_call(kernel, out_shape=outs, in_specs=[still] * loose + [whole]...]
  transfers between devices with their start and end apart: 16 -> 12, of which waited for: 9 -> 5; matrix products, arithmetic and copies ran while one was open for 0% -> 1% of each run, Pallas kernels for 6% -> 10%
where the time goes in v4:
time: 81.3 us; the launch traced here: 80.9 us
  starting transfers between devices  29.9 us (37%)
  waiting for transfers between devices  24.2 us (30%)
  Pallas kernels  21 us (26%)
  local copies, waits for them, and re-layouts  4.99 us (6%)
    pallas_call x11, Pallas kernels, call(): pl.pallas_call(kernel, out_shape=outs, in_specs=[still] * loose + [whole]...  21 us
    ppermute x3, starting transfers between devices, to_prev(): lax.ppermute(value, 'slab', [((i + 1) % slabs, i) for i in range(slabs)])  10.1 us
    ppermute x3, waiting for transfers between devices, to_next(): lax.ppermute(value, 'slab', [(i, (i + 1) % slabs) for i in range(slabs)])  7.88 us
    all_to_all x1, starting transfers between devices, body(): got = lax.all_to_all(sent, ('slab', 'chan'), 0, 0, tiled=True)  7.31 us
    all_to_all x1, waiting for transfers between devices, body(): got = lax.all_to_all(sent, ('slab', 'chan'), 0, 0, tiled=True)  7.12 us
    ppermute x4, starting transfers between devices, to_chan(): lax.ppermute(value, 'chan', [(i, (i + shift) % extent) for i in range(ext...  6.93 us
    all_to_all x1, waiting for transfers between devices, body(): lax.all_to_all(jnp.broadcast_to(own, (slabs, lines, wide)), 'slab', 0, 0,...  5.96 us
    unnamed x8, local copies, waits for them, and re-layouts  4.33 us
  transfers between devices with their start and end apart: 12, of which 5 were waited for; matrix products, arithmetic and copies ran while one was open for 1% of the time, Pallas kernels for 10%

profile of v4, /device:TPU:0, one launch (start us, length us, event | category | flops | bytes accessed | tf_op | source)
XLA Modules:
  0.0 80.9 jit_solution(11326373599891320029)
XLA Ops:
  0.6 0.0 copy-start.1
  0.6 1.1 %copy-done.1 = bf16[16,4,48,128]{3,2,1,0:T(8,128)(2,1)S(1)} copy-done((bf16[16,4,48,128]{3,2,1,0:T(8,128)(2,1)S(1)}, bf16[16,4,48,128]{3,2,1,0:T(8,128)(2,1)}, u32[]{:S(2)}) %copy-start.1) | copy-done | bytes 786456
  1.8 1.5 %shard_map.67 = (bf16[32,2,16,128]{3,2,1,0:T(8,128)(2,1)S(1)}, bf16[32,2,16,128]{3,2,1,0:T(8,128)(2,1)S(1)}, bf16[32,2,16,128]{3,2,1,0:T(8,128)(2,1)S(1)}, bf16[32,2,16,128]{3,2,1,0:T(8,128)(2,1)S(1)}) custom-call(bf16[16,4,48,128]{3,2,1,0:T(8,128)(2,1)S(1)} %copy-done.1), custom_call_target="tpu_custom_call" | custom-call | bytes 2359296 | tf_op jit(solution)/shard_map/pallas_call | solution.py:19
  3.3 3.0 %collective-permute-start.1 = (bf16[32,2,16,128]{3,2,1,0:T(8,128)(2,1)S(1)}, bf16[32,2,16,128]{3,2,1,0:T(8,128)(2,1)S(1)}, u32[]{:S(2)}, u32[]{:S(2)}) collective-permute-start(bf16[32,2,16,128]{3,2,1,0:T(8,128)(2,1)S(1)} %get-tuple-element.30), channel_id=1, source_target_pairs={{0,1},{1,0},{2,3},{3,2},{4,5},{5,4},{6,7},{7,6},{8,9},{9,8},{10,11... | collective-permute-start | bytes 786440 | tf_op jit(solution)/shard_map/ppermute | solution.py:391
  6.3 0.1 collective-permute-start.3
  6.3 0.0 copy-start.2
  6.3 0.9 %copy-done.2 = bf16[16,27,32]{2,0,1:T(8,128)(2,1)S(1)} copy-done((bf16[16,27,32]{2,0,1:T(8,128)(2,1)S(1)}, bf16[16,27,32]{2,0,1:T(8,128)(2,1)}, u32[]{:S(2)}) %copy-start.2) | copy-done | bytes 27672
  7.2 0.0 copy-start.3
  7.2 0.9 %copy-done.3 = bf16[16,27,32]{2,0,1:T(8,128)(2,1)S(1)} copy-done((bf16[16,27,32]{2,0,1:T(8,128)(2,1)S(1)}, bf16[16,27,32]{2,0,1:T(8,128)(2,1)}, u32[]{:S(2)}) %copy-start.3) | copy-done | bytes 27672
  8.1 0.1 shard_map.68.refs_0_
  8.2 2.0 %collective-permute-start.4 = (bf16[14,16,128]{2,1,0:T(8,128)(2,1)S(1)}, bf16[14,16,128]{2,1,0:T(8,128)(2,1)S(1)}, u32[]{:S(2)}, u32[]{:S(2)}) collective-permute-start(bf16[14,16,128]{2,1,0:T(8,128)(2,1)S(1)} %shard_map.68.refs_0_), channel_id=1, source_target_pairs={{0,1},{1,0},{2,3},{3,2},{4,5},{5,4},{6,7},{7,6},{8,9},{9,8},{10,11... | collective-permute-start | bytes 172040 | tf_op jit(solution)/shard_map/ppermute | solution.py:391
  10.3 3.2 %collective-permute-start.5 = (bf16[32,2,16,128]{3,2,1,0:T(8,128)(2,1)S(1)}, bf16[32,2,16,128]{3,2,1,0:T(8,128)(2,1)S(1)}, u32[]{:S(2)}, u32[]{:S(2)}) collective-permute-start(bf16[32,2,16,128]{3,2,1,0:T(8,128)(2,1)S(1)} %get-tuple-element.31.after.refs_2_.refs_9_), channel_id=1, source_target_pairs={{2,0},{4,2},{6,4},{8,6},{10,8},{12,10},{14,12},{16,14},{18,16},{20... | collective-permute-start | bytes 786440 | tf_op jit(solution)/shard_map/ppermute | solution.py:397
  13.4 0.0 collective-permute-start
  13.4 0.0 copy-start
  13.4 1.4 %copy-done = bf16[32,4,48,128]{3,2,1,0:T(8,128)(2,1)S(1)} copy-done((bf16[32,4,48,128]{3,2,1,0:T(8,128)(2,1)S(1)}, bf16[32,4,48,128]{3,2,1,0:T(8,128)(2,1)}, u32[]{:S(2)}) %copy-start) | copy-done | bytes 1572888
  14.8 1.3 %shard_map.70 = (bf16[28,2,32,128]{3,2,1,0:T(8,128)(2,1)S(1)}, bf16[28,2,32,128]{3,2,1,0:T(8,128)(2,1)S(1)}) custom-call(bf16[32,4,48,128]{3,2,1,0:T(8,128)(2,1)S(1)} %copy-done), custom_call_target="tpu_custom_call" | custom-call | bytes 3145728 | tf_op jit(solution)/shard_map/pallas_call | solution.py:19
  16.1 3.3 %collective-permute-done.4.refs_1_ = bf16[14,16,128]{2,1,0:T(8,128)(2,1)S(1)} collective-permute-done((bf16[14,16,128]{2,1,0:T(8,128)(2,1)S(1)}, bf16[14,16,128]{2,1,0:T(8,128)(2,1)S(1)}, u32[]{:S(2)}, u32[]{:S(2)}) %collective-permute-start.4) | collective-permute-done | bytes 57376 | tf_op jit(solution)/shard_map/ppermute | solution.py:391
  19.4 0.5 shard_map.69
  19.9 0.0 collective-permute-done.1.refs_5_.refs_12_
  20.0 0.1 collective-permute-start.2
  20.0 0.0 collective-permute-done.3.refs_0_
  20.0 4.4 %collective-permute-start.6 = (bf16[32,2,16,128]{3,2,1,0:T(8,128)(2,1)S(1)}, bf16[32,2,16,128]{3,2,1,0:T(8,128)(2,1)S(1)}, u32[]{:S(2)}, u32[]{:S(2)}) collective-permute-start(bf16[32,2,16,128]{3,2,1,0:T(8,128)(2,1)S(1)} %shard_map.71.refs_3_.refs_10_), channel_id=1, source_target_pairs={{2,0},{4,2},{6,4},{8,6},{10,8},{12,10},{14,12},{16,14},{18,16},{20... | collective-permute-start | bytes 786440 | tf_op jit(solution)/shard_map/ppermute | solution.py:397
  24.5 0.0 collective-permute-done.refs_0_.refs_7_
  24.5 0.0 collective-permute-done.5.refs_6_.refs_13_
  24.5 4.1 %collective-permute-done.2.refs_1_.refs_8_ = bf16[32,2,16,128]{3,2,1,0:T(8,128)(2,1)S(1)} collective-permute-done((bf16[32,2,16,128]{3,2,1,0:T(8,128)(2,1)S(1)}, bf16[32,2,16,128]{3,2,1,0:T(8,128)(2,1)S(1)}, u32[]{:S(2)}, u32[]{:S(2)}) %collective-permute-start.2) | collective-permute-done | bytes 262176 | tf_op jit(solution)/shard_map/ppermute | solution.py:394
  28.6 0.0 collective-permute-done.6.refs_7_.refs_14_
  28.6 5.1 %shard_map.72 = (bf16[30,2,32,128]{3,2,1,0:T(8,128)(2,1)S(1)}, bf16[30,2,32,128]{3,2,1,0:T(8,128)(2,1)S(1)}, bf16[30,2,32,128]{3,2,1,0:T(8,128)(2,1)S(1)}, bf16[...) custom-call(bf16[32,2,16,128]{3,2,1,0:T(8,128)(2,1)S(1)} %collective, ...), custom_call_target="tpu_custom_call" | custom-call | flops 1358954496 | bytes 3145728 | tf_op jit(solution)/shard_map/pallas_call | solution.py:19
  33.7 1.9 %collective-permute-start.7 = (bf16[28,2,32,128]{3,2,1,0:T(8,128)(2,1)S(1)}, bf16[28,2,32,128]{3,2,1,0:T(8,128)(2,1)S(1)}, u32[]{:S(2)}, u32[]{:S(2)}) collective-permute-start(bf16[28,2,32,128]{3,2,1,0:T(8,128)(2,1)S(1)} %get-tuple-element.37.refs_4_.refs_2_), channel_id=1, source_target_pairs={{0,2},{2,4},{4,6},{6,8},{8,10},{10,12},{12,14},{14,16},{16,18},{18... | collective-permute-start | bytes 1376264 | tf_op jit(solution)/shard_map/ppermute | solution.py:394
  35.7 2.6 %collective-permute-start.8 = (bf16[28,2,32,128]{3,2,1,0:T(8,128)(2,1)S(1)}, bf16[28,2,32,128]{3,2,1,0:T(8,128)(2,1)S(1)}, u32[]{:S(2)}, u32[]{:S(2)}) collective-permute-start(bf16[28,2,32,128]{3,2,1,0:T(8,128)(2,1)S(1)} %get-tuple-element.38.refs_3_.refs_1_), channel_id=1, source_target_pairs={{2,0},{4,2},{6,4},{8,6},{10,8},{12,10},{14,12},{16,14},{18,16},{20... | collective-permute-start | bytes 1376264 | tf_op jit(solution)/shard_map/ppermute | solution.py:397
  38.2 2.5 %shard_map.73.refs_16_ = f32[2,8,16,128]{3,2,1,0:T(8,128)S(1)} custom-call(bf16[30,2,32,128]{3,2,1,0:T(8,128)(2,1)S(1)} %get-tuple-element.43.refs_0_, bf16[30,2,32,128]{3,2,1,0:T(8,128)(2,1)S(1)} %get-tuple-element.44.refs_1_, bf16[30,2,32,128]{3,2,1,0:T(8,128)(2,1)S(1)} %get-tuple-element.45.refs_2_, ...), custom_call_target="tpu_custom_call" | custom-call | flops 679477248 | bytes 3145728 | tf_op jit(solution)/shard_map/pallas_call | solution.py:19
  40.8 3.7 %collective-permute-done.7.refs_0_ = bf16[28,2,32,128]{3,2,1,0:T(8,128)(2,1)S(1)} collective-permute-done((bf16[28,2,32,128]{3,2,1,0:T(8,128)(2,1)S(1)}, bf16[28,2,32,128]{3,2,1,0:T(8,128)(2,1)S(1)}, u32[]{:S(2)}, u32[]{:S(2)}) %collective-permute-start.7) | collective-permute-done | bytes 458784 | tf_op jit(solution)/shard_map/ppermute | solution.py:394
  44.5 0.0 collective-permute-done.8.refs_3_
  44.5 5.4 %shard_map.74 = (bf16[26,2,32,128]{3,2,1,0:T(8,128)(2,1)S(1)}, bf16[26,2,32,128]{3,2,1,0:T(8,128)(2,1)S(1)}, bf16[26,2,32,128]{3,2,1,0:T(8,128)(2,1)S(1)}, f32[16,2,16,128]{3,2,1,0:T(8,128)}) custom-call(bf16[28,2,32,128]{3,2,1,0:T(8,128)(2,1)S(1)} %collective-permute-done.7.refs_0_, bf16[28,2,32,128]{3,2,1,0:T(8,128)(2,1)S(1)} %get-tuple-element.38.refs_3_.refs_1_, ...), custom_call_target="tpu_custom_call" | custom-call | flops 1358954496 | bytes 3145728 | tf_op jit(solution)/shard_map/pallas_call | solution.py:19
  49.9 7.3 %all-to-all-start = ((f32[32,16,128]{2,1,0:T(8,128)}), f32[32,16,128]{2,1,0:T(8,128)S(1)}, u32[]{:S(2)}, u32[]{:S(2)}) async-start(f32[32,16,128]{2,1,0:T(8,128)} %bitcast.2), calls=%async_computation | async-start | bytes 524288 | tf_op jit(solution)/shard_map/all_to_all | solution.py:487
  57.2 1.7 %shard_map.75 = (bf16[24,4,16,128]{3,2,1,0:T(8,128)(2,1)S(1)}, bf16[24,4,16,128]{3,2,1,0:T(8,128)(2,1)S(1)}) custom-call(bf16[26,2,32,128]{3,2,1,0:T(8,128)(2,1)S(1)} %get-tuple-element.46.refs_0_, bf16[26,2,32,128]{3,2,1,0:T(8,128)(2,1)S(1)} %get-tuple-element.47.refs_1_, bf16[26,2,32,128]{3,2,1,0:T(8,128)(2,1)S(1)} %get-tuple-element.48.refs_2_, ...), custom_call_target="tpu_custom_call" | custom-call | flops 679477248 | bytes 1572864 | tf_op jit(solution)/shard_map/pallas_call | solution.py:19
  59.0 1.8 %collective-permute-start.9 = (bf16[24,4,16,128]{3,2,1,0:T(8,128)(2,1)S(1)}, bf16[24,4,16,128]{3,2,1,0:T(8,128)(2,1)S(1)}, u32[]{:S(2)}, u32[]{:S(2)}) collective-permute-start(bf16[24,4,16,128]{3,2,1,0:T(8,128)(2,1)S(1)} %get-tuple-element.51), channel_id=1, source_target_pairs={{0,1},{1,0},{2,3},{3,2},{4,5},{5,4},{6,7},{7,6},{8,9},{9,8},{10,11... | collective-permute-start | bytes 1179656 | tf_op jit(solution)/shard_map/ppermute | solution.py:391
  60.8 7.1 %all-to-all-done = f32[32,16,128]{2,1,0:T(8,128)S(1)} async-done(((f32[32,16,128]{2,1,0:T(8,128)}), f32[32,16,128]{2,1,0:T(8,128)S(1)}, u32[]{:S(2)}, u32[]{:S(2)}) %all-to-all-start) | async-done | bytes 262176 | tf_op jit(solution)/shard_map/all_to_all | solution.py:487
  68.0 0.7 broadcast_in_dim.2
  68.7 3.5 %all-to-all-start.1 = ((f32[16,16,128]{2,1,0:T(8,128)}), f32[16,16,128]{2,1,0:T(8,128)S(1)}, u32[]{:S(2)}, u32[]{:S(2)}) async-start(f32[16,16,128]{2,1,0:T(8,128)} %broadcast_in_dim.2), calls=%async_computation.1 | async-start | bytes 262144 | tf_op jit(solution)/shard_map/all_to_all | solution.py:489
  72.2 0.0 collective-permute-done.9.refs_1_
  72.2 1.9 %shard_map.76 = bf16[16,4,48,128]{3,2,1,0:T(8,128)(2,1)} custom-call(bf16[24,4,16,128]{3,2,1,0:T(8,128)(2,1)S(1)} %get-tuple-element.50.refs_0_, bf16[24,4,16,128]{3,2,1,0:T(8,128)(2,1)S(1)} %collective-permute-done.9.refs_1_), custom_call_target="tpu_custom_call" | custom-call | bytes 1572864 | tf_op jit(solution)/shard_map/pallas_call | solution.py:19
  74.1 6.0 %all-to-all-done.1.sums = f32[16,16,128]{2,1,0:T(8,128)S(1)} async-done(((f32[16,16,128]{2,1,0:T(8,128)}), f32[16,16,128]{2,1,0:T(8,128)S(1)}, u32[]{:S(2)}, u32[]{:S(2)}) %all-to-all-start.1) | async-done | bytes 131104 | tf_op jit(solution)/shard_map/all_to_all | solution.py:489
  80.1 0.9 %shard_map.77 = (f32[27,16,32]{2,1,0:T(8,128)}, f32[27,16,32]{2,1,0:T(8,128)}) custom-call(f32[16,16,128]{2,1,0:T(8,128)S(1)} %all-to-all-done.1.sums), custom_call_target="tpu_custom_call" | custom-call | tf_op jit(solution)/shard_map/pallas_call | solution.py:19
  (2 shorter events, 0.0 us)
Async XLA Ops:
  0.6 1.1 %copy-start.1 = (bf16[16,4,48,128]{3,2,1,0:T(8,128)(2,1)S(1)}, bf16[16,4,48,128]{3,2,1,0:T(8,128)(2,1)}, u32[]{:S(2)}) copy-start(bf16[16,4,48,128]{3,2,1,0:T(8,128)(2,1)} %x_ref.2) | copy-start | bytes 2359300
  3.3 16.7 %collective-permute-start.1 = (bf16[32,2,16,128]{3,2,1,0:T(8,128)(2,1)S(1)}, bf16[32,2,16,128]{3,2,1,0:T(8,128)(2,1)S(1)}, u32[]{:S(2)}, u32[]{:S(2)}) collective-permute-start(bf16[32,2,16,128]{3,2,1,0:T(8,128)(2,1)S(1)} %get-tuple-element.30), channel_id=1, source_target_pairs={{0,1},{1,0},{2,3},{3,2},{4,5},{5,4},{6,7},{7,6},{8,9},{9,8},{10,11... | collective-permute-start | bytes 786440 | tf_op jit(solution)/shard_map/ppermute | solution.py:391
  6.3 13.8 %collective-permute-start.3 = (bf16[32,2,16,128]{3,2,1,0:T(8,128)(2,1)S(1)}, bf16[32,2,16,128]{3,2,1,0:T(8,128)(2,1)S(1)}, u32[]{:S(2)}, u32[]{:S(2)}) collective-permute-start(bf16[32,2,16,128]{3,2,1,0:T(8,128)(2,1)S(1)} %get-tuple-element.32), channel_id=1, source_target_pairs={{0,1},{1,0},{2,3},{3,2},{4,5},{5,4},{6,7},{7,6},{8,9},{9,8},{10,11... | collective-permute-start | bytes 786440 | tf_op jit(solution)/shard_map/ppermute | solution.py:391
  6.3 0.9 %copy-start.2 = (bf16[16,27,32]{2,0,1:T(8,128)(2,1)S(1)}, bf16[16,27,32]{2,0,1:T(8,128)(2,1)}, u32[]{:S(2)}) copy-start(bf16[16,27,32]{2,0,1:T(8,128)(2,1)} %param.6) | copy-start | bytes 82948
  7.2 0.9 %copy-start.3 = (bf16[16,27,32]{2,0,1:T(8,128)(2,1)S(1)}, bf16[16,27,32]{2,0,1:T(8,128)(2,1)}, u32[]{:S(2)}) copy-start(bf16[16,27,32]{2,0,1:T(8,128)(2,1)} %param.7) | copy-start | bytes 82948
  8.2 11.2 %collective-permute-start.4 = (bf16[14,16,128]{2,1,0:T(8,128)(2,1)S(1)}, bf16[14,16,128]{2,1,0:T(8,128)(2,1)S(1)}, u32[]{:S(2)}, u32[]{:S(2)}) collective-permute-start(bf16[14,16,128]{2,1,0:T(8,128)(2,1)S(1)} %shard_map.68.refs_0_), channel_id=1, source_target_pairs={{0,1},{1,0},{2,3},{3,2},{4,5},{5,4},{6,7},{7,6},{8,9},{9,8},{10,11... | collective-permute-start | bytes 172040 | tf_op jit(solution)/shard_map/ppermute | solution.py:391
  10.3 14.2 %collective-permute-start.5 = (bf16[32,2,16,128]{3,2,1,0:T(8,128)(2,1)S(1)}, bf16[32,2,16,128]{3,2,1,0:T(8,128)(2,1)S(1)}, u32[]{:S(2)}, u32[]{:S(2)}) collective-permute-start(bf16[32,2,16,128]{3,2,1,0:T(8,128)(2,1)S(1)} %get-tuple-element.31.after.refs_2_.refs_9_), channel_id=1, source_target_pairs={{2,0},{4,2},{6,4},{8,6},{10,8},{12,10},{14,12},{16,14},{18,16},{20... | collective-permute-start | bytes 786440 | tf_op jit(solution)/shard_map/ppermute | solution.py:397
  13.4 11.0 %collective-permute-start = (bf16[32,2,16,128]{3,2,1,0:T(8,128)(2,1)S(1)}, bf16[32,2,16,128]{3,2,1,0:T(8,128)(2,1)S(1)}, u32[]{:S(2)}, u32[]{:S(2)}) collective-permute-start(bf16[32,2,16,128]{3,2,1,0:T(8,128)(2,1)S(1)} %get-tuple-element.29.refs_4_.refs_11_), channel_id=1, source_target_pairs={{0,2},{2,4},{4,6},{6,8},{8,10},{10,12},{12,14},{14,16},{16,18},{18... | collective-permute-start | bytes 786440 | tf_op jit(solution)/shard_map/ppermute | solution.py:394
  13.4 1.4 %copy-start = (bf16[32,4,48,128]{3,2,1,0:T(8,128)(2,1)S(1)}, bf16[32,4,48,128]{3,2,1,0:T(8,128)(2,1)}, u32[]{:S(2)}) copy-start(bf16[32,4,48,128]{3,2,1,0:T(8,128)(2,1)} %x_ref.3) | copy-start | bytes 4718596
  20.0 8.7 %collective-permute-start.2 = (bf16[32,2,16,128]{3,2,1,0:T(8,128)(2,1)S(1)}, bf16[32,2,16,128]{3,2,1,0:T(8,128)(2,1)S(1)}, u32[]{:S(2)}, u32[]{:S(2)}) collective-permute-start(bf16[32,2,16,128]{3,2,1,0:T(8,128)(2,1)S(1)} %collective-permute-done.1.refs_5_.refs_12_), channel_id=1, source_target_pairs={{0,2},{2,4},{4,6},{6,8},{8,10},{10,12},{12,14},{14,16},{16,18},{18... | collective-permute-start | bytes 786440 | tf_op jit(solution)/shard_map/ppermute | solution.py:394
  20.0 8.6 %collective-permute-start.6 = (bf16[32,2,16,128]{3,2,1,0:T(8,128)(2,1)S(1)}, bf16[32,2,16,128]{3,2,1,0:T(8,128)(2,1)S(1)}, u32[]{:S(2)}, u32[]{:S(2)}) collective-permute-start(bf16[32,2,16,128]{3,2,1,0:T(8,128)(2,1)S(1)} %shard_map.71.refs_3_.refs_10_), channel_id=1, source_target_pairs={{2,0},{4,2},{6,4},{8,6},{10,8},{12,10},{14,12},{16,14},{18,16},{20... | collective-permute-start | bytes 786440 | tf_op jit(solution)/shard_map/ppermute | solution.py:397
  33.7 10.8 %collective-permute-start.7 = (bf16[28,2,32,128]{3,2,1,0:T(8,128)(2,1)S(1)}, bf16[28,2,32,128]{3,2,1,0:T(8,128)(2,1)S(1)}, u32[]{:S(2)}, u32[]{:S(2)}) collective-permute-start(bf16[28,2,32,128]{3,2,1,0:T(8,128)(2,1)S(1)} %get-tuple-element.37.refs_4_.refs_2_), channel_id=1, source_target_pairs={{0,2},{2,4},{4,6},{6,8},{8,10},{10,12},{12,14},{14,16},{16,18},{18... | collective-permute-start | bytes 1376264 | tf_op jit(solution)/shard_map/ppermute | solution.py:394
  35.7 8.8 %collective-permute-start.8 = (bf16[28,2,32,128]{3,2,1,0:T(8,128)(2,1)S(1)}, bf16[28,2,32,128]{3,2,1,0:T(8,128)(2,1)S(1)}, u32[]{:S(2)}, u32[]{:S(2)}) collective-permute-start(bf16[28,2,32,128]{3,2,1,0:T(8,128)(2,1)S(1)} %get-tuple-element.38.refs_3_.refs_1_), channel_id=1, source_target_pairs={{2,0},{4,2},{6,4},{8,6},{10,8},{12,10},{14,12},{16,14},{18,16},{20... | collective-permute-start | bytes 1376264 | tf_op jit(solution)/shard_map/ppermute | solution.py:397
  49.9 18.0 %all-to-all-start = ((f32[32,16,128]{2,1,0:T(8,128)}), f32[32,16,128]{2,1,0:T(8,128)S(1)}, u32[]{:S(2)}, u32[]{:S(2)}) async-start(f32[32,16,128]{2,1,0:T(8,128)} %bitcast.2), calls=%async_computation | async-start | bytes 524288 | tf_op jit(solution)/shard_map/all_to_all | solution.py:487
  59.0 13.2 %collective-permute-start.9 = (bf16[24,4,16,128]{3,2,1,0:T(8,128)(2,1)S(1)}, bf16[24,4,16,128]{3,2,1,0:T(8,128)(2,1)S(1)}, u32[]{:S(2)}, u32[]{:S(2)}) collective-permute-start(bf16[24,4,16,128]{3,2,1,0:T(8,128)(2,1)S(1)} %get-tuple-element.51), channel_id=1, source_target_pairs={{0,1},{1,0},{2,3},{3,2},{4,5},{5,4},{6,7},{7,6},{8,9},{9,8},{10,11... | collective-permute-start | bytes 1179656 | tf_op jit(solution)/shard_map/ppermute | solution.py:391
  68.7 11.4 %all-to-all-start.1 = ((f32[16,16,128]{2,1,0:T(8,128)}), f32[16,16,128]{2,1,0:T(8,128)S(1)}, u32[]{:S(2)}, u32[]{:S(2)}) async-start(f32[16,16,128]{2,1,0:T(8,128)} %broadcast_in_dim.2), calls=%async_computation.1 | async-start | bytes 262144 | tf_op jit(solution)/shard_map/all_to_all | solution.py:489

commit v5 on v4

--- a/solution.py
+++ b/solution.py
@@ -13,7 +13,7 @@
 LIMIT = 16 * 1024 * 1024
 
 
-def call(kernel, outs, args, scratch=(), flops=0, moved=0, loose=0, same=None):
+def call(kernel, outs, args, scratch=(), flops=0, moved=0, loose=0, same=None, limit=LIMIT):
     whole = pl.BlockSpec(memory_space=pltpu.VMEM)
     still = pl.BlockSpec(memory_space=pl.ANY)
     return pl.pallas_call(
@@ -23,7 +23,7 @@
         out_specs=[whole if same is None else still] * len(outs),
         input_output_aliases=same or {},
         scratch_shapes=list(scratch),
-        compiler_params=pltpu.CompilerParams(vmem_limit_bytes=LIMIT),
+        compiler_params=pltpu.CompilerParams(vmem_limit_bytes=limit),
         cost_estimate=pl.CostEstimate(flops=flops, bytes_accessed=moved, transcendentals=0),
     )(*args)
 
@@ -43,13 +43,13 @@
         body(k)
 
 
-def widened(x_ref, wide):
-    count, planes, rows = x_ref.shape[:3]
+def widened(x_ref, wide, low, count):
+    planes, rows = x_ref.shape[1:3]
 
     def widen(i):
         for x in range(planes):
-            start = pl.multiple_of((i * planes + x) * rows, 8)
-            wide[pl.ds(start, rows), :] = x_ref[i, x].astype(F32)
+            start = pl.multiple_of(((low + i) * planes + x) * rows, 8)
+            wide[pl.ds(start, rows), :] = x_ref[low + i, x].astype(F32)
 
     in_blocks(count, widen)
 
@@ -66,53 +66,65 @@
     in_blocks(length, one)
 
 
-def field_kernel(extent, margin, x_ref, *refs):
-    outs, wide = refs[:-1], refs[-1]
+def field_kernel(extent, margin, x_ref, first_ref, second_ref, *refs):
+    outs = refs[:-6]
+    wide, held, first, second, field_done, weight_done = refs[-6:]
     count, planes, rows = x_ref.shape[:3]
     pairs = planes // 2
     share = rows // extent
-    widened(x_ref, wide)
+    length = share + 2 * margin
+    cuts = field_done.shape[0]
+    step = count // cuts
+    fields = []
+    for c in range(cuts):
+        part = pl.ds(c * step, step)
+        fields.append(pltpu.make_async_copy(x_ref.at[part], held.at[part], field_done.at[c]))
+        fields[-1].start()
+    weights = [
+        pltpu.make_async_copy(first_ref, first, weight_done.at[0]),
+        pltpu.make_async_copy(second_ref, second, weight_done.at[1]),
+    ]
+    for copy in weights:
+        copy.start()
+    for c in range(cuts):
+        fields[c].wait()
+        widened(held, wide, c * step, step)
     me = lax.axis_index("chan")
     for s in range(extent):
         base = lax.rem(me + s, extent) * share - margin + rows
-        turn(
-            wide,
-            outs[s * pairs : (s + 1) * pairs],
-            (count, planes, rows),
-            base,
-            share + 2 * margin,
-        )
-
-
-def pack_kernel(after, first, second, packed):
-    del after
+        turn(wide, outs[s * pairs : (s + 1) * pairs], (count, planes, rows), base, length)
+    for copy in weights:
+        copy.wait()
     blank = jnp.zeros(first.shape[1:], F32)
-    for h in range(packed.shape[0]):
+    for h in range(14):
         parts = []
         for ref in (first, second):
             for t in (2 * h, 2 * h + 1):
-                parts.append(ref[t].astype(F32) if t < ref.shape[0] else blank)
-        packed[h] = jnp.concatenate(parts, axis=1).astype(BF16)
-
-
-def grad_kernel(extent, margin, x_ref, *refs):
+                parts.append(ref[t].astype(F32) if t < 27 else blank)
+        tile = jnp.concatenate(parts, axis=1).astype(BF16)
+        for s in range(extent):
+            outs[(s + 1) * pairs - 1][length + h // 2, h % 2] = tile
+
+
+def grad_kernel(extent, margin, after, x_ref, *refs):
+    del after
     outs, wide = refs[:-1], refs[-1]
     count, planes, rows = x_ref.shape[:3]
     share = rows // extent
-    widened(x_ref, wide)
+    widened(x_ref, wide, 0, count)
     base = lax.axis_index("chan") * share - margin + rows
     turn(wide, outs, (count, planes, rows), base, share + 2 * margin)
 
 
 def matrix_kernel(extent, *refs):
-    packs, outs = refs[:extent], refs[extent:]
+    pieces, outs = refs[:extent], refs[extent:]
     me = lax.axis_index("chan")
-    halves = packs[0].shape[0]
-    quarter = packs[0].shape[2] // 4
+    quarter = pieces[0].shape[3] // 4
+    length = pieces[0].shape[0] - 7
     taps = []
     turned = []
-    for h in range(halves):
-        tiles = [pack[h].astype(F32) for pack in packs]
+    for h in range(14):
+        tiles = [piece[length + h // 2, h % 2].astype(F32) for piece in pieces]
         own = jnp.concatenate(tiles, axis=0)
         fixed = []
         for g in range(extent):
@@ -185,25 +197,28 @@
     return sig, sig * (1.0 + v * (1.0 - sig))
 
 
-def forward_kernel(groups, pairs, *refs):
+def forward_kernel(groups, fresh, ready, *refs):
     refs = list(refs)
-    fields = [[refs.pop(0) for _ in range(groups)] for _ in range(pairs + 2)]
-    grads = [refs.pop(0) for _ in range(pairs)]
+    fields = [[refs.pop(0) for _ in range(groups)] for _ in range(fresh + 1)]
+    hiddens = [refs.pop(0) for _ in range(ready)]
+    count = fresh + ready - 1
+    grads = [refs.pop(0) for _ in range(count)]
     first, second = refs.pop(0), refs.pop(0)
-    hiddens = [refs.pop(0) for _ in range(pairs + 1)]
-    slopes = [refs.pop(0) for _ in range(pairs + 1)]
-    deltas = [refs.pop(0) for _ in range(pairs)]
+    made = [refs.pop(0) for _ in range(fresh)]
+    slopes = [refs.pop(0) for _ in range(fresh)]
+    deltas = refs
+    hiddens = hiddens + made
 
     def one(r):
         row = 2 * r
         for p, sums in enumerate(taps(first[...], fields, row)):
             for q, v in enumerate(sums):
                 sig, slope = silu_parts(v)
-                shape = hiddens[p].shape[1:]
-                hiddens[p][row + q] = (v * sig).astype(BF16).reshape(shape)
+                shape = made[p].shape[1:]
+                made[p][row + q] = (v * sig).astype(BF16).reshape(shape)
                 slopes[p][row + q] = slope.astype(BF16).reshape(shape)
 
-    in_blocks(hiddens[0].shape[0] // 2, one)
+    in_blocks(made[0].shape[0] // 2, one)
 
     def two(r):
         row = 2 * r
@@ -214,7 +229,8 @@
                 slope = silu_parts(v)[1].reshape(shape)
                 deltas[p][row + q] = (out_grad * slope).astype(BF16)
 
-    in_blocks(deltas[0].shape[0] // 2, two)
+    if count > 0:
+        in_blocks(deltas[0].shape[0] // 2, two)
 
 
 def planes_of(pairs):
@@ -275,8 +291,8 @@
                 )
                 taps_of += [part[:, e * channels : (e + 1) * channels] for e in range(3)]
         blank = jnp.zeros((size, channels), F32)
-        taps_of += [blank] * 5
-        groups.append([jnp.concatenate(taps_of[4 * h : 4 * h + 4], axis=1) for h in range(8)])
+        taps_of.append(blank)
+        groups.append([jnp.concatenate(taps_of[4 * h : 4 * h + 4], axis=1) for h in range(7)])
     return groups
 
 
@@ -291,34 +307,58 @@
             raw[g, h] = tile
 
 
-def back_kernel(share, groups, pairs, *refs):
-    refs = list(refs)
-    deltas = [[refs.pop(0)] for _ in range(pairs + 2)]
-    slopes = [refs.pop(0) for _ in range(pairs + 1)]
-    fields = [[refs.pop(0) for _ in range(groups)] for _ in range(pairs + 2)]
-    weight, second = refs.pop(0), refs.pop(0)
-    firsts = [refs.pop(0) for _ in range(pairs + 1)]
-    sent, total = refs
-
+def first_deltas(weight, deltas, slopes, firsts):
     def one(r):
         row = 2 * r
-        for p, sums in enumerate(taps(weight[...], deltas, row)):
+        for p, sums in enumerate(taps(weight[...], [[delta] for delta in deltas], row)):
             for q, v in enumerate(sums):
                 shape = firsts[p].shape[1:]
                 slope = slopes[p][row + 2 + q].astype(F32)
                 firsts[p][row + q] = (v.reshape(shape) * slope).astype(BF16)
 
     in_blocks(firsts[0].shape[0] // 2, one)
+
+
+def back_kernel(count, *refs):
+    weight, refs = refs[0], refs[1:]
+    first_deltas(
+        weight, refs[: count + 1], refs[count + 1 : 2 * count + 1], refs[2 * count + 1 :]
+    )
+
+
+def first_kernel(share, groups, pairs, *refs):
+    refs = list(refs)
+    weight = refs.pop(0)
+    deltas = [refs.pop(0) for _ in range(2)]
+    slope = refs.pop(0)
+    later = [refs.pop(0) for _ in range(pairs)]
+    fields = [[refs.pop(0) for _ in range(groups)] for _ in range(pairs + 2)]
+    second = refs.pop(0)
+    first, keep, send, total = refs
+    first_deltas(weight, deltas, [slope], [first])
     near = planes_of(fields)[1:-1]
-    own = planes_of([[first] for first in firsts])[1:-1]
+    own = planes_of([[ref] for ref in [first] + later])[1:-1]
     weight_loop(total, near, 3, own, 1, share)
-    extent, size = sent.shape[1:3]
+    extent, halves, size = keep.shape[:3]
     me = lax.axis_index("chan")
-    for g, tiles in enumerate(weight_fold(total, size)):
-        there = lax.rem(me + extent - g, extent)
-        for h, tile in enumerate(tiles):
-            sent[h, there] = tile
-            sent[8 + h, g] = second[g, h]
+    groups_of = weight_fold(total, size)
+
+    def place(ours, theirs):
+        for g, tiles in enumerate(groups_of):
+            there = lax.rem(me + extent - g, extent)
+            for h in range(halves):
+                ours[g, h] = tiles[h]
+                theirs[g, h] = second[there, h]
+
+    odd = lax.rem(lax.axis_index("slab"), 2)
+
+    @pl.when(odd == 0)
+    def _():
+        place(keep, send)
+
+    @pl.when(odd == 1)
+    def _():
+        place(send, keep)
 
 
 def last_kernel(pairs, *refs):
@@ -341,12 +381,37 @@
     in_blocks(outs[0].shape[0] // 2, one)
 
 
-def finish_kernel(factor, sums, first, second):
+def finish_kernel(factor, mine, other, first, second):
     channels = first.shape[2]
-    for k, out in enumerate((first, second)):
-        for t in range(27):
-            low = t % 4 * channels
-            out[t] = sums[8 * k + t // 4, :, low : low + channels] * factor
+
+    def place(ours, theirs):
+        for out, sums in ((ours, mine), (theirs, other)):
+            for t in range(27):
+                low = t % 4 * channels
+                out[t] = sums[t // 4, :, low : low + channels] * factor
+
+    odd = lax.rem(lax.axis_index("slab"), 2)
+
+    @pl.when(odd == 0)
+    def _():
+        place(first, second)
+
+    @pl.when(odd == 1)
+    def _():
+        place(second, first)
+
+
+def split_kernel(after, one, two, *outs):
+    del after
+    for g, out in enumerate(outs):
+        out[...] = one[g] + two[g]
+
+
+def add_kernel(*refs):
+    values = [ref[...] for ref in refs[:-1]]
+    while len(values) > 1:
+        values = [sum(values[k + 1 : k + 2], values[k]) for k in range(0, len(values), 2)]
+    refs[-1][...] = values[0]
 
 
 def relay_kernel(*refs):
@@ -396,40 +461,54 @@
     def to_prev(value):
         return lax.ppermute(value, "slab", [((i + 1) % slabs, i) for i in range(slabs)])
 
+    def relayed(value, *others):
+        shape = jax.ShapeDtypeStruct(value.shape, value.dtype)
+        early = [value, *others]
+        return call(relay_kernel, [shape], early, loose=len(early), same={0: 0})[0]
+
     piece = jax.ShapeDtypeStruct((share + 8, 2, size, depth), BF16)
-    halves = 14
+    longer = jax.ShapeDtypeStruct((share + 15, 2, size, depth), BF16)
+    by_tap = (27, size, channels)
+    cuts = 4 if size % 4 == 0 else 1
     made = call(
         functools.partial(field_kernel, extent, 4),
-        [piece] * (extent * pairs),
-        [field],
-        [pltpu.VMEM((size * planes * rows, depth), F32)],
+        ([piece] * (pairs - 1) + [longer]) * extent,
+        [field, jnp.transpose(first_weight, (1, 0, 2)), jnp.transpose(second_weight, (1, 0, 2))],
+        [
+            pltpu.VMEM((size * planes * rows, depth), F32),
+            pltpu.VMEM(field.shape, BF16),
+            pltpu.VMEM(by_tap, BF16),
+            pltpu.VMEM(by_tap, BF16),
+            pltpu.SemaphoreType.DMA((cuts,)),
+            pltpu.SemaphoreType.DMA((2,)),
+        ],
         moved=field.size * 6,
-    )
-    parts = [made[:pairs]]
+        loose=3,
+        limit=60 * 1024 * 1024,
+    )
+    parts = [list(made[:pairs])]
     for j in range(1, extent):
-        parts.append([to_chan(piece, j) for piece in made[j * pairs : (j + 1) * pairs]])
-    (pack,) = call(
-        pack_kernel,
-        [jax.ShapeDtypeStruct((halves, size, 4 * channels), BF16)],
-        [made[0], jnp.transpose(first_weight, (1, 0, 2)), jnp.transpose(second_weight, (1, 0, 2))],
-        loose=1,
-    )
-    packs = [pack] + [to_chan(pack, j) for j in range(1, extent)]
+        sent = made[j * pairs : (j + 1) * pairs]
+        parts.append([to_chan(value, j) for value in reversed(sent)][::-1])
     matrix = jax.ShapeDtypeStruct((6 * channels, 12 * channels), BF16)
     first_wide, second_wide, first_back, second_back = call(
-        functools.partial(matrix_kernel, extent), [matrix] * 4, packs, moved=matrix.size * 8
-    )
+        functools.partial(matrix_kernel, extent),
+        [matrix] * 4,
+        [part[-1] for part in parts],
+        moved=matrix.size * 8,
+    )
+    arrived = parts[-1]
     grad_piece = jax.ShapeDtypeStruct((share + 4, 2, channels, depth), BF16)
     grads = call(
         functools.partial(grad_kernel, extent, 2),
         [grad_piece] * pairs,
-        [out_grad],
+        [arrived[-1], out_grad],
         [pltpu.VMEM((channels * planes * rows, depth), F32)],
         moved=out_grad.size * 4,
-    )
-    if extent > 1:
-        early = [parts[1][0], first_wide, grads[0]]
-        (parts[1][0],) = call(relay_kernel, [piece], early, loose=3, same={0: 0})
+        loose=1,
+    )
+    if extent > 1 and pairs > 1:
+        arrived[0] = relayed(arrived[0], grads[0])
     by_pair = [[parts[j][p] for j in range(extent)] for p in range(pairs)]
     groups = extent
     if size % 16 != 0:
@@ -439,77 +518,117 @@
     after = [to_prev(piece) for piece in by_pair[0]]
     fields = [before] + by_pair + [after]
 
-    def many(count, rows_each, dtype=BF16):
-        return [jax.ShapeDtypeStruct((rows_each, 2, channels, depth), dtype)] * count
-
-    flat_fields = [piece for pieces in fields for piece in pieces]
-    work = 2 * 27 * channels * channels * depth
+    def many(count, rows_each):
+        return [jax.ShapeDtypeStruct((rows_each, 2, channels, depth), BF16)] * count
+
+    def flat(lists):
+        return [piece for pieces in lists for piece in pieces]
+
+    work = 27 * 2 * channels * channels * depth * 2
+    space = 4 * channels * depth * share
+
     made = call(
-        functools.partial(forward_kernel, groups, pairs),
-        many(pairs + 1, share + 6) * 2 + many(pairs, share + 4),
-        flat_fields + list(grads) + [first_wide, second_wide],
-        flops=work * 2 * planes * share,
-        moved=8 * planes * share * channels * depth,
-    )
-    hiddens = made[: pairs + 1]
-    slopes = made[pairs + 1 : 2 * pairs + 2]
-    deltas = made[2 * pairs + 2 :]
-    all_deltas = [to_next(deltas[-1])] + list(deltas) + [to_prev(deltas[0])]
-
-    raw = jax.ShapeDtypeStruct((extent, 8, size, 4 * channels), F32)
-    ready = jax.ShapeDtypeStruct((16, extent, size, 4 * channels), F32)
+        functools.partial(forward_kernel, groups, pairs, 0),
+        many(2 * pairs, share + 6) + many(pairs - 1, share + 4),
+        flat(fields[: pairs + 1]) + list(grads[: pairs - 1]) + [first_wide, second_wide],
+        flops=work * (2 * pairs - 1) * share,
+        moved=space * 4 * pairs,
+    )
+    hiddens, slopes, deltas = made[:pairs], made[pairs : 2 * pairs], made[2 * pairs :]
+    made = call(
+        functools.partial(forward_kernel, groups, 1, 1),
+        many(2, share + 6) + many(1, share + 4),
+        flat(fields[pairs:]) + [hiddens[-1], grads[-1], first_wide, second_wide],
+        flops=work * 2 * share,
+        moved=space * 6,
+    )
+    hiddens = list(hiddens) + [made[0]]
+    slopes = list(slopes) + [made[1]]
+    deltas = list(deltas) + [made[2]]
+    delta_after = to_prev(deltas[0])
+    delta_before = to_next(deltas[-1])
+
+    raw = jax.ShapeDtypeStruct((extent, 7, size, 4 * channels), F32)
     total = pltpu.VMEM((6 * channels, 12 * channels), F32)
     (second_raw,) = call(
         functools.partial(second_kernel, share, pairs),
         [raw],
-        list(hiddens) + list(deltas),
+        hiddens + deltas,
         [total],
-        flops=work * planes * share,
-        moved=8 * planes * share * channels * depth,
-    )
-    made = call(
-        functools.partial(back_kernel, share, groups, pairs),
-        many(pairs + 1, share + 2) + [ready],
-        all_deltas + list(slopes) + flat_fields + [second_back, second_raw],
+        flops=work * pairs * share,
+        moved=space * 5,
+    )
+    later = call(
+        functools.partial(back_kernel, pairs),
+        many(pairs, share + 2),
+        [second_back] + deltas + [delta_after] + slopes[1:],
+        flops=work * pairs * share,
+        moved=space * 3 * pairs,
+    )
+    first, keep, send = call(
+        functools.partial(first_kernel, share, groups, pairs),
+        many(1, share + 2) + [raw] * 2,
+        [second_back, delta_before, deltas[0], slopes[0]]
+        + list(later)
+        + flat(fields)
+        + [second_raw],
         [total],
-        flops=work * 2 * planes * share,
-        moved=8 * planes * share * channels * depth,
-    )
-    firsts, sent = made[:-1], made[-1]
-
-    wide = 4 * channels
-    lines = 16 * size // slabs
-    if lines * slabs == 16 * size:
-        if lines != size:
-            sent = jnp.swapaxes(sent, 0, 1).reshape(extent, slabs, lines, wide)
-            sent = jnp.swapaxes(sent, 0, 1)
-        sent = sent.reshape(slabs * extent, lines, wide)
-        got = lax.all_to_all(sent, ("slab", "chan"), 0, 0, tiled=True)
-        own = jnp.sum(got, axis=0, keepdims=True)
-        sums = lax.all_to_all(
-            jnp.broadcast_to(own, (slabs, lines, wide)), "slab", 0, 0, tiled=True
-        )
-    else:
-        sums = lax.psum(sent, ("slab", "chan"))
-        sums = lax.dynamic_index_in_dim(sums, me, axis=1, keepdims=False)
-    sums = sums.reshape(16, size, wide)
-    by_tap = jax.ShapeDtypeStruct((27, size, channels), F32)
-    first_grad, second_grad = call(
-        functools.partial(finish_kernel, factor), [by_tap] * 2, [sums]
-    )
-    first_grad, second_grad = (jnp.transpose(g, (1, 0, 2)) for g in (first_grad, second_grad))
-
+        flops=work * (pairs + 1) * share,
+        moved=space * 4 * pairs,
+    )
+
+    def stepped(value, stride, shift=0):
+        if shift % extent == 0:
+            return lax.ppermute(value, "slab", [(i, i ^ stride) for i in range(slabs)])
+        pairs_of = []
+        for i in range(slabs):
+            for k in range(extent):
+                there = (i ^ stride) * extent + (k + shift) % extent
+                pairs_of.append((i * extent + k, there))
+        return lax.ppermute(value, ("slab", "chan"), pairs_of)
+
+    portion = jax.ShapeDtypeStruct(raw.shape[1:], F32)
     out_piece = jax.ShapeDtypeStruct((share, planes, size, depth), BF16)
     made = call(
         functools.partial(last_kernel, pairs),
         [out_piece] * extent,
-        list(firsts) + [first_back],
-        flops=work * planes * share,
-        moved=4 * planes * share * channels * depth,
-    )
+        [first] + list(later) + [first_back],
+        flops=work * pairs * share,
+        moved=space * 2 * pairs,
+    )
+    plain = slabs & (slabs - 1) == 0 and slabs >= 4
+    if plain:
+        kept = call(split_kernel, [portion] * extent, [made[0], keep, stepped(send, 1)], loose=1)
+        shares = [kept[0]] + [to_chan(kept[j], extent - j) for j in range(1, extent)]
+        shares += [stepped(kept[j], 2, extent - j) for j in range(extent)]
+        (mine,) = call(add_kernel, [portion], shares)
+        made = [made[0]] + [relayed(value, mine) for value in made[1:]]
     pieces = [made[0]] + [None] * (extent - 1)
     for j in range(1, extent):
         pieces[extent - j] = to_chan(made[j], extent - j)
+    if plain:
+        stride = 4
+        while stride < slabs:
+            radix = 4 if slabs % (4 * stride) == 0 else 2
+            got = [mine] + [stepped(mine, m * stride) for m in range(1, radix)]
+            (mine,) = call(add_kernel, [portion], got)
+            stride *= radix
+        other = stepped(mine, 1)
+    else:
+        mine, other = keep[0], send[0]
+        for j in range(1, extent):
+            mine, other = mine + to_chan(keep[j], extent - j), other + to_chan(send[j], extent - j)
+        even = lax.rem(lax.axis_index("slab"), 2) == 0
+        mine, other = jnp.where(even, mine, other), jnp.where(even, other, mine)
+        mine, other = lax.psum((mine, other), "slab")
+        mine, other = jnp.where(even, mine, other), jnp.where(even, other, mine)
+    first_grad, second_grad = call(
+        functools.partial(finish_kernel, factor),
+        [jax.ShapeDtypeStruct(by_tap, F32)] * 2,
+        [mine, other],
+    )
+    first_grad, second_grad = (jnp.transpose(g, (1, 0, 2)) for g in (first_grad, second_grad))
+
     (input_grad,) = call(
         functools.partial(merge_kernel, extent),
         [jax.ShapeDtypeStruct(field.shape, BF16)],

time: 81.3 us -> 72.7 us (0.89)
  starting transfers between devices: 29.9 us -> 23 us
  local copies, waits for them, and re-layouts: 4.99 us -> 1.41 us
  Pallas kernels: 21 us -> 24.1 us
  waiting for transfers between devices: 24.2 us -> 23.3 us
    all_to_all x2 -> x0, waiting for transfers between devices: 13.1 us -> none  [the longest x1 7.12 us: body(): got = lax.all_to_all(sent, ('slab', 'chan'), 0, 0, tiled=True)]
    all_to_all x2 -> x0, starting transfers between devices: 10.8 us -> none  [the longest x1 7.31 us: body(): got = lax.all_to_all(sent, ('slab', 'chan'), 0, 0, tiled=True)]
    ppermute x0 -> x7, starting transfers between devices: none -> 10.6 us  [the longest x6 7.63 us: stepped(): return lax.ppermute(value, 'slab', [(i, i ^ stride) for i in range(slabs)])]
    ppermute x0 -> x7, waiting for transfers between devices: none -> 7.52 us  [the longest x6 7.33 us: stepped(): return lax.ppermute(value, 'slab', [(i, i ^ stride) for i in range(slabs)])]
    ppermute x4, waiting for transfers between devices: 3.28 us -> 10.1 us  [to_chan(): lax.ppermute(value, 'chan', [(i, (i + shift) % extent) for i in range(ext...]
    ppermute x3, starting transfers between devices: 10.1 us -> 6.61 us  [to_prev(): lax.ppermute(value, 'slab', [((i + 1) % slabs, i) for i in range(slabs)])]
    pallas_call x11 -> x16, Pallas kernels: 21 us -> 24.1 us  [call(): pl.pallas_call(kernel, out_shape=outs, in_specs=[still] * loose + [whole]...]
    unnamed x8 -> x6, local copies, waits for them, and re-layouts: 4.33 us -> 1.41 us
  transfers between devices with their start and end apart: 12 -> 17, of which waited for: 5 -> 10; matrix products, arithmetic and copies ran while one was open for 1% -> 0% of each run, Pallas kernels for 10% -> 21%
where the time goes in v5:
time: 72.7 us; the launch traced here: 72.6 us
  Pallas kernels  24.1 us (33%)
  waiting for transfers between devices  23.3 us (32%)
  starting transfers between devices  23 us (32%)
  local copies, waits for them, and re-layouts  1.41 us (2%)
  between operations  0.79 us (1%)
    pallas_call x16, Pallas kernels, call(): pl.pallas_call(kernel, out_shape=outs, in_specs=[still] * loose + [whole]...  24.1 us
    ppermute x4, waiting for transfers between devices, to_chan(): lax.ppermute(value, 'chan', [(i, (i + shift) % extent) for i in range(ext...  10.1 us
    ppermute x6, starting transfers between devices, stepped(): return lax.ppermute(value, 'slab', [(i, i ^ stride) for i in range(slabs)])  7.63 us
    ppermute x6, waiting for transfers between devices, stepped(): return lax.ppermute(value, 'slab', [(i, i ^ stride) for i in range(slabs)])  7.33 us
    ppermute x3, starting transfers between devices, to_prev(): lax.ppermute(value, 'slab', [((i + 1) % slabs, i) for i in range(slabs)])  6.61 us
    ppermute x3, waiting for transfers between devices, to_next(): lax.ppermute(value, 'slab', [(i, (i + 1) % slabs) for i in range(slabs)])  5.62 us
    ppermute x4, starting transfers between devices, to_chan(): lax.ppermute(value, 'chan', [(i, (i + shift) % extent) for i in range(ext...  4.3 us
    ppermute x1, starting transfers between devices, stepped(): return lax.ppermute(value, ('slab', 'chan'), pairs_of)  2.94 us
  transfers between devices with their start and end apart: 17, of which 10 were waited for; matrix products, arithmetic and copies ran while one was open for 0% of the time, Pallas kernels for 21%

profile of v5, /device:TPU:0, one launch (start us, length us, event | category | flops | bytes accessed | tf_op | source)
XLA Modules:
  0.0 72.6 jit_solution(6142930760387441836)
XLA Ops:
  0.6 3.7 %shard_map.67 = (bf16[32,2,16,128]{3,2,1,0:T(8,128)(2,1)}, bf16[39,2,16,128]{3,2,1,0:T(8,128)(2,1)}, bf16[32,2,16,128]{3,2,1,0:T(8,128)(2,1)}, bf16[39,2,16,128]{3,2,1,0:T(8,128)(2,1)}) custom-call(bf16[16,4,48,128]{3,2,1,0:T(8,128)(2,1)} %x_ref.2, bf16[27,16,32]{2,1,0:T(8,128)(2,1)} %bitcast.4, bf16[27,16,32]{2,1,0:T(8,128)(2,1)} %bitcast.5), custom_call_target="tpu_custom_call" | custom-call | bytes 2359296 | tf_op jit(solution)/shard_map/pallas_call | solution.py:19
  4.4 3.0 %collective-permute-start = (bf16[39,2,16,128]{3,2,1,0:T(8,128)(2,1)}, bf16[39,2,16,128]{3,2,1,0:T(8,128)(2,1)S(1)}, u32[]{:S(2)}, u32[]{:S(2)}) collective-permute-start(bf16[39,2,16,128]{3,2,1,0:T(8,128)(2,1)} %get-tuple-element.33), channel_id=1, source_target_pairs={{0,1},{1,0},{2,3},{3,2},{4,5},{5,4},{6,7},{7,6},{8,9},{9,8},{10,11... | collective-permute-start | bytes 958472 | tf_op jit(solution)/shard_map/ppermute | solution.py:456
  7.4 0.1 collective-permute-start.2
  7.4 0.0 collective-permute-start.4
  7.4 8.5 %collective-permute-done.refs_1_.after.refs_5_.refs_11_ = bf16[39,2,16,128]{3,2,1,0:T(8,128)(2,1)S(1)} collective-permute-done((bf16[39,2,16,128]{3,2,1,0:T(8,128)(2,1)}, bf16[39,2,16,128]{3,2,1,0:T(8,128)(2,1)S(1)}, u32[]{:S(2)}, u32[]{:S(2)}) %collective-permute-start) | collective-permute-done | bytes 319520 | tf_op jit(solution)/shard_map/ppermute | solution.py:456
  15.9 0.0 collective-permute-start.5
  15.9 4.4 %collective-permute-start.1 = (bf16[32,2,16,128]{3,2,1,0:T(8,128)(2,1)}, bf16[32,2,16,128]{3,2,1,0:T(8,128)(2,1)S(1)}, u32[]{:S(2)}, u32[]{:S(2)}) collective-permute-start(bf16[32,2,16,128]{3,2,1,0:T(8,128)(2,1)} %get-tuple-element.35.refs_2_.refs_8_), channel_id=1, source_target_pairs={{2,0},{4,2},{6,4},{8,6},{10,8},{12,10},{14,12},{16,14},{18,16},{20... | collective-permute-start | bytes 786440 | tf_op jit(solution)/shard_map/ppermute | solution.py:462
  20.4 0.0 copy-start
  20.4 1.4 %copy-done = bf16[32,4,48,128]{3,2,1,0:T(8,128)(2,1)S(1)} copy-done((bf16[32,4,48,128]{3,2,1,0:T(8,128)(2,1)S(1)}, bf16[32,4,48,128]{3,2,1,0:T(8,128)(2,1)}, u32[]{:S(2)}) %copy-start) | copy-done | bytes 1572888
  21.8 0.0 copy-start.1
  21.8 0.0 copy-start.2
  21.8 1.3 %shard_map.69 = (bf16[28,2,32,128]{3,2,1,0:T(8,128)(2,1)S(1)}, bf16[28,2,32,128]{3,2,1,0:T(8,128)(2,1)S(1)}) custom-call(bf16[39,2,16,128]{3,2,1,0:T(8,128)(2,1)S(1)} %collective-permute-done.refs_1_.after.refs_5_.refs_11_, bf16[32,4,48,128]{3,2,1,0:T(8,128)(2,1)S(1)} %copy-done), custom_call_target="tpu_custom_call" | custom-call | bytes 3145728 | tf_op jit(solution)/shard_map/pallas_call | solution.py:19
  23.1 0.0 collective-permute-done.2.refs_0_
  23.1 1.0 %collective-permute-start.3 = (bf16[32,2,16,128]{3,2,1,0:T(8,128)(2,1)S(1)}, bf16[32,2,16,128]{3,2,1,0:T(8,128)(2,1)S(1)}, u32[]{:S(2)}, u32[]{:S(2)}) collective-permute-start(bf16[32,2,16,128]{3,2,1,0:T(8,128)(2,1)S(1)} %shard_map.70.refs_3_.refs_9_), channel_id=1, source_target_pairs={{2,0},{4,2},{6,4},{8,6},{10,8},{12,10},{14,12},{16,14},{18,16},{20... | collective-permute-start | bytes 786440 | tf_op jit(solution)/shard_map/ppermute | solution.py:462
  24.1 0.0 copy-done.1
  24.1 0.5 shard_map.68
  24.6 0.0 collective-permute-done.4.refs_0_.refs_6_
  24.6 0.5 collective-permute-done.5.refs_1_.refs_7_
  25.1 0.0 copy-done.2
  25.1 3.6 %shard_map.71 = (bf16[30,2,32,128]{3,2,1,0:T(8,128)(2,1)S(1)}, bf16[30,2,32,128]{3,2,1,0:T(8,128)(2,1)S(1)}, bf16[30,2,32,128]{3,2,1,0:T(8,128)(2,1)S(1)}, bf16[...) custom-call(bf16[39,2,16,128]{3,2,1,0:T(8,128)(2,1)S(1)} %collective-permute-done.4.refs_0_.refs_6_, ...), custom_call_target="tpu_custom_call" | custom-call | flops 1019215872 | bytes 3145728 | tf_op jit(solution)/shard_map/pallas_call | solution.py:19
  28.8 1.2 %collective-permute-start.7 = (bf16[28,2,32,128]{3,2,1,0:T(8,128)(2,1)S(1)}, bf16[28,2,32,128]{3,2,1,0:T(8,128)(2,1)S(1)}, u32[]{:S(2)}, u32[]{:S(2)}) collective-permute-start(bf16[28,2,32,128]{3,2,1,0:T(8,128)(2,1)S(1)} %get-tuple-element.43.refs_1_.refs_3_.refs_2_), channel_id=1, source_target_pairs={{2,0},{4,2},{6,4},{8,6},{10,8},{12,10},{14,12},{16,14},{18,16},{20... | collective-permute-start | bytes 1376264 | tf_op jit(solution)/shard_map/ppermute | solution.py:462
  29.9 0.0 collective-permute-done.1.refs_2_.refs_12_
  29.9 0.0 collective-permute-done.3.refs_3_.refs_13_
  29.9 2.8 %shard_map.72 = (bf16[30,2,32,128]{3,2,1,0:T(8,128)(2,1)S(1)}, bf16[30,2,32,128]{3,2,1,0:T(8,128)(2,1)S(1)}, bf16[28,2,32,128]{3,2,1,0:T(8,128)(2,1)S(1)}) custom-call(bf16[39,2,16,128]{3,2,1,0:T(8,128)(2,1)S(1)} %copy-done.1, bf16[39,2,16,128]{3,2,1,0:T(8,128)(2,1)S(1)} %collective-permute-done.refs_1_.after.refs_5_.refs_11_, ...), custom_call_target="tpu_custom_call" | custom-call | flops 679477248 | bytes 2359296 | tf_op jit(solution)/shard_map/pallas_call | solution.py:19
  32.7 1.5 %collective-permute-start.6 = (bf16[28,2,32,128]{3,2,1,0:T(8,128)(2,1)S(1)}, bf16[28,2,32,128]{3,2,1,0:T(8,128)(2,1)S(1)}, u32[]{:S(2)}, u32[]{:S(2)}) collective-permute-start(bf16[28,2,32,128]{3,2,1,0:T(8,128)(2,1)S(1)} %get-tuple-element.42.refs_2_.refs_4_), channel_id=1, source_target_pairs={{0,2},{2,4},{4,6},{6,8},{8,10},{10,12},{12,14},{14,16},{16,18},{18... | collective-permute-start | bytes 1376264 | tf_op jit(solution)/shard_map/ppermute | solution.py:459
  34.2 2.5 %shard_map.74.refs_14_ = f32[2,7,16,128]{3,2,1,0:T(8,128)S(1)} custom-call(bf16[30,2,32,128]{3,2,1,0:T(8,128)(2,1)S(1)} %get-tuple-element.49.refs_0_, bf16[30,2,32,128]{3,2,1,0:T(8,128)(2,1)S(1)} %get-tuple-element.40.refs_4_.refs_1_, bf16[30,2,32,128]{3,2,1,0:T(8,128)(2,1)S(1)} %get-tuple-element.50.refs_2_, ...), custom_call_target="tpu_custom_call" | custom-call | flops 679477248 | bytes 1966080 | tf_op jit(solution)/shard_map/pallas_call | solution.py:19
  36.8 0.0 collective-permute-done.7.refs_3_
  36.8 1.6 %shard_map.73 = (bf16[26,2,32,128]{3,2,1,0:T(8,128)(2,1)S(1)}, bf16[26,2,32,128]{3,2,1,0:T(8,128)(2,1)S(1)}) custom-call(bf16[192,384]{1,0:T(8,128)(2,1)S(1)} %get-tuple-element.34.refs_0_, bf16[28,2,32,128]{3,2,1,0:T(8,128)(2,1)S(1)} %get-tuple-element.43.refs_1_.refs_3_.refs_2_, bf16[28,2,32,128]{3,2,1,0:T(8,128)(2,1)S(1)} %get-tuple-element.42.refs_2_.refs_4_, ...), custom_call_target="tpu_custom_call" | custom-call | flops 679477248 | bytes 2359296 | tf_op jit(solution)/shard_map/pallas_call | solution.py:19
  38.4 5.1 %collective-permute-done.6.refs_1_ = bf16[28,2,32,128]{3,2,1,0:T(8,128)(2,1)S(1)} collective-permute-done((bf16[28,2,32,128]{3,2,1,0:T(8,128)(2,1)S(1)}, bf16[28,2,32,128]{3,2,1,0:T(8,128)(2,1)S(1)}, u32[]{:S(2)}, u32[]{:S(2)}) %collective-permute-start.6) | collective-permute-done | bytes 458784 | tf_op jit(solution)/shard_map/ppermute | solution.py:459
  43.5 3.4 %shard_map.75 = (bf16[26,2,32,128]{3,2,1,0:T(8,128)(2,1)S(1)}, f32[2,7,16,128]{3,2,1,0:T(8,128)S(1)}, f32[2,7,16,128]{3,2,1,0:T(8,128)S(1)}) custom-call(bf16[192,384]{1,0:T(8,128)(2,1)S(1)} %get-tuple-element.34.refs_0_, bf16[28,2,32,128]{3,2,1,0:T(8,128)(2,1)S(1)} %collective-permute-done.6.refs_1_, ...), custom_call_target="tpu_custom_call" | custom-call | flops 1019215872 | bytes 3145728 | tf_op jit(solution)/shard_map/pallas_call | solution.py:19
  46.9 3.1 %collective-permute-start.8 = (f32[2,7,16,128]{3,2,1,0:T(8,128)S(1)}, f32[2,7,16,128]{3,2,1,0:T(8,128)S(1)}, u32[]{:S(2)}, u32[]{:S(2)}) collective-permute-start(f32[2,7,16,128]{3,2,1,0:T(8,128)S(1)} %get-tuple-element.56), channel_id=1, source_target_pairs={{0,2},{2,0},{4,6},{6,4},{8,10},{10,8},{12,14},{14,12},{16,18},{18,... | collective-permute-start | bytes 344072 | tf_op jit(solution)/shard_map/ppermute | solution.py:582
  50.0 1.7 %shard_map.76 = (bf16[24,4,16,128]{3,2,1,0:T(8,128)(2,1)S(1)}, bf16[24,4,16,128]{3,2,1,0:T(8,128)(2,1)S(1)}) custom-call(bf16[26,2,32,128]{3,2,1,0:T(8,128)(2,1)S(1)} %get-tuple-element.51.refs_0_, bf16[26,2,32,128]{3,2,1,0:T(8,128)(2,1)S(1)} %get-tuple-element.47.refs_4_.refs_1_, bf16[26,2,32,128]{3,2,1,0:T(8,128)(2,1)S(1)} %get-tuple-element.48.refs_5_.refs_2_, ...), custom_call_target="tpu_custom_call" | custom-call | flops 679477248 | bytes 1572864 | tf_op jit(solution)/shard_map/pallas_call | solution.py:19
  51.8 0.0 collective-permute-done.8.two
  51.8 0.1 collective-permute-start.10
  51.9 2.9 %collective-permute-start.11 = (f32[7,16,128]{2,1,0:T(8,128)S(1)}, f32[7,16,128]{2,1,0:T(8,128)S(1)}, u32[]{:S(2)}, u32[]{:S(2)}) collective-permute-start(f32[7,16,128]{2,1,0:T(8,128)S(1)} %get-tuple-element.58), channel_id=1, source_target_pairs={{0,5},{1,4},{2,7},{3,6},{4,1},{5,0},{6,3},{7,2},{8,13},{9,12},{10,... | collective-permute-start | bytes 172040 | tf_op jit(solution)/shard_map/ppermute | solution.py:588
  54.8 0.5 collective-permute-start.9
  55.4 1.8 %collective-permute-done.10.refs_2_ = f32[7,16,128]{2,1,0:T(8,128)S(1)} collective-permute-done((f32[7,16,128]{2,1,0:T(8,128)S(1)}, f32[7,16,128]{2,1,0:T(8,128)S(1)}, u32[]{:S(2)}, u32[]{:S(2)}) %collective-permute-start.10) | collective-permute-done | bytes 57376 | tf_op jit(solution)/shard_map/ppermute | solution.py:582
  57.2 0.2 collective-permute-done.11.refs_3_
  57.4 1.6 %collective-permute-done.9.refs_1_ = f32[7,16,128]{2,1,0:T(8,128)S(1)} collective-permute-done((f32[7,16,128]{2,1,0:T(8,128)S(1)}, f32[7,16,128]{2,1,0:T(8,128)S(1)}, u32[]{:S(2)}, u32[]{:S(2)}) %collective-permute-start.9) | collective-permute-done | bytes 57376 | tf_op jit(solution)/shard_map/ppermute | solution.py:456
  59.0 0.7 collective-permute-start.12
  59.7 1.6 %collective-permute-start.13 = (f32[7,16,128]{2,1,0:T(8,128)S(1)}, f32[7,16,128]{2,1,0:T(8,128)S(1)}, u32[]{:S(2)}, u32[]{:S(2)}) collective-permute-start(f32[7,16,128]{2,1,0:T(8,128)S(1)} %shard_map.78.refs_1_.refs_0_), channel_id=1, source_target_pairs={{0,8},{2,10},{4,12},{6,14},{8,0},{10,2},{12,4},{14,6},{16,24},{18,... | collective-permute-start | bytes 172040 | tf_op jit(solution)/shard_map/ppermute | solution.py:582
  61.3 1.0 %collective-permute-start.14 = (f32[7,16,128]{2,1,0:T(8,128)S(1)}, f32[7,16,128]{2,1,0:T(8,128)S(1)}, u32[]{:S(2)}, u32[]{:S(2)}) collective-permute-start(f32[7,16,128]{2,1,0:T(8,128)S(1)} %shard_map.78.refs_1_.refs_0_), channel_id=1, source_target_pairs={{0,16},{2,18},{4,20},{6,22},{8,24},{10,26},{12,28},{14,30},{16,0},... | collective-permute-start | bytes 172040 | tf_op jit(solution)/shard_map/ppermute | solution.py:582
  62.3 1.8 %collective-permute-start.15 = (f32[7,16,128]{2,1,0:T(8,128)S(1)}, f32[7,16,128]{2,1,0:T(8,128)S(1)}, u32[]{:S(2)}, u32[]{:S(2)}) collective-permute-start(f32[7,16,128]{2,1,0:T(8,128)S(1)} %shard_map.78.refs_1_.refs_0_), channel_id=1, source_target_pairs={{0,24},{2,26},{4,28},{6,30},{8,16},{10,18},{12,20},{14,22},{16,8},... | collective-permute-start | bytes 172040 | tf_op jit(solution)/shard_map/ppermute | solution.py:582
  64.1 0.2 collective-permute-done.13.refs_1_
  64.3 2.8 %collective-permute-done.14.refs_2_ = f32[7,16,128]{2,1,0:T(8,128)S(1)} collective-permute-done((f32[7,16,128]{2,1,0:T(8,128)S(1)}, f32[7,16,128]{2,1,0:T(8,128)S(1)}, u32[]{:S(2)}, u32[]{:S(2)}) %collective-permute-start.14) | collective-permute-done | bytes 57376 | tf_op jit(solution)/shard_map/ppermute | solution.py:582
  67.1 1.3 %collective-permute-done.15.refs_3_ = f32[7,16,128]{2,1,0:T(8,128)S(1)} collective-permute-done((f32[7,16,128]{2,1,0:T(8,128)S(1)}, f32[7,16,128]{2,1,0:T(8,128)S(1)}, u32[]{:S(2)}, u32[]{:S(2)}) %collective-permute-start.15) | collective-permute-done | bytes 57376 | tf_op jit(solution)/shard_map/ppermute | solution.py:582
  68.4 0.1 collective-permute-start.16
  68.5 1.2 %collective-permute-done.16.other = f32[7,16,128]{2,1,0:T(8,128)S(1)} collective-permute-done((f32[7,16,128]{2,1,0:T(8,128)S(1)}, f32[7,16,128]{2,1,0:T(8,128)S(1)}, u32[]{:S(2)}, u32[]{:S(2)}) %collective-permute-start.16) | collective-permute-done | bytes 57376 | tf_op jit(solution)/shard_map/ppermute | solution.py:582
  69.7 0.9 %shard_map.82 = (f32[27,16,32]{2,1,0:T(8,128)}, f32[27,16,32]{2,1,0:T(8,128)}) custom-call(f32[7,16,128]{2,1,0:T(8,128)S(1)} %shard_map.81.mine, f32[7,16,128]{2,1,0:T(8,128)S(1)} %collective-permute-done.16.other), custom_call_target="tpu_custom_call" | custom-call | tf_op jit(solution)/shard_map/pallas_call | solution.py:19
  70.6 0.0 collective-permute-done.12.refs_1_
  70.6 1.9 %shard_map.80 = bf16[16,4,48,128]{3,2,1,0:T(8,128)(2,1)} custom-call(bf16[24,4,16,128]{3,2,1,0:T(8,128)(2,1)S(1)} %get-tuple-element.53.after.refs_0_, bf16[24,4,16,128]{3,2,1,0:T(8,128)(2,1)S(1)} %collective-permute-done.12.refs_1_), custom_call_target="tpu_custom_call" | custom-call | bytes 1572864 | tf_op jit(solution)/shard_map/pallas_call | solution.py:19
  (5 shorter events, 0.1 us)
Async XLA Ops:
  4.4 11.6 %collective-permute-start = (bf16[39,2,16,128]{3,2,1,0:T(8,128)(2,1)}, bf16[39,2,16,128]{3,2,1,0:T(8,128)(2,1)S(1)}, u32[]{:S(2)}, u32[]{:S(2)}) collective-permute-start(bf16[39,2,16,128]{3,2,1,0:T(8,128)(2,1)} %get-tuple-element.33), channel_id=1, source_target_pairs={{0,1},{1,0},{2,3},{3,2},{4,5},{5,4},{6,7},{7,6},{8,9},{9,8},{10,11... | collective-permute-start | bytes 958472 | tf_op jit(solution)/shard_map/ppermute | solution.py:456
  7.4 15.7 %collective-permute-start.2 = (bf16[32,2,16,128]{3,2,1,0:T(8,128)(2,1)}, bf16[32,2,16,128]{3,2,1,0:T(8,128)(2,1)S(1)}, u32[]{:S(2)}, u32[]{:S(2)}) collective-permute-start(bf16[32,2,16,128]{3,2,1,0:T(8,128)(2,1)} %get-tuple-element.36), channel_id=1, source_target_pairs={{0,1},{1,0},{2,3},{3,2},{4,5},{5,4},{6,7},{7,6},{8,9},{9,8},{10,11... | collective-permute-start | bytes 786440 | tf_op jit(solution)/shard_map/ppermute | solution.py:456
  7.4 17.2 %collective-permute-start.4 = (bf16[39,2,16,128]{3,2,1,0:T(8,128)(2,1)}, bf16[39,2,16,128]{3,2,1,0:T(8,128)(2,1)S(1)}, u32[]{:S(2)}, u32[]{:S(2)}) collective-permute-start(bf16[39,2,16,128]{3,2,1,0:T(8,128)(2,1)} %get-tuple-element.32.refs_0_.refs_4_.refs_10_), channel_id=1, source_target_pairs={{0,2},{2,4},{4,6},{6,8},{8,10},{10,12},{12,14},{14,16},{16,18},{18... | collective-permute-start | bytes 958472 | tf_op jit(solution)/shard_map/ppermute | solution.py:459
  15.9 9.2 %collective-permute-start.5 = (bf16[39,2,16,128]{3,2,1,0:T(8,128)(2,1)S(1)}, bf16[39,2,16,128]{3,2,1,0:T(8,128)(2,1)S(1)}, u32[]{:S(2)}, u32[]{:S(2)}) collective-permute-start(bf16[39,2,16,128]{3,2,1,0:T(8,128)(2,1)S(1)} %collective-permute-done.refs_1_.after.refs_5_.refs_11_), channel_id=1, source_target_pairs={{0,2},{2,4},{4,6},{6,8},{8,10},{10,12},{12,14},{14,16},{16,18},{18... | collective-permute-start | bytes 958472 | tf_op jit(solution)/shard_map/ppermute | solution.py:459
  15.9 14.0 %collective-permute-start.1 = (bf16[32,2,16,128]{3,2,1,0:T(8,128)(2,1)}, bf16[32,2,16,128]{3,2,1,0:T(8,128)(2,1)S(1)}, u32[]{:S(2)}, u32[]{:S(2)}) collective-permute-start(bf16[32,2,16,128]{3,2,1,0:T(8,128)(2,1)} %get-tuple-element.35.refs_2_.refs_8_), channel_id=1, source_target_pairs={{2,0},{4,2},{6,4},{8,6},{10,8},{12,10},{14,12},{16,14},{18,16},{20... | collective-permute-start | bytes 786440 | tf_op jit(solution)/shard_map/ppermute | solution.py:462
  20.4 1.4 %copy-start = (bf16[32,4,48,128]{3,2,1,0:T(8,128)(2,1)S(1)}, bf16[32,4,48,128]{3,2,1,0:T(8,128)(2,1)}, u32[]{:S(2)}) copy-start(bf16[32,4,48,128]{3,2,1,0:T(8,128)(2,1)} %x_ref.3) | copy-start | bytes 4718596
  21.8 2.3 %copy-start.1 = (bf16[39,2,16,128]{3,2,1,0:T(8,128)(2,1)S(1)}, bf16[39,2,16,128]{3,2,1,0:T(8,128)(2,1)}, u32[]{:S(2)}) copy-start(bf16[39,2,16,128]{3,2,1,0:T(8,128)(2,1)} %get-tuple-element.32.refs_0_.refs_4_.refs_10_) | copy-start | bytes 958468
  21.8 3.4 %copy-start.2 = (bf16[32,2,16,128]{3,2,1,0:T(8,128)(2,1)S(1)}, bf16[32,2,16,128]{3,2,1,0:T(8,128)(2,1)}, u32[]{:S(2)}) copy-start(bf16[32,2,16,128]{3,2,1,0:T(8,128)(2,1)} %get-tuple-element.35.refs_2_.refs_8_) | copy-start | bytes 786436
  23.1 6.8 %collective-permute-start.3 = (bf16[32,2,16,128]{3,2,1,0:T(8,128)(2,1)S(1)}, bf16[32,2,16,128]{3,2,1,0:T(8,128)(2,1)S(1)}, u32[]{:S(2)}, u32[]{:S(2)}) collective-permute-start(bf16[32,2,16,128]{3,2,1,0:T(8,128)(2,1)S(1)} %shard_map.70.refs_3_.refs_9_), channel_id=1, source_target_pairs={{2,0},{4,2},{6,4},{8,6},{10,8},{12,10},{14,12},{16,14},{18,16},{20... | collective-permute-start | bytes 786440 | tf_op jit(solution)/shard_map/ppermute | solution.py:462
  28.8 8.0 %collective-permute-start.7 = (bf16[28,2,32,128]{3,2,1,0:T(8,128)(2,1)S(1)}, bf16[28,2,32,128]{3,2,1,0:T(8,128)(2,1)S(1)}, u32[]{:S(2)}, u32[]{:S(2)}) collective-permute-start(bf16[28,2,32,128]{3,2,1,0:T(8,128)(2,1)S(1)} %get-tuple-element.43.refs_1_.refs_3_.refs_2_), channel_id=1, source_target_pairs={{2,0},{4,2},{6,4},{8,6},{10,8},{12,10},{14,12},{16,14},{18,16},{20... | collective-permute-start | bytes 1376264 | tf_op jit(solution)/shard_map/ppermute | solution.py:462
  32.7 10.8 %collective-permute-start.6 = (bf16[28,2,32,128]{3,2,1,0:T(8,128)(2,1)S(1)}, bf16[28,2,32,128]{3,2,1,0:T(8,128)(2,1)S(1)}, u32[]{:S(2)}, u32[]{:S(2)}) collective-permute-start(bf16[28,2,32,128]{3,2,1,0:T(8,128)(2,1)S(1)} %get-tuple-element.42.refs_2_.refs_4_), channel_id=1, source_target_pairs={{0,2},{2,4},{4,6},{6,8},{8,10},{10,12},{12,14},{14,16},{16,18},{18... | collective-permute-start | bytes 1376264 | tf_op jit(solution)/shard_map/ppermute | solution.py:459
  46.9 4.8 %collective-permute-start.8 = (f32[2,7,16,128]{3,2,1,0:T(8,128)S(1)}, f32[2,7,16,128]{3,2,1,0:T(8,128)S(1)}, u32[]{:S(2)}, u32[]{:S(2)}) collective-permute-start(f32[2,7,16,128]{3,2,1,0:T(8,128)S(1)} %get-tuple-element.56), channel_id=1, source_target_pairs={{0,2},{2,0},{4,6},{6,4},{8,10},{10,8},{12,14},{14,12},{16,18},{18,... | collective-permute-start | bytes 344072 | tf_op jit(solution)/shard_map/ppermute | solution.py:582
  51.8 5.4 %collective-permute-start.10 = (f32[7,16,128]{2,1,0:T(8,128)S(1)}, f32[7,16,128]{2,1,0:T(8,128)S(1)}, u32[]{:S(2)}, u32[]{:S(2)}) collective-permute-start(f32[7,16,128]{2,1,0:T(8,128)S(1)} %get-tuple-element.57.refs_0_), channel_id=1, source_target_pairs={{0,4},{2,6},{4,0},{6,2},{8,12},{10,14},{12,8},{14,10},{16,20},{18,... | collective-permute-start | bytes 172040 | tf_op jit(solution)/shard_map/ppermute | solution.py:582
  51.9 5.5 %collective-permute-start.11 = (f32[7,16,128]{2,1,0:T(8,128)S(1)}, f32[7,16,128]{2,1,0:T(8,128)S(1)}, u32[]{:S(2)}, u32[]{:S(2)}) collective-permute-start(f32[7,16,128]{2,1,0:T(8,128)S(1)} %get-tuple-element.58), channel_id=1, source_target_pairs={{0,5},{1,4},{2,7},{3,6},{4,1},{5,0},{6,3},{7,2},{8,13},{9,12},{10,... | collective-permute-start | bytes 172040 | tf_op jit(solution)/shard_map/ppermute | solution.py:588
  54.8 4.2 %collective-permute-start.9 = (f32[7,16,128]{2,1,0:T(8,128)S(1)}, f32[7,16,128]{2,1,0:T(8,128)S(1)}, u32[]{:S(2)}, u32[]{:S(2)}) collective-permute-start(f32[7,16,128]{2,1,0:T(8,128)S(1)} %get-tuple-element.58), channel_id=1, source_target_pairs={{0,1},{1,0},{2,3},{3,2},{4,5},{5,4},{6,7},{7,6},{8,9},{9,8},{10,11... | collective-permute-start | bytes 172040 | tf_op jit(solution)/shard_map/ppermute | solution.py:456
  59.0 11.6 %collective-permute-start.12 = (bf16[24,4,16,128]{3,2,1,0:T(8,128)(2,1)S(1)}, bf16[24,4,16,128]{3,2,1,0:T(8,128)(2,1)S(1)}, u32[]{:S(2)}, u32[]{:S(2)}) collective-permute-start(bf16[24,4,16,128]{3,2,1,0:T(8,128)(2,1)S(1)} %shard_map.79), channel_id=1, source_target_pairs={{0,1},{1,0},{2,3},{3,2},{4,5},{5,4},{6,7},{7,6},{8,9},{9,8},{10,11... | collective-permute-start | bytes 1179656 | tf_op jit(solution)/shard_map/ppermute | solution.py:456
  59.7 4.5 %collective-permute-start.13 = (f32[7,16,128]{2,1,0:T(8,128)S(1)}, f32[7,16,128]{2,1,0:T(8,128)S(1)}, u32[]{:S(2)}, u32[]{:S(2)}) collective-permute-start(f32[7,16,128]{2,1,0:T(8,128)S(1)} %shard_map.78.refs_1_.refs_0_), channel_id=1, source_target_pairs={{0,8},{2,10},{4,12},{6,14},{8,0},{10,2},{12,4},{14,6},{16,24},{18,... | collective-permute-start | bytes 172040 | tf_op jit(solution)/shard_map/ppermute | solution.py:582
  61.3 5.8 %collective-permute-start.14 = (f32[7,16,128]{2,1,0:T(8,128)S(1)}, f32[7,16,128]{2,1,0:T(8,128)S(1)}, u32[]{:S(2)}, u32[]{:S(2)}) collective-permute-start(f32[7,16,128]{2,1,0:T(8,128)S(1)} %shard_map.78.refs_1_.refs_0_), channel_id=1, source_target_pairs={{0,16},{2,18},{4,20},{6,22},{8,24},{10,26},{12,28},{14,30},{16,0},... | collective-permute-start | bytes 172040 | tf_op jit(solution)/shard_map/ppermute | solution.py:582
  62.3 6.1 %collective-permute-start.15 = (f32[7,16,128]{2,1,0:T(8,128)S(1)}, f32[7,16,128]{2,1,0:T(8,128)S(1)}, u32[]{:S(2)}, u32[]{:S(2)}) collective-permute-start(f32[7,16,128]{2,1,0:T(8,128)S(1)} %shard_map.78.refs_1_.refs_0_), channel_id=1, source_target_pairs={{0,24},{2,26},{4,28},{6,30},{8,16},{10,18},{12,20},{14,22},{16,8},... | collective-permute-start | bytes 172040 | tf_op jit(solution)/shard_map/ppermute | solution.py:582
  68.4 1.3 %collective-permute-start.16 = (f32[7,16,128]{2,1,0:T(8,128)S(1)}, f32[7,16,128]{2,1,0:T(8,128)S(1)}, u32[]{:S(2)}, u32[]{:S(2)}) collective-permute-start(f32[7,16,128]{2,1,0:T(8,128)S(1)} %shard_map.81.mine), channel_id=1, source_target_pairs={{0,2},{2,0},{4,6},{6,4},{8,10},{10,8},{12,14},{14,12},{16,18},{18,... | collective-permute-start | bytes 172040 | tf_op jit(solution)/shard_map/ppermute | solution.py:582

commit v6 on v5

--- a/solution.py
+++ b/solution.py
@@ -13,17 +13,17 @@
 LIMIT = 16 * 1024 * 1024
 
 
-def call(kernel, outs, args, scratch=(), flops=0, moved=0, loose=0, same=None, limit=LIMIT):
+def call(kernel, outs, args, scratch=(), flops=0, moved=0, loose=0, same=None):
     whole = pl.BlockSpec(memory_space=pltpu.VMEM)
     still = pl.BlockSpec(memory_space=pl.ANY)
     return pl.pallas_call(
         kernel,
         out_shape=outs,
         in_specs=[still] * loose + [whole] * (len(args) - loose),
-        out_specs=[whole if same is None else still] * len(outs),
+        out_specs=[still if k in (same or {}).values() else whole for k in range(len(outs))],
         input_output_aliases=same or {},
         scratch_shapes=list(scratch),
-        compiler_params=pltpu.CompilerParams(vmem_limit_bytes=limit),
+        compiler_params=pltpu.CompilerParams(vmem_limit_bytes=LIMIT),
         cost_estimate=pl.CostEstimate(flops=flops, bytes_accessed=moved, transcendentals=0),
     )(*args)
 
@@ -43,13 +43,13 @@
         body(k)
 
 
-def widened(x_ref, wide, low, count):
-    planes, rows = x_ref.shape[1:3]
+def widened(x_ref, wide):
+    count, planes, rows = x_ref.shape[:3]
 
     def widen(i):
         for x in range(planes):
-            start = pl.multiple_of(((low + i) * planes + x) * rows, 8)
-            wide[pl.ds(start, rows), :] = x_ref[low + i, x].astype(F32)
+            start = pl.multiple_of((i * planes + x) * rows, 8)
+            wide[pl.ds(start, rows), :] = x_ref[i, x].astype(F32)
 
     in_blocks(count, widen)
 
@@ -66,44 +66,33 @@
     in_blocks(length, one)
 
 
-def field_kernel(extent, margin, x_ref, first_ref, second_ref, *refs):
-    outs = refs[:-6]
-    wide, held, first, second, field_done, weight_done = refs[-6:]
+def field_kernel(extent, margin, x_ref, *refs):
+    outs, wide = refs[:-1], refs[-1]
     count, planes, rows = x_ref.shape[:3]
     pairs = planes // 2
     share = rows // extent
-    length = share + 2 * margin
-    cuts = field_done.shape[0]
-    step = count // cuts
-    fields = []
-    for c in range(cuts):
-        part = pl.ds(c * step, step)
-        fields.append(pltpu.make_async_copy(x_ref.at[part], held.at[part], field_done.at[c]))
-        fields[-1].start()
-    weights = [
-        pltpu.make_async_copy(first_ref, first, weight_done.at[0]),
-        pltpu.make_async_copy(second_ref, second, weight_done.at[1]),
-    ]
-    for copy in weights:
-        copy.start()
-    for c in range(cuts):
-        fields[c].wait()
-        widened(held, wide, c * step, step)
+    widened(x_ref, wide)
     me = lax.axis_index("chan")
     for s in range(extent):
         base = lax.rem(me + s, extent) * share - margin + rows
-        turn(wide, outs[s * pairs : (s + 1) * pairs], (count, planes, rows), base, length)
-    for copy in weights:
-        copy.wait()
+        turn(
+            wide,
+            outs[s * pairs : (s + 1) * pairs],
+            (count, planes, rows),
+            base,
+            share + 2 * margin,
+        )
+
+
+def pack_kernel(after, first, second, packed):
+    del after
     blank = jnp.zeros(first.shape[1:], F32)
-    for h in range(14):
+    for h in range(packed.shape[0]):
         parts = []
         for ref in (first, second):
             for t in (2 * h, 2 * h + 1):
-                parts.append(ref[t].astype(F32) if t < 27 else blank)
-        tile = jnp.concatenate(parts, axis=1).astype(BF16)
-        for s in range(extent):
-            outs[(s + 1) * pairs - 1][length + h // 2, h % 2] = tile
+                parts.append(ref[t].astype(F32) if t < ref.shape[0] else blank)
+        packed[h] = jnp.concatenate(parts, axis=1).astype(BF16)
 
 
 def grad_kernel(extent, margin, after, x_ref, *refs):
@@ -111,20 +100,20 @@
     outs, wide = refs[:-1], refs[-1]
     count, planes, rows = x_ref.shape[:3]
     share = rows // extent
-    widened(x_ref, wide, 0, count)
+    widened(x_ref, wide)
     base = lax.axis_index("chan") * share - margin + rows
     turn(wide, outs, (count, planes, rows), base, share + 2 * margin)
 
 
 def matrix_kernel(extent, *refs):
-    pieces, outs = refs[:extent], refs[extent:]
+    packs, outs = refs[:extent], refs[extent:]
     me = lax.axis_index("chan")
-    quarter = pieces[0].shape[3] // 4
-    length = pieces[0].shape[0] - 7
+    halves = packs[0].shape[0]
+    quarter = packs[0].shape[2] // 4
     taps = []
     turned = []
-    for h in range(14):
-        tiles = [piece[length + h // 2, h % 2].astype(F32) for piece in pieces]
+    for h in range(halves):
+        tiles = [pack[h].astype(F32) for pack in packs]
         own = jnp.concatenate(tiles, axis=0)
         fixed = []
         for g in range(extent):
@@ -238,9 +227,8 @@
 
 
 def weight_loop(total, pieces, first_row, deltas, delta_row, count):
-    total[...] = jnp.zeros_like(total)
-
-    together = max(k for k in range(1, 4) if (count // 2) % k == 0)
+    blocks = [k for k in range(1, 13) if count // 2 % k == 0 and k * len(deltas) <= 12]
+    together = max(blocks, default=1)
 
     def step(r, _):
         left, right = [], []
@@ -301,6 +289,7 @@
     hiddens = [[refs.pop(0)] for _ in range(pairs + 1)]
     deltas = [refs.pop(0) for _ in range(pairs)]
     raw, total = refs
+    total[...] = jnp.zeros_like(total)
     weight_loop(total, planes_of(hiddens), 2, planes_of([[d] for d in deltas]), 2, share)
     for g, tiles in enumerate(weight_fold(total, raw.shape[2])):
         for h, tile in enumerate(tiles):
@@ -319,26 +308,31 @@
     in_blocks(firsts[0].shape[0] // 2, one)
 
 
-def back_kernel(count, *refs):
-    weight, refs = refs[0], refs[1:]
-    first_deltas(
-        weight, refs[: count + 1], refs[count + 1 : 2 * count + 1], refs[2 * count + 1 :]
-    )
-
-
-def first_kernel(share, groups, pairs, *refs):
+def back_kernel(share, groups, count, *refs):
+    refs = list(refs)
+    weight = refs.pop(0)
+    deltas = [refs.pop(0) for _ in range(count + 1)]
+    slopes = [refs.pop(0) for _ in range(count)]
+    fields = [[refs.pop(0) for _ in range(groups)] for _ in range(count + 2)]
+    firsts, total = refs[:-1], refs[-1]
+    first_deltas(weight, deltas, slopes, firsts)
+    total[...] = jnp.zeros_like(total)
+    near = planes_of(fields)[2:-1]
+    weight_loop(total, near, 3, planes_of([[ref] for ref in firsts])[:-1], 1, share)
+
+
+def first_kernel(share, groups, after, *refs):
+    del after
     refs = list(refs)
     weight = refs.pop(0)
     deltas = [refs.pop(0) for _ in range(2)]
     slope = refs.pop(0)
-    later = [refs.pop(0) for _ in range(pairs)]
-    fields = [[refs.pop(0) for _ in range(groups)] for _ in range(pairs + 2)]
-    second = refs.pop(0)
+    fields = [[refs.pop(0) for _ in range(groups)] for _ in range(2)]
+    later, second = refs.pop(0), refs.pop(0)
     first, keep, send, total = refs
     first_deltas(weight, deltas, [slope], [first])
-    near = planes_of(fields)[1:-1]
-    own = planes_of([[ref] for ref in [first] + later])[1:-1]
-    weight_loop(total, near, 3, own, 1, share)
+    total[...] = later[...]
+    weight_loop(total, planes_of(fields)[1:], 3, planes_of([[first]])[1:], 1, share)
     extent, halves, size = keep.shape[:3]
     me = lax.axis_index("chan")
     groups_of = weight_fold(total, size)
@@ -401,8 +395,8 @@
         place(second, first)
 
 
-def split_kernel(after, one, two, *outs):
-    del after
+def split_kernel(ahead, *refs):
+    one, two, *outs = refs[ahead:]
     for g, out in enumerate(outs):
         out[...] = one[g] + two[g]
 
@@ -419,18 +413,21 @@
 
 
 def merge_kernel(extent, *refs):
-    pieces, out, wide = refs[:-2], refs[-2], refs[-1]
-    share, planes, size = pieces[0].shape[:3]
-    rows = out.shape[2]
+    pieces, out, wide = refs[1:-3], refs[-2], refs[-1]
+    size, planes, rows = out.shape[:3]
+    share = rows // extent
     me = lax.axis_index("chan")
-    for j, piece in enumerate(pieces):
+    for j in range(extent):
         base = lax.rem(me + extent - j, extent) * share
 
-        def widen(f, piece=piece, base=base):
-            for x in range(planes):
-                start = ((base + f) * planes + x) * size
-                start = pl.multiple_of(start, 8) if size % 8 == 0 else start
-                wide[pl.ds(start, size), :] = piece[f, x].astype(F32)
+        def widen(f, mine=pieces[j::extent], base=base):
+            x = 0
+            for piece in mine:
+                for k in range(piece.shape[1]):
+                    start = ((base + f) * planes + x) * size
+                    start = pl.multiple_of(start, 8) if size % 8 == 0 else start
+                    wide[pl.ds(start, size), :] = piece[f, k].astype(F32)
+                    x += 1
 
         in_blocks(share, widen)
 
@@ -467,34 +464,38 @@
         return call(relay_kernel, [shape], early, loose=len(early), same={0: 0})[0]
 
     piece = jax.ShapeDtypeStruct((share + 8, 2, size, depth), BF16)
-    longer = jax.ShapeDtypeStruct((share + 15, 2, size, depth), BF16)
     by_tap = (27, size, channels)
-    cuts = 4 if size % 4 == 0 else 1
     made = call(
         functools.partial(field_kernel, extent, 4),
-        ([piece] * (pairs - 1) + [longer]) * extent,
-        [field, jnp.transpose(first_weight, (1, 0, 2)), jnp.transpose(second_weight, (1, 0, 2))],
-        [
-            pltpu.VMEM((size * planes * rows, depth), F32),
-            pltpu.VMEM(field.shape, BF16),
-            pltpu.VMEM(by_tap, BF16),
-            pltpu.VMEM(by_tap, BF16),
-            pltpu.SemaphoreType.DMA((cuts,)),
-            pltpu.SemaphoreType.DMA((2,)),
-        ],
+        [piece] * (extent * pairs),
+        [field],
+        [pltpu.VMEM((size * planes * rows, depth), F32)],
         moved=field.size * 6,
-        loose=3,
-        limit=60 * 1024 * 1024,
-    )
+    )
+    (pack,) = call(
+        pack_kernel,
+        [jax.ShapeDtypeStruct((14, size, 4 * channels), BF16)],
+        [made[-1], jnp.transpose(first_weight, (1, 0, 2)), jnp.transpose(second_weight, (1, 0, 2))],
+        loose=1,
+    )
+    packs = [pack] + [to_chan(pack, j) for j in range(1, extent)]
     parts = [list(made[:pairs])]
+    whole = size % 16 == 0
+    own_before, own_after = [], []
+    if whole:
+        for p in sorted({0, pairs - 1}):
+            parts[0][p] = relayed(parts[0][p], pack)
+        own_before, own_after = [to_next(parts[0][-1])], [to_prev(parts[0][0])]
     for j in range(1, extent):
-        sent = made[j * pairs : (j + 1) * pairs]
-        parts.append([to_chan(value, j) for value in reversed(sent)][::-1])
+        sent = list(made[j * pairs : (j + 1) * pairs])
+        if whole and pairs > 1:
+            sent[0] = relayed(sent[0], *packs[1:])
+        parts.append([to_chan(value, j) for value in sent])
     matrix = jax.ShapeDtypeStruct((6 * channels, 12 * channels), BF16)
     first_wide, second_wide, first_back, second_back = call(
         functools.partial(matrix_kernel, extent),
         [matrix] * 4,
-        [part[-1] for part in parts],
+        packs,
         moved=matrix.size * 8,
     )
     arrived = parts[-1]
@@ -502,20 +503,20 @@
     grads = call(
         functools.partial(grad_kernel, extent, 2),
         [grad_piece] * pairs,
-        [arrived[-1], out_grad],
+        [own_after[0] if whole else arrived[-1], out_grad],
         [pltpu.VMEM((channels * planes * rows, depth), F32)],
         moved=out_grad.size * 4,
         loose=1,
     )
     if extent > 1 and pairs > 1:
-        arrived[0] = relayed(arrived[0], grads[0])
+        arrived[0] = relayed(arrived[0], grads[0], first_wide)
     by_pair = [[parts[j][p] for j in range(extent)] for p in range(pairs)]
     groups = extent
-    if size % 16 != 0:
+    if not whole:
         by_pair = [[jnp.concatenate(pieces, axis=2)] for pieces in by_pair]
         groups = 1
-    before = [to_next(piece) for piece in by_pair[-1]]
-    after = [to_prev(piece) for piece in by_pair[0]]
+    before = own_before + [to_next(piece) for piece in by_pair[-1][len(own_before) :]]
+    after = own_after + [to_prev(piece) for piece in by_pair[0][len(own_after) :]]
     fields = [before] + by_pair + [after]
 
     def many(count, rows_each):
@@ -558,23 +559,48 @@
         flops=work * pairs * share,
         moved=space * 5,
     )
-    later = call(
-        functools.partial(back_kernel, pairs),
-        many(pairs, share + 2),
-        [second_back] + deltas + [delta_after] + slopes[1:],
-        flops=work * pairs * share,
-        moved=space * 3 * pairs,
-    )
+    partial_sum = jax.ShapeDtypeStruct((6 * channels, 12 * channels), F32)
+    made = call(
+        functools.partial(back_kernel, share, groups, pairs),
+        many(pairs, share + 2) + [partial_sum],
+        [second_back] + deltas + [delta_after] + slopes[1:] + flat(fields),
+        flops=work * (2 * pairs - 1) * share,
+        moved=space * 6 * pairs,
+    )
+    later, partial_total = list(made[:-1]), made[-1]
+
+    def field_grad(firsts):
+        count = len(firsts) - 1
+        return list(
+            call(
+                functools.partial(last_kernel, count),
+                [jax.ShapeDtypeStruct((share, 2 * count, size, depth), BF16)] * extent,
+                firsts + [first_back],
+                flops=work * count * share,
+                moved=space * 2 * count,
+            )
+        )
+
+    def exchanged(made):
+        pieces = [made[0]] + [None] * (extent - 1)
+        for j in range(1, extent):
+            pieces[extent - j] = to_chan(made[j], extent - j)
+        return pieces
+
+    pieces, early = [], [later[0]]
+    if pairs > 1:
+        early = field_grad(later)
+        pieces = exchanged(early)
     first, keep, send = call(
-        functools.partial(first_kernel, share, groups, pairs),
+        functools.partial(first_kernel, share, groups),
         many(1, share + 2) + [raw] * 2,
-        [second_back, delta_before, deltas[0], slopes[0]]
-        + list(later)
-        + flat(fields)
-        + [second_raw],
+        [early[0], second_back, delta_before, deltas[0], slopes[0]]
+        + flat(fields[0:2])
+        + [partial_total, second_raw],
         [total],
-        flops=work * (pairs + 1) * share,
-        moved=space * 4 * pairs,
+        flops=work * 2 * share,
+        moved=space * 6,
+        loose=1,
     )
 
     def stepped(value, stride, shift=0):
@@ -588,24 +614,36 @@
         return lax.ppermute(value, ("slab", "chan"), pairs_of)
 
     portion = jax.ShapeDtypeStruct(raw.shape[1:], F32)
-    out_piece = jax.ShapeDtypeStruct((share, planes, size, depth), BF16)
-    made = call(
-        functools.partial(last_kernel, pairs),
-        [out_piece] * extent,
-        [first] + list(later) + [first_back],
-        flops=work * pairs * share,
-        moved=space * 2 * pairs,
-    )
+    made = field_grad([first, later[0]])
     plain = slabs & (slabs - 1) == 0 and slabs >= 4
     if plain:
-        kept = call(split_kernel, [portion] * extent, [made[0], keep, stepped(send, 1)], loose=1)
+        ahead = made[:1] + pieces[1:2]
+        kept = call(
+            functools.partial(split_kernel, len(ahead)),
+            [portion] * extent,
+            ahead + [keep, stepped(send, 1)],
+            loose=len(ahead),
+        )
         shares = [kept[0]] + [to_chan(kept[j], extent - j) for j in range(1, extent)]
         shares += [stepped(kept[j], 2, extent - j) for j in range(extent)]
         (mine,) = call(add_kernel, [portion], shares)
         made = [made[0]] + [relayed(value, mine) for value in made[1:]]
-    pieces = [made[0]] + [None] * (extent - 1)
-    for j in range(1, extent):
-        pieces[extent - j] = to_chan(made[j], extent - j)
+    pieces = exchanged(made) + pieces
+
+    def merged(value):
+        return call(
+            functools.partial(merge_kernel, extent),
+            [
+                jax.ShapeDtypeStruct(value.shape, value.dtype),
+                jax.ShapeDtypeStruct(field.shape, BF16),
+            ],
+            [value] + pieces,
+            [pltpu.VMEM((rows * planes * size, depth), F32)],
+            moved=4 * field.size,
+            loose=1,
+            same={0: 0},
+        )
+
     if plain:
         stride = 4
         while stride < slabs:
@@ -613,6 +651,7 @@
             got = [mine] + [stepped(mine, m * stride) for m in range(1, radix)]
             (mine,) = call(add_kernel, [portion], got)
             stride *= radix
+        mine, input_grad = merged(mine)
         other = stepped(mine, 1)
     else:
         mine, other = keep[0], send[0]
@@ -621,6 +660,7 @@
         even = lax.rem(lax.axis_index("slab"), 2) == 0
         mine, other = jnp.where(even, mine, other), jnp.where(even, other, mine)
         mine, other = lax.psum((mine, other), "slab")
+        mine, input_grad = merged(mine)
         mine, other = jnp.where(even, mine, other), jnp.where(even, other, mine)
     first_grad, second_grad = call(
         functools.partial(finish_kernel, factor),
@@ -628,14 +668,6 @@
         [mine, other],
     )
     first_grad, second_grad = (jnp.transpose(g, (1, 0, 2)) for g in (first_grad, second_grad))
-
-    (input_grad,) = call(
-        functools.partial(merge_kernel, extent),
-        [jax.ShapeDtypeStruct(field.shape, BF16)],
-        pieces,
-        [pltpu.VMEM((rows * planes * size, depth), F32)],
-        moved=4 * field.size,
-    )
     return input_grad, first_grad, second_grad
 
 

time: 72.7 us -> 72.6 us (level)
  Pallas kernels: 24.1 us -> 22.2 us
  starting transfers between devices: 23 us -> 24.6 us
  waiting for transfers between devices: 23.3 us -> 21.7 us
  local copies, waits for them, and re-layouts: 1.41 us -> 2.92 us
    ppermute x4 -> x6, waiting for transfers between devices: 10.1 us -> 4.53 us  [to_chan(): lax.ppermute(value, 'chan', [(i, (i + shift) % extent) for i in range(ext...]
    ppermute x4 -> x6, starting transfers between devices: 4.3 us -> 7.5 us  [to_chan(): lax.ppermute(value, 'chan', [(i, (i + shift) % extent) for i in range(ext...]
    ppermute x3, waiting for transfers between devices: 0.01 us -> 2.67 us  [to_prev(): lax.ppermute(value, 'slab', [((i + 1) % slabs, i) for i in range(slabs)])]
    ppermute x1, starting transfers between devices: 2.94 us -> 0.75 us  [stepped(): return lax.ppermute(value, ('slab', 'chan'), pairs_of)]
    ppermute x3, waiting for transfers between devices: 5.62 us -> 3.52 us  [to_next(): lax.ppermute(value, 'slab', [(i, (i + 1) % slabs) for i in range(slabs)])]
    ppermute x1, waiting for transfers between devices: 0.19 us -> 2.05 us  [stepped(): return lax.ppermute(value, ('slab', 'chan'), pairs_of)]
    pallas_call x16 -> x21, Pallas kernels: 24.1 us -> 22.2 us  [call(): pl.pallas_call(kernel, out_shape=outs, in_specs=[still] * loose + [whole]...]
    ppermute x6, waiting for transfers between devices: 7.33 us -> 8.98 us  [stepped(): return lax.ppermute(value, 'slab', [(i, i ^ stride) for i in range(slabs)])]
  transfers between devices with their start and end apart: 17 -> 19, of which waited for: 10 -> 13; matrix products, arithmetic and copies ran while one was open for 0% -> 0% of each run, Pallas kernels for 21% -> 25%
where the time goes in v6:
time: 72.6 us; the launch traced here: 72.4 us
  starting transfers between devices  24.6 us (34%)
  Pallas kernels  22.2 us (31%)
  waiting for transfers between devices  21.7 us (30%)
  local copies, waits for them, and re-layouts  2.92 us (4%)
  between operations  0.82 us (1%)
    pallas_call x21, Pallas kernels, call(): pl.pallas_call(kernel, out_shape=outs, in_specs=[still] * loose + [whole]...  22.2 us
    ppermute x6, waiting for transfers between devices, stepped(): return lax.ppermute(value, 'slab', [(i, i ^ stride) for i in range(slabs)])  8.98 us
    ppermute x6, starting transfers between devices, stepped(): return lax.ppermute(value, 'slab', [(i, i ^ stride) for i in range(slabs)])  8.05 us
    ppermute x6, starting transfers between devices, to_chan(): lax.ppermute(value, 'chan', [(i, (i + shift) % extent) for i in range(ext...  7.5 us
    ppermute x3, starting transfers between devices, to_prev(): lax.ppermute(value, 'slab', [((i + 1) % slabs, i) for i in range(slabs)])  6.14 us
    ppermute x6, waiting for transfers between devices, to_chan(): lax.ppermute(value, 'chan', [(i, (i + shift) % extent) for i in range(ext...  4.53 us
    ppermute x3, waiting for transfers between devices, to_next(): lax.ppermute(value, 'slab', [(i, (i + 1) % slabs) for i in range(slabs)])  3.52 us
    unnamed x8, local copies, waits for them, and re-layouts  2.92 us
  transfers between devices with their start and end apart: 19, of which 13 were waited for; matrix products, arithmetic and copies ran while one was open for 0% of the time, Pallas kernels for 25%

profile of v6, /device:TPU:0, one launch (start us, length us, event | category | flops | bytes accessed | tf_op | source)
XLA Modules:
  0.0 72.4 jit_solution(1406772281056043735)
XLA Ops:
  0.6 0.0 copy-start.1
  0.6 1.1 %copy-done.1 = bf16[16,4,48,128]{3,2,1,0:T(8,128)(2,1)S(1)} copy-done((bf16[16,4,48,128]{3,2,1,0:T(8,128)(2,1)S(1)}, bf16[16,4,48,128]{3,2,1,0:T(8,128)(2,1)}, u32[]{:S(2)}) %copy-start.1) | copy-done | bytes 786456
  1.8 0.0 copy-start
  1.8 1.5 %shard_map.67 = (bf16[32,2,16,128]{3,2,1,0:T(8,128)(2,1)S(1)}, bf16[32,2,16,128]{3,2,1,0:T(8,128)(2,1)S(1)}, bf16[32,2,16,128]{3,2,1,0:T(8,128)(2,1)S(1)}, bf16[32,2,16,128]{3,2,1,0:T(8,128)(2,1)S(1)}) custom-call(bf16[16,4,48,128]{3,2,1,0:T(8,128)(2,1)S(1)} %copy-done.1), custom_call_target="tpu_custom_call" | custom-call | bytes 2359296 | tf_op jit(solution)/shard_map/pallas_call | solution.py:19
  3.3 3.0 %collective-permute-start.2 = (bf16[32,2,16,128]{3,2,1,0:T(8,128)(2,1)S(1)}, bf16[32,2,16,128]{3,2,1,0:T(8,128)(2,1)S(1)}, u32[]{:S(2)}, u32[]{:S(2)}) collective-permute-start(bf16[32,2,16,128]{3,2,1,0:T(8,128)(2,1)S(1)} %get-tuple-element.37.after), channel_id=1, source_target_pairs={{0,1},{1,0},{2,3},{3,2},{4,5},{5,4},{6,7},{7,6},{8,9},{9,8},{10,11... | collective-permute-start | bytes 786440 | tf_op jit(solution)/shard_map/ppermute | solution.py:453
  6.3 0.0 copy-start.2
  6.3 0.9 %copy-done.2 = bf16[16,27,32]{2,0,1:T(8,128)(2,1)S(1)} copy-done((bf16[16,27,32]{2,0,1:T(8,128)(2,1)S(1)}, bf16[16,27,32]{2,0,1:T(8,128)(2,1)}, u32[]{:S(2)}) %copy-start.2) | copy-done | bytes 27672
  7.2 0.0 copy-start.3
  7.2 0.9 %copy-done.3 = bf16[16,27,32]{2,0,1:T(8,128)(2,1)S(1)} copy-done((bf16[16,27,32]{2,0,1:T(8,128)(2,1)S(1)}, bf16[16,27,32]{2,0,1:T(8,128)(2,1)}, u32[]{:S(2)}) %copy-start.3) | copy-done | bytes 27672
  8.1 0.1 shard_map.68.refs_0_.refs_1_
  8.2 0.1 collective-permute-start
  8.3 3.9 %collective-permute-start.5 = (bf16[32,2,16,128]{3,2,1,0:T(8,128)(2,1)S(1)}, bf16[32,2,16,128]{3,2,1,0:T(8,128)(2,1)S(1)}, u32[]{:S(2)}, u32[]{:S(2)}) collective-permute-start(bf16[32,2,16,128]{3,2,1,0:T(8,128)(2,1)S(1)} %shard_map.71.refs_2_.refs_8_.refs_6_), channel_id=1, source_target_pairs={{2,0},{4,2},{6,4},{8,6},{10,8},{12,10},{14,12},{16,14},{18,16},{20... | collective-permute-start | bytes 786440 | tf_op jit(solution)/shard_map/ppermute | solution.py:459
  12.2 1.6 %collective-permute-done.refs_1_ = bf16[14,16,128]{2,1,0:T(8,128)(2,1)S(1)} collective-permute-done((bf16[14,16,128]{2,1,0:T(8,128)(2,1)S(1)}, bf16[14,16,128]{2,1,0:T(8,128)(2,1)S(1)}, u32[]{:S(2)}, u32[]{:S(2)}) %collective-permute-start) | collective-permute-done | bytes 57376 | tf_op jit(solution)/shard_map/ppermute | solution.py:453
  13.8 1.7 %collective-permute-start.4 = (bf16[32,2,16,128]{3,2,1,0:T(8,128)(2,1)S(1)}, bf16[32,2,16,128]{3,2,1,0:T(8,128)(2,1)S(1)}, u32[]{:S(2)}, u32[]{:S(2)}) collective-permute-start(bf16[32,2,16,128]{3,2,1,0:T(8,128)(2,1)S(1)} %shard_map.72), channel_id=1, source_target_pairs={{0,1},{1,0},{2,3},{3,2},{4,5},{5,4},{6,7},{7,6},{8,9},{9,8},{10,11... | collective-permute-start | bytes 786440 | tf_op jit(solution)/shard_map/ppermute | solution.py:453
  15.5 0.0 collective-permute-start.1
  15.5 0.0 collective-permute-done.2.refs_5_.refs_1_.refs_11_
  15.5 1.6 %collective-permute-start.3 = (bf16[32,2,16,128]{3,2,1,0:T(8,128)(2,1)S(1)}, bf16[32,2,16,128]{3,2,1,0:T(8,128)(2,1)S(1)}, u32[]{:S(2)}, u32[]{:S(2)}) collective-permute-start(bf16[32,2,16,128]{3,2,1,0:T(8,128)(2,1)S(1)} %collective-permute-done.2.refs_5_.refs_1_.refs_11_), channel_id=1, source_target_pairs={{0,2},{2,4},{4,6},{6,8},{8,10},{10,12},{12,14},{14,16},{16,18},{18... | collective-permute-start | bytes 786440 | tf_op jit(solution)/shard_map/ppermute | solution.py:456
  17.2 0.5 shard_map.69
  17.7 0.0 collective-permute-done.5.after.refs_2_.refs_12_
  17.7 0.0 copy-done
  17.7 1.3 %shard_map.73 = (bf16[28,2,32,128]{3,2,1,0:T(8,128)(2,1)S(1)}, bf16[28,2,32,128]{3,2,1,0:T(8,128)(2,1)S(1)}) custom-call(bf16[32,2,16,128]{3,2,1,0:T(8,128)(2,1)S(1)} %collective-permute-done.5.after.refs_2_.refs_12_, bf16[32,4,48,128]{3,2,1,0:T(8,128)(2,1)S(1)} %copy-done), custom_call_target="tpu_custom_call" | custom-call | bytes 3145728 | tf_op jit(solution)/shard_map/pallas_call | solution.py:19
  19.0 2.2 %collective-permute-done.4.refs_0_ = bf16[32,2,16,128]{3,2,1,0:T(8,128)(2,1)S(1)} collective-permute-done((bf16[32,2,16,128]{3,2,1,0:T(8,128)(2,1)S(1)}, bf16[32,2,16,128]{3,2,1,0:T(8,128)(2,1)S(1)}, u32[]{:S(2)}, u32[]{:S(2)}) %collective-permute-start.4) | collective-permute-done | bytes 262176 | tf_op jit(solution)/shard_map/ppermute | solution.py:453
  21.3 2.1 %collective-permute-start.6 = (bf16[32,2,16,128]{3,2,1,0:T(8,128)(2,1)S(1)}, bf16[32,2,16,128]{3,2,1,0:T(8,128)(2,1)S(1)}, u32[]{:S(2)}, u32[]{:S(2)}) collective-permute-start(bf16[32,2,16,128]{3,2,1,0:T(8,128)(2,1)S(1)} %shard_map.74.refs_3_.refs_9_.refs_7_), channel_id=1, source_target_pairs={{2,0},{4,2},{6,4},{8,6},{10,8},{12,10},{14,12},{16,14},{18,16},{20... | collective-permute-start | bytes 786440 | tf_op jit(solution)/shard_map/ppermute | solution.py:459
  23.4 0.6 collective-permute-done.1.refs_0_.refs_6_.refs_4_
  24.0 2.9 %collective-permute-done.3.refs_1_.refs_7_.refs_5_ = bf16[32,2,16,128]{3,2,1,0:T(8,128)(2,1)S(1)} collective-permute-done((bf16[32,2,16,128]{3,2,1,0:T(8,128)(2,1)S(1)}, bf16[32,2,16,128]{3,2,1,0:T(8,128)(2,1)S(1)}, u32[]{:S(2)}, u32[]{:S(2)}) %collective-permute-start.3) | collective-permute-done | bytes 262176 | tf_op jit(solution)/shard_map/ppermute | solution.py:456
  26.9 3.6 %shard_map.75 = (bf16[30,2,32,128]{3,2,1,0:T(8,128)(2,1)S(1)}, bf16[30,2,32,128]{3,2,1,0:T(8,128)(2,1)S(1)}, bf16[30,2,32,128]{3,2,1,0:T(8,128)(2,1)S(1)}, bf16[...) custom-call(bf16[32,2,16,128]{3,2,1,0:T(8,128)(2,1)S(1)} %collective-permute-done.1.refs_0_.refs_6_.refs_4_, ...), custom_call_target="tpu_custom_call" | custom-call | flops 1019215872 | bytes 3145728 | tf_op jit(solution)/shard_map/pallas_call | solution.py:19
  30.5 0.1 collective-permute-start.7
  30.6 0.0 collective-permute-done.6.refs_3_.refs_13_
  30.6 2.8 %shard_map.76 = (bf16[30,2,32,128]{3,2,1,0:T(8,128)(2,1)S(1)}, bf16[30,2,32,128]{3,2,1,0:T(8,128)(2,1)S(1)}, bf16[28,2,32,128]{3,2,1,0:T(8,128)(2,1)S(1)}) custom-call(bf16[32,2,16,128]{3,2,1,0:T(8,128)(2,1)S(1)} %shard_map.70.refs_4_.refs_0_.refs_10_, bf16[32,2,16,128]{3,2,1,0:T(8,128)(2,1)S(1)} %collective-permute-done.2.refs_5_.refs_1_.refs_11_, ...), custom_call_target="tpu_custom_call" | custom-call | flops 679477248 | bytes 2359296 | tf_op jit(solution)/shard_map/pallas_call | solution.py:19
  33.4 0.5 collective-permute-start.8
  33.9 2.7 %collective-permute-done.7.refs_3_ = bf16[28,2,32,128]{3,2,1,0:T(8,128)(2,1)S(1)} collective-permute-done((bf16[28,2,32,128]{3,2,1,0:T(8,128)(2,1)S(1)}, bf16[28,2,32,128]{3,2,1,0:T(8,128)(2,1)S(1)}, u32[]{:S(2)}, u32[]{:S(2)}) %collective-permute-start.7) | collective-permute-done | bytes 458784 | tf_op jit(solution)/shard_map/ppermute | solution.py:459
  36.6 3.3 %shard_map.77 = (bf16[26,2,32,128]{3,2,1,0:T(8,128)(2,1)S(1)}, bf16[26,2,32,128]{3,2,1,0:T(8,128)(2,1)S(1)}, f32[192,384]{1,0:T(8,128)S(1)}) custom-call(bf16[192,384]{1,0:T(8,128)(2,1)S(1)} %get-tuple-element.38.refs_0_, bf16[28,2,32,128]{3,2,1,0:T(8,128)(2,1)S(1)} %get-tuple-element.45.refs_1_.refs_3_.refs_2_, ...), custom_call_target="tpu_custom_call" | custom-call | flops 1019215872 | bytes 4718592 | tf_op jit(solution)/shard_map/pallas_call | solution.py:19
  39.9 1.1 %shard_map.78 = (bf16[24,2,16,128]{3,2,1,0:T(8,128)(2,1)S(1)}, bf16[24,2,16,128]{3,2,1,0:T(8,128)(2,1)S(1)}) custom-call(bf16[26,2,32,128]{3,2,1,0:T(8,128)(2,1)S(1)} %get-tuple-element.51.refs_0_.refs_1_, bf16[26,2,32,128]{3,2,1,0:T(8,128)(2,1)S(1)} %get-tuple-element.52.refs_1_, bf16[192,384]{1,0:T(8,128)(2,1)S(1)} %get-tuple-element.53.refs_2_), custom_call_target="tpu_custom_call" | custom-call | flops 339738624 | bytes 786432 | tf_op jit(solution)/shard_map/pallas_call | solution.py:19
  41.0 0.5 collective-permute-start.9
  41.5 2.5 %shard_map.79.refs_9_ = f32[2,7,16,128]{3,2,1,0:T(8,128)S(1)} custom-call(bf16[30,2,32,128]{3,2,1,0:T(8,128)(2,1)S(1)} %get-tuple-element.57.refs_0_, bf16[30,2,32,128]{3,2,1,0:T(8,128)(2,1)S(1)} %get-tuple-element.46.refs_4_.refs_1_, bf16[30,2,32,128]{3,2,1,0:T(8,128)(2,1)S(1)} %get-tuple-element.58.refs_2_, ...), custom_call_target="tpu_custom_call" | custom-call | flops 679477248 | bytes 1966080 | tf_op jit(solution)/shard_map/pallas_call | solution.py:19
  44.1 0.0 collective-permute-done.8.refs_1_
  44.1 1.5 %shard_map.80 = (bf16[26,2,32,128]{3,2,1,0:T(8,128)(2,1)S(1)}, f32[2,7,16,128]{3,2,1,0:T(8,128)S(1)}, f32[2,7,16,128]{3,2,1,0:T(8,128)S(1)}) custom-call(bf16[24,2,16,128]{3,2,1,0:T(8,128)(2,1)S(1)} %get-tuple-element.54.after.refs_3_, bf16[192,384]{1,0:T(8,128)(2,1)S(1)} %get-tuple-element.38.refs_0_, ...), custom_call_target="tpu_custom_call" | custom-call | flops 679477248 | bytes 2359296 | tf_op jit(solution)/shard_map/pallas_call | solution.py:19
  45.6 0.1 collective-permute-start.10
  45.7 1.1 %shard_map.81 = (bf16[24,2,16,128]{3,2,1,0:T(8,128)(2,1)S(1)}, bf16[24,2,16,128]{3,2,1,0:T(8,128)(2,1)S(1)}) custom-call(bf16[26,2,32,128]{3,2,1,0:T(8,128)(2,1)S(1)} %get-tuple-element.59.refs_0_, bf16[26,2,32,128]{3,2,1,0:T(8,128)(2,1)S(1)} %get-tuple-element.51.refs_0_.refs_1_, bf16[192,384]{1,0:T(8,128)(2,1)S(1)} %get-tuple-element.53.refs_2_), custom_call_target="tpu_custom_call" | custom-call | flops 339738624 | bytes 786432 | tf_op jit(solution)/shard_map/pallas_call | solution.py:19
  46.8 0.2 collective-permute-done.10.refs_3_
  47.0 0.0 collective-permute-done.9.refs_1_.refs_4_
  47.0 1.7 %collective-permute-start.11 = (f32[7,16,128]{2,1,0:T(8,128)S(1)}, f32[7,16,128]{2,1,0:T(8,128)S(1)}, u32[]{:S(2)}, u32[]{:S(2)}) collective-permute-start(f32[7,16,128]{2,1,0:T(8,128)S(1)} %get-tuple-element.65), channel_id=1, source_target_pairs={{0,1},{1,0},{2,3},{3,2},{4,5},{5,4},{6,7},{7,6},{8,9},{9,8},{10,11... | collective-permute-start | bytes 172040 | tf_op jit(solution)/shard_map/ppermute | solution.py:453
  48.7 1.2 %collective-permute-start.12 = (f32[7,16,128]{2,1,0:T(8,128)S(1)}, f32[7,16,128]{2,1,0:T(8,128)S(1)}, u32[]{:S(2)}, u32[]{:S(2)}) collective-permute-start(f32[7,16,128]{2,1,0:T(8,128)S(1)} %get-tuple-element.64.refs_0_), channel_id=1, source_target_pairs={{0,4},{2,6},{4,0},{6,2},{8,12},{10,14},{12,8},{14,10},{16,20},{18,... | collective-permute-start | bytes 172040 | tf_op jit(solution)/shard_map/ppermute | solution.py:608
  49.8 0.7 %collective-permute-start.13 = (f32[7,16,128]{2,1,0:T(8,128)S(1)}, f32[7,16,128]{2,1,0:T(8,128)S(1)}, u32[]{:S(2)}, u32[]{:S(2)}) collective-permute-start(f32[7,16,128]{2,1,0:T(8,128)S(1)} %get-tuple-element.65), channel_id=1, source_target_pairs={{0,5},{1,4},{2,7},{3,6},{4,1},{5,0},{6,3},{7,2},{8,13},{9,12},{10,... | collective-permute-start | bytes 172040 | tf_op jit(solution)/shard_map/ppermute | solution.py:614
  50.6 0.7 collective-permute-done.11.refs_1_
  51.3 1.6 %collective-permute-done.12.refs_2_ = f32[7,16,128]{2,1,0:T(8,128)S(1)} collective-permute-done((f32[7,16,128]{2,1,0:T(8,128)S(1)}, f32[7,16,128]{2,1,0:T(8,128)S(1)}, u32[]{:S(2)}, u32[]{:S(2)}) %collective-permute-start.12) | collective-permute-done | bytes 57376 | tf_op jit(solution)/shard_map/ppermute | solution.py:608
  52.8 2.1 %collective-permute-done.13.refs_3_ = f32[7,16,128]{2,1,0:T(8,128)S(1)} collective-permute-done((f32[7,16,128]{2,1,0:T(8,128)S(1)}, f32[7,16,128]{2,1,0:T(8,128)S(1)}, u32[]{:S(2)}, u32[]{:S(2)}) %collective-permute-start.13) | collective-permute-done | bytes 57376 | tf_op jit(solution)/shard_map/ppermute | solution.py:614
  54.9 0.5 collective-permute-start.17
  55.4 4.2 %collective-permute-start.14 = (f32[7,16,128]{2,1,0:T(8,128)S(1)}, f32[7,16,128]{2,1,0:T(8,128)S(1)}, u32[]{:S(2)}, u32[]{:S(2)}) collective-permute-start(f32[7,16,128]{2,1,0:T(8,128)S(1)} %shard_map.83.refs_0_.refs_1_), channel_id=1, source_target_pairs={{0,8},{2,10},{4,12},{6,14},{8,0},{10,2},{12,4},{14,6},{16,24},{18,... | collective-permute-start | bytes 172040 | tf_op jit(solution)/shard_map/ppermute | solution.py:608
  59.7 2.6 %collective-permute-start.15 = (f32[7,16,128]{2,1,0:T(8,128)S(1)}, f32[7,16,128]{2,1,0:T(8,128)S(1)}, u32[]{:S(2)}, u32[]{:S(2)}) collective-permute-start(f32[7,16,128]{2,1,0:T(8,128)S(1)} %shard_map.83.refs_0_.refs_1_), channel_id=1, source_target_pairs={{0,16},{2,18},{4,20},{6,22},{8,24},{10,26},{12,28},{14,30},{16,0},... | collective-permute-start | bytes 172040 | tf_op jit(solution)/shard_map/ppermute | solution.py:608
  62.3 0.0 collective-permute-start.16
  62.3 0.1 collective-permute-done.14.refs_1_
  62.4 3.6 %collective-permute-done.15.refs_2_ = f32[7,16,128]{2,1,0:T(8,128)S(1)} collective-permute-done((f32[7,16,128]{2,1,0:T(8,128)S(1)}, f32[7,16,128]{2,1,0:T(8,128)S(1)}, u32[]{:S(2)}, u32[]{:S(2)}) %collective-permute-start.15) | collective-permute-done | bytes 57376 | tf_op jit(solution)/shard_map/ppermute | solution.py:608
  66.0 2.3 %collective-permute-done.16.refs_3_ = f32[7,16,128]{2,1,0:T(8,128)S(1)} collective-permute-done((f32[7,16,128]{2,1,0:T(8,128)S(1)}, f32[7,16,128]{2,1,0:T(8,128)S(1)}, u32[]{:S(2)}, u32[]{:S(2)}) %collective-permute-start.16) | collective-permute-done | bytes 57376 | tf_op jit(solution)/shard_map/ppermute | solution.py:608
  68.3 0.0 collective-permute-done.17.refs_2_
  68.3 1.9 %shard_map.86 = (f32[7,16,128]{2,1,0:T(8,128)S(1)}, bf16[16,4,48,128]{3,2,1,0:T(8,128)(2,1)}) custom-call(f32[7,16,128]{2,1,0:T(8,128)S(1)} %shard_map.84.refs_0_, bf16[24,2,16,128]{3,2,1,0:T(8,128)(2,1)S(1)} %get-tuple-element.60.refs_0_.refs_1_, bf16[24,2,16,128]{3,2,1,0:T(8,128)(2,1)S(1)} %collective-permute-done.17.refs_2_, ...), custom_call_target="tpu_custom_call", output_to_operand_aliasing={{0}: (0, {})} | custom-call | bytes 1572864 | tf_op jit(solution)/shard_map/pallas_call | solution.py:19
  70.2 0.0 collective-permute-start.18
  70.2 1.2 %collective-permute-done.18.other = f32[7,16,128]{2,1,0:T(8,128)S(1)} collective-permute-done((f32[7,16,128]{2,1,0:T(8,128)S(1)}, f32[7,16,128]{2,1,0:T(8,128)S(1)}, u32[]{:S(2)}, u32[]{:S(2)}) %collective-permute-start.18) | collective-permute-done | bytes 57376 | tf_op jit(solution)/shard_map/ppermute | solution.py:608
  71.4 0.9 %shard_map.87 = (f32[27,16,32]{2,1,0:T(8,128)}, f32[27,16,32]{2,1,0:T(8,128)}) custom-call(f32[7,16,128]{2,1,0:T(8,128)S(1)} %get-tuple-element.68.mine, f32[7,16,128]{2,1,0:T(8,128)S(1)} %collective-permute-done.18.other), custom_call_target="tpu_custom_call" | custom-call | tf_op jit(solution)/shard_map/pallas_call | solution.py:19
  (8 shorter events, 0.1 us)
Async XLA Ops:
  0.6 1.1 %copy-start.1 = (bf16[16,4,48,128]{3,2,1,0:T(8,128)(2,1)S(1)}, bf16[16,4,48,128]{3,2,1,0:T(8,128)(2,1)}, u32[]{:S(2)}) copy-start(bf16[16,4,48,128]{3,2,1,0:T(8,128)(2,1)} %x_ref.2) | copy-start | bytes 2359300
  1.8 16.0 %copy-start = (bf16[32,4,48,128]{3,2,1,0:T(8,128)(2,1)S(1)}, bf16[32,4,48,128]{3,2,1,0:T(8,128)(2,1)}, u32[]{:S(2)}) copy-start(bf16[32,4,48,128]{3,2,1,0:T(8,128)(2,1)} %x_ref.3) | copy-start | bytes 4718596
  3.3 12.3 %collective-permute-start.2 = (bf16[32,2,16,128]{3,2,1,0:T(8,128)(2,1)S(1)}, bf16[32,2,16,128]{3,2,1,0:T(8,128)(2,1)S(1)}, u32[]{:S(2)}, u32[]{:S(2)}) collective-permute-start(bf16[32,2,16,128]{3,2,1,0:T(8,128)(2,1)S(1)} %get-tuple-element.37.after), channel_id=1, source_target_pairs={{0,1},{1,0},{2,3},{3,2},{4,5},{5,4},{6,7},{7,6},{8,9},{9,8},{10,11... | collective-permute-start | bytes 786440 | tf_op jit(solution)/shard_map/ppermute | solution.py:453
  6.3 0.9 %copy-start.2 = (bf16[16,27,32]{2,0,1:T(8,128)(2,1)S(1)}, bf16[16,27,32]{2,0,1:T(8,128)(2,1)}, u32[]{:S(2)}) copy-start(bf16[16,27,32]{2,0,1:T(8,128)(2,1)} %param.6) | copy-start | bytes 82948
  7.2 0.9 %copy-start.3 = (bf16[16,27,32]{2,0,1:T(8,128)(2,1)S(1)}, bf16[16,27,32]{2,0,1:T(8,128)(2,1)}, u32[]{:S(2)}) copy-start(bf16[16,27,32]{2,0,1:T(8,128)(2,1)} %param.7) | copy-start | bytes 82948
  8.2 5.6 %collective-permute-start = (bf16[14,16,128]{2,1,0:T(8,128)(2,1)S(1)}, bf16[14,16,128]{2,1,0:T(8,128)(2,1)S(1)}, u32[]{:S(2)}, u32[]{:S(2)}) collective-permute-start(bf16[14,16,128]{2,1,0:T(8,128)(2,1)S(1)} %shard_map.68.refs_0_.refs_1_), channel_id=1, source_target_pairs={{0,1},{1,0},{2,3},{3,2},{4,5},{5,4},{6,7},{7,6},{8,9},{9,8},{10,11... | collective-permute-start | bytes 172040 | tf_op jit(solution)/shard_map/ppermute | solution.py:453
  8.3 9.5 %collective-permute-start.5 = (bf16[32,2,16,128]{3,2,1,0:T(8,128)(2,1)S(1)}, bf16[32,2,16,128]{3,2,1,0:T(8,128)(2,1)S(1)}, u32[]{:S(2)}, u32[]{:S(2)}) collective-permute-start(bf16[32,2,16,128]{3,2,1,0:T(8,128)(2,1)S(1)} %shard_map.71.refs_2_.refs_8_.refs_6_), channel_id=1, source_target_pairs={{2,0},{4,2},{6,4},{8,6},{10,8},{12,10},{14,12},{16,14},{18,16},{20... | collective-permute-start | bytes 786440 | tf_op jit(solution)/shard_map/ppermute | solution.py:459
  13.8 7.5 %collective-permute-start.4 = (bf16[32,2,16,128]{3,2,1,0:T(8,128)(2,1)S(1)}, bf16[32,2,16,128]{3,2,1,0:T(8,128)(2,1)S(1)}, u32[]{:S(2)}, u32[]{:S(2)}) collective-permute-start(bf16[32,2,16,128]{3,2,1,0:T(8,128)(2,1)S(1)} %shard_map.72), channel_id=1, source_target_pairs={{0,1},{1,0},{2,3},{3,2},{4,5},{5,4},{6,7},{7,6},{8,9},{9,8},{10,11... | collective-permute-start | bytes 786440 | tf_op jit(solution)/shard_map/ppermute | solution.py:453
  15.5 8.5 %collective-permute-start.1 = (bf16[32,2,16,128]{3,2,1,0:T(8,128)(2,1)S(1)}, bf16[32,2,16,128]{3,2,1,0:T(8,128)(2,1)S(1)}, u32[]{:S(2)}, u32[]{:S(2)}) collective-permute-start(bf16[32,2,16,128]{3,2,1,0:T(8,128)(2,1)S(1)} %shard_map.70.refs_4_.refs_0_.refs_10_), channel_id=1, source_target_pairs={{0,2},{2,4},{4,6},{6,8},{8,10},{10,12},{12,14},{14,16},{16,18},{18... | collective-permute-start | bytes 786440 | tf_op jit(solution)/shard_map/ppermute | solution.py:456
  15.5 11.4 %collective-permute-start.3 = (bf16[32,2,16,128]{3,2,1,0:T(8,128)(2,1)S(1)}, bf16[32,2,16,128]{3,2,1,0:T(8,128)(2,1)S(1)}, u32[]{:S(2)}, u32[]{:S(2)}) collective-permute-start(bf16[32,2,16,128]{3,2,1,0:T(8,128)(2,1)S(1)} %collective-permute-done.2.refs_5_.refs_1_.refs_11_), channel_id=1, source_target_pairs={{0,2},{2,4},{4,6},{6,8},{8,10},{10,12},{12,14},{14,16},{16,18},{18... | collective-permute-start | bytes 786440 | tf_op jit(solution)/shard_map/ppermute | solution.py:456
  21.3 9.3 %collective-permute-start.6 = (bf16[32,2,16,128]{3,2,1,0:T(8,128)(2,1)S(1)}, bf16[32,2,16,128]{3,2,1,0:T(8,128)(2,1)S(1)}, u32[]{:S(2)}, u32[]{:S(2)}) collective-permute-start(bf16[32,2,16,128]{3,2,1,0:T(8,128)(2,1)S(1)} %shard_map.74.refs_3_.refs_9_.refs_7_), channel_id=1, source_target_pairs={{2,0},{4,2},{6,4},{8,6},{10,8},{12,10},{14,12},{16,14},{18,16},{20... | collective-permute-start | bytes 786440 | tf_op jit(solution)/shard_map/ppermute | solution.py:459
  30.5 6.1 %collective-permute-start.7 = (bf16[28,2,32,128]{3,2,1,0:T(8,128)(2,1)S(1)}, bf16[28,2,32,128]{3,2,1,0:T(8,128)(2,1)S(1)}, u32[]{:S(2)}, u32[]{:S(2)}) collective-permute-start(bf16[28,2,32,128]{3,2,1,0:T(8,128)(2,1)S(1)} %get-tuple-element.45.refs_1_.refs_3_.refs_2_), channel_id=1, source_target_pairs={{2,0},{4,2},{6,4},{8,6},{10,8},{12,10},{14,12},{16,14},{18,16},{20... | collective-permute-start | bytes 1376264 | tf_op jit(solution)/shard_map/ppermute | solution.py:459
  33.4 10.7 %collective-permute-start.8 = (bf16[28,2,32,128]{3,2,1,0:T(8,128)(2,1)S(1)}, bf16[28,2,32,128]{3,2,1,0:T(8,128)(2,1)S(1)}, u32[]{:S(2)}, u32[]{:S(2)}) collective-permute-start(bf16[28,2,32,128]{3,2,1,0:T(8,128)(2,1)S(1)} %get-tuple-element.48.refs_2_.refs_4_), channel_id=1, source_target_pairs={{0,2},{2,4},{4,6},{6,8},{8,10},{10,12},{12,14},{14,16},{16,18},{18... | collective-permute-start | bytes 1376264 | tf_op jit(solution)/shard_map/ppermute | solution.py:456
  41.0 6.0 %collective-permute-start.9 = (bf16[24,2,16,128]{3,2,1,0:T(8,128)(2,1)S(1)}, bf16[24,2,16,128]{3,2,1,0:T(8,128)(2,1)S(1)}, u32[]{:S(2)}, u32[]{:S(2)}) collective-permute-start(bf16[24,2,16,128]{3,2,1,0:T(8,128)(2,1)S(1)} %get-tuple-element.61), channel_id=1, source_target_pairs={{0,1},{1,0},{2,3},{3,2},{4,5},{5,4},{6,7},{7,6},{8,9},{9,8},{10,11... | collective-permute-start | bytes 589832 | tf_op jit(solution)/shard_map/ppermute | solution.py:453
  45.6 1.4 %collective-permute-start.10 = (f32[2,7,16,128]{3,2,1,0:T(8,128)S(1)}, f32[2,7,16,128]{3,2,1,0:T(8,128)S(1)}, u32[]{:S(2)}, u32[]{:S(2)}) collective-permute-start(f32[2,7,16,128]{3,2,1,0:T(8,128)S(1)} %get-tuple-element.63), channel_id=1, source_target_pairs={{0,2},{2,0},{4,6},{6,4},{8,10},{10,8},{12,14},{14,12},{16,18},{18,... | collective-permute-start | bytes 344072 | tf_op jit(solution)/shard_map/ppermute | solution.py:608
  47.0 4.2 %collective-permute-start.11 = (f32[7,16,128]{2,1,0:T(8,128)S(1)}, f32[7,16,128]{2,1,0:T(8,128)S(1)}, u32[]{:S(2)}, u32[]{:S(2)}) collective-permute-start(f32[7,16,128]{2,1,0:T(8,128)S(1)} %get-tuple-element.65), channel_id=1, source_target_pairs={{0,1},{1,0},{2,3},{3,2},{4,5},{5,4},{6,7},{7,6},{8,9},{9,8},{10,11... | collective-permute-start | bytes 172040 | tf_op jit(solution)/shard_map/ppermute | solution.py:453
  48.7 4.2 %collective-permute-start.12 = (f32[7,16,128]{2,1,0:T(8,128)S(1)}, f32[7,16,128]{2,1,0:T(8,128)S(1)}, u32[]{:S(2)}, u32[]{:S(2)}) collective-permute-start(f32[7,16,128]{2,1,0:T(8,128)S(1)} %get-tuple-element.64.refs_0_), channel_id=1, source_target_pairs={{0,4},{2,6},{4,0},{6,2},{8,12},{10,14},{12,8},{14,10},{16,20},{18,... | collective-permute-start | bytes 172040 | tf_op jit(solution)/shard_map/ppermute | solution.py:608
  49.8 5.1 %collective-permute-start.13 = (f32[7,16,128]{2,1,0:T(8,128)S(1)}, f32[7,16,128]{2,1,0:T(8,128)S(1)}, u32[]{:S(2)}, u32[]{:S(2)}) collective-permute-start(f32[7,16,128]{2,1,0:T(8,128)S(1)} %get-tuple-element.65), channel_id=1, source_target_pairs={{0,5},{1,4},{2,7},{3,6},{4,1},{5,0},{6,3},{7,2},{8,13},{9,12},{10,... | collective-permute-start | bytes 172040 | tf_op jit(solution)/shard_map/ppermute | solution.py:614
  54.9 13.3 %collective-permute-start.17 = (bf16[24,2,16,128]{3,2,1,0:T(8,128)(2,1)S(1)}, bf16[24,2,16,128]{3,2,1,0:T(8,128)(2,1)S(1)}, u32[]{:S(2)}, u32[]{:S(2)}) collective-permute-start(bf16[24,2,16,128]{3,2,1,0:T(8,128)(2,1)S(1)} %shard_map.85), channel_id=1, source_target_pairs={{0,1},{1,0},{2,3},{3,2},{4,5},{5,4},{6,7},{7,6},{8,9},{9,8},{10,11... | collective-permute-start | bytes 589832 | tf_op jit(solution)/shard_map/ppermute | solution.py:453
  55.4 7.0 %collective-permute-start.14 = (f32[7,16,128]{2,1,0:T(8,128)S(1)}, f32[7,16,128]{2,1,0:T(8,128)S(1)}, u32[]{:S(2)}, u32[]{:S(2)}) collective-permute-start(f32[7,16,128]{2,1,0:T(8,128)S(1)} %shard_map.83.refs_0_.refs_1_), channel_id=1, source_target_pairs={{0,8},{2,10},{4,12},{6,14},{8,0},{10,2},{12,4},{14,6},{16,24},{18,... | collective-permute-start | bytes 172040 | tf_op jit(solution)/shard_map/ppermute | solution.py:608
  59.7 6.3 %collective-permute-start.15 = (f32[7,16,128]{2,1,0:T(8,128)S(1)}, f32[7,16,128]{2,1,0:T(8,128)S(1)}, u32[]{:S(2)}, u32[]{:S(2)}) collective-permute-start(f32[7,16,128]{2,1,0:T(8,128)S(1)} %shard_map.83.refs_0_.refs_1_), channel_id=1, source_target_pairs={{0,16},{2,18},{4,20},{6,22},{8,24},{10,26},{12,28},{14,30},{16,0},... | collective-permute-start | bytes 172040 | tf_op jit(solution)/shard_map/ppermute | solution.py:608
  62.3 6.0 %collective-permute-start.16 = (f32[7,16,128]{2,1,0:T(8,128)S(1)}, f32[7,16,128]{2,1,0:T(8,128)S(1)}, u32[]{:S(2)}, u32[]{:S(2)}) collective-permute-start(f32[7,16,128]{2,1,0:T(8,128)S(1)} %shard_map.83.refs_0_.refs_1_), channel_id=1, source_target_pairs={{0,24},{2,26},{4,28},{6,30},{8,16},{10,18},{12,20},{14,22},{16,8},... | collective-permute-start | bytes 172040 | tf_op jit(solution)/shard_map/ppermute | solution.py:608
  70.2 1.2 %collective-permute-start.18 = (f32[7,16,128]{2,1,0:T(8,128)S(1)}, f32[7,16,128]{2,1,0:T(8,128)S(1)}, u32[]{:S(2)}, u32[]{:S(2)}) collective-permute-start(f32[7,16,128]{2,1,0:T(8,128)S(1)} %get-tuple-element.68.mine), channel_id=1, source_target_pairs={{0,2},{2,0},{4,6},{6,4},{8,10},{10,8},{12,14},{14,12},{16,18},{18,... | collective-permute-start | bytes 172040 | tf_op jit(solution)/shard_map/ppermute | solution.py:608

commit v7 on v6

--- a/solution.py
+++ b/solution.py
@@ -483,14 +483,21 @@
     whole = size % 16 == 0
     own_before, own_after = [], []
     if whole:
-        for p in sorted({0, pairs - 1}):
-            parts[0][p] = relayed(parts[0][p], pack)
         own_before, own_after = [to_next(parts[0][-1])], [to_prev(parts[0][0])]
     for j in range(1, extent):
         sent = list(made[j * pairs : (j + 1) * pairs])
         if whole and pairs > 1:
-            sent[0] = relayed(sent[0], *packs[1:])
+            sent[0] = relayed(sent[0], *own_before, *packs[1:])
         parts.append([to_chan(value, j) for value in sent])
+    grad_piece = jax.ShapeDtypeStruct((share + 4, 2, channels, depth), BF16)
+    grads = call(
+        functools.partial(grad_kernel, extent, 2),
+        [grad_piece] * pairs,
+        [own_after[0] if whole else pack, out_grad],
+        [pltpu.VMEM((channels * planes * rows, depth), F32)],
+        moved=out_grad.size * 4,
+        loose=1,
+    )
     matrix = jax.ShapeDtypeStruct((6 * channels, 12 * channels), BF16)
     first_wide, second_wide, first_back, second_back = call(
         functools.partial(matrix_kernel, extent),
@@ -499,15 +506,6 @@
         moved=matrix.size * 8,
     )
     arrived = parts[-1]
-    grad_piece = jax.ShapeDtypeStruct((share + 4, 2, channels, depth), BF16)
-    grads = call(
-        functools.partial(grad_kernel, extent, 2),
-        [grad_piece] * pairs,
-        [own_after[0] if whole else arrived[-1], out_grad],
-        [pltpu.VMEM((channels * planes * rows, depth), F32)],
-        moved=out_grad.size * 4,
-        loose=1,
-    )
     if extent > 1 and pairs > 1:
         arrived[0] = relayed(arrived[0], grads[0], first_wide)
     by_pair = [[parts[j][p] for j in range(extent)] for p in range(pairs)]

time: 72.6 us -> 73.2 us (level)
  starting transfers between devices: 24.6 us -> 26.9 us
  waiting for transfers between devices: 21.7 us -> 20.1 us
    ppermute x3, waiting for transfers between devices: 3.52 us -> 0.28 us  [to_next(): lax.ppermute(value, 'slab', [(i, (i + 1) % slabs) for i in range(slabs)])]
    ppermute x6, waiting for transfers between devices: 4.53 us -> 6.85 us  [to_chan(): lax.ppermute(value, 'chan', [(i, (i + shift) % extent) for i in range(ext...]
    ppermute x3, starting transfers between devices: 2.18 us -> 0.63 us  [to_next(): lax.ppermute(value, 'slab', [(i, (i + 1) % slabs) for i in range(slabs)])]
    ppermute x6, starting transfers between devices: 7.5 us -> 8.95 us  [to_chan(): lax.ppermute(value, 'chan', [(i, (i + shift) % extent) for i in range(ext...]
    ppermute x3, starting transfers between devices: 6.14 us -> 7.37 us  [to_prev(): lax.ppermute(value, 'slab', [((i + 1) % slabs, i) for i in range(slabs)])]
    ppermute x6, waiting for transfers between devices: 8.98 us -> 7.78 us  [stepped(): return lax.ppermute(value, 'slab', [(i, i ^ stride) for i in range(slabs)])]
    ppermute x1, starting transfers between devices: 0.75 us -> 1.91 us  [stepped(): return lax.ppermute(value, ('slab', 'chan'), pairs_of)]
    pallas_call x21 -> x19, Pallas kernels: 22.2 us -> 22.2 us  [call(): pl.pallas_call(kernel, out_shape=outs, in_specs=[still] * loose + [whole]...]
  transfers between devices with their start and end apart: 19 -> 19, of which waited for: 13 -> 12; matrix products, arithmetic and copies ran while one was open for 0% -> 0% of each run, Pallas kernels for 25% -> 25%
where the time goes in v7:
time: 73.2 us; the launch traced here: 73 us
  starting transfers between devices  26.9 us (37%)
  Pallas kernels  22.2 us (30%)
  waiting for transfers between devices  20.1 us (27%)
  local copies, waits for them, and re-layouts  2.92 us (4%)
  between operations  0.81 us (1%)
    pallas_call x19, Pallas kernels, call(): pl.pallas_call(kernel, out_shape=outs, in_specs=[still] * loose + [whole]...  22.2 us
    ppermute x6, starting transfers between devices, to_chan(): lax.ppermute(value, 'chan', [(i, (i + shift) % extent) for i in range(ext...  8.95 us
    ppermute x6, starting transfers between devices, stepped(): return lax.ppermute(value, 'slab', [(i, i ^ stride) for i in range(slabs)])  8.05 us
    ppermute x6, waiting for transfers between devices, stepped(): return lax.ppermute(value, 'slab', [(i, i ^ stride) for i in range(slabs)])  7.78 us
    ppermute x3, starting transfers between devices, to_prev(): lax.ppermute(value, 'slab', [((i + 1) % slabs, i) for i in range(slabs)])  7.37 us
    ppermute x6, waiting for transfers between devices, to_chan(): lax.ppermute(value, 'chan', [(i, (i + shift) % extent) for i in range(ext...  6.85 us
    ppermute x3, waiting for transfers between devices, to_prev(): lax.ppermute(value, 'slab', [((i + 1) % slabs, i) for i in range(slabs)])  3.16 us
    unnamed x8, local copies, waits for them, and re-layouts  2.92 us
  transfers between devices with their start and end apart: 19, of which 12 were waited for; matrix products, arithmetic and copies ran while one was open for 0% of the time, Pallas kernels for 25%

profile of v7, /device:TPU:0, one launch (start us, length us, event | category | flops | bytes accessed | tf_op | source)
XLA Modules:
  0.0 73.0 jit_solution(7982870780593498581)
XLA Ops:
  0.6 0.0 copy-start.1
  0.6 1.1 %copy-done.1 = bf16[16,4,48,128]{3,2,1,0:T(8,128)(2,1)S(1)} copy-done((bf16[16,4,48,128]{3,2,1,0:T(8,128)(2,1)S(1)}, bf16[16,4,48,128]{3,2,1,0:T(8,128)(2,1)}, u32[]{:S(2)}) %copy-start.1) | copy-done | bytes 786456
  1.8 0.0 copy-start
  1.8 1.5 %shard_map.67 = (bf16[32,2,16,128]{3,2,1,0:T(8,128)(2,1)S(1)}, bf16[32,2,16,128]{3,2,1,0:T(8,128)(2,1)S(1)}, bf16[32,2,16,128]{3,2,1,0:T(8,128)(2,1)S(1)}, bf16[32,2,16,128]{3,2,1,0:T(8,128)(2,1)S(1)}) custom-call(bf16[16,4,48,128]{3,2,1,0:T(8,128)(2,1)S(1)} %copy-done.1), custom_call_target="tpu_custom_call" | custom-call | bytes 2359296 | tf_op jit(solution)/shard_map/pallas_call | solution.py:19
  3.3 0.5 collective-permute-start.1
  3.8 2.6 %collective-permute-start.2 = (bf16[32,2,16,128]{3,2,1,0:T(8,128)(2,1)S(1)}, bf16[32,2,16,128]{3,2,1,0:T(8,128)(2,1)S(1)}, u32[]{:S(2)}, u32[]{:S(2)}) collective-permute-start(bf16[32,2,16,128]{3,2,1,0:T(8,128)(2,1)S(1)} %get-tuple-element.37.after), channel_id=1, source_target_pairs={{0,1},{1,0},{2,3},{3,2},{4,5},{5,4},{6,7},{7,6},{8,9},{9,8},{10,11... | collective-permute-start | bytes 786440 | tf_op jit(solution)/shard_map/ppermute | solution.py:453
  6.3 0.0 copy-start.2
  6.3 0.9 %copy-done.2 = bf16[16,27,32]{2,0,1:T(8,128)(2,1)S(1)} copy-done((bf16[16,27,32]{2,0,1:T(8,128)(2,1)S(1)}, bf16[16,27,32]{2,0,1:T(8,128)(2,1)}, u32[]{:S(2)}) %copy-start.2) | copy-done | bytes 27672
  7.2 0.0 copy-start.3
  7.2 0.9 %copy-done.3 = bf16[16,27,32]{2,0,1:T(8,128)(2,1)S(1)} copy-done((bf16[16,27,32]{2,0,1:T(8,128)(2,1)S(1)}, bf16[16,27,32]{2,0,1:T(8,128)(2,1)}, u32[]{:S(2)}) %copy-start.3) | copy-done | bytes 27672
  8.1 0.1 shard_map.68.refs_0_
  8.2 0.1 collective-permute-start
  8.3 4.1 %collective-permute-start.5 = (bf16[32,2,16,128]{3,2,1,0:T(8,128)(2,1)S(1)}, bf16[32,2,16,128]{3,2,1,0:T(8,128)(2,1)S(1)}, u32[]{:S(2)}, u32[]{:S(2)}) collective-permute-start(bf16[32,2,16,128]{3,2,1,0:T(8,128)(2,1)S(1)} %get-tuple-element.40.refs_2_.refs_8_.refs_6_), channel_id=1, source_target_pairs={{2,0},{4,2},{6,4},{8,6},{10,8},{12,10},{14,12},{16,14},{18,16},{20... | collective-permute-start | bytes 786440 | tf_op jit(solution)/shard_map/ppermute | solution.py:459
  12.5 1.3 %collective-permute-done.refs_1_.refs_2_ = bf16[14,16,128]{2,1,0:T(8,128)(2,1)S(1)} collective-permute-done((bf16[14,16,128]{2,1,0:T(8,128)(2,1)S(1)}, bf16[14,16,128]{2,1,0:T(8,128)(2,1)S(1)}, u32[]{:S(2)}, u32[]{:S(2)}) %collective-permute-start) | collective-permute-done | bytes 57376 | tf_op jit(solution)/shard_map/ppermute | solution.py:453
  13.7 0.0 collective-permute-done.1.refs_1_.refs_0_.refs_6_.refs_4_
  13.7 2.5 %collective-permute-start.4 = (bf16[32,2,16,128]{3,2,1,0:T(8,128)(2,1)S(1)}, bf16[32,2,16,128]{3,2,1,0:T(8,128)(2,1)S(1)}, u32[]{:S(2)}, u32[]{:S(2)}) collective-permute-start(bf16[32,2,16,128]{3,2,1,0:T(8,128)(2,1)S(1)} %shard_map.70), channel_id=1, source_target_pairs={{0,1},{1,0},{2,3},{3,2},{4,5},{5,4},{6,7},{7,6},{8,9},{9,8},{10,11... | collective-permute-start | bytes 786440 | tf_op jit(solution)/shard_map/ppermute | solution.py:453
  16.2 0.0 collective-permute-done.2.refs_5_.refs_1_.refs_11_
  16.2 0.1 collective-permute-start.3
  16.3 0.5 shard_map.69
  16.8 0.0 collective-permute-done.5.after.refs_2_.refs_12_
  16.8 0.0 copy-done
  16.8 1.3 %shard_map.71 = (bf16[28,2,32,128]{3,2,1,0:T(8,128)(2,1)S(1)}, bf16[28,2,32,128]{3,2,1,0:T(8,128)(2,1)S(1)}) custom-call(bf16[32,2,16,128]{3,2,1,0:T(8,128)(2,1)S(1)} %collective-permute-done.5.after.refs_2_.refs_12_, bf16[32,4,48,128]{3,2,1,0:T(8,128)(2,1)S(1)} %copy-done), custom_call_target="tpu_custom_call" | custom-call | bytes 3145728 | tf_op jit(solution)/shard_map/pallas_call | solution.py:19
  18.1 4.9 %collective-permute-done.4.refs_0_ = bf16[32,2,16,128]{3,2,1,0:T(8,128)(2,1)S(1)} collective-permute-done((bf16[32,2,16,128]{3,2,1,0:T(8,128)(2,1)S(1)}, bf16[32,2,16,128]{3,2,1,0:T(8,128)(2,1)S(1)}, u32[]{:S(2)}, u32[]{:S(2)}) %collective-permute-start.4) | collective-permute-done | bytes 262176 | tf_op jit(solution)/shard_map/ppermute | solution.py:453
  23.0 1.4 %collective-permute-start.6 = (bf16[32,2,16,128]{3,2,1,0:T(8,128)(2,1)S(1)}, bf16[32,2,16,128]{3,2,1,0:T(8,128)(2,1)S(1)}, u32[]{:S(2)}, u32[]{:S(2)}) collective-permute-start(bf16[32,2,16,128]{3,2,1,0:T(8,128)(2,1)S(1)} %shard_map.72.refs_3_.refs_9_.refs_7_), channel_id=1, source_target_pairs={{2,0},{4,2},{6,4},{8,6},{10,8},{12,10},{14,12},{16,14},{18,16},{20... | collective-permute-start | bytes 786440 | tf_op jit(solution)/shard_map/ppermute | solution.py:459
  24.4 0.3 collective-permute-done.3.refs_1_.refs_7_.refs_5_
  24.7 3.6 %shard_map.73 = (bf16[30,2,32,128]{3,2,1,0:T(8,128)(2,1)S(1)}, bf16[30,2,32,128]{3,2,1,0:T(8,128)(2,1)S(1)}, bf16[30,2,32,128]{3,2,1,0:T(8,128)(2,1)S(1)}, bf16[...) custom-call(bf16[32,2,16,128]{3,2,1,0:T(8,128)(2,1)S(1)} %collective-permute-done.1.refs_1_.refs_0_.refs_6_.refs_4_, ...), custom_call_target="tpu_custom_call" | custom-call | flops 1019215872 | bytes 3145728 | tf_op jit(solution)/shard_map/pallas_call | solution.py:19
  28.3 1.8 %collective-permute-start.7 = (bf16[28,2,32,128]{3,2,1,0:T(8,128)(2,1)S(1)}, bf16[28,2,32,128]{3,2,1,0:T(8,128)(2,1)S(1)}, u32[]{:S(2)}, u32[]{:S(2)}) collective-permute-start(bf16[28,2,32,128]{3,2,1,0:T(8,128)(2,1)S(1)} %get-tuple-element.45.refs_1_.refs_3_.refs_2_), channel_id=1, source_target_pairs={{2,0},{4,2},{6,4},{8,6},{10,8},{12,10},{14,12},{16,14},{18,16},{20... | collective-permute-start | bytes 1376264 | tf_op jit(solution)/shard_map/ppermute | solution.py:459
  30.1 0.0 collective-permute-done.6.refs_3_.refs_13_
  30.1 2.8 %shard_map.74 = (bf16[30,2,32,128]{3,2,1,0:T(8,128)(2,1)S(1)}, bf16[30,2,32,128]{3,2,1,0:T(8,128)(2,1)S(1)}, bf16[28,2,32,128]{3,2,1,0:T(8,128)(2,1)S(1)}) custom-call(bf16[32,2,16,128]{3,2,1,0:T(8,128)(2,1)S(1)} %get-tuple-element.39.refs_4_.refs_0_.refs_10_, bf16[32,2,16,128]{3,2,1,0:T(8,128)(2,1)S(1)} %collective-permute-done.2.refs_5_.refs_1_.refs_11_, ...), custom_call_target="tpu_custom_call" | custom-call | flops 679477248 | bytes 2359296 | tf_op jit(solution)/shard_map/pallas_call | solution.py:19
  32.9 0.1 collective-permute-start.8
  33.0 3.2 %collective-permute-done.7.refs_3_ = bf16[28,2,32,128]{3,2,1,0:T(8,128)(2,1)S(1)} collective-permute-done((bf16[28,2,32,128]{3,2,1,0:T(8,128)(2,1)S(1)}, bf16[28,2,32,128]{3,2,1,0:T(8,128)(2,1)S(1)}, u32[]{:S(2)}, u32[]{:S(2)}) %collective-permute-start.7) | collective-permute-done | bytes 458784 | tf_op jit(solution)/shard_map/ppermute | solution.py:459
  36.1 3.3 %shard_map.75 = (bf16[26,2,32,128]{3,2,1,0:T(8,128)(2,1)S(1)}, bf16[26,2,32,128]{3,2,1,0:T(8,128)(2,1)S(1)}, f32[192,384]{1,0:T(8,128)S(1)}) custom-call(bf16[192,384]{1,0:T(8,128)(2,1)S(1)} %get-tuple-element.38.refs_0_, bf16[28,2,32,128]{3,2,1,0:T(8,128)(2,1)S(1)} %get-tuple-element.45.refs_1_.refs_3_.refs_2_, ...), custom_call_target="tpu_custom_call" | custom-call | flops 1019215872 | bytes 4718592 | tf_op jit(solution)/shard_map/pallas_call | solution.py:19
  39.4 1.1 %shard_map.76 = (bf16[24,2,16,128]{3,2,1,0:T(8,128)(2,1)S(1)}, bf16[24,2,16,128]{3,2,1,0:T(8,128)(2,1)S(1)}) custom-call(bf16[26,2,32,128]{3,2,1,0:T(8,128)(2,1)S(1)} %get-tuple-element.51.refs_0_.refs_1_, bf16[26,2,32,128]{3,2,1,0:T(8,128)(2,1)S(1)} %get-tuple-element.52.refs_1_, bf16[192,384]{1,0:T(8,128)(2,1)S(1)} %get-tuple-element.53.refs_2_), custom_call_target="tpu_custom_call" | custom-call | flops 339738624 | bytes 786432 | tf_op jit(solution)/shard_map/pallas_call | solution.py:19
  40.6 1.8 %collective-permute-start.9 = (bf16[24,2,16,128]{3,2,1,0:T(8,128)(2,1)S(1)}, bf16[24,2,16,128]{3,2,1,0:T(8,128)(2,1)S(1)}, u32[]{:S(2)}, u32[]{:S(2)}) collective-permute-start(bf16[24,2,16,128]{3,2,1,0:T(8,128)(2,1)S(1)} %get-tuple-element.61), channel_id=1, source_target_pairs={{0,1},{1,0},{2,3},{3,2},{4,5},{5,4},{6,7},{7,6},{8,9},{9,8},{10,11... | collective-permute-start | bytes 589832 | tf_op jit(solution)/shard_map/ppermute | solution.py:453
  42.4 2.5 %shard_map.77.refs_9_ = f32[2,7,16,128]{3,2,1,0:T(8,128)S(1)} custom-call(bf16[30,2,32,128]{3,2,1,0:T(8,128)(2,1)S(1)} %get-tuple-element.57.refs_0_, bf16[30,2,32,128]{3,2,1,0:T(8,128)(2,1)S(1)} %get-tuple-element.46.refs_4_.refs_1_, bf16[30,2,32,128]{3,2,1,0:T(8,128)(2,1)S(1)} %get-tuple-element.58.refs_2_, ...), custom_call_target="tpu_custom_call" | custom-call | flops 679477248 | bytes 1966080 | tf_op jit(solution)/shard_map/pallas_call | solution.py:19
  44.9 0.0 collective-permute-done.8.refs_1_
  44.9 1.5 %shard_map.78 = (bf16[26,2,32,128]{3,2,1,0:T(8,128)(2,1)S(1)}, f32[2,7,16,128]{3,2,1,0:T(8,128)S(1)}, f32[2,7,16,128]{3,2,1,0:T(8,128)S(1)}) custom-call(bf16[24,2,16,128]{3,2,1,0:T(8,128)(2,1)S(1)} %get-tuple-element.54.after.refs_3_, bf16[192,384]{1,0:T(8,128)(2,1)S(1)} %get-tuple-element.38.refs_0_, ...), custom_call_target="tpu_custom_call" | custom-call | flops 679477248 | bytes 2359296 | tf_op jit(solution)/shard_map/pallas_call | solution.py:19
  46.4 0.1 collective-permute-start.10
  46.5 1.1 %shard_map.79 = (bf16[24,2,16,128]{3,2,1,0:T(8,128)(2,1)S(1)}, bf16[24,2,16,128]{3,2,1,0:T(8,128)(2,1)S(1)}) custom-call(bf16[26,2,32,128]{3,2,1,0:T(8,128)(2,1)S(1)} %get-tuple-element.59.refs_0_, bf16[26,2,32,128]{3,2,1,0:T(8,128)(2,1)S(1)} %get-tuple-element.51.refs_0_.refs_1_, bf16[192,384]{1,0:T(8,128)(2,1)S(1)} %get-tuple-element.53.refs_2_), custom_call_target="tpu_custom_call" | custom-call | flops 339738624 | bytes 786432 | tf_op jit(solution)/shard_map/pallas_call | solution.py:19
  47.6 0.0 collective-permute-done.9.refs_1_.refs_4_
  47.7 0.2 collective-permute-done.10.refs_3_
  47.8 0.5 collective-permute-start.11
  48.3 1.2 %collective-permute-start.12 = (f32[7,16,128]{2,1,0:T(8,128)S(1)}, f32[7,16,128]{2,1,0:T(8,128)S(1)}, u32[]{:S(2)}, u32[]{:S(2)}) collective-permute-start(f32[7,16,128]{2,1,0:T(8,128)S(1)} %get-tuple-element.64.refs_0_), channel_id=1, source_target_pairs={{0,4},{2,6},{4,0},{6,2},{8,12},{10,14},{12,8},{14,10},{16,20},{18,... | collective-permute-start | bytes 172040 | tf_op jit(solution)/shard_map/ppermute | solution.py:606
  49.5 1.9 %collective-permute-start.13 = (f32[7,16,128]{2,1,0:T(8,128)S(1)}, f32[7,16,128]{2,1,0:T(8,128)S(1)}, u32[]{:S(2)}, u32[]{:S(2)}) collective-permute-start(f32[7,16,128]{2,1,0:T(8,128)S(1)} %get-tuple-element.65), channel_id=1, source_target_pairs={{0,5},{1,4},{2,7},{3,6},{4,1},{5,0},{6,3},{7,2},{8,13},{9,12},{10,... | collective-permute-start | bytes 172040 | tf_op jit(solution)/shard_map/ppermute | solution.py:612
  51.4 0.7 collective-permute-done.11.refs_1_
  52.1 0.4 collective-permute-done.12.refs_2_
  52.5 2.1 %collective-permute-done.13.refs_3_ = f32[7,16,128]{2,1,0:T(8,128)S(1)} collective-permute-done((f32[7,16,128]{2,1,0:T(8,128)S(1)}, f32[7,16,128]{2,1,0:T(8,128)S(1)}, u32[]{:S(2)}, u32[]{:S(2)}) %collective-permute-start.13) | collective-permute-done | bytes 57376 | tf_op jit(solution)/shard_map/ppermute | solution.py:612
  54.6 1.6 %collective-permute-start.17 = (bf16[24,2,16,128]{3,2,1,0:T(8,128)(2,1)S(1)}, bf16[24,2,16,128]{3,2,1,0:T(8,128)(2,1)S(1)}, u32[]{:S(2)}, u32[]{:S(2)}) collective-permute-start(bf16[24,2,16,128]{3,2,1,0:T(8,128)(2,1)S(1)} %shard_map.83), channel_id=1, source_target_pairs={{0,1},{1,0},{2,3},{3,2},{4,5},{5,4},{6,7},{7,6},{8,9},{9,8},{10,11... | collective-permute-start | bytes 589832 | tf_op jit(solution)/shard_map/ppermute | solution.py:453
  56.2 4.2 %collective-permute-start.14 = (f32[7,16,128]{2,1,0:T(8,128)S(1)}, f32[7,16,128]{2,1,0:T(8,128)S(1)}, u32[]{:S(2)}, u32[]{:S(2)}) collective-permute-start(f32[7,16,128]{2,1,0:T(8,128)S(1)} %shard_map.81.refs_0_.refs_1_), channel_id=1, source_target_pairs={{0,8},{2,10},{4,12},{6,14},{8,0},{10,2},{12,4},{14,6},{16,24},{18,... | collective-permute-start | bytes 172040 | tf_op jit(solution)/shard_map/ppermute | solution.py:606
  60.4 2.6 %collective-permute-start.15 = (f32[7,16,128]{2,1,0:T(8,128)S(1)}, f32[7,16,128]{2,1,0:T(8,128)S(1)}, u32[]{:S(2)}, u32[]{:S(2)}) collective-permute-start(f32[7,16,128]{2,1,0:T(8,128)S(1)} %shard_map.81.refs_0_.refs_1_), channel_id=1, source_target_pairs={{0,16},{2,18},{4,20},{6,22},{8,24},{10,26},{12,28},{14,30},{16,0},... | collective-permute-start | bytes 172040 | tf_op jit(solution)/shard_map/ppermute | solution.py:606
  62.9 0.0 collective-permute-start.16
  63.0 0.1 collective-permute-done.14.refs_1_
  63.1 3.6 %collective-permute-done.15.refs_2_ = f32[7,16,128]{2,1,0:T(8,128)S(1)} collective-permute-done((f32[7,16,128]{2,1,0:T(8,128)S(1)}, f32[7,16,128]{2,1,0:T(8,128)S(1)}, u32[]{:S(2)}, u32[]{:S(2)}) %collective-permute-start.15) | collective-permute-done | bytes 57376 | tf_op jit(solution)/shard_map/ppermute | solution.py:606
  66.7 2.3 %collective-permute-done.16.refs_3_ = f32[7,16,128]{2,1,0:T(8,128)S(1)} collective-permute-done((f32[7,16,128]{2,1,0:T(8,128)S(1)}, f32[7,16,128]{2,1,0:T(8,128)S(1)}, u32[]{:S(2)}, u32[]{:S(2)}) %collective-permute-start.16) | collective-permute-done | bytes 57376 | tf_op jit(solution)/shard_map/ppermute | solution.py:606
  68.9 0.0 collective-permute-done.17.refs_2_
  69.0 1.9 %shard_map.84 = (f32[7,16,128]{2,1,0:T(8,128)S(1)}, bf16[16,4,48,128]{3,2,1,0:T(8,128)(2,1)}) custom-call(f32[7,16,128]{2,1,0:T(8,128)S(1)} %shard_map.82.refs_0_, bf16[24,2,16,128]{3,2,1,0:T(8,128)(2,1)S(1)} %get-tuple-element.60.refs_0_.refs_1_, bf16[24,2,16,128]{3,2,1,0:T(8,128)(2,1)S(1)} %collective-permute-done.17.refs_2_, ...), custom_call_target="tpu_custom_call", output_to_operand_aliasing={{0}: (0, {})} | custom-call | bytes 1572864 | tf_op jit(solution)/shard_map/pallas_call | solution.py:19
  70.9 0.0 collective-permute-start.18
  70.9 1.2 %collective-permute-done.18.other = f32[7,16,128]{2,1,0:T(8,128)S(1)} collective-permute-done((f32[7,16,128]{2,1,0:T(8,128)S(1)}, f32[7,16,128]{2,1,0:T(8,128)S(1)}, u32[]{:S(2)}, u32[]{:S(2)}) %collective-permute-start.18) | collective-permute-done | bytes 57376 | tf_op jit(solution)/shard_map/ppermute | solution.py:606
  72.1 0.9 %shard_map.85 = (f32[27,16,32]{2,1,0:T(8,128)}, f32[27,16,32]{2,1,0:T(8,128)}) custom-call(f32[7,16,128]{2,1,0:T(8,128)S(1)} %get-tuple-element.68.mine, f32[7,16,128]{2,1,0:T(8,128)S(1)} %collective-permute-done.18.other), custom_call_target="tpu_custom_call" | custom-call | tf_op jit(solution)/shard_map/pallas_call | solution.py:19
  (6 shorter events, 0.0 us)
Async XLA Ops:
  0.6 1.1 %copy-start.1 = (bf16[16,4,48,128]{3,2,1,0:T(8,128)(2,1)S(1)}, bf16[16,4,48,128]{3,2,1,0:T(8,128)(2,1)}, u32[]{:S(2)}) copy-start(bf16[16,4,48,128]{3,2,1,0:T(8,128)(2,1)} %x_ref.2) | copy-start | bytes 2359300
  1.8 15.1 %copy-start = (bf16[32,4,48,128]{3,2,1,0:T(8,128)(2,1)S(1)}, bf16[32,4,48,128]{3,2,1,0:T(8,128)(2,1)}, u32[]{:S(2)}) copy-start(bf16[32,4,48,128]{3,2,1,0:T(8,128)(2,1)} %x_ref.3) | copy-start | bytes 4718596
  3.3 10.5 %collective-permute-start.1 = (bf16[32,2,16,128]{3,2,1,0:T(8,128)(2,1)S(1)}, bf16[32,2,16,128]{3,2,1,0:T(8,128)(2,1)S(1)}, u32[]{:S(2)}, u32[]{:S(2)}) collective-permute-start(bf16[32,2,16,128]{3,2,1,0:T(8,128)(2,1)S(1)} %get-tuple-element.39.refs_4_.refs_0_.refs_10_), channel_id=1, source_target_pairs={{0,2},{2,4},{4,6},{6,8},{8,10},{10,12},{12,14},{14,16},{16,18},{18... | collective-permute-start | bytes 786440 | tf_op jit(solution)/shard_map/ppermute | solution.py:456
  3.8 12.5 %collective-permute-start.2 = (bf16[32,2,16,128]{3,2,1,0:T(8,128)(2,1)S(1)}, bf16[32,2,16,128]{3,2,1,0:T(8,128)(2,1)S(1)}, u32[]{:S(2)}, u32[]{:S(2)}) collective-permute-start(bf16[32,2,16,128]{3,2,1,0:T(8,128)(2,1)S(1)} %get-tuple-element.37.after), channel_id=1, source_target_pairs={{0,1},{1,0},{2,3},{3,2},{4,5},{5,4},{6,7},{7,6},{8,9},{9,8},{10,11... | collective-permute-start | bytes 786440 | tf_op jit(solution)/shard_map/ppermute | solution.py:453
  6.3 0.9 %copy-start.2 = (bf16[16,27,32]{2,0,1:T(8,128)(2,1)S(1)}, bf16[16,27,32]{2,0,1:T(8,128)(2,1)}, u32[]{:S(2)}) copy-start(bf16[16,27,32]{2,0,1:T(8,128)(2,1)} %param.6) | copy-start | bytes 82948
  7.2 0.9 %copy-start.3 = (bf16[16,27,32]{2,0,1:T(8,128)(2,1)S(1)}, bf16[16,27,32]{2,0,1:T(8,128)(2,1)}, u32[]{:S(2)}) copy-start(bf16[16,27,32]{2,0,1:T(8,128)(2,1)} %param.7) | copy-start | bytes 82948
  8.2 5.5 %collective-permute-start = (bf16[14,16,128]{2,1,0:T(8,128)(2,1)S(1)}, bf16[14,16,128]{2,1,0:T(8,128)(2,1)S(1)}, u32[]{:S(2)}, u32[]{:S(2)}) collective-permute-start(bf16[14,16,128]{2,1,0:T(8,128)(2,1)S(1)} %shard_map.68.refs_0_), channel_id=1, source_target_pairs={{0,1},{1,0},{2,3},{3,2},{4,5},{5,4},{6,7},{7,6},{8,9},{9,8},{10,11... | collective-permute-start | bytes 172040 | tf_op jit(solution)/shard_map/ppermute | solution.py:453
  8.3 8.5 %collective-permute-start.5 = (bf16[32,2,16,128]{3,2,1,0:T(8,128)(2,1)S(1)}, bf16[32,2,16,128]{3,2,1,0:T(8,128)(2,1)S(1)}, u32[]{:S(2)}, u32[]{:S(2)}) collective-permute-start(bf16[32,2,16,128]{3,2,1,0:T(8,128)(2,1)S(1)} %get-tuple-element.40.refs_2_.refs_8_.refs_6_), channel_id=1, source_target_pairs={{2,0},{4,2},{6,4},{8,6},{10,8},{12,10},{14,12},{16,14},{18,16},{20... | collective-permute-start | bytes 786440 | tf_op jit(solution)/shard_map/ppermute | solution.py:459
  13.7 9.3 %collective-permute-start.4 = (bf16[32,2,16,128]{3,2,1,0:T(8,128)(2,1)S(1)}, bf16[32,2,16,128]{3,2,1,0:T(8,128)(2,1)S(1)}, u32[]{:S(2)}, u32[]{:S(2)}) collective-permute-start(bf16[32,2,16,128]{3,2,1,0:T(8,128)(2,1)S(1)} %shard_map.70), channel_id=1, source_target_pairs={{0,1},{1,0},{2,3},{3,2},{4,5},{5,4},{6,7},{7,6},{8,9},{9,8},{10,11... | collective-permute-start | bytes 786440 | tf_op jit(solution)/shard_map/ppermute | solution.py:453
  16.2 8.5 %collective-permute-start.3 = (bf16[32,2,16,128]{3,2,1,0:T(8,128)(2,1)S(1)}, bf16[32,2,16,128]{3,2,1,0:T(8,128)(2,1)S(1)}, u32[]{:S(2)}, u32[]{:S(2)}) collective-permute-start(bf16[32,2,16,128]{3,2,1,0:T(8,128)(2,1)S(1)} %collective-permute-done.2.refs_5_.refs_1_.refs_11_), channel_id=1, source_target_pairs={{0,2},{2,4},{4,6},{6,8},{8,10},{10,12},{12,14},{14,16},{16,18},{18... | collective-permute-start | bytes 786440 | tf_op jit(solution)/shard_map/ppermute | solution.py:456
  23.0 7.1 %collective-permute-start.6 = (bf16[32,2,16,128]{3,2,1,0:T(8,128)(2,1)S(1)}, bf16[32,2,16,128]{3,2,1,0:T(8,128)(2,1)S(1)}, u32[]{:S(2)}, u32[]{:S(2)}) collective-permute-start(bf16[32,2,16,128]{3,2,1,0:T(8,128)(2,1)S(1)} %shard_map.72.refs_3_.refs_9_.refs_7_), channel_id=1, source_target_pairs={{2,0},{4,2},{6,4},{8,6},{10,8},{12,10},{14,12},{16,14},{18,16},{20... | collective-permute-start | bytes 786440 | tf_op jit(solution)/shard_map/ppermute | solution.py:459
  28.3 7.8 %collective-permute-start.7 = (bf16[28,2,32,128]{3,2,1,0:T(8,128)(2,1)S(1)}, bf16[28,2,32,128]{3,2,1,0:T(8,128)(2,1)S(1)}, u32[]{:S(2)}, u32[]{:S(2)}) collective-permute-start(bf16[28,2,32,128]{3,2,1,0:T(8,128)(2,1)S(1)} %get-tuple-element.45.refs_1_.refs_3_.refs_2_), channel_id=1, source_target_pairs={{2,0},{4,2},{6,4},{8,6},{10,8},{12,10},{14,12},{16,14},{18,16},{20... | collective-permute-start | bytes 1376264 | tf_op jit(solution)/shard_map/ppermute | solution.py:459
  32.9 12.0 %collective-permute-start.8 = (bf16[28,2,32,128]{3,2,1,0:T(8,128)(2,1)S(1)}, bf16[28,2,32,128]{3,2,1,0:T(8,128)(2,1)S(1)}, u32[]{:S(2)}, u32[]{:S(2)}) collective-permute-start(bf16[28,2,32,128]{3,2,1,0:T(8,128)(2,1)S(1)} %get-tuple-element.48.refs_2_.refs_4_), channel_id=1, source_target_pairs={{0,2},{2,4},{4,6},{6,8},{8,10},{10,12},{12,14},{14,16},{16,18},{18... | collective-permute-start | bytes 1376264 | tf_op jit(solution)/shard_map/ppermute | solution.py:456
  40.6 7.1 %collective-permute-start.9 = (bf16[24,2,16,128]{3,2,1,0:T(8,128)(2,1)S(1)}, bf16[24,2,16,128]{3,2,1,0:T(8,128)(2,1)S(1)}, u32[]{:S(2)}, u32[]{:S(2)}) collective-permute-start(bf16[24,2,16,128]{3,2,1,0:T(8,128)(2,1)S(1)} %get-tuple-element.61), channel_id=1, source_target_pairs={{0,1},{1,0},{2,3},{3,2},{4,5},{5,4},{6,7},{7,6},{8,9},{9,8},{10,11... | collective-permute-start | bytes 589832 | tf_op jit(solution)/shard_map/ppermute | solution.py:453
  46.4 1.4 %collective-permute-start.10 = (f32[2,7,16,128]{3,2,1,0:T(8,128)S(1)}, f32[2,7,16,128]{3,2,1,0:T(8,128)S(1)}, u32[]{:S(2)}, u32[]{:S(2)}) collective-permute-start(f32[2,7,16,128]{3,2,1,0:T(8,128)S(1)} %get-tuple-element.63), channel_id=1, source_target_pairs={{0,2},{2,0},{4,6},{6,4},{8,10},{10,8},{12,14},{14,12},{16,18},{18,... | collective-permute-start | bytes 344072 | tf_op jit(solution)/shard_map/ppermute | solution.py:606
  47.8 4.2 %collective-permute-start.11 = (f32[7,16,128]{2,1,0:T(8,128)S(1)}, f32[7,16,128]{2,1,0:T(8,128)S(1)}, u32[]{:S(2)}, u32[]{:S(2)}) collective-permute-start(f32[7,16,128]{2,1,0:T(8,128)S(1)} %get-tuple-element.65), channel_id=1, source_target_pairs={{0,1},{1,0},{2,3},{3,2},{4,5},{5,4},{6,7},{7,6},{8,9},{9,8},{10,11... | collective-permute-start | bytes 172040 | tf_op jit(solution)/shard_map/ppermute | solution.py:453
  48.3 4.2 %collective-permute-start.12 = (f32[7,16,128]{2,1,0:T(8,128)S(1)}, f32[7,16,128]{2,1,0:T(8,128)S(1)}, u32[]{:S(2)}, u32[]{:S(2)}) collective-permute-start(f32[7,16,128]{2,1,0:T(8,128)S(1)} %get-tuple-element.64.refs_0_), channel_id=1, source_target_pairs={{0,4},{2,6},{4,0},{6,2},{8,12},{10,14},{12,8},{14,10},{16,20},{18,... | collective-permute-start | bytes 172040 | tf_op jit(solution)/shard_map/ppermute | solution.py:606
  49.5 5.1 %collective-permute-start.13 = (f32[7,16,128]{2,1,0:T(8,128)S(1)}, f32[7,16,128]{2,1,0:T(8,128)S(1)}, u32[]{:S(2)}, u32[]{:S(2)}) collective-permute-start(f32[7,16,128]{2,1,0:T(8,128)S(1)} %get-tuple-element.65), channel_id=1, source_target_pairs={{0,5},{1,4},{2,7},{3,6},{4,1},{5,0},{6,3},{7,2},{8,13},{9,12},{10,... | collective-permute-start | bytes 172040 | tf_op jit(solution)/shard_map/ppermute | solution.py:612
  54.6 14.3 %collective-permute-start.17 = (bf16[24,2,16,128]{3,2,1,0:T(8,128)(2,1)S(1)}, bf16[24,2,16,128]{3,2,1,0:T(8,128)(2,1)S(1)}, u32[]{:S(2)}, u32[]{:S(2)}) collective-permute-start(bf16[24,2,16,128]{3,2,1,0:T(8,128)(2,1)S(1)} %shard_map.83), channel_id=1, source_target_pairs={{0,1},{1,0},{2,3},{3,2},{4,5},{5,4},{6,7},{7,6},{8,9},{9,8},{10,11... | collective-permute-start | bytes 589832 | tf_op jit(solution)/shard_map/ppermute | solution.py:453
  56.2 6.9 %collective-permute-start.14 = (f32[7,16,128]{2,1,0:T(8,128)S(1)}, f32[7,16,128]{2,1,0:T(8,128)S(1)}, u32[]{:S(2)}, u32[]{:S(2)}) collective-permute-start(f32[7,16,128]{2,1,0:T(8,128)S(1)} %shard_map.81.refs_0_.refs_1_), channel_id=1, source_target_pairs={{0,8},{2,10},{4,12},{6,14},{8,0},{10,2},{12,4},{14,6},{16,24},{18,... | collective-permute-start | bytes 172040 | tf_op jit(solution)/shard_map/ppermute | solution.py:606
  60.4 6.3 %collective-permute-start.15 = (f32[7,16,128]{2,1,0:T(8,128)S(1)}, f32[7,16,128]{2,1,0:T(8,128)S(1)}, u32[]{:S(2)}, u32[]{:S(2)}) collective-permute-start(f32[7,16,128]{2,1,0:T(8,128)S(1)} %shard_map.81.refs_0_.refs_1_), channel_id=1, source_target_pairs={{0,16},{2,18},{4,20},{6,22},{8,24},{10,26},{12,28},{14,30},{16,0},... | collective-permute-start | bytes 172040 | tf_op jit(solution)/shard_map/ppermute | solution.py:606
  62.9 6.0 %collective-permute-start.16 = (f32[7,16,128]{2,1,0:T(8,128)S(1)}, f32[7,16,128]{2,1,0:T(8,128)S(1)}, u32[]{:S(2)}, u32[]{:S(2)}) collective-permute-start(f32[7,16,128]{2,1,0:T(8,128)S(1)} %shard_map.81.refs_0_.refs_1_), channel_id=1, source_target_pairs={{0,24},{2,26},{4,28},{6,30},{8,16},{10,18},{12,20},{14,22},{16,8},... | collective-permute-start | bytes 172040 | tf_op jit(solution)/shard_map/ppermute | solution.py:606
  70.9 1.2 %collective-permute-start.18 = (f32[7,16,128]{2,1,0:T(8,128)S(1)}, f32[7,16,128]{2,1,0:T(8,128)S(1)}, u32[]{:S(2)}, u32[]{:S(2)}) collective-permute-start(f32[7,16,128]{2,1,0:T(8,128)S(1)} %get-tuple-element.68.mine), channel_id=1, source_target_pairs={{0,2},{2,0},{4,6},{6,4},{8,10},{10,8},{12,14},{14,12},{16,18},{18,... | collective-permute-start | bytes 172040 | tf_op jit(solution)/shard_map/ppermute | solution.py:606

commit v8 on v7

--- a/solution.py
+++ b/solution.py
@@ -84,19 +84,26 @@
         )
 
 
-def pack_kernel(after, first, second, packed):
-    del after
+def pack_kernel(count, rows, *refs):
+    first, second = refs[count : count + 2]
+    pieces, packed, done = refs[count + 2 : -2], refs[-2], refs[-1]
     blank = jnp.zeros(first.shape[1:], F32)
-    for h in range(packed.shape[0]):
+    for h in range(14):
         parts = []
         for ref in (first, second):
             for t in (2 * h, 2 * h + 1):
                 parts.append(ref[t].astype(F32) if t < ref.shape[0] else blank)
-        packed[h] = jnp.concatenate(parts, axis=1).astype(BF16)
-
-
-def grad_kernel(extent, margin, after, x_ref, *refs):
-    del after
+        packed[h // 2, h % 2] = jnp.concatenate(parts, axis=1).astype(BF16)
+    copies = []
+    for k, piece in enumerate(pieces):
+        copies.append(pltpu.make_async_copy(packed, piece.at[pl.ds(rows, 7)], done.at[k]))
+        copies[-1].start()
+    for copy in copies:
+        copy.wait()
+
+
+def grad_kernel(extent, margin, one, two, x_ref, *refs):
+    del one, two
     outs, wide = refs[:-1], refs[-1]
     count, planes, rows = x_ref.shape[:3]
     share = rows // extent
@@ -108,12 +115,13 @@
 def matrix_kernel(extent, *refs):
     packs, outs = refs[:extent], refs[extent:]
     me = lax.axis_index("chan")
-    halves = packs[0].shape[0]
-    quarter = packs[0].shape[2] // 4
+    quarter = packs[0].shape[3] // 4
     taps = []
     turned = []
-    for h in range(halves):
-        tiles = [pack[h].astype(F32) for pack in packs]
+    for h in range(14):
+        tiles = [
+            pack[pack.shape[0] - 7 + h // 2, h % 2].astype(F32) for pack in packs
+        ]
         own = jnp.concatenate(tiles, axis=0)
         fixed = []
         for g in range(extent):
@@ -308,7 +316,8 @@
     in_blocks(firsts[0].shape[0] // 2, one)
 
 
-def back_kernel(share, groups, count, *refs):
+def back_kernel(share, groups, count, after, *refs):
+    del after
     refs = list(refs)
     weight = refs.pop(0)
     deltas = [refs.pop(0) for _ in range(count + 1)]
@@ -401,8 +410,8 @@
         out[...] = one[g] + two[g]
 
 
-def add_kernel(*refs):
-    values = [ref[...] for ref in refs[:-1]]
+def add_kernel(ahead, *refs):
+    values = [ref[...] for ref in refs[ahead:-1]]
     while len(values) > 1:
         values = [sum(values[k + 1 : k + 2], values[k]) for k in range(0, len(values), 2)]
     refs[-1][...] = values[0]
@@ -413,7 +422,8 @@
 
 
 def merge_kernel(extent, *refs):
-    pieces, out, wide = refs[1:-3], refs[-2], refs[-1]
+    pieces, token, out, wide = refs[:-3], refs[-3], refs[-2], refs[-1]
+    token[...] = jnp.zeros_like(token)
     size, planes, rows = out.shape[:3]
     share = rows // extent
     me = lax.axis_index("chan")
@@ -465,38 +475,44 @@
 
     piece = jax.ShapeDtypeStruct((share + 8, 2, size, depth), BF16)
     by_tap = (27, size, channels)
+    longer = jax.ShapeDtypeStruct((share + 15, 2, size, depth), BF16)
+    rest = [piece] * (pairs - 1)
     made = call(
         functools.partial(field_kernel, extent, 4),
-        [piece] * (extent * pairs),
+        [piece] + rest + ([longer] + rest) * (extent - 1),
         [field],
         [pltpu.VMEM((size * planes * rows, depth), F32)],
         moved=field.size * 6,
     )
-    (pack,) = call(
-        pack_kernel,
-        [jax.ShapeDtypeStruct((14, size, 4 * channels), BF16)],
-        [made[-1], jnp.transpose(first_weight, (1, 0, 2)), jnp.transpose(second_weight, (1, 0, 2))],
-        loose=1,
-    )
-    packs = [pack] + [to_chan(pack, j) for j in range(1, extent)]
+    first_sent = list(made[pairs::pairs])
+    others = extent - 1
+    packed = call(
+        functools.partial(pack_kernel, others, share + 8),
+        [longer] * others + [jax.ShapeDtypeStruct((7, 2, size, 4 * channels), BF16)],
+        first_sent
+        + [jnp.transpose(first_weight, (1, 0, 2)), jnp.transpose(second_weight, (1, 0, 2))],
+        [pltpu.SemaphoreType.DMA((max(others, 1),))],
+        loose=others,
+        same={k: k for k in range(others)},
+    )
+    first_sent, pack = packed[:-1], packed[-1]
     parts = [list(made[:pairs])]
     whole = size % 16 == 0
     own_before, own_after = [], []
     if whole:
         own_before, own_after = [to_next(parts[0][-1])], [to_prev(parts[0][0])]
     for j in range(1, extent):
-        sent = list(made[j * pairs : (j + 1) * pairs])
-        if whole and pairs > 1:
-            sent[0] = relayed(sent[0], *own_before, *packs[1:])
+        sent = [first_sent[j - 1]] + list(made[j * pairs + 1 : (j + 1) * pairs])
         parts.append([to_chan(value, j) for value in sent])
+    packs = [pack] + [part[0] for part in parts[1:]]
     grad_piece = jax.ShapeDtypeStruct((share + 4, 2, channels, depth), BF16)
     grads = call(
         functools.partial(grad_kernel, extent, 2),
         [grad_piece] * pairs,
-        [own_after[0] if whole else pack, out_grad],
+        [own_before[0], own_after[0], out_grad] if whole else [pack, pack, out_grad],
         [pltpu.VMEM((channels * planes * rows, depth), F32)],
         moved=out_grad.size * 4,
-        loose=1,
+        loose=2,
     )
     matrix = jax.ShapeDtypeStruct((6 * channels, 12 * channels), BF16)
     first_wide, second_wide, first_back, second_back = call(
@@ -507,11 +523,14 @@
     )
     arrived = parts[-1]
     if extent > 1 and pairs > 1:
-        arrived[0] = relayed(arrived[0], grads[0], first_wide)
+        arrived[0] = relayed(arrived[0], grads[0])
     by_pair = [[parts[j][p] for j in range(extent)] for p in range(pairs)]
     groups = extent
     if not whole:
-        by_pair = [[jnp.concatenate(pieces, axis=2)] for pieces in by_pair]
+        by_pair = [
+            [jnp.concatenate([piece[: share + 8] for piece in pieces], axis=2)]
+            for pieces in by_pair
+        ]
         groups = 1
     before = own_before + [to_next(piece) for piece in by_pair[-1][len(own_before) :]]
     after = own_after + [to_prev(piece) for piece in by_pair[0][len(own_after) :]]
@@ -561,9 +580,10 @@
     made = call(
         functools.partial(back_kernel, share, groups, pairs),
         many(pairs, share + 2) + [partial_sum],
-        [second_back] + deltas + [delta_after] + slopes[1:] + flat(fields),
+        [second_raw, second_back] + deltas + [delta_after] + slopes[1:] + flat(fields),
         flops=work * (2 * pairs - 1) * share,
         moved=space * 6 * pairs,
+        loose=1,
     )
     later, partial_total = list(made[:-1]), made[-1]
 
@@ -624,32 +644,28 @@
         )
         shares = [kept[0]] + [to_chan(kept[j], extent - j) for j in range(1, extent)]
         shares += [stepped(kept[j], 2, extent - j) for j in range(extent)]
-        (mine,) = call(add_kernel, [portion], shares)
+        (mine,) = call(functools.partial(add_kernel, 0), [portion], shares)
         made = [made[0]] + [relayed(value, mine) for value in made[1:]]
     pieces = exchanged(made) + pieces
 
-    def merged(value):
-        return call(
-            functools.partial(merge_kernel, extent),
-            [
-                jax.ShapeDtypeStruct(value.shape, value.dtype),
-                jax.ShapeDtypeStruct(field.shape, BF16),
-            ],
-            [value] + pieces,
-            [pltpu.VMEM((rows * planes * size, depth), F32)],
-            moved=4 * field.size,
-            loose=1,
-            same={0: 0},
-        )
-
+    token, input_grad = call(
+        functools.partial(merge_kernel, extent),
+        [jax.ShapeDtypeStruct((8, 128), F32), jax.ShapeDtypeStruct(field.shape, BF16)],
+        pieces,
+        [pltpu.VMEM((rows * planes * size, depth), F32)],
+        moved=4 * field.size,
+    )
     if plain:
         stride = 4
         while stride < slabs:
             radix = 4 if slabs % (4 * stride) == 0 else 2
             got = [mine] + [stepped(mine, m * stride) for m in range(1, radix)]
-            (mine,) = call(add_kernel, [portion], got)
+            last = stride * radix == slabs
+            ahead = [token] if last else []
+            (mine,) = call(
+                functools.partial(add_kernel, len(ahead)), [portion], ahead + got, loose=len(ahead)
+            )
             stride *= radix
-        mine, input_grad = merged(mine)
         other = stepped(mine, 1)
     else:
         mine, other = keep[0], send[0]
@@ -658,7 +674,6 @@
         even = lax.rem(lax.axis_index("slab"), 2) == 0
         mine, other = jnp.where(even, mine, other), jnp.where(even, other, mine)
         mine, other = lax.psum((mine, other), "slab")
-        mine, input_grad = merged(mine)
         mine, other = jnp.where(even, mine, other), jnp.where(even, other, mine)
     first_grad, second_grad = call(
         functools.partial(finish_kernel, factor),

time: 73.2 us -> 70.7 us (0.966)
  waiting for transfers between devices: 20.1 us -> 14.5 us
  starting transfers between devices: 26.9 us -> 28.4 us
  local copies, waits for them, and re-layouts: 2.92 us -> 4.33 us
    ppermute x3, waiting for transfers between devices: 0.28 us -> 5.05 us  [to_next(): lax.ppermute(value, 'slab', [(i, (i + 1) % slabs) for i in range(slabs)])]
    ppermute x6 -> x5, waiting for transfers between devices: 6.85 us -> 2.76 us  [to_chan(): lax.ppermute(value, 'chan', [(i, (i + shift) % extent) for i in range(ext...]
    ppermute x3, starting transfers between devices: 7.37 us -> 11.4 us  [to_prev(): lax.ppermute(value, 'slab', [((i + 1) % slabs, i) for i in range(slabs)])]
    ppermute x3, waiting for transfers between devices: 3.16 us -> 0.01 us  [to_prev(): lax.ppermute(value, 'slab', [((i + 1) % slabs, i) for i in range(slabs)])]
    ppermute x6 -> x5, starting transfers between devices: 8.95 us -> 6.25 us  [to_chan(): lax.ppermute(value, 'chan', [(i, (i + shift) % extent) for i in range(ext...]
    ppermute x6, waiting for transfers between devices: 7.78 us -> 6.04 us  [stepped(): return lax.ppermute(value, 'slab', [(i, i ^ stride) for i in range(slabs)])]
    ppermute x1, waiting for transfers between devices: 2.08 us -> 0.6 us  [stepped(): return lax.ppermute(value, ('slab', 'chan'), pairs_of)]
    ppermute x6, starting transfers between devices: 8.05 us -> 6.58 us  [stepped(): return lax.ppermute(value, 'slab', [(i, i ^ stride) for i in range(slabs)])]
  transfers between devices with their start and end apart: 19 -> 18, of which waited for: 12 -> 10; matrix products, arithmetic and copies ran while one was open for 0% -> 0% of each run, Pallas kernels for 25% -> 28%
where the time goes in v8:
time: 70.7 us; the launch traced here: 70.4 us
  starting transfers between devices  28.4 us (40%)
  Pallas kernels  22.4 us (32%)
  waiting for transfers between devices  14.5 us (21%)
  local copies, waits for them, and re-layouts  4.33 us (6%)
  between operations  0.8 us (1%)
    pallas_call x18, Pallas kernels, call(): pl.pallas_call(kernel, out_shape=outs, in_specs=[still] * loose + [whole]...  22.4 us
    ppermute x3, starting transfers between devices, to_prev(): lax.ppermute(value, 'slab', [((i + 1) % slabs, i) for i in range(slabs)])  11.4 us
    ppermute x6, starting transfers between devices, stepped(): return lax.ppermute(value, 'slab', [(i, i ^ stride) for i in range(slabs)])  6.58 us
    ppermute x5, starting transfers between devices, to_chan(): lax.ppermute(value, 'chan', [(i, (i + shift) % extent) for i in range(ext...  6.25 us
    ppermute x6, waiting for transfers between devices, stepped(): return lax.ppermute(value, 'slab', [(i, i ^ stride) for i in range(slabs)])  6.04 us
    ppermute x3, waiting for transfers between devices, to_next(): lax.ppermute(value, 'slab', [(i, (i + 1) % slabs) for i in range(slabs)])  5.05 us
    unnamed x8, local copies, waits for them, and re-layouts  4.33 us
    ppermute x1, starting transfers between devices, stepped(): return lax.ppermute(value, ('slab', 'chan'), pairs_of)  3.2 us
  transfers between devices with their start and end apart: 18, of which 10 were waited for; matrix products, arithmetic and copies ran while one was open for 0% of the time, Pallas kernels for 28%

profile of v8, /device:TPU:0, one launch (start us, length us, event | category | flops | bytes accessed | tf_op | source)
XLA Modules:
  0.0 70.4 jit_solution(18339915096132825720)
XLA Ops:
  0.6 0.0 copy-start.1
  0.6 1.1 %copy-done.1 = bf16[16,4,48,128]{3,2,1,0:T(8,128)(2,1)S(1)} copy-done((bf16[16,4,48,128]{3,2,1,0:T(8,128)(2,1)S(1)}, bf16[16,4,48,128]{3,2,1,0:T(8,128)(2,1)}, u32[]{:S(2)}) %copy-start.1) | copy-done | bytes 786456
  1.8 1.5 %shard_map.67 = (bf16[32,2,16,128]{3,2,1,0:T(8,128)(2,1)S(1)}, bf16[32,2,16,128]{3,2,1,0:T(8,128)(2,1)S(1)}, bf16[39,2,16,128]{3,2,1,0:T(8,128)(2,1)S(1)}, bf16[32,2,16,128]{3,2,1,0:T(8,128)(2,1)S(1)}) custom-call(bf16[16,4,48,128]{3,2,1,0:T(8,128)(2,1)S(1)} %copy-done.1), custom_call_target="tpu_custom_call" | custom-call | bytes 2359296 | tf_op jit(solution)/shard_map/pallas_call | solution.py:19
  3.3 3.0 %collective-permute-start.1 = (bf16[32,2,16,128]{3,2,1,0:T(8,128)(2,1)S(1)}, bf16[32,2,16,128]{3,2,1,0:T(8,128)(2,1)S(1)}, u32[]{:S(2)}, u32[]{:S(2)}) collective-permute-start(bf16[32,2,16,128]{3,2,1,0:T(8,128)(2,1)S(1)} %get-tuple-element.40), channel_id=1, source_target_pairs={{0,1},{1,0},{2,3},{3,2},{4,5},{5,4},{6,7},{7,6},{8,9},{9,8},{10,11... | collective-permute-start | bytes 786440 | tf_op jit(solution)/shard_map/ppermute | solution.py:463
  6.3 0.0 copy-start.2
  6.3 0.9 %copy-done.2 = bf16[16,27,32]{2,0,1:T(8,128)(2,1)S(1)} copy-done((bf16[16,27,32]{2,0,1:T(8,128)(2,1)S(1)}, bf16[16,27,32]{2,0,1:T(8,128)(2,1)}, u32[]{:S(2)}) %copy-start.2) | copy-done | bytes 27672
  7.2 0.0 copy-start.3
  7.2 0.9 %copy-done.3 = bf16[16,27,32]{2,0,1:T(8,128)(2,1)S(1)} copy-done((bf16[16,27,32]{2,0,1:T(8,128)(2,1)S(1)}, bf16[16,27,32]{2,0,1:T(8,128)(2,1)}, u32[]{:S(2)}) %copy-start.3) | copy-done | bytes 27672
  8.1 0.2 shard_map.68
  8.3 0.1 collective-permute-start.3
  8.3 0.1 collective-permute-start
  8.4 4.4 %collective-permute-start.4 = (bf16[32,2,16,128]{3,2,1,0:T(8,128)(2,1)S(1)}, bf16[32,2,16,128]{3,2,1,0:T(8,128)(2,1)S(1)}, u32[]{:S(2)}, u32[]{:S(2)}) collective-permute-start(bf16[32,2,16,128]{3,2,1,0:T(8,128)(2,1)S(1)} %get-tuple-element.41.refs_2_.refs_8_.refs_6_), channel_id=1, source_target_pairs={{2,0},{4,2},{6,4},{8,6},{10,8},{12,10},{14,12},{16,14},{18,16},{20... | collective-permute-start | bytes 786440 | tf_op jit(solution)/shard_map/ppermute | solution.py:469
  12.8 0.6 collective-permute-done.1.refs_5_.refs_1_.refs_11_
  13.4 0.0 collective-permute-start.2
  13.4 3.6 %collective-permute-done.one.refs_0_.refs_6_.refs_4_ = bf16[32,2,16,128]{3,2,1,0:T(8,128)(2,1)S(1)} collective-permute-done((bf16[32,2,16,128]{3,2,1,0:T(8,128)(2,1)S(1)}, bf16[32,2,16,128]{3,2,1,0:T(8,128)(2,1)S(1)}, u32[]{:S(2)}, u32[]{:S(2)}) %collective-permute-start) | collective-permute-done | bytes 262176 | tf_op jit(solution)/shard_map/ppermute | solution.py:466
  17.0 0.0 collective-permute-done.4.two.refs_2_.refs_12_
  17.0 0.0 copy-start
  17.0 1.4 %copy-done = bf16[32,4,48,128]{3,2,1,0:T(8,128)(2,1)S(1)} copy-done((bf16[32,4,48,128]{3,2,1,0:T(8,128)(2,1)S(1)}, bf16[32,4,48,128]{3,2,1,0:T(8,128)(2,1)}, u32[]{:S(2)}) %copy-start) | copy-done | bytes 1572888
  18.4 1.3 %shard_map.69 = (bf16[28,2,32,128]{3,2,1,0:T(8,128)(2,1)S(1)}, bf16[28,2,32,128]{3,2,1,0:T(8,128)(2,1)S(1)}) custom-call(bf16[32,2,16,128]{3,2,1,0:T(8,128)(2,1)S(1)} %collective-permute-done.one.refs_0_.refs_6_.refs_4_, bf16[32,2,16,128]{3,2,1,0:T(8,128)(2,1)S(1)} %collective-permute-done.4.two.refs_2_.refs_12_, bf16[32,4,48,128]{3,2,1,0:T(8,128)(2,1)S(1)} %copy-done), custom_call_target="tpu_custom_call" | custom-call | bytes 3145728 | tf_op jit(solution)/shard_map/pallas_call | solution.py:19
  19.7 0.0 collective-permute-done.3.refs_0_.refs_1_
  19.7 0.5 shard_map.71
  20.3 4.5 %collective-permute-start.5 = (bf16[39,2,16,128]{3,2,1,0:T(8,128)(2,1)S(1)}, bf16[39,2,16,128]{3,2,1,0:T(8,128)(2,1)S(1)}, u32[]{:S(2)}, u32[]{:S(2)}) collective-permute-start(bf16[39,2,16,128]{3,2,1,0:T(8,128)(2,1)S(1)} %shard_map.70.refs_3_.refs_9_.refs_7_), channel_id=1, source_target_pairs={{2,0},{4,2},{6,4},{8,6},{10,8},{12,10},{14,12},{16,14},{18,16},{20... | collective-permute-start | bytes 958472 | tf_op jit(solution)/shard_map/ppermute | solution.py:469
  24.8 0.0 collective-permute-done.2.refs_1_.refs_7_.refs_5_
  24.8 3.6 %shard_map.72 = (bf16[30,2,32,128]{3,2,1,0:T(8,128)(2,1)S(1)}, bf16[30,2,32,128]{3,2,1,0:T(8,128)(2,1)S(1)}, bf16[30,2,32,128]{3,2,1,0:T(8,128)(2,1)S(1)}, bf16[...) custom-call(bf16[32,2,16,128]{3,2,1,0:T(8,128)(2,1)S(1)} %collective-permute-done.one.refs_0_.refs_6_.refs_4_, ...), custom_call_target="tpu_custom_call" | custom-call | flops 1019215872 | bytes 3145728 | tf_op jit(solution)/shard_map/pallas_call | solution.py:19
  28.4 2.5 %collective-permute-start.6 = (bf16[28,2,32,128]{3,2,1,0:T(8,128)(2,1)S(1)}, bf16[28,2,32,128]{3,2,1,0:T(8,128)(2,1)S(1)}, u32[]{:S(2)}, u32[]{:S(2)}) collective-permute-start(bf16[28,2,32,128]{3,2,1,0:T(8,128)(2,1)S(1)} %get-tuple-element.52.refs_3_.refs_1_.refs_2_), channel_id=1, source_target_pairs={{2,0},{4,2},{6,4},{8,6},{10,8},{12,10},{14,12},{16,14},{18,16},{20... | collective-permute-start | bytes 1376264 | tf_op jit(solution)/shard_map/ppermute | solution.py:469
  30.9 0.0 collective-permute-done.5.refs_3_.refs_13_
  30.9 2.8 %shard_map.73 = (bf16[30,2,32,128]{3,2,1,0:T(8,128)(2,1)S(1)}, bf16[30,2,32,128]{3,2,1,0:T(8,128)(2,1)S(1)}, bf16[28,2,32,128]{3,2,1,0:T(8,128)(2,1)S(1)}) custom-call(bf16[32,2,16,128]{3,2,1,0:T(8,128)(2,1)S(1)} %get-tuple-element.39.refs_4_.refs_0_.refs_10_, bf16[32,2,16,128]{3,2,1,0:T(8,128)(2,1)S(1)} %collective-permute-done.1.refs_5_.refs_1_.refs_11_, ...), custom_call_target="tpu_custom_call" | custom-call | flops 679477248 | bytes 2359296 | tf_op jit(solution)/shard_map/pallas_call | solution.py:19
  33.7 0.9 %collective-permute-start.7 = (bf16[28,2,32,128]{3,2,1,0:T(8,128)(2,1)S(1)}, bf16[28,2,32,128]{3,2,1,0:T(8,128)(2,1)S(1)}, u32[]{:S(2)}, u32[]{:S(2)}) collective-permute-start(bf16[28,2,32,128]{3,2,1,0:T(8,128)(2,1)S(1)} %get-tuple-element.53.refs_4_.refs_2_), channel_id=1, source_target_pairs={{0,2},{2,4},{4,6},{6,8},{8,10},{10,12},{12,14},{14,16},{16,18},{18... | collective-permute-start | bytes 1376264 | tf_op jit(solution)/shard_map/ppermute | solution.py:466
  34.6 2.5 %shard_map.74.after.refs_9_ = f32[2,7,16,128]{3,2,1,0:T(8,128)S(1)} custom-call(bf16[30,2,32,128]{3,2,1,0:T(8,128)(2,1)S(1)} %get-tuple-element.48.refs_0_, bf16[30,2,32,128]{3,2,1,0:T(8,128)(2,1)S(1)} %get-tuple-element.49.refs_4_.refs_1_, bf16[30,2,32,128]{3,2,1,0:T(8,128)(2,1)S(1)} %get-tuple-element.51.refs_2_, ...), custom_call_target="tpu_custom_call" | custom-call | flops 679477248 | bytes 1966080 | tf_op jit(solution)/shard_map/pallas_call | solution.py:19
  37.1 0.0 collective-permute-done.6.refs_3_
  37.1 3.3 %shard_map.75 = (bf16[26,2,32,128]{3,2,1,0:T(8,128)(2,1)S(1)}, bf16[26,2,32,128]{3,2,1,0:T(8,128)(2,1)S(1)}, f32[192,384]{1,0:T(8,128)S(1)}) custom-call(f32[2,7,16,128]{3,2,1,0:T(8,128)S(1)} %shard_map.74.after.refs_9_, bf16[192,384]{1,0:T(8,128)(2,1)S(1)} %get-tuple-element.54.refs_0_, ...), custom_call_target="tpu_custom_call" | custom-call | flops 1019215872 | bytes 4718592 | tf_op jit(solution)/shard_map/pallas_call | solution.py:19
  40.5 1.1 %shard_map.76 = (bf16[24,2,16,128]{3,2,1,0:T(8,128)(2,1)S(1)}, bf16[24,2,16,128]{3,2,1,0:T(8,128)(2,1)S(1)}) custom-call(bf16[26,2,32,128]{3,2,1,0:T(8,128)(2,1)S(1)} %get-tuple-element.57.refs_0_.refs_1_, bf16[26,2,32,128]{3,2,1,0:T(8,128)(2,1)S(1)} %get-tuple-element.58.refs_1_, bf16[192,384]{1,0:T(8,128)(2,1)S(1)} %get-tuple-element.59.refs_2_), custom_call_target="tpu_custom_call" | custom-call | flops 339738624 | bytes 786432 | tf_op jit(solution)/shard_map/pallas_call | solution.py:19
  41.6 1.3 %collective-permute-start.8 = (bf16[24,2,16,128]{3,2,1,0:T(8,128)(2,1)S(1)}, bf16[24,2,16,128]{3,2,1,0:T(8,128)(2,1)S(1)}, u32[]{:S(2)}, u32[]{:S(2)}) collective-permute-start(bf16[24,2,16,128]{3,2,1,0:T(8,128)(2,1)S(1)} %get-tuple-element.66), channel_id=1, source_target_pairs={{0,1},{1,0},{2,3},{3,2},{4,5},{5,4},{6,7},{7,6},{8,9},{9,8},{10,11... | collective-permute-start | bytes 589832 | tf_op jit(solution)/shard_map/ppermute | solution.py:463
  42.9 1.4 %collective-permute-done.7.refs_1_ = bf16[28,2,32,128]{3,2,1,0:T(8,128)(2,1)S(1)} collective-permute-done((bf16[28,2,32,128]{3,2,1,0:T(8,128)(2,1)S(1)}, bf16[28,2,32,128]{3,2,1,0:T(8,128)(2,1)S(1)}, u32[]{:S(2)}, u32[]{:S(2)}) %collective-permute-start.7) | collective-permute-done | bytes 458784 | tf_op jit(solution)/shard_map/ppermute | solution.py:466
  44.4 1.5 %shard_map.77 = (bf16[26,2,32,128]{3,2,1,0:T(8,128)(2,1)S(1)}, f32[2,7,16,128]{3,2,1,0:T(8,128)S(1)}, f32[2,7,16,128]{3,2,1,0:T(8,128)S(1)}) custom-call(bf16[24,2,16,128]{3,2,1,0:T(8,128)(2,1)S(1)} %get-tuple-element.60.after.refs_2_, bf16[192,384]{1,0:T(8,128)(2,1)S(1)} %get-tuple-element.54.refs_0_, ...), custom_call_target="tpu_custom_call" | custom-call | flops 679477248 | bytes 2359296 | tf_op jit(solution)/shard_map/pallas_call | solution.py:19
  45.9 0.1 collective-permute-start.9
  46.0 1.1 %shard_map.78 = (bf16[24,2,16,128]{3,2,1,0:T(8,128)(2,1)S(1)}, bf16[24,2,16,128]{3,2,1,0:T(8,128)(2,1)S(1)}) custom-call(bf16[26,2,32,128]{3,2,1,0:T(8,128)(2,1)S(1)} %get-tuple-element.63.refs_0_, bf16[26,2,32,128]{3,2,1,0:T(8,128)(2,1)S(1)} %get-tuple-element.57.refs_0_.refs_1_, bf16[192,384]{1,0:T(8,128)(2,1)S(1)} %get-tuple-element.59.refs_2_), custom_call_target="tpu_custom_call" | custom-call | flops 339738624 | bytes 786432 | tf_op jit(solution)/shard_map/pallas_call | solution.py:19
  47.1 1.4 %collective-permute-done.8.refs_1_.refs_3_ = bf16[24,2,16,128]{3,2,1,0:T(8,128)(2,1)S(1)} collective-permute-done((bf16[24,2,16,128]{3,2,1,0:T(8,128)(2,1)S(1)}, bf16[24,2,16,128]{3,2,1,0:T(8,128)(2,1)S(1)}, u32[]{:S(2)}, u32[]{:S(2)}) %collective-permute-start.8) | collective-permute-done | bytes 196640 | tf_op jit(solution)/shard_map/ppermute | solution.py:463
  48.5 0.0 collective-permute-done.9.refs_3_
  48.5 0.4 collective-permute-start.10
  48.9 0.0 collective-permute-start.11
  48.9 3.2 %collective-permute-start.12 = (f32[7,16,128]{2,1,0:T(8,128)S(1)}, f32[7,16,128]{2,1,0:T(8,128)S(1)}, u32[]{:S(2)}, u32[]{:S(2)}) collective-permute-start(f32[7,16,128]{2,1,0:T(8,128)S(1)} %get-tuple-element.70), channel_id=1, source_target_pairs={{0,5},{1,4},{2,7},{3,6},{4,1},{5,0},{6,3},{7,2},{8,13},{9,12},{10,... | collective-permute-start | bytes 172040 | tf_op jit(solution)/shard_map/ppermute | solution.py:632
  52.1 0.8 %collective-permute-done.10.refs_1_ = f32[7,16,128]{2,1,0:T(8,128)S(1)} collective-permute-done((f32[7,16,128]{2,1,0:T(8,128)S(1)}, f32[7,16,128]{2,1,0:T(8,128)S(1)}, u32[]{:S(2)}, u32[]{:S(2)}) %collective-permute-start.10) | collective-permute-done | bytes 57376 | tf_op jit(solution)/shard_map/ppermute | solution.py:463
  52.9 0.8 %collective-permute-done.11.refs_2_ = f32[7,16,128]{2,1,0:T(8,128)S(1)} collective-permute-done((f32[7,16,128]{2,1,0:T(8,128)S(1)}, f32[7,16,128]{2,1,0:T(8,128)S(1)}, u32[]{:S(2)}, u32[]{:S(2)}) %collective-permute-start.11) | collective-permute-done | bytes 57376 | tf_op jit(solution)/shard_map/ppermute | solution.py:626
  53.6 0.6 collective-permute-done.12.refs_3_
  54.3 1.5 %collective-permute-start.13 = (bf16[24,2,16,128]{3,2,1,0:T(8,128)(2,1)S(1)}, bf16[24,2,16,128]{3,2,1,0:T(8,128)(2,1)S(1)}, u32[]{:S(2)}, u32[]{:S(2)}) collective-permute-start(bf16[24,2,16,128]{3,2,1,0:T(8,128)(2,1)S(1)} %shard_map.81), channel_id=1, source_target_pairs={{0,1},{1,0},{2,3},{3,2},{4,5},{5,4},{6,7},{7,6},{8,9},{9,8},{10,11... | collective-permute-start | bytes 589832 | tf_op jit(solution)/shard_map/ppermute | solution.py:463
  55.8 3.9 %collective-permute-start.14 = (f32[7,16,128]{2,1,0:T(8,128)S(1)}, f32[7,16,128]{2,1,0:T(8,128)S(1)}, u32[]{:S(2)}, u32[]{:S(2)}) collective-permute-start(f32[7,16,128]{2,1,0:T(8,128)S(1)} %shard_map.80.refs_1_), channel_id=1, source_target_pairs={{0,8},{2,10},{4,12},{6,14},{8,0},{10,2},{12,4},{14,6},{16,24},{18,... | collective-permute-start | bytes 172040 | tf_op jit(solution)/shard_map/ppermute | solution.py:626
  59.6 2.6 %collective-permute-start.15 = (f32[7,16,128]{2,1,0:T(8,128)S(1)}, f32[7,16,128]{2,1,0:T(8,128)S(1)}, u32[]{:S(2)}, u32[]{:S(2)}) collective-permute-start(f32[7,16,128]{2,1,0:T(8,128)S(1)} %shard_map.80.refs_1_), channel_id=1, source_target_pairs={{0,16},{2,18},{4,20},{6,22},{8,24},{10,26},{12,28},{14,30},{16,0},... | collective-permute-start | bytes 172040 | tf_op jit(solution)/shard_map/ppermute | solution.py:626
  62.2 0.0 collective-permute-start.16
  62.2 0.0 collective-permute-done.13.refs_1_
  62.2 1.9 %shard_map.82 = (f32[8,128]{1,0:T(8,128)S(1)}, bf16[16,4,48,128]{3,2,1,0:T(8,128)(2,1)}) custom-call(bf16[24,2,16,128]{3,2,1,0:T(8,128)(2,1)S(1)} %get-tuple-element.64.refs_0_, bf16[24,2,16,128]{3,2,1,0:T(8,128)(2,1)S(1)} %collective-permute-done.13.refs_1_, bf16[24,2,16,128]{3,2,1,0:T(8,128)(2,1)S(1)} %get-tuple-element.60.after.refs_2_, ...), custom_call_target="tpu_custom_call" | custom-call | bytes 1572864 | tf_op jit(solution)/shard_map/pallas_call | solution.py:19
  64.1 0.0 collective-permute-done.14.refs_2_
  64.1 1.7 %collective-permute-done.15.refs_3_ = f32[7,16,128]{2,1,0:T(8,128)S(1)} collective-permute-done((f32[7,16,128]{2,1,0:T(8,128)S(1)}, f32[7,16,128]{2,1,0:T(8,128)S(1)}, u32[]{:S(2)}, u32[]{:S(2)}) %collective-permute-start.15) | collective-permute-done | bytes 57376 | tf_op jit(solution)/shard_map/ppermute | solution.py:626
  65.8 2.3 %collective-permute-done.16.refs_4_ = f32[7,16,128]{2,1,0:T(8,128)S(1)} collective-permute-done((f32[7,16,128]{2,1,0:T(8,128)S(1)}, f32[7,16,128]{2,1,0:T(8,128)S(1)}, u32[]{:S(2)}, u32[]{:S(2)}) %collective-permute-start.16) | collective-permute-done | bytes 57376 | tf_op jit(solution)/shard_map/ppermute | solution.py:626
  68.2 0.1 collective-permute-start.17
  68.3 1.2 %collective-permute-done.17.other = f32[7,16,128]{2,1,0:T(8,128)S(1)} collective-permute-done((f32[7,16,128]{2,1,0:T(8,128)S(1)}, f32[7,16,128]{2,1,0:T(8,128)S(1)}, u32[]{:S(2)}, u32[]{:S(2)}) %collective-permute-start.17) | collective-permute-done | bytes 57376 | tf_op jit(solution)/shard_map/ppermute | solution.py:626
  69.5 0.9 %shard_map.84 = (f32[27,16,32]{2,1,0:T(8,128)}, f32[27,16,32]{2,1,0:T(8,128)}) custom-call(f32[7,16,128]{2,1,0:T(8,128)S(1)} %shard_map.83.mine, f32[7,16,128]{2,1,0:T(8,128)S(1)} %collective-permute-done.17.other), custom_call_target="tpu_custom_call" | custom-call | tf_op jit(solution)/shard_map/pallas_call | solution.py:19
  (5 shorter events, 0.1 us)
Async XLA Ops:
  0.6 1.1 %copy-start.1 = (bf16[16,4,48,128]{3,2,1,0:T(8,128)(2,1)S(1)}, bf16[16,4,48,128]{3,2,1,0:T(8,128)(2,1)}, u32[]{:S(2)}) copy-start(bf16[16,4,48,128]{3,2,1,0:T(8,128)(2,1)} %x_ref.2) | copy-start | bytes 2359300
  3.3 10.1 %collective-permute-start.1 = (bf16[32,2,16,128]{3,2,1,0:T(8,128)(2,1)S(1)}, bf16[32,2,16,128]{3,2,1,0:T(8,128)(2,1)S(1)}, u32[]{:S(2)}, u32[]{:S(2)}) collective-permute-start(bf16[32,2,16,128]{3,2,1,0:T(8,128)(2,1)S(1)} %get-tuple-element.40), channel_id=1, source_target_pairs={{0,1},{1,0},{2,3},{3,2},{4,5},{5,4},{6,7},{7,6},{8,9},{9,8},{10,11... | collective-permute-start | bytes 786440 | tf_op jit(solution)/shard_map/ppermute | solution.py:463
  6.3 0.9 %copy-start.2 = (bf16[16,27,32]{2,0,1:T(8,128)(2,1)S(1)}, bf16[16,27,32]{2,0,1:T(8,128)(2,1)}, u32[]{:S(2)}) copy-start(bf16[16,27,32]{2,0,1:T(8,128)(2,1)} %param.6) | copy-start | bytes 82948
  7.2 0.9 %copy-start.3 = (bf16[16,27,32]{2,0,1:T(8,128)(2,1)S(1)}, bf16[16,27,32]{2,0,1:T(8,128)(2,1)}, u32[]{:S(2)}) copy-start(bf16[16,27,32]{2,0,1:T(8,128)(2,1)} %param.7) | copy-start | bytes 82948
  8.3 11.5 %collective-permute-start.3 = (bf16[39,2,16,128]{3,2,1,0:T(8,128)(2,1)S(1)}, bf16[39,2,16,128]{3,2,1,0:T(8,128)(2,1)S(1)}, u32[]{:S(2)}, u32[]{:S(2)}) collective-permute-start(bf16[39,2,16,128]{3,2,1,0:T(8,128)(2,1)S(1)} %get-tuple-element.43), channel_id=1, source_target_pairs={{0,1},{1,0},{2,3},{3,2},{4,5},{5,4},{6,7},{7,6},{8,9},{9,8},{10,11... | collective-permute-start | bytes 958472 | tf_op jit(solution)/shard_map/ppermute | solution.py:463
  8.3 8.7 %collective-permute-start = (bf16[32,2,16,128]{3,2,1,0:T(8,128)(2,1)S(1)}, bf16[32,2,16,128]{3,2,1,0:T(8,128)(2,1)S(1)}, u32[]{:S(2)}, u32[]{:S(2)}) collective-permute-start(bf16[32,2,16,128]{3,2,1,0:T(8,128)(2,1)S(1)} %get-tuple-element.39.refs_4_.refs_0_.refs_10_), channel_id=1, source_target_pairs={{0,2},{2,4},{4,6},{6,8},{8,10},{10,12},{12,14},{14,16},{16,18},{18... | collective-permute-start | bytes 786440 | tf_op jit(solution)/shard_map/ppermute | solution.py:466
  8.4 8.6 %collective-permute-start.4 = (bf16[32,2,16,128]{3,2,1,0:T(8,128)(2,1)S(1)}, bf16[32,2,16,128]{3,2,1,0:T(8,128)(2,1)S(1)}, u32[]{:S(2)}, u32[]{:S(2)}) collective-permute-start(bf16[32,2,16,128]{3,2,1,0:T(8,128)(2,1)S(1)} %get-tuple-element.41.refs_2_.refs_8_.refs_6_), channel_id=1, source_target_pairs={{2,0},{4,2},{6,4},{8,6},{10,8},{12,10},{14,12},{16,14},{18,16},{20... | collective-permute-start | bytes 786440 | tf_op jit(solution)/shard_map/ppermute | solution.py:469
  13.4 11.4 %collective-permute-start.2 = (bf16[32,2,16,128]{3,2,1,0:T(8,128)(2,1)S(1)}, bf16[32,2,16,128]{3,2,1,0:T(8,128)(2,1)S(1)}, u32[]{:S(2)}, u32[]{:S(2)}) collective-permute-start(bf16[32,2,16,128]{3,2,1,0:T(8,128)(2,1)S(1)} %collective-permute-done.1.refs_5_.refs_1_.refs_11_), channel_id=1, source_target_pairs={{0,2},{2,4},{4,6},{6,8},{8,10},{10,12},{12,14},{14,16},{16,18},{18... | collective-permute-start | bytes 786440 | tf_op jit(solution)/shard_map/ppermute | solution.py:466
  17.0 1.4 %copy-start = (bf16[32,4,48,128]{3,2,1,0:T(8,128)(2,1)S(1)}, bf16[32,4,48,128]{3,2,1,0:T(8,128)(2,1)}, u32[]{:S(2)}) copy-start(bf16[32,4,48,128]{3,2,1,0:T(8,128)(2,1)} %x_ref.3) | copy-start | bytes 4718596
  20.3 10.6 %collective-permute-start.5 = (bf16[39,2,16,128]{3,2,1,0:T(8,128)(2,1)S(1)}, bf16[39,2,16,128]{3,2,1,0:T(8,128)(2,1)S(1)}, u32[]{:S(2)}, u32[]{:S(2)}) collective-permute-start(bf16[39,2,16,128]{3,2,1,0:T(8,128)(2,1)S(1)} %shard_map.70.refs_3_.refs_9_.refs_7_), channel_id=1, source_target_pairs={{2,0},{4,2},{6,4},{8,6},{10,8},{12,10},{14,12},{16,14},{18,16},{20... | collective-permute-start | bytes 958472 | tf_op jit(solution)/shard_map/ppermute | solution.py:469
  28.4 8.7 %collective-permute-start.6 = (bf16[28,2,32,128]{3,2,1,0:T(8,128)(2,1)S(1)}, bf16[28,2,32,128]{3,2,1,0:T(8,128)(2,1)S(1)}, u32[]{:S(2)}, u32[]{:S(2)}) collective-permute-start(bf16[28,2,32,128]{3,2,1,0:T(8,128)(2,1)S(1)} %get-tuple-element.52.refs_3_.refs_1_.refs_2_), channel_id=1, source_target_pairs={{2,0},{4,2},{6,4},{8,6},{10,8},{12,10},{14,12},{16,14},{18,16},{20... | collective-permute-start | bytes 1376264 | tf_op jit(solution)/shard_map/ppermute | solution.py:469
  33.7 10.7 %collective-permute-start.7 = (bf16[28,2,32,128]{3,2,1,0:T(8,128)(2,1)S(1)}, bf16[28,2,32,128]{3,2,1,0:T(8,128)(2,1)S(1)}, u32[]{:S(2)}, u32[]{:S(2)}) collective-permute-start(bf16[28,2,32,128]{3,2,1,0:T(8,128)(2,1)S(1)} %get-tuple-element.53.refs_4_.refs_2_), channel_id=1, source_target_pairs={{0,2},{2,4},{4,6},{6,8},{8,10},{10,12},{12,14},{14,16},{16,18},{18... | collective-permute-start | bytes 1376264 | tf_op jit(solution)/shard_map/ppermute | solution.py:466
  41.6 6.9 %collective-permute-start.8 = (bf16[24,2,16,128]{3,2,1,0:T(8,128)(2,1)S(1)}, bf16[24,2,16,128]{3,2,1,0:T(8,128)(2,1)S(1)}, u32[]{:S(2)}, u32[]{:S(2)}) collective-permute-start(bf16[24,2,16,128]{3,2,1,0:T(8,128)(2,1)S(1)} %get-tuple-element.66), channel_id=1, source_target_pairs={{0,1},{1,0},{2,3},{3,2},{4,5},{5,4},{6,7},{7,6},{8,9},{9,8},{10,11... | collective-permute-start | bytes 589832 | tf_op jit(solution)/shard_map/ppermute | solution.py:463
  45.9 2.6 %collective-permute-start.9 = (f32[2,7,16,128]{3,2,1,0:T(8,128)S(1)}, f32[2,7,16,128]{3,2,1,0:T(8,128)S(1)}, u32[]{:S(2)}, u32[]{:S(2)}) collective-permute-start(f32[2,7,16,128]{3,2,1,0:T(8,128)S(1)} %get-tuple-element.68), channel_id=1, source_target_pairs={{0,2},{2,0},{4,6},{6,4},{8,10},{10,8},{12,14},{14,12},{16,18},{18,... | collective-permute-start | bytes 344072 | tf_op jit(solution)/shard_map/ppermute | solution.py:626
  48.5 4.4 %collective-permute-start.10 = (f32[7,16,128]{2,1,0:T(8,128)S(1)}, f32[7,16,128]{2,1,0:T(8,128)S(1)}, u32[]{:S(2)}, u32[]{:S(2)}) collective-permute-start(f32[7,16,128]{2,1,0:T(8,128)S(1)} %get-tuple-element.70), channel_id=1, source_target_pairs={{0,1},{1,0},{2,3},{3,2},{4,5},{5,4},{6,7},{7,6},{8,9},{9,8},{10,11... | collective-permute-start | bytes 172040 | tf_op jit(solution)/shard_map/ppermute | solution.py:463
  48.9 4.8 %collective-permute-start.11 = (f32[7,16,128]{2,1,0:T(8,128)S(1)}, f32[7,16,128]{2,1,0:T(8,128)S(1)}, u32[]{:S(2)}, u32[]{:S(2)}) collective-permute-start(f32[7,16,128]{2,1,0:T(8,128)S(1)} %get-tuple-element.69.refs_0_), channel_id=1, source_target_pairs={{0,4},{2,6},{4,0},{6,2},{8,12},{10,14},{12,8},{14,10},{16,20},{18,... | collective-permute-start | bytes 172040 | tf_op jit(solution)/shard_map/ppermute | solution.py:626
  48.9 5.4 %collective-permute-start.12 = (f32[7,16,128]{2,1,0:T(8,128)S(1)}, f32[7,16,128]{2,1,0:T(8,128)S(1)}, u32[]{:S(2)}, u32[]{:S(2)}) collective-permute-start(f32[7,16,128]{2,1,0:T(8,128)S(1)} %get-tuple-element.70), channel_id=1, source_target_pairs={{0,5},{1,4},{2,7},{3,6},{4,1},{5,0},{6,3},{7,2},{8,13},{9,12},{10,... | collective-permute-start | bytes 172040 | tf_op jit(solution)/shard_map/ppermute | solution.py:632
  54.3 7.9 %collective-permute-start.13 = (bf16[24,2,16,128]{3,2,1,0:T(8,128)(2,1)S(1)}, bf16[24,2,16,128]{3,2,1,0:T(8,128)(2,1)S(1)}, u32[]{:S(2)}, u32[]{:S(2)}) collective-permute-start(bf16[24,2,16,128]{3,2,1,0:T(8,128)(2,1)S(1)} %shard_map.81), channel_id=1, source_target_pairs={{0,1},{1,0},{2,3},{3,2},{4,5},{5,4},{6,7},{7,6},{8,9},{9,8},{10,11... | collective-permute-start | bytes 589832 | tf_op jit(solution)/shard_map/ppermute | solution.py:463
  55.8 8.4 %collective-permute-start.14 = (f32[7,16,128]{2,1,0:T(8,128)S(1)}, f32[7,16,128]{2,1,0:T(8,128)S(1)}, u32[]{:S(2)}, u32[]{:S(2)}) collective-permute-start(f32[7,16,128]{2,1,0:T(8,128)S(1)} %shard_map.80.refs_1_), channel_id=1, source_target_pairs={{0,8},{2,10},{4,12},{6,14},{8,0},{10,2},{12,4},{14,6},{16,24},{18,... | collective-permute-start | bytes 172040 | tf_op jit(solution)/shard_map/ppermute | solution.py:626
  59.6 6.2 %collective-permute-start.15 = (f32[7,16,128]{2,1,0:T(8,128)S(1)}, f32[7,16,128]{2,1,0:T(8,128)S(1)}, u32[]{:S(2)}, u32[]{:S(2)}) collective-permute-start(f32[7,16,128]{2,1,0:T(8,128)S(1)} %shard_map.80.refs_1_), channel_id=1, source_target_pairs={{0,16},{2,18},{4,20},{6,22},{8,24},{10,26},{12,28},{14,30},{16,0},... | collective-permute-start | bytes 172040 | tf_op jit(solution)/shard_map/ppermute | solution.py:626
  62.2 6.0 %collective-permute-start.16 = (f32[7,16,128]{2,1,0:T(8,128)S(1)}, f32[7,16,128]{2,1,0:T(8,128)S(1)}, u32[]{:S(2)}, u32[]{:S(2)}) collective-permute-start(f32[7,16,128]{2,1,0:T(8,128)S(1)} %shard_map.80.refs_1_), channel_id=1, source_target_pairs={{0,24},{2,26},{4,28},{6,30},{8,16},{10,18},{12,20},{14,22},{16,8},... | collective-permute-start | bytes 172040 | tf_op jit(solution)/shard_map/ppermute | solution.py:626
  68.2 1.3 %collective-permute-start.17 = (f32[7,16,128]{2,1,0:T(8,128)S(1)}, f32[7,16,128]{2,1,0:T(8,128)S(1)}, u32[]{:S(2)}, u32[]{:S(2)}) collective-permute-start(f32[7,16,128]{2,1,0:T(8,128)S(1)} %shard_map.83.mine), channel_id=1, source_target_pairs={{0,2},{2,0},{4,6},{6,4},{8,10},{10,8},{12,14},{14,12},{16,18},{18,... | collective-permute-start | bytes 172040 | tf_op jit(solution)/shard_map/ppermute | solution.py:626

commit v9 on v8

--- a/solution.py
+++ b/solution.py
@@ -102,8 +102,8 @@
         copy.wait()
 
 
-def grad_kernel(extent, margin, one, two, x_ref, *refs):
-    del one, two
+def grad_kernel(extent, margin, after, x_ref, *refs):
+    del after
     outs, wide = refs[:-1], refs[-1]
     count, planes, rows = x_ref.shape[:3]
     share = rows // extent
@@ -292,18 +292,6 @@
     return groups
 
 
-def second_kernel(share, pairs, *refs):
-    refs = list(refs)
-    hiddens = [[refs.pop(0)] for _ in range(pairs + 1)]
-    deltas = [refs.pop(0) for _ in range(pairs)]
-    raw, total = refs
-    total[...] = jnp.zeros_like(total)
-    weight_loop(total, planes_of(hiddens), 2, planes_of([[d] for d in deltas]), 2, share)
-    for g, tiles in enumerate(weight_fold(total, raw.shape[2])):
-        for h, tile in enumerate(tiles):
-            raw[g, h] = tile
-
-
 def first_deltas(weight, deltas, slopes, firsts):
     def one(r):
         row = 2 * r
@@ -316,32 +304,51 @@
     in_blocks(firsts[0].shape[0] // 2, one)
 
 
-def back_kernel(share, groups, count, after, *refs):
+def back_part(share, kept, weight, deltas, slopes, fields, firsts, total):
+    first_deltas(weight, deltas, slopes, firsts)
+    near = planes_of(fields)
+    own = planes_of([[ref] for ref in firsts])
+    low, high = kept
+    weight_loop(total, near[low : high + 2], 3, own[low:high], 1, share)
+
+
+def middle_kernel(share, groups, pairs, *refs):
+    refs = list(refs)
+    hiddens = [[refs.pop(0)] for _ in range(pairs + 1)]
+    deltas = [refs.pop(0) for _ in range(pairs)]
+    weight = refs.pop(0)
+    count = pairs - 1
+    slopes = [refs.pop(0) for _ in range(count)]
+    fields = [[refs.pop(0) for _ in range(groups)] for _ in range(pairs)]
+    raw, first_total = refs.pop(0), refs.pop(0)
+    firsts, total = refs[:count], refs[-1]
+    total[...] = jnp.zeros_like(total)
+    weight_loop(total, planes_of(hiddens), 2, planes_of([[d] for d in deltas]), 2, share)
+    for g, tiles in enumerate(weight_fold(total, raw.shape[2])):
+        for h, tile in enumerate(tiles):
+            raw[g, h] = tile
+    first_total[...] = jnp.zeros_like(first_total)
+    if count > 0:
+        kept = (0, 2 * count)
+        back_part(share, kept, weight, deltas, slopes, fields, firsts, first_total)
+
+
+def back_kernel(share, groups, weight, one, two, slope, *refs):
+    refs = list(refs)
+    fields = [[refs.pop(0) for _ in range(groups)] for _ in range(2)]
+    before, first, total = refs
+    total[...] = before[...]
+    back_part(share, (0, 1), weight, [one, two], [slope], fields, [first], total)
+
+
+def first_kernel(share, groups, after, weight, one, two, slope, *refs):
     del after
     refs = list(refs)
-    weight = refs.pop(0)
-    deltas = [refs.pop(0) for _ in range(count + 1)]
-    slopes = [refs.pop(0) for _ in range(count)]
-    fields = [[refs.pop(0) for _ in range(groups)] for _ in range(count + 2)]
-    firsts, total = refs[:-1], refs[-1]
-    first_deltas(weight, deltas, slopes, firsts)
-    total[...] = jnp.zeros_like(total)
-    near = planes_of(fields)[2:-1]
-    weight_loop(total, near, 3, planes_of([[ref] for ref in firsts])[:-1], 1, share)
-
-
-def first_kernel(share, groups, after, *refs):
-    del after
-    refs = list(refs)
-    weight = refs.pop(0)
-    deltas = [refs.pop(0) for _ in range(2)]
-    slope = refs.pop(0)
     fields = [[refs.pop(0) for _ in range(groups)] for _ in range(2)]
-    later, second = refs.pop(0), refs.pop(0)
+    before, second = refs.pop(0), refs.pop(0)
     first, keep, send, total = refs
-    first_deltas(weight, deltas, [slope], [first])
-    total[...] = later[...]
-    weight_loop(total, planes_of(fields)[1:], 3, planes_of([[first]])[1:], 1, share)
+    total[...] = before[...]
+    back_part(share, (1, 2), weight, [one, two], [slope], fields, [first], total)
     extent, halves, size = keep.shape[:3]
     me = lax.axis_index("chan")
     groups_of = weight_fold(total, size)
@@ -509,10 +516,10 @@
     grads = call(
         functools.partial(grad_kernel, extent, 2),
         [grad_piece] * pairs,
-        [own_before[0], own_after[0], out_grad] if whole else [pack, pack, out_grad],
+        [pack, out_grad],
         [pltpu.VMEM((channels * planes * rows, depth), F32)],
         moved=out_grad.size * 4,
-        loose=2,
+        loose=1,
     )
     matrix = jax.ShapeDtypeStruct((6 * channels, 12 * channels), BF16)
     first_wide, second_wide, first_back, second_back = call(
@@ -521,9 +528,9 @@
         packs,
         moved=matrix.size * 8,
     )
-    arrived = parts[-1]
-    if extent > 1 and pairs > 1:
-        arrived[0] = relayed(arrived[0], grads[0])
+    if whole and extent > 1 and pairs > 1:
+        parts[1][-1] = relayed(parts[1][-1], grads[0])
+        parts[1][0] = relayed(parts[1][0], own_after[0])
     by_pair = [[parts[j][p] for j in range(extent)] for p in range(pairs)]
     groups = extent
     if not whole:
@@ -567,25 +574,25 @@
     delta_before = to_next(deltas[-1])
 
     raw = jax.ShapeDtypeStruct((extent, 7, size, 4 * channels), F32)
-    total = pltpu.VMEM((6 * channels, 12 * channels), F32)
-    (second_raw,) = call(
-        functools.partial(second_kernel, share, pairs),
-        [raw],
-        hiddens + deltas,
-        [total],
-        flops=work * pairs * share,
-        moved=space * 5,
-    )
-    partial_sum = jax.ShapeDtypeStruct((6 * channels, 12 * channels), F32)
+    whole_sum = (6 * channels, 12 * channels)
+    sums = jax.ShapeDtypeStruct(whole_sum, F32)
     made = call(
-        functools.partial(back_kernel, share, groups, pairs),
-        many(pairs, share + 2) + [partial_sum],
-        [second_raw, second_back] + deltas + [delta_after] + slopes[1:] + flat(fields),
-        flops=work * (2 * pairs - 1) * share,
-        moved=space * 6 * pairs,
-        loose=1,
-    )
-    later, partial_total = list(made[:-1]), made[-1]
+        functools.partial(middle_kernel, share, groups, pairs),
+        [raw, sums] + many(pairs - 1, share + 2),
+        hiddens + deltas + [second_back] + slopes[1:pairs] + flat(fields[1:-1]),
+        [pltpu.VMEM(whole_sum, F32)],
+        flops=work * (3 * pairs - 2) * share,
+        moved=space * 9,
+    )
+    second_raw, sums_then, later = made[0], made[1], list(made[2:])
+    made = call(
+        functools.partial(back_kernel, share, groups),
+        many(1, share + 2) + [sums],
+        [second_back, deltas[-1], delta_after, slopes[-1]] + flat(fields[-2:]) + [sums_then],
+        flops=work * 2 * share,
+        moved=space * 6,
+    )
+    later, sums_then = later + [made[0]], made[1]
 
     def field_grad(firsts):
         count = len(firsts) - 1
@@ -614,8 +621,8 @@
         many(1, share + 2) + [raw] * 2,
         [early[0], second_back, delta_before, deltas[0], slopes[0]]
         + flat(fields[0:2])
-        + [partial_total, second_raw],
-        [total],
+        + [sums_then, second_raw],
+        [pltpu.VMEM(whole_sum, F32)],
         flops=work * 2 * share,
         moved=space * 6,
         loose=1,
@@ -635,7 +642,7 @@
     made = field_grad([first, later[0]])
     plain = slabs & (slabs - 1) == 0 and slabs >= 4
     if plain:
-        ahead = made[:1] + pieces[1:2]
+        ahead = made[:1]
         kept = call(
             functools.partial(split_kernel, len(ahead)),
             [portion] * extent,
@@ -644,7 +651,10 @@
         )
         shares = [kept[0]] + [to_chan(kept[j], extent - j) for j in range(1, extent)]
         shares += [stepped(kept[j], 2, extent - j) for j in range(extent)]
-        (mine,) = call(functools.partial(add_kernel, 0), [portion], shares)
+        ahead = pieces[1:2]
+        (mine,) = call(
+            functools.partial(add_kernel, len(ahead)), [portion], ahead + shares, loose=len(ahead)
+        )
         made = [made[0]] + [relayed(value, mine) for value in made[1:]]
     pieces = exchanged(made) + pieces
 

time: 70.7 us -> 64.5 us (0.912)
  starting transfers between devices: 28.4 us -> 22.2 us
    ppermute x5, waiting for transfers between devices: 2.76 us -> 5.74 us  [to_chan(): lax.ppermute(value, 'chan', [(i, (i + shift) % extent) for i in range(ext...]
    ppermute x3, starting transfers between devices: 11.4 us -> 8.75 us  [to_prev(): lax.ppermute(value, 'slab', [((i + 1) % slabs, i) for i in range(slabs)])]
    ppermute x3, waiting for transfers between devices: 5.05 us -> 2.45 us  [to_next(): lax.ppermute(value, 'slab', [(i, (i + 1) % slabs) for i in range(slabs)])]
    ppermute x6, starting transfers between devices: 6.58 us -> 4.53 us  [stepped(): return lax.ppermute(value, 'slab', [(i, i ^ stride) for i in range(slabs)])]
    ppermute x1, starting transfers between devices: 3.2 us -> 1.99 us  [stepped(): return lax.ppermute(value, ('slab', 'chan'), pairs_of)]
    ppermute x3, starting transfers between devices: 0.94 us -> 0.12 us  [to_next(): lax.ppermute(value, 'slab', [(i, (i + 1) % slabs) for i in range(slabs)])]
    pallas_call x18 -> x19, Pallas kernels: 22.4 us -> 22.2 us  [call(): pl.pallas_call(kernel, out_shape=outs, in_specs=[still] * loose + [whole]...]
  transfers between devices with their start and end apart: 18 -> 18, of which waited for: 10 -> 9; matrix products, arithmetic and copies ran while one was open for 0% -> 0% of each run, Pallas kernels for 28% -> 31%
where the time goes in v9:
time: 64.5 us; the launch traced here: 64.2 us
  Pallas kernels  22.2 us (34%)
  starting transfers between devices  22.2 us (34%)
  waiting for transfers between devices  14.7 us (23%)
  local copies, waits for them, and re-layouts  4.33 us (7%)
  between operations  0.83 us (1%)
    pallas_call x19, Pallas kernels, call(): pl.pallas_call(kernel, out_shape=outs, in_specs=[still] * loose + [whole]...  22.2 us
    ppermute x3, starting transfers between devices, to_prev(): lax.ppermute(value, 'slab', [((i + 1) % slabs, i) for i in range(slabs)])  8.75 us
    ppermute x5, starting transfers between devices, to_chan(): lax.ppermute(value, 'chan', [(i, (i + shift) % extent) for i in range(ext...  6.82 us
    ppermute x6, waiting for transfers between devices, stepped(): return lax.ppermute(value, 'slab', [(i, i ^ stride) for i in range(slabs)])  6.48 us
    ppermute x5, waiting for transfers between devices, to_chan(): lax.ppermute(value, 'chan', [(i, (i + shift) % extent) for i in range(ext...  5.74 us
    ppermute x6, starting transfers between devices, stepped(): return lax.ppermute(value, 'slab', [(i, i ^ stride) for i in range(slabs)])  4.53 us
    unnamed x8, local copies, waits for them, and re-layouts  4.33 us
    ppermute x3, waiting for transfers between devices, to_next(): lax.ppermute(value, 'slab', [(i, (i + 1) % slabs) for i in range(slabs)])  2.45 us
  transfers between devices with their start and end apart: 18, of which 9 were waited for; matrix products, arithmetic and copies ran while one was open for 0% of the time, Pallas kernels for 31%

profile of v9, /device:TPU:0, one launch (start us, length us, event | category | flops | bytes accessed | tf_op | source)
XLA Modules:
  0.0 64.2 jit_solution(6795479982201027883)
XLA Ops:
  0.6 0.0 copy-start.1
  0.6 1.1 %copy-done.1 = bf16[16,4,48,128]{3,2,1,0:T(8,128)(2,1)S(1)} copy-done((bf16[16,4,48,128]{3,2,1,0:T(8,128)(2,1)S(1)}, bf16[16,4,48,128]{3,2,1,0:T(8,128)(2,1)}, u32[]{:S(2)}) %copy-start.1) | copy-done | bytes 786456
  1.8 1.5 %shard_map.67 = (bf16[32,2,16,128]{3,2,1,0:T(8,128)(2,1)S(1)}, bf16[32,2,16,128]{3,2,1,0:T(8,128)(2,1)S(1)}, bf16[39,2,16,128]{3,2,1,0:T(8,128)(2,1)S(1)}, bf16[32,2,16,128]{3,2,1,0:T(8,128)(2,1)S(1)}) custom-call(bf16[16,4,48,128]{3,2,1,0:T(8,128)(2,1)S(1)} %copy-done.1), custom_call_target="tpu_custom_call" | custom-call | bytes 2359296 | tf_op jit(solution)/shard_map/pallas_call | solution.py:19
  3.3 3.0 %collective-permute-start.1 = (bf16[32,2,16,128]{3,2,1,0:T(8,128)(2,1)S(1)}, bf16[32,2,16,128]{3,2,1,0:T(8,128)(2,1)S(1)}, u32[]{:S(2)}, u32[]{:S(2)}) collective-permute-start(bf16[32,2,16,128]{3,2,1,0:T(8,128)(2,1)S(1)} %get-tuple-element.42), channel_id=1, source_target_pairs={{0,1},{1,0},{2,3},{3,2},{4,5},{5,4},{6,7},{7,6},{8,9},{9,8},{10,11... | collective-permute-start | bytes 786440 | tf_op jit(solution)/shard_map/ppermute | solution.py:470
  6.3 0.0 copy-start.2
  6.3 0.9 %copy-done.2 = bf16[16,27,32]{2,0,1:T(8,128)(2,1)S(1)} copy-done((bf16[16,27,32]{2,0,1:T(8,128)(2,1)S(1)}, bf16[16,27,32]{2,0,1:T(8,128)(2,1)}, u32[]{:S(2)}) %copy-start.2) | copy-done | bytes 27672
  7.2 0.0 copy-start.3
  7.2 0.9 %copy-done.3 = bf16[16,27,32]{2,0,1:T(8,128)(2,1)S(1)} copy-done((bf16[16,27,32]{2,0,1:T(8,128)(2,1)S(1)}, bf16[16,27,32]{2,0,1:T(8,128)(2,1)}, u32[]{:S(2)}) %copy-start.3) | copy-done | bytes 27672
  8.1 0.2 shard_map.68
  8.3 0.1 collective-permute-start.3
  8.3 4.0 %collective-permute-start.4 = (bf16[32,2,16,128]{3,2,1,0:T(8,128)(2,1)S(1)}, bf16[32,2,16,128]{3,2,1,0:T(8,128)(2,1)S(1)}, u32[]{:S(2)}, u32[]{:S(2)}) collective-permute-start(bf16[32,2,16,128]{3,2,1,0:T(8,128)(2,1)S(1)} %get-tuple-element.46.refs_2_.refs_7_), channel_id=1, source_target_pairs={{2,0},{4,2},{6,4},{8,6},{10,8},{12,10},{14,12},{16,14},{18,16},{20... | collective-permute-start | bytes 786440 | tf_op jit(solution)/shard_map/ppermute | solution.py:476
  12.3 0.0 collective-permute-start
  12.3 0.0 copy-start
  12.3 1.4 %copy-done = bf16[32,4,48,128]{3,2,1,0:T(8,128)(2,1)S(1)} copy-done((bf16[32,4,48,128]{3,2,1,0:T(8,128)(2,1)S(1)}, bf16[32,4,48,128]{3,2,1,0:T(8,128)(2,1)}, u32[]{:S(2)}) %copy-start) | copy-done | bytes 1572888
  13.7 1.3 %shard_map.69 = (bf16[28,2,32,128]{3,2,1,0:T(8,128)(2,1)S(1)}, bf16[28,2,32,128]{3,2,1,0:T(8,128)(2,1)S(1)}) custom-call(bf16[7,2,16,128]{3,2,1,0:T(8,128)(2,1)S(1)} %get-tuple-element.44.after.refs_0_, bf16[32,4,48,128]{3,2,1,0:T(8,128)(2,1)S(1)} %copy-done), custom_call_target="tpu_custom_call" | custom-call | bytes 3145728 | tf_op jit(solution)/shard_map/pallas_call | solution.py:19
  15.0 0.0 collective-permute-done.1.refs_0_
  15.0 0.1 collective-permute-start.2
  15.1 4.3 %collective-permute-done.3.refs_0_.refs_1_ = bf16[39,2,16,128]{3,2,1,0:T(8,128)(2,1)S(1)} collective-permute-done((bf16[39,2,16,128]{3,2,1,0:T(8,128)(2,1)S(1)}, bf16[39,2,16,128]{3,2,1,0:T(8,128)(2,1)S(1)}, u32[]{:S(2)}, u32[]{:S(2)}) %collective-permute-start.3) | collective-permute-done | bytes 319520 | tf_op jit(solution)/shard_map/ppermute | solution.py:470
  19.4 0.5 shard_map.72
  19.9 0.0 collective-permute-done.4.refs_1_.refs_2_
  20.0 3.4 %collective-permute-start.5 = (bf16[39,2,16,128]{3,2,1,0:T(8,128)(2,1)S(1)}, bf16[39,2,16,128]{3,2,1,0:T(8,128)(2,1)S(1)}, u32[]{:S(2)}, u32[]{:S(2)}) collective-permute-start(bf16[39,2,16,128]{3,2,1,0:T(8,128)(2,1)S(1)} %shard_map.71.refs_3_.refs_8_), channel_id=1, source_target_pairs={{2,0},{4,2},{6,4},{8,6},{10,8},{12,10},{14,12},{16,14},{18,16},{20... | collective-permute-start | bytes 958472 | tf_op jit(solution)/shard_map/ppermute | solution.py:476
  23.4 0.0 collective-permute-done.refs_0_
  23.4 0.2 collective-permute-done.2.refs_1_
  23.6 3.6 %shard_map.73 = (bf16[30,2,32,128]{3,2,1,0:T(8,128)(2,1)S(1)}, bf16[30,2,32,128]{3,2,1,0:T(8,128)(2,1)S(1)}, bf16[30,2,32,128]{3,2,1,0:T(8,128)(2,1)S(1)}, bf16[...) custom-call(bf16[32,2,16,128]{3,2,1,0:T(8,128)(2,1)S(1)} %collective-permute-done.refs_0_, ...), custom_call_target="tpu_custom_call" | custom-call | flops 1019215872 | bytes 3145728 | tf_op jit(solution)/shard_map/pallas_call | solution.py:19
  27.2 1.4 %collective-permute-start.6 = (bf16[28,2,32,128]{3,2,1,0:T(8,128)(2,1)S(1)}, bf16[28,2,32,128]{3,2,1,0:T(8,128)(2,1)S(1)}, u32[]{:S(2)}, u32[]{:S(2)}) collective-permute-start(bf16[28,2,32,128]{3,2,1,0:T(8,128)(2,1)S(1)} %get-tuple-element.54.refs_3_.two), channel_id=1, source_target_pairs={{2,0},{4,2},{6,4},{8,6},{10,8},{12,10},{14,12},{16,14},{18,16},{20... | collective-permute-start | bytes 1376264 | tf_op jit(solution)/shard_map/ppermute | solution.py:476
  28.6 0.0 collective-permute-done.5.refs_3_
  28.6 2.8 %shard_map.74 = (bf16[30,2,32,128]{3,2,1,0:T(8,128)(2,1)S(1)}, bf16[30,2,32,128]{3,2,1,0:T(8,128)(2,1)S(1)}, bf16[28,2,32,128]{3,2,1,0:T(8,128)(2,1)S(1)}) custom-call(bf16[32,2,16,128]{3,2,1,0:T(8,128)(2,1)S(1)} %get-tuple-element.41.refs_4_.refs_0_.refs_9_, bf16[32,2,16,128]{3,2,1,0:T(8,128)(2,1)S(1)} %shard_map.70.refs_5_.refs_1_.refs_10_, ...), custom_call_target="tpu_custom_call" | custom-call | flops 679477248 | bytes 2359296 | tf_op jit(solution)/shard_map/pallas_call | solution.py:19
  31.4 0.1 collective-permute-start.7
  31.5 4.3 %shard_map.75 = (f32[2,7,16,128]{3,2,1,0:T(8,128)S(1)}, f32[192,384]{1,0:T(8,128)S(1)}, bf16[26,2,32,128]{3,2,1,0:T(8,128)(2,1)S(1)}) custom-call(bf16[30,2,32,128]{3,2,1,0:T(8,128)(2,1)S(1)} %get-tuple-element.50.refs_0_, bf16[30,2,32,128]{3,2,1,0:T(8,128)(2,1)S(1)} %get-tuple-element.51.refs_4_.refs_1_, ...), custom_call_target="tpu_custom_call" | custom-call | flops 1358954496 | bytes 3538944 | tf_op jit(solution)/shard_map/pallas_call | solution.py:19
  35.8 0.0 collective-permute-done.6.two
  35.8 1.3 %shard_map.76 = (bf16[26,2,32,128]{3,2,1,0:T(8,128)(2,1)S(1)}, f32[192,384]{1,0:T(8,128)S(1)}) custom-call(bf16[192,384]{1,0:T(8,128)(2,1)S(1)} %get-tuple-element.56.refs_5_.weight, bf16[28,2,32,128]{3,2,1,0:T(8,128)(2,1)S(1)} %get-tuple-element.55.refs_4_.one, bf16[28,2,32,128]{3,2,1,0:T(8,128)(2,1)S(1)} %collective-permute-done.6.two, ...), custom_call_target="tpu_custom_call" | custom-call | flops 679477248 | bytes 2359296 | tf_op jit(solution)/shard_map/pallas_call | solution.py:19
  37.1 1.1 %shard_map.77 = (bf16[24,2,16,128]{3,2,1,0:T(8,128)(2,1)S(1)}, bf16[24,2,16,128]{3,2,1,0:T(8,128)(2,1)S(1)}) custom-call(bf16[26,2,32,128]{3,2,1,0:T(8,128)(2,1)S(1)} %get-tuple-element.58.refs_0_.refs_1_, bf16[26,2,32,128]{3,2,1,0:T(8,128)(2,1)S(1)} %get-tuple-element.61.refs_1_, bf16[192,384]{1,0:T(8,128)(2,1)S(1)} %get-tuple-element.62.refs_2_), custom_call_target="tpu_custom_call" | custom-call | flops 339738624 | bytes 786432 | tf_op jit(solution)/shard_map/pallas_call | solution.py:19
  38.3 1.6 %collective-permute-start.8 = (bf16[24,2,16,128]{3,2,1,0:T(8,128)(2,1)S(1)}, bf16[24,2,16,128]{3,2,1,0:T(8,128)(2,1)S(1)}, u32[]{:S(2)}, u32[]{:S(2)}) collective-permute-start(bf16[24,2,16,128]{3,2,1,0:T(8,128)(2,1)S(1)} %get-tuple-element.70), channel_id=1, source_target_pairs={{0,1},{1,0},{2,3},{3,2},{4,5},{5,4},{6,7},{7,6},{8,9},{9,8},{10,11... | collective-permute-start | bytes 589832 | tf_op jit(solution)/shard_map/ppermute | solution.py:470
  39.8 2.2 %collective-permute-done.7.one = bf16[28,2,32,128]{3,2,1,0:T(8,128)(2,1)S(1)} collective-permute-done((bf16[28,2,32,128]{3,2,1,0:T(8,128)(2,1)S(1)}, bf16[28,2,32,128]{3,2,1,0:T(8,128)(2,1)S(1)}, u32[]{:S(2)}, u32[]{:S(2)}) %collective-permute-start.7) | collective-permute-done | bytes 458784 | tf_op jit(solution)/shard_map/ppermute | solution.py:473
  42.0 1.5 %shard_map.78 = (bf16[26,2,32,128]{3,2,1,0:T(8,128)(2,1)S(1)}, f32[2,7,16,128]{3,2,1,0:T(8,128)S(1)}, f32[2,7,16,128]{3,2,1,0:T(8,128)S(1)}) custom-call(bf16[24,2,16,128]{3,2,1,0:T(8,128)(2,1)S(1)} %get-tuple-element.63.after.refs_2_, bf16[192,384]{1,0:T(8,128)(2,1)S(1)} %get-tuple-element.56.refs_5_.weight, ...), custom_call_target="tpu_custom_call" | custom-call | flops 679477248 | bytes 2359296 | tf_op jit(solution)/shard_map/pallas_call | solution.py:19
  43.6 0.1 collective-permute-start.9
  43.7 1.1 %shard_map.79 = (bf16[24,2,16,128]{3,2,1,0:T(8,128)(2,1)S(1)}, bf16[24,2,16,128]{3,2,1,0:T(8,128)(2,1)S(1)}) custom-call(bf16[26,2,32,128]{3,2,1,0:T(8,128)(2,1)S(1)} %get-tuple-element.67.refs_0_, bf16[26,2,32,128]{3,2,1,0:T(8,128)(2,1)S(1)} %get-tuple-element.58.refs_0_.refs_1_, bf16[192,384]{1,0:T(8,128)(2,1)S(1)} %get-tuple-element.62.refs_2_), custom_call_target="tpu_custom_call" | custom-call | flops 339738624 | bytes 786432 | tf_op jit(solution)/shard_map/pallas_call | solution.py:19
  44.8 0.2 collective-permute-done.9.refs_2_
  45.0 1.6 %collective-permute-start.10 = (f32[7,16,128]{2,1,0:T(8,128)S(1)}, f32[7,16,128]{2,1,0:T(8,128)S(1)}, u32[]{:S(2)}, u32[]{:S(2)}) collective-permute-start(f32[7,16,128]{2,1,0:T(8,128)S(1)} %get-tuple-element.74), channel_id=1, source_target_pairs={{0,1},{1,0},{2,3},{3,2},{4,5},{5,4},{6,7},{7,6},{8,9},{9,8},{10,11... | collective-permute-start | bytes 172040 | tf_op jit(solution)/shard_map/ppermute | solution.py:470
  46.5 0.0 collective-permute-start.11
  46.5 2.0 %collective-permute-start.12 = (f32[7,16,128]{2,1,0:T(8,128)S(1)}, f32[7,16,128]{2,1,0:T(8,128)S(1)}, u32[]{:S(2)}, u32[]{:S(2)}) collective-permute-start(f32[7,16,128]{2,1,0:T(8,128)S(1)} %get-tuple-element.74), channel_id=1, source_target_pairs={{0,5},{1,4},{2,7},{3,6},{4,1},{5,0},{6,3},{7,2},{8,13},{9,12},{10,... | collective-permute-start | bytes 172040 | tf_op jit(solution)/shard_map/ppermute | solution.py:639
  48.5 0.0 collective-permute-done.8.refs_0_.refs_3_
  48.5 0.7 %collective-permute-done.10.refs_2_ = f32[7,16,128]{2,1,0:T(8,128)S(1)} collective-permute-done((f32[7,16,128]{2,1,0:T(8,128)S(1)}, f32[7,16,128]{2,1,0:T(8,128)S(1)}, u32[]{:S(2)}, u32[]{:S(2)}) %collective-permute-start.10) | collective-permute-done | bytes 57376 | tf_op jit(solution)/shard_map/ppermute | solution.py:470
  49.2 2.7 %collective-permute-done.11.refs_3_ = f32[7,16,128]{2,1,0:T(8,128)S(1)} collective-permute-done((f32[7,16,128]{2,1,0:T(8,128)S(1)}, f32[7,16,128]{2,1,0:T(8,128)S(1)}, u32[]{:S(2)}, u32[]{:S(2)}) %collective-permute-start.11) | collective-permute-done | bytes 57376 | tf_op jit(solution)/shard_map/ppermute | solution.py:633
  51.9 0.0 collective-permute-done.12.refs_4_
  52.0 0.6 collective-permute-start.13
  52.6 0.2 collective-permute-start.14
  52.8 3.2 %collective-permute-start.15 = (f32[7,16,128]{2,1,0:T(8,128)S(1)}, f32[7,16,128]{2,1,0:T(8,128)S(1)}, u32[]{:S(2)}, u32[]{:S(2)}) collective-permute-start(f32[7,16,128]{2,1,0:T(8,128)S(1)} %shard_map.81.refs_1_), channel_id=1, source_target_pairs={{0,16},{2,18},{4,20},{6,22},{8,24},{10,26},{12,28},{14,30},{16,0},... | collective-permute-start | bytes 172040 | tf_op jit(solution)/shard_map/ppermute | solution.py:633
  56.0 0.9 %collective-permute-start.16 = (f32[7,16,128]{2,1,0:T(8,128)S(1)}, f32[7,16,128]{2,1,0:T(8,128)S(1)}, u32[]{:S(2)}, u32[]{:S(2)}) collective-permute-start(f32[7,16,128]{2,1,0:T(8,128)S(1)} %shard_map.81.refs_1_), channel_id=1, source_target_pairs={{0,24},{2,26},{4,28},{6,30},{8,16},{10,18},{12,20},{14,22},{16,8},... | collective-permute-start | bytes 172040 | tf_op jit(solution)/shard_map/ppermute | solution.py:633
  57.0 0.7 %collective-permute-done.13.refs_1_ = bf16[24,2,16,128]{3,2,1,0:T(8,128)(2,1)S(1)} collective-permute-done((bf16[24,2,16,128]{3,2,1,0:T(8,128)(2,1)S(1)}, bf16[24,2,16,128]{3,2,1,0:T(8,128)(2,1)S(1)}, u32[]{:S(2)}, u32[]{:S(2)}) %collective-permute-start.13) | collective-permute-done | bytes 196640 | tf_op jit(solution)/shard_map/ppermute | solution.py:470
  57.7 1.9 %shard_map.83 = (f32[8,128]{1,0:T(8,128)S(1)}, bf16[16,4,48,128]{3,2,1,0:T(8,128)(2,1)}) custom-call(bf16[24,2,16,128]{3,2,1,0:T(8,128)(2,1)S(1)} %get-tuple-element.68.refs_0_, bf16[24,2,16,128]{3,2,1,0:T(8,128)(2,1)S(1)} %collective-permute-done.13.refs_1_, bf16[24,2,16,128]{3,2,1,0:T(8,128)(2,1)S(1)} %get-tuple-element.63.after.refs_2_, ...), custom_call_target="tpu_custom_call" | custom-call | bytes 1572864 | tf_op jit(solution)/shard_map/pallas_call | solution.py:19
  59.6 0.0 collective-permute-done.14.refs_2_
  59.6 0.0 collective-permute-done.15.refs_3_
  59.6 2.4 %collective-permute-done.16.refs_4_ = f32[7,16,128]{2,1,0:T(8,128)S(1)} collective-permute-done((f32[7,16,128]{2,1,0:T(8,128)S(1)}, f32[7,16,128]{2,1,0:T(8,128)S(1)}, u32[]{:S(2)}, u32[]{:S(2)}) %collective-permute-start.16) | collective-permute-done | bytes 57376 | tf_op jit(solution)/shard_map/ppermute | solution.py:633
  62.0 0.1 collective-permute-start.17
  62.1 1.2 %collective-permute-done.17.other = f32[7,16,128]{2,1,0:T(8,128)S(1)} collective-permute-done((f32[7,16,128]{2,1,0:T(8,128)S(1)}, f32[7,16,128]{2,1,0:T(8,128)S(1)}, u32[]{:S(2)}, u32[]{:S(2)}) %collective-permute-start.17) | collective-permute-done | bytes 57376 | tf_op jit(solution)/shard_map/ppermute | solution.py:633
  63.3 0.9 %shard_map.85 = (f32[27,16,32]{2,1,0:T(8,128)}, f32[27,16,32]{2,1,0:T(8,128)}) custom-call(f32[7,16,128]{2,1,0:T(8,128)S(1)} %shard_map.84.mine, f32[7,16,128]{2,1,0:T(8,128)S(1)} %collective-permute-done.17.other), custom_call_target="tpu_custom_call" | custom-call | tf_op jit(solution)/shard_map/pallas_call | solution.py:19
  (6 shorter events, 0.1 us)
Async XLA Ops:
  0.6 1.1 %copy-start.1 = (bf16[16,4,48,128]{3,2,1,0:T(8,128)(2,1)S(1)}, bf16[16,4,48,128]{3,2,1,0:T(8,128)(2,1)}, u32[]{:S(2)}) copy-start(bf16[16,4,48,128]{3,2,1,0:T(8,128)(2,1)} %x_ref.2) | copy-start | bytes 2359300
  3.3 11.8 %collective-permute-start.1 = (bf16[32,2,16,128]{3,2,1,0:T(8,128)(2,1)S(1)}, bf16[32,2,16,128]{3,2,1,0:T(8,128)(2,1)S(1)}, u32[]{:S(2)}, u32[]{:S(2)}) collective-permute-start(bf16[32,2,16,128]{3,2,1,0:T(8,128)(2,1)S(1)} %get-tuple-element.42), channel_id=1, source_target_pairs={{0,1},{1,0},{2,3},{3,2},{4,5},{5,4},{6,7},{7,6},{8,9},{9,8},{10,11... | collective-permute-start | bytes 786440 | tf_op jit(solution)/shard_map/ppermute | solution.py:470
  6.3 0.9 %copy-start.2 = (bf16[16,27,32]{2,0,1:T(8,128)(2,1)S(1)}, bf16[16,27,32]{2,0,1:T(8,128)(2,1)}, u32[]{:S(2)}) copy-start(bf16[16,27,32]{2,0,1:T(8,128)(2,1)} %param.6) | copy-start | bytes 82948
  7.2 0.9 %copy-start.3 = (bf16[16,27,32]{2,0,1:T(8,128)(2,1)S(1)}, bf16[16,27,32]{2,0,1:T(8,128)(2,1)}, u32[]{:S(2)}) copy-start(bf16[16,27,32]{2,0,1:T(8,128)(2,1)} %param.7) | copy-start | bytes 82948
  8.3 11.2 %collective-permute-start.3 = (bf16[39,2,16,128]{3,2,1,0:T(8,128)(2,1)S(1)}, bf16[39,2,16,128]{3,2,1,0:T(8,128)(2,1)S(1)}, u32[]{:S(2)}, u32[]{:S(2)}) collective-permute-start(bf16[39,2,16,128]{3,2,1,0:T(8,128)(2,1)S(1)} %get-tuple-element.47), channel_id=1, source_target_pairs={{0,1},{1,0},{2,3},{3,2},{4,5},{5,4},{6,7},{7,6},{8,9},{9,8},{10,11... | collective-permute-start | bytes 958472 | tf_op jit(solution)/shard_map/ppermute | solution.py:470
  8.3 11.6 %collective-permute-start.4 = (bf16[32,2,16,128]{3,2,1,0:T(8,128)(2,1)S(1)}, bf16[32,2,16,128]{3,2,1,0:T(8,128)(2,1)S(1)}, u32[]{:S(2)}, u32[]{:S(2)}) collective-permute-start(bf16[32,2,16,128]{3,2,1,0:T(8,128)(2,1)S(1)} %get-tuple-element.46.refs_2_.refs_7_), channel_id=1, source_target_pairs={{2,0},{4,2},{6,4},{8,6},{10,8},{12,10},{14,12},{16,14},{18,16},{20... | collective-permute-start | bytes 786440 | tf_op jit(solution)/shard_map/ppermute | solution.py:476
  12.3 11.1 %collective-permute-start = (bf16[32,2,16,128]{3,2,1,0:T(8,128)(2,1)S(1)}, bf16[32,2,16,128]{3,2,1,0:T(8,128)(2,1)S(1)}, u32[]{:S(2)}, u32[]{:S(2)}) collective-permute-start(bf16[32,2,16,128]{3,2,1,0:T(8,128)(2,1)S(1)} %get-tuple-element.41.refs_4_.refs_0_.refs_9_), channel_id=1, source_target_pairs={{0,2},{2,4},{4,6},{6,8},{8,10},{10,12},{12,14},{14,16},{16,18},{18... | collective-permute-start | bytes 786440 | tf_op jit(solution)/shard_map/ppermute | solution.py:473
  12.3 1.4 %copy-start = (bf16[32,4,48,128]{3,2,1,0:T(8,128)(2,1)S(1)}, bf16[32,4,48,128]{3,2,1,0:T(8,128)(2,1)}, u32[]{:S(2)}) copy-start(bf16[32,4,48,128]{3,2,1,0:T(8,128)(2,1)} %x_ref.3) | copy-start | bytes 4718596
  15.0 8.6 %collective-permute-start.2 = (bf16[32,2,16,128]{3,2,1,0:T(8,128)(2,1)S(1)}, bf16[32,2,16,128]{3,2,1,0:T(8,128)(2,1)S(1)}, u32[]{:S(2)}, u32[]{:S(2)}) collective-permute-start(bf16[32,2,16,128]{3,2,1,0:T(8,128)(2,1)S(1)} %shard_map.70.refs_5_.refs_1_.refs_10_), channel_id=1, source_target_pairs={{0,2},{2,4},{4,6},{6,8},{8,10},{10,12},{12,14},{14,16},{16,18},{18... | collective-permute-start | bytes 786440 | tf_op jit(solution)/shard_map/ppermute | solution.py:473
  20.0 8.6 %collective-permute-start.5 = (bf16[39,2,16,128]{3,2,1,0:T(8,128)(2,1)S(1)}, bf16[39,2,16,128]{3,2,1,0:T(8,128)(2,1)S(1)}, u32[]{:S(2)}, u32[]{:S(2)}) collective-permute-start(bf16[39,2,16,128]{3,2,1,0:T(8,128)(2,1)S(1)} %shard_map.71.refs_3_.refs_8_), channel_id=1, source_target_pairs={{2,0},{4,2},{6,4},{8,6},{10,8},{12,10},{14,12},{16,14},{18,16},{20... | collective-permute-start | bytes 958472 | tf_op jit(solution)/shard_map/ppermute | solution.py:476
  27.2 8.6 %collective-permute-start.6 = (bf16[28,2,32,128]{3,2,1,0:T(8,128)(2,1)S(1)}, bf16[28,2,32,128]{3,2,1,0:T(8,128)(2,1)S(1)}, u32[]{:S(2)}, u32[]{:S(2)}) collective-permute-start(bf16[28,2,32,128]{3,2,1,0:T(8,128)(2,1)S(1)} %get-tuple-element.54.refs_3_.two), channel_id=1, source_target_pairs={{2,0},{4,2},{6,4},{8,6},{10,8},{12,10},{14,12},{16,14},{18,16},{20... | collective-permute-start | bytes 1376264 | tf_op jit(solution)/shard_map/ppermute | solution.py:476
  31.4 10.7 %collective-permute-start.7 = (bf16[28,2,32,128]{3,2,1,0:T(8,128)(2,1)S(1)}, bf16[28,2,32,128]{3,2,1,0:T(8,128)(2,1)S(1)}, u32[]{:S(2)}, u32[]{:S(2)}) collective-permute-start(bf16[28,2,32,128]{3,2,1,0:T(8,128)(2,1)S(1)} %get-tuple-element.55.refs_4_.one), channel_id=1, source_target_pairs={{0,2},{2,4},{4,6},{6,8},{8,10},{10,12},{12,14},{14,16},{16,18},{18... | collective-permute-start | bytes 1376264 | tf_op jit(solution)/shard_map/ppermute | solution.py:473
  38.3 10.3 %collective-permute-start.8 = (bf16[24,2,16,128]{3,2,1,0:T(8,128)(2,1)S(1)}, bf16[24,2,16,128]{3,2,1,0:T(8,128)(2,1)S(1)}, u32[]{:S(2)}, u32[]{:S(2)}) collective-permute-start(bf16[24,2,16,128]{3,2,1,0:T(8,128)(2,1)S(1)} %get-tuple-element.70), channel_id=1, source_target_pairs={{0,1},{1,0},{2,3},{3,2},{4,5},{5,4},{6,7},{7,6},{8,9},{9,8},{10,11... | collective-permute-start | bytes 589832 | tf_op jit(solution)/shard_map/ppermute | solution.py:470
  43.6 1.4 %collective-permute-start.9 = (f32[2,7,16,128]{3,2,1,0:T(8,128)S(1)}, f32[2,7,16,128]{3,2,1,0:T(8,128)S(1)}, u32[]{:S(2)}, u32[]{:S(2)}) collective-permute-start(f32[2,7,16,128]{3,2,1,0:T(8,128)S(1)} %get-tuple-element.72), channel_id=1, source_target_pairs={{0,2},{2,0},{4,6},{6,4},{8,10},{10,8},{12,14},{14,12},{16,18},{18,... | collective-permute-start | bytes 344072 | tf_op jit(solution)/shard_map/ppermute | solution.py:633
  45.0 4.2 %collective-permute-start.10 = (f32[7,16,128]{2,1,0:T(8,128)S(1)}, f32[7,16,128]{2,1,0:T(8,128)S(1)}, u32[]{:S(2)}, u32[]{:S(2)}) collective-permute-start(f32[7,16,128]{2,1,0:T(8,128)S(1)} %get-tuple-element.74), channel_id=1, source_target_pairs={{0,1},{1,0},{2,3},{3,2},{4,5},{5,4},{6,7},{7,6},{8,9},{9,8},{10,11... | collective-permute-start | bytes 172040 | tf_op jit(solution)/shard_map/ppermute | solution.py:470
  46.5 5.4 %collective-permute-start.11 = (f32[7,16,128]{2,1,0:T(8,128)S(1)}, f32[7,16,128]{2,1,0:T(8,128)S(1)}, u32[]{:S(2)}, u32[]{:S(2)}) collective-permute-start(f32[7,16,128]{2,1,0:T(8,128)S(1)} %get-tuple-element.73.refs_1_), channel_id=1, source_target_pairs={{0,4},{2,6},{4,0},{6,2},{8,12},{10,14},{12,8},{14,10},{16,20},{18,... | collective-permute-start | bytes 172040 | tf_op jit(solution)/shard_map/ppermute | solution.py:633
  46.5 5.4 %collective-permute-start.12 = (f32[7,16,128]{2,1,0:T(8,128)S(1)}, f32[7,16,128]{2,1,0:T(8,128)S(1)}, u32[]{:S(2)}, u32[]{:S(2)}) collective-permute-start(f32[7,16,128]{2,1,0:T(8,128)S(1)} %get-tuple-element.74), channel_id=1, source_target_pairs={{0,5},{1,4},{2,7},{3,6},{4,1},{5,0},{6,3},{7,2},{8,13},{9,12},{10,... | collective-permute-start | bytes 172040 | tf_op jit(solution)/shard_map/ppermute | solution.py:639
  52.0 5.7 %collective-permute-start.13 = (bf16[24,2,16,128]{3,2,1,0:T(8,128)(2,1)S(1)}, bf16[24,2,16,128]{3,2,1,0:T(8,128)(2,1)S(1)}, u32[]{:S(2)}, u32[]{:S(2)}) collective-permute-start(bf16[24,2,16,128]{3,2,1,0:T(8,128)(2,1)S(1)} %shard_map.82), channel_id=1, source_target_pairs={{0,1},{1,0},{2,3},{3,2},{4,5},{5,4},{6,7},{7,6},{8,9},{9,8},{10,11... | collective-permute-start | bytes 589832 | tf_op jit(solution)/shard_map/ppermute | solution.py:470
  52.6 7.1 %collective-permute-start.14 = (f32[7,16,128]{2,1,0:T(8,128)S(1)}, f32[7,16,128]{2,1,0:T(8,128)S(1)}, u32[]{:S(2)}, u32[]{:S(2)}) collective-permute-start(f32[7,16,128]{2,1,0:T(8,128)S(1)} %shard_map.81.refs_1_), channel_id=1, source_target_pairs={{0,8},{2,10},{4,12},{6,14},{8,0},{10,2},{12,4},{14,6},{16,24},{18,... | collective-permute-start | bytes 172040 | tf_op jit(solution)/shard_map/ppermute | solution.py:633
  52.8 6.8 %collective-permute-start.15 = (f32[7,16,128]{2,1,0:T(8,128)S(1)}, f32[7,16,128]{2,1,0:T(8,128)S(1)}, u32[]{:S(2)}, u32[]{:S(2)}) collective-permute-start(f32[7,16,128]{2,1,0:T(8,128)S(1)} %shard_map.81.refs_1_), channel_id=1, source_target_pairs={{0,16},{2,18},{4,20},{6,22},{8,24},{10,26},{12,28},{14,30},{16,0},... | collective-permute-start | bytes 172040 | tf_op jit(solution)/shard_map/ppermute | solution.py:633
  56.0 6.0 %collective-permute-start.16 = (f32[7,16,128]{2,1,0:T(8,128)S(1)}, f32[7,16,128]{2,1,0:T(8,128)S(1)}, u32[]{:S(2)}, u32[]{:S(2)}) collective-permute-start(f32[7,16,128]{2,1,0:T(8,128)S(1)} %shard_map.81.refs_1_), channel_id=1, source_target_pairs={{0,24},{2,26},{4,28},{6,30},{8,16},{10,18},{12,20},{14,22},{16,8},... | collective-permute-start | bytes 172040 | tf_op jit(solution)/shard_map/ppermute | solution.py:633
  62.0 1.3 %collective-permute-start.17 = (f32[7,16,128]{2,1,0:T(8,128)S(1)}, f32[7,16,128]{2,1,0:T(8,128)S(1)}, u32[]{:S(2)}, u32[]{:S(2)}) collective-permute-start(f32[7,16,128]{2,1,0:T(8,128)S(1)} %shard_map.84.mine), channel_id=1, source_target_pairs={{0,2},{2,0},{4,6},{6,4},{8,10},{10,8},{12,14},{14,12},{16,18},{18,... | collective-permute-start | bytes 172040 | tf_op jit(solution)/shard_map/ppermute | solution.py:633

commit v10 on v9

--- a/solution.py
+++ b/solution.py
@@ -84,22 +84,15 @@
         )
 
 
-def pack_kernel(count, rows, *refs):
-    first, second = refs[count : count + 2]
-    pieces, packed, done = refs[count + 2 : -2], refs[-2], refs[-1]
+def pack_kernel(after, first, second, packed):
+    del after
     blank = jnp.zeros(first.shape[1:], F32)
-    for h in range(14):
+    for h in range(packed.shape[0]):
         parts = []
         for ref in (first, second):
             for t in (2 * h, 2 * h + 1):
                 parts.append(ref[t].astype(F32) if t < ref.shape[0] else blank)
-        packed[h // 2, h % 2] = jnp.concatenate(parts, axis=1).astype(BF16)
-    copies = []
-    for k, piece in enumerate(pieces):
-        copies.append(pltpu.make_async_copy(packed, piece.at[pl.ds(rows, 7)], done.at[k]))
-        copies[-1].start()
-    for copy in copies:
-        copy.wait()
+        packed[h] = jnp.concatenate(parts, axis=1).astype(BF16)
 
 
 def grad_kernel(extent, margin, after, x_ref, *refs):
@@ -115,13 +108,11 @@
 def matrix_kernel(extent, *refs):
     packs, outs = refs[:extent], refs[extent:]
     me = lax.axis_index("chan")
-    quarter = packs[0].shape[3] // 4
+    quarter = packs[0].shape[2] // 4
     taps = []
     turned = []
-    for h in range(14):
-        tiles = [
-            pack[pack.shape[0] - 7 + h // 2, h % 2].astype(F32) for pack in packs
-        ]
+    for h in range(packs[0].shape[0]):
+        tiles = [pack[h].astype(F32) for pack in packs]
         own = jnp.concatenate(tiles, axis=0)
         fixed = []
         for g in range(extent):
@@ -346,10 +337,12 @@
     refs = list(refs)
     fields = [[refs.pop(0) for _ in range(groups)] for _ in range(2)]
     before, second = refs.pop(0), refs.pop(0)
-    first, keep, send, total = refs
+    first, total = refs[0], refs[-1]
+    extent = (len(refs) - 2) // 2
+    keep, send = refs[1 : 1 + extent], refs[1 + extent : -1]
     total[...] = before[...]
     back_part(share, (1, 2), weight, [one, two], [slope], fields, [first], total)
-    extent, halves, size = keep.shape[:3]
+    halves, size = keep[0].shape[:2]
     me = lax.axis_index("chan")
     groups_of = weight_fold(total, size)
 
@@ -357,8 +350,8 @@
         for g, tiles in enumerate(groups_of):
             there = lax.rem(me + extent - g, extent)
             for h in range(halves):
-                ours[g, h] = tiles[h]
-                theirs[g, h] = second[there, h]
+                ours[g][h] = tiles[h]
+                theirs[g][h] = second[there, h]
 
     odd = lax.rem(lax.axis_index("slab"), 2)
 
@@ -411,12 +404,6 @@
         place(second, first)
 
 
-def split_kernel(ahead, *refs):
-    one, two, *outs = refs[ahead:]
-    for g, out in enumerate(outs):
-        out[...] = one[g] + two[g]
-
-
 def add_kernel(ahead, *refs):
     values = [ref[...] for ref in refs[ahead:-1]]
     while len(values) > 1:
@@ -482,36 +469,27 @@
 
     piece = jax.ShapeDtypeStruct((share + 8, 2, size, depth), BF16)
     by_tap = (27, size, channels)
-    longer = jax.ShapeDtypeStruct((share + 15, 2, size, depth), BF16)
-    rest = [piece] * (pairs - 1)
     made = call(
         functools.partial(field_kernel, extent, 4),
-        [piece] + rest + ([longer] + rest) * (extent - 1),
+        [piece] * (extent * pairs),
         [field],
         [pltpu.VMEM((size * planes * rows, depth), F32)],
         moved=field.size * 6,
     )
-    first_sent = list(made[pairs::pairs])
-    others = extent - 1
-    packed = call(
-        functools.partial(pack_kernel, others, share + 8),
-        [longer] * others + [jax.ShapeDtypeStruct((7, 2, size, 4 * channels), BF16)],
-        first_sent
-        + [jnp.transpose(first_weight, (1, 0, 2)), jnp.transpose(second_weight, (1, 0, 2))],
-        [pltpu.SemaphoreType.DMA((max(others, 1),))],
-        loose=others,
-        same={k: k for k in range(others)},
-    )
-    first_sent, pack = packed[:-1], packed[-1]
     parts = [list(made[:pairs])]
+    for j in range(1, extent):
+        parts.append([to_chan(value, j) for value in made[j * pairs : (j + 1) * pairs]])
+    (pack,) = call(
+        pack_kernel,
+        [jax.ShapeDtypeStruct((14, size, 4 * channels), BF16)],
+        [made[0], jnp.transpose(first_weight, (1, 0, 2)), jnp.transpose(second_weight, (1, 0, 2))],
+        loose=1,
+    )
+    packs = [pack] + [to_chan(pack, j) for j in range(1, extent)]
     whole = size % 16 == 0
     own_before, own_after = [], []
     if whole:
         own_before, own_after = [to_next(parts[0][-1])], [to_prev(parts[0][0])]
-    for j in range(1, extent):
-        sent = [first_sent[j - 1]] + list(made[j * pairs + 1 : (j + 1) * pairs])
-        parts.append([to_chan(value, j) for value in sent])
-    packs = [pack] + [part[0] for part in parts[1:]]
     grad_piece = jax.ShapeDtypeStruct((share + 4, 2, channels, depth), BF16)
     grads = call(
         functools.partial(grad_kernel, extent, 2),
@@ -530,14 +508,11 @@
     )
     if whole and extent > 1 and pairs > 1:
         parts[1][-1] = relayed(parts[1][-1], grads[0])
-        parts[1][0] = relayed(parts[1][0], own_after[0])
+        parts[1][0] = relayed(parts[1][0], own_after[0], *packs[1:])
     by_pair = [[parts[j][p] for j in range(extent)] for p in range(pairs)]
     groups = extent
     if not whole:
-        by_pair = [
-            [jnp.concatenate([piece[: share + 8] for piece in pieces], axis=2)]
-            for pieces in by_pair
-        ]
+        by_pair = [[jnp.concatenate(pieces, axis=2)] for pieces in by_pair]
         groups = 1
     before = own_before + [to_next(piece) for piece in by_pair[-1][len(own_before) :]]
     after = own_after + [to_prev(piece) for piece in by_pair[0][len(own_after) :]]
@@ -616,9 +591,10 @@
     if pairs > 1:
         early = field_grad(later)
         pieces = exchanged(early)
-    first, keep, send = call(
+    portion = jax.ShapeDtypeStruct(raw.shape[1:], F32)
+    made = call(
         functools.partial(first_kernel, share, groups),
-        many(1, share + 2) + [raw] * 2,
+        many(1, share + 2) + [portion] * (2 * extent),
         [early[0], second_back, delta_before, deltas[0], slopes[0]]
         + flat(fields[0:2])
         + [sums_then, second_raw],
@@ -627,6 +603,8 @@
         moved=space * 6,
         loose=1,
     )
+
+    first, keep, send = made[0], made[1 : 1 + extent], made[1 + extent :]
 
     def stepped(value, stride, shift=0):
         if shift % extent == 0:
@@ -638,20 +616,13 @@
                 pairs_of.append((i * extent + k, there))
         return lax.ppermute(value, ("slab", "chan"), pairs_of)
 
-    portion = jax.ShapeDtypeStruct(raw.shape[1:], F32)
     made = field_grad([first, later[0]])
     plain = slabs & (slabs - 1) == 0 and slabs >= 4
     if plain:
-        ahead = made[:1]
-        kept = call(
-            functools.partial(split_kernel, len(ahead)),
-            [portion] * extent,
-            ahead + [keep, stepped(send, 1)],
-            loose=len(ahead),
-        )
-        shares = [kept[0]] + [to_chan(kept[j], extent - j) for j in range(1, extent)]
-        shares += [stepped(kept[j], 2, extent - j) for j in range(extent)]
-        ahead = pieces[1:2]
+        shares = [keep[0], stepped(send[0], 1)]
+        for j in range(1, extent):
+            shares += [to_chan(keep[j], extent - j), stepped(send[j], 1, extent - j)]
+        ahead = made[:1] + pieces[1:2]
         (mine,) = call(
             functools.partial(add_kernel, len(ahead)), [portion], ahead + shares, loose=len(ahead)
         )
@@ -666,7 +637,7 @@
         moved=4 * field.size,
     )
     if plain:
-        stride = 4
+        stride = 2
         while stride < slabs:
             radix = 4 if slabs % (4 * stride) == 0 else 2
             got = [mine] + [stepped(mine, m * stride) for m in range(1, radix)]

time: 64.5 us -> 65.1 us (level)
  starting transfers between devices: 22.2 us -> 25.5 us
  waiting for transfers between devices: 14.7 us -> 12.2 us
    ppermute x5 -> x6, starting transfers between devices: 6.82 us -> 9.43 us  [to_chan(): lax.ppermute(value, 'chan', [(i, (i + shift) % extent) for i in range(ext...]
    ppermute x6, starting transfers between devices: 4.53 us -> 6.97 us  [stepped(): return lax.ppermute(value, 'slab', [(i, i ^ stride) for i in range(slabs)])]
    ppermute x5 -> x6, waiting for transfers between devices: 5.74 us -> 4.03 us  [to_chan(): lax.ppermute(value, 'chan', [(i, (i + shift) % extent) for i in range(ext...]
    ppermute x6, waiting for transfers between devices: 6.48 us -> 4.78 us  [stepped(): return lax.ppermute(value, 'slab', [(i, i ^ stride) for i in range(slabs)])]
    ppermute x1, starting transfers between devices: 1.99 us -> 0.31 us  [stepped(): return lax.ppermute(value, ('slab', 'chan'), pairs_of)]
    ppermute x1, waiting for transfers between devices: 0.01 us -> 1.09 us  [stepped(): return lax.ppermute(value, ('slab', 'chan'), pairs_of)]
  transfers between devices with their start and end apart: 18 -> 19, of which waited for: 9 -> 9; matrix products, arithmetic and copies ran while one was open for 0% -> 0% of each run, Pallas kernels for 31% -> 30%
where the time goes in v10:
time: 65.1 us; the launch traced here: 64.9 us
  starting transfers between devices  25.5 us (39%)
  Pallas kernels  22 us (34%)
  waiting for transfers between devices  12.2 us (19%)
  local copies, waits for them, and re-layouts  4.32 us (7%)
  between operations  0.84 us (1%)
    pallas_call x19, Pallas kernels, call(): pl.pallas_call(kernel, out_shape=outs, in_specs=[still] * loose + [whole]...  22 us
    ppermute x6, starting transfers between devices, to_chan(): lax.ppermute(value, 'chan', [(i, (i + shift) % extent) for i in range(ext...  9.43 us
    ppermute x3, starting transfers between devices, to_prev(): lax.ppermute(value, 'slab', [((i + 1) % slabs, i) for i in range(slabs)])  8.69 us
    ppermute x6, starting transfers between devices, stepped(): return lax.ppermute(value, 'slab', [(i, i ^ stride) for i in range(slabs)])  6.97 us
    ppermute x6, waiting for transfers between devices, stepped(): return lax.ppermute(value, 'slab', [(i, i ^ stride) for i in range(slabs)])  4.78 us
    unnamed x8, local copies, waits for them, and re-layouts  4.32 us
    ppermute x6, waiting for transfers between devices, to_chan(): lax.ppermute(value, 'chan', [(i, (i + shift) % extent) for i in range(ext...  4.03 us
    ppermute x3, waiting for transfers between devices, to_next(): lax.ppermute(value, 'slab', [(i, (i + 1) % slabs) for i in range(slabs)])  2.27 us
  transfers between devices with their start and end apart: 19, of which 9 were waited for; matrix products, arithmetic and copies ran while one was open for 0% of the time, Pallas kernels for 30%

profile of v10, /device:TPU:0, one launch (start us, length us, event | category | flops | bytes accessed | tf_op | source)
XLA Modules:
  0.0 64.9 jit_solution(14932615525958719358)
XLA Ops:
  0.6 0.0 copy-start.1
  0.6 1.1 %copy-done.1 = bf16[16,4,48,128]{3,2,1,0:T(8,128)(2,1)S(1)} copy-done((bf16[16,4,48,128]{3,2,1,0:T(8,128)(2,1)S(1)}, bf16[16,4,48,128]{3,2,1,0:T(8,128)(2,1)}, u32[]{:S(2)}) %copy-start.1) | copy-done | bytes 786456
  1.8 1.5 %shard_map.67 = (bf16[32,2,16,128]{3,2,1,0:T(8,128)(2,1)S(1)}, bf16[32,2,16,128]{3,2,1,0:T(8,128)(2,1)S(1)}, bf16[32,2,16,128]{3,2,1,0:T(8,128)(2,1)S(1)}, bf16[32,2,16,128]{3,2,1,0:T(8,128)(2,1)S(1)}) custom-call(bf16[16,4,48,128]{3,2,1,0:T(8,128)(2,1)S(1)} %copy-done.1), custom_call_target="tpu_custom_call" | custom-call | bytes 2359296 | tf_op jit(solution)/shard_map/pallas_call | solution.py:19
  3.3 3.0 %collective-permute-start.1 = (bf16[32,2,16,128]{3,2,1,0:T(8,128)(2,1)S(1)}, bf16[32,2,16,128]{3,2,1,0:T(8,128)(2,1)S(1)}, u32[]{:S(2)}, u32[]{:S(2)}) collective-permute-start(bf16[32,2,16,128]{3,2,1,0:T(8,128)(2,1)S(1)} %get-tuple-element.40), channel_id=1, source_target_pairs={{0,1},{1,0},{2,3},{3,2},{4,5},{5,4},{6,7},{7,6},{8,9},{9,8},{10,11... | collective-permute-start | bytes 786440 | tf_op jit(solution)/shard_map/ppermute | solution.py:457
  6.3 3.7 %collective-permute-start.4 = (bf16[32,2,16,128]{3,2,1,0:T(8,128)(2,1)S(1)}, bf16[32,2,16,128]{3,2,1,0:T(8,128)(2,1)S(1)}, u32[]{:S(2)}, u32[]{:S(2)}) collective-permute-start(bf16[32,2,16,128]{3,2,1,0:T(8,128)(2,1)S(1)} %get-tuple-element.41.after.refs_2_.refs_7_), channel_id=1, source_target_pairs={{2,0},{4,2},{6,4},{8,6},{10,8},{12,10},{14,12},{16,14},{18,16},{20... | collective-permute-start | bytes 786440 | tf_op jit(solution)/shard_map/ppermute | solution.py:463
  10.0 0.5 collective-permute-start.3
  10.5 0.0 collective-permute-start
  10.5 0.0 copy-start.2
  10.5 0.9 %copy-done.2 = bf16[16,27,32]{2,0,1:T(8,128)(2,1)S(1)} copy-done((bf16[16,27,32]{2,0,1:T(8,128)(2,1)S(1)}, bf16[16,27,32]{2,0,1:T(8,128)(2,1)}, u32[]{:S(2)}) %copy-start.2) | copy-done | bytes 27672
  11.4 0.0 copy-start.3
  11.4 0.9 %copy-done.3 = bf16[16,27,32]{2,0,1:T(8,128)(2,1)S(1)} copy-done((bf16[16,27,32]{2,0,1:T(8,128)(2,1)S(1)}, bf16[16,27,32]{2,0,1:T(8,128)(2,1)}, u32[]{:S(2)}) %copy-start.3) | copy-done | bytes 27672
  12.3 0.1 shard_map.68.after.refs_0_
  12.4 0.0 copy-start
  12.4 1.4 %copy-done = bf16[32,4,48,128]{3,2,1,0:T(8,128)(2,1)S(1)} copy-done((bf16[32,4,48,128]{3,2,1,0:T(8,128)(2,1)S(1)}, bf16[32,4,48,128]{3,2,1,0:T(8,128)(2,1)}, u32[]{:S(2)}) %copy-start) | copy-done | bytes 1572888
  13.8 1.3 %shard_map.69 = (bf16[28,2,32,128]{3,2,1,0:T(8,128)(2,1)S(1)}, bf16[28,2,32,128]{3,2,1,0:T(8,128)(2,1)S(1)}) custom-call(bf16[14,16,128]{2,1,0:T(8,128)(2,1)S(1)} %shard_map.68.after.refs_0_, bf16[32,4,48,128]{3,2,1,0:T(8,128)(2,1)S(1)} %copy-done), custom_call_target="tpu_custom_call" | custom-call | bytes 3145728 | tf_op jit(solution)/shard_map/pallas_call | solution.py:19
  15.1 0.0 collective-permute-done.1.refs_0_
  15.2 0.1 collective-permute-start.2
  15.2 1.6 %collective-permute-start.5 = (bf16[14,16,128]{2,1,0:T(8,128)(2,1)S(1)}, bf16[14,16,128]{2,1,0:T(8,128)(2,1)S(1)}, u32[]{:S(2)}, u32[]{:S(2)}) collective-permute-start(bf16[14,16,128]{2,1,0:T(8,128)(2,1)S(1)} %shard_map.68.after.refs_0_), channel_id=1, source_target_pairs={{0,1},{1,0},{2,3},{3,2},{4,5},{5,4},{6,7},{7,6},{8,9},{9,8},{10,11... | collective-permute-start | bytes 172040 | tf_op jit(solution)/shard_map/ppermute | solution.py:457
  16.8 2.7 %collective-permute-done.5.refs_2_.refs_1_ = bf16[14,16,128]{2,1,0:T(8,128)(2,1)S(1)} collective-permute-done((bf16[14,16,128]{2,1,0:T(8,128)(2,1)S(1)}, bf16[14,16,128]{2,1,0:T(8,128)(2,1)S(1)}, u32[]{:S(2)}, u32[]{:S(2)}) %collective-permute-start.5) | collective-permute-done | bytes 57376 | tf_op jit(solution)/shard_map/ppermute | solution.py:457
  19.5 0.0 collective-permute-done.4.refs_1_.refs_2_
  19.5 0.0 collective-permute-done.3.refs_0_
  19.5 3.9 %collective-permute-start.6 = (bf16[32,2,16,128]{3,2,1,0:T(8,128)(2,1)S(1)}, bf16[32,2,16,128]{3,2,1,0:T(8,128)(2,1)S(1)}, u32[]{:S(2)}, u32[]{:S(2)}) collective-permute-start(bf16[32,2,16,128]{3,2,1,0:T(8,128)(2,1)S(1)} %shard_map.71.refs_3_.refs_8_), channel_id=1, source_target_pairs={{2,0},{4,2},{6,4},{8,6},{10,8},{12,10},{14,12},{16,14},{18,16},{20... | collective-permute-start | bytes 786440 | tf_op jit(solution)/shard_map/ppermute | solution.py:463
  23.4 0.5 shard_map.72
  23.9 0.0 collective-permute-done.refs_0_
  23.9 0.0 collective-permute-done.2.refs_1_
  23.9 3.6 %shard_map.73 = (bf16[30,2,32,128]{3,2,1,0:T(8,128)(2,1)S(1)}, bf16[30,2,32,128]{3,2,1,0:T(8,128)(2,1)S(1)}, bf16[30,2,32,128]{3,2,1,0:T(8,128)(2,1)S(1)}, bf16[...) custom-call(bf16[32,2,16,128]{3,2,1,0:T(8,128)(2,1)S(1)} %collective-permute-done.refs_0_, ...), custom_call_target="tpu_custom_call" | custom-call | flops 1019215872 | bytes 3145728 | tf_op jit(solution)/shard_map/pallas_call | solution.py:19
  27.5 1.1 %collective-permute-start.7 = (bf16[28,2,32,128]{3,2,1,0:T(8,128)(2,1)S(1)}, bf16[28,2,32,128]{3,2,1,0:T(8,128)(2,1)S(1)}, u32[]{:S(2)}, u32[]{:S(2)}) collective-permute-start(bf16[28,2,32,128]{3,2,1,0:T(8,128)(2,1)S(1)} %get-tuple-element.50.refs_3_.two), channel_id=1, source_target_pairs={{2,0},{4,2},{6,4},{8,6},{10,8},{12,10},{14,12},{16,14},{18,16},{20... | collective-permute-start | bytes 1376264 | tf_op jit(solution)/shard_map/ppermute | solution.py:463
  28.6 0.0 collective-permute-done.6.refs_3_
  28.6 2.8 %shard_map.74 = (bf16[30,2,32,128]{3,2,1,0:T(8,128)(2,1)S(1)}, bf16[30,2,32,128]{3,2,1,0:T(8,128)(2,1)S(1)}, bf16[28,2,32,128]{3,2,1,0:T(8,128)(2,1)S(1)}) custom-call(bf16[32,2,16,128]{3,2,1,0:T(8,128)(2,1)S(1)} %get-tuple-element.39.refs_4_.refs_0_.refs_9_, bf16[32,2,16,128]{3,2,1,0:T(8,128)(2,1)S(1)} %shard_map.70.refs_5_.refs_1_.refs_10_, ...), custom_call_target="tpu_custom_call" | custom-call | flops 679477248 | bytes 2359296 | tf_op jit(solution)/shard_map/pallas_call | solution.py:19
  31.4 0.1 collective-permute-start.8
  31.5 4.3 %shard_map.75 = (f32[2,7,16,128]{3,2,1,0:T(8,128)S(1)}, f32[192,384]{1,0:T(8,128)S(1)}, bf16[26,2,32,128]{3,2,1,0:T(8,128)(2,1)S(1)}) custom-call(bf16[30,2,32,128]{3,2,1,0:T(8,128)(2,1)S(1)} %get-tuple-element.46.refs_0_, bf16[30,2,32,128]{3,2,1,0:T(8,128)(2,1)S(1)} %get-tuple-element.47.refs_4_.refs_1_, ...), custom_call_target="tpu_custom_call" | custom-call | flops 1358954496 | bytes 3538944 | tf_op jit(solution)/shard_map/pallas_call | solution.py:19
  35.8 0.0 collective-permute-done.7.two
  35.8 1.3 %shard_map.76 = (bf16[26,2,32,128]{3,2,1,0:T(8,128)(2,1)S(1)}, f32[192,384]{1,0:T(8,128)S(1)}) custom-call(bf16[192,384]{1,0:T(8,128)(2,1)S(1)} %get-tuple-element.52.refs_5_.weight, bf16[28,2,32,128]{3,2,1,0:T(8,128)(2,1)S(1)} %get-tuple-element.51.refs_4_.one, bf16[28,2,32,128]{3,2,1,0:T(8,128)(2,1)S(1)} %collective-permute-done.7.two, ...), custom_call_target="tpu_custom_call" | custom-call | flops 679477248 | bytes 2359296 | tf_op jit(solution)/shard_map/pallas_call | solution.py:19
  37.1 1.1 %shard_map.77 = (bf16[24,2,16,128]{3,2,1,0:T(8,128)(2,1)S(1)}, bf16[24,2,16,128]{3,2,1,0:T(8,128)(2,1)S(1)}) custom-call(bf16[26,2,32,128]{3,2,1,0:T(8,128)(2,1)S(1)} %get-tuple-element.54.refs_0_.refs_1_, bf16[26,2,32,128]{3,2,1,0:T(8,128)(2,1)S(1)} %get-tuple-element.57.refs_1_, bf16[192,384]{1,0:T(8,128)(2,1)S(1)} %get-tuple-element.58.refs_2_), custom_call_target="tpu_custom_call" | custom-call | flops 339738624 | bytes 786432 | tf_op jit(solution)/shard_map/pallas_call | solution.py:19
  38.2 1.5 %collective-permute-start.9 = (bf16[24,2,16,128]{3,2,1,0:T(8,128)(2,1)S(1)}, bf16[24,2,16,128]{3,2,1,0:T(8,128)(2,1)S(1)}, u32[]{:S(2)}, u32[]{:S(2)}) collective-permute-start(bf16[24,2,16,128]{3,2,1,0:T(8,128)(2,1)S(1)} %get-tuple-element.66), channel_id=1, source_target_pairs={{0,1},{1,0},{2,3},{3,2},{4,5},{5,4},{6,7},{7,6},{8,9},{9,8},{10,11... | collective-permute-start | bytes 589832 | tf_op jit(solution)/shard_map/ppermute | solution.py:457
  39.8 2.3 %collective-permute-done.8.one = bf16[28,2,32,128]{3,2,1,0:T(8,128)(2,1)S(1)} collective-permute-done((bf16[28,2,32,128]{3,2,1,0:T(8,128)(2,1)S(1)}, bf16[28,2,32,128]{3,2,1,0:T(8,128)(2,1)S(1)}, u32[]{:S(2)}, u32[]{:S(2)}) %collective-permute-start.8) | collective-permute-done | bytes 458784 | tf_op jit(solution)/shard_map/ppermute | solution.py:460
  42.1 1.5 %shard_map.78 = (bf16[26,2,32,128]{3,2,1,0:T(8,128)(2,1)S(1)}, f32[7,16,128]{2,1,0:T(8,128)S(1)}, f32[7,16,128]{2,1,0:T(8,128)S(1)}, f32[7,16,128]{2,1,0:T(8,128)S(1)}, f32[7,16,128]{2,1,0:T(8,128)S(1)}) custom-call(bf16[24,2,16,128]{3,2,1,0:T(8,128)(2,1)S(1)} %get-tuple-element.59.after.refs_2_, bf16[192,384]{1,0:T(8,128)(2,1)S(1)} %get-tuple-element.52.refs_5_.weight, ...), custom_call_target="tpu_custom_call" | custom-call | flops 679477248 | bytes 2359296 | tf_op jit(solution)/shard_map/pallas_call | solution.py:19
  43.6 0.1 collective-permute-start.10
  43.6 1.6 %collective-permute-start.11 = (f32[7,16,128]{2,1,0:T(8,128)S(1)}, f32[7,16,128]{2,1,0:T(8,128)S(1)}, u32[]{:S(2)}, u32[]{:S(2)}) collective-permute-start(f32[7,16,128]{2,1,0:T(8,128)S(1)} %get-tuple-element.69), channel_id=1, source_target_pairs={{0,1},{1,0},{2,3},{3,2},{4,5},{5,4},{6,7},{7,6},{8,9},{9,8},{10,11... | collective-permute-start | bytes 172040 | tf_op jit(solution)/shard_map/ppermute | solution.py:457
  45.2 0.3 collective-permute-start.12
  45.5 1.1 %shard_map.79 = (bf16[24,2,16,128]{3,2,1,0:T(8,128)(2,1)S(1)}, bf16[24,2,16,128]{3,2,1,0:T(8,128)(2,1)S(1)}) custom-call(bf16[26,2,32,128]{3,2,1,0:T(8,128)(2,1)S(1)} %get-tuple-element.63.refs_0_, bf16[26,2,32,128]{3,2,1,0:T(8,128)(2,1)S(1)} %get-tuple-element.54.refs_0_.refs_1_, bf16[192,384]{1,0:T(8,128)(2,1)S(1)} %get-tuple-element.58.refs_2_), custom_call_target="tpu_custom_call" | custom-call | flops 339738624 | bytes 786432 | tf_op jit(solution)/shard_map/pallas_call | solution.py:19
  46.6 0.0 collective-permute-done.10.refs_3_
  46.6 1.3 %collective-permute-done.11.refs_4_ = f32[7,16,128]{2,1,0:T(8,128)S(1)} collective-permute-done((f32[7,16,128]{2,1,0:T(8,128)S(1)}, f32[7,16,128]{2,1,0:T(8,128)S(1)}, u32[]{:S(2)}, u32[]{:S(2)}) %collective-permute-start.11) | collective-permute-done | bytes 57376 | tf_op jit(solution)/shard_map/ppermute | solution.py:457
  48.0 1.1 %collective-permute-done.12.refs_5_ = f32[7,16,128]{2,1,0:T(8,128)S(1)} collective-permute-done((f32[7,16,128]{2,1,0:T(8,128)S(1)}, f32[7,16,128]{2,1,0:T(8,128)S(1)}, u32[]{:S(2)}, u32[]{:S(2)}) %collective-permute-start.12) | collective-permute-done | bytes 57376 | tf_op jit(solution)/shard_map/ppermute | solution.py:617
  49.1 0.0 collective-permute-done.9.refs_1_.refs_3_
  49.1 1.2 %collective-permute-start.13 = (bf16[24,2,16,128]{3,2,1,0:T(8,128)(2,1)S(1)}, bf16[24,2,16,128]{3,2,1,0:T(8,128)(2,1)S(1)}, u32[]{:S(2)}, u32[]{:S(2)}) collective-permute-start(bf16[24,2,16,128]{3,2,1,0:T(8,128)(2,1)S(1)} %shard_map.81), channel_id=1, source_target_pairs={{0,1},{1,0},{2,3},{3,2},{4,5},{5,4},{6,7},{7,6},{8,9},{9,8},{10,11... | collective-permute-start | bytes 589832 | tf_op jit(solution)/shard_map/ppermute | solution.py:457
  50.3 0.0 collective-permute-start.14
  50.3 0.3 collective-permute-start.15
  50.6 3.2 %collective-permute-start.16 = (f32[7,16,128]{2,1,0:T(8,128)S(1)}, f32[7,16,128]{2,1,0:T(8,128)S(1)}, u32[]{:S(2)}, u32[]{:S(2)}) collective-permute-start(f32[7,16,128]{2,1,0:T(8,128)S(1)} %shard_map.80.refs_1_.refs_0_), channel_id=1, source_target_pairs={{0,12},{2,14},{4,8},{6,10},{8,4},{10,6},{12,0},{14,2},{16,28},{18,... | collective-permute-start | bytes 172040 | tf_op jit(solution)/shard_map/ppermute | solution.py:611
  53.8 0.7 %collective-permute-done.14.refs_1_ = f32[7,16,128]{2,1,0:T(8,128)S(1)} collective-permute-done((f32[7,16,128]{2,1,0:T(8,128)S(1)}, f32[7,16,128]{2,1,0:T(8,128)S(1)}, u32[]{:S(2)}, u32[]{:S(2)}) %collective-permute-start.14) | collective-permute-done | bytes 57376 | tf_op jit(solution)/shard_map/ppermute | solution.py:611
  54.5 0.4 collective-permute-done.15.refs_2_
  54.9 1.7 %collective-permute-done.16.refs_3_ = f32[7,16,128]{2,1,0:T(8,128)S(1)} collective-permute-done((f32[7,16,128]{2,1,0:T(8,128)S(1)}, f32[7,16,128]{2,1,0:T(8,128)S(1)}, u32[]{:S(2)}, u32[]{:S(2)}) %collective-permute-start.16) | collective-permute-done | bytes 57376 | tf_op jit(solution)/shard_map/ppermute | solution.py:611
  56.6 3.3 %collective-permute-start.17 = (f32[7,16,128]{2,1,0:T(8,128)S(1)}, f32[7,16,128]{2,1,0:T(8,128)S(1)}, u32[]{:S(2)}, u32[]{:S(2)}) collective-permute-start(f32[7,16,128]{2,1,0:T(8,128)S(1)} %shard_map.83.refs_1_), channel_id=1, source_target_pairs={{0,16},{2,18},{4,20},{6,22},{8,24},{10,26},{12,28},{14,30},{16,0},... | collective-permute-start | bytes 172040 | tf_op jit(solution)/shard_map/ppermute | solution.py:611
  59.9 0.0 collective-permute-done.13.refs_1_
  60.0 1.9 %shard_map.82 = (f32[8,128]{1,0:T(8,128)S(1)}, bf16[16,4,48,128]{3,2,1,0:T(8,128)(2,1)}) custom-call(bf16[24,2,16,128]{3,2,1,0:T(8,128)(2,1)S(1)} %get-tuple-element.64.refs_0_, bf16[24,2,16,128]{3,2,1,0:T(8,128)(2,1)S(1)} %collective-permute-done.13.refs_1_, bf16[24,2,16,128]{3,2,1,0:T(8,128)(2,1)S(1)} %get-tuple-element.59.after.refs_2_, ...), custom_call_target="tpu_custom_call" | custom-call | bytes 1572864 | tf_op jit(solution)/shard_map/pallas_call | solution.py:19
  61.9 0.8 %collective-permute-done.17.refs_2_ = f32[7,16,128]{2,1,0:T(8,128)S(1)} collective-permute-done((f32[7,16,128]{2,1,0:T(8,128)S(1)}, f32[7,16,128]{2,1,0:T(8,128)S(1)}, u32[]{:S(2)}, u32[]{:S(2)}) %collective-permute-start.17) | collective-permute-done | bytes 57376 | tf_op jit(solution)/shard_map/ppermute | solution.py:611
  62.7 0.1 collective-permute-start.18
  62.7 1.2 %collective-permute-done.18.other = f32[7,16,128]{2,1,0:T(8,128)S(1)} collective-permute-done((f32[7,16,128]{2,1,0:T(8,128)S(1)}, f32[7,16,128]{2,1,0:T(8,128)S(1)}, u32[]{:S(2)}, u32[]{:S(2)}) %collective-permute-start.18) | collective-permute-done | bytes 57376 | tf_op jit(solution)/shard_map/ppermute | solution.py:611
  64.0 0.9 %shard_map.85 = (f32[27,16,32]{2,1,0:T(8,128)}, f32[27,16,32]{2,1,0:T(8,128)}) custom-call(f32[7,16,128]{2,1,0:T(8,128)S(1)} %shard_map.84.mine, f32[7,16,128]{2,1,0:T(8,128)S(1)} %collective-permute-done.18.other), custom_call_target="tpu_custom_call" | custom-call | tf_op jit(solution)/shard_map/pallas_call | solution.py:19
  (6 shorter events, 0.0 us)
Async XLA Ops:
  0.6 1.1 %copy-start.1 = (bf16[16,4,48,128]{3,2,1,0:T(8,128)(2,1)S(1)}, bf16[16,4,48,128]{3,2,1,0:T(8,128)(2,1)}, u32[]{:S(2)}) copy-start(bf16[16,4,48,128]{3,2,1,0:T(8,128)(2,1)} %x_ref.2) | copy-start | bytes 2359300
  3.3 11.9 %collective-permute-start.1 = (bf16[32,2,16,128]{3,2,1,0:T(8,128)(2,1)S(1)}, bf16[32,2,16,128]{3,2,1,0:T(8,128)(2,1)S(1)}, u32[]{:S(2)}, u32[]{:S(2)}) collective-permute-start(bf16[32,2,16,128]{3,2,1,0:T(8,128)(2,1)S(1)} %get-tuple-element.40), channel_id=1, source_target_pairs={{0,1},{1,0},{2,3},{3,2},{4,5},{5,4},{6,7},{7,6},{8,9},{9,8},{10,11... | collective-permute-start | bytes 786440 | tf_op jit(solution)/shard_map/ppermute | solution.py:457
  6.3 13.2 %collective-permute-start.4 = (bf16[32,2,16,128]{3,2,1,0:T(8,128)(2,1)S(1)}, bf16[32,2,16,128]{3,2,1,0:T(8,128)(2,1)S(1)}, u32[]{:S(2)}, u32[]{:S(2)}) collective-permute-start(bf16[32,2,16,128]{3,2,1,0:T(8,128)(2,1)S(1)} %get-tuple-element.41.after.refs_2_.refs_7_), channel_id=1, source_target_pairs={{2,0},{4,2},{6,4},{8,6},{10,8},{12,10},{14,12},{16,14},{18,16},{20... | collective-permute-start | bytes 786440 | tf_op jit(solution)/shard_map/ppermute | solution.py:463
  10.0 9.5 %collective-permute-start.3 = (bf16[32,2,16,128]{3,2,1,0:T(8,128)(2,1)S(1)}, bf16[32,2,16,128]{3,2,1,0:T(8,128)(2,1)S(1)}, u32[]{:S(2)}, u32[]{:S(2)}) collective-permute-start(bf16[32,2,16,128]{3,2,1,0:T(8,128)(2,1)S(1)} %get-tuple-element.43), channel_id=1, source_target_pairs={{0,1},{1,0},{2,3},{3,2},{4,5},{5,4},{6,7},{7,6},{8,9},{9,8},{10,11... | collective-permute-start | bytes 786440 | tf_op jit(solution)/shard_map/ppermute | solution.py:457
  10.5 13.4 %collective-permute-start = (bf16[32,2,16,128]{3,2,1,0:T(8,128)(2,1)S(1)}, bf16[32,2,16,128]{3,2,1,0:T(8,128)(2,1)S(1)}, u32[]{:S(2)}, u32[]{:S(2)}) collective-permute-start(bf16[32,2,16,128]{3,2,1,0:T(8,128)(2,1)S(1)} %get-tuple-element.39.refs_4_.refs_0_.refs_9_), channel_id=1, source_target_pairs={{0,2},{2,4},{4,6},{6,8},{8,10},{10,12},{12,14},{14,16},{16,18},{18... | collective-permute-start | bytes 786440 | tf_op jit(solution)/shard_map/ppermute | solution.py:460
  10.5 0.9 %copy-start.2 = (bf16[16,27,32]{2,0,1:T(8,128)(2,1)S(1)}, bf16[16,27,32]{2,0,1:T(8,128)(2,1)}, u32[]{:S(2)}) copy-start(bf16[16,27,32]{2,0,1:T(8,128)(2,1)} %param.6) | copy-start | bytes 82948
  11.4 0.9 %copy-start.3 = (bf16[16,27,32]{2,0,1:T(8,128)(2,1)S(1)}, bf16[16,27,32]{2,0,1:T(8,128)(2,1)}, u32[]{:S(2)}) copy-start(bf16[16,27,32]{2,0,1:T(8,128)(2,1)} %param.7) | copy-start | bytes 82948
  12.4 1.4 %copy-start = (bf16[32,4,48,128]{3,2,1,0:T(8,128)(2,1)S(1)}, bf16[32,4,48,128]{3,2,1,0:T(8,128)(2,1)}, u32[]{:S(2)}) copy-start(bf16[32,4,48,128]{3,2,1,0:T(8,128)(2,1)} %x_ref.3) | copy-start | bytes 4718596
  15.2 8.8 %collective-permute-start.2 = (bf16[32,2,16,128]{3,2,1,0:T(8,128)(2,1)S(1)}, bf16[32,2,16,128]{3,2,1,0:T(8,128)(2,1)S(1)}, u32[]{:S(2)}, u32[]{:S(2)}) collective-permute-start(bf16[32,2,16,128]{3,2,1,0:T(8,128)(2,1)S(1)} %shard_map.70.refs_5_.refs_1_.refs_10_), channel_id=1, source_target_pairs={{0,2},{2,4},{4,6},{6,8},{8,10},{10,12},{12,14},{14,16},{16,18},{18... | collective-permute-start | bytes 786440 | tf_op jit(solution)/shard_map/ppermute | solution.py:460
  15.2 4.2 %collective-permute-start.5 = (bf16[14,16,128]{2,1,0:T(8,128)(2,1)S(1)}, bf16[14,16,128]{2,1,0:T(8,128)(2,1)S(1)}, u32[]{:S(2)}, u32[]{:S(2)}) collective-permute-start(bf16[14,16,128]{2,1,0:T(8,128)(2,1)S(1)} %shard_map.68.after.refs_0_), channel_id=1, source_target_pairs={{0,1},{1,0},{2,3},{3,2},{4,5},{5,4},{6,7},{7,6},{8,9},{9,8},{10,11... | collective-permute-start | bytes 172040 | tf_op jit(solution)/shard_map/ppermute | solution.py:457
  19.5 9.1 %collective-permute-start.6 = (bf16[32,2,16,128]{3,2,1,0:T(8,128)(2,1)S(1)}, bf16[32,2,16,128]{3,2,1,0:T(8,128)(2,1)S(1)}, u32[]{:S(2)}, u32[]{:S(2)}) collective-permute-start(bf16[32,2,16,128]{3,2,1,0:T(8,128)(2,1)S(1)} %shard_map.71.refs_3_.refs_8_), channel_id=1, source_target_pairs={{2,0},{4,2},{6,4},{8,6},{10,8},{12,10},{14,12},{16,14},{18,16},{20... | collective-permute-start | bytes 786440 | tf_op jit(solution)/shard_map/ppermute | solution.py:463
  27.5 8.3 %collective-permute-start.7 = (bf16[28,2,32,128]{3,2,1,0:T(8,128)(2,1)S(1)}, bf16[28,2,32,128]{3,2,1,0:T(8,128)(2,1)S(1)}, u32[]{:S(2)}, u32[]{:S(2)}) collective-permute-start(bf16[28,2,32,128]{3,2,1,0:T(8,128)(2,1)S(1)} %get-tuple-element.50.refs_3_.two), channel_id=1, source_target_pairs={{2,0},{4,2},{6,4},{8,6},{10,8},{12,10},{14,12},{16,14},{18,16},{20... | collective-permute-start | bytes 1376264 | tf_op jit(solution)/shard_map/ppermute | solution.py:463
  31.4 10.7 %collective-permute-start.8 = (bf16[28,2,32,128]{3,2,1,0:T(8,128)(2,1)S(1)}, bf16[28,2,32,128]{3,2,1,0:T(8,128)(2,1)S(1)}, u32[]{:S(2)}, u32[]{:S(2)}) collective-permute-start(bf16[28,2,32,128]{3,2,1,0:T(8,128)(2,1)S(1)} %get-tuple-element.51.refs_4_.one), channel_id=1, source_target_pairs={{0,2},{2,4},{4,6},{6,8},{8,10},{10,12},{12,14},{14,16},{16,18},{18... | collective-permute-start | bytes 1376264 | tf_op jit(solution)/shard_map/ppermute | solution.py:460
  38.2 10.8 %collective-permute-start.9 = (bf16[24,2,16,128]{3,2,1,0:T(8,128)(2,1)S(1)}, bf16[24,2,16,128]{3,2,1,0:T(8,128)(2,1)S(1)}, u32[]{:S(2)}, u32[]{:S(2)}) collective-permute-start(bf16[24,2,16,128]{3,2,1,0:T(8,128)(2,1)S(1)} %get-tuple-element.66), channel_id=1, source_target_pairs={{0,1},{1,0},{2,3},{3,2},{4,5},{5,4},{6,7},{7,6},{8,9},{9,8},{10,11... | collective-permute-start | bytes 589832 | tf_op jit(solution)/shard_map/ppermute | solution.py:457
  43.6 3.1 %collective-permute-start.10 = (f32[7,16,128]{2,1,0:T(8,128)S(1)}, f32[7,16,128]{2,1,0:T(8,128)S(1)}, u32[]{:S(2)}, u32[]{:S(2)}) collective-permute-start(f32[7,16,128]{2,1,0:T(8,128)S(1)} %get-tuple-element.68), channel_id=1, source_target_pairs={{0,2},{2,0},{4,6},{6,4},{8,10},{10,8},{12,14},{14,12},{16,18},{18,... | collective-permute-start | bytes 172040 | tf_op jit(solution)/shard_map/ppermute | solution.py:611
  43.6 4.3 %collective-permute-start.11 = (f32[7,16,128]{2,1,0:T(8,128)S(1)}, f32[7,16,128]{2,1,0:T(8,128)S(1)}, u32[]{:S(2)}, u32[]{:S(2)}) collective-permute-start(f32[7,16,128]{2,1,0:T(8,128)S(1)} %get-tuple-element.69), channel_id=1, source_target_pairs={{0,1},{1,0},{2,3},{3,2},{4,5},{5,4},{6,7},{7,6},{8,9},{9,8},{10,11... | collective-permute-start | bytes 172040 | tf_op jit(solution)/shard_map/ppermute | solution.py:457
  45.2 3.9 %collective-permute-start.12 = (f32[7,16,128]{2,1,0:T(8,128)S(1)}, f32[7,16,128]{2,1,0:T(8,128)S(1)}, u32[]{:S(2)}, u32[]{:S(2)}) collective-permute-start(f32[7,16,128]{2,1,0:T(8,128)S(1)} %get-tuple-element.70), channel_id=1, source_target_pairs={{0,3},{1,2},{2,1},{3,0},{4,7},{5,6},{6,5},{7,4},{8,11},{9,10},{10,... | collective-permute-start | bytes 172040 | tf_op jit(solution)/shard_map/ppermute | solution.py:617
  49.1 10.8 %collective-permute-start.13 = (bf16[24,2,16,128]{3,2,1,0:T(8,128)(2,1)S(1)}, bf16[24,2,16,128]{3,2,1,0:T(8,128)(2,1)S(1)}, u32[]{:S(2)}, u32[]{:S(2)}) collective-permute-start(bf16[24,2,16,128]{3,2,1,0:T(8,128)(2,1)S(1)} %shard_map.81), channel_id=1, source_target_pairs={{0,1},{1,0},{2,3},{3,2},{4,5},{5,4},{6,7},{7,6},{8,9},{9,8},{10,11... | collective-permute-start | bytes 589832 | tf_op jit(solution)/shard_map/ppermute | solution.py:457
  50.3 4.2 %collective-permute-start.14 = (f32[7,16,128]{2,1,0:T(8,128)S(1)}, f32[7,16,128]{2,1,0:T(8,128)S(1)}, u32[]{:S(2)}, u32[]{:S(2)}) collective-permute-start(f32[7,16,128]{2,1,0:T(8,128)S(1)} %shard_map.80.refs_1_.refs_0_), channel_id=1, source_target_pairs={{0,4},{2,6},{4,0},{6,2},{8,12},{10,14},{12,8},{14,10},{16,20},{18,... | collective-permute-start | bytes 172040 | tf_op jit(solution)/shard_map/ppermute | solution.py:611
  50.3 4.6 %collective-permute-start.15 = (f32[7,16,128]{2,1,0:T(8,128)S(1)}, f32[7,16,128]{2,1,0:T(8,128)S(1)}, u32[]{:S(2)}, u32[]{:S(2)}) collective-permute-start(f32[7,16,128]{2,1,0:T(8,128)S(1)} %shard_map.80.refs_1_.refs_0_), channel_id=1, source_target_pairs={{0,8},{2,10},{4,12},{6,14},{8,0},{10,2},{12,4},{14,6},{16,24},{18,... | collective-permute-start | bytes 172040 | tf_op jit(solution)/shard_map/ppermute | solution.py:611
  50.6 5.9 %collective-permute-start.16 = (f32[7,16,128]{2,1,0:T(8,128)S(1)}, f32[7,16,128]{2,1,0:T(8,128)S(1)}, u32[]{:S(2)}, u32[]{:S(2)}) collective-permute-start(f32[7,16,128]{2,1,0:T(8,128)S(1)} %shard_map.80.refs_1_.refs_0_), channel_id=1, source_target_pairs={{0,12},{2,14},{4,8},{6,10},{8,4},{10,6},{12,0},{14,2},{16,28},{18,... | collective-permute-start | bytes 172040 | tf_op jit(solution)/shard_map/ppermute | solution.py:611
  56.6 6.0 %collective-permute-start.17 = (f32[7,16,128]{2,1,0:T(8,128)S(1)}, f32[7,16,128]{2,1,0:T(8,128)S(1)}, u32[]{:S(2)}, u32[]{:S(2)}) collective-permute-start(f32[7,16,128]{2,1,0:T(8,128)S(1)} %shard_map.83.refs_1_), channel_id=1, source_target_pairs={{0,16},{2,18},{4,20},{6,22},{8,24},{10,26},{12,28},{14,30},{16,0},... | collective-permute-start | bytes 172040 | tf_op jit(solution)/shard_map/ppermute | solution.py:611
  62.7 1.3 %collective-permute-start.18 = (f32[7,16,128]{2,1,0:T(8,128)S(1)}, f32[7,16,128]{2,1,0:T(8,128)S(1)}, u32[]{:S(2)}, u32[]{:S(2)}) collective-permute-start(f32[7,16,128]{2,1,0:T(8,128)S(1)} %shard_map.84.mine), channel_id=1, source_target_pairs={{0,2},{2,0},{4,6},{6,4},{8,10},{10,8},{12,14},{14,12},{16,18},{18,... | collective-permute-start | bytes 172040 | tf_op jit(solution)/shard_map/ppermute | solution.py:611

commit v11 on v10

--- a/solution.py
+++ b/solution.py
@@ -159,13 +159,13 @@
     return jnp.concatenate(parts, axis=0)
 
 
-def taps(weight, pairs, row):
+def taps(weight, inputs, row):
     sides = []
-    for p in range(len(pairs) - 1):
+    for above, below in inputs:
         for q in range(2):
-            above = stacked(pairs[p], row + q, 3)
-            below = stacked(pairs[p + 1], row + q, 3)
-            sides.append(jnp.concatenate([above, below], axis=0))
+            sides.append(
+                jnp.concatenate([stacked(above, row + q, 3), stacked(below, row + q, 3)], axis=0)
+            )
     lifted = jnp.dot(weight, jnp.concatenate(sides, axis=1), preferred_element_type=F32)
     third = lifted.shape[0] // 3
     depth = sides[0].shape[1]
@@ -177,7 +177,11 @@
             + pltpu.roll(side[:third], 1, 1)
             + pltpu.roll(side[2 * third :], depth - 1, 1)
         )
-    return [sums[2 * p : 2 * p + 2] for p in range(len(pairs) - 1)]
+    return [sums[2 * p : 2 * p + 2] for p in range(len(inputs))]
+
+
+def neighbours(pairs):
+    return list(zip(pairs[:-1], pairs[1:]))
 
 
 def silu_parts(v):
@@ -199,7 +203,7 @@
 
     def one(r):
         row = 2 * r
-        for p, sums in enumerate(taps(first[...], fields, row)):
+        for p, sums in enumerate(taps(first[...], neighbours(fields), row)):
             for q, v in enumerate(sums):
                 sig, slope = silu_parts(v)
                 shape = made[p].shape[1:]
@@ -210,7 +214,7 @@
 
     def two(r):
         row = 2 * r
-        for p, sums in enumerate(taps(second[...], [[ref] for ref in hiddens], row)):
+        for p, sums in enumerate(taps(second[...], neighbours([[ref] for ref in hiddens]), row)):
             for q, v in enumerate(sums):
                 shape = deltas[p].shape[1:]
                 out_grad = grads[p][row + q].astype(F32)
@@ -283,10 +287,10 @@
     return groups
 
 
-def first_deltas(weight, deltas, slopes, firsts):
+def first_deltas(weight, inputs, slopes, firsts):
     def one(r):
         row = 2 * r
-        for p, sums in enumerate(taps(weight[...], [[delta] for delta in deltas], row)):
+        for p, sums in enumerate(taps(weight[...], inputs, row)):
             for q, v in enumerate(sums):
                 shape = firsts[p].shape[1:]
                 slope = slopes[p][row + 2 + q].astype(F32)
@@ -295,63 +299,35 @@
     in_blocks(firsts[0].shape[0] // 2, one)
 
 
-def back_part(share, kept, weight, deltas, slopes, fields, firsts, total):
-    first_deltas(weight, deltas, slopes, firsts)
-    near = planes_of(fields)
-    own = planes_of([[ref] for ref in firsts])
-    low, high = kept
-    weight_loop(total, near[low : high + 2], 3, own[low:high], 1, share)
-
-
-def middle_kernel(share, groups, pairs, *refs):
+def gradient_kernel(share, groups, extent, pairs, *refs):
     refs = list(refs)
     hiddens = [[refs.pop(0)] for _ in range(pairs + 1)]
-    deltas = [refs.pop(0) for _ in range(pairs)]
+    deltas = [[refs.pop(0)] for _ in range(pairs)]
     weight = refs.pop(0)
-    count = pairs - 1
-    slopes = [refs.pop(0) for _ in range(count)]
-    fields = [[refs.pop(0) for _ in range(groups)] for _ in range(pairs)]
-    raw, first_total = refs.pop(0), refs.pop(0)
-    firsts, total = refs[:count], refs[-1]
-    total[...] = jnp.zeros_like(total)
-    weight_loop(total, planes_of(hiddens), 2, planes_of([[d] for d in deltas]), 2, share)
-    for g, tiles in enumerate(weight_fold(total, raw.shape[2])):
-        for h, tile in enumerate(tiles):
-            raw[g, h] = tile
+    slopes = [refs.pop(0) for _ in range(pairs + 1)]
+    fields = [[refs.pop(0) for _ in range(groups)] for _ in range(pairs + 2)]
+    keep, send = refs.pop(0), refs.pop(0)
+    inner = [refs.pop(0) for _ in range(pairs - 1)]
+    head, tail, none, second_total, first_total = refs
+    none[...] = jnp.zeros_like(none)
+    second_total[...] = jnp.zeros_like(second_total)
     first_total[...] = jnp.zeros_like(first_total)
-    if count > 0:
-        kept = (0, 2 * count)
-        back_part(share, kept, weight, deltas, slopes, fields, firsts, first_total)
-
-
-def back_kernel(share, groups, weight, one, two, slope, *refs):
-    refs = list(refs)
-    fields = [[refs.pop(0) for _ in range(groups)] for _ in range(2)]
-    before, first, total = refs
-    total[...] = before[...]
-    back_part(share, (0, 1), weight, [one, two], [slope], fields, [first], total)
-
-
-def first_kernel(share, groups, after, weight, one, two, slope, *refs):
-    del after
-    refs = list(refs)
-    fields = [[refs.pop(0) for _ in range(groups)] for _ in range(2)]
-    before, second = refs.pop(0), refs.pop(0)
-    first, total = refs[0], refs[-1]
-    extent = (len(refs) - 2) // 2
-    keep, send = refs[1 : 1 + extent], refs[1 + extent : -1]
-    total[...] = before[...]
-    back_part(share, (1, 2), weight, [one, two], [slope], fields, [first], total)
-    halves, size = keep[0].shape[:2]
+    weight_loop(second_total, planes_of(hiddens), 2, planes_of(deltas), 2, share)
+    firsts = [head] + inner + [tail]
+    first_deltas(weight, neighbours([[none]] + deltas + [[none]]), slopes, firsts)
+    parts = planes_of([[first] for first in firsts])
+    weight_loop(first_total, planes_of(fields), 3, parts, 1, share)
+    halves, size = keep.shape[1:3]
     me = lax.axis_index("chan")
-    groups_of = weight_fold(total, size)
+    of_first = weight_fold(first_total, size)
+    of_second = weight_fold(second_total, size)
 
     def place(ours, theirs):
-        for g, tiles in enumerate(groups_of):
+        for g in range(extent):
             there = lax.rem(me + extent - g, extent)
             for h in range(halves):
-                ours[g][h] = tiles[h]
-                theirs[g][h] = second[there, h]
+                ours[g, h] = of_first[g][h]
+                theirs[there, h] = of_second[g][h]
 
     odd = lax.rem(lax.axis_index("slab"), 2)
 
@@ -364,7 +340,13 @@
         place(send, keep)
 
 
-def last_kernel(pairs, *refs):
+def back_kernel(then, weight, one, two, slope, first):
+    del then
+    first_deltas(weight, [([one], [two])], [slope], [first])
+
+
+def last_kernel(pairs, after, *refs):
+    del after
     refs = list(refs)
     firsts = [refs.pop(0) for _ in range(pairs + 1)]
     weight = refs.pop(0)
@@ -374,7 +356,7 @@
         row = 2 * r
         size = outs[0].shape[2]
         channels = len(outs) * size
-        for p, sums in enumerate(taps(weight[...], [[first] for first in firsts], row)):
+        for p, sums in enumerate(taps(weight[...], neighbours([[first] for first in firsts]), row)):
             for q, v in enumerate(sums):
                 for x in range(2):
                     for j, out in enumerate(outs):
@@ -404,6 +386,12 @@
         place(second, first)
 
 
+def split_kernel(ahead, *refs):
+    one, two, *outs = refs[ahead:]
+    for g, out in enumerate(outs):
+        out[...] = one[g] + two[g]
+
+
 def add_kernel(ahead, *refs):
     values = [ref[...] for ref in refs[ahead:-1]]
     while len(values) > 1:
@@ -416,8 +404,7 @@
 
 
 def merge_kernel(extent, *refs):
-    pieces, token, out, wide = refs[:-3], refs[-3], refs[-2], refs[-1]
-    token[...] = jnp.zeros_like(token)
+    pieces, out, wide = refs[:-2], refs[-2], refs[-1]
     size, planes, rows = out.shape[:3]
     share = rows // extent
     me = lax.axis_index("chan")
@@ -549,35 +536,41 @@
     delta_before = to_next(deltas[-1])
 
     raw = jax.ShapeDtypeStruct((extent, 7, size, 4 * channels), F32)
-    whole_sum = (6 * channels, 12 * channels)
-    sums = jax.ShapeDtypeStruct(whole_sum, F32)
+    portion = jax.ShapeDtypeStruct(raw.shape[1:], F32)
+    total = pltpu.VMEM((6 * channels, 12 * channels), F32)
+
+    def room(rows_each):
+        return pltpu.VMEM((rows_each, 2, channels, depth), BF16)
+
     made = call(
-        functools.partial(middle_kernel, share, groups, pairs),
-        [raw, sums] + many(pairs - 1, share + 2),
-        hiddens + deltas + [second_back] + slopes[1:pairs] + flat(fields[1:-1]),
-        [pltpu.VMEM(whole_sum, F32)],
-        flops=work * (3 * pairs - 2) * share,
-        moved=space * 9,
-    )
-    second_raw, sums_then, later = made[0], made[1], list(made[2:])
-    made = call(
-        functools.partial(back_kernel, share, groups),
-        many(1, share + 2) + [sums],
-        [second_back, deltas[-1], delta_after, slopes[-1]] + flat(fields[-2:]) + [sums_then],
-        flops=work * 2 * share,
-        moved=space * 6,
-    )
-    later, sums_then = later + [made[0]], made[1]
-
-    def field_grad(firsts):
+        functools.partial(gradient_kernel, share, groups, extent, pairs),
+        [raw] * 2 + many(pairs - 1, share + 2),
+        hiddens + deltas + [second_back] + slopes + flat(fields),
+        [room(share + 2), room(share + 2), room(share + 4), total, total],
+    )
+    keep, send, inner = made[0], made[1], list(made[2:])
+    def outer(then, one, two, slope):
+        return call(
+            back_kernel,
+            many(1, share + 2),
+            [then, second_back, one, two, slope],
+            flops=work * share,
+            moved=space * 2,
+            loose=1,
+        )[0]
+
+    last = outer(keep, deltas[-1], delta_after, slopes[-1])
+
+    def field_grad(firsts, after):
         count = len(firsts) - 1
         return list(
             call(
                 functools.partial(last_kernel, count),
                 [jax.ShapeDtypeStruct((share, 2 * count, size, depth), BF16)] * extent,
-                firsts + [first_back],
+                [after] + firsts + [first_back],
                 flops=work * count * share,
                 moved=space * 2 * count,
+                loose=1,
             )
         )
 
@@ -586,25 +579,6 @@
         for j in range(1, extent):
             pieces[extent - j] = to_chan(made[j], extent - j)
         return pieces
-
-    pieces, early = [], [later[0]]
-    if pairs > 1:
-        early = field_grad(later)
-        pieces = exchanged(early)
-    portion = jax.ShapeDtypeStruct(raw.shape[1:], F32)
-    made = call(
-        functools.partial(first_kernel, share, groups),
-        many(1, share + 2) + [portion] * (2 * extent),
-        [early[0], second_back, delta_before, deltas[0], slopes[0]]
-        + flat(fields[0:2])
-        + [sums_then, second_raw],
-        [pltpu.VMEM(whole_sum, F32)],
-        flops=work * 2 * share,
-        moved=space * 6,
-        loose=1,
-    )
-
-    first, keep, send = made[0], made[1 : 1 + extent], made[1 + extent :]
 
     def stepped(value, stride, shift=0):
         if shift % extent == 0:
@@ -616,36 +590,38 @@
                 pairs_of.append((i * extent + k, there))
         return lax.ppermute(value, ("slab", "chan"), pairs_of)
 
-    made = field_grad([first, later[0]])
     plain = slabs & (slabs - 1) == 0 and slabs >= 4
     if plain:
-        shares = [keep[0], stepped(send[0], 1)]
-        for j in range(1, extent):
-            shares += [to_chan(keep[j], extent - j), stepped(send[j], 1, extent - j)]
-        ahead = made[:1] + pieces[1:2]
+        ahead = [last]
+        kept = call(
+            functools.partial(split_kernel, len(ahead)),
+            [portion] * extent,
+            ahead + [keep, stepped(send, 1)],
+            loose=len(ahead),
+        )
+        shares = [kept[0]] + [to_chan(kept[j], extent - j) for j in range(1, extent)]
+        shares += [stepped(kept[j], 2, extent - j) for j in range(extent)]
+        after = kept[0]
+    else:
+        after = keep
+    first = outer(after, delta_before, deltas[0], slopes[0])
+    firsts = [first] + inner + [last]
+    halves = [field_grad(firsts[:2], after)]
+    if pairs > 1:
+        halves.append(field_grad(firsts[1:], after))
+    if plain:
+        ahead = [made[0] for made in halves]
         (mine,) = call(
             functools.partial(add_kernel, len(ahead)), [portion], ahead + shares, loose=len(ahead)
         )
-        made = [made[0]] + [relayed(value, mine) for value in made[1:]]
-    pieces = exchanged(made) + pieces
-
-    token, input_grad = call(
-        functools.partial(merge_kernel, extent),
-        [jax.ShapeDtypeStruct((8, 128), F32), jax.ShapeDtypeStruct(field.shape, BF16)],
-        pieces,
-        [pltpu.VMEM((rows * planes * size, depth), F32)],
-        moved=4 * field.size,
-    )
+        halves = [made[:1] + [relayed(value, mine) for value in made[1:]] for made in halves]
+    pieces = [piece for made in halves for piece in exchanged(made)]
     if plain:
-        stride = 2
+        stride = 4
         while stride < slabs:
             radix = 4 if slabs % (4 * stride) == 0 else 2
             got = [mine] + [stepped(mine, m * stride) for m in range(1, radix)]
-            last = stride * radix == slabs
-            ahead = [token] if last else []
-            (mine,) = call(
-                functools.partial(add_kernel, len(ahead)), [portion], ahead + got, loose=len(ahead)
-            )
+            (mine,) = call(functools.partial(add_kernel, 0), [portion], got)
             stride *= radix
         other = stepped(mine, 1)
     else:
@@ -656,6 +632,13 @@
         mine, other = jnp.where(even, mine, other), jnp.where(even, other, mine)
         mine, other = lax.psum((mine, other), "slab")
         mine, other = jnp.where(even, mine, other), jnp.where(even, other, mine)
+    (input_grad,) = call(
+        functools.partial(merge_kernel, extent),
+        [jax.ShapeDtypeStruct(field.shape, BF16)],
+        pieces,
+        [pltpu.VMEM((rows * planes * size, depth), F32)],
+        moved=4 * field.size,
+    )
     first_grad, second_grad = call(
         functools.partial(finish_kernel, factor),
         [jax.ShapeDtypeStruct(by_tap, F32)] * 2,

time: 65.1 us -> 65.3 us (level)
  Pallas kernels: 22 us -> 25.1 us
  waiting for transfers between devices: 12.2 us -> 10.3 us
  starting transfers between devices: 25.5 us -> 24.5 us
    pallas_call x19 -> x20, Pallas kernels: 22 us -> 25.1 us  [call(): pl.pallas_call(kernel, out_shape=outs, in_specs=[still] * loose + [whole]...]
    ppermute x6, waiting for transfers between devices: 4.78 us -> 7.61 us  [stepped(): return lax.ppermute(value, 'slab', [(i, i ^ stride) for i in range(slabs)])]
    ppermute x3, waiting for transfers between devices: 2.27 us -> 0.01 us  [to_next(): lax.ppermute(value, 'slab', [(i, (i + 1) % slabs) for i in range(slabs)])]
    ppermute x6, waiting for transfers between devices: 4.03 us -> 2.7 us  [to_chan(): lax.ppermute(value, 'chan', [(i, (i + shift) % extent) for i in range(ext...]
    ppermute x1, waiting for transfers between devices: 1.09 us -> 0.01 us  [stepped(): return lax.ppermute(value, ('slab', 'chan'), pairs_of)]
    ppermute x6, starting transfers between devices: 9.43 us -> 8.75 us  [to_chan(): lax.ppermute(value, 'chan', [(i, (i + shift) % extent) for i in range(ext...]
  transfers between devices with their start and end apart: 19 -> 19, of which waited for: 9 -> 5; matrix products, arithmetic and copies ran while one was open for 0% -> 0% of each run, Pallas kernels for 30% -> 33%
where the time goes in v11:
time: 65.3 us; the launch traced here: 65.1 us
  Pallas kernels  25.1 us (38%)
  starting transfers between devices  24.5 us (38%)
  waiting for transfers between devices  10.3 us (16%)
  local copies, waits for them, and re-layouts  4.32 us (7%)
  between operations  0.85 us (1%)
    pallas_call x20, Pallas kernels, call(): pl.pallas_call(kernel, out_shape=outs, in_specs=[still] * loose + [whole]...  25.1 us
    ppermute x6, starting transfers between devices, to_chan(): lax.ppermute(value, 'chan', [(i, (i + shift) % extent) for i in range(ext...  8.75 us
    ppermute x3, starting transfers between devices, to_prev(): lax.ppermute(value, 'slab', [((i + 1) % slabs, i) for i in range(slabs)])  8.69 us
    ppermute x6, waiting for transfers between devices, stepped(): return lax.ppermute(value, 'slab', [(i, i ^ stride) for i in range(slabs)])  7.61 us
    ppermute x6, starting transfers between devices, stepped(): return lax.ppermute(value, 'slab', [(i, i ^ stride) for i in range(slabs)])  6.93 us
    unnamed x8, local copies, waits for them, and re-layouts  4.32 us
    ppermute x6, waiting for transfers between devices, to_chan(): lax.ppermute(value, 'chan', [(i, (i + shift) % extent) for i in range(ext...  2.7 us
  transfers between devices with their start and end apart: 19, of which 5 were waited for; matrix products, arithmetic and copies ran while one was open for 0% of the time, Pallas kernels for 33%

profile of v11, /device:TPU:0, one launch (start us, length us, event | category | flops | bytes accessed | tf_op | source)
XLA Modules:
  0.0 65.1 jit_solution(8934159394956103803)
XLA Ops:
  0.6 0.0 copy-start.1
  0.6 1.1 %copy-done.1 = bf16[16,4,48,128]{3,2,1,0:T(8,128)(2,1)S(1)} copy-done((bf16[16,4,48,128]{3,2,1,0:T(8,128)(2,1)S(1)}, bf16[16,4,48,128]{3,2,1,0:T(8,128)(2,1)}, u32[]{:S(2)}) %copy-start.1) | copy-done | bytes 786456
  1.8 1.5 %shard_map.67 = (bf16[32,2,16,128]{3,2,1,0:T(8,128)(2,1)S(1)}, bf16[32,2,16,128]{3,2,1,0:T(8,128)(2,1)S(1)}, bf16[32,2,16,128]{3,2,1,0:T(8,128)(2,1)S(1)}, bf16[32,2,16,128]{3,2,1,0:T(8,128)(2,1)S(1)}) custom-call(bf16[16,4,48,128]{3,2,1,0:T(8,128)(2,1)S(1)} %copy-done.1), custom_call_target="tpu_custom_call" | custom-call | bytes 2359296 | tf_op jit(solution)/shard_map/pallas_call | solution.py:19
  3.3 3.0 %collective-permute-start.1 = (bf16[32,2,16,128]{3,2,1,0:T(8,128)(2,1)S(1)}, bf16[32,2,16,128]{3,2,1,0:T(8,128)(2,1)S(1)}, u32[]{:S(2)}, u32[]{:S(2)}) collective-permute-start(bf16[32,2,16,128]{3,2,1,0:T(8,128)(2,1)S(1)} %get-tuple-element.33), channel_id=1, source_target_pairs={{0,1},{1,0},{2,3},{3,2},{4,5},{5,4},{6,7},{7,6},{8,9},{9,8},{10,11... | collective-permute-start | bytes 786440 | tf_op jit(solution)/shard_map/ppermute | solution.py:444
  6.3 3.7 %collective-permute-start.4 = (bf16[32,2,16,128]{3,2,1,0:T(8,128)(2,1)S(1)}, bf16[32,2,16,128]{3,2,1,0:T(8,128)(2,1)S(1)}, u32[]{:S(2)}, u32[]{:S(2)}) collective-permute-start(bf16[32,2,16,128]{3,2,1,0:T(8,128)(2,1)S(1)} %get-tuple-element.34.after.refs_2_.refs_11_), channel_id=1, source_target_pairs={{2,0},{4,2},{6,4},{8,6},{10,8},{12,10},{14,12},{16,14},{18,16},{20... | collective-permute-start | bytes 786440 | tf_op jit(solution)/shard_map/ppermute | solution.py:450
  10.0 0.5 collective-permute-start.3
  10.5 0.0 collective-permute-start
  10.5 0.0 copy-start.2
  10.5 0.9 %copy-done.2 = bf16[16,27,32]{2,0,1:T(8,128)(2,1)S(1)} copy-done((bf16[16,27,32]{2,0,1:T(8,128)(2,1)S(1)}, bf16[16,27,32]{2,0,1:T(8,128)(2,1)}, u32[]{:S(2)}) %copy-start.2) | copy-done | bytes 27672
  11.4 0.0 copy-start.3
  11.4 0.9 %copy-done.3 = bf16[16,27,32]{2,0,1:T(8,128)(2,1)S(1)} copy-done((bf16[16,27,32]{2,0,1:T(8,128)(2,1)S(1)}, bf16[16,27,32]{2,0,1:T(8,128)(2,1)}, u32[]{:S(2)}) %copy-start.3) | copy-done | bytes 27672
  12.3 0.1 shard_map.68.after.refs_0_
  12.4 0.0 copy-start
  12.4 1.4 %copy-done = bf16[32,4,48,128]{3,2,1,0:T(8,128)(2,1)S(1)} copy-done((bf16[32,4,48,128]{3,2,1,0:T(8,128)(2,1)S(1)}, bf16[32,4,48,128]{3,2,1,0:T(8,128)(2,1)}, u32[]{:S(2)}) %copy-start) | copy-done | bytes 1572888
  13.8 1.3 %shard_map.69 = (bf16[28,2,32,128]{3,2,1,0:T(8,128)(2,1)S(1)}, bf16[28,2,32,128]{3,2,1,0:T(8,128)(2,1)S(1)}) custom-call(bf16[14,16,128]{2,1,0:T(8,128)(2,1)S(1)} %shard_map.68.after.refs_0_, bf16[32,4,48,128]{3,2,1,0:T(8,128)(2,1)S(1)} %copy-done), custom_call_target="tpu_custom_call" | custom-call | bytes 3145728 | tf_op jit(solution)/shard_map/pallas_call | solution.py:19
  15.1 0.0 collective-permute-done.1.refs_0_
  15.2 0.1 collective-permute-start.2
  15.2 1.6 %collective-permute-start.5 = (bf16[14,16,128]{2,1,0:T(8,128)(2,1)S(1)}, bf16[14,16,128]{2,1,0:T(8,128)(2,1)S(1)}, u32[]{:S(2)}, u32[]{:S(2)}) collective-permute-start(bf16[14,16,128]{2,1,0:T(8,128)(2,1)S(1)} %shard_map.68.after.refs_0_), channel_id=1, source_target_pairs={{0,1},{1,0},{2,3},{3,2},{4,5},{5,4},{6,7},{7,6},{8,9},{9,8},{10,11... | collective-permute-start | bytes 172040 | tf_op jit(solution)/shard_map/ppermute | solution.py:444
  16.8 2.7 %collective-permute-done.5.refs_2_.refs_1_ = bf16[14,16,128]{2,1,0:T(8,128)(2,1)S(1)} collective-permute-done((bf16[14,16,128]{2,1,0:T(8,128)(2,1)S(1)}, bf16[14,16,128]{2,1,0:T(8,128)(2,1)S(1)}, u32[]{:S(2)}, u32[]{:S(2)}) %collective-permute-start.5) | collective-permute-done | bytes 57376 | tf_op jit(solution)/shard_map/ppermute | solution.py:444
  19.5 0.0 collective-permute-done.4.refs_1_.refs_2_.refs_15_
  19.5 0.0 collective-permute-done.3.refs_0_
  19.5 3.9 %collective-permute-start.6 = (bf16[32,2,16,128]{3,2,1,0:T(8,128)(2,1)S(1)}, bf16[32,2,16,128]{3,2,1,0:T(8,128)(2,1)S(1)}, u32[]{:S(2)}, u32[]{:S(2)}) collective-permute-start(bf16[32,2,16,128]{3,2,1,0:T(8,128)(2,1)S(1)} %shard_map.71.refs_3_.refs_12_), channel_id=1, source_target_pairs={{2,0},{4,2},{6,4},{8,6},{10,8},{12,10},{14,12},{16,14},{18,16},{20... | collective-permute-start | bytes 786440 | tf_op jit(solution)/shard_map/ppermute | solution.py:450
  23.4 0.5 shard_map.72
  23.9 0.0 collective-permute-done.refs_0_.refs_9_
  23.9 0.0 collective-permute-done.2.refs_1_.refs_10_
  23.9 3.6 %shard_map.73 = (bf16[30,2,32,128]{3,2,1,0:T(8,128)(2,1)S(1)}, bf16[30,2,32,128]{3,2,1,0:T(8,128)(2,1)S(1)}, bf16[30,2,32,128]{3,2,1,0:T(8,128)(2,1)S(1)}, bf16[...) custom-call(bf16[32,2,16,128]{3,2,1,0:T(8,128)(2,1)S(1)} %collective-permute-done.refs_0_.refs_9_, ...), custom_call_target="tpu_custom_call" | custom-call | flops 1019215872 | bytes 3145728 | tf_op jit(solution)/shard_map/pallas_call | solution.py:19
  27.5 1.1 %collective-permute-start.7 = (bf16[28,2,32,128]{3,2,1,0:T(8,128)(2,1)S(1)}, bf16[28,2,32,128]{3,2,1,0:T(8,128)(2,1)S(1)}, u32[]{:S(2)}, u32[]{:S(2)}) collective-permute-start(bf16[28,2,32,128]{3,2,1,0:T(8,128)(2,1)S(1)} %get-tuple-element.43.refs_3_.two), channel_id=1, source_target_pairs={{2,0},{4,2},{6,4},{8,6},{10,8},{12,10},{14,12},{16,14},{18,16},{20... | collective-permute-start | bytes 1376264 | tf_op jit(solution)/shard_map/ppermute | solution.py:450
  28.6 0.0 collective-permute-done.6.refs_3_.refs_16_
  28.6 2.8 %shard_map.74 = (bf16[30,2,32,128]{3,2,1,0:T(8,128)(2,1)S(1)}, bf16[30,2,32,128]{3,2,1,0:T(8,128)(2,1)S(1)}, bf16[28,2,32,128]{3,2,1,0:T(8,128)(2,1)S(1)}) custom-call(bf16[32,2,16,128]{3,2,1,0:T(8,128)(2,1)S(1)} %get-tuple-element.32.refs_4_.refs_0_.refs_13_, bf16[32,2,16,128]{3,2,1,0:T(8,128)(2,1)S(1)} %shard_map.70.refs_5_.refs_1_.refs_14_, ...), custom_call_target="tpu_custom_call" | custom-call | flops 679477248 | bytes 2359296 | tf_op jit(solution)/shard_map/pallas_call | solution.py:19
  31.4 0.1 collective-permute-start.9
  31.4 8.4 %shard_map.75 = (f32[2,7,16,128]{3,2,1,0:T(8,128)S(1)}, f32[2,7,16,128]{3,2,1,0:T(8,128)S(1)}, bf16[26,2,32,128]{3,2,1,0:T(8,128)(2,1)S(1)}) custom-call(bf16[30,2,32,128]{3,2,1,0:T(8,128)(2,1)S(1)} %get-tuple-element.39.refs_0_, bf16[30,2,32,128]{3,2,1,0:T(8,128)(2,1)S(1)} %get-tuple-element.40.refs_4_.refs_1_, ...), custom_call_target="tpu_custom_call" | custom-call | tf_op jit(solution)/shard_map/pallas_call | solution.py:19
  39.8 0.1 collective-permute-start.8
  39.9 0.0 collective-permute-done.7.two
  39.9 0.9 %shard_map.76.refs_0_.refs_1_ = bf16[26,2,32,128]{3,2,1,0:T(8,128)(2,1)S(1)} custom-call(f32[2,7,16,128]{3,2,1,0:T(8,128)S(1)} %get-tuple-element.49.then.refs_1_, bf16[192,384]{1,0:T(8,128)(2,1)S(1)} %get-tuple-element.45.refs_5_.weight, bf16[28,2,32,128]{3,2,1,0:T(8,128)(2,1)S(1)} %get-tuple-element.44.refs_4_.one, ...), custom_call_target="tpu_custom_call" | custom-call | flops 339738624 | bytes 786432 | tf_op jit(solution)/shard_map/pallas_call | solution.py:19
  40.8 0.4 collective-permute-done.8.refs_2_
  41.2 1.6 %collective-permute-start.10 = (f32[7,16,128]{2,1,0:T(8,128)S(1)}, f32[7,16,128]{2,1,0:T(8,128)S(1)}, u32[]{:S(2)}, u32[]{:S(2)}) collective-permute-start(f32[7,16,128]{2,1,0:T(8,128)S(1)} %get-tuple-element.57), channel_id=1, source_target_pairs={{0,1},{1,0},{2,3},{3,2},{4,5},{5,4},{6,7},{7,6},{8,9},{9,8},{10,11... | collective-permute-start | bytes 172040 | tf_op jit(solution)/shard_map/ppermute | solution.py:444
  42.8 0.0 collective-permute-start.12
  42.8 2.0 %collective-permute-start.11 = (f32[7,16,128]{2,1,0:T(8,128)S(1)}, f32[7,16,128]{2,1,0:T(8,128)S(1)}, u32[]{:S(2)}, u32[]{:S(2)}) collective-permute-start(f32[7,16,128]{2,1,0:T(8,128)S(1)} %get-tuple-element.51.then.after.refs_2_), channel_id=1, source_target_pairs={{0,4},{2,6},{4,0},{6,2},{8,12},{10,14},{12,8},{14,10},{16,20},{18,... | collective-permute-start | bytes 172040 | tf_op jit(solution)/shard_map/ppermute | solution.py:585
  44.8 1.1 %shard_map.80 = (bf16[24,2,16,128]{3,2,1,0:T(8,128)(2,1)S(1)}, bf16[24,2,16,128]{3,2,1,0:T(8,128)(2,1)S(1)}) custom-call(f32[7,16,128]{2,1,0:T(8,128)S(1)} %get-tuple-element.51.then.after.refs_2_, bf16[26,2,32,128]{3,2,1,0:T(8,128)(2,1)S(1)} %get-tuple-element.52.refs_1_.refs_0_, bf16[26,2,32,128]{3,2,1,0:T(8,128)(2,1)S(1)} %shard_map.76.refs_0_.refs_1_, ...), custom_call_target="tpu_custom_call" | custom-call | flops 339738624 | bytes 786432 | tf_op jit(solution)/shard_map/pallas_call | solution.py:19
  45.9 0.0 collective-permute-done.9.one
  45.9 0.9 %shard_map.78.refs_0_ = bf16[26,2,32,128]{3,2,1,0:T(8,128)(2,1)S(1)} custom-call(f32[7,16,128]{2,1,0:T(8,128)S(1)} %get-tuple-element.51.then.after.refs_2_, bf16[192,384]{1,0:T(8,128)(2,1)S(1)} %get-tuple-element.45.refs_5_.weight, bf16[28,2,32,128]{3,2,1,0:T(8,128)(2,1)S(1)} %collective-permute-done.9.one, ...), custom_call_target="tpu_custom_call" | custom-call | flops 339738624 | bytes 786432 | tf_op jit(solution)/shard_map/pallas_call | solution.py:19
  46.8 1.1 %shard_map.79 = (bf16[24,2,16,128]{3,2,1,0:T(8,128)(2,1)S(1)}, bf16[24,2,16,128]{3,2,1,0:T(8,128)(2,1)S(1)}) custom-call(f32[7,16,128]{2,1,0:T(8,128)S(1)} %get-tuple-element.51.then.after.refs_2_, bf16[26,2,32,128]{3,2,1,0:T(8,128)(2,1)S(1)} %shard_map.78.refs_0_, bf16[26,2,32,128]{3,2,1,0:T(8,128)(2,1)S(1)} %get-tuple-element.52.refs_1_.refs_0_, ...), custom_call_target="tpu_custom_call" | custom-call | flops 339738624 | bytes 786432 | tf_op jit(solution)/shard_map/pallas_call | solution.py:19
  48.0 0.0 collective-permute-done.10.refs_3_
  48.0 0.0 collective-permute-done.11.refs_4_
  48.0 0.0 collective-permute-done.12.refs_5_
  48.0 1.6 %collective-permute-start.14 = (bf16[24,2,16,128]{3,2,1,0:T(8,128)(2,1)S(1)}, bf16[24,2,16,128]{3,2,1,0:T(8,128)(2,1)S(1)}, u32[]{:S(2)}, u32[]{:S(2)}) collective-permute-start(bf16[24,2,16,128]{3,2,1,0:T(8,128)(2,1)S(1)} %shard_map.83), channel_id=1, source_target_pairs={{0,1},{1,0},{2,3},{3,2},{4,5},{5,4},{6,7},{7,6},{8,9},{9,8},{10,11... | collective-permute-start | bytes 589832 | tf_op jit(solution)/shard_map/ppermute | solution.py:444
  49.6 0.5 collective-permute-start.13
  50.1 0.4 collective-permute-start.15
  50.5 4.4 %collective-permute-start.16 = (f32[7,16,128]{2,1,0:T(8,128)S(1)}, f32[7,16,128]{2,1,0:T(8,128)S(1)}, u32[]{:S(2)}, u32[]{:S(2)}) collective-permute-start(f32[7,16,128]{2,1,0:T(8,128)S(1)} %shard_map.81.refs_1_.refs_0_), channel_id=1, source_target_pairs={{0,16},{2,18},{4,20},{6,22},{8,24},{10,26},{12,28},{14,30},{16,0},... | collective-permute-start | bytes 172040 | tf_op jit(solution)/shard_map/ppermute | solution.py:585
  54.9 0.0 collective-permute-start.17
  54.9 0.0 collective-permute-done.15.refs_1_
  54.9 2.8 %collective-permute-done.16.refs_2_ = f32[7,16,128]{2,1,0:T(8,128)S(1)} collective-permute-done((f32[7,16,128]{2,1,0:T(8,128)S(1)}, f32[7,16,128]{2,1,0:T(8,128)S(1)}, u32[]{:S(2)}, u32[]{:S(2)}) %collective-permute-start.16) | collective-permute-done | bytes 57376 | tf_op jit(solution)/shard_map/ppermute | solution.py:585
  57.7 3.2 %collective-permute-done.17.refs_3_ = f32[7,16,128]{2,1,0:T(8,128)S(1)} collective-permute-done((f32[7,16,128]{2,1,0:T(8,128)S(1)}, f32[7,16,128]{2,1,0:T(8,128)S(1)}, u32[]{:S(2)}, u32[]{:S(2)}) %collective-permute-start.17) | collective-permute-done | bytes 57376 | tf_op jit(solution)/shard_map/ppermute | solution.py:585
  60.9 0.1 collective-permute-start.18
  61.0 1.2 %collective-permute-done.18.other = f32[7,16,128]{2,1,0:T(8,128)S(1)} collective-permute-done((f32[7,16,128]{2,1,0:T(8,128)S(1)}, f32[7,16,128]{2,1,0:T(8,128)S(1)}, u32[]{:S(2)}, u32[]{:S(2)}) %collective-permute-start.18) | collective-permute-done | bytes 57376 | tf_op jit(solution)/shard_map/ppermute | solution.py:585
  62.2 0.9 %shard_map.86 = (f32[27,16,32]{2,1,0:T(8,128)}, f32[27,16,32]{2,1,0:T(8,128)}) custom-call(f32[7,16,128]{2,1,0:T(8,128)S(1)} %shard_map.85.mine, f32[7,16,128]{2,1,0:T(8,128)S(1)} %collective-permute-done.18.other), custom_call_target="tpu_custom_call" | custom-call | tf_op jit(solution)/shard_map/pallas_call | solution.py:19
  63.1 0.0 collective-permute-done.14.refs_3_
  63.1 0.0 collective-permute-done.13.refs_1_
  63.1 1.9 %shard_map.84 = bf16[16,4,48,128]{3,2,1,0:T(8,128)(2,1)} custom-call(bf16[24,2,16,128]{3,2,1,0:T(8,128)(2,1)S(1)} %get-tuple-element.54.refs_0_, bf16[24,2,16,128]{3,2,1,0:T(8,128)(2,1)S(1)} %collective-permute-done.13.refs_1_, bf16[24,2,16,128]{3,2,1,0:T(8,128)(2,1)S(1)} %get-tuple-element.56.refs_1_.refs_2_, ...), custom_call_target="tpu_custom_call" | custom-call | bytes 1572864 | tf_op jit(solution)/shard_map/pallas_call | solution.py:19
  (7 shorter events, 0.1 us)
Async XLA Ops:
  0.6 1.1 %copy-start.1 = (bf16[16,4,48,128]{3,2,1,0:T(8,128)(2,1)S(1)}, bf16[16,4,48,128]{3,2,1,0:T(8,128)(2,1)}, u32[]{:S(2)}) copy-start(bf16[16,4,48,128]{3,2,1,0:T(8,128)(2,1)} %x_ref.2) | copy-start | bytes 2359300
  3.3 11.9 %collective-permute-start.1 = (bf16[32,2,16,128]{3,2,1,0:T(8,128)(2,1)S(1)}, bf16[32,2,16,128]{3,2,1,0:T(8,128)(2,1)S(1)}, u32[]{:S(2)}, u32[]{:S(2)}) collective-permute-start(bf16[32,2,16,128]{3,2,1,0:T(8,128)(2,1)S(1)} %get-tuple-element.33), channel_id=1, source_target_pairs={{0,1},{1,0},{2,3},{3,2},{4,5},{5,4},{6,7},{7,6},{8,9},{9,8},{10,11... | collective-permute-start | bytes 786440 | tf_op jit(solution)/shard_map/ppermute | solution.py:444
  6.3 13.2 %collective-permute-start.4 = (bf16[32,2,16,128]{3,2,1,0:T(8,128)(2,1)S(1)}, bf16[32,2,16,128]{3,2,1,0:T(8,128)(2,1)S(1)}, u32[]{:S(2)}, u32[]{:S(2)}) collective-permute-start(bf16[32,2,16,128]{3,2,1,0:T(8,128)(2,1)S(1)} %get-tuple-element.34.after.refs_2_.refs_11_), channel_id=1, source_target_pairs={{2,0},{4,2},{6,4},{8,6},{10,8},{12,10},{14,12},{16,14},{18,16},{20... | collective-permute-start | bytes 786440 | tf_op jit(solution)/shard_map/ppermute | solution.py:450
  10.0 9.5 %collective-permute-start.3 = (bf16[32,2,16,128]{3,2,1,0:T(8,128)(2,1)S(1)}, bf16[32,2,16,128]{3,2,1,0:T(8,128)(2,1)S(1)}, u32[]{:S(2)}, u32[]{:S(2)}) collective-permute-start(bf16[32,2,16,128]{3,2,1,0:T(8,128)(2,1)S(1)} %get-tuple-element.36), channel_id=1, source_target_pairs={{0,1},{1,0},{2,3},{3,2},{4,5},{5,4},{6,7},{7,6},{8,9},{9,8},{10,11... | collective-permute-start | bytes 786440 | tf_op jit(solution)/shard_map/ppermute | solution.py:444
  10.5 13.4 %collective-permute-start = (bf16[32,2,16,128]{3,2,1,0:T(8,128)(2,1)S(1)}, bf16[32,2,16,128]{3,2,1,0:T(8,128)(2,1)S(1)}, u32[]{:S(2)}, u32[]{:S(2)}) collective-permute-start(bf16[32,2,16,128]{3,2,1,0:T(8,128)(2,1)S(1)} %get-tuple-element.32.refs_4_.refs_0_.refs_13_), channel_id=1, source_target_pairs={{0,2},{2,4},{4,6},{6,8},{8,10},{10,12},{12,14},{14,16},{16,18},{18... | collective-permute-start | bytes 786440 | tf_op jit(solution)/shard_map/ppermute | solution.py:447
  10.5 0.9 %copy-start.2 = (bf16[16,27,32]{2,0,1:T(8,128)(2,1)S(1)}, bf16[16,27,32]{2,0,1:T(8,128)(2,1)}, u32[]{:S(2)}) copy-start(bf16[16,27,32]{2,0,1:T(8,128)(2,1)} %param.6) | copy-start | bytes 82948
  11.4 0.9 %copy-start.3 = (bf16[16,27,32]{2,0,1:T(8,128)(2,1)S(1)}, bf16[16,27,32]{2,0,1:T(8,128)(2,1)}, u32[]{:S(2)}) copy-start(bf16[16,27,32]{2,0,1:T(8,128)(2,1)} %param.7) | copy-start | bytes 82948
  12.4 1.4 %copy-start = (bf16[32,4,48,128]{3,2,1,0:T(8,128)(2,1)S(1)}, bf16[32,4,48,128]{3,2,1,0:T(8,128)(2,1)}, u32[]{:S(2)}) copy-start(bf16[32,4,48,128]{3,2,1,0:T(8,128)(2,1)} %x_ref.3) | copy-start | bytes 4718596
  15.2 8.8 %collective-permute-start.2 = (bf16[32,2,16,128]{3,2,1,0:T(8,128)(2,1)S(1)}, bf16[32,2,16,128]{3,2,1,0:T(8,128)(2,1)S(1)}, u32[]{:S(2)}, u32[]{:S(2)}) collective-permute-start(bf16[32,2,16,128]{3,2,1,0:T(8,128)(2,1)S(1)} %shard_map.70.refs_5_.refs_1_.refs_14_), channel_id=1, source_target_pairs={{0,2},{2,4},{4,6},{6,8},{8,10},{10,12},{12,14},{14,16},{16,18},{18... | collective-permute-start | bytes 786440 | tf_op jit(solution)/shard_map/ppermute | solution.py:447
  15.2 4.2 %collective-permute-start.5 = (bf16[14,16,128]{2,1,0:T(8,128)(2,1)S(1)}, bf16[14,16,128]{2,1,0:T(8,128)(2,1)S(1)}, u32[]{:S(2)}, u32[]{:S(2)}) collective-permute-start(bf16[14,16,128]{2,1,0:T(8,128)(2,1)S(1)} %shard_map.68.after.refs_0_), channel_id=1, source_target_pairs={{0,1},{1,0},{2,3},{3,2},{4,5},{5,4},{6,7},{7,6},{8,9},{9,8},{10,11... | collective-permute-start | bytes 172040 | tf_op jit(solution)/shard_map/ppermute | solution.py:444
  19.5 9.1 %collective-permute-start.6 = (bf16[32,2,16,128]{3,2,1,0:T(8,128)(2,1)S(1)}, bf16[32,2,16,128]{3,2,1,0:T(8,128)(2,1)S(1)}, u32[]{:S(2)}, u32[]{:S(2)}) collective-permute-start(bf16[32,2,16,128]{3,2,1,0:T(8,128)(2,1)S(1)} %shard_map.71.refs_3_.refs_12_), channel_id=1, source_target_pairs={{2,0},{4,2},{6,4},{8,6},{10,8},{12,10},{14,12},{16,14},{18,16},{20... | collective-permute-start | bytes 786440 | tf_op jit(solution)/shard_map/ppermute | solution.py:450
  27.5 12.4 %collective-permute-start.7 = (bf16[28,2,32,128]{3,2,1,0:T(8,128)(2,1)S(1)}, bf16[28,2,32,128]{3,2,1,0:T(8,128)(2,1)S(1)}, u32[]{:S(2)}, u32[]{:S(2)}) collective-permute-start(bf16[28,2,32,128]{3,2,1,0:T(8,128)(2,1)S(1)} %get-tuple-element.43.refs_3_.two), channel_id=1, source_target_pairs={{2,0},{4,2},{6,4},{8,6},{10,8},{12,10},{14,12},{16,14},{18,16},{20... | collective-permute-start | bytes 1376264 | tf_op jit(solution)/shard_map/ppermute | solution.py:450
  31.4 14.5 %collective-permute-start.9 = (bf16[28,2,32,128]{3,2,1,0:T(8,128)(2,1)S(1)}, bf16[28,2,32,128]{3,2,1,0:T(8,128)(2,1)S(1)}, u32[]{:S(2)}, u32[]{:S(2)}) collective-permute-start(bf16[28,2,32,128]{3,2,1,0:T(8,128)(2,1)S(1)} %get-tuple-element.44.refs_4_.one), channel_id=1, source_target_pairs={{0,2},{2,4},{4,6},{6,8},{8,10},{10,12},{12,14},{14,16},{16,18},{18... | collective-permute-start | bytes 1376264 | tf_op jit(solution)/shard_map/ppermute | solution.py:447
  39.8 1.4 %collective-permute-start.8 = (f32[2,7,16,128]{3,2,1,0:T(8,128)S(1)}, f32[2,7,16,128]{3,2,1,0:T(8,128)S(1)}, u32[]{:S(2)}, u32[]{:S(2)}) collective-permute-start(f32[2,7,16,128]{3,2,1,0:T(8,128)S(1)} %get-tuple-element.50), channel_id=1, source_target_pairs={{0,2},{2,0},{4,6},{6,4},{8,10},{10,8},{12,14},{14,12},{16,18},{18,... | collective-permute-start | bytes 344072 | tf_op jit(solution)/shard_map/ppermute | solution.py:585
  41.2 6.7 %collective-permute-start.10 = (f32[7,16,128]{2,1,0:T(8,128)S(1)}, f32[7,16,128]{2,1,0:T(8,128)S(1)}, u32[]{:S(2)}, u32[]{:S(2)}) collective-permute-start(f32[7,16,128]{2,1,0:T(8,128)S(1)} %get-tuple-element.57), channel_id=1, source_target_pairs={{0,1},{1,0},{2,3},{3,2},{4,5},{5,4},{6,7},{7,6},{8,9},{9,8},{10,11... | collective-permute-start | bytes 172040 | tf_op jit(solution)/shard_map/ppermute | solution.py:444
  42.8 5.2 %collective-permute-start.12 = (f32[7,16,128]{2,1,0:T(8,128)S(1)}, f32[7,16,128]{2,1,0:T(8,128)S(1)}, u32[]{:S(2)}, u32[]{:S(2)}) collective-permute-start(f32[7,16,128]{2,1,0:T(8,128)S(1)} %get-tuple-element.57), channel_id=1, source_target_pairs={{0,5},{1,4},{2,7},{3,6},{4,1},{5,0},{6,3},{7,2},{8,13},{9,12},{10,... | collective-permute-start | bytes 172040 | tf_op jit(solution)/shard_map/ppermute | solution.py:591
  42.8 5.2 %collective-permute-start.11 = (f32[7,16,128]{2,1,0:T(8,128)S(1)}, f32[7,16,128]{2,1,0:T(8,128)S(1)}, u32[]{:S(2)}, u32[]{:S(2)}) collective-permute-start(f32[7,16,128]{2,1,0:T(8,128)S(1)} %get-tuple-element.51.then.after.refs_2_), channel_id=1, source_target_pairs={{0,4},{2,6},{4,0},{6,2},{8,12},{10,14},{12,8},{14,10},{16,20},{18,... | collective-permute-start | bytes 172040 | tf_op jit(solution)/shard_map/ppermute | solution.py:585
  48.0 15.1 %collective-permute-start.14 = (bf16[24,2,16,128]{3,2,1,0:T(8,128)(2,1)S(1)}, bf16[24,2,16,128]{3,2,1,0:T(8,128)(2,1)S(1)}, u32[]{:S(2)}, u32[]{:S(2)}) collective-permute-start(bf16[24,2,16,128]{3,2,1,0:T(8,128)(2,1)S(1)} %shard_map.83), channel_id=1, source_target_pairs={{0,1},{1,0},{2,3},{3,2},{4,5},{5,4},{6,7},{7,6},{8,9},{9,8},{10,11... | collective-permute-start | bytes 589832 | tf_op jit(solution)/shard_map/ppermute | solution.py:444
  49.6 13.5 %collective-permute-start.13 = (bf16[24,2,16,128]{3,2,1,0:T(8,128)(2,1)S(1)}, bf16[24,2,16,128]{3,2,1,0:T(8,128)(2,1)S(1)}, u32[]{:S(2)}, u32[]{:S(2)}) collective-permute-start(bf16[24,2,16,128]{3,2,1,0:T(8,128)(2,1)S(1)} %shard_map.82), channel_id=1, source_target_pairs={{0,1},{1,0},{2,3},{3,2},{4,5},{5,4},{6,7},{7,6},{8,9},{9,8},{10,11... | collective-permute-start | bytes 589832 | tf_op jit(solution)/shard_map/ppermute | solution.py:444
  50.1 4.8 %collective-permute-start.15 = (f32[7,16,128]{2,1,0:T(8,128)S(1)}, f32[7,16,128]{2,1,0:T(8,128)S(1)}, u32[]{:S(2)}, u32[]{:S(2)}) collective-permute-start(f32[7,16,128]{2,1,0:T(8,128)S(1)} %shard_map.81.refs_1_.refs_0_), channel_id=1, source_target_pairs={{0,8},{2,10},{4,12},{6,14},{8,0},{10,2},{12,4},{14,6},{16,24},{18,... | collective-permute-start | bytes 172040 | tf_op jit(solution)/shard_map/ppermute | solution.py:585
  50.5 7.2 %collective-permute-start.16 = (f32[7,16,128]{2,1,0:T(8,128)S(1)}, f32[7,16,128]{2,1,0:T(8,128)S(1)}, u32[]{:S(2)}, u32[]{:S(2)}) collective-permute-start(f32[7,16,128]{2,1,0:T(8,128)S(1)} %shard_map.81.refs_1_.refs_0_), channel_id=1, source_target_pairs={{0,16},{2,18},{4,20},{6,22},{8,24},{10,26},{12,28},{14,30},{16,0},... | collective-permute-start | bytes 172040 | tf_op jit(solution)/shard_map/ppermute | solution.py:585
  54.9 6.0 %collective-permute-start.17 = (f32[7,16,128]{2,1,0:T(8,128)S(1)}, f32[7,16,128]{2,1,0:T(8,128)S(1)}, u32[]{:S(2)}, u32[]{:S(2)}) collective-permute-start(f32[7,16,128]{2,1,0:T(8,128)S(1)} %shard_map.81.refs_1_.refs_0_), channel_id=1, source_target_pairs={{0,24},{2,26},{4,28},{6,30},{8,16},{10,18},{12,20},{14,22},{16,8},... | collective-permute-start | bytes 172040 | tf_op jit(solution)/shard_map/ppermute | solution.py:585
  60.9 1.3 %collective-permute-start.18 = (f32[7,16,128]{2,1,0:T(8,128)S(1)}, f32[7,16,128]{2,1,0:T(8,128)S(1)}, u32[]{:S(2)}, u32[]{:S(2)}) collective-permute-start(f32[7,16,128]{2,1,0:T(8,128)S(1)} %shard_map.85.mine), channel_id=1, source_target_pairs={{0,2},{2,0},{4,6},{6,4},{8,10},{10,8},{12,14},{14,12},{16,18},{18,... | collective-permute-start | bytes 172040 | tf_op jit(solution)/shard_map/ppermute | solution.py:585

commit v12 on v11

--- a/solution.py
+++ b/solution.py
@@ -241,13 +241,8 @@
                 rows = []
                 for q in range(2):
                     wide = delta[delta_row + row + q, place]
-                    plain = wide.astype(F32)
-                    depth = plain.shape[1]
-                    rows += [
-                        pltpu.roll(plain, depth - 1, 1).astype(BF16),
-                        wide,
-                        pltpu.roll(plain, 1, 1).astype(BF16),
-                    ]
+                    depth = wide.shape[1]
+                    rows += [pltpu.roll(wide, depth - 1, 1), wide, pltpu.roll(wide, 1, 1)]
                 left.append(jnp.concatenate(rows, axis=0))
                 rows = []
                 for refs, side in pieces[x : x + 3]:
@@ -340,23 +335,22 @@
         place(send, keep)
 
 
-def back_kernel(then, weight, one, two, slope, first):
-    del then
-    first_deltas(weight, [([one], [two])], [slope], [first])
-
-
-def last_kernel(pairs, after, *refs):
+def field_kernel_back(inner, groups, after, *refs):
     del after
     refs = list(refs)
-    firsts = [refs.pop(0) for _ in range(pairs + 1)]
-    weight = refs.pop(0)
-    outs = refs
+    back, weight = refs.pop(0), refs.pop(0)
+    before, first, last, behind = [[refs.pop(0)] for _ in range(4)]
+    slopes = [refs.pop(0) for _ in range(2)]
+    middle = [refs.pop(0) for _ in range(inner)]
+    outs, ends = refs[:groups], refs[groups:]
+    first_deltas(back, [(before, first), (last, behind)], slopes, ends)
+    firsts = [ends[0]] + middle + [ends[1]]
 
     def one(r):
         row = 2 * r
         size = outs[0].shape[2]
         channels = len(outs) * size
-        for p, sums in enumerate(taps(weight[...], neighbours([[first] for first in firsts]), row)):
+        for p, sums in enumerate(taps(weight[...], neighbours([[ref] for ref in firsts]), row)):
             for q, v in enumerate(sums):
                 for x in range(2):
                     for j, out in enumerate(outs):
@@ -366,7 +360,8 @@
     in_blocks(outs[0].shape[0] // 2, one)
 
 
-def finish_kernel(factor, mine, other, first, second):
+def finish_kernel(factor, after, mine, other, first, second):
+    del after
     channels = first.shape[2]
 
     def place(ours, theirs):
@@ -386,8 +381,7 @@
         place(second, first)
 
 
-def split_kernel(ahead, *refs):
-    one, two, *outs = refs[ahead:]
+def split_kernel(one, two, *outs):
     for g, out in enumerate(outs):
         out[...] = one[g] + two[g]
 
@@ -404,7 +398,8 @@
 
 
 def merge_kernel(extent, *refs):
-    pieces, out, wide = refs[:-2], refs[-2], refs[-1]
+    pieces, token, out, wide = refs[:-3], refs[-3], refs[-2], refs[-1]
+    token[...] = jnp.zeros_like(token)
     size, planes, rows = out.shape[:3]
     share = rows // extent
     me = lax.axis_index("chan")
@@ -549,31 +544,6 @@
         [room(share + 2), room(share + 2), room(share + 4), total, total],
     )
     keep, send, inner = made[0], made[1], list(made[2:])
-    def outer(then, one, two, slope):
-        return call(
-            back_kernel,
-            many(1, share + 2),
-            [then, second_back, one, two, slope],
-            flops=work * share,
-            moved=space * 2,
-            loose=1,
-        )[0]
-
-    last = outer(keep, deltas[-1], delta_after, slopes[-1])
-
-    def field_grad(firsts, after):
-        count = len(firsts) - 1
-        return list(
-            call(
-                functools.partial(last_kernel, count),
-                [jax.ShapeDtypeStruct((share, 2 * count, size, depth), BF16)] * extent,
-                [after] + firsts + [first_back],
-                flops=work * count * share,
-                moved=space * 2 * count,
-                loose=1,
-            )
-        )
-
     def exchanged(made):
         pieces = [made[0]] + [None] * (extent - 1)
         for j in range(1, extent):
@@ -592,30 +562,30 @@
 
     plain = slabs & (slabs - 1) == 0 and slabs >= 4
     if plain:
-        ahead = [last]
-        kept = call(
-            functools.partial(split_kernel, len(ahead)),
-            [portion] * extent,
-            ahead + [keep, stepped(send, 1)],
-            loose=len(ahead),
-        )
+        kept = call(split_kernel, [portion] * extent, [keep, stepped(send, 1)])
         shares = [kept[0]] + [to_chan(kept[j], extent - j) for j in range(1, extent)]
         shares += [stepped(kept[j], 2, extent - j) for j in range(extent)]
         after = kept[0]
     else:
         after = keep
-    first = outer(after, delta_before, deltas[0], slopes[0])
-    firsts = [first] + inner + [last]
-    halves = [field_grad(firsts[:2], after)]
-    if pairs > 1:
-        halves.append(field_grad(firsts[1:], after))
+    made = call(
+        functools.partial(field_kernel_back, pairs - 1, extent),
+        [jax.ShapeDtypeStruct((share, planes, size, depth), BF16)] * extent,
+        [after, second_back, first_back]
+        + [delta_before, deltas[0], deltas[-1], delta_after, slopes[0], slopes[-1]]
+        + inner,
+        [room(share + 2), room(share + 2)],
+        flops=work * (pairs + 2) * share,
+        moved=space * 6,
+        loose=1,
+    )
     if plain:
-        ahead = [made[0] for made in halves]
+        ahead = list(made[:1])
         (mine,) = call(
             functools.partial(add_kernel, len(ahead)), [portion], ahead + shares, loose=len(ahead)
         )
-        halves = [made[:1] + [relayed(value, mine) for value in made[1:]] for made in halves]
-    pieces = [piece for made in halves for piece in exchanged(made)]
+        made = list(made[:1]) + [relayed(value, mine) for value in made[1:]]
+    pieces = exchanged(made)
     if plain:
         stride = 4
         while stride < slabs:
@@ -632,9 +602,9 @@
         mine, other = jnp.where(even, mine, other), jnp.where(even, other, mine)
         mine, other = lax.psum((mine, other), "slab")
         mine, other = jnp.where(even, mine, other), jnp.where(even, other, mine)
-    (input_grad,) = call(
+    token, input_grad = call(
         functools.partial(merge_kernel, extent),
-        [jax.ShapeDtypeStruct(field.shape, BF16)],
+        [jax.ShapeDtypeStruct((8, 128), F32), jax.ShapeDtypeStruct(field.shape, BF16)],
         pieces,
         [pltpu.VMEM((rows * planes * size, depth), F32)],
         moved=4 * field.size,
@@ -642,7 +612,8 @@
     first_grad, second_grad = call(
         functools.partial(finish_kernel, factor),
         [jax.ShapeDtypeStruct(by_tap, F32)] * 2,
-        [mine, other],
+        [token, mine, other],
+        loose=1,
     )
     first_grad, second_grad = (jnp.transpose(g, (1, 0, 2)) for g in (first_grad, second_grad))
     return input_grad, first_grad, second_grad

time: 65.3 us -> 64.9 us (level)
  starting transfers between devices: 24.5 us -> 26.9 us
  waiting for transfers between devices: 10.3 us -> 8.35 us
  Pallas kernels: 25.1 us -> 24.3 us
    ppermute x6, waiting for transfers between devices: 7.61 us -> 4.19 us  [stepped(): return lax.ppermute(value, 'slab', [(i, i ^ stride) for i in range(slabs)])]
    ppermute x3, starting transfers between devices: 8.69 us -> 12 us  [to_prev(): lax.ppermute(value, 'slab', [((i + 1) % slabs, i) for i in range(slabs)])]
    ppermute x6 -> x5, waiting for transfers between devices: 2.7 us -> 4.14 us  [to_chan(): lax.ppermute(value, 'chan', [(i, (i + shift) % extent) for i in range(ext...]
    pallas_call x20 -> x16, Pallas kernels: 25.1 us -> 24.3 us  [call(): pl.pallas_call(kernel, out_shape=outs, in_specs=[still] * loose + [whole]...]
    ppermute x6 -> x5, starting transfers between devices: 8.75 us -> 8.25 us  [to_chan(): lax.ppermute(value, 'chan', [(i, (i + shift) % extent) for i in range(ext...]
  transfers between devices with their start and end apart: 19 -> 18, of which waited for: 5 -> 5; matrix products, arithmetic and copies ran while one was open for 0% -> 0% of each run, Pallas kernels for 33% -> 30%
where the time goes in v12:
time: 64.9 us; the launch traced here: 64.7 us
  starting transfers between devices  26.9 us (41%)
  Pallas kernels  24.3 us (37%)
  waiting for transfers between devices  8.35 us (13%)
  local copies, waits for them, and re-layouts  4.32 us (7%)
  between operations  0.84 us (1%)
    pallas_call x16, Pallas kernels, call(): pl.pallas_call(kernel, out_shape=outs, in_specs=[still] * loose + [whole]...  24.3 us
    ppermute x3, starting transfers between devices, to_prev(): lax.ppermute(value, 'slab', [((i + 1) % slabs, i) for i in range(slabs)])  12 us
    ppermute x5, starting transfers between devices, to_chan(): lax.ppermute(value, 'chan', [(i, (i + shift) % extent) for i in range(ext...  8.25 us
    ppermute x6, starting transfers between devices, stepped(): return lax.ppermute(value, 'slab', [(i, i ^ stride) for i in range(slabs)])  6.5 us
    unnamed x8, local copies, waits for them, and re-layouts  4.32 us
    ppermute x6, waiting for transfers between devices, stepped(): return lax.ppermute(value, 'slab', [(i, i ^ stride) for i in range(slabs)])  4.19 us
    ppermute x5, waiting for transfers between devices, to_chan(): lax.ppermute(value, 'chan', [(i, (i + shift) % extent) for i in range(ext...  4.14 us
  transfers between devices with their start and end apart: 18, of which 5 were waited for; matrix products, arithmetic and copies ran while one was open for 0% of the time, Pallas kernels for 30%

profile of v12, /device:TPU:0, one launch (start us, length us, event | category | flops | bytes accessed | tf_op | source)
XLA Modules:
  0.0 64.7 jit_solution(13205688034331610921)
XLA Ops:
  0.6 0.0 copy-start.1
  0.6 1.1 %copy-done.1 = bf16[16,4,48,128]{3,2,1,0:T(8,128)(2,1)S(1)} copy-done((bf16[16,4,48,128]{3,2,1,0:T(8,128)(2,1)S(1)}, bf16[16,4,48,128]{3,2,1,0:T(8,128)(2,1)}, u32[]{:S(2)}) %copy-start.1) | copy-done | bytes 786456
  1.8 1.5 %shard_map.67 = (bf16[32,2,16,128]{3,2,1,0:T(8,128)(2,1)S(1)}, bf16[32,2,16,128]{3,2,1,0:T(8,128)(2,1)S(1)}, bf16[32,2,16,128]{3,2,1,0:T(8,128)(2,1)S(1)}, bf16[32,2,16,128]{3,2,1,0:T(8,128)(2,1)S(1)}) custom-call(bf16[16,4,48,128]{3,2,1,0:T(8,128)(2,1)S(1)} %copy-done.1), custom_call_target="tpu_custom_call" | custom-call | bytes 2359296 | tf_op jit(solution)/shard_map/pallas_call | solution.py:19
  3.3 3.0 %collective-permute-start.1 = (bf16[32,2,16,128]{3,2,1,0:T(8,128)(2,1)S(1)}, bf16[32,2,16,128]{3,2,1,0:T(8,128)(2,1)S(1)}, u32[]{:S(2)}, u32[]{:S(2)}) collective-permute-start(bf16[32,2,16,128]{3,2,1,0:T(8,128)(2,1)S(1)} %get-tuple-element.33), channel_id=1, source_target_pairs={{0,1},{1,0},{2,3},{3,2},{4,5},{5,4},{6,7},{7,6},{8,9},{9,8},{10,11... | collective-permute-start | bytes 786440 | tf_op jit(solution)/shard_map/ppermute | solution.py:439
  6.3 3.7 %collective-permute-start.4 = (bf16[32,2,16,128]{3,2,1,0:T(8,128)(2,1)S(1)}, bf16[32,2,16,128]{3,2,1,0:T(8,128)(2,1)S(1)}, u32[]{:S(2)}, u32[]{:S(2)}) collective-permute-start(bf16[32,2,16,128]{3,2,1,0:T(8,128)(2,1)S(1)} %get-tuple-element.34.after.refs_2_.refs_11_), channel_id=1, source_target_pairs={{2,0},{4,2},{6,4},{8,6},{10,8},{12,10},{14,12},{16,14},{18,16},{20... | collective-permute-start | bytes 786440 | tf_op jit(solution)/shard_map/ppermute | solution.py:445
  10.0 0.5 collective-permute-start.3
  10.5 0.0 collective-permute-start
  10.5 0.0 copy-start.2
  10.5 0.9 %copy-done.2 = bf16[16,27,32]{2,0,1:T(8,128)(2,1)S(1)} copy-done((bf16[16,27,32]{2,0,1:T(8,128)(2,1)S(1)}, bf16[16,27,32]{2,0,1:T(8,128)(2,1)}, u32[]{:S(2)}) %copy-start.2) | copy-done | bytes 27672
  11.4 0.0 copy-start.3
  11.4 0.9 %copy-done.3 = bf16[16,27,32]{2,0,1:T(8,128)(2,1)S(1)} copy-done((bf16[16,27,32]{2,0,1:T(8,128)(2,1)S(1)}, bf16[16,27,32]{2,0,1:T(8,128)(2,1)}, u32[]{:S(2)}) %copy-start.3) | copy-done | bytes 27672
  12.3 0.1 shard_map.68.after.refs_0_
  12.4 0.0 copy-start
  12.4 1.4 %copy-done = bf16[32,4,48,128]{3,2,1,0:T(8,128)(2,1)S(1)} copy-done((bf16[32,4,48,128]{3,2,1,0:T(8,128)(2,1)S(1)}, bf16[32,4,48,128]{3,2,1,0:T(8,128)(2,1)}, u32[]{:S(2)}) %copy-start) | copy-done | bytes 1572888
  13.8 1.3 %shard_map.69 = (bf16[28,2,32,128]{3,2,1,0:T(8,128)(2,1)S(1)}, bf16[28,2,32,128]{3,2,1,0:T(8,128)(2,1)S(1)}) custom-call(bf16[14,16,128]{2,1,0:T(8,128)(2,1)S(1)} %shard_map.68.after.refs_0_, bf16[32,4,48,128]{3,2,1,0:T(8,128)(2,1)S(1)} %copy-done), custom_call_target="tpu_custom_call" | custom-call | bytes 3145728 | tf_op jit(solution)/shard_map/pallas_call | solution.py:19
  15.1 0.0 collective-permute-done.1.refs_0_
  15.2 0.1 collective-permute-start.2
  15.2 1.6 %collective-permute-start.5 = (bf16[14,16,128]{2,1,0:T(8,128)(2,1)S(1)}, bf16[14,16,128]{2,1,0:T(8,128)(2,1)S(1)}, u32[]{:S(2)}, u32[]{:S(2)}) collective-permute-start(bf16[14,16,128]{2,1,0:T(8,128)(2,1)S(1)} %shard_map.68.after.refs_0_), channel_id=1, source_target_pairs={{0,1},{1,0},{2,3},{3,2},{4,5},{5,4},{6,7},{7,6},{8,9},{9,8},{10,11... | collective-permute-start | bytes 172040 | tf_op jit(solution)/shard_map/ppermute | solution.py:439
  16.8 2.7 %collective-permute-done.5.refs_2_.refs_1_ = bf16[14,16,128]{2,1,0:T(8,128)(2,1)S(1)} collective-permute-done((bf16[14,16,128]{2,1,0:T(8,128)(2,1)S(1)}, bf16[14,16,128]{2,1,0:T(8,128)(2,1)S(1)}, u32[]{:S(2)}, u32[]{:S(2)}) %collective-permute-start.5) | collective-permute-done | bytes 57376 | tf_op jit(solution)/shard_map/ppermute | solution.py:439
  19.5 0.0 collective-permute-done.4.refs_1_.refs_2_.refs_15_
  19.5 0.0 collective-permute-done.3.refs_0_
  19.5 3.9 %collective-permute-start.6 = (bf16[32,2,16,128]{3,2,1,0:T(8,128)(2,1)S(1)}, bf16[32,2,16,128]{3,2,1,0:T(8,128)(2,1)S(1)}, u32[]{:S(2)}, u32[]{:S(2)}) collective-permute-start(bf16[32,2,16,128]{3,2,1,0:T(8,128)(2,1)S(1)} %shard_map.71.refs_3_.refs_12_), channel_id=1, source_target_pairs={{2,0},{4,2},{6,4},{8,6},{10,8},{12,10},{14,12},{16,14},{18,16},{20... | collective-permute-start | bytes 786440 | tf_op jit(solution)/shard_map/ppermute | solution.py:445
  23.4 0.5 shard_map.72
  23.9 0.0 collective-permute-done.refs_0_.refs_9_
  23.9 0.0 collective-permute-done.2.refs_1_.refs_10_
  23.9 3.6 %shard_map.73 = (bf16[30,2,32,128]{3,2,1,0:T(8,128)(2,1)S(1)}, bf16[30,2,32,128]{3,2,1,0:T(8,128)(2,1)S(1)}, bf16[30,2,32,128]{3,2,1,0:T(8,128)(2,1)S(1)}, bf16[...) custom-call(bf16[32,2,16,128]{3,2,1,0:T(8,128)(2,1)S(1)} %collective-permute-done.refs_0_.refs_9_, ...), custom_call_target="tpu_custom_call" | custom-call | flops 1019215872 | bytes 3145728 | tf_op jit(solution)/shard_map/pallas_call | solution.py:19
  27.5 0.0 collective-permute-done.6.refs_3_.refs_16_
  27.6 2.8 %shard_map.74 = (bf16[30,2,32,128]{3,2,1,0:T(8,128)(2,1)S(1)}, bf16[30,2,32,128]{3,2,1,0:T(8,128)(2,1)S(1)}, bf16[28,2,32,128]{3,2,1,0:T(8,128)(2,1)S(1)}) custom-call(bf16[32,2,16,128]{3,2,1,0:T(8,128)(2,1)S(1)} %get-tuple-element.32.refs_4_.refs_0_.refs_13_, bf16[32,2,16,128]{3,2,1,0:T(8,128)(2,1)S(1)} %shard_map.70.refs_5_.refs_1_.refs_14_, ...), custom_call_target="tpu_custom_call" | custom-call | flops 679477248 | bytes 2359296 | tf_op jit(solution)/shard_map/pallas_call | solution.py:19
  30.3 0.1 collective-permute-start.8
  30.4 4.4 %collective-permute-start.9 = (bf16[28,2,32,128]{3,2,1,0:T(8,128)(2,1)S(1)}, bf16[28,2,32,128]{3,2,1,0:T(8,128)(2,1)S(1)}, u32[]{:S(2)}, u32[]{:S(2)}) collective-permute-start(bf16[28,2,32,128]{3,2,1,0:T(8,128)(2,1)S(1)} %get-tuple-element.43.refs_3_), channel_id=1, source_target_pairs={{2,0},{4,2},{6,4},{8,6},{10,8},{12,10},{14,12},{16,14},{18,16},{20... | collective-permute-start | bytes 1376264 | tf_op jit(solution)/shard_map/ppermute | solution.py:445
  34.8 8.3 %shard_map.75 = (f32[2,7,16,128]{3,2,1,0:T(8,128)S(1)}, f32[2,7,16,128]{3,2,1,0:T(8,128)S(1)}, bf16[26,2,32,128]{3,2,1,0:T(8,128)(2,1)S(1)}) custom-call(bf16[30,2,32,128]{3,2,1,0:T(8,128)(2,1)S(1)} %get-tuple-element.39.refs_0_, bf16[30,2,32,128]{3,2,1,0:T(8,128)(2,1)S(1)} %get-tuple-element.40.refs_4_.refs_1_, ...), custom_call_target="tpu_custom_call" | custom-call | tf_op jit(solution)/shard_map/pallas_call | solution.py:19
  43.1 0.1 collective-permute-start.7
  43.2 1.3 %collective-permute-done.7.two = f32[2,7,16,128]{3,2,1,0:T(8,128)S(1)} collective-permute-done((f32[2,7,16,128]{3,2,1,0:T(8,128)S(1)}, f32[2,7,16,128]{3,2,1,0:T(8,128)S(1)}, u32[]{:S(2)}, u32[]{:S(2)}) %collective-permute-start.7) | collective-permute-done | bytes 114720 | tf_op jit(solution)/shard_map/ppermute | solution.py:555
  44.5 1.6 %collective-permute-start.10 = (f32[7,16,128]{2,1,0:T(8,128)S(1)}, f32[7,16,128]{2,1,0:T(8,128)S(1)}, u32[]{:S(2)}, u32[]{:S(2)}) collective-permute-start(f32[7,16,128]{2,1,0:T(8,128)S(1)} %get-tuple-element.56), channel_id=1, source_target_pairs={{0,1},{1,0},{2,3},{3,2},{4,5},{5,4},{6,7},{7,6},{8,9},{9,8},{10,11... | collective-permute-start | bytes 172040 | tf_op jit(solution)/shard_map/ppermute | solution.py:439
  46.1 0.0 collective-permute-start.12
  46.1 2.0 %collective-permute-start.11 = (f32[7,16,128]{2,1,0:T(8,128)S(1)}, f32[7,16,128]{2,1,0:T(8,128)S(1)}, u32[]{:S(2)}, u32[]{:S(2)}) collective-permute-start(f32[7,16,128]{2,1,0:T(8,128)S(1)} %get-tuple-element.51.after.refs_1_), channel_id=1, source_target_pairs={{0,4},{2,6},{4,0},{6,2},{8,12},{10,14},{12,8},{14,10},{16,20},{18,... | collective-permute-start | bytes 172040 | tf_op jit(solution)/shard_map/ppermute | solution.py:555
  48.1 0.0 collective-permute-done.8.refs_2_
  48.1 0.0 collective-permute-done.9.refs_5_
  48.1 3.3 %shard_map.77 = (bf16[24,4,16,128]{3,2,1,0:T(8,128)(2,1)S(1)}, bf16[24,4,16,128]{3,2,1,0:T(8,128)(2,1)S(1)}) custom-call(f32[7,16,128]{2,1,0:T(8,128)S(1)} %get-tuple-element.51.after.refs_1_, bf16[192,384]{1,0:T(8,128)(2,1)S(1)} %get-tuple-element.45.refs_5_.refs_0_, bf16[192,384]{1,0:T(8,128)(2,1)S(1)} %get-tuple-element.52.refs_1_, ...), custom_call_target="tpu_custom_call" | custom-call | flops 1358954496 | bytes 2359296 | tf_op jit(solution)/shard_map/pallas_call | solution.py:19
  51.4 0.0 collective-permute-done.10.refs_2_
  51.4 0.0 collective-permute-done.11.refs_3_
  51.4 0.0 collective-permute-done.12.refs_4_
  51.5 1.6 %collective-permute-start.13 = (bf16[24,4,16,128]{3,2,1,0:T(8,128)(2,1)S(1)}, bf16[24,4,16,128]{3,2,1,0:T(8,128)(2,1)S(1)}, u32[]{:S(2)}, u32[]{:S(2)}) collective-permute-start(bf16[24,4,16,128]{3,2,1,0:T(8,128)(2,1)S(1)} %shard_map.79), channel_id=1, source_target_pairs={{0,1},{1,0},{2,3},{3,2},{4,5},{5,4},{6,7},{7,6},{8,9},{9,8},{10,11... | collective-permute-start | bytes 1179656 | tf_op jit(solution)/shard_map/ppermute | solution.py:439
  53.1 0.0 collective-permute-start.14
  53.1 0.6 collective-permute-start.15
  53.6 3.8 %collective-permute-start.16 = (f32[7,16,128]{2,1,0:T(8,128)S(1)}, f32[7,16,128]{2,1,0:T(8,128)S(1)}, u32[]{:S(2)}, u32[]{:S(2)}) collective-permute-start(f32[7,16,128]{2,1,0:T(8,128)S(1)} %shard_map.78.refs_1_.refs_0_), channel_id=1, source_target_pairs={{0,24},{2,26},{4,28},{6,30},{8,16},{10,18},{12,20},{14,22},{16,8},... | collective-permute-start | bytes 172040 | tf_op jit(solution)/shard_map/ppermute | solution.py:555
  57.5 0.0 collective-permute-done.14.refs_1_
  57.5 1.2 %collective-permute-done.15.refs_2_ = f32[7,16,128]{2,1,0:T(8,128)S(1)} collective-permute-done((f32[7,16,128]{2,1,0:T(8,128)S(1)}, f32[7,16,128]{2,1,0:T(8,128)S(1)}, u32[]{:S(2)}, u32[]{:S(2)}) %collective-permute-start.15) | collective-permute-done | bytes 57376 | tf_op jit(solution)/shard_map/ppermute | solution.py:555
  58.7 1.7 %collective-permute-done.16.refs_3_ = f32[7,16,128]{2,1,0:T(8,128)S(1)} collective-permute-done((f32[7,16,128]{2,1,0:T(8,128)S(1)}, f32[7,16,128]{2,1,0:T(8,128)S(1)}, u32[]{:S(2)}, u32[]{:S(2)}) %collective-permute-start.16) | collective-permute-done | bytes 57376 | tf_op jit(solution)/shard_map/ppermute | solution.py:555
  60.4 0.1 collective-permute-start.17
  60.4 1.4 %collective-permute-done.13.refs_1_ = bf16[24,4,16,128]{3,2,1,0:T(8,128)(2,1)S(1)} collective-permute-done((bf16[24,4,16,128]{3,2,1,0:T(8,128)(2,1)S(1)}, bf16[24,4,16,128]{3,2,1,0:T(8,128)(2,1)S(1)}, u32[]{:S(2)}, u32[]{:S(2)}) %collective-permute-start.13) | collective-permute-done | bytes 393248 | tf_op jit(solution)/shard_map/ppermute | solution.py:439
  61.9 1.9 %shard_map.80 = (f32[8,128]{1,0:T(8,128)S(1)}, bf16[16,4,48,128]{3,2,1,0:T(8,128)(2,1)}) custom-call(bf16[24,4,16,128]{3,2,1,0:T(8,128)(2,1)S(1)} %get-tuple-element.54.refs_0_, bf16[24,4,16,128]{3,2,1,0:T(8,128)(2,1)S(1)} %collective-permute-done.13.refs_1_), custom_call_target="tpu_custom_call" | custom-call | bytes 1572864 | tf_op jit(solution)/shard_map/pallas_call | solution.py:19
  63.8 0.0 collective-permute-done.17.other
  63.8 0.9 %shard_map.82 = (f32[27,16,32]{2,1,0:T(8,128)}, f32[27,16,32]{2,1,0:T(8,128)}) custom-call(f32[8,128]{1,0:T(8,128)S(1)} %get-tuple-element.58.after, f32[7,16,128]{2,1,0:T(8,128)S(1)} %shard_map.81.mine, f32[7,16,128]{2,1,0:T(8,128)S(1)} %collective-permute-done.17.other), custom_call_target="tpu_custom_call" | custom-call | tf_op jit(solution)/shard_map/pallas_call | solution.py:19
  (6 shorter events, 0.1 us)
Async XLA Ops:
  0.6 1.1 %copy-start.1 = (bf16[16,4,48,128]{3,2,1,0:T(8,128)(2,1)S(1)}, bf16[16,4,48,128]{3,2,1,0:T(8,128)(2,1)}, u32[]{:S(2)}) copy-start(bf16[16,4,48,128]{3,2,1,0:T(8,128)(2,1)} %x_ref.2) | copy-start | bytes 2359300
  3.3 11.9 %collective-permute-start.1 = (bf16[32,2,16,128]{3,2,1,0:T(8,128)(2,1)S(1)}, bf16[32,2,16,128]{3,2,1,0:T(8,128)(2,1)S(1)}, u32[]{:S(2)}, u32[]{:S(2)}) collective-permute-start(bf16[32,2,16,128]{3,2,1,0:T(8,128)(2,1)S(1)} %get-tuple-element.33), channel_id=1, source_target_pairs={{0,1},{1,0},{2,3},{3,2},{4,5},{5,4},{6,7},{7,6},{8,9},{9,8},{10,11... | collective-permute-start | bytes 786440 | tf_op jit(solution)/shard_map/ppermute | solution.py:439
  6.3 13.2 %collective-permute-start.4 = (bf16[32,2,16,128]{3,2,1,0:T(8,128)(2,1)S(1)}, bf16[32,2,16,128]{3,2,1,0:T(8,128)(2,1)S(1)}, u32[]{:S(2)}, u32[]{:S(2)}) collective-permute-start(bf16[32,2,16,128]{3,2,1,0:T(8,128)(2,1)S(1)} %get-tuple-element.34.after.refs_2_.refs_11_), channel_id=1, source_target_pairs={{2,0},{4,2},{6,4},{8,6},{10,8},{12,10},{14,12},{16,14},{18,16},{20... | collective-permute-start | bytes 786440 | tf_op jit(solution)/shard_map/ppermute | solution.py:445
  10.0 9.5 %collective-permute-start.3 = (bf16[32,2,16,128]{3,2,1,0:T(8,128)(2,1)S(1)}, bf16[32,2,16,128]{3,2,1,0:T(8,128)(2,1)S(1)}, u32[]{:S(2)}, u32[]{:S(2)}) collective-permute-start(bf16[32,2,16,128]{3,2,1,0:T(8,128)(2,1)S(1)} %get-tuple-element.36), channel_id=1, source_target_pairs={{0,1},{1,0},{2,3},{3,2},{4,5},{5,4},{6,7},{7,6},{8,9},{9,8},{10,11... | collective-permute-start | bytes 786440 | tf_op jit(solution)/shard_map/ppermute | solution.py:439
  10.5 13.4 %collective-permute-start = (bf16[32,2,16,128]{3,2,1,0:T(8,128)(2,1)S(1)}, bf16[32,2,16,128]{3,2,1,0:T(8,128)(2,1)S(1)}, u32[]{:S(2)}, u32[]{:S(2)}) collective-permute-start(bf16[32,2,16,128]{3,2,1,0:T(8,128)(2,1)S(1)} %get-tuple-element.32.refs_4_.refs_0_.refs_13_), channel_id=1, source_target_pairs={{0,2},{2,4},{4,6},{6,8},{8,10},{10,12},{12,14},{14,16},{16,18},{18... | collective-permute-start | bytes 786440 | tf_op jit(solution)/shard_map/ppermute | solution.py:442
  10.5 0.9 %copy-start.2 = (bf16[16,27,32]{2,0,1:T(8,128)(2,1)S(1)}, bf16[16,27,32]{2,0,1:T(8,128)(2,1)}, u32[]{:S(2)}) copy-start(bf16[16,27,32]{2,0,1:T(8,128)(2,1)} %param.6) | copy-start | bytes 82948
  11.4 0.9 %copy-start.3 = (bf16[16,27,32]{2,0,1:T(8,128)(2,1)S(1)}, bf16[16,27,32]{2,0,1:T(8,128)(2,1)}, u32[]{:S(2)}) copy-start(bf16[16,27,32]{2,0,1:T(8,128)(2,1)} %param.7) | copy-start | bytes 82948
  12.4 1.4 %copy-start = (bf16[32,4,48,128]{3,2,1,0:T(8,128)(2,1)S(1)}, bf16[32,4,48,128]{3,2,1,0:T(8,128)(2,1)}, u32[]{:S(2)}) copy-start(bf16[32,4,48,128]{3,2,1,0:T(8,128)(2,1)} %x_ref.3) | copy-start | bytes 4718596
  15.2 8.8 %collective-permute-start.2 = (bf16[32,2,16,128]{3,2,1,0:T(8,128)(2,1)S(1)}, bf16[32,2,16,128]{3,2,1,0:T(8,128)(2,1)S(1)}, u32[]{:S(2)}, u32[]{:S(2)}) collective-permute-start(bf16[32,2,16,128]{3,2,1,0:T(8,128)(2,1)S(1)} %shard_map.70.refs_5_.refs_1_.refs_14_), channel_id=1, source_target_pairs={{0,2},{2,4},{4,6},{6,8},{8,10},{10,12},{12,14},{14,16},{16,18},{18... | collective-permute-start | bytes 786440 | tf_op jit(solution)/shard_map/ppermute | solution.py:442
  15.2 4.2 %collective-permute-start.5 = (bf16[14,16,128]{2,1,0:T(8,128)(2,1)S(1)}, bf16[14,16,128]{2,1,0:T(8,128)(2,1)S(1)}, u32[]{:S(2)}, u32[]{:S(2)}) collective-permute-start(bf16[14,16,128]{2,1,0:T(8,128)(2,1)S(1)} %shard_map.68.after.refs_0_), channel_id=1, source_target_pairs={{0,1},{1,0},{2,3},{3,2},{4,5},{5,4},{6,7},{7,6},{8,9},{9,8},{10,11... | collective-permute-start | bytes 172040 | tf_op jit(solution)/shard_map/ppermute | solution.py:439
  19.5 8.1 %collective-permute-start.6 = (bf16[32,2,16,128]{3,2,1,0:T(8,128)(2,1)S(1)}, bf16[32,2,16,128]{3,2,1,0:T(8,128)(2,1)S(1)}, u32[]{:S(2)}, u32[]{:S(2)}) collective-permute-start(bf16[32,2,16,128]{3,2,1,0:T(8,128)(2,1)S(1)} %shard_map.71.refs_3_.refs_12_), channel_id=1, source_target_pairs={{2,0},{4,2},{6,4},{8,6},{10,8},{12,10},{14,12},{16,14},{18,16},{20... | collective-permute-start | bytes 786440 | tf_op jit(solution)/shard_map/ppermute | solution.py:445
  30.3 17.7 %collective-permute-start.8 = (bf16[28,2,32,128]{3,2,1,0:T(8,128)(2,1)S(1)}, bf16[28,2,32,128]{3,2,1,0:T(8,128)(2,1)S(1)}, u32[]{:S(2)}, u32[]{:S(2)}) collective-permute-start(bf16[28,2,32,128]{3,2,1,0:T(8,128)(2,1)S(1)} %get-tuple-element.44.refs_4_), channel_id=1, source_target_pairs={{0,2},{2,4},{4,6},{6,8},{8,10},{10,12},{12,14},{14,16},{16,18},{18... | collective-permute-start | bytes 1376264 | tf_op jit(solution)/shard_map/ppermute | solution.py:442
  30.4 17.7 %collective-permute-start.9 = (bf16[28,2,32,128]{3,2,1,0:T(8,128)(2,1)S(1)}, bf16[28,2,32,128]{3,2,1,0:T(8,128)(2,1)S(1)}, u32[]{:S(2)}, u32[]{:S(2)}) collective-permute-start(bf16[28,2,32,128]{3,2,1,0:T(8,128)(2,1)S(1)} %get-tuple-element.43.refs_3_), channel_id=1, source_target_pairs={{2,0},{4,2},{6,4},{8,6},{10,8},{12,10},{14,12},{16,14},{18,16},{20... | collective-permute-start | bytes 1376264 | tf_op jit(solution)/shard_map/ppermute | solution.py:445
  43.1 1.4 %collective-permute-start.7 = (f32[2,7,16,128]{3,2,1,0:T(8,128)S(1)}, f32[2,7,16,128]{3,2,1,0:T(8,128)S(1)}, u32[]{:S(2)}, u32[]{:S(2)}) collective-permute-start(f32[2,7,16,128]{3,2,1,0:T(8,128)S(1)} %get-tuple-element.50), channel_id=1, source_target_pairs={{0,2},{2,0},{4,6},{6,4},{8,10},{10,8},{12,14},{14,12},{16,18},{18,... | collective-permute-start | bytes 344072 | tf_op jit(solution)/shard_map/ppermute | solution.py:555
  44.5 6.9 %collective-permute-start.10 = (f32[7,16,128]{2,1,0:T(8,128)S(1)}, f32[7,16,128]{2,1,0:T(8,128)S(1)}, u32[]{:S(2)}, u32[]{:S(2)}) collective-permute-start(f32[7,16,128]{2,1,0:T(8,128)S(1)} %get-tuple-element.56), channel_id=1, source_target_pairs={{0,1},{1,0},{2,3},{3,2},{4,5},{5,4},{6,7},{7,6},{8,9},{9,8},{10,11... | collective-permute-start | bytes 172040 | tf_op jit(solution)/shard_map/ppermute | solution.py:439
  46.1 5.3 %collective-permute-start.12 = (f32[7,16,128]{2,1,0:T(8,128)S(1)}, f32[7,16,128]{2,1,0:T(8,128)S(1)}, u32[]{:S(2)}, u32[]{:S(2)}) collective-permute-start(f32[7,16,128]{2,1,0:T(8,128)S(1)} %get-tuple-element.56), channel_id=1, source_target_pairs={{0,5},{1,4},{2,7},{3,6},{4,1},{5,0},{6,3},{7,2},{8,13},{9,12},{10,... | collective-permute-start | bytes 172040 | tf_op jit(solution)/shard_map/ppermute | solution.py:561
  46.1 5.3 %collective-permute-start.11 = (f32[7,16,128]{2,1,0:T(8,128)S(1)}, f32[7,16,128]{2,1,0:T(8,128)S(1)}, u32[]{:S(2)}, u32[]{:S(2)}) collective-permute-start(f32[7,16,128]{2,1,0:T(8,128)S(1)} %get-tuple-element.51.after.refs_1_), channel_id=1, source_target_pairs={{0,4},{2,6},{4,0},{6,2},{8,12},{10,14},{12,8},{14,10},{16,20},{18,... | collective-permute-start | bytes 172040 | tf_op jit(solution)/shard_map/ppermute | solution.py:555
  51.5 10.4 %collective-permute-start.13 = (bf16[24,4,16,128]{3,2,1,0:T(8,128)(2,1)S(1)}, bf16[24,4,16,128]{3,2,1,0:T(8,128)(2,1)S(1)}, u32[]{:S(2)}, u32[]{:S(2)}) collective-permute-start(bf16[24,4,16,128]{3,2,1,0:T(8,128)(2,1)S(1)} %shard_map.79), channel_id=1, source_target_pairs={{0,1},{1,0},{2,3},{3,2},{4,5},{5,4},{6,7},{7,6},{8,9},{9,8},{10,11... | collective-permute-start | bytes 1179656 | tf_op jit(solution)/shard_map/ppermute | solution.py:439
  53.1 4.4 %collective-permute-start.14 = (f32[7,16,128]{2,1,0:T(8,128)S(1)}, f32[7,16,128]{2,1,0:T(8,128)S(1)}, u32[]{:S(2)}, u32[]{:S(2)}) collective-permute-start(f32[7,16,128]{2,1,0:T(8,128)S(1)} %shard_map.78.refs_1_.refs_0_), channel_id=1, source_target_pairs={{0,8},{2,10},{4,12},{6,14},{8,0},{10,2},{12,4},{14,6},{16,24},{18,... | collective-permute-start | bytes 172040 | tf_op jit(solution)/shard_map/ppermute | solution.py:555
  53.1 5.6 %collective-permute-start.15 = (f32[7,16,128]{2,1,0:T(8,128)S(1)}, f32[7,16,128]{2,1,0:T(8,128)S(1)}, u32[]{:S(2)}, u32[]{:S(2)}) collective-permute-start(f32[7,16,128]{2,1,0:T(8,128)S(1)} %shard_map.78.refs_1_.refs_0_), channel_id=1, source_target_pairs={{0,16},{2,18},{4,20},{6,22},{8,24},{10,26},{12,28},{14,30},{16,0},... | collective-permute-start | bytes 172040 | tf_op jit(solution)/shard_map/ppermute | solution.py:555
  53.6 6.7 %collective-permute-start.16 = (f32[7,16,128]{2,1,0:T(8,128)S(1)}, f32[7,16,128]{2,1,0:T(8,128)S(1)}, u32[]{:S(2)}, u32[]{:S(2)}) collective-permute-start(f32[7,16,128]{2,1,0:T(8,128)S(1)} %shard_map.78.refs_1_.refs_0_), channel_id=1, source_target_pairs={{0,24},{2,26},{4,28},{6,30},{8,16},{10,18},{12,20},{14,22},{16,8},... | collective-permute-start | bytes 172040 | tf_op jit(solution)/shard_map/ppermute | solution.py:555
  60.4 3.4 %collective-permute-start.17 = (f32[7,16,128]{2,1,0:T(8,128)S(1)}, f32[7,16,128]{2,1,0:T(8,128)S(1)}, u32[]{:S(2)}, u32[]{:S(2)}) collective-permute-start(f32[7,16,128]{2,1,0:T(8,128)S(1)} %shard_map.81.mine), channel_id=1, source_target_pairs={{0,2},{2,0},{4,6},{6,4},{8,10},{10,8},{12,14},{14,12},{16,18},{18,... | collective-permute-start | bytes 172040 | tf_op jit(solution)/shard_map/ppermute | solution.py:555

commit v13 on v12

--- a/solution.py
+++ b/solution.py
@@ -29,9 +29,7 @@
 
 
 def in_blocks(count, body):
-    block = max(k for k in range(1, 8) if count % k == 0)
-    if block < 4:
-        block = min(count, 15)
+    block = max(k for k in range(1, 17) if count % k == 0)
 
     def several(r, _):
         for k in range(block):
@@ -243,13 +241,14 @@
                     wide = delta[delta_row + row + q, place]
                     depth = wide.shape[1]
                     rows += [pltpu.roll(wide, depth - 1, 1), wide, pltpu.roll(wide, 1, 1)]
-                left.append(jnp.concatenate(rows, axis=0))
+                    rows.append(jnp.zeros_like(wide))
+                right.append(jnp.concatenate(rows, axis=0))
                 rows = []
                 for refs, side in pieces[x : x + 3]:
                     for b in range(4):
                         for ref in refs:
                             rows.append(ref[first_row + row + b, side])
-                right.append(jnp.concatenate(rows, axis=0))
+                left.append(jnp.concatenate(rows, axis=0))
         total[...] += lax.dot_general(
             jnp.concatenate(left, axis=1),
             jnp.concatenate(right, axis=1),
@@ -262,9 +261,9 @@
 
 
 def weight_fold(total, size):
-    lanes = total.shape[0] // 2
-    channels = total.shape[1] // 12
-    upper, lower = total[:lanes, :].T, total[lanes:, :].T
+    lanes = total.shape[1] // 2
+    channels = total.shape[0] // 12
+    upper, lower = total[:, :lanes], total[:, lanes:]
     groups = []
     for g in range(channels // size):
         taps_of = []
@@ -532,7 +531,7 @@
 
     raw = jax.ShapeDtypeStruct((extent, 7, size, 4 * channels), F32)
     portion = jax.ShapeDtypeStruct(raw.shape[1:], F32)
-    total = pltpu.VMEM((6 * channels, 12 * channels), F32)
+    total = pltpu.VMEM((12 * channels, 8 * channels), F32)
 
     def room(rows_each):
         return pltpu.VMEM((rows_each, 2, channels, depth), BF16)

time: 64.9 us -> 63.3 us (0.975)
  Pallas kernels: 24.3 us -> 21.5 us
  waiting for transfers between devices: 8.35 us -> 9.54 us
    pallas_call x16, Pallas kernels: 24.3 us -> 21.5 us  [call(): pl.pallas_call(kernel, out_shape=outs, in_specs=[still] * loose + [whole]...]
    ppermute x3, waiting for transfers between devices: 0.01 us -> 0.73 us  [to_prev(): lax.ppermute(value, 'slab', [((i + 1) % slabs, i) for i in range(slabs)])]
  transfers between devices with their start and end apart: 18 -> 18, of which waited for: 5 -> 7; matrix products, arithmetic and copies ran while one was open for 0% -> 0% of each run, Pallas kernels for 30% -> 28%
where the time goes in v13:
time: 63.3 us; the launch traced here: 63 us
  starting transfers between devices  26.9 us (42%)
  Pallas kernels  21.5 us (34%)
  waiting for transfers between devices  9.54 us (15%)
  local copies, waits for them, and re-layouts  4.32 us (7%)
  between operations  0.81 us (1%)
    pallas_call x16, Pallas kernels, call(): pl.pallas_call(kernel, out_shape=outs, in_specs=[still] * loose + [whole]...  21.5 us
    ppermute x3, starting transfers between devices, to_prev(): lax.ppermute(value, 'slab', [((i + 1) % slabs, i) for i in range(slabs)])  12.4 us
    ppermute x5, starting transfers between devices, to_chan(): lax.ppermute(value, 'chan', [(i, (i + shift) % extent) for i in range(ext...  7.87 us
    ppermute x6, starting transfers between devices, stepped(): return lax.ppermute(value, 'slab', [(i, i ^ stride) for i in range(slabs)])  6.53 us
    ppermute x6, waiting for transfers between devices, stepped(): return lax.ppermute(value, 'slab', [(i, i ^ stride) for i in range(slabs)])  4.56 us
    unnamed x8, local copies, waits for them, and re-layouts  4.32 us
    ppermute x5, waiting for transfers between devices, to_chan(): lax.ppermute(value, 'chan', [(i, (i + shift) % extent) for i in range(ext...  4.23 us
  transfers between devices with their start and end apart: 18, of which 7 were waited for; matrix products, arithmetic and copies ran while one was open for 0% of the time, Pallas kernels for 28%

profile of v13, /device:TPU:0, one launch (start us, length us, event | category | flops | bytes accessed | tf_op | source)
XLA Modules:
  0.0 63.0 jit_solution(1953597990658332621)
XLA Ops:
  0.6 0.0 copy-start.1
  0.6 1.1 %copy-done.1 = bf16[16,4,48,128]{3,2,1,0:T(8,128)(2,1)S(1)} copy-done((bf16[16,4,48,128]{3,2,1,0:T(8,128)(2,1)S(1)}, bf16[16,4,48,128]{3,2,1,0:T(8,128)(2,1)}, u32[]{:S(2)}) %copy-start.1) | copy-done | bytes 786456
  1.8 1.3 %shard_map.67 = (bf16[32,2,16,128]{3,2,1,0:T(8,128)(2,1)S(1)}, bf16[32,2,16,128]{3,2,1,0:T(8,128)(2,1)S(1)}, bf16[32,2,16,128]{3,2,1,0:T(8,128)(2,1)S(1)}, bf16[32,2,16,128]{3,2,1,0:T(8,128)(2,1)S(1)}) custom-call(bf16[16,4,48,128]{3,2,1,0:T(8,128)(2,1)S(1)} %copy-done.1), custom_call_target="tpu_custom_call" | custom-call | bytes 2359296 | tf_op jit(solution)/shard_map/pallas_call | solution.py:19
  3.1 3.0 %collective-permute-start.1 = (bf16[32,2,16,128]{3,2,1,0:T(8,128)(2,1)S(1)}, bf16[32,2,16,128]{3,2,1,0:T(8,128)(2,1)S(1)}, u32[]{:S(2)}, u32[]{:S(2)}) collective-permute-start(bf16[32,2,16,128]{3,2,1,0:T(8,128)(2,1)S(1)} %get-tuple-element.33), channel_id=1, source_target_pairs={{0,1},{1,0},{2,3},{3,2},{4,5},{5,4},{6,7},{7,6},{8,9},{9,8},{10,11... | collective-permute-start | bytes 786440 | tf_op jit(solution)/shard_map/ppermute | solution.py:438
  6.1 3.7 %collective-permute-start.4 = (bf16[32,2,16,128]{3,2,1,0:T(8,128)(2,1)S(1)}, bf16[32,2,16,128]{3,2,1,0:T(8,128)(2,1)S(1)}, u32[]{:S(2)}, u32[]{:S(2)}) collective-permute-start(bf16[32,2,16,128]{3,2,1,0:T(8,128)(2,1)S(1)} %get-tuple-element.34.after.refs_2_.refs_11_), channel_id=1, source_target_pairs={{2,0},{4,2},{6,4},{8,6},{10,8},{12,10},{14,12},{16,14},{18,16},{20... | collective-permute-start | bytes 786440 | tf_op jit(solution)/shard_map/ppermute | solution.py:444
  9.8 0.5 collective-permute-start.3
  10.3 0.0 collective-permute-start
  10.3 0.0 copy-start.2
  10.4 0.9 %copy-done.2 = bf16[16,27,32]{2,0,1:T(8,128)(2,1)S(1)} copy-done((bf16[16,27,32]{2,0,1:T(8,128)(2,1)S(1)}, bf16[16,27,32]{2,0,1:T(8,128)(2,1)}, u32[]{:S(2)}) %copy-start.2) | copy-done | bytes 27672
  11.2 0.0 copy-start.3
  11.2 0.9 %copy-done.3 = bf16[16,27,32]{2,0,1:T(8,128)(2,1)S(1)} copy-done((bf16[16,27,32]{2,0,1:T(8,128)(2,1)S(1)}, bf16[16,27,32]{2,0,1:T(8,128)(2,1)}, u32[]{:S(2)}) %copy-start.3) | copy-done | bytes 27672
  12.1 0.1 shard_map.68.after.refs_0_
  12.3 0.0 copy-start
  12.3 1.4 %copy-done = bf16[32,4,48,128]{3,2,1,0:T(8,128)(2,1)S(1)} copy-done((bf16[32,4,48,128]{3,2,1,0:T(8,128)(2,1)S(1)}, bf16[32,4,48,128]{3,2,1,0:T(8,128)(2,1)}, u32[]{:S(2)}) %copy-start) | copy-done | bytes 1572888
  13.7 1.2 %shard_map.69 = (bf16[28,2,32,128]{3,2,1,0:T(8,128)(2,1)S(1)}, bf16[28,2,32,128]{3,2,1,0:T(8,128)(2,1)S(1)}) custom-call(bf16[14,16,128]{2,1,0:T(8,128)(2,1)S(1)} %shard_map.68.after.refs_0_, bf16[32,4,48,128]{3,2,1,0:T(8,128)(2,1)S(1)} %copy-done), custom_call_target="tpu_custom_call" | custom-call | bytes 3145728 | tf_op jit(solution)/shard_map/pallas_call | solution.py:19
  14.9 0.0 collective-permute-done.1.refs_0_
  14.9 0.1 collective-permute-start.2
  15.0 1.6 %collective-permute-start.5 = (bf16[14,16,128]{2,1,0:T(8,128)(2,1)S(1)}, bf16[14,16,128]{2,1,0:T(8,128)(2,1)S(1)}, u32[]{:S(2)}, u32[]{:S(2)}) collective-permute-start(bf16[14,16,128]{2,1,0:T(8,128)(2,1)S(1)} %shard_map.68.after.refs_0_), channel_id=1, source_target_pairs={{0,1},{1,0},{2,3},{3,2},{4,5},{5,4},{6,7},{7,6},{8,9},{9,8},{10,11... | collective-permute-start | bytes 172040 | tf_op jit(solution)/shard_map/ppermute | solution.py:438
  16.6 2.7 %collective-permute-done.5.refs_2_.refs_1_ = bf16[14,16,128]{2,1,0:T(8,128)(2,1)S(1)} collective-permute-done((bf16[14,16,128]{2,1,0:T(8,128)(2,1)S(1)}, bf16[14,16,128]{2,1,0:T(8,128)(2,1)S(1)}, u32[]{:S(2)}, u32[]{:S(2)}) %collective-permute-start.5) | collective-permute-done | bytes 57376 | tf_op jit(solution)/shard_map/ppermute | solution.py:438
  19.3 0.0 collective-permute-done.4.refs_1_.refs_2_.refs_15_
  19.3 0.0 collective-permute-done.3.refs_0_
  19.3 4.0 %collective-permute-start.6 = (bf16[32,2,16,128]{3,2,1,0:T(8,128)(2,1)S(1)}, bf16[32,2,16,128]{3,2,1,0:T(8,128)(2,1)S(1)}, u32[]{:S(2)}, u32[]{:S(2)}) collective-permute-start(bf16[32,2,16,128]{3,2,1,0:T(8,128)(2,1)S(1)} %shard_map.71.refs_3_.refs_12_), channel_id=1, source_target_pairs={{2,0},{4,2},{6,4},{8,6},{10,8},{12,10},{14,12},{16,14},{18,16},{20... | collective-permute-start | bytes 786440 | tf_op jit(solution)/shard_map/ppermute | solution.py:444
  23.3 0.5 shard_map.72
  23.8 0.0 collective-permute-done.refs_0_.refs_9_
  23.8 0.0 collective-permute-done.2.refs_1_.refs_10_
  23.8 2.6 %shard_map.73 = (bf16[30,2,32,128]{3,2,1,0:T(8,128)(2,1)S(1)}, bf16[30,2,32,128]{3,2,1,0:T(8,128)(2,1)S(1)}, bf16[30,2,32,128]{3,2,1,0:T(8,128)(2,1)S(1)}, bf16[...) custom-call(bf16[32,2,16,128]{3,2,1,0:T(8,128)(2,1)S(1)} %collective-permute-done.refs_0_.refs_9_, ...), custom_call_target="tpu_custom_call" | custom-call | flops 1019215872 | bytes 3145728 | tf_op jit(solution)/shard_map/pallas_call | solution.py:19
  26.4 0.7 %collective-permute-done.6.refs_3_.refs_16_ = bf16[32,2,16,128]{3,2,1,0:T(8,128)(2,1)S(1)} collective-permute-done((bf16[32,2,16,128]{3,2,1,0:T(8,128)(2,1)S(1)}, bf16[32,2,16,128]{3,2,1,0:T(8,128)(2,1)S(1)}, u32[]{:S(2)}, u32[]{:S(2)}) %collective-permute-start.6) | collective-permute-done | bytes 262176 | tf_op jit(solution)/shard_map/ppermute | solution.py:444
  27.2 1.8 %shard_map.74 = (bf16[30,2,32,128]{3,2,1,0:T(8,128)(2,1)S(1)}, bf16[30,2,32,128]{3,2,1,0:T(8,128)(2,1)S(1)}, bf16[28,2,32,128]{3,2,1,0:T(8,128)(2,1)S(1)}) custom-call(bf16[32,2,16,128]{3,2,1,0:T(8,128)(2,1)S(1)} %get-tuple-element.32.refs_4_.refs_0_.refs_13_, bf16[32,2,16,128]{3,2,1,0:T(8,128)(2,1)S(1)} %shard_map.70.refs_5_.refs_1_.refs_14_, ...), custom_call_target="tpu_custom_call" | custom-call | flops 679477248 | bytes 2359296 | tf_op jit(solution)/shard_map/pallas_call | solution.py:19
  28.9 0.1 collective-permute-start.8
  29.0 4.7 %collective-permute-start.9 = (bf16[28,2,32,128]{3,2,1,0:T(8,128)(2,1)S(1)}, bf16[28,2,32,128]{3,2,1,0:T(8,128)(2,1)S(1)}, u32[]{:S(2)}, u32[]{:S(2)}) collective-permute-start(bf16[28,2,32,128]{3,2,1,0:T(8,128)(2,1)S(1)} %get-tuple-element.43.refs_3_), channel_id=1, source_target_pairs={{2,0},{4,2},{6,4},{8,6},{10,8},{12,10},{14,12},{16,14},{18,16},{20... | collective-permute-start | bytes 1376264 | tf_op jit(solution)/shard_map/ppermute | solution.py:444
  33.7 8.3 %shard_map.75 = (f32[2,7,16,128]{3,2,1,0:T(8,128)S(1)}, f32[2,7,16,128]{3,2,1,0:T(8,128)S(1)}, bf16[26,2,32,128]{3,2,1,0:T(8,128)(2,1)S(1)}) custom-call(bf16[30,2,32,128]{3,2,1,0:T(8,128)(2,1)S(1)} %get-tuple-element.39.refs_0_, bf16[30,2,32,128]{3,2,1,0:T(8,128)(2,1)S(1)} %get-tuple-element.40.refs_4_.refs_1_, ...), custom_call_target="tpu_custom_call" | custom-call | tf_op jit(solution)/shard_map/pallas_call | solution.py:19
  41.9 0.1 collective-permute-start.7
  42.0 1.3 %collective-permute-done.7.two = f32[2,7,16,128]{3,2,1,0:T(8,128)S(1)} collective-permute-done((f32[2,7,16,128]{3,2,1,0:T(8,128)S(1)}, f32[2,7,16,128]{3,2,1,0:T(8,128)S(1)}, u32[]{:S(2)}, u32[]{:S(2)}) %collective-permute-start.7) | collective-permute-done | bytes 114720 | tf_op jit(solution)/shard_map/ppermute | solution.py:554
  43.4 1.6 %collective-permute-start.10 = (f32[7,16,128]{2,1,0:T(8,128)S(1)}, f32[7,16,128]{2,1,0:T(8,128)S(1)}, u32[]{:S(2)}, u32[]{:S(2)}) collective-permute-start(f32[7,16,128]{2,1,0:T(8,128)S(1)} %get-tuple-element.56), channel_id=1, source_target_pairs={{0,1},{1,0},{2,3},{3,2},{4,5},{5,4},{6,7},{7,6},{8,9},{9,8},{10,11... | collective-permute-start | bytes 172040 | tf_op jit(solution)/shard_map/ppermute | solution.py:438
  44.9 0.0 collective-permute-start.12
  44.9 2.0 %collective-permute-start.11 = (f32[7,16,128]{2,1,0:T(8,128)S(1)}, f32[7,16,128]{2,1,0:T(8,128)S(1)}, u32[]{:S(2)}, u32[]{:S(2)}) collective-permute-start(f32[7,16,128]{2,1,0:T(8,128)S(1)} %get-tuple-element.51.after.refs_1_), channel_id=1, source_target_pairs={{0,4},{2,6},{4,0},{6,2},{8,12},{10,14},{12,8},{14,10},{16,20},{18,... | collective-permute-start | bytes 172040 | tf_op jit(solution)/shard_map/ppermute | solution.py:554
  46.9 0.0 collective-permute-done.8.refs_2_
  46.9 0.0 collective-permute-done.9.refs_5_
  46.9 2.8 %shard_map.77 = (bf16[24,4,16,128]{3,2,1,0:T(8,128)(2,1)S(1)}, bf16[24,4,16,128]{3,2,1,0:T(8,128)(2,1)S(1)}) custom-call(f32[7,16,128]{2,1,0:T(8,128)S(1)} %get-tuple-element.51.after.refs_1_, bf16[192,384]{1,0:T(8,128)(2,1)S(1)} %get-tuple-element.45.refs_5_.refs_0_, bf16[192,384]{1,0:T(8,128)(2,1)S(1)} %get-tuple-element.52.refs_1_, ...), custom_call_target="tpu_custom_call" | custom-call | flops 1358954496 | bytes 2359296 | tf_op jit(solution)/shard_map/pallas_call | solution.py:19
  49.7 0.0 collective-permute-done.10.refs_2_
  49.7 0.4 collective-permute-done.11.refs_3_
  50.1 0.0 collective-permute-done.12.refs_4_
  50.1 1.2 %collective-permute-start.13 = (bf16[24,4,16,128]{3,2,1,0:T(8,128)(2,1)S(1)}, bf16[24,4,16,128]{3,2,1,0:T(8,128)(2,1)S(1)}, u32[]{:S(2)}, u32[]{:S(2)}) collective-permute-start(bf16[24,4,16,128]{3,2,1,0:T(8,128)(2,1)S(1)} %shard_map.79), channel_id=1, source_target_pairs={{0,1},{1,0},{2,3},{3,2},{4,5},{5,4},{6,7},{7,6},{8,9},{9,8},{10,11... | collective-permute-start | bytes 1179656 | tf_op jit(solution)/shard_map/ppermute | solution.py:438
  51.4 0.0 collective-permute-start.14
  51.4 1.2 %collective-permute-start.15 = (f32[7,16,128]{2,1,0:T(8,128)S(1)}, f32[7,16,128]{2,1,0:T(8,128)S(1)}, u32[]{:S(2)}, u32[]{:S(2)}) collective-permute-start(f32[7,16,128]{2,1,0:T(8,128)S(1)} %shard_map.78.refs_1_.refs_0_), channel_id=1, source_target_pairs={{0,16},{2,18},{4,20},{6,22},{8,24},{10,26},{12,28},{14,30},{16,0},... | collective-permute-start | bytes 172040 | tf_op jit(solution)/shard_map/ppermute | solution.py:554
  52.5 3.2 %collective-permute-start.16 = (f32[7,16,128]{2,1,0:T(8,128)S(1)}, f32[7,16,128]{2,1,0:T(8,128)S(1)}, u32[]{:S(2)}, u32[]{:S(2)}) collective-permute-start(f32[7,16,128]{2,1,0:T(8,128)S(1)} %shard_map.78.refs_1_.refs_0_), channel_id=1, source_target_pairs={{0,24},{2,26},{4,28},{6,30},{8,16},{10,18},{12,20},{14,22},{16,8},... | collective-permute-start | bytes 172040 | tf_op jit(solution)/shard_map/ppermute | solution.py:554
  55.8 0.0 collective-permute-done.14.refs_1_
  55.8 1.5 %collective-permute-done.15.refs_2_ = f32[7,16,128]{2,1,0:T(8,128)S(1)} collective-permute-done((f32[7,16,128]{2,1,0:T(8,128)S(1)}, f32[7,16,128]{2,1,0:T(8,128)S(1)}, u32[]{:S(2)}, u32[]{:S(2)}) %collective-permute-start.15) | collective-permute-done | bytes 57376 | tf_op jit(solution)/shard_map/ppermute | solution.py:554
  57.3 1.4 %collective-permute-done.16.refs_3_ = f32[7,16,128]{2,1,0:T(8,128)S(1)} collective-permute-done((f32[7,16,128]{2,1,0:T(8,128)S(1)}, f32[7,16,128]{2,1,0:T(8,128)S(1)}, u32[]{:S(2)}, u32[]{:S(2)}) %collective-permute-start.16) | collective-permute-done | bytes 57376 | tf_op jit(solution)/shard_map/ppermute | solution.py:554
  58.6 0.1 collective-permute-start.17
  58.7 1.5 %collective-permute-done.13.refs_1_ = bf16[24,4,16,128]{3,2,1,0:T(8,128)(2,1)S(1)} collective-permute-done((bf16[24,4,16,128]{3,2,1,0:T(8,128)(2,1)S(1)}, bf16[24,4,16,128]{3,2,1,0:T(8,128)(2,1)S(1)}, u32[]{:S(2)}, u32[]{:S(2)}) %collective-permute-start.13) | collective-permute-done | bytes 393248 | tf_op jit(solution)/shard_map/ppermute | solution.py:438
  60.3 1.9 %shard_map.80 = (f32[8,128]{1,0:T(8,128)S(1)}, bf16[16,4,48,128]{3,2,1,0:T(8,128)(2,1)}) custom-call(bf16[24,4,16,128]{3,2,1,0:T(8,128)(2,1)S(1)} %get-tuple-element.54.refs_0_, bf16[24,4,16,128]{3,2,1,0:T(8,128)(2,1)S(1)} %collective-permute-done.13.refs_1_), custom_call_target="tpu_custom_call" | custom-call | bytes 1572864 | tf_op jit(solution)/shard_map/pallas_call | solution.py:19
  62.1 0.0 collective-permute-done.17.other
  62.1 0.9 %shard_map.82 = (f32[27,16,32]{2,1,0:T(8,128)}, f32[27,16,32]{2,1,0:T(8,128)}) custom-call(f32[8,128]{1,0:T(8,128)S(1)} %get-tuple-element.58.after, f32[7,16,128]{2,1,0:T(8,128)S(1)} %shard_map.81.mine, f32[7,16,128]{2,1,0:T(8,128)S(1)} %collective-permute-done.17.other), custom_call_target="tpu_custom_call" | custom-call | tf_op jit(solution)/shard_map/pallas_call | solution.py:19
  (6 shorter events, 0.1 us)
Async XLA Ops:
  0.6 1.1 %copy-start.1 = (bf16[16,4,48,128]{3,2,1,0:T(8,128)(2,1)S(1)}, bf16[16,4,48,128]{3,2,1,0:T(8,128)(2,1)}, u32[]{:S(2)}) copy-start(bf16[16,4,48,128]{3,2,1,0:T(8,128)(2,1)} %x_ref.2) | copy-start | bytes 2359300
  3.1 11.8 %collective-permute-start.1 = (bf16[32,2,16,128]{3,2,1,0:T(8,128)(2,1)S(1)}, bf16[32,2,16,128]{3,2,1,0:T(8,128)(2,1)S(1)}, u32[]{:S(2)}, u32[]{:S(2)}) collective-permute-start(bf16[32,2,16,128]{3,2,1,0:T(8,128)(2,1)S(1)} %get-tuple-element.33), channel_id=1, source_target_pairs={{0,1},{1,0},{2,3},{3,2},{4,5},{5,4},{6,7},{7,6},{8,9},{9,8},{10,11... | collective-permute-start | bytes 786440 | tf_op jit(solution)/shard_map/ppermute | solution.py:438
  6.1 13.2 %collective-permute-start.4 = (bf16[32,2,16,128]{3,2,1,0:T(8,128)(2,1)S(1)}, bf16[32,2,16,128]{3,2,1,0:T(8,128)(2,1)S(1)}, u32[]{:S(2)}, u32[]{:S(2)}) collective-permute-start(bf16[32,2,16,128]{3,2,1,0:T(8,128)(2,1)S(1)} %get-tuple-element.34.after.refs_2_.refs_11_), channel_id=1, source_target_pairs={{2,0},{4,2},{6,4},{8,6},{10,8},{12,10},{14,12},{16,14},{18,16},{20... | collective-permute-start | bytes 786440 | tf_op jit(solution)/shard_map/ppermute | solution.py:444
  9.8 9.5 %collective-permute-start.3 = (bf16[32,2,16,128]{3,2,1,0:T(8,128)(2,1)S(1)}, bf16[32,2,16,128]{3,2,1,0:T(8,128)(2,1)S(1)}, u32[]{:S(2)}, u32[]{:S(2)}) collective-permute-start(bf16[32,2,16,128]{3,2,1,0:T(8,128)(2,1)S(1)} %get-tuple-element.36), channel_id=1, source_target_pairs={{0,1},{1,0},{2,3},{3,2},{4,5},{5,4},{6,7},{7,6},{8,9},{9,8},{10,11... | collective-permute-start | bytes 786440 | tf_op jit(solution)/shard_map/ppermute | solution.py:438
  10.3 13.5 %collective-permute-start = (bf16[32,2,16,128]{3,2,1,0:T(8,128)(2,1)S(1)}, bf16[32,2,16,128]{3,2,1,0:T(8,128)(2,1)S(1)}, u32[]{:S(2)}, u32[]{:S(2)}) collective-permute-start(bf16[32,2,16,128]{3,2,1,0:T(8,128)(2,1)S(1)} %get-tuple-element.32.refs_4_.refs_0_.refs_13_), channel_id=1, source_target_pairs={{0,2},{2,4},{4,6},{6,8},{8,10},{10,12},{12,14},{14,16},{16,18},{18... | collective-permute-start | bytes 786440 | tf_op jit(solution)/shard_map/ppermute | solution.py:441
  10.3 0.9 %copy-start.2 = (bf16[16,27,32]{2,0,1:T(8,128)(2,1)S(1)}, bf16[16,27,32]{2,0,1:T(8,128)(2,1)}, u32[]{:S(2)}) copy-start(bf16[16,27,32]{2,0,1:T(8,128)(2,1)} %param.6) | copy-start | bytes 82948
  11.2 0.9 %copy-start.3 = (bf16[16,27,32]{2,0,1:T(8,128)(2,1)S(1)}, bf16[16,27,32]{2,0,1:T(8,128)(2,1)}, u32[]{:S(2)}) copy-start(bf16[16,27,32]{2,0,1:T(8,128)(2,1)} %param.7) | copy-start | bytes 82948
  12.3 1.4 %copy-start = (bf16[32,4,48,128]{3,2,1,0:T(8,128)(2,1)S(1)}, bf16[32,4,48,128]{3,2,1,0:T(8,128)(2,1)}, u32[]{:S(2)}) copy-start(bf16[32,4,48,128]{3,2,1,0:T(8,128)(2,1)} %x_ref.3) | copy-start | bytes 4718596
  14.9 8.9 %collective-permute-start.2 = (bf16[32,2,16,128]{3,2,1,0:T(8,128)(2,1)S(1)}, bf16[32,2,16,128]{3,2,1,0:T(8,128)(2,1)S(1)}, u32[]{:S(2)}, u32[]{:S(2)}) collective-permute-start(bf16[32,2,16,128]{3,2,1,0:T(8,128)(2,1)S(1)} %shard_map.70.refs_5_.refs_1_.refs_14_), channel_id=1, source_target_pairs={{0,2},{2,4},{4,6},{6,8},{8,10},{10,12},{12,14},{14,16},{16,18},{18... | collective-permute-start | bytes 786440 | tf_op jit(solution)/shard_map/ppermute | solution.py:441
  15.0 4.2 %collective-permute-start.5 = (bf16[14,16,128]{2,1,0:T(8,128)(2,1)S(1)}, bf16[14,16,128]{2,1,0:T(8,128)(2,1)S(1)}, u32[]{:S(2)}, u32[]{:S(2)}) collective-permute-start(bf16[14,16,128]{2,1,0:T(8,128)(2,1)S(1)} %shard_map.68.after.refs_0_), channel_id=1, source_target_pairs={{0,1},{1,0},{2,3},{3,2},{4,5},{5,4},{6,7},{7,6},{8,9},{9,8},{10,11... | collective-permute-start | bytes 172040 | tf_op jit(solution)/shard_map/ppermute | solution.py:438
  19.3 7.9 %collective-permute-start.6 = (bf16[32,2,16,128]{3,2,1,0:T(8,128)(2,1)S(1)}, bf16[32,2,16,128]{3,2,1,0:T(8,128)(2,1)S(1)}, u32[]{:S(2)}, u32[]{:S(2)}) collective-permute-start(bf16[32,2,16,128]{3,2,1,0:T(8,128)(2,1)S(1)} %shard_map.71.refs_3_.refs_12_), channel_id=1, source_target_pairs={{2,0},{4,2},{6,4},{8,6},{10,8},{12,10},{14,12},{16,14},{18,16},{20... | collective-permute-start | bytes 786440 | tf_op jit(solution)/shard_map/ppermute | solution.py:444
  28.9 18.0 %collective-permute-start.8 = (bf16[28,2,32,128]{3,2,1,0:T(8,128)(2,1)S(1)}, bf16[28,2,32,128]{3,2,1,0:T(8,128)(2,1)S(1)}, u32[]{:S(2)}, u32[]{:S(2)}) collective-permute-start(bf16[28,2,32,128]{3,2,1,0:T(8,128)(2,1)S(1)} %get-tuple-element.44.refs_4_), channel_id=1, source_target_pairs={{0,2},{2,4},{4,6},{6,8},{8,10},{10,12},{12,14},{14,16},{16,18},{18... | collective-permute-start | bytes 1376264 | tf_op jit(solution)/shard_map/ppermute | solution.py:441
  29.0 17.9 %collective-permute-start.9 = (bf16[28,2,32,128]{3,2,1,0:T(8,128)(2,1)S(1)}, bf16[28,2,32,128]{3,2,1,0:T(8,128)(2,1)S(1)}, u32[]{:S(2)}, u32[]{:S(2)}) collective-permute-start(bf16[28,2,32,128]{3,2,1,0:T(8,128)(2,1)S(1)} %get-tuple-element.43.refs_3_), channel_id=1, source_target_pairs={{2,0},{4,2},{6,4},{8,6},{10,8},{12,10},{14,12},{16,14},{18,16},{20... | collective-permute-start | bytes 1376264 | tf_op jit(solution)/shard_map/ppermute | solution.py:444
  41.9 1.4 %collective-permute-start.7 = (f32[2,7,16,128]{3,2,1,0:T(8,128)S(1)}, f32[2,7,16,128]{3,2,1,0:T(8,128)S(1)}, u32[]{:S(2)}, u32[]{:S(2)}) collective-permute-start(f32[2,7,16,128]{3,2,1,0:T(8,128)S(1)} %get-tuple-element.50), channel_id=1, source_target_pairs={{0,2},{2,0},{4,6},{6,4},{8,10},{10,8},{12,14},{14,12},{16,18},{18,... | collective-permute-start | bytes 344072 | tf_op jit(solution)/shard_map/ppermute | solution.py:554
  43.4 6.4 %collective-permute-start.10 = (f32[7,16,128]{2,1,0:T(8,128)S(1)}, f32[7,16,128]{2,1,0:T(8,128)S(1)}, u32[]{:S(2)}, u32[]{:S(2)}) collective-permute-start(f32[7,16,128]{2,1,0:T(8,128)S(1)} %get-tuple-element.56), channel_id=1, source_target_pairs={{0,1},{1,0},{2,3},{3,2},{4,5},{5,4},{6,7},{7,6},{8,9},{9,8},{10,11... | collective-permute-start | bytes 172040 | tf_op jit(solution)/shard_map/ppermute | solution.py:438
  44.9 5.2 %collective-permute-start.12 = (f32[7,16,128]{2,1,0:T(8,128)S(1)}, f32[7,16,128]{2,1,0:T(8,128)S(1)}, u32[]{:S(2)}, u32[]{:S(2)}) collective-permute-start(f32[7,16,128]{2,1,0:T(8,128)S(1)} %get-tuple-element.56), channel_id=1, source_target_pairs={{0,5},{1,4},{2,7},{3,6},{4,1},{5,0},{6,3},{7,2},{8,13},{9,12},{10,... | collective-permute-start | bytes 172040 | tf_op jit(solution)/shard_map/ppermute | solution.py:560
  44.9 5.2 %collective-permute-start.11 = (f32[7,16,128]{2,1,0:T(8,128)S(1)}, f32[7,16,128]{2,1,0:T(8,128)S(1)}, u32[]{:S(2)}, u32[]{:S(2)}) collective-permute-start(f32[7,16,128]{2,1,0:T(8,128)S(1)} %get-tuple-element.51.after.refs_1_), channel_id=1, source_target_pairs={{0,4},{2,6},{4,0},{6,2},{8,12},{10,14},{12,8},{14,10},{16,20},{18,... | collective-permute-start | bytes 172040 | tf_op jit(solution)/shard_map/ppermute | solution.py:554
  50.1 10.1 %collective-permute-start.13 = (bf16[24,4,16,128]{3,2,1,0:T(8,128)(2,1)S(1)}, bf16[24,4,16,128]{3,2,1,0:T(8,128)(2,1)S(1)}, u32[]{:S(2)}, u32[]{:S(2)}) collective-permute-start(bf16[24,4,16,128]{3,2,1,0:T(8,128)(2,1)S(1)} %shard_map.79), channel_id=1, source_target_pairs={{0,1},{1,0},{2,3},{3,2},{4,5},{5,4},{6,7},{7,6},{8,9},{9,8},{10,11... | collective-permute-start | bytes 1179656 | tf_op jit(solution)/shard_map/ppermute | solution.py:438
  51.4 4.4 %collective-permute-start.14 = (f32[7,16,128]{2,1,0:T(8,128)S(1)}, f32[7,16,128]{2,1,0:T(8,128)S(1)}, u32[]{:S(2)}, u32[]{:S(2)}) collective-permute-start(f32[7,16,128]{2,1,0:T(8,128)S(1)} %shard_map.78.refs_1_.refs_0_), channel_id=1, source_target_pairs={{0,8},{2,10},{4,12},{6,14},{8,0},{10,2},{12,4},{14,6},{16,24},{18,... | collective-permute-start | bytes 172040 | tf_op jit(solution)/shard_map/ppermute | solution.py:554
  51.4 5.9 %collective-permute-start.15 = (f32[7,16,128]{2,1,0:T(8,128)S(1)}, f32[7,16,128]{2,1,0:T(8,128)S(1)}, u32[]{:S(2)}, u32[]{:S(2)}) collective-permute-start(f32[7,16,128]{2,1,0:T(8,128)S(1)} %shard_map.78.refs_1_.refs_0_), channel_id=1, source_target_pairs={{0,16},{2,18},{4,20},{6,22},{8,24},{10,26},{12,28},{14,30},{16,0},... | collective-permute-start | bytes 172040 | tf_op jit(solution)/shard_map/ppermute | solution.py:554
  52.5 6.1 %collective-permute-start.16 = (f32[7,16,128]{2,1,0:T(8,128)S(1)}, f32[7,16,128]{2,1,0:T(8,128)S(1)}, u32[]{:S(2)}, u32[]{:S(2)}) collective-permute-start(f32[7,16,128]{2,1,0:T(8,128)S(1)} %shard_map.78.refs_1_.refs_0_), channel_id=1, source_target_pairs={{0,24},{2,26},{4,28},{6,30},{8,16},{10,18},{12,20},{14,22},{16,8},... | collective-permute-start | bytes 172040 | tf_op jit(solution)/shard_map/ppermute | solution.py:554
  58.6 3.5 %collective-permute-start.17 = (f32[7,16,128]{2,1,0:T(8,128)S(1)}, f32[7,16,128]{2,1,0:T(8,128)S(1)}, u32[]{:S(2)}, u32[]{:S(2)}) collective-permute-start(f32[7,16,128]{2,1,0:T(8,128)S(1)} %shard_map.81.mine), channel_id=1, source_target_pairs={{0,2},{2,0},{4,6},{6,4},{8,10},{10,8},{12,14},{14,12},{16,18},{18,... | collective-permute-start | bytes 172040 | tf_op jit(solution)/shard_map/ppermute | solution.py:554

commit v14 on v13

--- a/solution.py
+++ b/solution.py
@@ -380,7 +380,8 @@
         place(second, first)
 
 
-def split_kernel(one, two, *outs):
+def split_kernel(after, one, two, *outs):
+    del after
     for g, out in enumerate(outs):
         out[...] = one[g] + two[g]
 
@@ -488,8 +489,8 @@
         moved=matrix.size * 8,
     )
     if whole and extent > 1 and pairs > 1:
-        parts[1][-1] = relayed(parts[1][-1], grads[0])
-        parts[1][0] = relayed(parts[1][0], own_after[0], *packs[1:])
+        parts[1][-1] = relayed(parts[1][-1], pack)
+        parts[1][0] = relayed(relayed(parts[1][0], grads[0], *packs[1:]), own_after[0])
     by_pair = [[parts[j][p] for j in range(extent)] for p in range(pairs)]
     groups = extent
     if not whole:
@@ -561,7 +562,9 @@
 
     plain = slabs & (slabs - 1) == 0 and slabs >= 4
     if plain:
-        kept = call(split_kernel, [portion] * extent, [keep, stepped(send, 1)])
+        kept = call(
+            split_kernel, [portion] * extent, [delta_after, keep, stepped(send, 1)], loose=1
+        )
         shares = [kept[0]] + [to_chan(kept[j], extent - j) for j in range(1, extent)]
         shares += [stepped(kept[j], 2, extent - j) for j in range(extent)]
         after = kept[0]

time: 63.3 us -> 61.3 us (0.968)
  starting transfers between devices: 26.9 us -> 24.3 us
  waiting for transfers between devices: 9.54 us -> 11.6 us
  local copies, waits for them, and re-layouts: 4.32 us -> 2.92 us
    ppermute x3, starting transfers between devices: 12.4 us -> 8.99 us  [to_prev(): lax.ppermute(value, 'slab', [((i + 1) % slabs, i) for i in range(slabs)])]
    ppermute x6, waiting for transfers between devices: 4.56 us -> 7.67 us  [stepped(): return lax.ppermute(value, 'slab', [(i, i ^ stride) for i in range(slabs)])]
    unnamed x8, local copies, waits for them, and re-layouts: 4.32 us -> 2.92 us
    ppermute x3, waiting for transfers between devices: 0.73 us -> 0.01 us  [to_prev(): lax.ppermute(value, 'slab', [((i + 1) % slabs, i) for i in range(slabs)])]
    pallas_call x16 -> x17, Pallas kernels: 21.5 us -> 21.5 us  [call(): pl.pallas_call(kernel, out_shape=outs, in_specs=[still] * loose + [whole]...]
  transfers between devices with their start and end apart: 18 -> 18, of which waited for: 7 -> 6; matrix products, arithmetic and copies ran while one was open for 0% -> 0% of each run, Pallas kernels for 28% -> 32%
where the time goes in v14:
time: 61.3 us; the launch traced here: 61 us
  starting transfers between devices  24.3 us (40%)
  Pallas kernels  21.5 us (35%)
  waiting for transfers between devices  11.6 us (19%)
  local copies, waits for them, and re-layouts  2.92 us (5%)
  between operations  0.79 us (1%)
    pallas_call x17, Pallas kernels, call(): pl.pallas_call(kernel, out_shape=outs, in_specs=[still] * loose + [whole]...  21.5 us
    ppermute x3, starting transfers between devices, to_prev(): lax.ppermute(value, 'slab', [((i + 1) % slabs, i) for i in range(slabs)])  8.99 us
    ppermute x5, starting transfers between devices, to_chan(): lax.ppermute(value, 'chan', [(i, (i + shift) % extent) for i in range(ext...  7.91 us
    ppermute x6, waiting for transfers between devices, stepped(): return lax.ppermute(value, 'slab', [(i, i ^ stride) for i in range(slabs)])  7.67 us
    ppermute x6, starting transfers between devices, stepped(): return lax.ppermute(value, 'slab', [(i, i ^ stride) for i in range(slabs)])  7.06 us
    ppermute x5, waiting for transfers between devices, to_chan(): lax.ppermute(value, 'chan', [(i, (i + shift) % extent) for i in range(ext...  3.87 us
    unnamed x8, local copies, waits for them, and re-layouts  2.92 us
  transfers between devices with their start and end apart: 18, of which 6 were waited for; matrix products, arithmetic and copies ran while one was open for 0% of the time, Pallas kernels for 32%

profile of v14, /device:TPU:0, one launch (start us, length us, event | category | flops | bytes accessed | tf_op | source)
XLA Modules:
  0.0 61.0 jit_solution(1312054880225294631)
XLA Ops:
  0.6 0.0 copy-start.1
  0.6 1.1 %copy-done.1 = bf16[16,4,48,128]{3,2,1,0:T(8,128)(2,1)S(1)} copy-done((bf16[16,4,48,128]{3,2,1,0:T(8,128)(2,1)S(1)}, bf16[16,4,48,128]{3,2,1,0:T(8,128)(2,1)}, u32[]{:S(2)}) %copy-start.1) | copy-done | bytes 786456
  1.8 0.0 copy-start
  1.8 1.3 %shard_map.67 = (bf16[32,2,16,128]{3,2,1,0:T(8,128)(2,1)S(1)}, bf16[32,2,16,128]{3,2,1,0:T(8,128)(2,1)S(1)}, bf16[32,2,16,128]{3,2,1,0:T(8,128)(2,1)S(1)}, bf16[32,2,16,128]{3,2,1,0:T(8,128)(2,1)S(1)}) custom-call(bf16[16,4,48,128]{3,2,1,0:T(8,128)(2,1)S(1)} %copy-done.1), custom_call_target="tpu_custom_call" | custom-call | bytes 2359296 | tf_op jit(solution)/shard_map/pallas_call | solution.py:19
  3.1 3.0 %collective-permute-start.1 = (bf16[32,2,16,128]{3,2,1,0:T(8,128)(2,1)S(1)}, bf16[32,2,16,128]{3,2,1,0:T(8,128)(2,1)S(1)}, u32[]{:S(2)}, u32[]{:S(2)}) collective-permute-start(bf16[32,2,16,128]{3,2,1,0:T(8,128)(2,1)S(1)} %get-tuple-element.33), channel_id=1, source_target_pairs={{0,1},{1,0},{2,3},{3,2},{4,5},{5,4},{6,7},{7,6},{8,9},{9,8},{10,11... | collective-permute-start | bytes 786440 | tf_op jit(solution)/shard_map/ppermute | solution.py:439
  6.1 0.1 collective-permute-start.3
  6.2 3.9 %collective-permute-start.5 = (bf16[32,2,16,128]{3,2,1,0:T(8,128)(2,1)S(1)}, bf16[32,2,16,128]{3,2,1,0:T(8,128)(2,1)S(1)}, u32[]{:S(2)}, u32[]{:S(2)}) collective-permute-start(bf16[32,2,16,128]{3,2,1,0:T(8,128)(2,1)S(1)} %get-tuple-element.34.after.refs_2_.refs_11_), channel_id=1, source_target_pairs={{2,0},{4,2},{6,4},{8,6},{10,8},{12,10},{14,12},{16,14},{18,16},{20... | collective-permute-start | bytes 786440 | tf_op jit(solution)/shard_map/ppermute | solution.py:445
  10.1 0.0 collective-permute-start
  10.1 0.0 copy-start.2
  10.1 0.9 %copy-done.2 = bf16[16,27,32]{2,0,1:T(8,128)(2,1)S(1)} copy-done((bf16[16,27,32]{2,0,1:T(8,128)(2,1)S(1)}, bf16[16,27,32]{2,0,1:T(8,128)(2,1)}, u32[]{:S(2)}) %copy-start.2) | copy-done | bytes 27672
  11.0 0.0 copy-start.3
  11.0 0.9 %copy-done.3 = bf16[16,27,32]{2,0,1:T(8,128)(2,1)S(1)} copy-done((bf16[16,27,32]{2,0,1:T(8,128)(2,1)S(1)}, bf16[16,27,32]{2,0,1:T(8,128)(2,1)}, u32[]{:S(2)}) %copy-start.3) | copy-done | bytes 27672
  11.9 0.1 shard_map.68.refs_1_.after.refs_0_
  12.0 1.2 %collective-permute-done.1.refs_0_ = bf16[32,2,16,128]{3,2,1,0:T(8,128)(2,1)S(1)} collective-permute-done((bf16[32,2,16,128]{3,2,1,0:T(8,128)(2,1)S(1)}, bf16[32,2,16,128]{3,2,1,0:T(8,128)(2,1)S(1)}, u32[]{:S(2)}, u32[]{:S(2)}) %collective-permute-start.1) | collective-permute-done | bytes 262176 | tf_op jit(solution)/shard_map/ppermute | solution.py:439
  13.2 0.0 collective-permute-start.2
  13.2 2.1 %collective-permute-start.4 = (bf16[14,16,128]{2,1,0:T(8,128)(2,1)S(1)}, bf16[14,16,128]{2,1,0:T(8,128)(2,1)S(1)}, u32[]{:S(2)}, u32[]{:S(2)}) collective-permute-start(bf16[14,16,128]{2,1,0:T(8,128)(2,1)S(1)} %shard_map.68.refs_1_.after.refs_0_), channel_id=1, source_target_pairs={{0,1},{1,0},{2,3},{3,2},{4,5},{5,4},{6,7},{7,6},{8,9},{9,8},{10,11... | collective-permute-start | bytes 172040 | tf_op jit(solution)/shard_map/ppermute | solution.py:439
  15.3 0.0 copy-done
  15.3 1.2 %shard_map.70 = (bf16[28,2,32,128]{3,2,1,0:T(8,128)(2,1)S(1)}, bf16[28,2,32,128]{3,2,1,0:T(8,128)(2,1)S(1)}) custom-call(bf16[14,16,128]{2,1,0:T(8,128)(2,1)S(1)} %shard_map.68.refs_1_.after.refs_0_, bf16[32,4,48,128]{3,2,1,0:T(8,128)(2,1)S(1)} %copy-done), custom_call_target="tpu_custom_call" | custom-call | bytes 3145728 | tf_op jit(solution)/shard_map/pallas_call | solution.py:19
  16.5 2.6 %collective-permute-done.4.refs_2_.refs_1_ = bf16[14,16,128]{2,1,0:T(8,128)(2,1)S(1)} collective-permute-done((bf16[14,16,128]{2,1,0:T(8,128)(2,1)S(1)}, bf16[14,16,128]{2,1,0:T(8,128)(2,1)S(1)}, u32[]{:S(2)}, u32[]{:S(2)}) %collective-permute-start.4) | collective-permute-done | bytes 57376 | tf_op jit(solution)/shard_map/ppermute | solution.py:439
  19.2 0.0 collective-permute-done.3.refs_0_
  19.2 0.0 collective-permute-done.5.refs_1_.refs_2_.refs_15_
  19.2 3.5 %collective-permute-start.7 = (bf16[32,2,16,128]{3,2,1,0:T(8,128)(2,1)S(1)}, bf16[32,2,16,128]{3,2,1,0:T(8,128)(2,1)S(1)}, u32[]{:S(2)}, u32[]{:S(2)}) collective-permute-start(bf16[32,2,16,128]{3,2,1,0:T(8,128)(2,1)S(1)} %shard_map.72.refs_3_.refs_12_), channel_id=1, source_target_pairs={{2,0},{4,2},{6,4},{8,6},{10,8},{12,10},{14,12},{16,14},{18,16},{20... | collective-permute-start | bytes 786440 | tf_op jit(solution)/shard_map/ppermute | solution.py:445
  22.7 0.5 shard_map.73
  23.2 0.0 collective-permute-done.refs_0_.refs_9_
  23.2 0.0 collective-permute-done.2.refs_1_.refs_10_
  23.2 2.6 %shard_map.74 = (bf16[30,2,32,128]{3,2,1,0:T(8,128)(2,1)S(1)}, bf16[30,2,32,128]{3,2,1,0:T(8,128)(2,1)S(1)}, bf16[30,2,32,128]{3,2,1,0:T(8,128)(2,1)S(1)}, bf16[...) custom-call(bf16[32,2,16,128]{3,2,1,0:T(8,128)(2,1)S(1)} %collective-permute-done.refs_0_.refs_9_, ...), custom_call_target="tpu_custom_call" | custom-call | flops 1019215872 | bytes 3145728 | tf_op jit(solution)/shard_map/pallas_call | solution.py:19
  25.8 1.6 %collective-permute-start.6 = (bf16[28,2,32,128]{3,2,1,0:T(8,128)(2,1)S(1)}, bf16[28,2,32,128]{3,2,1,0:T(8,128)(2,1)S(1)}, u32[]{:S(2)}, u32[]{:S(2)}) collective-permute-start(bf16[28,2,32,128]{3,2,1,0:T(8,128)(2,1)S(1)} %get-tuple-element.39.refs_3_), channel_id=1, source_target_pairs={{2,0},{4,2},{6,4},{8,6},{10,8},{12,10},{14,12},{16,14},{18,16},{20... | collective-permute-start | bytes 1376264 | tf_op jit(solution)/shard_map/ppermute | solution.py:445
  27.4 0.0 collective-permute-done.7.refs_3_.refs_16_
  27.4 1.8 %shard_map.75 = (bf16[30,2,32,128]{3,2,1,0:T(8,128)(2,1)S(1)}, bf16[30,2,32,128]{3,2,1,0:T(8,128)(2,1)S(1)}, bf16[28,2,32,128]{3,2,1,0:T(8,128)(2,1)S(1)}) custom-call(bf16[32,2,16,128]{3,2,1,0:T(8,128)(2,1)S(1)} %get-tuple-element.32.refs_4_.refs_0_.refs_13_, bf16[32,2,16,128]{3,2,1,0:T(8,128)(2,1)S(1)} %shard_map.69.refs_5_.refs_1_.refs_14_, ...), custom_call_target="tpu_custom_call" | custom-call | flops 679477248 | bytes 2359296 | tf_op jit(solution)/shard_map/pallas_call | solution.py:19
  29.2 0.1 collective-permute-start.9
  29.3 8.3 %shard_map.76 = (f32[2,7,16,128]{3,2,1,0:T(8,128)S(1)}, f32[2,7,16,128]{3,2,1,0:T(8,128)S(1)}, bf16[26,2,32,128]{3,2,1,0:T(8,128)(2,1)S(1)}) custom-call(bf16[30,2,32,128]{3,2,1,0:T(8,128)(2,1)S(1)} %get-tuple-element.40.refs_0_, bf16[30,2,32,128]{3,2,1,0:T(8,128)(2,1)S(1)} %get-tuple-element.41.refs_4_.refs_1_, ...), custom_call_target="tpu_custom_call" | custom-call | tf_op jit(solution)/shard_map/pallas_call | solution.py:19
  37.6 0.1 collective-permute-start.8
  37.6 1.3 %collective-permute-done.8.two = f32[2,7,16,128]{3,2,1,0:T(8,128)S(1)} collective-permute-done((f32[2,7,16,128]{3,2,1,0:T(8,128)S(1)}, f32[2,7,16,128]{3,2,1,0:T(8,128)S(1)}, u32[]{:S(2)}, u32[]{:S(2)}) %collective-permute-start.8) | collective-permute-done | bytes 114720 | tf_op jit(solution)/shard_map/ppermute | solution.py:555
  39.0 0.0 collective-permute-done.6.after.refs_5_
  39.0 1.6 %collective-permute-start.10 = (f32[7,16,128]{2,1,0:T(8,128)S(1)}, f32[7,16,128]{2,1,0:T(8,128)S(1)}, u32[]{:S(2)}, u32[]{:S(2)}) collective-permute-start(f32[7,16,128]{2,1,0:T(8,128)S(1)} %get-tuple-element.56), channel_id=1, source_target_pairs={{0,1},{1,0},{2,3},{3,2},{4,5},{5,4},{6,7},{7,6},{8,9},{9,8},{10,11... | collective-permute-start | bytes 172040 | tf_op jit(solution)/shard_map/ppermute | solution.py:439
  40.5 0.2 collective-permute-start.12
  40.8 1.8 %collective-permute-start.11 = (f32[7,16,128]{2,1,0:T(8,128)S(1)}, f32[7,16,128]{2,1,0:T(8,128)S(1)}, u32[]{:S(2)}, u32[]{:S(2)}) collective-permute-start(f32[7,16,128]{2,1,0:T(8,128)S(1)} %get-tuple-element.51.after.refs_1_), channel_id=1, source_target_pairs={{0,4},{2,6},{4,0},{6,2},{8,12},{10,14},{12,8},{14,10},{16,20},{18,... | collective-permute-start | bytes 172040 | tf_op jit(solution)/shard_map/ppermute | solution.py:555
  42.5 0.0 collective-permute-done.9.refs_2_
  42.5 2.8 %shard_map.78 = (bf16[24,4,16,128]{3,2,1,0:T(8,128)(2,1)S(1)}, bf16[24,4,16,128]{3,2,1,0:T(8,128)(2,1)S(1)}) custom-call(f32[7,16,128]{2,1,0:T(8,128)S(1)} %get-tuple-element.51.after.refs_1_, bf16[192,384]{1,0:T(8,128)(2,1)S(1)} %get-tuple-element.45.refs_5_.refs_0_, bf16[192,384]{1,0:T(8,128)(2,1)S(1)} %get-tuple-element.52.refs_1_, ...), custom_call_target="tpu_custom_call" | custom-call | flops 1358954496 | bytes 2359296 | tf_op jit(solution)/shard_map/pallas_call | solution.py:19
  45.4 0.0 collective-permute-done.10.refs_2_
  45.4 0.4 collective-permute-done.11.refs_3_
  45.8 0.0 collective-permute-done.12.refs_4_
  45.8 1.2 %collective-permute-start.13 = (bf16[24,4,16,128]{3,2,1,0:T(8,128)(2,1)S(1)}, bf16[24,4,16,128]{3,2,1,0:T(8,128)(2,1)S(1)}, u32[]{:S(2)}, u32[]{:S(2)}) collective-permute-start(bf16[24,4,16,128]{3,2,1,0:T(8,128)(2,1)S(1)} %shard_map.80), channel_id=1, source_target_pairs={{0,1},{1,0},{2,3},{3,2},{4,5},{5,4},{6,7},{7,6},{8,9},{9,8},{10,11... | collective-permute-start | bytes 1179656 | tf_op jit(solution)/shard_map/ppermute | solution.py:439
  47.0 1.1 %collective-permute-start.14 = (f32[7,16,128]{2,1,0:T(8,128)S(1)}, f32[7,16,128]{2,1,0:T(8,128)S(1)}, u32[]{:S(2)}, u32[]{:S(2)}) collective-permute-start(f32[7,16,128]{2,1,0:T(8,128)S(1)} %shard_map.79.refs_1_.refs_0_), channel_id=1, source_target_pairs={{0,8},{2,10},{4,12},{6,14},{8,0},{10,2},{12,4},{14,6},{16,24},{18,... | collective-permute-start | bytes 172040 | tf_op jit(solution)/shard_map/ppermute | solution.py:555
  48.1 4.0 %collective-permute-start.15 = (f32[7,16,128]{2,1,0:T(8,128)S(1)}, f32[7,16,128]{2,1,0:T(8,128)S(1)}, u32[]{:S(2)}, u32[]{:S(2)}) collective-permute-start(f32[7,16,128]{2,1,0:T(8,128)S(1)} %shard_map.79.refs_1_.refs_0_), channel_id=1, source_target_pairs={{0,16},{2,18},{4,20},{6,22},{8,24},{10,26},{12,28},{14,30},{16,0},... | collective-permute-start | bytes 172040 | tf_op jit(solution)/shard_map/ppermute | solution.py:555
  52.1 0.0 collective-permute-start.16
  52.2 0.0 collective-permute-done.14.refs_1_
  52.2 3.1 %collective-permute-done.15.refs_2_ = f32[7,16,128]{2,1,0:T(8,128)S(1)} collective-permute-done((f32[7,16,128]{2,1,0:T(8,128)S(1)}, f32[7,16,128]{2,1,0:T(8,128)S(1)}, u32[]{:S(2)}, u32[]{:S(2)}) %collective-permute-start.15) | collective-permute-done | bytes 57376 | tf_op jit(solution)/shard_map/ppermute | solution.py:555
  55.2 2.9 %collective-permute-done.16.refs_3_ = f32[7,16,128]{2,1,0:T(8,128)S(1)} collective-permute-done((f32[7,16,128]{2,1,0:T(8,128)S(1)}, f32[7,16,128]{2,1,0:T(8,128)S(1)}, u32[]{:S(2)}, u32[]{:S(2)}) %collective-permute-start.16) | collective-permute-done | bytes 57376 | tf_op jit(solution)/shard_map/ppermute | solution.py:555
  58.1 0.1 collective-permute-start.17
  58.2 0.0 collective-permute-done.13.refs_1_
  58.2 1.9 %shard_map.81 = (f32[8,128]{1,0:T(8,128)S(1)}, bf16[16,4,48,128]{3,2,1,0:T(8,128)(2,1)}) custom-call(bf16[24,4,16,128]{3,2,1,0:T(8,128)(2,1)S(1)} %get-tuple-element.54.refs_0_, bf16[24,4,16,128]{3,2,1,0:T(8,128)(2,1)S(1)} %collective-permute-done.13.refs_1_), custom_call_target="tpu_custom_call" | custom-call | bytes 1572864 | tf_op jit(solution)/shard_map/pallas_call | solution.py:19
  60.1 0.0 collective-permute-done.17.other
  60.1 0.9 %shard_map.83 = (f32[27,16,32]{2,1,0:T(8,128)}, f32[27,16,32]{2,1,0:T(8,128)}) custom-call(f32[8,128]{1,0:T(8,128)S(1)} %get-tuple-element.58.after, f32[7,16,128]{2,1,0:T(8,128)S(1)} %shard_map.82.mine, f32[7,16,128]{2,1,0:T(8,128)S(1)} %collective-permute-done.17.other), custom_call_target="tpu_custom_call" | custom-call | tf_op jit(solution)/shard_map/pallas_call | solution.py:19
  (7 shorter events, 0.1 us)
Async XLA Ops:
  0.6 1.1 %copy-start.1 = (bf16[16,4,48,128]{3,2,1,0:T(8,128)(2,1)S(1)}, bf16[16,4,48,128]{3,2,1,0:T(8,128)(2,1)}, u32[]{:S(2)}) copy-start(bf16[16,4,48,128]{3,2,1,0:T(8,128)(2,1)} %x_ref.2) | copy-start | bytes 2359300
  1.8 13.5 %copy-start = (bf16[32,4,48,128]{3,2,1,0:T(8,128)(2,1)S(1)}, bf16[32,4,48,128]{3,2,1,0:T(8,128)(2,1)}, u32[]{:S(2)}) copy-start(bf16[32,4,48,128]{3,2,1,0:T(8,128)(2,1)} %x_ref.3) | copy-start | bytes 4718596
  3.1 10.1 %collective-permute-start.1 = (bf16[32,2,16,128]{3,2,1,0:T(8,128)(2,1)S(1)}, bf16[32,2,16,128]{3,2,1,0:T(8,128)(2,1)S(1)}, u32[]{:S(2)}, u32[]{:S(2)}) collective-permute-start(bf16[32,2,16,128]{3,2,1,0:T(8,128)(2,1)S(1)} %get-tuple-element.33), channel_id=1, source_target_pairs={{0,1},{1,0},{2,3},{3,2},{4,5},{5,4},{6,7},{7,6},{8,9},{9,8},{10,11... | collective-permute-start | bytes 786440 | tf_op jit(solution)/shard_map/ppermute | solution.py:439
  6.1 13.1 %collective-permute-start.3 = (bf16[32,2,16,128]{3,2,1,0:T(8,128)(2,1)S(1)}, bf16[32,2,16,128]{3,2,1,0:T(8,128)(2,1)S(1)}, u32[]{:S(2)}, u32[]{:S(2)}) collective-permute-start(bf16[32,2,16,128]{3,2,1,0:T(8,128)(2,1)S(1)} %get-tuple-element.35), channel_id=1, source_target_pairs={{0,1},{1,0},{2,3},{3,2},{4,5},{5,4},{6,7},{7,6},{8,9},{9,8},{10,11... | collective-permute-start | bytes 786440 | tf_op jit(solution)/shard_map/ppermute | solution.py:439
  6.2 13.0 %collective-permute-start.5 = (bf16[32,2,16,128]{3,2,1,0:T(8,128)(2,1)S(1)}, bf16[32,2,16,128]{3,2,1,0:T(8,128)(2,1)S(1)}, u32[]{:S(2)}, u32[]{:S(2)}) collective-permute-start(bf16[32,2,16,128]{3,2,1,0:T(8,128)(2,1)S(1)} %get-tuple-element.34.after.refs_2_.refs_11_), channel_id=1, source_target_pairs={{2,0},{4,2},{6,4},{8,6},{10,8},{12,10},{14,12},{16,14},{18,16},{20... | collective-permute-start | bytes 786440 | tf_op jit(solution)/shard_map/ppermute | solution.py:445
  10.1 13.2 %collective-permute-start = (bf16[32,2,16,128]{3,2,1,0:T(8,128)(2,1)S(1)}, bf16[32,2,16,128]{3,2,1,0:T(8,128)(2,1)S(1)}, u32[]{:S(2)}, u32[]{:S(2)}) collective-permute-start(bf16[32,2,16,128]{3,2,1,0:T(8,128)(2,1)S(1)} %get-tuple-element.32.refs_4_.refs_0_.refs_13_), channel_id=1, source_target_pairs={{0,2},{2,4},{4,6},{6,8},{8,10},{10,12},{12,14},{14,16},{16,18},{18... | collective-permute-start | bytes 786440 | tf_op jit(solution)/shard_map/ppermute | solution.py:442
  10.1 0.9 %copy-start.2 = (bf16[16,27,32]{2,0,1:T(8,128)(2,1)S(1)}, bf16[16,27,32]{2,0,1:T(8,128)(2,1)}, u32[]{:S(2)}) copy-start(bf16[16,27,32]{2,0,1:T(8,128)(2,1)} %param.6) | copy-start | bytes 82948
  11.0 0.9 %copy-start.3 = (bf16[16,27,32]{2,0,1:T(8,128)(2,1)S(1)}, bf16[16,27,32]{2,0,1:T(8,128)(2,1)}, u32[]{:S(2)}) copy-start(bf16[16,27,32]{2,0,1:T(8,128)(2,1)} %param.7) | copy-start | bytes 82948
  13.2 10.0 %collective-permute-start.2 = (bf16[32,2,16,128]{3,2,1,0:T(8,128)(2,1)S(1)}, bf16[32,2,16,128]{3,2,1,0:T(8,128)(2,1)S(1)}, u32[]{:S(2)}, u32[]{:S(2)}) collective-permute-start(bf16[32,2,16,128]{3,2,1,0:T(8,128)(2,1)S(1)} %shard_map.69.refs_5_.refs_1_.refs_14_), channel_id=1, source_target_pairs={{0,2},{2,4},{4,6},{6,8},{8,10},{10,12},{12,14},{14,16},{16,18},{18... | collective-permute-start | bytes 786440 | tf_op jit(solution)/shard_map/ppermute | solution.py:442
  13.2 5.9 %collective-permute-start.4 = (bf16[14,16,128]{2,1,0:T(8,128)(2,1)S(1)}, bf16[14,16,128]{2,1,0:T(8,128)(2,1)S(1)}, u32[]{:S(2)}, u32[]{:S(2)}) collective-permute-start(bf16[14,16,128]{2,1,0:T(8,128)(2,1)S(1)} %shard_map.68.refs_1_.after.refs_0_), channel_id=1, source_target_pairs={{0,1},{1,0},{2,3},{3,2},{4,5},{5,4},{6,7},{7,6},{8,9},{9,8},{10,11... | collective-permute-start | bytes 172040 | tf_op jit(solution)/shard_map/ppermute | solution.py:439
  19.2 8.2 %collective-permute-start.7 = (bf16[32,2,16,128]{3,2,1,0:T(8,128)(2,1)S(1)}, bf16[32,2,16,128]{3,2,1,0:T(8,128)(2,1)S(1)}, u32[]{:S(2)}, u32[]{:S(2)}) collective-permute-start(bf16[32,2,16,128]{3,2,1,0:T(8,128)(2,1)S(1)} %shard_map.72.refs_3_.refs_12_), channel_id=1, source_target_pairs={{2,0},{4,2},{6,4},{8,6},{10,8},{12,10},{14,12},{16,14},{18,16},{20... | collective-permute-start | bytes 786440 | tf_op jit(solution)/shard_map/ppermute | solution.py:445
  25.8 13.1 %collective-permute-start.6 = (bf16[28,2,32,128]{3,2,1,0:T(8,128)(2,1)S(1)}, bf16[28,2,32,128]{3,2,1,0:T(8,128)(2,1)S(1)}, u32[]{:S(2)}, u32[]{:S(2)}) collective-permute-start(bf16[28,2,32,128]{3,2,1,0:T(8,128)(2,1)S(1)} %get-tuple-element.39.refs_3_), channel_id=1, source_target_pairs={{2,0},{4,2},{6,4},{8,6},{10,8},{12,10},{14,12},{16,14},{18,16},{20... | collective-permute-start | bytes 1376264 | tf_op jit(solution)/shard_map/ppermute | solution.py:445
  29.2 13.3 %collective-permute-start.9 = (bf16[28,2,32,128]{3,2,1,0:T(8,128)(2,1)S(1)}, bf16[28,2,32,128]{3,2,1,0:T(8,128)(2,1)S(1)}, u32[]{:S(2)}, u32[]{:S(2)}) collective-permute-start(bf16[28,2,32,128]{3,2,1,0:T(8,128)(2,1)S(1)} %get-tuple-element.44.refs_4_), channel_id=1, source_target_pairs={{0,2},{2,4},{4,6},{6,8},{8,10},{10,12},{12,14},{14,16},{16,18},{18... | collective-permute-start | bytes 1376264 | tf_op jit(solution)/shard_map/ppermute | solution.py:442
  37.6 1.4 %collective-permute-start.8 = (f32[2,7,16,128]{3,2,1,0:T(8,128)S(1)}, f32[2,7,16,128]{3,2,1,0:T(8,128)S(1)}, u32[]{:S(2)}, u32[]{:S(2)}) collective-permute-start(f32[2,7,16,128]{3,2,1,0:T(8,128)S(1)} %get-tuple-element.50), channel_id=1, source_target_pairs={{0,2},{2,0},{4,6},{6,4},{8,10},{10,8},{12,14},{14,12},{16,18},{18,... | collective-permute-start | bytes 344072 | tf_op jit(solution)/shard_map/ppermute | solution.py:555
  39.0 6.4 %collective-permute-start.10 = (f32[7,16,128]{2,1,0:T(8,128)S(1)}, f32[7,16,128]{2,1,0:T(8,128)S(1)}, u32[]{:S(2)}, u32[]{:S(2)}) collective-permute-start(f32[7,16,128]{2,1,0:T(8,128)S(1)} %get-tuple-element.56), channel_id=1, source_target_pairs={{0,1},{1,0},{2,3},{3,2},{4,5},{5,4},{6,7},{7,6},{8,9},{9,8},{10,11... | collective-permute-start | bytes 172040 | tf_op jit(solution)/shard_map/ppermute | solution.py:439
  40.5 5.2 %collective-permute-start.12 = (f32[7,16,128]{2,1,0:T(8,128)S(1)}, f32[7,16,128]{2,1,0:T(8,128)S(1)}, u32[]{:S(2)}, u32[]{:S(2)}) collective-permute-start(f32[7,16,128]{2,1,0:T(8,128)S(1)} %get-tuple-element.56), channel_id=1, source_target_pairs={{0,5},{1,4},{2,7},{3,6},{4,1},{5,0},{6,3},{7,2},{8,13},{9,12},{10,... | collective-permute-start | bytes 172040 | tf_op jit(solution)/shard_map/ppermute | solution.py:561
  40.8 5.0 %collective-permute-start.11 = (f32[7,16,128]{2,1,0:T(8,128)S(1)}, f32[7,16,128]{2,1,0:T(8,128)S(1)}, u32[]{:S(2)}, u32[]{:S(2)}) collective-permute-start(f32[7,16,128]{2,1,0:T(8,128)S(1)} %get-tuple-element.51.after.refs_1_), channel_id=1, source_target_pairs={{0,4},{2,6},{4,0},{6,2},{8,12},{10,14},{12,8},{14,10},{16,20},{18,... | collective-permute-start | bytes 172040 | tf_op jit(solution)/shard_map/ppermute | solution.py:555
  45.8 12.4 %collective-permute-start.13 = (bf16[24,4,16,128]{3,2,1,0:T(8,128)(2,1)S(1)}, bf16[24,4,16,128]{3,2,1,0:T(8,128)(2,1)S(1)}, u32[]{:S(2)}, u32[]{:S(2)}) collective-permute-start(bf16[24,4,16,128]{3,2,1,0:T(8,128)(2,1)S(1)} %shard_map.80), channel_id=1, source_target_pairs={{0,1},{1,0},{2,3},{3,2},{4,5},{5,4},{6,7},{7,6},{8,9},{9,8},{10,11... | collective-permute-start | bytes 1179656 | tf_op jit(solution)/shard_map/ppermute | solution.py:439
  47.0 5.2 %collective-permute-start.14 = (f32[7,16,128]{2,1,0:T(8,128)S(1)}, f32[7,16,128]{2,1,0:T(8,128)S(1)}, u32[]{:S(2)}, u32[]{:S(2)}) collective-permute-start(f32[7,16,128]{2,1,0:T(8,128)S(1)} %shard_map.79.refs_1_.refs_0_), channel_id=1, source_target_pairs={{0,8},{2,10},{4,12},{6,14},{8,0},{10,2},{12,4},{14,6},{16,24},{18,... | collective-permute-start | bytes 172040 | tf_op jit(solution)/shard_map/ppermute | solution.py:555
  48.1 7.1 %collective-permute-start.15 = (f32[7,16,128]{2,1,0:T(8,128)S(1)}, f32[7,16,128]{2,1,0:T(8,128)S(1)}, u32[]{:S(2)}, u32[]{:S(2)}) collective-permute-start(f32[7,16,128]{2,1,0:T(8,128)S(1)} %shard_map.79.refs_1_.refs_0_), channel_id=1, source_target_pairs={{0,16},{2,18},{4,20},{6,22},{8,24},{10,26},{12,28},{14,30},{16,0},... | collective-permute-start | bytes 172040 | tf_op jit(solution)/shard_map/ppermute | solution.py:555
  52.1 6.0 %collective-permute-start.16 = (f32[7,16,128]{2,1,0:T(8,128)S(1)}, f32[7,16,128]{2,1,0:T(8,128)S(1)}, u32[]{:S(2)}, u32[]{:S(2)}) collective-permute-start(f32[7,16,128]{2,1,0:T(8,128)S(1)} %shard_map.79.refs_1_.refs_0_), channel_id=1, source_target_pairs={{0,24},{2,26},{4,28},{6,30},{8,16},{10,18},{12,20},{14,22},{16,8},... | collective-permute-start | bytes 172040 | tf_op jit(solution)/shard_map/ppermute | solution.py:555
  58.1 2.0 %collective-permute-start.17 = (f32[7,16,128]{2,1,0:T(8,128)S(1)}, f32[7,16,128]{2,1,0:T(8,128)S(1)}, u32[]{:S(2)}, u32[]{:S(2)}) collective-permute-start(f32[7,16,128]{2,1,0:T(8,128)S(1)} %shard_map.82.mine), channel_id=1, source_target_pairs={{0,2},{2,0},{4,6},{6,4},{8,10},{10,8},{12,14},{14,12},{16,18},{18,... | collective-permute-start | bytes 172040 | tf_op jit(solution)/shard_map/ppermute | solution.py:555

commit v15 on v14

--- a/solution.py
+++ b/solution.py
@@ -231,7 +231,7 @@
     blocks = [k for k in range(1, 13) if count // 2 % k == 0 and k * len(deltas) <= 12]
     together = max(blocks, default=1)
 
-    def step(r, _):
+    def product(r):
         left, right = [], []
         for k in range(together):
             row = 2 * (r * together + k)
@@ -249,15 +249,17 @@
                         for ref in refs:
                             rows.append(ref[first_row + row + b, side])
                 left.append(jnp.concatenate(rows, axis=0))
-        total[...] += lax.dot_general(
+        return lax.dot_general(
             jnp.concatenate(left, axis=1),
             jnp.concatenate(right, axis=1),
             (((1,), (1,)), ((), ())),
             preferred_element_type=F32,
         )
-        return 0
-
-    lax.fori_loop(0, count // 2 // together, step, 0)
+
+    value = total[...]
+    for r in range(count // 2 // together):
+        value = value + product(r)
+    total[...] = value
 
 
 def weight_fold(total, size):
@@ -359,27 +361,6 @@
     in_blocks(outs[0].shape[0] // 2, one)
 
 
-def finish_kernel(factor, after, mine, other, first, second):
-    del after
-    channels = first.shape[2]
-
-    def place(ours, theirs):
-        for out, sums in ((ours, mine), (theirs, other)):
-            for t in range(27):
-                low = t % 4 * channels
-                out[t] = sums[t // 4, :, low : low + channels] * factor
-
-    odd = lax.rem(lax.axis_index("slab"), 2)
-
-    @pl.when(odd == 0)
-    def _():
-        place(first, second)
-
-    @pl.when(odd == 1)
-    def _():
-        place(second, first)
-
-
 def split_kernel(after, one, two, *outs):
     del after
     for g, out in enumerate(outs):
@@ -397,9 +378,27 @@
     pass
 
 
-def merge_kernel(extent, *refs):
-    pieces, token, out, wide = refs[:-3], refs[-3], refs[-2], refs[-1]
-    token[...] = jnp.zeros_like(token)
+def merge_kernel(extent, factor, *refs):
+    mine, other, *pieces = refs[:-4]
+    out, first, second, wide = refs[-4:]
+    channels = first.shape[2]
+
+    def place(ours, theirs):
+        for result, sums in ((ours, mine), (theirs, other)):
+            for t in range(27):
+                low = t % 4 * channels
+                result[t] = sums[t // 4, :, low : low + channels] * factor
+
+    odd = lax.rem(lax.axis_index("slab"), 2)
+
+    @pl.when(odd == 0)
+    def _():
+        place(first, second)
+
+    @pl.when(odd == 1)
+    def _():
+        place(second, first)
+
     size, planes, rows = out.shape[:3]
     share = rows // extent
     me = lax.axis_index("chan")
@@ -489,8 +488,8 @@
         moved=matrix.size * 8,
     )
     if whole and extent > 1 and pairs > 1:
-        parts[1][-1] = relayed(parts[1][-1], pack)
-        parts[1][0] = relayed(relayed(parts[1][0], grads[0], *packs[1:]), own_after[0])
+        parts[1][-1] = relayed(parts[1][-1], *packs[1:])
+        parts[1][0] = relayed(relayed(parts[1][0], grads[0], first_wide), own_after[0])
     by_pair = [[parts[j][p] for j in range(extent)] for p in range(pairs)]
     groups = extent
     if not whole:
@@ -604,18 +603,12 @@
         mine, other = jnp.where(even, mine, other), jnp.where(even, other, mine)
         mine, other = lax.psum((mine, other), "slab")
         mine, other = jnp.where(even, mine, other), jnp.where(even, other, mine)
-    token, input_grad = call(
-        functools.partial(merge_kernel, extent),
-        [jax.ShapeDtypeStruct((8, 128), F32), jax.ShapeDtypeStruct(field.shape, BF16)],
-        pieces,
+    input_grad, first_grad, second_grad = call(
+        functools.partial(merge_kernel, extent, factor),
+        [jax.ShapeDtypeStruct(field.shape, BF16)] + [jax.ShapeDtypeStruct(by_tap, F32)] * 2,
+        [mine, other] + pieces,
         [pltpu.VMEM((rows * planes * size, depth), F32)],
         moved=4 * field.size,
-    )
-    first_grad, second_grad = call(
-        functools.partial(finish_kernel, factor),
-        [jax.ShapeDtypeStruct(by_tap, F32)] * 2,
-        [token, mine, other],
-        loose=1,
     )
     first_grad, second_grad = (jnp.transpose(g, (1, 0, 2)) for g in (first_grad, second_grad))
     return input_grad, first_grad, second_grad

time: 61.3 us -> 64.1 us (1.046)
  waiting for transfers between devices: 11.6 us -> 17.1 us
  Pallas kernels: 21.5 us -> 19.7 us
  starting transfers between devices: 24.3 us -> 23.4 us
    ppermute x3, waiting for transfers between devices: 0.01 us -> 2.27 us  [to_next(): lax.ppermute(value, 'slab', [(i, (i + 1) % slabs) for i in range(slabs)])]
    ppermute x5, waiting for transfers between devices: 3.87 us -> 5.71 us  [to_chan(): lax.ppermute(value, 'chan', [(i, (i + shift) % extent) for i in range(ext...]
    pallas_call x17 -> x16, Pallas kernels: 21.5 us -> 19.7 us  [call(): pl.pallas_call(kernel, out_shape=outs, in_specs=[still] * loose + [whole]...]
    ppermute x6, waiting for transfers between devices: 7.67 us -> 9.15 us  [stepped(): return lax.ppermute(value, 'slab', [(i, i ^ stride) for i in range(slabs)])]
    ppermute x6, starting transfers between devices: 7.06 us -> 6.1 us  [stepped(): return lax.ppermute(value, 'slab', [(i, i ^ stride) for i in range(slabs)])]
    ppermute x3, starting transfers between devices: 0.06 us -> 0.73 us  [to_next(): lax.ppermute(value, 'slab', [(i, (i + 1) % slabs) for i in range(slabs)])]
  transfers between devices with their start and end apart: 18 -> 18, of which waited for: 6 -> 7; matrix products, arithmetic and copies ran while one was open for 0% -> 0% of each run, Pallas kernels for 32% -> 26%
where the time goes in v15:
time: 64.1 us; the launch traced here: 63.9 us
  starting transfers between devices  23.4 us (37%)
  Pallas kernels  19.7 us (31%)
  waiting for transfers between devices  17.1 us (27%)
  local copies, waits for them, and re-layouts  2.92 us (5%)
  between operations  0.79 us (1%)
    pallas_call x16, Pallas kernels, call(): pl.pallas_call(kernel, out_shape=outs, in_specs=[still] * loose + [whole]...  19.7 us
    ppermute x6, waiting for transfers between devices, stepped(): return lax.ppermute(value, 'slab', [(i, i ^ stride) for i in range(slabs)])  9.15 us
    ppermute x3, starting transfers between devices, to_prev(): lax.ppermute(value, 'slab', [((i + 1) % slabs, i) for i in range(slabs)])  8.43 us
    ppermute x5, starting transfers between devices, to_chan(): lax.ppermute(value, 'chan', [(i, (i + shift) % extent) for i in range(ext...  7.73 us
    ppermute x6, starting transfers between devices, stepped(): return lax.ppermute(value, 'slab', [(i, i ^ stride) for i in range(slabs)])  6.1 us
    ppermute x5, waiting for transfers between devices, to_chan(): lax.ppermute(value, 'chan', [(i, (i + shift) % extent) for i in range(ext...  5.71 us
    unnamed x8, local copies, waits for them, and re-layouts  2.92 us
    ppermute x3, waiting for transfers between devices, to_next(): lax.ppermute(value, 'slab', [(i, (i + 1) % slabs) for i in range(slabs)])  2.27 us
  transfers between devices with their start and end apart: 18, of which 7 were waited for; matrix products, arithmetic and copies ran while one was open for 0% of the time, Pallas kernels for 26%

profile of v15, /device:TPU:0, one launch (start us, length us, event | category | flops | bytes accessed | tf_op | source)
XLA Modules:
  0.0 63.9 jit_solution(4988842460115827469)
XLA Ops:
  0.6 0.0 copy-start.1
  0.6 1.1 %copy-done.1 = bf16[16,4,48,128]{3,2,1,0:T(8,128)(2,1)S(1)} copy-done((bf16[16,4,48,128]{3,2,1,0:T(8,128)(2,1)S(1)}, bf16[16,4,48,128]{3,2,1,0:T(8,128)(2,1)}, u32[]{:S(2)}) %copy-start.1) | copy-done | bytes 786456
  1.8 0.0 copy-start
  1.8 1.3 %shard_map.67 = (bf16[32,2,16,128]{3,2,1,0:T(8,128)(2,1)S(1)}, bf16[32,2,16,128]{3,2,1,0:T(8,128)(2,1)S(1)}, bf16[32,2,16,128]{3,2,1,0:T(8,128)(2,1)S(1)}, bf16[32,2,16,128]{3,2,1,0:T(8,128)(2,1)S(1)}) custom-call(bf16[16,4,48,128]{3,2,1,0:T(8,128)(2,1)S(1)} %copy-done.1), custom_call_target="tpu_custom_call" | custom-call | bytes 2359296 | tf_op jit(solution)/shard_map/pallas_call | solution.py:19
  3.1 3.0 %collective-permute-start.1 = (bf16[32,2,16,128]{3,2,1,0:T(8,128)(2,1)S(1)}, bf16[32,2,16,128]{3,2,1,0:T(8,128)(2,1)S(1)}, u32[]{:S(2)}, u32[]{:S(2)}) collective-permute-start(bf16[32,2,16,128]{3,2,1,0:T(8,128)(2,1)S(1)} %get-tuple-element.32), channel_id=1, source_target_pairs={{0,1},{1,0},{2,3},{3,2},{4,5},{5,4},{6,7},{7,6},{8,9},{9,8},{10,11... | collective-permute-start | bytes 786440 | tf_op jit(solution)/shard_map/ppermute | solution.py:438
  6.1 0.1 collective-permute-start.4
  6.2 3.9 %collective-permute-start.5 = (bf16[32,2,16,128]{3,2,1,0:T(8,128)(2,1)S(1)}, bf16[32,2,16,128]{3,2,1,0:T(8,128)(2,1)S(1)}, u32[]{:S(2)}, u32[]{:S(2)}) collective-permute-start(bf16[32,2,16,128]{3,2,1,0:T(8,128)(2,1)S(1)} %get-tuple-element.33.after.refs_2_.refs_11_), channel_id=1, source_target_pairs={{2,0},{4,2},{6,4},{8,6},{10,8},{12,10},{14,12},{16,14},{18,16},{20... | collective-permute-start | bytes 786440 | tf_op jit(solution)/shard_map/ppermute | solution.py:444
  10.1 0.0 copy-start.2
  10.1 0.9 %copy-done.2 = bf16[16,27,32]{2,0,1:T(8,128)(2,1)S(1)} copy-done((bf16[16,27,32]{2,0,1:T(8,128)(2,1)S(1)}, bf16[16,27,32]{2,0,1:T(8,128)(2,1)}, u32[]{:S(2)}) %copy-start.2) | copy-done | bytes 27672
  11.0 0.0 copy-start.3
  11.0 0.9 %copy-done.3 = bf16[16,27,32]{2,0,1:T(8,128)(2,1)S(1)} copy-done((bf16[16,27,32]{2,0,1:T(8,128)(2,1)S(1)}, bf16[16,27,32]{2,0,1:T(8,128)(2,1)}, u32[]{:S(2)}) %copy-start.3) | copy-done | bytes 27672
  11.9 0.1 shard_map.68.after.refs_0_
  12.0 1.6 %collective-permute-start.2 = (bf16[14,16,128]{2,1,0:T(8,128)(2,1)S(1)}, bf16[14,16,128]{2,1,0:T(8,128)(2,1)S(1)}, u32[]{:S(2)}, u32[]{:S(2)}) collective-permute-start(bf16[14,16,128]{2,1,0:T(8,128)(2,1)S(1)} %shard_map.68.after.refs_0_), channel_id=1, source_target_pairs={{0,1},{1,0},{2,3},{3,2},{4,5},{5,4},{6,7},{7,6},{8,9},{9,8},{10,11... | collective-permute-start | bytes 172040 | tf_op jit(solution)/shard_map/ppermute | solution.py:438
  13.5 0.0 collective-permute-start
  13.5 5.7 %collective-permute-done.2.refs_1_ = bf16[14,16,128]{2,1,0:T(8,128)(2,1)S(1)} collective-permute-done((bf16[14,16,128]{2,1,0:T(8,128)(2,1)S(1)}, bf16[14,16,128]{2,1,0:T(8,128)(2,1)S(1)}, u32[]{:S(2)}, u32[]{:S(2)}) %collective-permute-start.2) | collective-permute-done | bytes 57376 | tf_op jit(solution)/shard_map/ppermute | solution.py:438
  19.2 0.0 collective-permute-done.1.refs_0_
  19.3 0.0 collective-permute-start.3
  19.3 0.0 copy-done
  19.3 1.3 %shard_map.70 = (bf16[28,2,32,128]{3,2,1,0:T(8,128)(2,1)S(1)}, bf16[28,2,32,128]{3,2,1,0:T(8,128)(2,1)S(1)}) custom-call(bf16[14,16,128]{2,1,0:T(8,128)(2,1)S(1)} %shard_map.68.after.refs_0_, bf16[32,4,48,128]{3,2,1,0:T(8,128)(2,1)S(1)} %copy-done), custom_call_target="tpu_custom_call" | custom-call | bytes 3145728 | tf_op jit(solution)/shard_map/pallas_call | solution.py:19
  20.5 0.5 shard_map.71
  21.1 0.0 collective-permute-done.4.refs_0_
  21.1 0.0 collective-permute-done.5.refs_1_.refs_2_.refs_15_
  21.1 4.5 %collective-permute-start.7 = (bf16[32,2,16,128]{3,2,1,0:T(8,128)(2,1)S(1)}, bf16[32,2,16,128]{3,2,1,0:T(8,128)(2,1)S(1)}, u32[]{:S(2)}, u32[]{:S(2)}) collective-permute-start(bf16[32,2,16,128]{3,2,1,0:T(8,128)(2,1)S(1)} %shard_map.73.refs_3_.refs_12_), channel_id=1, source_target_pairs={{2,0},{4,2},{6,4},{8,6},{10,8},{12,10},{14,12},{16,14},{18,16},{20... | collective-permute-start | bytes 786440 | tf_op jit(solution)/shard_map/ppermute | solution.py:444
  25.6 0.0 collective-permute-done.refs_0_.refs_9_
  25.6 2.3 %collective-permute-done.3.refs_1_.refs_10_ = bf16[32,2,16,128]{3,2,1,0:T(8,128)(2,1)S(1)} collective-permute-done((bf16[32,2,16,128]{3,2,1,0:T(8,128)(2,1)S(1)}, bf16[32,2,16,128]{3,2,1,0:T(8,128)(2,1)S(1)}, u32[]{:S(2)}, u32[]{:S(2)}) %collective-permute-start.3) | collective-permute-done | bytes 262176 | tf_op jit(solution)/shard_map/ppermute | solution.py:441
  27.9 2.6 %shard_map.74 = (bf16[30,2,32,128]{3,2,1,0:T(8,128)(2,1)S(1)}, bf16[30,2,32,128]{3,2,1,0:T(8,128)(2,1)S(1)}, bf16[30,2,32,128]{3,2,1,0:T(8,128)(2,1)S(1)}, bf16[...) custom-call(bf16[32,2,16,128]{3,2,1,0:T(8,128)(2,1)S(1)} %collective-permute-done.refs_0_.refs_9_, ...), custom_call_target="tpu_custom_call" | custom-call | flops 1019215872 | bytes 3145728 | tf_op jit(solution)/shard_map/pallas_call | solution.py:19
  30.5 0.1 collective-permute-start.6
  30.5 0.0 collective-permute-done.7.refs_3_.refs_16_
  30.5 1.8 %shard_map.75 = (bf16[30,2,32,128]{3,2,1,0:T(8,128)(2,1)S(1)}, bf16[30,2,32,128]{3,2,1,0:T(8,128)(2,1)S(1)}, bf16[28,2,32,128]{3,2,1,0:T(8,128)(2,1)S(1)}) custom-call(bf16[32,2,16,128]{3,2,1,0:T(8,128)(2,1)S(1)} %get-tuple-element.31.refs_4_.refs_0_.refs_13_, bf16[32,2,16,128]{3,2,1,0:T(8,128)(2,1)S(1)} %shard_map.69.refs_5_.refs_1_.refs_14_, ...), custom_call_target="tpu_custom_call" | custom-call | flops 679477248 | bytes 2359296 | tf_op jit(solution)/shard_map/pallas_call | solution.py:19
  32.3 0.7 %collective-permute-start.9 = (bf16[28,2,32,128]{3,2,1,0:T(8,128)(2,1)S(1)}, bf16[28,2,32,128]{3,2,1,0:T(8,128)(2,1)S(1)}, u32[]{:S(2)}, u32[]{:S(2)}) collective-permute-start(bf16[28,2,32,128]{3,2,1,0:T(8,128)(2,1)S(1)} %get-tuple-element.43.refs_4_), channel_id=1, source_target_pairs={{0,2},{2,4},{4,6},{6,8},{8,10},{10,12},{12,14},{14,16},{16,18},{18... | collective-permute-start | bytes 1376264 | tf_op jit(solution)/shard_map/ppermute | solution.py:441
  33.1 7.2 %shard_map.76 = (f32[2,7,16,128]{3,2,1,0:T(8,128)S(1)}, f32[2,7,16,128]{3,2,1,0:T(8,128)S(1)}, bf16[26,2,32,128]{3,2,1,0:T(8,128)(2,1)S(1)}) custom-call(bf16[30,2,32,128]{3,2,1,0:T(8,128)(2,1)S(1)} %get-tuple-element.39.refs_0_, bf16[30,2,32,128]{3,2,1,0:T(8,128)(2,1)S(1)} %get-tuple-element.40.refs_4_.refs_1_, ...), custom_call_target="tpu_custom_call" | custom-call | tf_op jit(solution)/shard_map/pallas_call | solution.py:19
  40.2 0.1 collective-permute-start.8
  40.3 1.3 %collective-permute-done.8.two = f32[2,7,16,128]{3,2,1,0:T(8,128)S(1)} collective-permute-done((f32[2,7,16,128]{3,2,1,0:T(8,128)S(1)}, f32[2,7,16,128]{3,2,1,0:T(8,128)S(1)}, u32[]{:S(2)}, u32[]{:S(2)}) %collective-permute-start.8) | collective-permute-done | bytes 114720 | tf_op jit(solution)/shard_map/ppermute | solution.py:554
  41.6 0.0 collective-permute-done.6.after.refs_5_
  41.6 1.8 %collective-permute-start.10 = (f32[7,16,128]{2,1,0:T(8,128)S(1)}, f32[7,16,128]{2,1,0:T(8,128)S(1)}, u32[]{:S(2)}, u32[]{:S(2)}) collective-permute-start(f32[7,16,128]{2,1,0:T(8,128)S(1)} %get-tuple-element.54), channel_id=1, source_target_pairs={{0,1},{1,0},{2,3},{3,2},{4,5},{5,4},{6,7},{7,6},{8,9},{9,8},{10,11... | collective-permute-start | bytes 172040 | tf_op jit(solution)/shard_map/ppermute | solution.py:438
  43.4 0.4 collective-permute-start.12
  43.8 1.4 %collective-permute-start.11 = (f32[7,16,128]{2,1,0:T(8,128)S(1)}, f32[7,16,128]{2,1,0:T(8,128)S(1)}, u32[]{:S(2)}, u32[]{:S(2)}) collective-permute-start(f32[7,16,128]{2,1,0:T(8,128)S(1)} %get-tuple-element.50.after.refs_1_), channel_id=1, source_target_pairs={{0,4},{2,6},{4,0},{6,2},{8,12},{10,14},{12,8},{14,10},{16,20},{18,... | collective-permute-start | bytes 172040 | tf_op jit(solution)/shard_map/ppermute | solution.py:554
  45.2 0.0 collective-permute-done.9.refs_2_
  45.2 2.8 %shard_map.78 = (bf16[24,4,16,128]{3,2,1,0:T(8,128)(2,1)S(1)}, bf16[24,4,16,128]{3,2,1,0:T(8,128)(2,1)S(1)}) custom-call(f32[7,16,128]{2,1,0:T(8,128)S(1)} %get-tuple-element.50.after.refs_1_, bf16[192,384]{1,0:T(8,128)(2,1)S(1)} %get-tuple-element.44.refs_5_.refs_0_, bf16[192,384]{1,0:T(8,128)(2,1)S(1)} %get-tuple-element.51.refs_1_, ...), custom_call_target="tpu_custom_call" | custom-call | flops 1358954496 | bytes 2359296 | tf_op jit(solution)/shard_map/pallas_call | solution.py:19
  48.0 0.0 collective-permute-done.10.refs_2_
  48.0 0.6 %collective-permute-done.11.refs_3_ = f32[7,16,128]{2,1,0:T(8,128)S(1)} collective-permute-done((f32[7,16,128]{2,1,0:T(8,128)S(1)}, f32[7,16,128]{2,1,0:T(8,128)S(1)}, u32[]{:S(2)}, u32[]{:S(2)}) %collective-permute-start.11) | collective-permute-done | bytes 57376 | tf_op jit(solution)/shard_map/ppermute | solution.py:554
  48.7 0.0 collective-permute-done.12.refs_4_
  48.7 1.3 %collective-permute-start.17 = (bf16[24,4,16,128]{3,2,1,0:T(8,128)(2,1)S(1)}, bf16[24,4,16,128]{3,2,1,0:T(8,128)(2,1)S(1)}, u32[]{:S(2)}, u32[]{:S(2)}) collective-permute-start(bf16[24,4,16,128]{3,2,1,0:T(8,128)(2,1)S(1)} %shard_map.81), channel_id=1, source_target_pairs={{0,1},{1,0},{2,3},{3,2},{4,5},{5,4},{6,7},{7,6},{8,9},{9,8},{10,11... | collective-permute-start | bytes 1179656 | tf_op jit(solution)/shard_map/ppermute | solution.py:438
  50.0 1.5 %collective-permute-start.13 = (f32[7,16,128]{2,1,0:T(8,128)S(1)}, f32[7,16,128]{2,1,0:T(8,128)S(1)}, u32[]{:S(2)}, u32[]{:S(2)}) collective-permute-start(f32[7,16,128]{2,1,0:T(8,128)S(1)} %shard_map.79.refs_0_.refs_1_), channel_id=1, source_target_pairs={{0,8},{2,10},{4,12},{6,14},{8,0},{10,2},{12,4},{14,6},{16,24},{18,... | collective-permute-start | bytes 172040 | tf_op jit(solution)/shard_map/ppermute | solution.py:554
  51.5 3.1 %collective-permute-start.14 = (f32[7,16,128]{2,1,0:T(8,128)S(1)}, f32[7,16,128]{2,1,0:T(8,128)S(1)}, u32[]{:S(2)}, u32[]{:S(2)}) collective-permute-start(f32[7,16,128]{2,1,0:T(8,128)S(1)} %shard_map.79.refs_0_.refs_1_), channel_id=1, source_target_pairs={{0,16},{2,18},{4,20},{6,22},{8,24},{10,26},{12,28},{14,30},{16,0},... | collective-permute-start | bytes 172040 | tf_op jit(solution)/shard_map/ppermute | solution.py:554
  54.6 0.0 collective-permute-start.15
  54.6 0.0 collective-permute-done.13.refs_1_
  54.6 3.1 %collective-permute-done.14.refs_2_ = f32[7,16,128]{2,1,0:T(8,128)S(1)} collective-permute-done((f32[7,16,128]{2,1,0:T(8,128)S(1)}, f32[7,16,128]{2,1,0:T(8,128)S(1)}, u32[]{:S(2)}, u32[]{:S(2)}) %collective-permute-start.14) | collective-permute-done | bytes 57376 | tf_op jit(solution)/shard_map/ppermute | solution.py:554
  57.7 2.9 %collective-permute-done.15.refs_3_ = f32[7,16,128]{2,1,0:T(8,128)S(1)} collective-permute-done((f32[7,16,128]{2,1,0:T(8,128)S(1)}, f32[7,16,128]{2,1,0:T(8,128)S(1)}, u32[]{:S(2)}, u32[]{:S(2)}) %collective-permute-start.15) | collective-permute-done | bytes 57376 | tf_op jit(solution)/shard_map/ppermute | solution.py:554
  60.6 0.1 collective-permute-start.16
  60.6 1.2 %collective-permute-done.16.refs_1_ = f32[7,16,128]{2,1,0:T(8,128)S(1)} collective-permute-done((f32[7,16,128]{2,1,0:T(8,128)S(1)}, f32[7,16,128]{2,1,0:T(8,128)S(1)}, u32[]{:S(2)}, u32[]{:S(2)}) %collective-permute-start.16) | collective-permute-done | bytes 57376 | tf_op jit(solution)/shard_map/ppermute | solution.py:554
  61.9 0.0 collective-permute-done.17.refs_3_
  61.9 2.0 %shard_map.82 = (bf16[16,4,48,128]{3,2,1,0:T(8,128)(2,1)}, f32[27,16,32]{2,1,0:T(8,128)}, f32[27,16,32]{2,1,0:T(8,128)}) custom-call(f32[7,16,128]{2,1,0:T(8,128)S(1)} %shard_map.80.refs_0_, f32[7,16,128]{2,1,0:T(8,128)S(1)} %collective-permute-done.16.refs_1_, bf16[24,4,16,128]{3,2,1,0:T(8,128)(2,1)S(1)} %get-tuple-element.53.refs_0_.refs_2_, ...), custom_call_target="tpu_custom_call" | custom-call | bytes 1572864 | tf_op jit(solution)/shard_map/pallas_call | solution.py:19
  (7 shorter events, 0.1 us)
Async XLA Ops:
  0.6 1.1 %copy-start.1 = (bf16[16,4,48,128]{3,2,1,0:T(8,128)(2,1)S(1)}, bf16[16,4,48,128]{3,2,1,0:T(8,128)(2,1)}, u32[]{:S(2)}) copy-start(bf16[16,4,48,128]{3,2,1,0:T(8,128)(2,1)} %x_ref.2) | copy-start | bytes 2359300
  1.8 17.5 %copy-start = (bf16[32,4,48,128]{3,2,1,0:T(8,128)(2,1)S(1)}, bf16[32,4,48,128]{3,2,1,0:T(8,128)(2,1)}, u32[]{:S(2)}) copy-start(bf16[32,4,48,128]{3,2,1,0:T(8,128)(2,1)} %x_ref.3) | copy-start | bytes 4718596
  3.1 16.2 %collective-permute-start.1 = (bf16[32,2,16,128]{3,2,1,0:T(8,128)(2,1)S(1)}, bf16[32,2,16,128]{3,2,1,0:T(8,128)(2,1)S(1)}, u32[]{:S(2)}, u32[]{:S(2)}) collective-permute-start(bf16[32,2,16,128]{3,2,1,0:T(8,128)(2,1)S(1)} %get-tuple-element.32), channel_id=1, source_target_pairs={{0,1},{1,0},{2,3},{3,2},{4,5},{5,4},{6,7},{7,6},{8,9},{9,8},{10,11... | collective-permute-start | bytes 786440 | tf_op jit(solution)/shard_map/ppermute | solution.py:438
  6.1 15.0 %collective-permute-start.4 = (bf16[32,2,16,128]{3,2,1,0:T(8,128)(2,1)S(1)}, bf16[32,2,16,128]{3,2,1,0:T(8,128)(2,1)S(1)}, u32[]{:S(2)}, u32[]{:S(2)}) collective-permute-start(bf16[32,2,16,128]{3,2,1,0:T(8,128)(2,1)S(1)} %get-tuple-element.34), channel_id=1, source_target_pairs={{0,1},{1,0},{2,3},{3,2},{4,5},{5,4},{6,7},{7,6},{8,9},{9,8},{10,11... | collective-permute-start | bytes 786440 | tf_op jit(solution)/shard_map/ppermute | solution.py:438
  6.2 14.9 %collective-permute-start.5 = (bf16[32,2,16,128]{3,2,1,0:T(8,128)(2,1)S(1)}, bf16[32,2,16,128]{3,2,1,0:T(8,128)(2,1)S(1)}, u32[]{:S(2)}, u32[]{:S(2)}) collective-permute-start(bf16[32,2,16,128]{3,2,1,0:T(8,128)(2,1)S(1)} %get-tuple-element.33.after.refs_2_.refs_11_), channel_id=1, source_target_pairs={{2,0},{4,2},{6,4},{8,6},{10,8},{12,10},{14,12},{16,14},{18,16},{20... | collective-permute-start | bytes 786440 | tf_op jit(solution)/shard_map/ppermute | solution.py:444
  10.1 0.9 %copy-start.2 = (bf16[16,27,32]{2,0,1:T(8,128)(2,1)S(1)}, bf16[16,27,32]{2,0,1:T(8,128)(2,1)}, u32[]{:S(2)}) copy-start(bf16[16,27,32]{2,0,1:T(8,128)(2,1)} %param.6) | copy-start | bytes 82948
  11.0 0.9 %copy-start.3 = (bf16[16,27,32]{2,0,1:T(8,128)(2,1)S(1)}, bf16[16,27,32]{2,0,1:T(8,128)(2,1)}, u32[]{:S(2)}) copy-start(bf16[16,27,32]{2,0,1:T(8,128)(2,1)} %param.7) | copy-start | bytes 82948
  12.0 7.3 %collective-permute-start.2 = (bf16[14,16,128]{2,1,0:T(8,128)(2,1)S(1)}, bf16[14,16,128]{2,1,0:T(8,128)(2,1)S(1)}, u32[]{:S(2)}, u32[]{:S(2)}) collective-permute-start(bf16[14,16,128]{2,1,0:T(8,128)(2,1)S(1)} %shard_map.68.after.refs_0_), channel_id=1, source_target_pairs={{0,1},{1,0},{2,3},{3,2},{4,5},{5,4},{6,7},{7,6},{8,9},{9,8},{10,11... | collective-permute-start | bytes 172040 | tf_op jit(solution)/shard_map/ppermute | solution.py:438
  13.5 12.0 %collective-permute-start = (bf16[32,2,16,128]{3,2,1,0:T(8,128)(2,1)S(1)}, bf16[32,2,16,128]{3,2,1,0:T(8,128)(2,1)S(1)}, u32[]{:S(2)}, u32[]{:S(2)}) collective-permute-start(bf16[32,2,16,128]{3,2,1,0:T(8,128)(2,1)S(1)} %get-tuple-element.31.refs_4_.refs_0_.refs_13_), channel_id=1, source_target_pairs={{0,2},{2,4},{4,6},{6,8},{8,10},{10,12},{12,14},{14,16},{16,18},{18... | collective-permute-start | bytes 786440 | tf_op jit(solution)/shard_map/ppermute | solution.py:441
  19.3 8.6 %collective-permute-start.3 = (bf16[32,2,16,128]{3,2,1,0:T(8,128)(2,1)S(1)}, bf16[32,2,16,128]{3,2,1,0:T(8,128)(2,1)S(1)}, u32[]{:S(2)}, u32[]{:S(2)}) collective-permute-start(bf16[32,2,16,128]{3,2,1,0:T(8,128)(2,1)S(1)} %shard_map.69.refs_5_.refs_1_.refs_14_), channel_id=1, source_target_pairs={{0,2},{2,4},{4,6},{6,8},{8,10},{10,12},{12,14},{14,16},{16,18},{18... | collective-permute-start | bytes 786440 | tf_op jit(solution)/shard_map/ppermute | solution.py:441
  21.1 9.4 %collective-permute-start.7 = (bf16[32,2,16,128]{3,2,1,0:T(8,128)(2,1)S(1)}, bf16[32,2,16,128]{3,2,1,0:T(8,128)(2,1)S(1)}, u32[]{:S(2)}, u32[]{:S(2)}) collective-permute-start(bf16[32,2,16,128]{3,2,1,0:T(8,128)(2,1)S(1)} %shard_map.73.refs_3_.refs_12_), channel_id=1, source_target_pairs={{2,0},{4,2},{6,4},{8,6},{10,8},{12,10},{14,12},{16,14},{18,16},{20... | collective-permute-start | bytes 786440 | tf_op jit(solution)/shard_map/ppermute | solution.py:444
  30.5 11.2 %collective-permute-start.6 = (bf16[28,2,32,128]{3,2,1,0:T(8,128)(2,1)S(1)}, bf16[28,2,32,128]{3,2,1,0:T(8,128)(2,1)S(1)}, u32[]{:S(2)}, u32[]{:S(2)}) collective-permute-start(bf16[28,2,32,128]{3,2,1,0:T(8,128)(2,1)S(1)} %get-tuple-element.38.refs_3_), channel_id=1, source_target_pairs={{2,0},{4,2},{6,4},{8,6},{10,8},{12,10},{14,12},{16,14},{18,16},{20... | collective-permute-start | bytes 1376264 | tf_op jit(solution)/shard_map/ppermute | solution.py:444
  32.3 12.9 %collective-permute-start.9 = (bf16[28,2,32,128]{3,2,1,0:T(8,128)(2,1)S(1)}, bf16[28,2,32,128]{3,2,1,0:T(8,128)(2,1)S(1)}, u32[]{:S(2)}, u32[]{:S(2)}) collective-permute-start(bf16[28,2,32,128]{3,2,1,0:T(8,128)(2,1)S(1)} %get-tuple-element.43.refs_4_), channel_id=1, source_target_pairs={{0,2},{2,4},{4,6},{6,8},{8,10},{10,12},{12,14},{14,16},{16,18},{18... | collective-permute-start | bytes 1376264 | tf_op jit(solution)/shard_map/ppermute | solution.py:441
  40.2 1.4 %collective-permute-start.8 = (f32[2,7,16,128]{3,2,1,0:T(8,128)S(1)}, f32[2,7,16,128]{3,2,1,0:T(8,128)S(1)}, u32[]{:S(2)}, u32[]{:S(2)}) collective-permute-start(f32[2,7,16,128]{3,2,1,0:T(8,128)S(1)} %get-tuple-element.49), channel_id=1, source_target_pairs={{0,2},{2,0},{4,6},{6,4},{8,10},{10,8},{12,14},{14,12},{16,18},{18,... | collective-permute-start | bytes 344072 | tf_op jit(solution)/shard_map/ppermute | solution.py:554
  41.6 6.4 %collective-permute-start.10 = (f32[7,16,128]{2,1,0:T(8,128)S(1)}, f32[7,16,128]{2,1,0:T(8,128)S(1)}, u32[]{:S(2)}, u32[]{:S(2)}) collective-permute-start(f32[7,16,128]{2,1,0:T(8,128)S(1)} %get-tuple-element.54), channel_id=1, source_target_pairs={{0,1},{1,0},{2,3},{3,2},{4,5},{5,4},{6,7},{7,6},{8,9},{9,8},{10,11... | collective-permute-start | bytes 172040 | tf_op jit(solution)/shard_map/ppermute | solution.py:438
  43.4 5.2 %collective-permute-start.12 = (f32[7,16,128]{2,1,0:T(8,128)S(1)}, f32[7,16,128]{2,1,0:T(8,128)S(1)}, u32[]{:S(2)}, u32[]{:S(2)}) collective-permute-start(f32[7,16,128]{2,1,0:T(8,128)S(1)} %get-tuple-element.54), channel_id=1, source_target_pairs={{0,5},{1,4},{2,7},{3,6},{4,1},{5,0},{6,3},{7,2},{8,13},{9,12},{10,... | collective-permute-start | bytes 172040 | tf_op jit(solution)/shard_map/ppermute | solution.py:560
  43.8 4.8 %collective-permute-start.11 = (f32[7,16,128]{2,1,0:T(8,128)S(1)}, f32[7,16,128]{2,1,0:T(8,128)S(1)}, u32[]{:S(2)}, u32[]{:S(2)}) collective-permute-start(f32[7,16,128]{2,1,0:T(8,128)S(1)} %get-tuple-element.50.after.refs_1_), channel_id=1, source_target_pairs={{0,4},{2,6},{4,0},{6,2},{8,12},{10,14},{12,8},{14,10},{16,20},{18,... | collective-permute-start | bytes 172040 | tf_op jit(solution)/shard_map/ppermute | solution.py:554
  48.7 13.2 %collective-permute-start.17 = (bf16[24,4,16,128]{3,2,1,0:T(8,128)(2,1)S(1)}, bf16[24,4,16,128]{3,2,1,0:T(8,128)(2,1)S(1)}, u32[]{:S(2)}, u32[]{:S(2)}) collective-permute-start(bf16[24,4,16,128]{3,2,1,0:T(8,128)(2,1)S(1)} %shard_map.81), channel_id=1, source_target_pairs={{0,1},{1,0},{2,3},{3,2},{4,5},{5,4},{6,7},{7,6},{8,9},{9,8},{10,11... | collective-permute-start | bytes 1179656 | tf_op jit(solution)/shard_map/ppermute | solution.py:438
  50.0 4.6 %collective-permute-start.13 = (f32[7,16,128]{2,1,0:T(8,128)S(1)}, f32[7,16,128]{2,1,0:T(8,128)S(1)}, u32[]{:S(2)}, u32[]{:S(2)}) collective-permute-start(f32[7,16,128]{2,1,0:T(8,128)S(1)} %shard_map.79.refs_0_.refs_1_), channel_id=1, source_target_pairs={{0,8},{2,10},{4,12},{6,14},{8,0},{10,2},{12,4},{14,6},{16,24},{18,... | collective-permute-start | bytes 172040 | tf_op jit(solution)/shard_map/ppermute | solution.py:554
  51.5 6.2 %collective-permute-start.14 = (f32[7,16,128]{2,1,0:T(8,128)S(1)}, f32[7,16,128]{2,1,0:T(8,128)S(1)}, u32[]{:S(2)}, u32[]{:S(2)}) collective-permute-start(f32[7,16,128]{2,1,0:T(8,128)S(1)} %shard_map.79.refs_0_.refs_1_), channel_id=1, source_target_pairs={{0,16},{2,18},{4,20},{6,22},{8,24},{10,26},{12,28},{14,30},{16,0},... | collective-permute-start | bytes 172040 | tf_op jit(solution)/shard_map/ppermute | solution.py:554
  54.6 6.0 %collective-permute-start.15 = (f32[7,16,128]{2,1,0:T(8,128)S(1)}, f32[7,16,128]{2,1,0:T(8,128)S(1)}, u32[]{:S(2)}, u32[]{:S(2)}) collective-permute-start(f32[7,16,128]{2,1,0:T(8,128)S(1)} %shard_map.79.refs_0_.refs_1_), channel_id=1, source_target_pairs={{0,24},{2,26},{4,28},{6,30},{8,16},{10,18},{12,20},{14,22},{16,8},... | collective-permute-start | bytes 172040 | tf_op jit(solution)/shard_map/ppermute | solution.py:554
  60.6 1.3 %collective-permute-start.16 = (f32[7,16,128]{2,1,0:T(8,128)S(1)}, f32[7,16,128]{2,1,0:T(8,128)S(1)}, u32[]{:S(2)}, u32[]{:S(2)}) collective-permute-start(f32[7,16,128]{2,1,0:T(8,128)S(1)} %shard_map.80.refs_0_), channel_id=1, source_target_pairs={{0,2},{2,0},{4,6},{6,4},{8,10},{10,8},{12,14},{14,12},{16,18},{18,... | collective-permute-start | bytes 172040 | tf_op jit(solution)/shard_map/ppermute | solution.py:554

commit v16 on v15

--- a/solution.py
+++ b/solution.py
@@ -488,8 +488,8 @@
         moved=matrix.size * 8,
     )
     if whole and extent > 1 and pairs > 1:
-        parts[1][-1] = relayed(parts[1][-1], *packs[1:])
-        parts[1][0] = relayed(relayed(parts[1][0], grads[0], first_wide), own_after[0])
+        parts[1][-1] = relayed(parts[1][-1], pack)
+        parts[1][0] = relayed(relayed(parts[1][0], grads[0], *packs[1:]), own_after[0])
     by_pair = [[parts[j][p] for j in range(extent)] for p in range(pairs)]
     groups = extent
     if not whole:

time: 64.1 us -> 60.8 us (0.949)
  waiting for transfers between devices: 17.1 us -> 12.8 us
  starting transfers between devices: 23.4 us -> 24.4 us
    ppermute x3, waiting for transfers between devices: 2.27 us -> 0.01 us  [to_next(): lax.ppermute(value, 'slab', [(i, (i + 1) % slabs) for i in range(slabs)])]
    ppermute x5, waiting for transfers between devices: 5.71 us -> 3.87 us  [to_chan(): lax.ppermute(value, 'chan', [(i, (i + shift) % extent) for i in range(ext...]
    ppermute x6, starting transfers between devices: 6.1 us -> 7.06 us  [stepped(): return lax.ppermute(value, 'slab', [(i, i ^ stride) for i in range(slabs)])]
  transfers between devices with their start and end apart: 18 -> 18, of which waited for: 7 -> 7; matrix products, arithmetic and copies ran while one was open for 0% -> 0% of each run, Pallas kernels for 26% -> 27%
where the time goes in v16:
time: 60.8 us; the launch traced here: 60.5 us
  starting transfers between devices  24.4 us (40%)
  Pallas kernels  19.6 us (32%)
  waiting for transfers between devices  12.8 us (21%)
  local copies, waits for them, and re-layouts  2.92 us (5%)
  between operations  0.78 us (1%)
    pallas_call x16, Pallas kernels, call(): pl.pallas_call(kernel, out_shape=outs, in_specs=[still] * loose + [whole]...  19.6 us
    ppermute x3, starting transfers between devices, to_prev(): lax.ppermute(value, 'slab', [((i + 1) % slabs, i) for i in range(slabs)])  8.99 us
    ppermute x6, waiting for transfers between devices, stepped(): return lax.ppermute(value, 'slab', [(i, i ^ stride) for i in range(slabs)])  8.9 us
    ppermute x5, starting transfers between devices, to_chan(): lax.ppermute(value, 'chan', [(i, (i + shift) % extent) for i in range(ext...  7.91 us
    ppermute x6, starting transfers between devices, stepped(): return lax.ppermute(value, 'slab', [(i, i ^ stride) for i in range(slabs)])  7.06 us
    ppermute x5, waiting for transfers between devices, to_chan(): lax.ppermute(value, 'chan', [(i, (i + shift) % extent) for i in range(ext...  3.87 us
    unnamed x8, local copies, waits for them, and re-layouts  2.92 us
  transfers between devices with their start and end apart: 18, of which 7 were waited for; matrix products, arithmetic and copies ran while one was open for 0% of the time, Pallas kernels for 27%

profile of v16, /device:TPU:0, one launch (start us, length us, event | category | flops | bytes accessed | tf_op | source)
XLA Modules:
  0.0 60.5 jit_solution(2788002857079015344)
XLA Ops:
  0.6 0.0 copy-start.1
  0.6 1.1 %copy-done.1 = bf16[16,4,48,128]{3,2,1,0:T(8,128)(2,1)S(1)} copy-done((bf16[16,4,48,128]{3,2,1,0:T(8,128)(2,1)S(1)}, bf16[16,4,48,128]{3,2,1,0:T(8,128)(2,1)}, u32[]{:S(2)}) %copy-start.1) | copy-done | bytes 786456
  1.8 0.0 copy-start
  1.8 1.3 %shard_map.67 = (bf16[32,2,16,128]{3,2,1,0:T(8,128)(2,1)S(1)}, bf16[32,2,16,128]{3,2,1,0:T(8,128)(2,1)S(1)}, bf16[32,2,16,128]{3,2,1,0:T(8,128)(2,1)S(1)}, bf16[32,2,16,128]{3,2,1,0:T(8,128)(2,1)S(1)}) custom-call(bf16[16,4,48,128]{3,2,1,0:T(8,128)(2,1)S(1)} %copy-done.1), custom_call_target="tpu_custom_call" | custom-call | bytes 2359296 | tf_op jit(solution)/shard_map/pallas_call | solution.py:19
  3.1 3.0 %collective-permute-start.1 = (bf16[32,2,16,128]{3,2,1,0:T(8,128)(2,1)S(1)}, bf16[32,2,16,128]{3,2,1,0:T(8,128)(2,1)S(1)}, u32[]{:S(2)}, u32[]{:S(2)}) collective-permute-start(bf16[32,2,16,128]{3,2,1,0:T(8,128)(2,1)S(1)} %get-tuple-element.32), channel_id=1, source_target_pairs={{0,1},{1,0},{2,3},{3,2},{4,5},{5,4},{6,7},{7,6},{8,9},{9,8},{10,11... | collective-permute-start | bytes 786440 | tf_op jit(solution)/shard_map/ppermute | solution.py:438
  6.1 0.1 collective-permute-start.3
  6.2 3.9 %collective-permute-start.5 = (bf16[32,2,16,128]{3,2,1,0:T(8,128)(2,1)S(1)}, bf16[32,2,16,128]{3,2,1,0:T(8,128)(2,1)S(1)}, u32[]{:S(2)}, u32[]{:S(2)}) collective-permute-start(bf16[32,2,16,128]{3,2,1,0:T(8,128)(2,1)S(1)} %get-tuple-element.33.after.refs_2_.refs_11_), channel_id=1, source_target_pairs={{2,0},{4,2},{6,4},{8,6},{10,8},{12,10},{14,12},{16,14},{18,16},{20... | collective-permute-start | bytes 786440 | tf_op jit(solution)/shard_map/ppermute | solution.py:444
  10.1 0.0 collective-permute-start
  10.1 0.0 copy-start.2
  10.1 0.9 %copy-done.2 = bf16[16,27,32]{2,0,1:T(8,128)(2,1)S(1)} copy-done((bf16[16,27,32]{2,0,1:T(8,128)(2,1)S(1)}, bf16[16,27,32]{2,0,1:T(8,128)(2,1)}, u32[]{:S(2)}) %copy-start.2) | copy-done | bytes 27672
  11.0 0.0 copy-start.3
  11.0 0.9 %copy-done.3 = bf16[16,27,32]{2,0,1:T(8,128)(2,1)S(1)} copy-done((bf16[16,27,32]{2,0,1:T(8,128)(2,1)S(1)}, bf16[16,27,32]{2,0,1:T(8,128)(2,1)}, u32[]{:S(2)}) %copy-start.3) | copy-done | bytes 27672
  11.9 0.1 shard_map.68.refs_1_.after.refs_0_
  12.0 1.2 %collective-permute-done.1.refs_0_ = bf16[32,2,16,128]{3,2,1,0:T(8,128)(2,1)S(1)} collective-permute-done((bf16[32,2,16,128]{3,2,1,0:T(8,128)(2,1)S(1)}, bf16[32,2,16,128]{3,2,1,0:T(8,128)(2,1)S(1)}, u32[]{:S(2)}, u32[]{:S(2)}) %collective-permute-start.1) | collective-permute-done | bytes 262176 | tf_op jit(solution)/shard_map/ppermute | solution.py:438
  13.2 0.0 collective-permute-start.2
  13.2 2.1 %collective-permute-start.4 = (bf16[14,16,128]{2,1,0:T(8,128)(2,1)S(1)}, bf16[14,16,128]{2,1,0:T(8,128)(2,1)S(1)}, u32[]{:S(2)}, u32[]{:S(2)}) collective-permute-start(bf16[14,16,128]{2,1,0:T(8,128)(2,1)S(1)} %shard_map.68.refs_1_.after.refs_0_), channel_id=1, source_target_pairs={{0,1},{1,0},{2,3},{3,2},{4,5},{5,4},{6,7},{7,6},{8,9},{9,8},{10,11... | collective-permute-start | bytes 172040 | tf_op jit(solution)/shard_map/ppermute | solution.py:438
  15.3 0.0 copy-done
  15.3 1.2 %shard_map.70 = (bf16[28,2,32,128]{3,2,1,0:T(8,128)(2,1)S(1)}, bf16[28,2,32,128]{3,2,1,0:T(8,128)(2,1)S(1)}) custom-call(bf16[14,16,128]{2,1,0:T(8,128)(2,1)S(1)} %shard_map.68.refs_1_.after.refs_0_, bf16[32,4,48,128]{3,2,1,0:T(8,128)(2,1)S(1)} %copy-done), custom_call_target="tpu_custom_call" | custom-call | bytes 3145728 | tf_op jit(solution)/shard_map/pallas_call | solution.py:19
  16.5 2.6 %collective-permute-done.4.refs_2_.refs_1_ = bf16[14,16,128]{2,1,0:T(8,128)(2,1)S(1)} collective-permute-done((bf16[14,16,128]{2,1,0:T(8,128)(2,1)S(1)}, bf16[14,16,128]{2,1,0:T(8,128)(2,1)S(1)}, u32[]{:S(2)}, u32[]{:S(2)}) %collective-permute-start.4) | collective-permute-done | bytes 57376 | tf_op jit(solution)/shard_map/ppermute | solution.py:438
  19.2 0.0 collective-permute-done.3.refs_0_
  19.2 0.0 collective-permute-done.5.refs_1_.refs_2_.refs_15_
  19.2 3.5 %collective-permute-start.7 = (bf16[32,2,16,128]{3,2,1,0:T(8,128)(2,1)S(1)}, bf16[32,2,16,128]{3,2,1,0:T(8,128)(2,1)S(1)}, u32[]{:S(2)}, u32[]{:S(2)}) collective-permute-start(bf16[32,2,16,128]{3,2,1,0:T(8,128)(2,1)S(1)} %shard_map.72.refs_3_.refs_12_), channel_id=1, source_target_pairs={{2,0},{4,2},{6,4},{8,6},{10,8},{12,10},{14,12},{16,14},{18,16},{20... | collective-permute-start | bytes 786440 | tf_op jit(solution)/shard_map/ppermute | solution.py:444
  22.7 0.5 shard_map.73
  23.2 0.0 collective-permute-done.refs_0_.refs_9_
  23.2 0.0 collective-permute-done.2.refs_1_.refs_10_
  23.2 2.6 %shard_map.74 = (bf16[30,2,32,128]{3,2,1,0:T(8,128)(2,1)S(1)}, bf16[30,2,32,128]{3,2,1,0:T(8,128)(2,1)S(1)}, bf16[30,2,32,128]{3,2,1,0:T(8,128)(2,1)S(1)}, bf16[...) custom-call(bf16[32,2,16,128]{3,2,1,0:T(8,128)(2,1)S(1)} %collective-permute-done.refs_0_.refs_9_, ...), custom_call_target="tpu_custom_call" | custom-call | flops 1019215872 | bytes 3145728 | tf_op jit(solution)/shard_map/pallas_call | solution.py:19
  25.8 1.6 %collective-permute-start.6 = (bf16[28,2,32,128]{3,2,1,0:T(8,128)(2,1)S(1)}, bf16[28,2,32,128]{3,2,1,0:T(8,128)(2,1)S(1)}, u32[]{:S(2)}, u32[]{:S(2)}) collective-permute-start(bf16[28,2,32,128]{3,2,1,0:T(8,128)(2,1)S(1)} %get-tuple-element.38.refs_3_), channel_id=1, source_target_pairs={{2,0},{4,2},{6,4},{8,6},{10,8},{12,10},{14,12},{16,14},{18,16},{20... | collective-permute-start | bytes 1376264 | tf_op jit(solution)/shard_map/ppermute | solution.py:444
  27.4 0.0 collective-permute-done.7.refs_3_.refs_16_
  27.4 1.8 %shard_map.75 = (bf16[30,2,32,128]{3,2,1,0:T(8,128)(2,1)S(1)}, bf16[30,2,32,128]{3,2,1,0:T(8,128)(2,1)S(1)}, bf16[28,2,32,128]{3,2,1,0:T(8,128)(2,1)S(1)}) custom-call(bf16[32,2,16,128]{3,2,1,0:T(8,128)(2,1)S(1)} %get-tuple-element.31.refs_4_.refs_0_.refs_13_, bf16[32,2,16,128]{3,2,1,0:T(8,128)(2,1)S(1)} %shard_map.69.refs_5_.refs_1_.refs_14_, ...), custom_call_target="tpu_custom_call" | custom-call | flops 679477248 | bytes 2359296 | tf_op jit(solution)/shard_map/pallas_call | solution.py:19
  29.2 0.2 collective-permute-start.9
  29.5 7.2 %shard_map.76 = (f32[2,7,16,128]{3,2,1,0:T(8,128)S(1)}, f32[2,7,16,128]{3,2,1,0:T(8,128)S(1)}, bf16[26,2,32,128]{3,2,1,0:T(8,128)(2,1)S(1)}) custom-call(bf16[30,2,32,128]{3,2,1,0:T(8,128)(2,1)S(1)} %get-tuple-element.39.refs_0_, bf16[30,2,32,128]{3,2,1,0:T(8,128)(2,1)S(1)} %get-tuple-element.40.refs_4_.refs_1_, ...), custom_call_target="tpu_custom_call" | custom-call | tf_op jit(solution)/shard_map/pallas_call | solution.py:19
  36.6 0.1 collective-permute-start.8
  36.7 1.3 %collective-permute-done.8.two = f32[2,7,16,128]{3,2,1,0:T(8,128)S(1)} collective-permute-done((f32[2,7,16,128]{3,2,1,0:T(8,128)S(1)}, f32[2,7,16,128]{3,2,1,0:T(8,128)S(1)}, u32[]{:S(2)}, u32[]{:S(2)}) %collective-permute-start.8) | collective-permute-done | bytes 114720 | tf_op jit(solution)/shard_map/ppermute | solution.py:554
  38.0 0.0 collective-permute-done.6.after.refs_5_
  38.0 1.6 %collective-permute-start.10 = (f32[7,16,128]{2,1,0:T(8,128)S(1)}, f32[7,16,128]{2,1,0:T(8,128)S(1)}, u32[]{:S(2)}, u32[]{:S(2)}) collective-permute-start(f32[7,16,128]{2,1,0:T(8,128)S(1)} %get-tuple-element.54), channel_id=1, source_target_pairs={{0,1},{1,0},{2,3},{3,2},{4,5},{5,4},{6,7},{7,6},{8,9},{9,8},{10,11... | collective-permute-start | bytes 172040 | tf_op jit(solution)/shard_map/ppermute | solution.py:438
  39.6 0.2 collective-permute-start.12
  39.8 1.8 %collective-permute-start.11 = (f32[7,16,128]{2,1,0:T(8,128)S(1)}, f32[7,16,128]{2,1,0:T(8,128)S(1)}, u32[]{:S(2)}, u32[]{:S(2)}) collective-permute-start(f32[7,16,128]{2,1,0:T(8,128)S(1)} %get-tuple-element.50.after.refs_1_), channel_id=1, source_target_pairs={{0,4},{2,6},{4,0},{6,2},{8,12},{10,14},{12,8},{14,10},{16,20},{18,... | collective-permute-start | bytes 172040 | tf_op jit(solution)/shard_map/ppermute | solution.py:554
  41.6 0.0 collective-permute-done.9.refs_2_
  41.6 2.8 %shard_map.78 = (bf16[24,4,16,128]{3,2,1,0:T(8,128)(2,1)S(1)}, bf16[24,4,16,128]{3,2,1,0:T(8,128)(2,1)S(1)}) custom-call(f32[7,16,128]{2,1,0:T(8,128)S(1)} %get-tuple-element.50.after.refs_1_, bf16[192,384]{1,0:T(8,128)(2,1)S(1)} %get-tuple-element.44.refs_5_.refs_0_, bf16[192,384]{1,0:T(8,128)(2,1)S(1)} %get-tuple-element.51.refs_1_, ...), custom_call_target="tpu_custom_call" | custom-call | flops 1358954496 | bytes 2359296 | tf_op jit(solution)/shard_map/pallas_call | solution.py:19
  44.4 0.0 collective-permute-done.10.refs_2_
  44.4 0.4 collective-permute-done.11.refs_3_
  44.8 0.0 collective-permute-done.12.refs_4_
  44.8 1.2 %collective-permute-start.17 = (bf16[24,4,16,128]{3,2,1,0:T(8,128)(2,1)S(1)}, bf16[24,4,16,128]{3,2,1,0:T(8,128)(2,1)S(1)}, u32[]{:S(2)}, u32[]{:S(2)}) collective-permute-start(bf16[24,4,16,128]{3,2,1,0:T(8,128)(2,1)S(1)} %shard_map.81), channel_id=1, source_target_pairs={{0,1},{1,0},{2,3},{3,2},{4,5},{5,4},{6,7},{7,6},{8,9},{9,8},{10,11... | collective-permute-start | bytes 1179656 | tf_op jit(solution)/shard_map/ppermute | solution.py:438
  46.1 1.1 %collective-permute-start.13 = (f32[7,16,128]{2,1,0:T(8,128)S(1)}, f32[7,16,128]{2,1,0:T(8,128)S(1)}, u32[]{:S(2)}, u32[]{:S(2)}) collective-permute-start(f32[7,16,128]{2,1,0:T(8,128)S(1)} %shard_map.79.refs_0_.refs_1_), channel_id=1, source_target_pairs={{0,8},{2,10},{4,12},{6,14},{8,0},{10,2},{12,4},{14,6},{16,24},{18,... | collective-permute-start | bytes 172040 | tf_op jit(solution)/shard_map/ppermute | solution.py:554
  47.2 4.0 %collective-permute-start.14 = (f32[7,16,128]{2,1,0:T(8,128)S(1)}, f32[7,16,128]{2,1,0:T(8,128)S(1)}, u32[]{:S(2)}, u32[]{:S(2)}) collective-permute-start(f32[7,16,128]{2,1,0:T(8,128)S(1)} %shard_map.79.refs_0_.refs_1_), channel_id=1, source_target_pairs={{0,16},{2,18},{4,20},{6,22},{8,24},{10,26},{12,28},{14,30},{16,0},... | collective-permute-start | bytes 172040 | tf_op jit(solution)/shard_map/ppermute | solution.py:554
  51.2 0.0 collective-permute-start.15
  51.2 0.0 collective-permute-done.13.refs_1_
  51.2 3.1 %collective-permute-done.14.refs_2_ = f32[7,16,128]{2,1,0:T(8,128)S(1)} collective-permute-done((f32[7,16,128]{2,1,0:T(8,128)S(1)}, f32[7,16,128]{2,1,0:T(8,128)S(1)}, u32[]{:S(2)}, u32[]{:S(2)}) %collective-permute-start.14) | collective-permute-done | bytes 57376 | tf_op jit(solution)/shard_map/ppermute | solution.py:554
  54.3 2.9 %collective-permute-done.15.refs_3_ = f32[7,16,128]{2,1,0:T(8,128)S(1)} collective-permute-done((f32[7,16,128]{2,1,0:T(8,128)S(1)}, f32[7,16,128]{2,1,0:T(8,128)S(1)}, u32[]{:S(2)}, u32[]{:S(2)}) %collective-permute-start.15) | collective-permute-done | bytes 57376 | tf_op jit(solution)/shard_map/ppermute | solution.py:554
  57.2 0.1 collective-permute-start.16
  57.3 1.2 %collective-permute-done.16.refs_1_ = f32[7,16,128]{2,1,0:T(8,128)S(1)} collective-permute-done((f32[7,16,128]{2,1,0:T(8,128)S(1)}, f32[7,16,128]{2,1,0:T(8,128)S(1)}, u32[]{:S(2)}, u32[]{:S(2)}) %collective-permute-start.16) | collective-permute-done | bytes 57376 | tf_op jit(solution)/shard_map/ppermute | solution.py:554
  58.5 0.0 collective-permute-done.17.refs_3_
  58.5 2.0 %shard_map.82 = (bf16[16,4,48,128]{3,2,1,0:T(8,128)(2,1)}, f32[27,16,32]{2,1,0:T(8,128)}, f32[27,16,32]{2,1,0:T(8,128)}) custom-call(f32[7,16,128]{2,1,0:T(8,128)S(1)} %shard_map.80.refs_0_, f32[7,16,128]{2,1,0:T(8,128)S(1)} %collective-permute-done.16.refs_1_, bf16[24,4,16,128]{3,2,1,0:T(8,128)(2,1)S(1)} %get-tuple-element.53.refs_0_.refs_2_, ...), custom_call_target="tpu_custom_call" | custom-call | bytes 1572864 | tf_op jit(solution)/shard_map/pallas_call | solution.py:19
  (7 shorter events, 0.1 us)
Async XLA Ops:
  0.6 1.1 %copy-start.1 = (bf16[16,4,48,128]{3,2,1,0:T(8,128)(2,1)S(1)}, bf16[16,4,48,128]{3,2,1,0:T(8,128)(2,1)}, u32[]{:S(2)}) copy-start(bf16[16,4,48,128]{3,2,1,0:T(8,128)(2,1)} %x_ref.2) | copy-start | bytes 2359300
  1.8 13.5 %copy-start = (bf16[32,4,48,128]{3,2,1,0:T(8,128)(2,1)S(1)}, bf16[32,4,48,128]{3,2,1,0:T(8,128)(2,1)}, u32[]{:S(2)}) copy-start(bf16[32,4,48,128]{3,2,1,0:T(8,128)(2,1)} %x_ref.3) | copy-start | bytes 4718596
  3.1 10.1 %collective-permute-start.1 = (bf16[32,2,16,128]{3,2,1,0:T(8,128)(2,1)S(1)}, bf16[32,2,16,128]{3,2,1,0:T(8,128)(2,1)S(1)}, u32[]{:S(2)}, u32[]{:S(2)}) collective-permute-start(bf16[32,2,16,128]{3,2,1,0:T(8,128)(2,1)S(1)} %get-tuple-element.32), channel_id=1, source_target_pairs={{0,1},{1,0},{2,3},{3,2},{4,5},{5,4},{6,7},{7,6},{8,9},{9,8},{10,11... | collective-permute-start | bytes 786440 | tf_op jit(solution)/shard_map/ppermute | solution.py:438
  6.1 13.1 %collective-permute-start.3 = (bf16[32,2,16,128]{3,2,1,0:T(8,128)(2,1)S(1)}, bf16[32,2,16,128]{3,2,1,0:T(8,128)(2,1)S(1)}, u32[]{:S(2)}, u32[]{:S(2)}) collective-permute-start(bf16[32,2,16,128]{3,2,1,0:T(8,128)(2,1)S(1)} %get-tuple-element.34), channel_id=1, source_target_pairs={{0,1},{1,0},{2,3},{3,2},{4,5},{5,4},{6,7},{7,6},{8,9},{9,8},{10,11... | collective-permute-start | bytes 786440 | tf_op jit(solution)/shard_map/ppermute | solution.py:438
  6.2 13.0 %collective-permute-start.5 = (bf16[32,2,16,128]{3,2,1,0:T(8,128)(2,1)S(1)}, bf16[32,2,16,128]{3,2,1,0:T(8,128)(2,1)S(1)}, u32[]{:S(2)}, u32[]{:S(2)}) collective-permute-start(bf16[32,2,16,128]{3,2,1,0:T(8,128)(2,1)S(1)} %get-tuple-element.33.after.refs_2_.refs_11_), channel_id=1, source_target_pairs={{2,0},{4,2},{6,4},{8,6},{10,8},{12,10},{14,12},{16,14},{18,16},{20... | collective-permute-start | bytes 786440 | tf_op jit(solution)/shard_map/ppermute | solution.py:444
  10.1 13.2 %collective-permute-start = (bf16[32,2,16,128]{3,2,1,0:T(8,128)(2,1)S(1)}, bf16[32,2,16,128]{3,2,1,0:T(8,128)(2,1)S(1)}, u32[]{:S(2)}, u32[]{:S(2)}) collective-permute-start(bf16[32,2,16,128]{3,2,1,0:T(8,128)(2,1)S(1)} %get-tuple-element.31.refs_4_.refs_0_.refs_13_), channel_id=1, source_target_pairs={{0,2},{2,4},{4,6},{6,8},{8,10},{10,12},{12,14},{14,16},{16,18},{18... | collective-permute-start | bytes 786440 | tf_op jit(solution)/shard_map/ppermute | solution.py:441
  10.1 0.9 %copy-start.2 = (bf16[16,27,32]{2,0,1:T(8,128)(2,1)S(1)}, bf16[16,27,32]{2,0,1:T(8,128)(2,1)}, u32[]{:S(2)}) copy-start(bf16[16,27,32]{2,0,1:T(8,128)(2,1)} %param.6) | copy-start | bytes 82948
  11.0 0.9 %copy-start.3 = (bf16[16,27,32]{2,0,1:T(8,128)(2,1)S(1)}, bf16[16,27,32]{2,0,1:T(8,128)(2,1)}, u32[]{:S(2)}) copy-start(bf16[16,27,32]{2,0,1:T(8,128)(2,1)} %param.7) | copy-start | bytes 82948
  13.2 10.0 %collective-permute-start.2 = (bf16[32,2,16,128]{3,2,1,0:T(8,128)(2,1)S(1)}, bf16[32,2,16,128]{3,2,1,0:T(8,128)(2,1)S(1)}, u32[]{:S(2)}, u32[]{:S(2)}) collective-permute-start(bf16[32,2,16,128]{3,2,1,0:T(8,128)(2,1)S(1)} %shard_map.69.refs_5_.refs_1_.refs_14_), channel_id=1, source_target_pairs={{0,2},{2,4},{4,6},{6,8},{8,10},{10,12},{12,14},{14,16},{16,18},{18... | collective-permute-start | bytes 786440 | tf_op jit(solution)/shard_map/ppermute | solution.py:441
  13.2 5.9 %collective-permute-start.4 = (bf16[14,16,128]{2,1,0:T(8,128)(2,1)S(1)}, bf16[14,16,128]{2,1,0:T(8,128)(2,1)S(1)}, u32[]{:S(2)}, u32[]{:S(2)}) collective-permute-start(bf16[14,16,128]{2,1,0:T(8,128)(2,1)S(1)} %shard_map.68.refs_1_.after.refs_0_), channel_id=1, source_target_pairs={{0,1},{1,0},{2,3},{3,2},{4,5},{5,4},{6,7},{7,6},{8,9},{9,8},{10,11... | collective-permute-start | bytes 172040 | tf_op jit(solution)/shard_map/ppermute | solution.py:438
  19.2 8.2 %collective-permute-start.7 = (bf16[32,2,16,128]{3,2,1,0:T(8,128)(2,1)S(1)}, bf16[32,2,16,128]{3,2,1,0:T(8,128)(2,1)S(1)}, u32[]{:S(2)}, u32[]{:S(2)}) collective-permute-start(bf16[32,2,16,128]{3,2,1,0:T(8,128)(2,1)S(1)} %shard_map.72.refs_3_.refs_12_), channel_id=1, source_target_pairs={{2,0},{4,2},{6,4},{8,6},{10,8},{12,10},{14,12},{16,14},{18,16},{20... | collective-permute-start | bytes 786440 | tf_op jit(solution)/shard_map/ppermute | solution.py:444
  25.8 12.2 %collective-permute-start.6 = (bf16[28,2,32,128]{3,2,1,0:T(8,128)(2,1)S(1)}, bf16[28,2,32,128]{3,2,1,0:T(8,128)(2,1)S(1)}, u32[]{:S(2)}, u32[]{:S(2)}) collective-permute-start(bf16[28,2,32,128]{3,2,1,0:T(8,128)(2,1)S(1)} %get-tuple-element.38.refs_3_), channel_id=1, source_target_pairs={{2,0},{4,2},{6,4},{8,6},{10,8},{12,10},{14,12},{16,14},{18,16},{20... | collective-permute-start | bytes 1376264 | tf_op jit(solution)/shard_map/ppermute | solution.py:444
  29.2 12.4 %collective-permute-start.9 = (bf16[28,2,32,128]{3,2,1,0:T(8,128)(2,1)S(1)}, bf16[28,2,32,128]{3,2,1,0:T(8,128)(2,1)S(1)}, u32[]{:S(2)}, u32[]{:S(2)}) collective-permute-start(bf16[28,2,32,128]{3,2,1,0:T(8,128)(2,1)S(1)} %get-tuple-element.43.refs_4_), channel_id=1, source_target_pairs={{0,2},{2,4},{4,6},{6,8},{8,10},{10,12},{12,14},{14,16},{16,18},{18... | collective-permute-start | bytes 1376264 | tf_op jit(solution)/shard_map/ppermute | solution.py:441
  36.6 1.4 %collective-permute-start.8 = (f32[2,7,16,128]{3,2,1,0:T(8,128)S(1)}, f32[2,7,16,128]{3,2,1,0:T(8,128)S(1)}, u32[]{:S(2)}, u32[]{:S(2)}) collective-permute-start(f32[2,7,16,128]{3,2,1,0:T(8,128)S(1)} %get-tuple-element.49), channel_id=1, source_target_pairs={{0,2},{2,0},{4,6},{6,4},{8,10},{10,8},{12,14},{14,12},{16,18},{18,... | collective-permute-start | bytes 344072 | tf_op jit(solution)/shard_map/ppermute | solution.py:554
  38.0 6.4 %collective-permute-start.10 = (f32[7,16,128]{2,1,0:T(8,128)S(1)}, f32[7,16,128]{2,1,0:T(8,128)S(1)}, u32[]{:S(2)}, u32[]{:S(2)}) collective-permute-start(f32[7,16,128]{2,1,0:T(8,128)S(1)} %get-tuple-element.54), channel_id=1, source_target_pairs={{0,1},{1,0},{2,3},{3,2},{4,5},{5,4},{6,7},{7,6},{8,9},{9,8},{10,11... | collective-permute-start | bytes 172040 | tf_op jit(solution)/shard_map/ppermute | solution.py:438
  39.6 5.2 %collective-permute-start.12 = (f32[7,16,128]{2,1,0:T(8,128)S(1)}, f32[7,16,128]{2,1,0:T(8,128)S(1)}, u32[]{:S(2)}, u32[]{:S(2)}) collective-permute-start(f32[7,16,128]{2,1,0:T(8,128)S(1)} %get-tuple-element.54), channel_id=1, source_target_pairs={{0,5},{1,4},{2,7},{3,6},{4,1},{5,0},{6,3},{7,2},{8,13},{9,12},{10,... | collective-permute-start | bytes 172040 | tf_op jit(solution)/shard_map/ppermute | solution.py:560
  39.8 5.0 %collective-permute-start.11 = (f32[7,16,128]{2,1,0:T(8,128)S(1)}, f32[7,16,128]{2,1,0:T(8,128)S(1)}, u32[]{:S(2)}, u32[]{:S(2)}) collective-permute-start(f32[7,16,128]{2,1,0:T(8,128)S(1)} %get-tuple-element.50.after.refs_1_), channel_id=1, source_target_pairs={{0,4},{2,6},{4,0},{6,2},{8,12},{10,14},{12,8},{14,10},{16,20},{18,... | collective-permute-start | bytes 172040 | tf_op jit(solution)/shard_map/ppermute | solution.py:554
  44.8 13.7 %collective-permute-start.17 = (bf16[24,4,16,128]{3,2,1,0:T(8,128)(2,1)S(1)}, bf16[24,4,16,128]{3,2,1,0:T(8,128)(2,1)S(1)}, u32[]{:S(2)}, u32[]{:S(2)}) collective-permute-start(bf16[24,4,16,128]{3,2,1,0:T(8,128)(2,1)S(1)} %shard_map.81), channel_id=1, source_target_pairs={{0,1},{1,0},{2,3},{3,2},{4,5},{5,4},{6,7},{7,6},{8,9},{9,8},{10,11... | collective-permute-start | bytes 1179656 | tf_op jit(solution)/shard_map/ppermute | solution.py:438
  46.1 5.2 %collective-permute-start.13 = (f32[7,16,128]{2,1,0:T(8,128)S(1)}, f32[7,16,128]{2,1,0:T(8,128)S(1)}, u32[]{:S(2)}, u32[]{:S(2)}) collective-permute-start(f32[7,16,128]{2,1,0:T(8,128)S(1)} %shard_map.79.refs_0_.refs_1_), channel_id=1, source_target_pairs={{0,8},{2,10},{4,12},{6,14},{8,0},{10,2},{12,4},{14,6},{16,24},{18,... | collective-permute-start | bytes 172040 | tf_op jit(solution)/shard_map/ppermute | solution.py:554
  47.2 7.1 %collective-permute-start.14 = (f32[7,16,128]{2,1,0:T(8,128)S(1)}, f32[7,16,128]{2,1,0:T(8,128)S(1)}, u32[]{:S(2)}, u32[]{:S(2)}) collective-permute-start(f32[7,16,128]{2,1,0:T(8,128)S(1)} %shard_map.79.refs_0_.refs_1_), channel_id=1, source_target_pairs={{0,16},{2,18},{4,20},{6,22},{8,24},{10,26},{12,28},{14,30},{16,0},... | collective-permute-start | bytes 172040 | tf_op jit(solution)/shard_map/ppermute | solution.py:554
  51.2 6.0 %collective-permute-start.15 = (f32[7,16,128]{2,1,0:T(8,128)S(1)}, f32[7,16,128]{2,1,0:T(8,128)S(1)}, u32[]{:S(2)}, u32[]{:S(2)}) collective-permute-start(f32[7,16,128]{2,1,0:T(8,128)S(1)} %shard_map.79.refs_0_.refs_1_), channel_id=1, source_target_pairs={{0,24},{2,26},{4,28},{6,30},{8,16},{10,18},{12,20},{14,22},{16,8},... | collective-permute-start | bytes 172040 | tf_op jit(solution)/shard_map/ppermute | solution.py:554
  57.2 1.3 %collective-permute-start.16 = (f32[7,16,128]{2,1,0:T(8,128)S(1)}, f32[7,16,128]{2,1,0:T(8,128)S(1)}, u32[]{:S(2)}, u32[]{:S(2)}) collective-permute-start(f32[7,16,128]{2,1,0:T(8,128)S(1)} %shard_map.80.refs_0_), channel_id=1, source_target_pairs={{0,2},{2,0},{4,6},{6,4},{8,10},{10,8},{12,14},{14,12},{16,18},{18,... | collective-permute-start | bytes 172040 | tf_op jit(solution)/shard_map/ppermute | solution.py:554

commit v17 on v16

--- a/solution.py
+++ b/solution.py
@@ -378,9 +378,8 @@
     pass
 
 
-def merge_kernel(extent, factor, *refs):
-    mine, other, *pieces = refs[:-4]
-    out, first, second, wide = refs[-4:]
+def finish_kernel(factor, after, mine, other, first, second):
+    del after
     channels = first.shape[2]
 
     def place(ours, theirs):
@@ -399,6 +398,10 @@
     def _():
         place(second, first)
 
+
+def merge_kernel(extent, *refs):
+    pieces, token, out, wide = refs[:-3], refs[-3], refs[-2], refs[-1]
+    token[...] = jnp.zeros_like(token)
     size, planes, rows = out.shape[:3]
     share = rows // extent
     me = lax.axis_index("chan")
@@ -590,10 +593,9 @@
     if plain:
         stride = 4
         while stride < slabs:
-            radix = 4 if slabs % (4 * stride) == 0 else 2
-            got = [mine] + [stepped(mine, m * stride) for m in range(1, radix)]
+            got = [mine, stepped(mine, stride)]
             (mine,) = call(functools.partial(add_kernel, 0), [portion], got)
-            stride *= radix
+            stride *= 2
         other = stepped(mine, 1)
     else:
         mine, other = keep[0], send[0]
@@ -603,12 +605,18 @@
         mine, other = jnp.where(even, mine, other), jnp.where(even, other, mine)
         mine, other = lax.psum((mine, other), "slab")
         mine, other = jnp.where(even, mine, other), jnp.where(even, other, mine)
-    input_grad, first_grad, second_grad = call(
-        functools.partial(merge_kernel, extent, factor),
-        [jax.ShapeDtypeStruct(field.shape, BF16)] + [jax.ShapeDtypeStruct(by_tap, F32)] * 2,
-        [mine, other] + pieces,
+    token, input_grad = call(
+        functools.partial(merge_kernel, extent),
+        [jax.ShapeDtypeStruct((8, 128), F32), jax.ShapeDtypeStruct(field.shape, BF16)],
+        pieces,
         [pltpu.VMEM((rows * planes * size, depth), F32)],
         moved=4 * field.size,
+    )
+    first_grad, second_grad = call(
+        functools.partial(finish_kernel, factor),
+        [jax.ShapeDtypeStruct(by_tap, F32)] * 2,
+        [token, mine, other],
+        loose=1,
     )
     first_grad, second_grad = (jnp.transpose(g, (1, 0, 2)) for g in (first_grad, second_grad))
     return input_grad, first_grad, second_grad

time: 60.8 us -> 58.7 us (0.965)
  waiting for transfers between devices: 12.8 us -> 10.8 us
  Pallas kernels: 19.6 us -> 20.4 us
  starting transfers between devices: 24.4 us -> 23.6 us
    ppermute x6 -> x5, waiting for transfers between devices: 8.9 us -> 6.91 us  [stepped(): return lax.ppermute(value, 'slab', [(i, i ^ stride) for i in range(slabs)])]
    ppermute x6 -> x5, starting transfers between devices: 7.06 us -> 6.23 us  [stepped(): return lax.ppermute(value, 'slab', [(i, i ^ stride) for i in range(slabs)])]
    pallas_call x16 -> x18, Pallas kernels: 19.6 us -> 20.4 us  [call(): pl.pallas_call(kernel, out_shape=outs, in_specs=[still] * loose + [whole]...]
  transfers between devices with their start and end apart: 18 -> 17, of which waited for: 7 -> 6; matrix products, arithmetic and copies ran while one was open for 0% -> 0% of each run, Pallas kernels for 27% -> 31%
where the time goes in v17:
time: 58.7 us; the launch traced here: 58.5 us
  starting transfers between devices  23.6 us (40%)
  Pallas kernels  20.4 us (35%)
  waiting for transfers between devices  10.8 us (18%)
  local copies, waits for them, and re-layouts  2.92 us (5%)
  between operations  0.79 us (1%)
    pallas_call x18, Pallas kernels, call(): pl.pallas_call(kernel, out_shape=outs, in_specs=[still] * loose + [whole]...  20.4 us
    ppermute x3, starting transfers between devices, to_prev(): lax.ppermute(value, 'slab', [((i + 1) % slabs, i) for i in range(slabs)])  8.99 us
    ppermute x5, starting transfers between devices, to_chan(): lax.ppermute(value, 'chan', [(i, (i + shift) % extent) for i in range(ext...  7.91 us
    ppermute x5, waiting for transfers between devices, stepped(): return lax.ppermute(value, 'slab', [(i, i ^ stride) for i in range(slabs)])  6.91 us
    ppermute x5, starting transfers between devices, stepped(): return lax.ppermute(value, 'slab', [(i, i ^ stride) for i in range(slabs)])  6.23 us
    ppermute x5, waiting for transfers between devices, to_chan(): lax.ppermute(value, 'chan', [(i, (i + shift) % extent) for i in range(ext...  3.87 us
    unnamed x8, local copies, waits for them, and re-layouts  2.92 us
  transfers between devices with their start and end apart: 17, of which 6 were waited for; matrix products, arithmetic and copies ran while one was open for 0% of the time, Pallas kernels for 31%

profile of v17, /device:TPU:0, one launch (start us, length us, event | category | flops | bytes accessed | tf_op | source)
XLA Modules:
  0.0 58.5 jit_solution(3656090357110398056)
XLA Ops:
  0.6 0.0 copy-start.1
  0.6 1.1 %copy-done.1 = bf16[16,4,48,128]{3,2,1,0:T(8,128)(2,1)S(1)} copy-done((bf16[16,4,48,128]{3,2,1,0:T(8,128)(2,1)S(1)}, bf16[16,4,48,128]{3,2,1,0:T(8,128)(2,1)}, u32[]{:S(2)}) %copy-start.1) | copy-done | bytes 786456
  1.8 0.0 copy-start
  1.8 1.3 %shard_map.67 = (bf16[32,2,16,128]{3,2,1,0:T(8,128)(2,1)S(1)}, bf16[32,2,16,128]{3,2,1,0:T(8,128)(2,1)S(1)}, bf16[32,2,16,128]{3,2,1,0:T(8,128)(2,1)S(1)}, bf16[32,2,16,128]{3,2,1,0:T(8,128)(2,1)S(1)}) custom-call(bf16[16,4,48,128]{3,2,1,0:T(8,128)(2,1)S(1)} %copy-done.1), custom_call_target="tpu_custom_call" | custom-call | bytes 2359296 | tf_op jit(solution)/shard_map/pallas_call | solution.py:19
  3.1 3.0 %collective-permute-start.1 = (bf16[32,2,16,128]{3,2,1,0:T(8,128)(2,1)S(1)}, bf16[32,2,16,128]{3,2,1,0:T(8,128)(2,1)S(1)}, u32[]{:S(2)}, u32[]{:S(2)}) collective-permute-start(bf16[32,2,16,128]{3,2,1,0:T(8,128)(2,1)S(1)} %get-tuple-element.33), channel_id=1, source_target_pairs={{0,1},{1,0},{2,3},{3,2},{4,5},{5,4},{6,7},{7,6},{8,9},{9,8},{10,11... | collective-permute-start | bytes 786440 | tf_op jit(solution)/shard_map/ppermute | solution.py:441
  6.1 0.1 collective-permute-start.3
  6.2 3.9 %collective-permute-start.5 = (bf16[32,2,16,128]{3,2,1,0:T(8,128)(2,1)S(1)}, bf16[32,2,16,128]{3,2,1,0:T(8,128)(2,1)S(1)}, u32[]{:S(2)}, u32[]{:S(2)}) collective-permute-start(bf16[32,2,16,128]{3,2,1,0:T(8,128)(2,1)S(1)} %get-tuple-element.34.after.refs_2_.refs_11_), channel_id=1, source_target_pairs={{2,0},{4,2},{6,4},{8,6},{10,8},{12,10},{14,12},{16,14},{18,16},{20... | collective-permute-start | bytes 786440 | tf_op jit(solution)/shard_map/ppermute | solution.py:447
  10.1 0.0 collective-permute-start
  10.1 0.0 copy-start.2
  10.1 0.9 %copy-done.2 = bf16[16,27,32]{2,0,1:T(8,128)(2,1)S(1)} copy-done((bf16[16,27,32]{2,0,1:T(8,128)(2,1)S(1)}, bf16[16,27,32]{2,0,1:T(8,128)(2,1)}, u32[]{:S(2)}) %copy-start.2) | copy-done | bytes 27672
  11.0 0.0 copy-start.3
  11.0 0.9 %copy-done.3 = bf16[16,27,32]{2,0,1:T(8,128)(2,1)S(1)} copy-done((bf16[16,27,32]{2,0,1:T(8,128)(2,1)S(1)}, bf16[16,27,32]{2,0,1:T(8,128)(2,1)}, u32[]{:S(2)}) %copy-start.3) | copy-done | bytes 27672
  11.9 0.1 shard_map.68.refs_1_.after.refs_0_
  12.0 1.2 %collective-permute-done.1.refs_0_ = bf16[32,2,16,128]{3,2,1,0:T(8,128)(2,1)S(1)} collective-permute-done((bf16[32,2,16,128]{3,2,1,0:T(8,128)(2,1)S(1)}, bf16[32,2,16,128]{3,2,1,0:T(8,128)(2,1)S(1)}, u32[]{:S(2)}, u32[]{:S(2)}) %collective-permute-start.1) | collective-permute-done | bytes 262176 | tf_op jit(solution)/shard_map/ppermute | solution.py:441
  13.2 0.0 collective-permute-start.2
  13.2 2.1 %collective-permute-start.4 = (bf16[14,16,128]{2,1,0:T(8,128)(2,1)S(1)}, bf16[14,16,128]{2,1,0:T(8,128)(2,1)S(1)}, u32[]{:S(2)}, u32[]{:S(2)}) collective-permute-start(bf16[14,16,128]{2,1,0:T(8,128)(2,1)S(1)} %shard_map.68.refs_1_.after.refs_0_), channel_id=1, source_target_pairs={{0,1},{1,0},{2,3},{3,2},{4,5},{5,4},{6,7},{7,6},{8,9},{9,8},{10,11... | collective-permute-start | bytes 172040 | tf_op jit(solution)/shard_map/ppermute | solution.py:441
  15.3 0.0 copy-done
  15.3 1.2 %shard_map.70 = (bf16[28,2,32,128]{3,2,1,0:T(8,128)(2,1)S(1)}, bf16[28,2,32,128]{3,2,1,0:T(8,128)(2,1)S(1)}) custom-call(bf16[14,16,128]{2,1,0:T(8,128)(2,1)S(1)} %shard_map.68.refs_1_.after.refs_0_, bf16[32,4,48,128]{3,2,1,0:T(8,128)(2,1)S(1)} %copy-done), custom_call_target="tpu_custom_call" | custom-call | bytes 3145728 | tf_op jit(solution)/shard_map/pallas_call | solution.py:19
  16.5 2.6 %collective-permute-done.4.refs_2_.refs_1_ = bf16[14,16,128]{2,1,0:T(8,128)(2,1)S(1)} collective-permute-done((bf16[14,16,128]{2,1,0:T(8,128)(2,1)S(1)}, bf16[14,16,128]{2,1,0:T(8,128)(2,1)S(1)}, u32[]{:S(2)}, u32[]{:S(2)}) %collective-permute-start.4) | collective-permute-done | bytes 57376 | tf_op jit(solution)/shard_map/ppermute | solution.py:441
  19.2 0.0 collective-permute-done.3.refs_0_
  19.2 0.0 collective-permute-done.5.refs_1_.refs_2_.refs_15_
  19.2 3.5 %collective-permute-start.7 = (bf16[32,2,16,128]{3,2,1,0:T(8,128)(2,1)S(1)}, bf16[32,2,16,128]{3,2,1,0:T(8,128)(2,1)S(1)}, u32[]{:S(2)}, u32[]{:S(2)}) collective-permute-start(bf16[32,2,16,128]{3,2,1,0:T(8,128)(2,1)S(1)} %shard_map.72.refs_3_.refs_12_), channel_id=1, source_target_pairs={{2,0},{4,2},{6,4},{8,6},{10,8},{12,10},{14,12},{16,14},{18,16},{20... | collective-permute-start | bytes 786440 | tf_op jit(solution)/shard_map/ppermute | solution.py:447
  22.7 0.5 shard_map.73
  23.2 0.0 collective-permute-done.refs_0_.refs_9_
  23.2 0.0 collective-permute-done.2.refs_1_.refs_10_
  23.2 2.6 %shard_map.74 = (bf16[30,2,32,128]{3,2,1,0:T(8,128)(2,1)S(1)}, bf16[30,2,32,128]{3,2,1,0:T(8,128)(2,1)S(1)}, bf16[30,2,32,128]{3,2,1,0:T(8,128)(2,1)S(1)}, bf16[...) custom-call(bf16[32,2,16,128]{3,2,1,0:T(8,128)(2,1)S(1)} %collective-permute-done.refs_0_.refs_9_, ...), custom_call_target="tpu_custom_call" | custom-call | flops 1019215872 | bytes 3145728 | tf_op jit(solution)/shard_map/pallas_call | solution.py:19
  25.8 1.6 %collective-permute-start.6 = (bf16[28,2,32,128]{3,2,1,0:T(8,128)(2,1)S(1)}, bf16[28,2,32,128]{3,2,1,0:T(8,128)(2,1)S(1)}, u32[]{:S(2)}, u32[]{:S(2)}) collective-permute-start(bf16[28,2,32,128]{3,2,1,0:T(8,128)(2,1)S(1)} %get-tuple-element.39.refs_3_), channel_id=1, source_target_pairs={{2,0},{4,2},{6,4},{8,6},{10,8},{12,10},{14,12},{16,14},{18,16},{20... | collective-permute-start | bytes 1376264 | tf_op jit(solution)/shard_map/ppermute | solution.py:447
  27.4 0.0 collective-permute-done.7.refs_3_.refs_16_
  27.4 1.8 %shard_map.75 = (bf16[30,2,32,128]{3,2,1,0:T(8,128)(2,1)S(1)}, bf16[30,2,32,128]{3,2,1,0:T(8,128)(2,1)S(1)}, bf16[28,2,32,128]{3,2,1,0:T(8,128)(2,1)S(1)}) custom-call(bf16[32,2,16,128]{3,2,1,0:T(8,128)(2,1)S(1)} %get-tuple-element.32.refs_4_.refs_0_.refs_13_, bf16[32,2,16,128]{3,2,1,0:T(8,128)(2,1)S(1)} %shard_map.69.refs_5_.refs_1_.refs_14_, ...), custom_call_target="tpu_custom_call" | custom-call | flops 679477248 | bytes 2359296 | tf_op jit(solution)/shard_map/pallas_call | solution.py:19
  29.2 0.2 collective-permute-start.9
  29.5 7.2 %shard_map.76 = (f32[2,7,16,128]{3,2,1,0:T(8,128)S(1)}, f32[2,7,16,128]{3,2,1,0:T(8,128)S(1)}, bf16[26,2,32,128]{3,2,1,0:T(8,128)(2,1)S(1)}) custom-call(bf16[30,2,32,128]{3,2,1,0:T(8,128)(2,1)S(1)} %get-tuple-element.40.refs_0_, bf16[30,2,32,128]{3,2,1,0:T(8,128)(2,1)S(1)} %get-tuple-element.41.refs_4_.refs_1_, ...), custom_call_target="tpu_custom_call" | custom-call | tf_op jit(solution)/shard_map/pallas_call | solution.py:19
  36.6 0.1 collective-permute-start.8
  36.7 1.3 %collective-permute-done.8.two = f32[2,7,16,128]{3,2,1,0:T(8,128)S(1)} collective-permute-done((f32[2,7,16,128]{3,2,1,0:T(8,128)S(1)}, f32[2,7,16,128]{3,2,1,0:T(8,128)S(1)}, u32[]{:S(2)}, u32[]{:S(2)}) %collective-permute-start.8) | collective-permute-done | bytes 114720 | tf_op jit(solution)/shard_map/ppermute | solution.py:557
  38.0 0.0 collective-permute-done.6.after.refs_5_
  38.0 1.6 %collective-permute-start.10 = (f32[7,16,128]{2,1,0:T(8,128)S(1)}, f32[7,16,128]{2,1,0:T(8,128)S(1)}, u32[]{:S(2)}, u32[]{:S(2)}) collective-permute-start(f32[7,16,128]{2,1,0:T(8,128)S(1)} %get-tuple-element.56), channel_id=1, source_target_pairs={{0,1},{1,0},{2,3},{3,2},{4,5},{5,4},{6,7},{7,6},{8,9},{9,8},{10,11... | collective-permute-start | bytes 172040 | tf_op jit(solution)/shard_map/ppermute | solution.py:441
  39.6 0.2 collective-permute-start.12
  39.8 1.8 %collective-permute-start.11 = (f32[7,16,128]{2,1,0:T(8,128)S(1)}, f32[7,16,128]{2,1,0:T(8,128)S(1)}, u32[]{:S(2)}, u32[]{:S(2)}) collective-permute-start(f32[7,16,128]{2,1,0:T(8,128)S(1)} %get-tuple-element.51.after.refs_1_), channel_id=1, source_target_pairs={{0,4},{2,6},{4,0},{6,2},{8,12},{10,14},{12,8},{14,10},{16,20},{18,... | collective-permute-start | bytes 172040 | tf_op jit(solution)/shard_map/ppermute | solution.py:557
  41.6 0.0 collective-permute-done.9.refs_2_
  41.6 2.8 %shard_map.78 = (bf16[24,4,16,128]{3,2,1,0:T(8,128)(2,1)S(1)}, bf16[24,4,16,128]{3,2,1,0:T(8,128)(2,1)S(1)}) custom-call(f32[7,16,128]{2,1,0:T(8,128)S(1)} %get-tuple-element.51.after.refs_1_, bf16[192,384]{1,0:T(8,128)(2,1)S(1)} %get-tuple-element.45.refs_5_.refs_0_, bf16[192,384]{1,0:T(8,128)(2,1)S(1)} %get-tuple-element.52.refs_1_, ...), custom_call_target="tpu_custom_call" | custom-call | flops 1358954496 | bytes 2359296 | tf_op jit(solution)/shard_map/pallas_call | solution.py:19
  44.4 0.0 collective-permute-done.10.refs_2_
  44.4 0.4 collective-permute-done.11.refs_3_
  44.8 0.0 collective-permute-done.12.refs_4_
  44.8 1.2 %collective-permute-start.13 = (bf16[24,4,16,128]{3,2,1,0:T(8,128)(2,1)S(1)}, bf16[24,4,16,128]{3,2,1,0:T(8,128)(2,1)S(1)}, u32[]{:S(2)}, u32[]{:S(2)}) collective-permute-start(bf16[24,4,16,128]{3,2,1,0:T(8,128)(2,1)S(1)} %shard_map.80), channel_id=1, source_target_pairs={{0,1},{1,0},{2,3},{3,2},{4,5},{5,4},{6,7},{7,6},{8,9},{9,8},{10,11... | collective-permute-start | bytes 1179656 | tf_op jit(solution)/shard_map/ppermute | solution.py:441
  46.1 1.1 %collective-permute-start.14 = (f32[7,16,128]{2,1,0:T(8,128)S(1)}, f32[7,16,128]{2,1,0:T(8,128)S(1)}, u32[]{:S(2)}, u32[]{:S(2)}) collective-permute-start(f32[7,16,128]{2,1,0:T(8,128)S(1)} %shard_map.79.refs_1_.refs_0_), channel_id=1, source_target_pairs={{0,8},{2,10},{4,12},{6,14},{8,0},{10,2},{12,4},{14,6},{16,24},{18,... | collective-permute-start | bytes 172040 | tf_op jit(solution)/shard_map/ppermute | solution.py:557
  47.2 3.0 %collective-permute-done.14.refs_1_ = f32[7,16,128]{2,1,0:T(8,128)S(1)} collective-permute-done((f32[7,16,128]{2,1,0:T(8,128)S(1)}, f32[7,16,128]{2,1,0:T(8,128)S(1)}, u32[]{:S(2)}, u32[]{:S(2)}) %collective-permute-start.14) | collective-permute-done | bytes 57376 | tf_op jit(solution)/shard_map/ppermute | solution.py:557
  50.2 3.2 %collective-permute-start.15 = (f32[7,16,128]{2,1,0:T(8,128)S(1)}, f32[7,16,128]{2,1,0:T(8,128)S(1)}, u32[]{:S(2)}, u32[]{:S(2)}) collective-permute-start(f32[7,16,128]{2,1,0:T(8,128)S(1)} %shard_map.82.refs_0_), channel_id=1, source_target_pairs={{0,16},{2,18},{4,20},{6,22},{8,24},{10,26},{12,28},{14,30},{16,0},... | collective-permute-start | bytes 172040 | tf_op jit(solution)/shard_map/ppermute | solution.py:557
  53.4 2.2 %collective-permute-done.15.refs_1_ = f32[7,16,128]{2,1,0:T(8,128)S(1)} collective-permute-done((f32[7,16,128]{2,1,0:T(8,128)S(1)}, f32[7,16,128]{2,1,0:T(8,128)S(1)}, u32[]{:S(2)}, u32[]{:S(2)}) %collective-permute-start.15) | collective-permute-done | bytes 57376 | tf_op jit(solution)/shard_map/ppermute | solution.py:557
  55.6 0.1 collective-permute-start.16
  55.7 0.0 collective-permute-done.13.refs_1_
  55.7 1.9 %shard_map.81 = (f32[8,128]{1,0:T(8,128)S(1)}, bf16[16,4,48,128]{3,2,1,0:T(8,128)(2,1)}) custom-call(bf16[24,4,16,128]{3,2,1,0:T(8,128)(2,1)S(1)} %get-tuple-element.54.refs_0_, bf16[24,4,16,128]{3,2,1,0:T(8,128)(2,1)S(1)} %collective-permute-done.13.refs_1_), custom_call_target="tpu_custom_call" | custom-call | bytes 1572864 | tf_op jit(solution)/shard_map/pallas_call | solution.py:19
  57.6 0.0 collective-permute-done.16.other
  57.6 0.9 %shard_map.84 = (f32[27,16,32]{2,1,0:T(8,128)}, f32[27,16,32]{2,1,0:T(8,128)}) custom-call(f32[8,128]{1,0:T(8,128)S(1)} %get-tuple-element.58.after, f32[7,16,128]{2,1,0:T(8,128)S(1)} %shard_map.83.mine, f32[7,16,128]{2,1,0:T(8,128)S(1)} %collective-permute-done.16.other), custom_call_target="tpu_custom_call" | custom-call | tf_op jit(solution)/shard_map/pallas_call | solution.py:19
  (8 shorter events, 0.1 us)
Async XLA Ops:
  0.6 1.1 %copy-start.1 = (bf16[16,4,48,128]{3,2,1,0:T(8,128)(2,1)S(1)}, bf16[16,4,48,128]{3,2,1,0:T(8,128)(2,1)}, u32[]{:S(2)}) copy-start(bf16[16,4,48,128]{3,2,1,0:T(8,128)(2,1)} %x_ref.2) | copy-start | bytes 2359300
  1.8 13.5 %copy-start = (bf16[32,4,48,128]{3,2,1,0:T(8,128)(2,1)S(1)}, bf16[32,4,48,128]{3,2,1,0:T(8,128)(2,1)}, u32[]{:S(2)}) copy-start(bf16[32,4,48,128]{3,2,1,0:T(8,128)(2,1)} %x_ref.3) | copy-start | bytes 4718596
  3.1 10.1 %collective-permute-start.1 = (bf16[32,2,16,128]{3,2,1,0:T(8,128)(2,1)S(1)}, bf16[32,2,16,128]{3,2,1,0:T(8,128)(2,1)S(1)}, u32[]{:S(2)}, u32[]{:S(2)}) collective-permute-start(bf16[32,2,16,128]{3,2,1,0:T(8,128)(2,1)S(1)} %get-tuple-element.33), channel_id=1, source_target_pairs={{0,1},{1,0},{2,3},{3,2},{4,5},{5,4},{6,7},{7,6},{8,9},{9,8},{10,11... | collective-permute-start | bytes 786440 | tf_op jit(solution)/shard_map/ppermute | solution.py:441
  6.1 13.1 %collective-permute-start.3 = (bf16[32,2,16,128]{3,2,1,0:T(8,128)(2,1)S(1)}, bf16[32,2,16,128]{3,2,1,0:T(8,128)(2,1)S(1)}, u32[]{:S(2)}, u32[]{:S(2)}) collective-permute-start(bf16[32,2,16,128]{3,2,1,0:T(8,128)(2,1)S(1)} %get-tuple-element.35), channel_id=1, source_target_pairs={{0,1},{1,0},{2,3},{3,2},{4,5},{5,4},{6,7},{7,6},{8,9},{9,8},{10,11... | collective-permute-start | bytes 786440 | tf_op jit(solution)/shard_map/ppermute | solution.py:441
  6.2 13.0 %collective-permute-start.5 = (bf16[32,2,16,128]{3,2,1,0:T(8,128)(2,1)S(1)}, bf16[32,2,16,128]{3,2,1,0:T(8,128)(2,1)S(1)}, u32[]{:S(2)}, u32[]{:S(2)}) collective-permute-start(bf16[32,2,16,128]{3,2,1,0:T(8,128)(2,1)S(1)} %get-tuple-element.34.after.refs_2_.refs_11_), channel_id=1, source_target_pairs={{2,0},{4,2},{6,4},{8,6},{10,8},{12,10},{14,12},{16,14},{18,16},{20... | collective-permute-start | bytes 786440 | tf_op jit(solution)/shard_map/ppermute | solution.py:447
  10.1 13.2 %collective-permute-start = (bf16[32,2,16,128]{3,2,1,0:T(8,128)(2,1)S(1)}, bf16[32,2,16,128]{3,2,1,0:T(8,128)(2,1)S(1)}, u32[]{:S(2)}, u32[]{:S(2)}) collective-permute-start(bf16[32,2,16,128]{3,2,1,0:T(8,128)(2,1)S(1)} %get-tuple-element.32.refs_4_.refs_0_.refs_13_), channel_id=1, source_target_pairs={{0,2},{2,4},{4,6},{6,8},{8,10},{10,12},{12,14},{14,16},{16,18},{18... | collective-permute-start | bytes 786440 | tf_op jit(solution)/shard_map/ppermute | solution.py:444
  10.1 0.9 %copy-start.2 = (bf16[16,27,32]{2,0,1:T(8,128)(2,1)S(1)}, bf16[16,27,32]{2,0,1:T(8,128)(2,1)}, u32[]{:S(2)}) copy-start(bf16[16,27,32]{2,0,1:T(8,128)(2,1)} %param.6) | copy-start | bytes 82948
  11.0 0.9 %copy-start.3 = (bf16[16,27,32]{2,0,1:T(8,128)(2,1)S(1)}, bf16[16,27,32]{2,0,1:T(8,128)(2,1)}, u32[]{:S(2)}) copy-start(bf16[16,27,32]{2,0,1:T(8,128)(2,1)} %param.7) | copy-start | bytes 82948
  13.2 10.0 %collective-permute-start.2 = (bf16[32,2,16,128]{3,2,1,0:T(8,128)(2,1)S(1)}, bf16[32,2,16,128]{3,2,1,0:T(8,128)(2,1)S(1)}, u32[]{:S(2)}, u32[]{:S(2)}) collective-permute-start(bf16[32,2,16,128]{3,2,1,0:T(8,128)(2,1)S(1)} %shard_map.69.refs_5_.refs_1_.refs_14_), channel_id=1, source_target_pairs={{0,2},{2,4},{4,6},{6,8},{8,10},{10,12},{12,14},{14,16},{16,18},{18... | collective-permute-start | bytes 786440 | tf_op jit(solution)/shard_map/ppermute | solution.py:444
  13.2 5.9 %collective-permute-start.4 = (bf16[14,16,128]{2,1,0:T(8,128)(2,1)S(1)}, bf16[14,16,128]{2,1,0:T(8,128)(2,1)S(1)}, u32[]{:S(2)}, u32[]{:S(2)}) collective-permute-start(bf16[14,16,128]{2,1,0:T(8,128)(2,1)S(1)} %shard_map.68.refs_1_.after.refs_0_), channel_id=1, source_target_pairs={{0,1},{1,0},{2,3},{3,2},{4,5},{5,4},{6,7},{7,6},{8,9},{9,8},{10,11... | collective-permute-start | bytes 172040 | tf_op jit(solution)/shard_map/ppermute | solution.py:441
  19.2 8.2 %collective-permute-start.7 = (bf16[32,2,16,128]{3,2,1,0:T(8,128)(2,1)S(1)}, bf16[32,2,16,128]{3,2,1,0:T(8,128)(2,1)S(1)}, u32[]{:S(2)}, u32[]{:S(2)}) collective-permute-start(bf16[32,2,16,128]{3,2,1,0:T(8,128)(2,1)S(1)} %shard_map.72.refs_3_.refs_12_), channel_id=1, source_target_pairs={{2,0},{4,2},{6,4},{8,6},{10,8},{12,10},{14,12},{16,14},{18,16},{20... | collective-permute-start | bytes 786440 | tf_op jit(solution)/shard_map/ppermute | solution.py:447
  25.8 12.2 %collective-permute-start.6 = (bf16[28,2,32,128]{3,2,1,0:T(8,128)(2,1)S(1)}, bf16[28,2,32,128]{3,2,1,0:T(8,128)(2,1)S(1)}, u32[]{:S(2)}, u32[]{:S(2)}) collective-permute-start(bf16[28,2,32,128]{3,2,1,0:T(8,128)(2,1)S(1)} %get-tuple-element.39.refs_3_), channel_id=1, source_target_pairs={{2,0},{4,2},{6,4},{8,6},{10,8},{12,10},{14,12},{16,14},{18,16},{20... | collective-permute-start | bytes 1376264 | tf_op jit(solution)/shard_map/ppermute | solution.py:447
  29.2 12.4 %collective-permute-start.9 = (bf16[28,2,32,128]{3,2,1,0:T(8,128)(2,1)S(1)}, bf16[28,2,32,128]{3,2,1,0:T(8,128)(2,1)S(1)}, u32[]{:S(2)}, u32[]{:S(2)}) collective-permute-start(bf16[28,2,32,128]{3,2,1,0:T(8,128)(2,1)S(1)} %get-tuple-element.44.refs_4_), channel_id=1, source_target_pairs={{0,2},{2,4},{4,6},{6,8},{8,10},{10,12},{12,14},{14,16},{16,18},{18... | collective-permute-start | bytes 1376264 | tf_op jit(solution)/shard_map/ppermute | solution.py:444
  36.6 1.4 %collective-permute-start.8 = (f32[2,7,16,128]{3,2,1,0:T(8,128)S(1)}, f32[2,7,16,128]{3,2,1,0:T(8,128)S(1)}, u32[]{:S(2)}, u32[]{:S(2)}) collective-permute-start(f32[2,7,16,128]{3,2,1,0:T(8,128)S(1)} %get-tuple-element.50), channel_id=1, source_target_pairs={{0,2},{2,0},{4,6},{6,4},{8,10},{10,8},{12,14},{14,12},{16,18},{18,... | collective-permute-start | bytes 344072 | tf_op jit(solution)/shard_map/ppermute | solution.py:557
  38.0 6.4 %collective-permute-start.10 = (f32[7,16,128]{2,1,0:T(8,128)S(1)}, f32[7,16,128]{2,1,0:T(8,128)S(1)}, u32[]{:S(2)}, u32[]{:S(2)}) collective-permute-start(f32[7,16,128]{2,1,0:T(8,128)S(1)} %get-tuple-element.56), channel_id=1, source_target_pairs={{0,1},{1,0},{2,3},{3,2},{4,5},{5,4},{6,7},{7,6},{8,9},{9,8},{10,11... | collective-permute-start | bytes 172040 | tf_op jit(solution)/shard_map/ppermute | solution.py:441
  39.6 5.2 %collective-permute-start.12 = (f32[7,16,128]{2,1,0:T(8,128)S(1)}, f32[7,16,128]{2,1,0:T(8,128)S(1)}, u32[]{:S(2)}, u32[]{:S(2)}) collective-permute-start(f32[7,16,128]{2,1,0:T(8,128)S(1)} %get-tuple-element.56), channel_id=1, source_target_pairs={{0,5},{1,4},{2,7},{3,6},{4,1},{5,0},{6,3},{7,2},{8,13},{9,12},{10,... | collective-permute-start | bytes 172040 | tf_op jit(solution)/shard_map/ppermute | solution.py:563
  39.8 5.0 %collective-permute-start.11 = (f32[7,16,128]{2,1,0:T(8,128)S(1)}, f32[7,16,128]{2,1,0:T(8,128)S(1)}, u32[]{:S(2)}, u32[]{:S(2)}) collective-permute-start(f32[7,16,128]{2,1,0:T(8,128)S(1)} %get-tuple-element.51.after.refs_1_), channel_id=1, source_target_pairs={{0,4},{2,6},{4,0},{6,2},{8,12},{10,14},{12,8},{14,10},{16,20},{18,... | collective-permute-start | bytes 172040 | tf_op jit(solution)/shard_map/ppermute | solution.py:557
  44.8 10.8 %collective-permute-start.13 = (bf16[24,4,16,128]{3,2,1,0:T(8,128)(2,1)S(1)}, bf16[24,4,16,128]{3,2,1,0:T(8,128)(2,1)S(1)}, u32[]{:S(2)}, u32[]{:S(2)}) collective-permute-start(bf16[24,4,16,128]{3,2,1,0:T(8,128)(2,1)S(1)} %shard_map.80), channel_id=1, source_target_pairs={{0,1},{1,0},{2,3},{3,2},{4,5},{5,4},{6,7},{7,6},{8,9},{9,8},{10,11... | collective-permute-start | bytes 1179656 | tf_op jit(solution)/shard_map/ppermute | solution.py:441
  46.1 4.2 %collective-permute-start.14 = (f32[7,16,128]{2,1,0:T(8,128)S(1)}, f32[7,16,128]{2,1,0:T(8,128)S(1)}, u32[]{:S(2)}, u32[]{:S(2)}) collective-permute-start(f32[7,16,128]{2,1,0:T(8,128)S(1)} %shard_map.79.refs_1_.refs_0_), channel_id=1, source_target_pairs={{0,8},{2,10},{4,12},{6,14},{8,0},{10,2},{12,4},{14,6},{16,24},{18,... | collective-permute-start | bytes 172040 | tf_op jit(solution)/shard_map/ppermute | solution.py:557
  50.2 5.4 %collective-permute-start.15 = (f32[7,16,128]{2,1,0:T(8,128)S(1)}, f32[7,16,128]{2,1,0:T(8,128)S(1)}, u32[]{:S(2)}, u32[]{:S(2)}) collective-permute-start(f32[7,16,128]{2,1,0:T(8,128)S(1)} %shard_map.82.refs_0_), channel_id=1, source_target_pairs={{0,16},{2,18},{4,20},{6,22},{8,24},{10,26},{12,28},{14,30},{16,0},... | collective-permute-start | bytes 172040 | tf_op jit(solution)/shard_map/ppermute | solution.py:557
  55.6 2.0 %collective-permute-start.16 = (f32[7,16,128]{2,1,0:T(8,128)S(1)}, f32[7,16,128]{2,1,0:T(8,128)S(1)}, u32[]{:S(2)}, u32[]{:S(2)}) collective-permute-start(f32[7,16,128]{2,1,0:T(8,128)S(1)} %shard_map.83.mine), channel_id=1, source_target_pairs={{0,2},{2,0},{4,6},{6,4},{8,10},{10,8},{12,14},{14,12},{16,18},{18,... | collective-permute-start | bytes 172040 | tf_op jit(solution)/shard_map/ppermute | solution.py:557

commit v18 on v17

--- a/solution.py
+++ b/solution.py
@@ -41,12 +41,12 @@
         body(k)
 
 
-def widened(x_ref, wide):
-    count, planes, rows = x_ref.shape[:3]
+def widened(x_ref, wide, low, high):
+    count, _, rows = x_ref.shape[:3]
 
     def widen(i):
-        for x in range(planes):
-            start = pl.multiple_of((i * planes + x) * rows, 8)
+        for x in range(low, high):
+            start = pl.multiple_of((i * (high - low) + x - low) * rows, 8)
             wide[pl.ds(start, rows), :] = x_ref[i, x].astype(F32)
 
     in_blocks(count, widen)
@@ -64,12 +64,14 @@
     in_blocks(length, one)
 
 
-def field_kernel(extent, margin, x_ref, *refs):
+def field_kernel(extent, margin, low, high, after, x_ref, *refs):
+    del after
     outs, wide = refs[:-1], refs[-1]
-    count, planes, rows = x_ref.shape[:3]
+    count, _, rows = x_ref.shape[:3]
+    planes = high - low
     pairs = planes // 2
     share = rows // extent
-    widened(x_ref, wide)
+    widened(x_ref, wide, low, high)
     me = lax.axis_index("chan")
     for s in range(extent):
         base = lax.rem(me + s, extent) * share - margin + rows
@@ -98,7 +100,7 @@
     outs, wide = refs[:-1], refs[-1]
     count, planes, rows = x_ref.shape[:3]
     share = rows // extent
-    widened(x_ref, wide)
+    widened(x_ref, wide, 0, planes)
     base = lax.axis_index("chan") * share - margin + rows
     turn(wide, outs, (count, planes, rows), base, share + 2 * margin)
 
@@ -146,7 +148,12 @@
                                 t = 26 - t if flip else t
                                 chunks.append(blocks[t][k] if inside else blank)
                     low = (2 * e + x) * channels
-                    out[low : low + channels, :] = jnp.concatenate(chunks, axis=1).astype(BF16)
+                    line = jnp.concatenate(chunks, axis=1).astype(BF16)
+                    out[low : low + channels, :] = line
+                    if k == 1 and flip:
+                        half = line.shape[1] // 2
+                        outs[4][low : low + channels, :] = line[:, :half]
+                        outs[5][low : low + channels, :] = line[:, half:]
 
 
 def stacked(refs, row, count):
@@ -159,11 +166,10 @@
 
 def taps(weight, inputs, row):
     sides = []
-    for above, below in inputs:
+    for pair in inputs:
         for q in range(2):
-            sides.append(
-                jnp.concatenate([stacked(above, row + q, 3), stacked(below, row + q, 3)], axis=0)
-            )
+            parts = [stacked(refs, row + q, 3) for refs in pair]
+            sides.append(jnp.concatenate(parts, axis=0) if len(parts) > 1 else parts[0])
     lifted = jnp.dot(weight, jnp.concatenate(sides, axis=1), preferred_element_type=F32)
     third = lifted.shape[0] // 3
     depth = sides[0].shape[1]
@@ -299,18 +305,20 @@
     refs = list(refs)
     hiddens = [[refs.pop(0)] for _ in range(pairs + 1)]
     deltas = [[refs.pop(0)] for _ in range(pairs)]
-    weight = refs.pop(0)
+    weight, from_above, from_below = [refs.pop(0) for _ in range(3)]
     slopes = [refs.pop(0) for _ in range(pairs + 1)]
     fields = [[refs.pop(0) for _ in range(groups)] for _ in range(pairs + 2)]
     keep, send = refs.pop(0), refs.pop(0)
     inner = [refs.pop(0) for _ in range(pairs - 1)]
-    head, tail, none, second_total, first_total = refs
-    none[...] = jnp.zeros_like(none)
+    head, tail, second_total, first_total = refs
     second_total[...] = jnp.zeros_like(second_total)
     first_total[...] = jnp.zeros_like(first_total)
     weight_loop(second_total, planes_of(hiddens), 2, planes_of(deltas), 2, share)
     firsts = [head] + inner + [tail]
-    first_deltas(weight, neighbours([[none]] + deltas + [[none]]), slopes, firsts)
+    first_deltas(from_below, [(deltas[0],)], slopes[:1], [head])
+    if inner:
+        first_deltas(weight, neighbours(deltas), slopes[1:-1], inner)
+    first_deltas(from_above, [(deltas[-1],)], slopes[-1:], [tail])
     parts = planes_of([[first] for first in firsts])
     weight_loop(first_total, planes_of(fields), 3, parts, 1, share)
     halves, size = keep.shape[1:3]
@@ -453,20 +461,29 @@
 
     piece = jax.ShapeDtypeStruct((share + 8, 2, size, depth), BF16)
     by_tap = (27, size, channels)
-    made = call(
-        functools.partial(field_kernel, extent, 4),
-        [piece] * (extent * pairs),
-        [field],
-        [pltpu.VMEM((size * planes * rows, depth), F32)],
-        moved=field.size * 6,
-    )
-    parts = [list(made[:pairs])]
+    def field_pieces(low, high, after):
+        count = (high - low) // 2
+        made = call(
+            functools.partial(field_kernel, extent, 4, low, high),
+            [piece] * (extent * count),
+            [after, field],
+            [pltpu.VMEM((size * (high - low) * rows, depth), F32)],
+            moved=field.size * 3,
+            loose=1,
+        )
+        return [list(made[j * count : (j + 1) * count]) for j in range(extent)]
+
+    made = field_pieces(planes - 2, planes, field)
+    if pairs > 1:
+        others = field_pieces(0, planes - 2, made[0][0])
+        made = [first + last for first, last in zip(others, made)]
+    parts = [made[0]]
     for j in range(1, extent):
-        parts.append([to_chan(value, j) for value in made[j * pairs : (j + 1) * pairs]])
+        parts.append([to_chan(value, j) for value in made[j]])
     (pack,) = call(
         pack_kernel,
         [jax.ShapeDtypeStruct((14, size, 4 * channels), BF16)],
-        [made[0], jnp.transpose(first_weight, (1, 0, 2)), jnp.transpose(second_weight, (1, 0, 2))],
+        [made[0][0], jnp.transpose(first_weight, (1, 0, 2)), jnp.transpose(second_weight, (1, 0, 2))],
         loose=1,
     )
     packs = [pack] + [to_chan(pack, j) for j in range(1, extent)]
@@ -484,9 +501,10 @@
         loose=1,
     )
     matrix = jax.ShapeDtypeStruct((6 * channels, 12 * channels), BF16)
-    first_wide, second_wide, first_back, second_back = call(
+    half = jax.ShapeDtypeStruct((6 * channels, 6 * channels), BF16)
+    first_wide, second_wide, first_back, second_back, from_above, from_below = call(
         functools.partial(matrix_kernel, extent),
-        [matrix] * 4,
+        [matrix] * 4 + [half] * 2,
         packs,
         moved=matrix.size * 8,
     )
@@ -542,8 +560,8 @@
     made = call(
         functools.partial(gradient_kernel, share, groups, extent, pairs),
         [raw] * 2 + many(pairs - 1, share + 2),
-        hiddens + deltas + [second_back] + slopes + flat(fields),
-        [room(share + 2), room(share + 2), room(share + 4), total, total],
+        hiddens + deltas + [second_back, from_above, from_below] + slopes + flat(fields),
+        [room(share + 2), room(share + 2), total, total],
     )
     keep, send, inner = made[0], made[1], list(made[2:])
     def exchanged(made):

time: 58.7 us -> 57.1 us (0.973)
  local copies, waits for them, and re-layouts: 2.92 us -> 1.14 us
  waiting for transfers between devices: 10.8 us -> 11.9 us
  Pallas kernels: 20.4 us -> 19.5 us
    unnamed x8, local copies, waits for them, and re-layouts: 2.92 us -> 1.14 us
    ppermute x5, waiting for transfers between devices: 3.87 us -> 4.89 us  [to_chan(): lax.ppermute(value, 'chan', [(i, (i + shift) % extent) for i in range(ext...]
    pallas_call x18 -> x19, Pallas kernels: 20.4 us -> 19.5 us  [call(): pl.pallas_call(kernel, out_shape=outs, in_specs=[still] * loose + [whole]...]
where the time goes in v18:
time: 57.1 us; the launch traced here: 56.9 us
  starting transfers between devices  23.6 us (41%)
  Pallas kernels  19.5 us (34%)
  waiting for transfers between devices  11.9 us (21%)
  local copies, waits for them, and re-layouts  1.14 us (2%)
  between operations  0.8 us (1%)
    pallas_call x19, Pallas kernels, call(): pl.pallas_call(kernel, out_shape=outs, in_specs=[still] * loose + [whole]...  19.5 us
    ppermute x3, starting transfers between devices, to_prev(): lax.ppermute(value, 'slab', [((i + 1) % slabs, i) for i in range(slabs)])  9.06 us
    ppermute x5, starting transfers between devices, to_chan(): lax.ppermute(value, 'chan', [(i, (i + shift) % extent) for i in range(ext...  7.92 us
    ppermute x5, waiting for transfers between devices, stepped(): return lax.ppermute(value, 'slab', [(i, i ^ stride) for i in range(slabs)])  6.98 us
    ppermute x5, starting transfers between devices, stepped(): return lax.ppermute(value, 'slab', [(i, i ^ stride) for i in range(slabs)])  6.22 us
    ppermute x5, waiting for transfers between devices, to_chan(): lax.ppermute(value, 'chan', [(i, (i + shift) % extent) for i in range(ext...  4.89 us
  transfers between devices with their start and end apart: 17, of which 6 were waited for; matrix products, arithmetic and copies ran while one was open for 0% of the time, Pallas kernels for 31%

profile of v18, /device:TPU:0, one launch (start us, length us, event | category | flops | bytes accessed | tf_op | source)
XLA Modules:
  0.0 56.9 jit_solution(1010208485514748875)
XLA Ops:
  0.6 0.0 copy-start
  0.6 1.1 %copy-done = bf16[16,4,48,128]{3,2,1,0:T(8,128)(2,1)S(1)} copy-done((bf16[16,4,48,128]{3,2,1,0:T(8,128)(2,1)S(1)}, bf16[16,4,48,128]{3,2,1,0:T(8,128)(2,1)}, u32[]{:S(2)}) %copy-start) | copy-done | bytes 786456
  1.8 0.0 copy-start.2
  1.8 0.0 copy-start.3
  1.8 0.0 copy-start.1
  1.8 0.7 %shard_map.67 = (bf16[32,2,16,128]{3,2,1,0:T(8,128)(2,1)S(1)}, bf16[32,2,16,128]{3,2,1,0:T(8,128)(2,1)S(1)}) custom-call(bf16[16,4,48,128]{3,2,1,0:T(8,128)(2,1)S(1)} %copy-done, bf16[16,4,48,128]{3,2,1,0:T(8,128)(2,1)S(1)} %copy-done), custom_call_target="tpu_custom_call" | custom-call | bytes 1179648 | tf_op jit(solution)/shard_map/pallas_call | solution.py:19
  2.5 3.0 %collective-permute-start.1 = (bf16[32,2,16,128]{3,2,1,0:T(8,128)(2,1)S(1)}, bf16[32,2,16,128]{3,2,1,0:T(8,128)(2,1)S(1)}, u32[]{:S(2)}, u32[]{:S(2)}) collective-permute-start(bf16[32,2,16,128]{3,2,1,0:T(8,128)(2,1)S(1)} %get-tuple-element.35), channel_id=1, source_target_pairs={{0,1},{1,0},{2,3},{3,2},{4,5},{5,4},{6,7},{7,6},{8,9},{9,8},{10,11... | collective-permute-start | bytes 786440 | tf_op jit(solution)/shard_map/ppermute | solution.py:449
  5.5 0.7 %shard_map.68 = (bf16[32,2,16,128]{3,2,1,0:T(8,128)(2,1)S(1)}, bf16[32,2,16,128]{3,2,1,0:T(8,128)(2,1)S(1)}) custom-call(bf16[32,2,16,128]{3,2,1,0:T(8,128)(2,1)S(1)} %get-tuple-element.34.after.refs_4_.refs_0_.refs_15_, bf16[16,4,48,128]{3,2,1,0:T(8,128)(2,1)S(1)} %copy-done), custom_call_target="tpu_custom_call" | custom-call | bytes 1179648 | tf_op jit(solution)/shard_map/pallas_call | solution.py:19
  6.2 0.1 collective-permute-start.3
  6.3 4.0 %collective-permute-start.5 = (bf16[32,2,16,128]{3,2,1,0:T(8,128)(2,1)S(1)}, bf16[32,2,16,128]{3,2,1,0:T(8,128)(2,1)S(1)}, u32[]{:S(2)}, u32[]{:S(2)}) collective-permute-start(bf16[32,2,16,128]{3,2,1,0:T(8,128)(2,1)S(1)} %get-tuple-element.36.after.refs_2_.refs_13_), channel_id=1, source_target_pairs={{2,0},{4,2},{6,4},{8,6},{10,8},{12,10},{14,12},{16,14},{18,16},{20... | collective-permute-start | bytes 786440 | tf_op jit(solution)/shard_map/ppermute | solution.py:455
  10.2 0.0 collective-permute-start
  10.2 0.0 copy-done.2
  10.2 0.0 copy-done.3
  10.2 0.1 shard_map.69.refs_1_.after.refs_0_
  10.4 2.3 %collective-permute-done.1.refs_0_ = bf16[32,2,16,128]{3,2,1,0:T(8,128)(2,1)S(1)} collective-permute-done((bf16[32,2,16,128]{3,2,1,0:T(8,128)(2,1)S(1)}, bf16[32,2,16,128]{3,2,1,0:T(8,128)(2,1)S(1)}, u32[]{:S(2)}, u32[]{:S(2)}) %collective-permute-start.1) | collective-permute-done | bytes 262176 | tf_op jit(solution)/shard_map/ppermute | solution.py:449
  12.6 0.0 collective-permute-start.2
  12.6 2.1 %collective-permute-start.4 = (bf16[14,16,128]{2,1,0:T(8,128)(2,1)S(1)}, bf16[14,16,128]{2,1,0:T(8,128)(2,1)S(1)}, u32[]{:S(2)}, u32[]{:S(2)}) collective-permute-start(bf16[14,16,128]{2,1,0:T(8,128)(2,1)S(1)} %shard_map.69.refs_1_.after.refs_0_), channel_id=1, source_target_pairs={{0,1},{1,0},{2,3},{3,2},{4,5},{5,4},{6,7},{7,6},{8,9},{9,8},{10,11... | collective-permute-start | bytes 172040 | tf_op jit(solution)/shard_map/ppermute | solution.py:449
  14.7 0.0 copy-done.1
  14.7 1.2 %shard_map.71 = (bf16[28,2,32,128]{3,2,1,0:T(8,128)(2,1)S(1)}, bf16[28,2,32,128]{3,2,1,0:T(8,128)(2,1)S(1)}) custom-call(bf16[14,16,128]{2,1,0:T(8,128)(2,1)S(1)} %shard_map.69.refs_1_.after.refs_0_, bf16[32,4,48,128]{3,2,1,0:T(8,128)(2,1)S(1)} %copy-done.1), custom_call_target="tpu_custom_call" | custom-call | bytes 3145728 | tf_op jit(solution)/shard_map/pallas_call | solution.py:19
  15.9 2.6 %collective-permute-done.4.refs_2_.refs_1_ = bf16[14,16,128]{2,1,0:T(8,128)(2,1)S(1)} collective-permute-done((bf16[14,16,128]{2,1,0:T(8,128)(2,1)S(1)}, bf16[14,16,128]{2,1,0:T(8,128)(2,1)S(1)}, u32[]{:S(2)}, u32[]{:S(2)}) %collective-permute-start.4) | collective-permute-done | bytes 57376 | tf_op jit(solution)/shard_map/ppermute | solution.py:449
  18.6 0.0 collective-permute-done.3.refs_0_
  18.6 0.0 collective-permute-done.5.refs_1_.refs_2_.refs_17_
  18.6 3.5 %collective-permute-start.7 = (bf16[32,2,16,128]{3,2,1,0:T(8,128)(2,1)S(1)}, bf16[32,2,16,128]{3,2,1,0:T(8,128)(2,1)S(1)}, u32[]{:S(2)}, u32[]{:S(2)}) collective-permute-start(bf16[32,2,16,128]{3,2,1,0:T(8,128)(2,1)S(1)} %shard_map.73.refs_3_.refs_14_), channel_id=1, source_target_pairs={{2,0},{4,2},{6,4},{8,6},{10,8},{12,10},{14,12},{16,14},{18,16},{20... | collective-permute-start | bytes 786440 | tf_op jit(solution)/shard_map/ppermute | solution.py:455
  22.1 0.6 %shard_map.74 = (bf16[192,384]{1,0:T(8,128)(2,1)S(1)}, bf16[192,384]{1,0:T(8,128)(2,1)S(1)}, bf16[192,384]{1,0:T(8,128)(2,1)S(1)}, bf16[192,384]{1,0:T(8,128)(2,...) custom-call(bf16[14,16,128]{2,1,0:T(8,128)(2,1)S(1)} %shard_map.69.refs_1_.after.refs_0_, ...), custom_call_target="tpu_custom_call" | custom-call | bytes 589824 | tf_op jit(solution)/shard_map/pallas_call | solution.py:19
  22.7 0.0 collective-permute-done.refs_0_.refs_11_
  22.7 0.0 collective-permute-done.2.refs_1_.refs_12_
  22.7 2.6 %shard_map.75 = (bf16[30,2,32,128]{3,2,1,0:T(8,128)(2,1)S(1)}, bf16[30,2,32,128]{3,2,1,0:T(8,128)(2,1)S(1)}, bf16[30,2,32,128]{3,2,1,0:T(8,128)(2,1)S(1)}, bf16[...) custom-call(bf16[32,2,16,128]{3,2,1,0:T(8,128)(2,1)S(1)} %collective-permute-done.refs_0_.refs_11_, ...), custom_call_target="tpu_custom_call" | custom-call | flops 1019215872 | bytes 3145728 | tf_op jit(solution)/shard_map/pallas_call | solution.py:19
  25.3 1.6 %collective-permute-start.6 = (bf16[28,2,32,128]{3,2,1,0:T(8,128)(2,1)S(1)}, bf16[28,2,32,128]{3,2,1,0:T(8,128)(2,1)S(1)}, u32[]{:S(2)}, u32[]{:S(2)}) collective-permute-start(bf16[28,2,32,128]{3,2,1,0:T(8,128)(2,1)S(1)} %get-tuple-element.41.refs_3_), channel_id=1, source_target_pairs={{2,0},{4,2},{6,4},{8,6},{10,8},{12,10},{14,12},{16,14},{18,16},{20... | collective-permute-start | bytes 1376264 | tf_op jit(solution)/shard_map/ppermute | solution.py:455
  26.9 0.0 collective-permute-done.7.refs_3_.refs_18_
  26.9 1.8 %shard_map.76 = (bf16[30,2,32,128]{3,2,1,0:T(8,128)(2,1)S(1)}, bf16[30,2,32,128]{3,2,1,0:T(8,128)(2,1)S(1)}, bf16[28,2,32,128]{3,2,1,0:T(8,128)(2,1)S(1)}) custom-call(bf16[32,2,16,128]{3,2,1,0:T(8,128)(2,1)S(1)} %get-tuple-element.34.after.refs_4_.refs_0_.refs_15_, bf16[32,2,16,128]{3,2,1,0:T(8,128)(2,1)S(1)} %shard_map.70.refs_5_.refs_1_.refs_16_, ...), custom_call_target="tpu_custom_call" | custom-call | flops 679477248 | bytes 2359296 | tf_op jit(solution)/shard_map/pallas_call | solution.py:19
  28.7 0.2 collective-permute-start.9
  28.9 6.1 %shard_map.77 = (f32[2,7,16,128]{3,2,1,0:T(8,128)S(1)}, f32[2,7,16,128]{3,2,1,0:T(8,128)S(1)}, bf16[26,2,32,128]{3,2,1,0:T(8,128)(2,1)S(1)}) custom-call(bf16[30,2,32,128]{3,2,1,0:T(8,128)(2,1)S(1)} %get-tuple-element.42.refs_0_, bf16[30,2,32,128]{3,2,1,0:T(8,128)(2,1)S(1)} %get-tuple-element.43.refs_4_.refs_1_, ...), custom_call_target="tpu_custom_call" | custom-call | tf_op jit(solution)/shard_map/pallas_call | solution.py:19
  35.1 0.1 collective-permute-start.8
  35.1 1.3 %collective-permute-done.8.two = f32[2,7,16,128]{3,2,1,0:T(8,128)S(1)} collective-permute-done((f32[2,7,16,128]{3,2,1,0:T(8,128)S(1)}, f32[2,7,16,128]{3,2,1,0:T(8,128)S(1)}, u32[]{:S(2)}, u32[]{:S(2)}) %collective-permute-start.8) | collective-permute-done | bytes 114720 | tf_op jit(solution)/shard_map/ppermute | solution.py:575
  36.5 0.0 collective-permute-done.6.after.refs_5_
  36.5 1.6 %collective-permute-start.10 = (f32[7,16,128]{2,1,0:T(8,128)S(1)}, f32[7,16,128]{2,1,0:T(8,128)S(1)}, u32[]{:S(2)}, u32[]{:S(2)}) collective-permute-start(f32[7,16,128]{2,1,0:T(8,128)S(1)} %get-tuple-element.60), channel_id=1, source_target_pairs={{0,1},{1,0},{2,3},{3,2},{4,5},{5,4},{6,7},{7,6},{8,9},{9,8},{10,11... | collective-permute-start | bytes 172040 | tf_op jit(solution)/shard_map/ppermute | solution.py:449
  38.0 0.2 collective-permute-start.12
  38.2 1.8 %collective-permute-start.11 = (f32[7,16,128]{2,1,0:T(8,128)S(1)}, f32[7,16,128]{2,1,0:T(8,128)S(1)}, u32[]{:S(2)}, u32[]{:S(2)}) collective-permute-start(f32[7,16,128]{2,1,0:T(8,128)S(1)} %get-tuple-element.55.after.refs_1_), channel_id=1, source_target_pairs={{0,4},{2,6},{4,0},{6,2},{8,12},{10,14},{12,8},{14,10},{16,20},{18,... | collective-permute-start | bytes 172040 | tf_op jit(solution)/shard_map/ppermute | solution.py:575
  40.0 0.0 collective-permute-done.9.refs_2_
  40.0 2.8 %shard_map.79 = (bf16[24,4,16,128]{3,2,1,0:T(8,128)(2,1)S(1)}, bf16[24,4,16,128]{3,2,1,0:T(8,128)(2,1)S(1)}) custom-call(f32[7,16,128]{2,1,0:T(8,128)S(1)} %get-tuple-element.55.after.refs_1_, bf16[192,384]{1,0:T(8,128)(2,1)S(1)} %get-tuple-element.47.refs_5_.refs_0_, bf16[192,384]{1,0:T(8,128)(2,1)S(1)} %get-tuple-element.56.refs_1_, ...), custom_call_target="tpu_custom_call" | custom-call | flops 1358954496 | bytes 2359296 | tf_op jit(solution)/shard_map/pallas_call | solution.py:19
  42.9 0.0 collective-permute-done.10.refs_2_
  42.9 0.4 collective-permute-done.11.refs_3_
  43.2 0.0 collective-permute-done.12.refs_4_
  43.3 1.2 %collective-permute-start.13 = (bf16[24,4,16,128]{3,2,1,0:T(8,128)(2,1)S(1)}, bf16[24,4,16,128]{3,2,1,0:T(8,128)(2,1)S(1)}, u32[]{:S(2)}, u32[]{:S(2)}) collective-permute-start(bf16[24,4,16,128]{3,2,1,0:T(8,128)(2,1)S(1)} %shard_map.81), channel_id=1, source_target_pairs={{0,1},{1,0},{2,3},{3,2},{4,5},{5,4},{6,7},{7,6},{8,9},{9,8},{10,11... | collective-permute-start | bytes 1179656 | tf_op jit(solution)/shard_map/ppermute | solution.py:449
  44.5 1.0 %collective-permute-start.14 = (f32[7,16,128]{2,1,0:T(8,128)S(1)}, f32[7,16,128]{2,1,0:T(8,128)S(1)}, u32[]{:S(2)}, u32[]{:S(2)}) collective-permute-start(f32[7,16,128]{2,1,0:T(8,128)S(1)} %shard_map.80.refs_1_.refs_0_), channel_id=1, source_target_pairs={{0,8},{2,10},{4,12},{6,14},{8,0},{10,2},{12,4},{14,6},{16,24},{18,... | collective-permute-start | bytes 172040 | tf_op jit(solution)/shard_map/ppermute | solution.py:575
  45.5 3.1 %collective-permute-done.14.refs_1_ = f32[7,16,128]{2,1,0:T(8,128)S(1)} collective-permute-done((f32[7,16,128]{2,1,0:T(8,128)S(1)}, f32[7,16,128]{2,1,0:T(8,128)S(1)}, u32[]{:S(2)}, u32[]{:S(2)}) %collective-permute-start.14) | collective-permute-done | bytes 57376 | tf_op jit(solution)/shard_map/ppermute | solution.py:575
  48.7 3.2 %collective-permute-start.15 = (f32[7,16,128]{2,1,0:T(8,128)S(1)}, f32[7,16,128]{2,1,0:T(8,128)S(1)}, u32[]{:S(2)}, u32[]{:S(2)}) collective-permute-start(f32[7,16,128]{2,1,0:T(8,128)S(1)} %shard_map.83.refs_0_), channel_id=1, source_target_pairs={{0,16},{2,18},{4,20},{6,22},{8,24},{10,26},{12,28},{14,30},{16,0},... | collective-permute-start | bytes 172040 | tf_op jit(solution)/shard_map/ppermute | solution.py:575
  51.9 2.2 %collective-permute-done.15.refs_1_ = f32[7,16,128]{2,1,0:T(8,128)S(1)} collective-permute-done((f32[7,16,128]{2,1,0:T(8,128)S(1)}, f32[7,16,128]{2,1,0:T(8,128)S(1)}, u32[]{:S(2)}, u32[]{:S(2)}) %collective-permute-start.15) | collective-permute-done | bytes 57376 | tf_op jit(solution)/shard_map/ppermute | solution.py:575
  54.0 0.1 collective-permute-start.16
  54.1 0.0 collective-permute-done.13.refs_1_
  54.1 1.9 %shard_map.82 = (f32[8,128]{1,0:T(8,128)S(1)}, bf16[16,4,48,128]{3,2,1,0:T(8,128)(2,1)}) custom-call(bf16[24,4,16,128]{3,2,1,0:T(8,128)(2,1)S(1)} %get-tuple-element.58.refs_0_, bf16[24,4,16,128]{3,2,1,0:T(8,128)(2,1)S(1)} %collective-permute-done.13.refs_1_), custom_call_target="tpu_custom_call" | custom-call | bytes 1572864 | tf_op jit(solution)/shard_map/pallas_call | solution.py:19
  56.0 0.0 collective-permute-done.16.other
  56.0 0.9 %shard_map.85 = (f32[27,16,32]{2,1,0:T(8,128)}, f32[27,16,32]{2,1,0:T(8,128)}) custom-call(f32[8,128]{1,0:T(8,128)S(1)} %get-tuple-element.62.after, f32[7,16,128]{2,1,0:T(8,128)S(1)} %shard_map.84.mine, f32[7,16,128]{2,1,0:T(8,128)S(1)} %collective-permute-done.16.other), custom_call_target="tpu_custom_call" | custom-call | tf_op jit(solution)/shard_map/pallas_call | solution.py:19
  (8 shorter events, 0.1 us)
Async XLA Ops:
  0.6 1.1 %copy-start = (bf16[16,4,48,128]{3,2,1,0:T(8,128)(2,1)S(1)}, bf16[16,4,48,128]{3,2,1,0:T(8,128)(2,1)}, u32[]{:S(2)}) copy-start(bf16[16,4,48,128]{3,2,1,0:T(8,128)(2,1)} %x_ref.4) | copy-start | bytes 2359300
  1.8 8.5 %copy-start.2 = (bf16[16,27,32]{2,0,1:T(8,128)(2,1)S(1)}, bf16[16,27,32]{2,0,1:T(8,128)(2,1)}, u32[]{:S(2)}) copy-start(bf16[16,27,32]{2,0,1:T(8,128)(2,1)} %param.6) | copy-start | bytes 82948
  1.8 8.5 %copy-start.3 = (bf16[16,27,32]{2,0,1:T(8,128)(2,1)S(1)}, bf16[16,27,32]{2,0,1:T(8,128)(2,1)}, u32[]{:S(2)}) copy-start(bf16[16,27,32]{2,0,1:T(8,128)(2,1)} %param.7) | copy-start | bytes 82948
  1.8 12.9 %copy-start.1 = (bf16[32,4,48,128]{3,2,1,0:T(8,128)(2,1)S(1)}, bf16[32,4,48,128]{3,2,1,0:T(8,128)(2,1)}, u32[]{:S(2)}) copy-start(bf16[32,4,48,128]{3,2,1,0:T(8,128)(2,1)} %x_ref.5) | copy-start | bytes 4718596
  2.5 10.1 %collective-permute-start.1 = (bf16[32,2,16,128]{3,2,1,0:T(8,128)(2,1)S(1)}, bf16[32,2,16,128]{3,2,1,0:T(8,128)(2,1)S(1)}, u32[]{:S(2)}, u32[]{:S(2)}) collective-permute-start(bf16[32,2,16,128]{3,2,1,0:T(8,128)(2,1)S(1)} %get-tuple-element.35), channel_id=1, source_target_pairs={{0,1},{1,0},{2,3},{3,2},{4,5},{5,4},{6,7},{7,6},{8,9},{9,8},{10,11... | collective-permute-start | bytes 786440 | tf_op jit(solution)/shard_map/ppermute | solution.py:449
  6.2 12.4 %collective-permute-start.3 = (bf16[32,2,16,128]{3,2,1,0:T(8,128)(2,1)S(1)}, bf16[32,2,16,128]{3,2,1,0:T(8,128)(2,1)S(1)}, u32[]{:S(2)}, u32[]{:S(2)}) collective-permute-start(bf16[32,2,16,128]{3,2,1,0:T(8,128)(2,1)S(1)} %get-tuple-element.37), channel_id=1, source_target_pairs={{0,1},{1,0},{2,3},{3,2},{4,5},{5,4},{6,7},{7,6},{8,9},{9,8},{10,11... | collective-permute-start | bytes 786440 | tf_op jit(solution)/shard_map/ppermute | solution.py:449
  6.3 12.3 %collective-permute-start.5 = (bf16[32,2,16,128]{3,2,1,0:T(8,128)(2,1)S(1)}, bf16[32,2,16,128]{3,2,1,0:T(8,128)(2,1)S(1)}, u32[]{:S(2)}, u32[]{:S(2)}) collective-permute-start(bf16[32,2,16,128]{3,2,1,0:T(8,128)(2,1)S(1)} %get-tuple-element.36.after.refs_2_.refs_13_), channel_id=1, source_target_pairs={{2,0},{4,2},{6,4},{8,6},{10,8},{12,10},{14,12},{16,14},{18,16},{20... | collective-permute-start | bytes 786440 | tf_op jit(solution)/shard_map/ppermute | solution.py:455
  10.2 12.5 %collective-permute-start = (bf16[32,2,16,128]{3,2,1,0:T(8,128)(2,1)S(1)}, bf16[32,2,16,128]{3,2,1,0:T(8,128)(2,1)S(1)}, u32[]{:S(2)}, u32[]{:S(2)}) collective-permute-start(bf16[32,2,16,128]{3,2,1,0:T(8,128)(2,1)S(1)} %get-tuple-element.34.after.refs_4_.refs_0_.refs_15_), channel_id=1, source_target_pairs={{0,2},{2,4},{4,6},{6,8},{8,10},{10,12},{12,14},{14,16},{16,18},{18... | collective-permute-start | bytes 786440 | tf_op jit(solution)/shard_map/ppermute | solution.py:452
  12.6 10.1 %collective-permute-start.2 = (bf16[32,2,16,128]{3,2,1,0:T(8,128)(2,1)S(1)}, bf16[32,2,16,128]{3,2,1,0:T(8,128)(2,1)S(1)}, u32[]{:S(2)}, u32[]{:S(2)}) collective-permute-start(bf16[32,2,16,128]{3,2,1,0:T(8,128)(2,1)S(1)} %shard_map.70.refs_5_.refs_1_.refs_16_), channel_id=1, source_target_pairs={{0,2},{2,4},{4,6},{6,8},{8,10},{10,12},{12,14},{14,16},{16,18},{18... | collective-permute-start | bytes 786440 | tf_op jit(solution)/shard_map/ppermute | solution.py:452
  12.6 5.9 %collective-permute-start.4 = (bf16[14,16,128]{2,1,0:T(8,128)(2,1)S(1)}, bf16[14,16,128]{2,1,0:T(8,128)(2,1)S(1)}, u32[]{:S(2)}, u32[]{:S(2)}) collective-permute-start(bf16[14,16,128]{2,1,0:T(8,128)(2,1)S(1)} %shard_map.69.refs_1_.after.refs_0_), channel_id=1, source_target_pairs={{0,1},{1,0},{2,3},{3,2},{4,5},{5,4},{6,7},{7,6},{8,9},{9,8},{10,11... | collective-permute-start | bytes 172040 | tf_op jit(solution)/shard_map/ppermute | solution.py:449
  18.6 8.3 %collective-permute-start.7 = (bf16[32,2,16,128]{3,2,1,0:T(8,128)(2,1)S(1)}, bf16[32,2,16,128]{3,2,1,0:T(8,128)(2,1)S(1)}, u32[]{:S(2)}, u32[]{:S(2)}) collective-permute-start(bf16[32,2,16,128]{3,2,1,0:T(8,128)(2,1)S(1)} %shard_map.73.refs_3_.refs_14_), channel_id=1, source_target_pairs={{2,0},{4,2},{6,4},{8,6},{10,8},{12,10},{14,12},{16,14},{18,16},{20... | collective-permute-start | bytes 786440 | tf_op jit(solution)/shard_map/ppermute | solution.py:455
  25.3 11.2 %collective-permute-start.6 = (bf16[28,2,32,128]{3,2,1,0:T(8,128)(2,1)S(1)}, bf16[28,2,32,128]{3,2,1,0:T(8,128)(2,1)S(1)}, u32[]{:S(2)}, u32[]{:S(2)}) collective-permute-start(bf16[28,2,32,128]{3,2,1,0:T(8,128)(2,1)S(1)} %get-tuple-element.41.refs_3_), channel_id=1, source_target_pairs={{2,0},{4,2},{6,4},{8,6},{10,8},{12,10},{14,12},{16,14},{18,16},{20... | collective-permute-start | bytes 1376264 | tf_op jit(solution)/shard_map/ppermute | solution.py:455
  28.7 11.4 %collective-permute-start.9 = (bf16[28,2,32,128]{3,2,1,0:T(8,128)(2,1)S(1)}, bf16[28,2,32,128]{3,2,1,0:T(8,128)(2,1)S(1)}, u32[]{:S(2)}, u32[]{:S(2)}) collective-permute-start(bf16[28,2,32,128]{3,2,1,0:T(8,128)(2,1)S(1)} %get-tuple-element.46.refs_4_), channel_id=1, source_target_pairs={{0,2},{2,4},{4,6},{6,8},{8,10},{10,12},{12,14},{14,16},{16,18},{18... | collective-permute-start | bytes 1376264 | tf_op jit(solution)/shard_map/ppermute | solution.py:452
  35.1 1.4 %collective-permute-start.8 = (f32[2,7,16,128]{3,2,1,0:T(8,128)S(1)}, f32[2,7,16,128]{3,2,1,0:T(8,128)S(1)}, u32[]{:S(2)}, u32[]{:S(2)}) collective-permute-start(f32[2,7,16,128]{3,2,1,0:T(8,128)S(1)} %get-tuple-element.54), channel_id=1, source_target_pairs={{0,2},{2,0},{4,6},{6,4},{8,10},{10,8},{12,14},{14,12},{16,18},{18,... | collective-permute-start | bytes 344072 | tf_op jit(solution)/shard_map/ppermute | solution.py:575
  36.5 6.4 %collective-permute-start.10 = (f32[7,16,128]{2,1,0:T(8,128)S(1)}, f32[7,16,128]{2,1,0:T(8,128)S(1)}, u32[]{:S(2)}, u32[]{:S(2)}) collective-permute-start(f32[7,16,128]{2,1,0:T(8,128)S(1)} %get-tuple-element.60), channel_id=1, source_target_pairs={{0,1},{1,0},{2,3},{3,2},{4,5},{5,4},{6,7},{7,6},{8,9},{9,8},{10,11... | collective-permute-start | bytes 172040 | tf_op jit(solution)/shard_map/ppermute | solution.py:449
  38.0 5.2 %collective-permute-start.12 = (f32[7,16,128]{2,1,0:T(8,128)S(1)}, f32[7,16,128]{2,1,0:T(8,128)S(1)}, u32[]{:S(2)}, u32[]{:S(2)}) collective-permute-start(f32[7,16,128]{2,1,0:T(8,128)S(1)} %get-tuple-element.60), channel_id=1, source_target_pairs={{0,5},{1,4},{2,7},{3,6},{4,1},{5,0},{6,3},{7,2},{8,13},{9,12},{10,... | collective-permute-start | bytes 172040 | tf_op jit(solution)/shard_map/ppermute | solution.py:581
  38.2 5.1 %collective-permute-start.11 = (f32[7,16,128]{2,1,0:T(8,128)S(1)}, f32[7,16,128]{2,1,0:T(8,128)S(1)}, u32[]{:S(2)}, u32[]{:S(2)}) collective-permute-start(f32[7,16,128]{2,1,0:T(8,128)S(1)} %get-tuple-element.55.after.refs_1_), channel_id=1, source_target_pairs={{0,4},{2,6},{4,0},{6,2},{8,12},{10,14},{12,8},{14,10},{16,20},{18,... | collective-permute-start | bytes 172040 | tf_op jit(solution)/shard_map/ppermute | solution.py:575
  43.3 10.8 %collective-permute-start.13 = (bf16[24,4,16,128]{3,2,1,0:T(8,128)(2,1)S(1)}, bf16[24,4,16,128]{3,2,1,0:T(8,128)(2,1)S(1)}, u32[]{:S(2)}, u32[]{:S(2)}) collective-permute-start(bf16[24,4,16,128]{3,2,1,0:T(8,128)(2,1)S(1)} %shard_map.81), channel_id=1, source_target_pairs={{0,1},{1,0},{2,3},{3,2},{4,5},{5,4},{6,7},{7,6},{8,9},{9,8},{10,11... | collective-permute-start | bytes 1179656 | tf_op jit(solution)/shard_map/ppermute | solution.py:449
  44.5 4.2 %collective-permute-start.14 = (f32[7,16,128]{2,1,0:T(8,128)S(1)}, f32[7,16,128]{2,1,0:T(8,128)S(1)}, u32[]{:S(2)}, u32[]{:S(2)}) collective-permute-start(f32[7,16,128]{2,1,0:T(8,128)S(1)} %shard_map.80.refs_1_.refs_0_), channel_id=1, source_target_pairs={{0,8},{2,10},{4,12},{6,14},{8,0},{10,2},{12,4},{14,6},{16,24},{18,... | collective-permute-start | bytes 172040 | tf_op jit(solution)/shard_map/ppermute | solution.py:575
  48.7 5.3 %collective-permute-start.15 = (f32[7,16,128]{2,1,0:T(8,128)S(1)}, f32[7,16,128]{2,1,0:T(8,128)S(1)}, u32[]{:S(2)}, u32[]{:S(2)}) collective-permute-start(f32[7,16,128]{2,1,0:T(8,128)S(1)} %shard_map.83.refs_0_), channel_id=1, source_target_pairs={{0,16},{2,18},{4,20},{6,22},{8,24},{10,26},{12,28},{14,30},{16,0},... | collective-permute-start | bytes 172040 | tf_op jit(solution)/shard_map/ppermute | solution.py:575
  54.0 2.0 %collective-permute-start.16 = (f32[7,16,128]{2,1,0:T(8,128)S(1)}, f32[7,16,128]{2,1,0:T(8,128)S(1)}, u32[]{:S(2)}, u32[]{:S(2)}) collective-permute-start(f32[7,16,128]{2,1,0:T(8,128)S(1)} %shard_map.84.mine), channel_id=1, source_target_pairs={{0,2},{2,0},{4,6},{6,4},{8,10},{10,8},{12,14},{14,12},{16,18},{18,... | collective-permute-start | bytes 172040 | tf_op jit(solution)/shard_map/ppermute | solution.py:575

commit v19 on v18

--- a/solution.py
+++ b/solution.py
@@ -344,16 +344,21 @@
         place(send, keep)
 
 
+def tail_kernel(after, weight, above, below, slope, first):
+    del after
+    first_deltas(weight, [([above], [below])], [slope], [first])
+
+
 def field_kernel_back(inner, groups, after, *refs):
     del after
     refs = list(refs)
     back, weight = refs.pop(0), refs.pop(0)
-    before, first, last, behind = [[refs.pop(0)] for _ in range(4)]
-    slopes = [refs.pop(0) for _ in range(2)]
-    middle = [refs.pop(0) for _ in range(inner)]
-    outs, ends = refs[:groups], refs[groups:]
-    first_deltas(back, [(before, first), (last, behind)], slopes, ends)
-    firsts = [ends[0]] + middle + [ends[1]]
+    above, below = [[refs.pop(0)] for _ in range(2)]
+    slope = refs.pop(0)
+    later = [refs.pop(0) for _ in range(inner + 1)]
+    outs, head = refs[:groups], refs[groups]
+    first_deltas(back, [(above, below)], [slope], [head])
+    firsts = [head] + later
 
     def one(r):
         row = 2 * r
@@ -580,10 +585,18 @@
                 pairs_of.append((i * extent + k, there))
         return lax.ppermute(value, ("slab", "chan"), pairs_of)
 
+    (tail,) = call(
+        tail_kernel,
+        many(1, share + 2),
+        [keep, second_back, deltas[-1], delta_after, slopes[-1]],
+        flops=work * share,
+        moved=space * 2,
+        loose=1,
+    )
     plain = slabs & (slabs - 1) == 0 and slabs >= 4
     if plain:
         kept = call(
-            split_kernel, [portion] * extent, [delta_after, keep, stepped(send, 1)], loose=1
+            split_kernel, [portion] * extent, [tail, keep, stepped(send, 1)], loose=1
         )
         shares = [kept[0]] + [to_chan(kept[j], extent - j) for j in range(1, extent)]
         shares += [stepped(kept[j], 2, extent - j) for j in range(extent)]
@@ -593,10 +606,8 @@
     made = call(
         functools.partial(field_kernel_back, pairs - 1, extent),
         [jax.ShapeDtypeStruct((share, planes, size, depth), BF16)] * extent,
-        [after, second_back, first_back]
-        + [delta_before, deltas[0], deltas[-1], delta_after, slopes[0], slopes[-1]]
-        + inner,
-        [room(share + 2), room(share + 2)],
+        [after, second_back, first_back, delta_before, deltas[0], slopes[0]] + inner + [tail],
+        [room(share + 2)],
         flops=work * (pairs + 2) * share,
         moved=space * 6,
         loose=1,

time: 57.1 us -> 57.1 us (level)
  waiting for transfers between devices: 11.9 us -> 11.2 us
    ppermute x5, waiting for transfers between devices: 6.98 us -> 6.31 us  [stepped(): return lax.ppermute(value, 'slab', [(i, i ^ stride) for i in range(slabs)])]
    pallas_call x19 -> x20, Pallas kernels: 19.5 us -> 19.7 us  [call(): pl.pallas_call(kernel, out_shape=outs, in_specs=[still] * loose + [whole]...]
  transfers between devices with their start and end apart: 17 -> 17, of which waited for: 6 -> 6; matrix products, arithmetic and copies ran while one was open for 0% -> 0% of each run, Pallas kernels for 31% -> 32%
where the time goes in v19:
time: 57.1 us; the launch traced here: 56.9 us
  starting transfers between devices  24 us (42%)
  Pallas kernels  19.7 us (35%)
  waiting for transfers between devices  11.2 us (20%)
  local copies, waits for them, and re-layouts  1.14 us (2%)
  between operations  0.82 us (1%)
    pallas_call x20, Pallas kernels, call(): pl.pallas_call(kernel, out_shape=outs, in_specs=[still] * loose + [whole]...  19.7 us
    ppermute x3, starting transfers between devices, to_prev(): lax.ppermute(value, 'slab', [((i + 1) % slabs, i) for i in range(slabs)])  9.06 us
    ppermute x5, starting transfers between devices, to_chan(): lax.ppermute(value, 'chan', [(i, (i + shift) % extent) for i in range(ext...  7.92 us
    ppermute x5, starting transfers between devices, stepped(): return lax.ppermute(value, 'slab', [(i, i ^ stride) for i in range(slabs)])  6.63 us
    ppermute x5, waiting for transfers between devices, stepped(): return lax.ppermute(value, 'slab', [(i, i ^ stride) for i in range(slabs)])  6.31 us
    ppermute x5, waiting for transfers between devices, to_chan(): lax.ppermute(value, 'chan', [(i, (i + shift) % extent) for i in range(ext...  4.89 us
  transfers between devices with their start and end apart: 17, of which 6 were waited for; matrix products, arithmetic and copies ran while one was open for 0% of the time, Pallas kernels for 32%

profile of v19, /device:TPU:0, one launch (start us, length us, event | category | flops | bytes accessed | tf_op | source)
XLA Modules:
  0.0 56.9 jit_solution(6090971562337503302)
XLA Ops:
  0.6 0.0 copy-start
  0.6 1.1 %copy-done = bf16[16,4,48,128]{3,2,1,0:T(8,128)(2,1)S(1)} copy-done((bf16[16,4,48,128]{3,2,1,0:T(8,128)(2,1)S(1)}, bf16[16,4,48,128]{3,2,1,0:T(8,128)(2,1)}, u32[]{:S(2)}) %copy-start) | copy-done | bytes 786456
  1.8 0.0 copy-start.2
  1.8 0.0 copy-start.3
  1.8 0.0 copy-start.1
  1.8 0.7 %shard_map.67 = (bf16[32,2,16,128]{3,2,1,0:T(8,128)(2,1)S(1)}, bf16[32,2,16,128]{3,2,1,0:T(8,128)(2,1)S(1)}) custom-call(bf16[16,4,48,128]{3,2,1,0:T(8,128)(2,1)S(1)} %copy-done, bf16[16,4,48,128]{3,2,1,0:T(8,128)(2,1)S(1)} %copy-done), custom_call_target="tpu_custom_call" | custom-call | bytes 1179648 | tf_op jit(solution)/shard_map/pallas_call | solution.py:19
  2.5 3.0 %collective-permute-start.1 = (bf16[32,2,16,128]{3,2,1,0:T(8,128)(2,1)S(1)}, bf16[32,2,16,128]{3,2,1,0:T(8,128)(2,1)S(1)}, u32[]{:S(2)}, u32[]{:S(2)}) collective-permute-start(bf16[32,2,16,128]{3,2,1,0:T(8,128)(2,1)S(1)} %get-tuple-element.35), channel_id=1, source_target_pairs={{0,1},{1,0},{2,3},{3,2},{4,5},{5,4},{6,7},{7,6},{8,9},{9,8},{10,11... | collective-permute-start | bytes 786440 | tf_op jit(solution)/shard_map/ppermute | solution.py:454
  5.5 0.7 %shard_map.68 = (bf16[32,2,16,128]{3,2,1,0:T(8,128)(2,1)S(1)}, bf16[32,2,16,128]{3,2,1,0:T(8,128)(2,1)S(1)}) custom-call(bf16[32,2,16,128]{3,2,1,0:T(8,128)(2,1)S(1)} %get-tuple-element.34.after.refs_4_.refs_0_.refs_15_, bf16[16,4,48,128]{3,2,1,0:T(8,128)(2,1)S(1)} %copy-done), custom_call_target="tpu_custom_call" | custom-call | bytes 1179648 | tf_op jit(solution)/shard_map/pallas_call | solution.py:19
  6.2 0.1 collective-permute-start.3
  6.3 4.0 %collective-permute-start.5 = (bf16[32,2,16,128]{3,2,1,0:T(8,128)(2,1)S(1)}, bf16[32,2,16,128]{3,2,1,0:T(8,128)(2,1)S(1)}, u32[]{:S(2)}, u32[]{:S(2)}) collective-permute-start(bf16[32,2,16,128]{3,2,1,0:T(8,128)(2,1)S(1)} %get-tuple-element.36.after.refs_2_.refs_13_), channel_id=1, source_target_pairs={{2,0},{4,2},{6,4},{8,6},{10,8},{12,10},{14,12},{16,14},{18,16},{20... | collective-permute-start | bytes 786440 | tf_op jit(solution)/shard_map/ppermute | solution.py:460
  10.2 0.0 collective-permute-start
  10.2 0.0 copy-done.2
  10.2 0.0 copy-done.3
  10.2 0.1 shard_map.69.refs_1_.after.refs_0_
  10.4 2.3 %collective-permute-done.1.refs_0_ = bf16[32,2,16,128]{3,2,1,0:T(8,128)(2,1)S(1)} collective-permute-done((bf16[32,2,16,128]{3,2,1,0:T(8,128)(2,1)S(1)}, bf16[32,2,16,128]{3,2,1,0:T(8,128)(2,1)S(1)}, u32[]{:S(2)}, u32[]{:S(2)}) %collective-permute-start.1) | collective-permute-done | bytes 262176 | tf_op jit(solution)/shard_map/ppermute | solution.py:454
  12.6 0.0 collective-permute-start.2
  12.6 2.1 %collective-permute-start.4 = (bf16[14,16,128]{2,1,0:T(8,128)(2,1)S(1)}, bf16[14,16,128]{2,1,0:T(8,128)(2,1)S(1)}, u32[]{:S(2)}, u32[]{:S(2)}) collective-permute-start(bf16[14,16,128]{2,1,0:T(8,128)(2,1)S(1)} %shard_map.69.refs_1_.after.refs_0_), channel_id=1, source_target_pairs={{0,1},{1,0},{2,3},{3,2},{4,5},{5,4},{6,7},{7,6},{8,9},{9,8},{10,11... | collective-permute-start | bytes 172040 | tf_op jit(solution)/shard_map/ppermute | solution.py:454
  14.7 0.0 copy-done.1
  14.7 1.2 %shard_map.71 = (bf16[28,2,32,128]{3,2,1,0:T(8,128)(2,1)S(1)}, bf16[28,2,32,128]{3,2,1,0:T(8,128)(2,1)S(1)}) custom-call(bf16[14,16,128]{2,1,0:T(8,128)(2,1)S(1)} %shard_map.69.refs_1_.after.refs_0_, bf16[32,4,48,128]{3,2,1,0:T(8,128)(2,1)S(1)} %copy-done.1), custom_call_target="tpu_custom_call" | custom-call | bytes 3145728 | tf_op jit(solution)/shard_map/pallas_call | solution.py:19
  15.9 2.6 %collective-permute-done.4.refs_2_.refs_1_ = bf16[14,16,128]{2,1,0:T(8,128)(2,1)S(1)} collective-permute-done((bf16[14,16,128]{2,1,0:T(8,128)(2,1)S(1)}, bf16[14,16,128]{2,1,0:T(8,128)(2,1)S(1)}, u32[]{:S(2)}, u32[]{:S(2)}) %collective-permute-start.4) | collective-permute-done | bytes 57376 | tf_op jit(solution)/shard_map/ppermute | solution.py:454
  18.6 0.0 collective-permute-done.3.refs_0_
  18.6 0.0 collective-permute-done.5.refs_1_.refs_2_.refs_17_
  18.6 3.5 %collective-permute-start.6 = (bf16[32,2,16,128]{3,2,1,0:T(8,128)(2,1)S(1)}, bf16[32,2,16,128]{3,2,1,0:T(8,128)(2,1)S(1)}, u32[]{:S(2)}, u32[]{:S(2)}) collective-permute-start(bf16[32,2,16,128]{3,2,1,0:T(8,128)(2,1)S(1)} %shard_map.73.refs_3_.refs_14_), channel_id=1, source_target_pairs={{2,0},{4,2},{6,4},{8,6},{10,8},{12,10},{14,12},{16,14},{18,16},{20... | collective-permute-start | bytes 786440 | tf_op jit(solution)/shard_map/ppermute | solution.py:460
  22.1 0.6 %shard_map.74 = (bf16[192,384]{1,0:T(8,128)(2,1)S(1)}, bf16[192,384]{1,0:T(8,128)(2,1)S(1)}, bf16[192,384]{1,0:T(8,128)(2,1)S(1)}, bf16[192,384]{1,0:T(8,128)(2,...) custom-call(bf16[14,16,128]{2,1,0:T(8,128)(2,1)S(1)} %shard_map.69.refs_1_.after.refs_0_, ...), custom_call_target="tpu_custom_call" | custom-call | bytes 589824 | tf_op jit(solution)/shard_map/pallas_call | solution.py:19
  22.7 0.0 collective-permute-done.refs_0_.refs_11_
  22.7 0.0 collective-permute-done.2.refs_1_.refs_12_
  22.7 2.6 %shard_map.75 = (bf16[30,2,32,128]{3,2,1,0:T(8,128)(2,1)S(1)}, bf16[30,2,32,128]{3,2,1,0:T(8,128)(2,1)S(1)}, bf16[30,2,32,128]{3,2,1,0:T(8,128)(2,1)S(1)}, bf16[...) custom-call(bf16[32,2,16,128]{3,2,1,0:T(8,128)(2,1)S(1)} %collective-permute-done.refs_0_.refs_11_, ...), custom_call_target="tpu_custom_call" | custom-call | flops 1019215872 | bytes 3145728 | tf_op jit(solution)/shard_map/pallas_call | solution.py:19
  25.3 1.6 %collective-permute-start.7 = (bf16[28,2,32,128]{3,2,1,0:T(8,128)(2,1)S(1)}, bf16[28,2,32,128]{3,2,1,0:T(8,128)(2,1)S(1)}, u32[]{:S(2)}, u32[]{:S(2)}) collective-permute-start(bf16[28,2,32,128]{3,2,1,0:T(8,128)(2,1)S(1)} %get-tuple-element.45.refs_3_), channel_id=1, source_target_pairs={{2,0},{4,2},{6,4},{8,6},{10,8},{12,10},{14,12},{16,14},{18,16},{20... | collective-permute-start | bytes 1376264 | tf_op jit(solution)/shard_map/ppermute | solution.py:460
  26.9 0.0 collective-permute-done.6.refs_3_.refs_18_
  26.9 1.8 %shard_map.76 = (bf16[30,2,32,128]{3,2,1,0:T(8,128)(2,1)S(1)}, bf16[30,2,32,128]{3,2,1,0:T(8,128)(2,1)S(1)}, bf16[28,2,32,128]{3,2,1,0:T(8,128)(2,1)S(1)}) custom-call(bf16[32,2,16,128]{3,2,1,0:T(8,128)(2,1)S(1)} %get-tuple-element.34.after.refs_4_.refs_0_.refs_15_, bf16[32,2,16,128]{3,2,1,0:T(8,128)(2,1)S(1)} %shard_map.70.refs_5_.refs_1_.refs_16_, ...), custom_call_target="tpu_custom_call" | custom-call | flops 679477248 | bytes 2359296 | tf_op jit(solution)/shard_map/pallas_call | solution.py:19
  28.7 0.2 collective-permute-start.9
  28.9 6.1 %shard_map.77 = (f32[2,7,16,128]{3,2,1,0:T(8,128)S(1)}, f32[2,7,16,128]{3,2,1,0:T(8,128)S(1)}, bf16[26,2,32,128]{3,2,1,0:T(8,128)(2,1)S(1)}) custom-call(bf16[30,2,32,128]{3,2,1,0:T(8,128)(2,1)S(1)} %get-tuple-element.41.refs_0_, bf16[30,2,32,128]{3,2,1,0:T(8,128)(2,1)S(1)} %get-tuple-element.42.refs_4_.refs_1_, ...), custom_call_target="tpu_custom_call" | custom-call | tf_op jit(solution)/shard_map/pallas_call | solution.py:19
  35.0 0.1 collective-permute-start.8
  35.1 0.0 collective-permute-done.7.below
  35.1 0.9 %shard_map.78.after.refs_6_ = bf16[26,2,32,128]{3,2,1,0:T(8,128)(2,1)S(1)} custom-call(f32[2,7,16,128]{3,2,1,0:T(8,128)S(1)} %get-tuple-element.53.after.one, bf16[192,384]{1,0:T(8,128)(2,1)S(1)} %get-tuple-element.47.refs_5_.weight.refs_0_, bf16[28,2,32,128]{3,2,1,0:T(8,128)(2,1)S(1)} %get-tuple-element.46.refs_4_.above, ...), custom_call_target="tpu_custom_call" | custom-call | flops 339738624 | bytes 786432 | tf_op jit(solution)/shard_map/pallas_call | solution.py:19
  36.0 0.4 collective-permute-done.8.two
  36.5 1.6 %collective-permute-start.10 = (f32[7,16,128]{2,1,0:T(8,128)S(1)}, f32[7,16,128]{2,1,0:T(8,128)S(1)}, u32[]{:S(2)}, u32[]{:S(2)}) collective-permute-start(f32[7,16,128]{2,1,0:T(8,128)S(1)} %get-tuple-element.60), channel_id=1, source_target_pairs={{0,1},{1,0},{2,3},{3,2},{4,5},{5,4},{6,7},{7,6},{8,9},{9,8},{10,11... | collective-permute-start | bytes 172040 | tf_op jit(solution)/shard_map/ppermute | solution.py:454
  38.0 0.2 collective-permute-start.12
  38.2 1.8 %collective-permute-start.11 = (f32[7,16,128]{2,1,0:T(8,128)S(1)}, f32[7,16,128]{2,1,0:T(8,128)S(1)}, u32[]{:S(2)}, u32[]{:S(2)}) collective-permute-start(f32[7,16,128]{2,1,0:T(8,128)S(1)} %get-tuple-element.55.after.refs_1_), channel_id=1, source_target_pairs={{0,4},{2,6},{4,0},{6,2},{8,12},{10,14},{12,8},{14,10},{16,20},{18,... | collective-permute-start | bytes 172040 | tf_op jit(solution)/shard_map/ppermute | solution.py:580
  40.0 0.0 collective-permute-done.9.refs_2_
  40.0 2.1 %shard_map.80 = (bf16[24,4,16,128]{3,2,1,0:T(8,128)(2,1)S(1)}, bf16[24,4,16,128]{3,2,1,0:T(8,128)(2,1)S(1)}) custom-call(f32[7,16,128]{2,1,0:T(8,128)S(1)} %get-tuple-element.55.after.refs_1_, bf16[192,384]{1,0:T(8,128)(2,1)S(1)} %get-tuple-element.47.refs_5_.weight.refs_0_, bf16[192,384]{1,0:T(8,128)(2,1)S(1)} %get-tuple-element.56.refs_1_, ...), custom_call_target="tpu_custom_call" | custom-call | flops 1358954496 | bytes 2359296 | tf_op jit(solution)/shard_map/pallas_call | solution.py:19
  42.2 0.0 collective-permute-done.10.refs_2_
  42.2 1.0 %collective-permute-done.11.refs_3_ = f32[7,16,128]{2,1,0:T(8,128)S(1)} collective-permute-done((f32[7,16,128]{2,1,0:T(8,128)S(1)}, f32[7,16,128]{2,1,0:T(8,128)S(1)}, u32[]{:S(2)}, u32[]{:S(2)}) %collective-permute-start.11) | collective-permute-done | bytes 57376 | tf_op jit(solution)/shard_map/ppermute | solution.py:580
  43.2 0.0 collective-permute-done.12.refs_4_
  43.2 1.2 %collective-permute-start.13 = (bf16[24,4,16,128]{3,2,1,0:T(8,128)(2,1)S(1)}, bf16[24,4,16,128]{3,2,1,0:T(8,128)(2,1)S(1)}, u32[]{:S(2)}, u32[]{:S(2)}) collective-permute-start(bf16[24,4,16,128]{3,2,1,0:T(8,128)(2,1)S(1)} %shard_map.82), channel_id=1, source_target_pairs={{0,1},{1,0},{2,3},{3,2},{4,5},{5,4},{6,7},{7,6},{8,9},{9,8},{10,11... | collective-permute-start | bytes 1179656 | tf_op jit(solution)/shard_map/ppermute | solution.py:454
  44.5 1.5 %collective-permute-start.14 = (f32[7,16,128]{2,1,0:T(8,128)S(1)}, f32[7,16,128]{2,1,0:T(8,128)S(1)}, u32[]{:S(2)}, u32[]{:S(2)}) collective-permute-start(f32[7,16,128]{2,1,0:T(8,128)S(1)} %shard_map.81.refs_1_.refs_0_), channel_id=1, source_target_pairs={{0,8},{2,10},{4,12},{6,14},{8,0},{10,2},{12,4},{14,6},{16,24},{18,... | collective-permute-start | bytes 172040 | tf_op jit(solution)/shard_map/ppermute | solution.py:580
  45.9 2.7 %collective-permute-done.14.refs_1_ = f32[7,16,128]{2,1,0:T(8,128)S(1)} collective-permute-done((f32[7,16,128]{2,1,0:T(8,128)S(1)}, f32[7,16,128]{2,1,0:T(8,128)S(1)}, u32[]{:S(2)}, u32[]{:S(2)}) %collective-permute-start.14) | collective-permute-done | bytes 57376 | tf_op jit(solution)/shard_map/ppermute | solution.py:580
  48.7 3.2 %collective-permute-start.15 = (f32[7,16,128]{2,1,0:T(8,128)S(1)}, f32[7,16,128]{2,1,0:T(8,128)S(1)}, u32[]{:S(2)}, u32[]{:S(2)}) collective-permute-start(f32[7,16,128]{2,1,0:T(8,128)S(1)} %shard_map.84.refs_0_), channel_id=1, source_target_pairs={{0,16},{2,18},{4,20},{6,22},{8,24},{10,26},{12,28},{14,30},{16,0},... | collective-permute-start | bytes 172040 | tf_op jit(solution)/shard_map/ppermute | solution.py:580
  51.8 2.2 %collective-permute-done.15.refs_1_ = f32[7,16,128]{2,1,0:T(8,128)S(1)} collective-permute-done((f32[7,16,128]{2,1,0:T(8,128)S(1)}, f32[7,16,128]{2,1,0:T(8,128)S(1)}, u32[]{:S(2)}, u32[]{:S(2)}) %collective-permute-start.15) | collective-permute-done | bytes 57376 | tf_op jit(solution)/shard_map/ppermute | solution.py:580
  54.0 0.1 collective-permute-start.16
  54.1 0.0 collective-permute-done.13.refs_1_
  54.1 1.9 %shard_map.83 = (f32[8,128]{1,0:T(8,128)S(1)}, bf16[16,4,48,128]{3,2,1,0:T(8,128)(2,1)}) custom-call(bf16[24,4,16,128]{3,2,1,0:T(8,128)(2,1)S(1)} %get-tuple-element.58.refs_0_, bf16[24,4,16,128]{3,2,1,0:T(8,128)(2,1)S(1)} %collective-permute-done.13.refs_1_), custom_call_target="tpu_custom_call" | custom-call | bytes 1572864 | tf_op jit(solution)/shard_map/pallas_call | solution.py:19
  56.0 0.0 collective-permute-done.16.other
  56.0 0.9 %shard_map.86 = (f32[27,16,32]{2,1,0:T(8,128)}, f32[27,16,32]{2,1,0:T(8,128)}) custom-call(f32[8,128]{1,0:T(8,128)S(1)} %get-tuple-element.62.after, f32[7,16,128]{2,1,0:T(8,128)S(1)} %shard_map.85.mine, f32[7,16,128]{2,1,0:T(8,128)S(1)} %collective-permute-done.16.other), custom_call_target="tpu_custom_call" | custom-call | tf_op jit(solution)/shard_map/pallas_call | solution.py:19
  (8 shorter events, 0.0 us)
Async XLA Ops:
  0.6 1.1 %copy-start = (bf16[16,4,48,128]{3,2,1,0:T(8,128)(2,1)S(1)}, bf16[16,4,48,128]{3,2,1,0:T(8,128)(2,1)}, u32[]{:S(2)}) copy-start(bf16[16,4,48,128]{3,2,1,0:T(8,128)(2,1)} %x_ref.4) | copy-start | bytes 2359300
  1.8 8.5 %copy-start.2 = (bf16[16,27,32]{2,0,1:T(8,128)(2,1)S(1)}, bf16[16,27,32]{2,0,1:T(8,128)(2,1)}, u32[]{:S(2)}) copy-start(bf16[16,27,32]{2,0,1:T(8,128)(2,1)} %param.6) | copy-start | bytes 82948
  1.8 8.5 %copy-start.3 = (bf16[16,27,32]{2,0,1:T(8,128)(2,1)S(1)}, bf16[16,27,32]{2,0,1:T(8,128)(2,1)}, u32[]{:S(2)}) copy-start(bf16[16,27,32]{2,0,1:T(8,128)(2,1)} %param.7) | copy-start | bytes 82948
  1.8 12.9 %copy-start.1 = (bf16[32,4,48,128]{3,2,1,0:T(8,128)(2,1)S(1)}, bf16[32,4,48,128]{3,2,1,0:T(8,128)(2,1)}, u32[]{:S(2)}) copy-start(bf16[32,4,48,128]{3,2,1,0:T(8,128)(2,1)} %x_ref.5) | copy-start | bytes 4718596
  2.5 10.1 %collective-permute-start.1 = (bf16[32,2,16,128]{3,2,1,0:T(8,128)(2,1)S(1)}, bf16[32,2,16,128]{3,2,1,0:T(8,128)(2,1)S(1)}, u32[]{:S(2)}, u32[]{:S(2)}) collective-permute-start(bf16[32,2,16,128]{3,2,1,0:T(8,128)(2,1)S(1)} %get-tuple-element.35), channel_id=1, source_target_pairs={{0,1},{1,0},{2,3},{3,2},{4,5},{5,4},{6,7},{7,6},{8,9},{9,8},{10,11... | collective-permute-start | bytes 786440 | tf_op jit(solution)/shard_map/ppermute | solution.py:454
  6.2 12.4 %collective-permute-start.3 = (bf16[32,2,16,128]{3,2,1,0:T(8,128)(2,1)S(1)}, bf16[32,2,16,128]{3,2,1,0:T(8,128)(2,1)S(1)}, u32[]{:S(2)}, u32[]{:S(2)}) collective-permute-start(bf16[32,2,16,128]{3,2,1,0:T(8,128)(2,1)S(1)} %get-tuple-element.37), channel_id=1, source_target_pairs={{0,1},{1,0},{2,3},{3,2},{4,5},{5,4},{6,7},{7,6},{8,9},{9,8},{10,11... | collective-permute-start | bytes 786440 | tf_op jit(solution)/shard_map/ppermute | solution.py:454
  6.3 12.3 %collective-permute-start.5 = (bf16[32,2,16,128]{3,2,1,0:T(8,128)(2,1)S(1)}, bf16[32,2,16,128]{3,2,1,0:T(8,128)(2,1)S(1)}, u32[]{:S(2)}, u32[]{:S(2)}) collective-permute-start(bf16[32,2,16,128]{3,2,1,0:T(8,128)(2,1)S(1)} %get-tuple-element.36.after.refs_2_.refs_13_), channel_id=1, source_target_pairs={{2,0},{4,2},{6,4},{8,6},{10,8},{12,10},{14,12},{16,14},{18,16},{20... | collective-permute-start | bytes 786440 | tf_op jit(solution)/shard_map/ppermute | solution.py:460
  10.2 12.5 %collective-permute-start = (bf16[32,2,16,128]{3,2,1,0:T(8,128)(2,1)S(1)}, bf16[32,2,16,128]{3,2,1,0:T(8,128)(2,1)S(1)}, u32[]{:S(2)}, u32[]{:S(2)}) collective-permute-start(bf16[32,2,16,128]{3,2,1,0:T(8,128)(2,1)S(1)} %get-tuple-element.34.after.refs_4_.refs_0_.refs_15_), channel_id=1, source_target_pairs={{0,2},{2,4},{4,6},{6,8},{8,10},{10,12},{12,14},{14,16},{16,18},{18... | collective-permute-start | bytes 786440 | tf_op jit(solution)/shard_map/ppermute | solution.py:457
  12.6 10.1 %collective-permute-start.2 = (bf16[32,2,16,128]{3,2,1,0:T(8,128)(2,1)S(1)}, bf16[32,2,16,128]{3,2,1,0:T(8,128)(2,1)S(1)}, u32[]{:S(2)}, u32[]{:S(2)}) collective-permute-start(bf16[32,2,16,128]{3,2,1,0:T(8,128)(2,1)S(1)} %shard_map.70.refs_5_.refs_1_.refs_16_), channel_id=1, source_target_pairs={{0,2},{2,4},{4,6},{6,8},{8,10},{10,12},{12,14},{14,16},{16,18},{18... | collective-permute-start | bytes 786440 | tf_op jit(solution)/shard_map/ppermute | solution.py:457
  12.6 5.9 %collective-permute-start.4 = (bf16[14,16,128]{2,1,0:T(8,128)(2,1)S(1)}, bf16[14,16,128]{2,1,0:T(8,128)(2,1)S(1)}, u32[]{:S(2)}, u32[]{:S(2)}) collective-permute-start(bf16[14,16,128]{2,1,0:T(8,128)(2,1)S(1)} %shard_map.69.refs_1_.after.refs_0_), channel_id=1, source_target_pairs={{0,1},{1,0},{2,3},{3,2},{4,5},{5,4},{6,7},{7,6},{8,9},{9,8},{10,11... | collective-permute-start | bytes 172040 | tf_op jit(solution)/shard_map/ppermute | solution.py:454
  18.6 8.3 %collective-permute-start.6 = (bf16[32,2,16,128]{3,2,1,0:T(8,128)(2,1)S(1)}, bf16[32,2,16,128]{3,2,1,0:T(8,128)(2,1)S(1)}, u32[]{:S(2)}, u32[]{:S(2)}) collective-permute-start(bf16[32,2,16,128]{3,2,1,0:T(8,128)(2,1)S(1)} %shard_map.73.refs_3_.refs_14_), channel_id=1, source_target_pairs={{2,0},{4,2},{6,4},{8,6},{10,8},{12,10},{14,12},{16,14},{18,16},{20... | collective-permute-start | bytes 786440 | tf_op jit(solution)/shard_map/ppermute | solution.py:460
  25.3 9.8 %collective-permute-start.7 = (bf16[28,2,32,128]{3,2,1,0:T(8,128)(2,1)S(1)}, bf16[28,2,32,128]{3,2,1,0:T(8,128)(2,1)S(1)}, u32[]{:S(2)}, u32[]{:S(2)}) collective-permute-start(bf16[28,2,32,128]{3,2,1,0:T(8,128)(2,1)S(1)} %get-tuple-element.45.refs_3_), channel_id=1, source_target_pairs={{2,0},{4,2},{6,4},{8,6},{10,8},{12,10},{14,12},{16,14},{18,16},{20... | collective-permute-start | bytes 1376264 | tf_op jit(solution)/shard_map/ppermute | solution.py:460
  28.7 11.3 %collective-permute-start.9 = (bf16[28,2,32,128]{3,2,1,0:T(8,128)(2,1)S(1)}, bf16[28,2,32,128]{3,2,1,0:T(8,128)(2,1)S(1)}, u32[]{:S(2)}, u32[]{:S(2)}) collective-permute-start(bf16[28,2,32,128]{3,2,1,0:T(8,128)(2,1)S(1)} %get-tuple-element.46.refs_4_.above), channel_id=1, source_target_pairs={{0,2},{2,4},{4,6},{6,8},{8,10},{10,12},{12,14},{14,16},{16,18},{18... | collective-permute-start | bytes 1376264 | tf_op jit(solution)/shard_map/ppermute | solution.py:457
  35.0 1.4 %collective-permute-start.8 = (f32[2,7,16,128]{3,2,1,0:T(8,128)S(1)}, f32[2,7,16,128]{3,2,1,0:T(8,128)S(1)}, u32[]{:S(2)}, u32[]{:S(2)}) collective-permute-start(f32[2,7,16,128]{3,2,1,0:T(8,128)S(1)} %get-tuple-element.54), channel_id=1, source_target_pairs={{0,2},{2,0},{4,6},{6,4},{8,10},{10,8},{12,14},{14,12},{16,18},{18,... | collective-permute-start | bytes 344072 | tf_op jit(solution)/shard_map/ppermute | solution.py:580
  36.5 5.7 %collective-permute-start.10 = (f32[7,16,128]{2,1,0:T(8,128)S(1)}, f32[7,16,128]{2,1,0:T(8,128)S(1)}, u32[]{:S(2)}, u32[]{:S(2)}) collective-permute-start(f32[7,16,128]{2,1,0:T(8,128)S(1)} %get-tuple-element.60), channel_id=1, source_target_pairs={{0,1},{1,0},{2,3},{3,2},{4,5},{5,4},{6,7},{7,6},{8,9},{9,8},{10,11... | collective-permute-start | bytes 172040 | tf_op jit(solution)/shard_map/ppermute | solution.py:454
  38.0 5.2 %collective-permute-start.12 = (f32[7,16,128]{2,1,0:T(8,128)S(1)}, f32[7,16,128]{2,1,0:T(8,128)S(1)}, u32[]{:S(2)}, u32[]{:S(2)}) collective-permute-start(f32[7,16,128]{2,1,0:T(8,128)S(1)} %get-tuple-element.60), channel_id=1, source_target_pairs={{0,5},{1,4},{2,7},{3,6},{4,1},{5,0},{6,3},{7,2},{8,13},{9,12},{10,... | collective-permute-start | bytes 172040 | tf_op jit(solution)/shard_map/ppermute | solution.py:586
  38.2 5.0 %collective-permute-start.11 = (f32[7,16,128]{2,1,0:T(8,128)S(1)}, f32[7,16,128]{2,1,0:T(8,128)S(1)}, u32[]{:S(2)}, u32[]{:S(2)}) collective-permute-start(f32[7,16,128]{2,1,0:T(8,128)S(1)} %get-tuple-element.55.after.refs_1_), channel_id=1, source_target_pairs={{0,4},{2,6},{4,0},{6,2},{8,12},{10,14},{12,8},{14,10},{16,20},{18,... | collective-permute-start | bytes 172040 | tf_op jit(solution)/shard_map/ppermute | solution.py:580
  43.2 10.8 %collective-permute-start.13 = (bf16[24,4,16,128]{3,2,1,0:T(8,128)(2,1)S(1)}, bf16[24,4,16,128]{3,2,1,0:T(8,128)(2,1)S(1)}, u32[]{:S(2)}, u32[]{:S(2)}) collective-permute-start(bf16[24,4,16,128]{3,2,1,0:T(8,128)(2,1)S(1)} %shard_map.82), channel_id=1, source_target_pairs={{0,1},{1,0},{2,3},{3,2},{4,5},{5,4},{6,7},{7,6},{8,9},{9,8},{10,11... | collective-permute-start | bytes 1179656 | tf_op jit(solution)/shard_map/ppermute | solution.py:454
  44.5 4.2 %collective-permute-start.14 = (f32[7,16,128]{2,1,0:T(8,128)S(1)}, f32[7,16,128]{2,1,0:T(8,128)S(1)}, u32[]{:S(2)}, u32[]{:S(2)}) collective-permute-start(f32[7,16,128]{2,1,0:T(8,128)S(1)} %shard_map.81.refs_1_.refs_0_), channel_id=1, source_target_pairs={{0,8},{2,10},{4,12},{6,14},{8,0},{10,2},{12,4},{14,6},{16,24},{18,... | collective-permute-start | bytes 172040 | tf_op jit(solution)/shard_map/ppermute | solution.py:580
  48.7 5.3 %collective-permute-start.15 = (f32[7,16,128]{2,1,0:T(8,128)S(1)}, f32[7,16,128]{2,1,0:T(8,128)S(1)}, u32[]{:S(2)}, u32[]{:S(2)}) collective-permute-start(f32[7,16,128]{2,1,0:T(8,128)S(1)} %shard_map.84.refs_0_), channel_id=1, source_target_pairs={{0,16},{2,18},{4,20},{6,22},{8,24},{10,26},{12,28},{14,30},{16,0},... | collective-permute-start | bytes 172040 | tf_op jit(solution)/shard_map/ppermute | solution.py:580
  54.0 2.0 %collective-permute-start.16 = (f32[7,16,128]{2,1,0:T(8,128)S(1)}, f32[7,16,128]{2,1,0:T(8,128)S(1)}, u32[]{:S(2)}, u32[]{:S(2)}) collective-permute-start(f32[7,16,128]{2,1,0:T(8,128)S(1)} %shard_map.85.mine), channel_id=1, source_target_pairs={{0,2},{2,0},{4,6},{6,4},{8,10},{10,8},{12,14},{14,12},{16,18},{18,... | collective-permute-start | bytes 172040 | tf_op jit(solution)/shard_map/ppermute | solution.py:580

commit v20 on v19

--- a/solution.py
+++ b/solution.py
@@ -234,7 +234,7 @@
 
 
 def weight_loop(total, pieces, first_row, deltas, delta_row, count):
-    blocks = [k for k in range(1, 13) if count // 2 % k == 0 and k * len(deltas) <= 12]
+    blocks = [k for k in range(1, 13) if count // 2 % k == 0 and k * len(deltas) <= 24]
     together = max(blocks, default=1)
 
     def product(r):

time: 57.1 us -> 57.1 us (level)
  no operation moved by 1% of the time
where the time goes in v20:
time: 57.1 us; the launch traced here: 56.9 us
  starting transfers between devices  24 us (42%)
  Pallas kernels  19.7 us (35%)
  waiting for transfers between devices  11.2 us (20%)
  local copies, waits for them, and re-layouts  1.14 us (2%)
  between operations  0.82 us (1%)
    pallas_call x20, Pallas kernels, call(): pl.pallas_call(kernel, out_shape=outs, in_specs=[still] * loose + [whole]...  19.7 us
    ppermute x3, starting transfers between devices, to_prev(): lax.ppermute(value, 'slab', [((i + 1) % slabs, i) for i in range(slabs)])  9.06 us
    ppermute x5, starting transfers between devices, to_chan(): lax.ppermute(value, 'chan', [(i, (i + shift) % extent) for i in range(ext...  7.92 us
    ppermute x5, starting transfers between devices, stepped(): return lax.ppermute(value, 'slab', [(i, i ^ stride) for i in range(slabs)])  6.63 us
    ppermute x5, waiting for transfers between devices, stepped(): return lax.ppermute(value, 'slab', [(i, i ^ stride) for i in range(slabs)])  6.31 us
    ppermute x5, waiting for transfers between devices, to_chan(): lax.ppermute(value, 'chan', [(i, (i + shift) % extent) for i in range(ext...  4.89 us
  transfers between devices with their start and end apart: 17, of which 6 were waited for; matrix products, arithmetic and copies ran while one was open for 0% of the time, Pallas kernels for 32%

profile of v20, /device:TPU:0, one launch (start us, length us, event | category | flops | bytes accessed | tf_op | source)
XLA Modules:
  0.0 56.9 jit_solution(6090971562337503302)
XLA Ops:
  0.6 0.0 copy-start
  0.6 1.1 %copy-done = bf16[16,4,48,128]{3,2,1,0:T(8,128)(2,1)S(1)} copy-done((bf16[16,4,48,128]{3,2,1,0:T(8,128)(2,1)S(1)}, bf16[16,4,48,128]{3,2,1,0:T(8,128)(2,1)}, u32[]{:S(2)}) %copy-start) | copy-done | bytes 786456
  1.8 0.0 copy-start.2
  1.8 0.0 copy-start.3
  1.8 0.0 copy-start.1
  1.8 0.7 %shard_map.67 = (bf16[32,2,16,128]{3,2,1,0:T(8,128)(2,1)S(1)}, bf16[32,2,16,128]{3,2,1,0:T(8,128)(2,1)S(1)}) custom-call(bf16[16,4,48,128]{3,2,1,0:T(8,128)(2,1)S(1)} %copy-done, bf16[16,4,48,128]{3,2,1,0:T(8,128)(2,1)S(1)} %copy-done), custom_call_target="tpu_custom_call" | custom-call | bytes 1179648 | tf_op jit(solution)/shard_map/pallas_call | solution.py:19
  2.5 3.0 %collective-permute-start.1 = (bf16[32,2,16,128]{3,2,1,0:T(8,128)(2,1)S(1)}, bf16[32,2,16,128]{3,2,1,0:T(8,128)(2,1)S(1)}, u32[]{:S(2)}, u32[]{:S(2)}) collective-permute-start(bf16[32,2,16,128]{3,2,1,0:T(8,128)(2,1)S(1)} %get-tuple-element.35), channel_id=1, source_target_pairs={{0,1},{1,0},{2,3},{3,2},{4,5},{5,4},{6,7},{7,6},{8,9},{9,8},{10,11... | collective-permute-start | bytes 786440 | tf_op jit(solution)/shard_map/ppermute | solution.py:454
  5.5 0.7 %shard_map.68 = (bf16[32,2,16,128]{3,2,1,0:T(8,128)(2,1)S(1)}, bf16[32,2,16,128]{3,2,1,0:T(8,128)(2,1)S(1)}) custom-call(bf16[32,2,16,128]{3,2,1,0:T(8,128)(2,1)S(1)} %get-tuple-element.34.after.refs_4_.refs_0_.refs_15_, bf16[16,4,48,128]{3,2,1,0:T(8,128)(2,1)S(1)} %copy-done), custom_call_target="tpu_custom_call" | custom-call | bytes 1179648 | tf_op jit(solution)/shard_map/pallas_call | solution.py:19
  6.2 0.1 collective-permute-start.3
  6.3 4.0 %collective-permute-start.5 = (bf16[32,2,16,128]{3,2,1,0:T(8,128)(2,1)S(1)}, bf16[32,2,16,128]{3,2,1,0:T(8,128)(2,1)S(1)}, u32[]{:S(2)}, u32[]{:S(2)}) collective-permute-start(bf16[32,2,16,128]{3,2,1,0:T(8,128)(2,1)S(1)} %get-tuple-element.36.after.refs_2_.refs_13_), channel_id=1, source_target_pairs={{2,0},{4,2},{6,4},{8,6},{10,8},{12,10},{14,12},{16,14},{18,16},{20... | collective-permute-start | bytes 786440 | tf_op jit(solution)/shard_map/ppermute | solution.py:460
  10.2 0.0 collective-permute-start
  10.2 0.0 copy-done.2
  10.2 0.0 copy-done.3
  10.2 0.1 shard_map.69.refs_1_.after.refs_0_
  10.4 2.3 %collective-permute-done.1.refs_0_ = bf16[32,2,16,128]{3,2,1,0:T(8,128)(2,1)S(1)} collective-permute-done((bf16[32,2,16,128]{3,2,1,0:T(8,128)(2,1)S(1)}, bf16[32,2,16,128]{3,2,1,0:T(8,128)(2,1)S(1)}, u32[]{:S(2)}, u32[]{:S(2)}) %collective-permute-start.1) | collective-permute-done | bytes 262176 | tf_op jit(solution)/shard_map/ppermute | solution.py:454
  12.6 0.0 collective-permute-start.2
  12.6 2.1 %collective-permute-start.4 = (bf16[14,16,128]{2,1,0:T(8,128)(2,1)S(1)}, bf16[14,16,128]{2,1,0:T(8,128)(2,1)S(1)}, u32[]{:S(2)}, u32[]{:S(2)}) collective-permute-start(bf16[14,16,128]{2,1,0:T(8,128)(2,1)S(1)} %shard_map.69.refs_1_.after.refs_0_), channel_id=1, source_target_pairs={{0,1},{1,0},{2,3},{3,2},{4,5},{5,4},{6,7},{7,6},{8,9},{9,8},{10,11... | collective-permute-start | bytes 172040 | tf_op jit(solution)/shard_map/ppermute | solution.py:454
  14.7 0.0 copy-done.1
  14.7 1.2 %shard_map.71 = (bf16[28,2,32,128]{3,2,1,0:T(8,128)(2,1)S(1)}, bf16[28,2,32,128]{3,2,1,0:T(8,128)(2,1)S(1)}) custom-call(bf16[14,16,128]{2,1,0:T(8,128)(2,1)S(1)} %shard_map.69.refs_1_.after.refs_0_, bf16[32,4,48,128]{3,2,1,0:T(8,128)(2,1)S(1)} %copy-done.1), custom_call_target="tpu_custom_call" | custom-call | bytes 3145728 | tf_op jit(solution)/shard_map/pallas_call | solution.py:19
  15.9 2.6 %collective-permute-done.4.refs_2_.refs_1_ = bf16[14,16,128]{2,1,0:T(8,128)(2,1)S(1)} collective-permute-done((bf16[14,16,128]{2,1,0:T(8,128)(2,1)S(1)}, bf16[14,16,128]{2,1,0:T(8,128)(2,1)S(1)}, u32[]{:S(2)}, u32[]{:S(2)}) %collective-permute-start.4) | collective-permute-done | bytes 57376 | tf_op jit(solution)/shard_map/ppermute | solution.py:454
  18.6 0.0 collective-permute-done.3.refs_0_
  18.6 0.0 collective-permute-done.5.refs_1_.refs_2_.refs_17_
  18.6 3.5 %collective-permute-start.6 = (bf16[32,2,16,128]{3,2,1,0:T(8,128)(2,1)S(1)}, bf16[32,2,16,128]{3,2,1,0:T(8,128)(2,1)S(1)}, u32[]{:S(2)}, u32[]{:S(2)}) collective-permute-start(bf16[32,2,16,128]{3,2,1,0:T(8,128)(2,1)S(1)} %shard_map.73.refs_3_.refs_14_), channel_id=1, source_target_pairs={{2,0},{4,2},{6,4},{8,6},{10,8},{12,10},{14,12},{16,14},{18,16},{20... | collective-permute-start | bytes 786440 | tf_op jit(solution)/shard_map/ppermute | solution.py:460
  22.1 0.6 %shard_map.74 = (bf16[192,384]{1,0:T(8,128)(2,1)S(1)}, bf16[192,384]{1,0:T(8,128)(2,1)S(1)}, bf16[192,384]{1,0:T(8,128)(2,1)S(1)}, bf16[192,384]{1,0:T(8,128)(2,...) custom-call(bf16[14,16,128]{2,1,0:T(8,128)(2,1)S(1)} %shard_map.69.refs_1_.after.refs_0_, ...), custom_call_target="tpu_custom_call" | custom-call | bytes 589824 | tf_op jit(solution)/shard_map/pallas_call | solution.py:19
  22.7 0.0 collective-permute-done.refs_0_.refs_11_
  22.7 0.0 collective-permute-done.2.refs_1_.refs_12_
  22.7 2.6 %shard_map.75 = (bf16[30,2,32,128]{3,2,1,0:T(8,128)(2,1)S(1)}, bf16[30,2,32,128]{3,2,1,0:T(8,128)(2,1)S(1)}, bf16[30,2,32,128]{3,2,1,0:T(8,128)(2,1)S(1)}, bf16[...) custom-call(bf16[32,2,16,128]{3,2,1,0:T(8,128)(2,1)S(1)} %collective-permute-done.refs_0_.refs_11_, ...), custom_call_target="tpu_custom_call" | custom-call | flops 1019215872 | bytes 3145728 | tf_op jit(solution)/shard_map/pallas_call | solution.py:19
  25.3 1.6 %collective-permute-start.7 = (bf16[28,2,32,128]{3,2,1,0:T(8,128)(2,1)S(1)}, bf16[28,2,32,128]{3,2,1,0:T(8,128)(2,1)S(1)}, u32[]{:S(2)}, u32[]{:S(2)}) collective-permute-start(bf16[28,2,32,128]{3,2,1,0:T(8,128)(2,1)S(1)} %get-tuple-element.45.refs_3_), channel_id=1, source_target_pairs={{2,0},{4,2},{6,4},{8,6},{10,8},{12,10},{14,12},{16,14},{18,16},{20... | collective-permute-start | bytes 1376264 | tf_op jit(solution)/shard_map/ppermute | solution.py:460
  26.9 0.0 collective-permute-done.6.refs_3_.refs_18_
  26.9 1.8 %shard_map.76 = (bf16[30,2,32,128]{3,2,1,0:T(8,128)(2,1)S(1)}, bf16[30,2,32,128]{3,2,1,0:T(8,128)(2,1)S(1)}, bf16[28,2,32,128]{3,2,1,0:T(8,128)(2,1)S(1)}) custom-call(bf16[32,2,16,128]{3,2,1,0:T(8,128)(2,1)S(1)} %get-tuple-element.34.after.refs_4_.refs_0_.refs_15_, bf16[32,2,16,128]{3,2,1,0:T(8,128)(2,1)S(1)} %shard_map.70.refs_5_.refs_1_.refs_16_, ...), custom_call_target="tpu_custom_call" | custom-call | flops 679477248 | bytes 2359296 | tf_op jit(solution)/shard_map/pallas_call | solution.py:19
  28.7 0.2 collective-permute-start.9
  28.9 6.1 %shard_map.77 = (f32[2,7,16,128]{3,2,1,0:T(8,128)S(1)}, f32[2,7,16,128]{3,2,1,0:T(8,128)S(1)}, bf16[26,2,32,128]{3,2,1,0:T(8,128)(2,1)S(1)}) custom-call(bf16[30,2,32,128]{3,2,1,0:T(8,128)(2,1)S(1)} %get-tuple-element.41.refs_0_, bf16[30,2,32,128]{3,2,1,0:T(8,128)(2,1)S(1)} %get-tuple-element.42.refs_4_.refs_1_, ...), custom_call_target="tpu_custom_call" | custom-call | tf_op jit(solution)/shard_map/pallas_call | solution.py:19
  35.0 0.1 collective-permute-start.8
  35.1 0.0 collective-permute-done.7.below
  35.1 0.9 %shard_map.78.after.refs_6_ = bf16[26,2,32,128]{3,2,1,0:T(8,128)(2,1)S(1)} custom-call(f32[2,7,16,128]{3,2,1,0:T(8,128)S(1)} %get-tuple-element.53.after.one, bf16[192,384]{1,0:T(8,128)(2,1)S(1)} %get-tuple-element.47.refs_5_.weight.refs_0_, bf16[28,2,32,128]{3,2,1,0:T(8,128)(2,1)S(1)} %get-tuple-element.46.refs_4_.above, ...), custom_call_target="tpu_custom_call" | custom-call | flops 339738624 | bytes 786432 | tf_op jit(solution)/shard_map/pallas_call | solution.py:19
  36.0 0.4 collective-permute-done.8.two
  36.5 1.6 %collective-permute-start.10 = (f32[7,16,128]{2,1,0:T(8,128)S(1)}, f32[7,16,128]{2,1,0:T(8,128)S(1)}, u32[]{:S(2)}, u32[]{:S(2)}) collective-permute-start(f32[7,16,128]{2,1,0:T(8,128)S(1)} %get-tuple-element.60), channel_id=1, source_target_pairs={{0,1},{1,0},{2,3},{3,2},{4,5},{5,4},{6,7},{7,6},{8,9},{9,8},{10,11... | collective-permute-start | bytes 172040 | tf_op jit(solution)/shard_map/ppermute | solution.py:454
  38.0 0.2 collective-permute-start.12
  38.2 1.8 %collective-permute-start.11 = (f32[7,16,128]{2,1,0:T(8,128)S(1)}, f32[7,16,128]{2,1,0:T(8,128)S(1)}, u32[]{:S(2)}, u32[]{:S(2)}) collective-permute-start(f32[7,16,128]{2,1,0:T(8,128)S(1)} %get-tuple-element.55.after.refs_1_), channel_id=1, source_target_pairs={{0,4},{2,6},{4,0},{6,2},{8,12},{10,14},{12,8},{14,10},{16,20},{18,... | collective-permute-start | bytes 172040 | tf_op jit(solution)/shard_map/ppermute | solution.py:580
  40.0 0.0 collective-permute-done.9.refs_2_
  40.0 2.1 %shard_map.80 = (bf16[24,4,16,128]{3,2,1,0:T(8,128)(2,1)S(1)}, bf16[24,4,16,128]{3,2,1,0:T(8,128)(2,1)S(1)}) custom-call(f32[7,16,128]{2,1,0:T(8,128)S(1)} %get-tuple-element.55.after.refs_1_, bf16[192,384]{1,0:T(8,128)(2,1)S(1)} %get-tuple-element.47.refs_5_.weight.refs_0_, bf16[192,384]{1,0:T(8,128)(2,1)S(1)} %get-tuple-element.56.refs_1_, ...), custom_call_target="tpu_custom_call" | custom-call | flops 1358954496 | bytes 2359296 | tf_op jit(solution)/shard_map/pallas_call | solution.py:19
  42.2 0.0 collective-permute-done.10.refs_2_
  42.2 1.0 %collective-permute-done.11.refs_3_ = f32[7,16,128]{2,1,0:T(8,128)S(1)} collective-permute-done((f32[7,16,128]{2,1,0:T(8,128)S(1)}, f32[7,16,128]{2,1,0:T(8,128)S(1)}, u32[]{:S(2)}, u32[]{:S(2)}) %collective-permute-start.11) | collective-permute-done | bytes 57376 | tf_op jit(solution)/shard_map/ppermute | solution.py:580
  43.2 0.0 collective-permute-done.12.refs_4_
  43.2 1.2 %collective-permute-start.13 = (bf16[24,4,16,128]{3,2,1,0:T(8,128)(2,1)S(1)}, bf16[24,4,16,128]{3,2,1,0:T(8,128)(2,1)S(1)}, u32[]{:S(2)}, u32[]{:S(2)}) collective-permute-start(bf16[24,4,16,128]{3,2,1,0:T(8,128)(2,1)S(1)} %shard_map.82), channel_id=1, source_target_pairs={{0,1},{1,0},{2,3},{3,2},{4,5},{5,4},{6,7},{7,6},{8,9},{9,8},{10,11... | collective-permute-start | bytes 1179656 | tf_op jit(solution)/shard_map/ppermute | solution.py:454
  44.5 1.5 %collective-permute-start.14 = (f32[7,16,128]{2,1,0:T(8,128)S(1)}, f32[7,16,128]{2,1,0:T(8,128)S(1)}, u32[]{:S(2)}, u32[]{:S(2)}) collective-permute-start(f32[7,16,128]{2,1,0:T(8,128)S(1)} %shard_map.81.refs_1_.refs_0_), channel_id=1, source_target_pairs={{0,8},{2,10},{4,12},{6,14},{8,0},{10,2},{12,4},{14,6},{16,24},{18,... | collective-permute-start | bytes 172040 | tf_op jit(solution)/shard_map/ppermute | solution.py:580
  45.9 2.7 %collective-permute-done.14.refs_1_ = f32[7,16,128]{2,1,0:T(8,128)S(1)} collective-permute-done((f32[7,16,128]{2,1,0:T(8,128)S(1)}, f32[7,16,128]{2,1,0:T(8,128)S(1)}, u32[]{:S(2)}, u32[]{:S(2)}) %collective-permute-start.14) | collective-permute-done | bytes 57376 | tf_op jit(solution)/shard_map/ppermute | solution.py:580
  48.7 3.2 %collective-permute-start.15 = (f32[7,16,128]{2,1,0:T(8,128)S(1)}, f32[7,16,128]{2,1,0:T(8,128)S(1)}, u32[]{:S(2)}, u32[]{:S(2)}) collective-permute-start(f32[7,16,128]{2,1,0:T(8,128)S(1)} %shard_map.84.refs_0_), channel_id=1, source_target_pairs={{0,16},{2,18},{4,20},{6,22},{8,24},{10,26},{12,28},{14,30},{16,0},... | collective-permute-start | bytes 172040 | tf_op jit(solution)/shard_map/ppermute | solution.py:580
  51.8 2.2 %collective-permute-done.15.refs_1_ = f32[7,16,128]{2,1,0:T(8,128)S(1)} collective-permute-done((f32[7,16,128]{2,1,0:T(8,128)S(1)}, f32[7,16,128]{2,1,0:T(8,128)S(1)}, u32[]{:S(2)}, u32[]{:S(2)}) %collective-permute-start.15) | collective-permute-done | bytes 57376 | tf_op jit(solution)/shard_map/ppermute | solution.py:580
  54.0 0.1 collective-permute-start.16
  54.1 0.0 collective-permute-done.13.refs_1_
  54.1 1.9 %shard_map.83 = (f32[8,128]{1,0:T(8,128)S(1)}, bf16[16,4,48,128]{3,2,1,0:T(8,128)(2,1)}) custom-call(bf16[24,4,16,128]{3,2,1,0:T(8,128)(2,1)S(1)} %get-tuple-element.58.refs_0_, bf16[24,4,16,128]{3,2,1,0:T(8,128)(2,1)S(1)} %collective-permute-done.13.refs_1_), custom_call_target="tpu_custom_call" | custom-call | bytes 1572864 | tf_op jit(solution)/shard_map/pallas_call | solution.py:19
  56.0 0.0 collective-permute-done.16.other
  56.0 0.9 %shard_map.86 = (f32[27,16,32]{2,1,0:T(8,128)}, f32[27,16,32]{2,1,0:T(8,128)}) custom-call(f32[8,128]{1,0:T(8,128)S(1)} %get-tuple-element.62.after, f32[7,16,128]{2,1,0:T(8,128)S(1)} %shard_map.85.mine, f32[7,16,128]{2,1,0:T(8,128)S(1)} %collective-permute-done.16.other), custom_call_target="tpu_custom_call" | custom-call | tf_op jit(solution)/shard_map/pallas_call | solution.py:19
  (8 shorter events, 0.0 us)
Async XLA Ops:
  0.6 1.1 %copy-start = (bf16[16,4,48,128]{3,2,1,0:T(8,128)(2,1)S(1)}, bf16[16,4,48,128]{3,2,1,0:T(8,128)(2,1)}, u32[]{:S(2)}) copy-start(bf16[16,4,48,128]{3,2,1,0:T(8,128)(2,1)} %x_ref.4) | copy-start | bytes 2359300
  1.8 8.5 %copy-start.2 = (bf16[16,27,32]{2,0,1:T(8,128)(2,1)S(1)}, bf16[16,27,32]{2,0,1:T(8,128)(2,1)}, u32[]{:S(2)}) copy-start(bf16[16,27,32]{2,0,1:T(8,128)(2,1)} %param.6) | copy-start | bytes 82948
  1.8 8.5 %copy-start.3 = (bf16[16,27,32]{2,0,1:T(8,128)(2,1)S(1)}, bf16[16,27,32]{2,0,1:T(8,128)(2,1)}, u32[]{:S(2)}) copy-start(bf16[16,27,32]{2,0,1:T(8,128)(2,1)} %param.7) | copy-start | bytes 82948
  1.8 12.9 %copy-start.1 = (bf16[32,4,48,128]{3,2,1,0:T(8,128)(2,1)S(1)}, bf16[32,4,48,128]{3,2,1,0:T(8,128)(2,1)}, u32[]{:S(2)}) copy-start(bf16[32,4,48,128]{3,2,1,0:T(8,128)(2,1)} %x_ref.5) | copy-start | bytes 4718596
  2.5 10.1 %collective-permute-start.1 = (bf16[32,2,16,128]{3,2,1,0:T(8,128)(2,1)S(1)}, bf16[32,2,16,128]{3,2,1,0:T(8,128)(2,1)S(1)}, u32[]{:S(2)}, u32[]{:S(2)}) collective-permute-start(bf16[32,2,16,128]{3,2,1,0:T(8,128)(2,1)S(1)} %get-tuple-element.35), channel_id=1, source_target_pairs={{0,1},{1,0},{2,3},{3,2},{4,5},{5,4},{6,7},{7,6},{8,9},{9,8},{10,11... | collective-permute-start | bytes 786440 | tf_op jit(solution)/shard_map/ppermute | solution.py:454
  6.2 12.4 %collective-permute-start.3 = (bf16[32,2,16,128]{3,2,1,0:T(8,128)(2,1)S(1)}, bf16[32,2,16,128]{3,2,1,0:T(8,128)(2,1)S(1)}, u32[]{:S(2)}, u32[]{:S(2)}) collective-permute-start(bf16[32,2,16,128]{3,2,1,0:T(8,128)(2,1)S(1)} %get-tuple-element.37), channel_id=1, source_target_pairs={{0,1},{1,0},{2,3},{3,2},{4,5},{5,4},{6,7},{7,6},{8,9},{9,8},{10,11... | collective-permute-start | bytes 786440 | tf_op jit(solution)/shard_map/ppermute | solution.py:454
  6.3 12.3 %collective-permute-start.5 = (bf16[32,2,16,128]{3,2,1,0:T(8,128)(2,1)S(1)}, bf16[32,2,16,128]{3,2,1,0:T(8,128)(2,1)S(1)}, u32[]{:S(2)}, u32[]{:S(2)}) collective-permute-start(bf16[32,2,16,128]{3,2,1,0:T(8,128)(2,1)S(1)} %get-tuple-element.36.after.refs_2_.refs_13_), channel_id=1, source_target_pairs={{2,0},{4,2},{6,4},{8,6},{10,8},{12,10},{14,12},{16,14},{18,16},{20... | collective-permute-start | bytes 786440 | tf_op jit(solution)/shard_map/ppermute | solution.py:460
  10.2 12.5 %collective-permute-start = (bf16[32,2,16,128]{3,2,1,0:T(8,128)(2,1)S(1)}, bf16[32,2,16,128]{3,2,1,0:T(8,128)(2,1)S(1)}, u32[]{:S(2)}, u32[]{:S(2)}) collective-permute-start(bf16[32,2,16,128]{3,2,1,0:T(8,128)(2,1)S(1)} %get-tuple-element.34.after.refs_4_.refs_0_.refs_15_), channel_id=1, source_target_pairs={{0,2},{2,4},{4,6},{6,8},{8,10},{10,12},{12,14},{14,16},{16,18},{18... | collective-permute-start | bytes 786440 | tf_op jit(solution)/shard_map/ppermute | solution.py:457
  12.6 10.1 %collective-permute-start.2 = (bf16[32,2,16,128]{3,2,1,0:T(8,128)(2,1)S(1)}, bf16[32,2,16,128]{3,2,1,0:T(8,128)(2,1)S(1)}, u32[]{:S(2)}, u32[]{:S(2)}) collective-permute-start(bf16[32,2,16,128]{3,2,1,0:T(8,128)(2,1)S(1)} %shard_map.70.refs_5_.refs_1_.refs_16_), channel_id=1, source_target_pairs={{0,2},{2,4},{4,6},{6,8},{8,10},{10,12},{12,14},{14,16},{16,18},{18... | collective-permute-start | bytes 786440 | tf_op jit(solution)/shard_map/ppermute | solution.py:457
  12.6 5.9 %collective-permute-start.4 = (bf16[14,16,128]{2,1,0:T(8,128)(2,1)S(1)}, bf16[14,16,128]{2,1,0:T(8,128)(2,1)S(1)}, u32[]{:S(2)}, u32[]{:S(2)}) collective-permute-start(bf16[14,16,128]{2,1,0:T(8,128)(2,1)S(1)} %shard_map.69.refs_1_.after.refs_0_), channel_id=1, source_target_pairs={{0,1},{1,0},{2,3},{3,2},{4,5},{5,4},{6,7},{7,6},{8,9},{9,8},{10,11... | collective-permute-start | bytes 172040 | tf_op jit(solution)/shard_map/ppermute | solution.py:454
  18.6 8.3 %collective-permute-start.6 = (bf16[32,2,16,128]{3,2,1,0:T(8,128)(2,1)S(1)}, bf16[32,2,16,128]{3,2,1,0:T(8,128)(2,1)S(1)}, u32[]{:S(2)}, u32[]{:S(2)}) collective-permute-start(bf16[32,2,16,128]{3,2,1,0:T(8,128)(2,1)S(1)} %shard_map.73.refs_3_.refs_14_), channel_id=1, source_target_pairs={{2,0},{4,2},{6,4},{8,6},{10,8},{12,10},{14,12},{16,14},{18,16},{20... | collective-permute-start | bytes 786440 | tf_op jit(solution)/shard_map/ppermute | solution.py:460
  25.3 9.8 %collective-permute-start.7 = (bf16[28,2,32,128]{3,2,1,0:T(8,128)(2,1)S(1)}, bf16[28,2,32,128]{3,2,1,0:T(8,128)(2,1)S(1)}, u32[]{:S(2)}, u32[]{:S(2)}) collective-permute-start(bf16[28,2,32,128]{3,2,1,0:T(8,128)(2,1)S(1)} %get-tuple-element.45.refs_3_), channel_id=1, source_target_pairs={{2,0},{4,2},{6,4},{8,6},{10,8},{12,10},{14,12},{16,14},{18,16},{20... | collective-permute-start | bytes 1376264 | tf_op jit(solution)/shard_map/ppermute | solution.py:460
  28.7 11.3 %collective-permute-start.9 = (bf16[28,2,32,128]{3,2,1,0:T(8,128)(2,1)S(1)}, bf16[28,2,32,128]{3,2,1,0:T(8,128)(2,1)S(1)}, u32[]{:S(2)}, u32[]{:S(2)}) collective-permute-start(bf16[28,2,32,128]{3,2,1,0:T(8,128)(2,1)S(1)} %get-tuple-element.46.refs_4_.above), channel_id=1, source_target_pairs={{0,2},{2,4},{4,6},{6,8},{8,10},{10,12},{12,14},{14,16},{16,18},{18... | collective-permute-start | bytes 1376264 | tf_op jit(solution)/shard_map/ppermute | solution.py:457
  35.0 1.4 %collective-permute-start.8 = (f32[2,7,16,128]{3,2,1,0:T(8,128)S(1)}, f32[2,7,16,128]{3,2,1,0:T(8,128)S(1)}, u32[]{:S(2)}, u32[]{:S(2)}) collective-permute-start(f32[2,7,16,128]{3,2,1,0:T(8,128)S(1)} %get-tuple-element.54), channel_id=1, source_target_pairs={{0,2},{2,0},{4,6},{6,4},{8,10},{10,8},{12,14},{14,12},{16,18},{18,... | collective-permute-start | bytes 344072 | tf_op jit(solution)/shard_map/ppermute | solution.py:580
  36.5 5.7 %collective-permute-start.10 = (f32[7,16,128]{2,1,0:T(8,128)S(1)}, f32[7,16,128]{2,1,0:T(8,128)S(1)}, u32[]{:S(2)}, u32[]{:S(2)}) collective-permute-start(f32[7,16,128]{2,1,0:T(8,128)S(1)} %get-tuple-element.60), channel_id=1, source_target_pairs={{0,1},{1,0},{2,3},{3,2},{4,5},{5,4},{6,7},{7,6},{8,9},{9,8},{10,11... | collective-permute-start | bytes 172040 | tf_op jit(solution)/shard_map/ppermute | solution.py:454
  38.0 5.2 %collective-permute-start.12 = (f32[7,16,128]{2,1,0:T(8,128)S(1)}, f32[7,16,128]{2,1,0:T(8,128)S(1)}, u32[]{:S(2)}, u32[]{:S(2)}) collective-permute-start(f32[7,16,128]{2,1,0:T(8,128)S(1)} %get-tuple-element.60), channel_id=1, source_target_pairs={{0,5},{1,4},{2,7},{3,6},{4,1},{5,0},{6,3},{7,2},{8,13},{9,12},{10,... | collective-permute-start | bytes 172040 | tf_op jit(solution)/shard_map/ppermute | solution.py:586
  38.2 5.0 %collective-permute-start.11 = (f32[7,16,128]{2,1,0:T(8,128)S(1)}, f32[7,16,128]{2,1,0:T(8,128)S(1)}, u32[]{:S(2)}, u32[]{:S(2)}) collective-permute-start(f32[7,16,128]{2,1,0:T(8,128)S(1)} %get-tuple-element.55.after.refs_1_), channel_id=1, source_target_pairs={{0,4},{2,6},{4,0},{6,2},{8,12},{10,14},{12,8},{14,10},{16,20},{18,... | collective-permute-start | bytes 172040 | tf_op jit(solution)/shard_map/ppermute | solution.py:580
  43.2 10.8 %collective-permute-start.13 = (bf16[24,4,16,128]{3,2,1,0:T(8,128)(2,1)S(1)}, bf16[24,4,16,128]{3,2,1,0:T(8,128)(2,1)S(1)}, u32[]{:S(2)}, u32[]{:S(2)}) collective-permute-start(bf16[24,4,16,128]{3,2,1,0:T(8,128)(2,1)S(1)} %shard_map.82), channel_id=1, source_target_pairs={{0,1},{1,0},{2,3},{3,2},{4,5},{5,4},{6,7},{7,6},{8,9},{9,8},{10,11... | collective-permute-start | bytes 1179656 | tf_op jit(solution)/shard_map/ppermute | solution.py:454
  44.5 4.2 %collective-permute-start.14 = (f32[7,16,128]{2,1,0:T(8,128)S(1)}, f32[7,16,128]{2,1,0:T(8,128)S(1)}, u32[]{:S(2)}, u32[]{:S(2)}) collective-permute-start(f32[7,16,128]{2,1,0:T(8,128)S(1)} %shard_map.81.refs_1_.refs_0_), channel_id=1, source_target_pairs={{0,8},{2,10},{4,12},{6,14},{8,0},{10,2},{12,4},{14,6},{16,24},{18,... | collective-permute-start | bytes 172040 | tf_op jit(solution)/shard_map/ppermute | solution.py:580
  48.7 5.3 %collective-permute-start.15 = (f32[7,16,128]{2,1,0:T(8,128)S(1)}, f32[7,16,128]{2,1,0:T(8,128)S(1)}, u32[]{:S(2)}, u32[]{:S(2)}) collective-permute-start(f32[7,16,128]{2,1,0:T(8,128)S(1)} %shard_map.84.refs_0_), channel_id=1, source_target_pairs={{0,16},{2,18},{4,20},{6,22},{8,24},{10,26},{12,28},{14,30},{16,0},... | collective-permute-start | bytes 172040 | tf_op jit(solution)/shard_map/ppermute | solution.py:580
  54.0 2.0 %collective-permute-start.16 = (f32[7,16,128]{2,1,0:T(8,128)S(1)}, f32[7,16,128]{2,1,0:T(8,128)S(1)}, u32[]{:S(2)}, u32[]{:S(2)}) collective-permute-start(f32[7,16,128]{2,1,0:T(8,128)S(1)} %shard_map.85.mine), channel_id=1, source_target_pairs={{0,2},{2,0},{4,6},{6,4},{8,10},{10,8},{12,14},{14,12},{16,18},{18,... | collective-permute-start | bytes 172040 | tf_op jit(solution)/shard_map/ppermute | solution.py:580

commit v21 on v19

--- a/solution.py
+++ b/solution.py
@@ -13,14 +13,16 @@
 LIMIT = 16 * 1024 * 1024
 
 
-def call(kernel, outs, args, scratch=(), flops=0, moved=0, loose=0, same=None):
+def call(kernel, outs, args, scratch=(), flops=0, moved=0, loose=0, same=None, left=()):
     whole = pl.BlockSpec(memory_space=pltpu.VMEM)
     still = pl.BlockSpec(memory_space=pl.ANY)
     return pl.pallas_call(
         kernel,
         out_shape=outs,
         in_specs=[still] * loose + [whole] * (len(args) - loose),
-        out_specs=[still if k in (same or {}).values() else whole for k in range(len(outs))],
+        out_specs=[
+            still if k in left or k in (same or {}).values() else whole for k in range(len(outs))
+        ],
         input_output_aliases=same or {},
         scratch_shapes=list(scratch),
         compiler_params=pltpu.CompilerParams(vmem_limit_bytes=LIMIT),
@@ -413,7 +415,7 @@
 
 
 def merge_kernel(extent, *refs):
-    pieces, token, out, wide = refs[:-3], refs[-3], refs[-2], refs[-1]
+    pieces, (token, out, wide, held, done) = refs[:-5], refs[-5:]
     token[...] = jnp.zeros_like(token)
     size, planes, rows = out.shape[:3]
     share = rows // extent
@@ -432,12 +434,18 @@
 
         in_blocks(share, widen)
 
-    def back(i):
-        for x in range(planes):
-            tile = wide[pl.ds(x * size + i, rows, stride=planes * size), :]
-            out[i, x] = tile.astype(BF16)
-
-    in_blocks(size, back)
+    cuts = done.shape[0]
+    copies = []
+    for c in range(cuts):
+        part = pl.ds(c * size // cuts, size // cuts)
+        for i in range(c * size // cuts, (c + 1) * size // cuts):
+            for x in range(planes):
+                tile = wide[pl.ds(x * size + i, rows, stride=planes * size), :]
+                held[i, x] = tile.astype(BF16)
+        copies.append(pltpu.make_async_copy(held.at[part], out.at[part], done.at[c]))
+        copies[-1].start()
+    for copy in copies:
+        copy.wait()
 
 
 def body(field, out_grad, first_weight, second_weight):
@@ -638,8 +646,13 @@
         functools.partial(merge_kernel, extent),
         [jax.ShapeDtypeStruct((8, 128), F32), jax.ShapeDtypeStruct(field.shape, BF16)],
         pieces,
-        [pltpu.VMEM((rows * planes * size, depth), F32)],
+        [
+            pltpu.VMEM((rows * planes * size, depth), F32),
+            pltpu.VMEM(field.shape, BF16),
+            pltpu.SemaphoreType.DMA((4 if size % 4 == 0 else 1,)),
+        ],
         moved=4 * field.size,
+        left=(1,),
     )
     first_grad, second_grad = call(
         functools.partial(finish_kernel, factor),

time: 57.1 us -> 56.9 us (level)
  no operation moved by 1% of the time
where the time goes in v21:
time: 56.9 us; the launch traced here: 56.8 us
  starting transfers between devices  24 us (42%)
  Pallas kernels  19.6 us (34%)
  waiting for transfers between devices  11.2 us (20%)
  local copies, waits for them, and re-layouts  1.14 us (2%)
  between operations  0.83 us (1%)
    pallas_call x20, Pallas kernels, call(): pl.pallas_call(kernel, out_shape=outs, in_specs=[still] * loose + [whole]...  19.6 us
    ppermute x3, starting transfers between devices, to_prev(): lax.ppermute(value, 'slab', [((i + 1) % slabs, i) for i in range(slabs)])  9.06 us
    ppermute x5, starting transfers between devices, to_chan(): lax.ppermute(value, 'chan', [(i, (i + shift) % extent) for i in range(ext...  7.92 us
    ppermute x5, starting transfers between devices, stepped(): return lax.ppermute(value, 'slab', [(i, i ^ stride) for i in range(slabs)])  6.63 us
    ppermute x5, waiting for transfers between devices, stepped(): return lax.ppermute(value, 'slab', [(i, i ^ stride) for i in range(slabs)])  6.31 us
    ppermute x5, waiting for transfers between devices, to_chan(): lax.ppermute(value, 'chan', [(i, (i + shift) % extent) for i in range(ext...  4.89 us
  transfers between devices with their start and end apart: 17, of which 6 were waited for; matrix products, arithmetic and copies ran while one was open for 0% of the time, Pallas kernels for 32%

profile of v21, /device:TPU:0, one launch (start us, length us, event | category | flops | bytes accessed | tf_op | source)
XLA Modules:
  0.0 56.8 jit_solution(7712056466226785668)
XLA Ops:
  0.6 0.0 copy-start
  0.6 1.1 %copy-done = bf16[16,4,48,128]{3,2,1,0:T(8,128)(2,1)S(1)} copy-done((bf16[16,4,48,128]{3,2,1,0:T(8,128)(2,1)S(1)}, bf16[16,4,48,128]{3,2,1,0:T(8,128)(2,1)}, u32[]{:S(2)}) %copy-start) | copy-done | bytes 786456
  1.8 0.0 copy-start.2
  1.8 0.0 copy-start.3
  1.8 0.0 copy-start.1
  1.8 0.7 %shard_map.67 = (bf16[32,2,16,128]{3,2,1,0:T(8,128)(2,1)S(1)}, bf16[32,2,16,128]{3,2,1,0:T(8,128)(2,1)S(1)}) custom-call(bf16[16,4,48,128]{3,2,1,0:T(8,128)(2,1)S(1)} %copy-done, bf16[16,4,48,128]{3,2,1,0:T(8,128)(2,1)S(1)} %copy-done), custom_call_target="tpu_custom_call" | custom-call | bytes 1179648 | tf_op jit(solution)/shard_map/pallas_call | solution.py:19
  2.5 3.0 %collective-permute-start.1 = (bf16[32,2,16,128]{3,2,1,0:T(8,128)(2,1)S(1)}, bf16[32,2,16,128]{3,2,1,0:T(8,128)(2,1)S(1)}, u32[]{:S(2)}, u32[]{:S(2)}) collective-permute-start(bf16[32,2,16,128]{3,2,1,0:T(8,128)(2,1)S(1)} %get-tuple-element.35), channel_id=1, source_target_pairs={{0,1},{1,0},{2,3},{3,2},{4,5},{5,4},{6,7},{7,6},{8,9},{9,8},{10,11... | collective-permute-start | bytes 786440 | tf_op jit(solution)/shard_map/ppermute | solution.py:462
  5.5 0.7 %shard_map.68 = (bf16[32,2,16,128]{3,2,1,0:T(8,128)(2,1)S(1)}, bf16[32,2,16,128]{3,2,1,0:T(8,128)(2,1)S(1)}) custom-call(bf16[32,2,16,128]{3,2,1,0:T(8,128)(2,1)S(1)} %get-tuple-element.34.after.refs_4_.refs_0_.refs_15_, bf16[16,4,48,128]{3,2,1,0:T(8,128)(2,1)S(1)} %copy-done), custom_call_target="tpu_custom_call" | custom-call | bytes 1179648 | tf_op jit(solution)/shard_map/pallas_call | solution.py:19
  6.2 0.1 collective-permute-start.3
  6.3 4.0 %collective-permute-start.5 = (bf16[32,2,16,128]{3,2,1,0:T(8,128)(2,1)S(1)}, bf16[32,2,16,128]{3,2,1,0:T(8,128)(2,1)S(1)}, u32[]{:S(2)}, u32[]{:S(2)}) collective-permute-start(bf16[32,2,16,128]{3,2,1,0:T(8,128)(2,1)S(1)} %get-tuple-element.36.after.refs_2_.refs_13_), channel_id=1, source_target_pairs={{2,0},{4,2},{6,4},{8,6},{10,8},{12,10},{14,12},{16,14},{18,16},{20... | collective-permute-start | bytes 786440 | tf_op jit(solution)/shard_map/ppermute | solution.py:468
  10.2 0.0 collective-permute-start
  10.2 0.0 copy-done.2
  10.2 0.0 copy-done.3
  10.2 0.1 shard_map.69.refs_1_.after.refs_0_
  10.4 2.3 %collective-permute-done.1.refs_0_ = bf16[32,2,16,128]{3,2,1,0:T(8,128)(2,1)S(1)} collective-permute-done((bf16[32,2,16,128]{3,2,1,0:T(8,128)(2,1)S(1)}, bf16[32,2,16,128]{3,2,1,0:T(8,128)(2,1)S(1)}, u32[]{:S(2)}, u32[]{:S(2)}) %collective-permute-start.1) | collective-permute-done | bytes 262176 | tf_op jit(solution)/shard_map/ppermute | solution.py:462
  12.6 0.0 collective-permute-start.2
  12.6 2.1 %collective-permute-start.4 = (bf16[14,16,128]{2,1,0:T(8,128)(2,1)S(1)}, bf16[14,16,128]{2,1,0:T(8,128)(2,1)S(1)}, u32[]{:S(2)}, u32[]{:S(2)}) collective-permute-start(bf16[14,16,128]{2,1,0:T(8,128)(2,1)S(1)} %shard_map.69.refs_1_.after.refs_0_), channel_id=1, source_target_pairs={{0,1},{1,0},{2,3},{3,2},{4,5},{5,4},{6,7},{7,6},{8,9},{9,8},{10,11... | collective-permute-start | bytes 172040 | tf_op jit(solution)/shard_map/ppermute | solution.py:462
  14.7 0.0 copy-done.1
  14.7 1.2 %shard_map.71 = (bf16[28,2,32,128]{3,2,1,0:T(8,128)(2,1)S(1)}, bf16[28,2,32,128]{3,2,1,0:T(8,128)(2,1)S(1)}) custom-call(bf16[14,16,128]{2,1,0:T(8,128)(2,1)S(1)} %shard_map.69.refs_1_.after.refs_0_, bf16[32,4,48,128]{3,2,1,0:T(8,128)(2,1)S(1)} %copy-done.1), custom_call_target="tpu_custom_call" | custom-call | bytes 3145728 | tf_op jit(solution)/shard_map/pallas_call | solution.py:19
  15.9 2.6 %collective-permute-done.4.refs_2_.refs_1_ = bf16[14,16,128]{2,1,0:T(8,128)(2,1)S(1)} collective-permute-done((bf16[14,16,128]{2,1,0:T(8,128)(2,1)S(1)}, bf16[14,16,128]{2,1,0:T(8,128)(2,1)S(1)}, u32[]{:S(2)}, u32[]{:S(2)}) %collective-permute-start.4) | collective-permute-done | bytes 57376 | tf_op jit(solution)/shard_map/ppermute | solution.py:462
  18.6 0.0 collective-permute-done.3.refs_0_
  18.6 0.0 collective-permute-done.5.refs_1_.refs_2_.refs_17_
  18.6 3.5 %collective-permute-start.6 = (bf16[32,2,16,128]{3,2,1,0:T(8,128)(2,1)S(1)}, bf16[32,2,16,128]{3,2,1,0:T(8,128)(2,1)S(1)}, u32[]{:S(2)}, u32[]{:S(2)}) collective-permute-start(bf16[32,2,16,128]{3,2,1,0:T(8,128)(2,1)S(1)} %shard_map.73.refs_3_.refs_14_), channel_id=1, source_target_pairs={{2,0},{4,2},{6,4},{8,6},{10,8},{12,10},{14,12},{16,14},{18,16},{20... | collective-permute-start | bytes 786440 | tf_op jit(solution)/shard_map/ppermute | solution.py:468
  22.1 0.6 %shard_map.74 = (bf16[192,384]{1,0:T(8,128)(2,1)S(1)}, bf16[192,384]{1,0:T(8,128)(2,1)S(1)}, bf16[192,384]{1,0:T(8,128)(2,1)S(1)}, bf16[192,384]{1,0:T(8,128)(2,...) custom-call(bf16[14,16,128]{2,1,0:T(8,128)(2,1)S(1)} %shard_map.69.refs_1_.after.refs_0_, ...), custom_call_target="tpu_custom_call" | custom-call | bytes 589824 | tf_op jit(solution)/shard_map/pallas_call | solution.py:19
  22.7 0.0 collective-permute-done.refs_0_.refs_11_
  22.7 0.0 collective-permute-done.2.refs_1_.refs_12_
  22.7 2.6 %shard_map.75 = (bf16[30,2,32,128]{3,2,1,0:T(8,128)(2,1)S(1)}, bf16[30,2,32,128]{3,2,1,0:T(8,128)(2,1)S(1)}, bf16[30,2,32,128]{3,2,1,0:T(8,128)(2,1)S(1)}, bf16[...) custom-call(bf16[32,2,16,128]{3,2,1,0:T(8,128)(2,1)S(1)} %collective-permute-done.refs_0_.refs_11_, ...), custom_call_target="tpu_custom_call" | custom-call | flops 1019215872 | bytes 3145728 | tf_op jit(solution)/shard_map/pallas_call | solution.py:19
  25.3 1.6 %collective-permute-start.7 = (bf16[28,2,32,128]{3,2,1,0:T(8,128)(2,1)S(1)}, bf16[28,2,32,128]{3,2,1,0:T(8,128)(2,1)S(1)}, u32[]{:S(2)}, u32[]{:S(2)}) collective-permute-start(bf16[28,2,32,128]{3,2,1,0:T(8,128)(2,1)S(1)} %get-tuple-element.45.refs_3_), channel_id=1, source_target_pairs={{2,0},{4,2},{6,4},{8,6},{10,8},{12,10},{14,12},{16,14},{18,16},{20... | collective-permute-start | bytes 1376264 | tf_op jit(solution)/shard_map/ppermute | solution.py:468
  26.9 0.0 collective-permute-done.6.refs_3_.refs_18_
  26.9 1.8 %shard_map.76 = (bf16[30,2,32,128]{3,2,1,0:T(8,128)(2,1)S(1)}, bf16[30,2,32,128]{3,2,1,0:T(8,128)(2,1)S(1)}, bf16[28,2,32,128]{3,2,1,0:T(8,128)(2,1)S(1)}) custom-call(bf16[32,2,16,128]{3,2,1,0:T(8,128)(2,1)S(1)} %get-tuple-element.34.after.refs_4_.refs_0_.refs_15_, bf16[32,2,16,128]{3,2,1,0:T(8,128)(2,1)S(1)} %shard_map.70.refs_5_.refs_1_.refs_16_, ...), custom_call_target="tpu_custom_call" | custom-call | flops 679477248 | bytes 2359296 | tf_op jit(solution)/shard_map/pallas_call | solution.py:19
  28.7 0.2 collective-permute-start.9
  28.9 6.1 %shard_map.77 = (f32[2,7,16,128]{3,2,1,0:T(8,128)S(1)}, f32[2,7,16,128]{3,2,1,0:T(8,128)S(1)}, bf16[26,2,32,128]{3,2,1,0:T(8,128)(2,1)S(1)}) custom-call(bf16[30,2,32,128]{3,2,1,0:T(8,128)(2,1)S(1)} %get-tuple-element.41.refs_0_, bf16[30,2,32,128]{3,2,1,0:T(8,128)(2,1)S(1)} %get-tuple-element.42.refs_4_.refs_1_, ...), custom_call_target="tpu_custom_call" | custom-call | tf_op jit(solution)/shard_map/pallas_call | solution.py:19
  35.0 0.1 collective-permute-start.8
  35.1 0.0 collective-permute-done.7.below
  35.1 0.9 %shard_map.78.after.refs_6_ = bf16[26,2,32,128]{3,2,1,0:T(8,128)(2,1)S(1)} custom-call(f32[2,7,16,128]{3,2,1,0:T(8,128)S(1)} %get-tuple-element.53.after.one, bf16[192,384]{1,0:T(8,128)(2,1)S(1)} %get-tuple-element.47.refs_5_.weight.refs_0_, bf16[28,2,32,128]{3,2,1,0:T(8,128)(2,1)S(1)} %get-tuple-element.46.refs_4_.above, ...), custom_call_target="tpu_custom_call" | custom-call | flops 339738624 | bytes 786432 | tf_op jit(solution)/shard_map/pallas_call | solution.py:19
  36.0 0.4 collective-permute-done.8.two
  36.5 1.6 %collective-permute-start.10 = (f32[7,16,128]{2,1,0:T(8,128)S(1)}, f32[7,16,128]{2,1,0:T(8,128)S(1)}, u32[]{:S(2)}, u32[]{:S(2)}) collective-permute-start(f32[7,16,128]{2,1,0:T(8,128)S(1)} %get-tuple-element.60), channel_id=1, source_target_pairs={{0,1},{1,0},{2,3},{3,2},{4,5},{5,4},{6,7},{7,6},{8,9},{9,8},{10,11... | collective-permute-start | bytes 172040 | tf_op jit(solution)/shard_map/ppermute | solution.py:462
  38.0 0.2 collective-permute-start.12
  38.2 1.8 %collective-permute-start.11 = (f32[7,16,128]{2,1,0:T(8,128)S(1)}, f32[7,16,128]{2,1,0:T(8,128)S(1)}, u32[]{:S(2)}, u32[]{:S(2)}) collective-permute-start(f32[7,16,128]{2,1,0:T(8,128)S(1)} %get-tuple-element.55.after.refs_1_), channel_id=1, source_target_pairs={{0,4},{2,6},{4,0},{6,2},{8,12},{10,14},{12,8},{14,10},{16,20},{18,... | collective-permute-start | bytes 172040 | tf_op jit(solution)/shard_map/ppermute | solution.py:588
  40.0 0.0 collective-permute-done.9.refs_2_
  40.0 2.1 %shard_map.80 = (bf16[24,4,16,128]{3,2,1,0:T(8,128)(2,1)S(1)}, bf16[24,4,16,128]{3,2,1,0:T(8,128)(2,1)S(1)}) custom-call(f32[7,16,128]{2,1,0:T(8,128)S(1)} %get-tuple-element.55.after.refs_1_, bf16[192,384]{1,0:T(8,128)(2,1)S(1)} %get-tuple-element.47.refs_5_.weight.refs_0_, bf16[192,384]{1,0:T(8,128)(2,1)S(1)} %get-tuple-element.56.refs_1_, ...), custom_call_target="tpu_custom_call" | custom-call | flops 1358954496 | bytes 2359296 | tf_op jit(solution)/shard_map/pallas_call | solution.py:19
  42.2 0.0 collective-permute-done.10.refs_2_
  42.2 1.0 %collective-permute-done.11.refs_3_ = f32[7,16,128]{2,1,0:T(8,128)S(1)} collective-permute-done((f32[7,16,128]{2,1,0:T(8,128)S(1)}, f32[7,16,128]{2,1,0:T(8,128)S(1)}, u32[]{:S(2)}, u32[]{:S(2)}) %collective-permute-start.11) | collective-permute-done | bytes 57376 | tf_op jit(solution)/shard_map/ppermute | solution.py:588
  43.2 0.0 collective-permute-done.12.refs_4_
  43.2 1.2 %collective-permute-start.13 = (bf16[24,4,16,128]{3,2,1,0:T(8,128)(2,1)S(1)}, bf16[24,4,16,128]{3,2,1,0:T(8,128)(2,1)S(1)}, u32[]{:S(2)}, u32[]{:S(2)}) collective-permute-start(bf16[24,4,16,128]{3,2,1,0:T(8,128)(2,1)S(1)} %shard_map.82), channel_id=1, source_target_pairs={{0,1},{1,0},{2,3},{3,2},{4,5},{5,4},{6,7},{7,6},{8,9},{9,8},{10,11... | collective-permute-start | bytes 1179656 | tf_op jit(solution)/shard_map/ppermute | solution.py:462
  44.5 1.5 %collective-permute-start.14 = (f32[7,16,128]{2,1,0:T(8,128)S(1)}, f32[7,16,128]{2,1,0:T(8,128)S(1)}, u32[]{:S(2)}, u32[]{:S(2)}) collective-permute-start(f32[7,16,128]{2,1,0:T(8,128)S(1)} %shard_map.81.refs_1_.refs_0_), channel_id=1, source_target_pairs={{0,8},{2,10},{4,12},{6,14},{8,0},{10,2},{12,4},{14,6},{16,24},{18,... | collective-permute-start | bytes 172040 | tf_op jit(solution)/shard_map/ppermute | solution.py:588
  45.9 2.7 %collective-permute-done.14.refs_1_ = f32[7,16,128]{2,1,0:T(8,128)S(1)} collective-permute-done((f32[7,16,128]{2,1,0:T(8,128)S(1)}, f32[7,16,128]{2,1,0:T(8,128)S(1)}, u32[]{:S(2)}, u32[]{:S(2)}) %collective-permute-start.14) | collective-permute-done | bytes 57376 | tf_op jit(solution)/shard_map/ppermute | solution.py:588
  48.7 3.2 %collective-permute-start.15 = (f32[7,16,128]{2,1,0:T(8,128)S(1)}, f32[7,16,128]{2,1,0:T(8,128)S(1)}, u32[]{:S(2)}, u32[]{:S(2)}) collective-permute-start(f32[7,16,128]{2,1,0:T(8,128)S(1)} %shard_map.84.refs_0_), channel_id=1, source_target_pairs={{0,16},{2,18},{4,20},{6,22},{8,24},{10,26},{12,28},{14,30},{16,0},... | collective-permute-start | bytes 172040 | tf_op jit(solution)/shard_map/ppermute | solution.py:588
  51.8 2.2 %collective-permute-done.15.refs_1_ = f32[7,16,128]{2,1,0:T(8,128)S(1)} collective-permute-done((f32[7,16,128]{2,1,0:T(8,128)S(1)}, f32[7,16,128]{2,1,0:T(8,128)S(1)}, u32[]{:S(2)}, u32[]{:S(2)}) %collective-permute-start.15) | collective-permute-done | bytes 57376 | tf_op jit(solution)/shard_map/ppermute | solution.py:588
  54.0 0.1 collective-permute-start.16
  54.1 0.0 collective-permute-done.13.refs_1_
  54.1 1.7 %shard_map.83 = (f32[8,128]{1,0:T(8,128)S(1)}, bf16[16,4,48,128]{3,2,1,0:T(8,128)(2,1)}) custom-call(bf16[24,4,16,128]{3,2,1,0:T(8,128)(2,1)S(1)} %get-tuple-element.58.refs_0_, bf16[24,4,16,128]{3,2,1,0:T(8,128)(2,1)S(1)} %collective-permute-done.13.refs_1_), custom_call_target="tpu_custom_call" | custom-call | bytes 1572864 | tf_op jit(solution)/shard_map/pallas_call | solution.py:19
  55.8 0.0 collective-permute-done.16.other
  55.8 0.9 %shard_map.86 = (f32[27,16,32]{2,1,0:T(8,128)}, f32[27,16,32]{2,1,0:T(8,128)}) custom-call(f32[8,128]{1,0:T(8,128)S(1)} %get-tuple-element.62.after, f32[7,16,128]{2,1,0:T(8,128)S(1)} %shard_map.85.mine, f32[7,16,128]{2,1,0:T(8,128)S(1)} %collective-permute-done.16.other), custom_call_target="tpu_custom_call" | custom-call | tf_op jit(solution)/shard_map/pallas_call | solution.py:19
  (8 shorter events, 0.0 us)
Async XLA Ops:
  0.6 1.1 %copy-start = (bf16[16,4,48,128]{3,2,1,0:T(8,128)(2,1)S(1)}, bf16[16,4,48,128]{3,2,1,0:T(8,128)(2,1)}, u32[]{:S(2)}) copy-start(bf16[16,4,48,128]{3,2,1,0:T(8,128)(2,1)} %x_ref.4) | copy-start | bytes 2359300
  1.8 8.5 %copy-start.2 = (bf16[16,27,32]{2,0,1:T(8,128)(2,1)S(1)}, bf16[16,27,32]{2,0,1:T(8,128)(2,1)}, u32[]{:S(2)}) copy-start(bf16[16,27,32]{2,0,1:T(8,128)(2,1)} %param.6) | copy-start | bytes 82948
  1.8 8.5 %copy-start.3 = (bf16[16,27,32]{2,0,1:T(8,128)(2,1)S(1)}, bf16[16,27,32]{2,0,1:T(8,128)(2,1)}, u32[]{:S(2)}) copy-start(bf16[16,27,32]{2,0,1:T(8,128)(2,1)} %param.7) | copy-start | bytes 82948
  1.8 12.9 %copy-start.1 = (bf16[32,4,48,128]{3,2,1,0:T(8,128)(2,1)S(1)}, bf16[32,4,48,128]{3,2,1,0:T(8,128)(2,1)}, u32[]{:S(2)}) copy-start(bf16[32,4,48,128]{3,2,1,0:T(8,128)(2,1)} %x_ref.5) | copy-start | bytes 4718596
  2.5 10.1 %collective-permute-start.1 = (bf16[32,2,16,128]{3,2,1,0:T(8,128)(2,1)S(1)}, bf16[32,2,16,128]{3,2,1,0:T(8,128)(2,1)S(1)}, u32[]{:S(2)}, u32[]{:S(2)}) collective-permute-start(bf16[32,2,16,128]{3,2,1,0:T(8,128)(2,1)S(1)} %get-tuple-element.35), channel_id=1, source_target_pairs={{0,1},{1,0},{2,3},{3,2},{4,5},{5,4},{6,7},{7,6},{8,9},{9,8},{10,11... | collective-permute-start | bytes 786440 | tf_op jit(solution)/shard_map/ppermute | solution.py:462
  6.2 12.4 %collective-permute-start.3 = (bf16[32,2,16,128]{3,2,1,0:T(8,128)(2,1)S(1)}, bf16[32,2,16,128]{3,2,1,0:T(8,128)(2,1)S(1)}, u32[]{:S(2)}, u32[]{:S(2)}) collective-permute-start(bf16[32,2,16,128]{3,2,1,0:T(8,128)(2,1)S(1)} %get-tuple-element.37), channel_id=1, source_target_pairs={{0,1},{1,0},{2,3},{3,2},{4,5},{5,4},{6,7},{7,6},{8,9},{9,8},{10,11... | collective-permute-start | bytes 786440 | tf_op jit(solution)/shard_map/ppermute | solution.py:462
  6.3 12.3 %collective-permute-start.5 = (bf16[32,2,16,128]{3,2,1,0:T(8,128)(2,1)S(1)}, bf16[32,2,16,128]{3,2,1,0:T(8,128)(2,1)S(1)}, u32[]{:S(2)}, u32[]{:S(2)}) collective-permute-start(bf16[32,2,16,128]{3,2,1,0:T(8,128)(2,1)S(1)} %get-tuple-element.36.after.refs_2_.refs_13_), channel_id=1, source_target_pairs={{2,0},{4,2},{6,4},{8,6},{10,8},{12,10},{14,12},{16,14},{18,16},{20... | collective-permute-start | bytes 786440 | tf_op jit(solution)/shard_map/ppermute | solution.py:468
  10.2 12.5 %collective-permute-start = (bf16[32,2,16,128]{3,2,1,0:T(8,128)(2,1)S(1)}, bf16[32,2,16,128]{3,2,1,0:T(8,128)(2,1)S(1)}, u32[]{:S(2)}, u32[]{:S(2)}) collective-permute-start(bf16[32,2,16,128]{3,2,1,0:T(8,128)(2,1)S(1)} %get-tuple-element.34.after.refs_4_.refs_0_.refs_15_), channel_id=1, source_target_pairs={{0,2},{2,4},{4,6},{6,8},{8,10},{10,12},{12,14},{14,16},{16,18},{18... | collective-permute-start | bytes 786440 | tf_op jit(solution)/shard_map/ppermute | solution.py:465
  12.6 10.1 %collective-permute-start.2 = (bf16[32,2,16,128]{3,2,1,0:T(8,128)(2,1)S(1)}, bf16[32,2,16,128]{3,2,1,0:T(8,128)(2,1)S(1)}, u32[]{:S(2)}, u32[]{:S(2)}) collective-permute-start(bf16[32,2,16,128]{3,2,1,0:T(8,128)(2,1)S(1)} %shard_map.70.refs_5_.refs_1_.refs_16_), channel_id=1, source_target_pairs={{0,2},{2,4},{4,6},{6,8},{8,10},{10,12},{12,14},{14,16},{16,18},{18... | collective-permute-start | bytes 786440 | tf_op jit(solution)/shard_map/ppermute | solution.py:465
  12.6 5.9 %collective-permute-start.4 = (bf16[14,16,128]{2,1,0:T(8,128)(2,1)S(1)}, bf16[14,16,128]{2,1,0:T(8,128)(2,1)S(1)}, u32[]{:S(2)}, u32[]{:S(2)}) collective-permute-start(bf16[14,16,128]{2,1,0:T(8,128)(2,1)S(1)} %shard_map.69.refs_1_.after.refs_0_), channel_id=1, source_target_pairs={{0,1},{1,0},{2,3},{3,2},{4,5},{5,4},{6,7},{7,6},{8,9},{9,8},{10,11... | collective-permute-start | bytes 172040 | tf_op jit(solution)/shard_map/ppermute | solution.py:462
  18.6 8.3 %collective-permute-start.6 = (bf16[32,2,16,128]{3,2,1,0:T(8,128)(2,1)S(1)}, bf16[32,2,16,128]{3,2,1,0:T(8,128)(2,1)S(1)}, u32[]{:S(2)}, u32[]{:S(2)}) collective-permute-start(bf16[32,2,16,128]{3,2,1,0:T(8,128)(2,1)S(1)} %shard_map.73.refs_3_.refs_14_), channel_id=1, source_target_pairs={{2,0},{4,2},{6,4},{8,6},{10,8},{12,10},{14,12},{16,14},{18,16},{20... | collective-permute-start | bytes 786440 | tf_op jit(solution)/shard_map/ppermute | solution.py:468
  25.3 9.8 %collective-permute-start.7 = (bf16[28,2,32,128]{3,2,1,0:T(8,128)(2,1)S(1)}, bf16[28,2,32,128]{3,2,1,0:T(8,128)(2,1)S(1)}, u32[]{:S(2)}, u32[]{:S(2)}) collective-permute-start(bf16[28,2,32,128]{3,2,1,0:T(8,128)(2,1)S(1)} %get-tuple-element.45.refs_3_), channel_id=1, source_target_pairs={{2,0},{4,2},{6,4},{8,6},{10,8},{12,10},{14,12},{16,14},{18,16},{20... | collective-permute-start | bytes 1376264 | tf_op jit(solution)/shard_map/ppermute | solution.py:468
  28.7 11.3 %collective-permute-start.9 = (bf16[28,2,32,128]{3,2,1,0:T(8,128)(2,1)S(1)}, bf16[28,2,32,128]{3,2,1,0:T(8,128)(2,1)S(1)}, u32[]{:S(2)}, u32[]{:S(2)}) collective-permute-start(bf16[28,2,32,128]{3,2,1,0:T(8,128)(2,1)S(1)} %get-tuple-element.46.refs_4_.above), channel_id=1, source_target_pairs={{0,2},{2,4},{4,6},{6,8},{8,10},{10,12},{12,14},{14,16},{16,18},{18... | collective-permute-start | bytes 1376264 | tf_op jit(solution)/shard_map/ppermute | solution.py:465
  35.0 1.4 %collective-permute-start.8 = (f32[2,7,16,128]{3,2,1,0:T(8,128)S(1)}, f32[2,7,16,128]{3,2,1,0:T(8,128)S(1)}, u32[]{:S(2)}, u32[]{:S(2)}) collective-permute-start(f32[2,7,16,128]{3,2,1,0:T(8,128)S(1)} %get-tuple-element.54), channel_id=1, source_target_pairs={{0,2},{2,0},{4,6},{6,4},{8,10},{10,8},{12,14},{14,12},{16,18},{18,... | collective-permute-start | bytes 344072 | tf_op jit(solution)/shard_map/ppermute | solution.py:588
  36.5 5.7 %collective-permute-start.10 = (f32[7,16,128]{2,1,0:T(8,128)S(1)}, f32[7,16,128]{2,1,0:T(8,128)S(1)}, u32[]{:S(2)}, u32[]{:S(2)}) collective-permute-start(f32[7,16,128]{2,1,0:T(8,128)S(1)} %get-tuple-element.60), channel_id=1, source_target_pairs={{0,1},{1,0},{2,3},{3,2},{4,5},{5,4},{6,7},{7,6},{8,9},{9,8},{10,11... | collective-permute-start | bytes 172040 | tf_op jit(solution)/shard_map/ppermute | solution.py:462
  38.0 5.2 %collective-permute-start.12 = (f32[7,16,128]{2,1,0:T(8,128)S(1)}, f32[7,16,128]{2,1,0:T(8,128)S(1)}, u32[]{:S(2)}, u32[]{:S(2)}) collective-permute-start(f32[7,16,128]{2,1,0:T(8,128)S(1)} %get-tuple-element.60), channel_id=1, source_target_pairs={{0,5},{1,4},{2,7},{3,6},{4,1},{5,0},{6,3},{7,2},{8,13},{9,12},{10,... | collective-permute-start | bytes 172040 | tf_op jit(solution)/shard_map/ppermute | solution.py:594
  38.2 5.0 %collective-permute-start.11 = (f32[7,16,128]{2,1,0:T(8,128)S(1)}, f32[7,16,128]{2,1,0:T(8,128)S(1)}, u32[]{:S(2)}, u32[]{:S(2)}) collective-permute-start(f32[7,16,128]{2,1,0:T(8,128)S(1)} %get-tuple-element.55.after.refs_1_), channel_id=1, source_target_pairs={{0,4},{2,6},{4,0},{6,2},{8,12},{10,14},{12,8},{14,10},{16,20},{18,... | collective-permute-start | bytes 172040 | tf_op jit(solution)/shard_map/ppermute | solution.py:588
  43.2 10.8 %collective-permute-start.13 = (bf16[24,4,16,128]{3,2,1,0:T(8,128)(2,1)S(1)}, bf16[24,4,16,128]{3,2,1,0:T(8,128)(2,1)S(1)}, u32[]{:S(2)}, u32[]{:S(2)}) collective-permute-start(bf16[24,4,16,128]{3,2,1,0:T(8,128)(2,1)S(1)} %shard_map.82), channel_id=1, source_target_pairs={{0,1},{1,0},{2,3},{3,2},{4,5},{5,4},{6,7},{7,6},{8,9},{9,8},{10,11... | collective-permute-start | bytes 1179656 | tf_op jit(solution)/shard_map/ppermute | solution.py:462
  44.5 4.2 %collective-permute-start.14 = (f32[7,16,128]{2,1,0:T(8,128)S(1)}, f32[7,16,128]{2,1,0:T(8,128)S(1)}, u32[]{:S(2)}, u32[]{:S(2)}) collective-permute-start(f32[7,16,128]{2,1,0:T(8,128)S(1)} %shard_map.81.refs_1_.refs_0_), channel_id=1, source_target_pairs={{0,8},{2,10},{4,12},{6,14},{8,0},{10,2},{12,4},{14,6},{16,24},{18,... | collective-permute-start | bytes 172040 | tf_op jit(solution)/shard_map/ppermute | solution.py:588
  48.7 5.3 %collective-permute-start.15 = (f32[7,16,128]{2,1,0:T(8,128)S(1)}, f32[7,16,128]{2,1,0:T(8,128)S(1)}, u32[]{:S(2)}, u32[]{:S(2)}) collective-permute-start(f32[7,16,128]{2,1,0:T(8,128)S(1)} %shard_map.84.refs_0_), channel_id=1, source_target_pairs={{0,16},{2,18},{4,20},{6,22},{8,24},{10,26},{12,28},{14,30},{16,0},... | collective-permute-start | bytes 172040 | tf_op jit(solution)/shard_map/ppermute | solution.py:588
  54.0 1.8 %collective-permute-start.16 = (f32[7,16,128]{2,1,0:T(8,128)S(1)}, f32[7,16,128]{2,1,0:T(8,128)S(1)}, u32[]{:S(2)}, u32[]{:S(2)}) collective-permute-start(f32[7,16,128]{2,1,0:T(8,128)S(1)} %shard_map.85.mine), channel_id=1, source_target_pairs={{0,2},{2,0},{4,6},{6,4},{8,10},{10,8},{12,14},{14,12},{16,18},{18,... | collective-permute-start | bytes 172040 | tf_op jit(solution)/shard_map/ppermute | solution.py:588

commit v22 on v21

--- a/solution.py
+++ b/solution.py
@@ -393,30 +393,44 @@
     pass
 
 
-def finish_kernel(factor, after, mine, other, first, second):
-    del after
-    channels = first.shape[2]
-
-    def place(ours, theirs):
-        for result, sums in ((ours, mine), (theirs, other)):
-            for t in range(27):
-                low = t % 4 * channels
-                result[t] = sums[t // 4, :, low : low + channels] * factor
-
+def by_taps(sums, result, factor):
+    channels = result.shape[2]
+    for t in range(27):
+        low = t % 4 * channels
+        result[t] = sums[t // 4, :, low : low + channels] * factor
+
+
+def finish_kernel(factor, first_in, second_in, other, first, second, held, done):
+    del first_in, second_in
+    by_taps(other, held, factor)
     odd = lax.rem(lax.axis_index("slab"), 2)
 
     @pl.when(odd == 0)
     def _():
-        place(first, second)
+        copy = pltpu.make_async_copy(held, second, done.at[0])
+        copy.start()
+        copy.wait()
 
     @pl.when(odd == 1)
     def _():
-        place(second, first)
-
-
-def merge_kernel(extent, *refs):
-    pieces, (token, out, wide, held, done) = refs[:-5], refs[-5:]
-    token[...] = jnp.zeros_like(token)
+        copy = pltpu.make_async_copy(held, first, done.at[0])
+        copy.start()
+        copy.wait()
+
+
+def merge_kernel(extent, factor, mine, *refs):
+    pieces, (out, first, second, wide, held, own, done, own_done) = refs[:-8], refs[-8:]
+    by_taps(mine, own, factor)
+    odd = lax.rem(lax.axis_index("slab"), 2)
+
+    @pl.when(odd == 0)
+    def _():
+        pltpu.make_async_copy(own, first, own_done.at[0]).start()
+
+    @pl.when(odd == 1)
+    def _():
+        pltpu.make_async_copy(own, second, own_done.at[0]).start()
+
     size, planes, rows = out.shape[:3]
     share = rows // extent
     me = lax.axis_index("chan")
@@ -446,6 +460,14 @@
         copies[-1].start()
     for copy in copies:
         copy.wait()
+
+    @pl.when(odd == 0)
+    def _():
+        pltpu.make_async_copy(own, first, own_done.at[0]).wait()
+
+    @pl.when(odd == 1)
+    def _():
+        pltpu.make_async_copy(own, second, own_done.at[0]).wait()
 
 
 def body(field, out_grad, first_weight, second_weight):
@@ -642,23 +664,28 @@
         mine, other = jnp.where(even, mine, other), jnp.where(even, other, mine)
         mine, other = lax.psum((mine, other), "slab")
         mine, other = jnp.where(even, mine, other), jnp.where(even, other, mine)
-    token, input_grad = call(
-        functools.partial(merge_kernel, extent),
-        [jax.ShapeDtypeStruct((8, 128), F32), jax.ShapeDtypeStruct(field.shape, BF16)],
-        pieces,
+    result = jax.ShapeDtypeStruct(by_tap, F32)
+    input_grad, first_grad, second_grad = call(
+        functools.partial(merge_kernel, extent, factor),
+        [jax.ShapeDtypeStruct(field.shape, BF16), result, result],
+        [mine] + pieces,
         [
             pltpu.VMEM((rows * planes * size, depth), F32),
             pltpu.VMEM(field.shape, BF16),
+            pltpu.VMEM(by_tap, F32),
             pltpu.SemaphoreType.DMA((4 if size % 4 == 0 else 1,)),
+            pltpu.SemaphoreType.DMA((1,)),
         ],
         moved=4 * field.size,
-        left=(1,),
+        left=(0, 1, 2),
     )
     first_grad, second_grad = call(
         functools.partial(finish_kernel, factor),
-        [jax.ShapeDtypeStruct(by_tap, F32)] * 2,
-        [token, mine, other],
-        loose=1,
+        [result, result],
+        [first_grad, second_grad, other],
+        [pltpu.VMEM(by_tap, F32), pltpu.SemaphoreType.DMA((1,))],
+        loose=2,
+        same={0: 0, 1: 1},
     )
     first_grad, second_grad = (jnp.transpose(g, (1, 0, 2)) for g in (first_grad, second_grad))
     return input_grad, first_grad, second_grad

time: 56.9 us -> 57.1 us (level)
  no operation moved by 1% of the time
where the time goes in v22:
time: 57.1 us; the launch traced here: 56.9 us
  starting transfers between devices  24 us (42%)
  Pallas kernels  19.6 us (34%)
  waiting for transfers between devices  11.2 us (20%)
  local copies, waits for them, and re-layouts  1.14 us (2%)
  between operations  0.99 us (2%)
    pallas_call x20, Pallas kernels, call(): pl.pallas_call(kernel, out_shape=outs, in_specs=[still] * loose + [whole]...  19.6 us
    ppermute x3, starting transfers between devices, to_prev(): lax.ppermute(value, 'slab', [((i + 1) % slabs, i) for i in range(slabs)])  9.06 us
    ppermute x5, starting transfers between devices, to_chan(): lax.ppermute(value, 'chan', [(i, (i + shift) % extent) for i in range(ext...  7.92 us
    ppermute x5, starting transfers between devices, stepped(): return lax.ppermute(value, 'slab', [(i, i ^ stride) for i in range(slabs)])  6.63 us
    ppermute x5, waiting for transfers between devices, stepped(): return lax.ppermute(value, 'slab', [(i, i ^ stride) for i in range(slabs)])  6.31 us
    ppermute x5, waiting for transfers between devices, to_chan(): lax.ppermute(value, 'chan', [(i, (i + shift) % extent) for i in range(ext...  4.89 us
  transfers between devices with their start and end apart: 17, of which 6 were waited for; matrix products, arithmetic and copies ran while one was open for 0% of the time, Pallas kernels for 32%

profile of v22, /device:TPU:0, one launch (start us, length us, event | category | flops | bytes accessed | tf_op | source)
XLA Modules:
  0.0 56.9 jit_solution(2528666661768879231)
XLA Ops:
  0.6 0.0 copy-start
  0.6 1.1 %copy-done = bf16[16,4,48,128]{3,2,1,0:T(8,128)(2,1)S(1)} copy-done((bf16[16,4,48,128]{3,2,1,0:T(8,128)(2,1)S(1)}, bf16[16,4,48,128]{3,2,1,0:T(8,128)(2,1)}, u32[]{:S(2)}) %copy-start) | copy-done | bytes 786456
  1.8 0.0 copy-start.2
  1.8 0.0 copy-start.3
  1.8 0.0 copy-start.1
  1.8 0.7 %shard_map.67 = (bf16[32,2,16,128]{3,2,1,0:T(8,128)(2,1)S(1)}, bf16[32,2,16,128]{3,2,1,0:T(8,128)(2,1)S(1)}) custom-call(bf16[16,4,48,128]{3,2,1,0:T(8,128)(2,1)S(1)} %copy-done, bf16[16,4,48,128]{3,2,1,0:T(8,128)(2,1)S(1)} %copy-done), custom_call_target="tpu_custom_call" | custom-call | bytes 1179648 | tf_op jit(solution)/shard_map/pallas_call | solution.py:19
  2.5 3.0 %collective-permute-start.1 = (bf16[32,2,16,128]{3,2,1,0:T(8,128)(2,1)S(1)}, bf16[32,2,16,128]{3,2,1,0:T(8,128)(2,1)S(1)}, u32[]{:S(2)}, u32[]{:S(2)}) collective-permute-start(bf16[32,2,16,128]{3,2,1,0:T(8,128)(2,1)S(1)} %get-tuple-element.36), channel_id=1, source_target_pairs={{0,1},{1,0},{2,3},{3,2},{4,5},{5,4},{6,7},{7,6},{8,9},{9,8},{10,11... | collective-permute-start | bytes 786440 | tf_op jit(solution)/shard_map/ppermute | solution.py:484
  5.5 0.7 %shard_map.68 = (bf16[32,2,16,128]{3,2,1,0:T(8,128)(2,1)S(1)}, bf16[32,2,16,128]{3,2,1,0:T(8,128)(2,1)S(1)}) custom-call(bf16[32,2,16,128]{3,2,1,0:T(8,128)(2,1)S(1)} %get-tuple-element.35.after.refs_4_.refs_0_.refs_15_, bf16[16,4,48,128]{3,2,1,0:T(8,128)(2,1)S(1)} %copy-done), custom_call_target="tpu_custom_call" | custom-call | bytes 1179648 | tf_op jit(solution)/shard_map/pallas_call | solution.py:19
  6.2 0.1 collective-permute-start.3
  6.3 4.0 %collective-permute-start.5 = (bf16[32,2,16,128]{3,2,1,0:T(8,128)(2,1)S(1)}, bf16[32,2,16,128]{3,2,1,0:T(8,128)(2,1)S(1)}, u32[]{:S(2)}, u32[]{:S(2)}) collective-permute-start(bf16[32,2,16,128]{3,2,1,0:T(8,128)(2,1)S(1)} %get-tuple-element.37.after.refs_2_.refs_13_), channel_id=1, source_target_pairs={{2,0},{4,2},{6,4},{8,6},{10,8},{12,10},{14,12},{16,14},{18,16},{20... | collective-permute-start | bytes 786440 | tf_op jit(solution)/shard_map/ppermute | solution.py:490
  10.2 0.0 collective-permute-start
  10.2 0.0 copy-done.2
  10.2 0.0 copy-done.3
  10.2 0.1 shard_map.69.refs_1_.after.refs_0_
  10.4 2.3 %collective-permute-done.1.refs_0_ = bf16[32,2,16,128]{3,2,1,0:T(8,128)(2,1)S(1)} collective-permute-done((bf16[32,2,16,128]{3,2,1,0:T(8,128)(2,1)S(1)}, bf16[32,2,16,128]{3,2,1,0:T(8,128)(2,1)S(1)}, u32[]{:S(2)}, u32[]{:S(2)}) %collective-permute-start.1) | collective-permute-done | bytes 262176 | tf_op jit(solution)/shard_map/ppermute | solution.py:484
  12.6 0.0 collective-permute-start.2
  12.6 2.1 %collective-permute-start.4 = (bf16[14,16,128]{2,1,0:T(8,128)(2,1)S(1)}, bf16[14,16,128]{2,1,0:T(8,128)(2,1)S(1)}, u32[]{:S(2)}, u32[]{:S(2)}) collective-permute-start(bf16[14,16,128]{2,1,0:T(8,128)(2,1)S(1)} %shard_map.69.refs_1_.after.refs_0_), channel_id=1, source_target_pairs={{0,1},{1,0},{2,3},{3,2},{4,5},{5,4},{6,7},{7,6},{8,9},{9,8},{10,11... | collective-permute-start | bytes 172040 | tf_op jit(solution)/shard_map/ppermute | solution.py:484
  14.7 0.0 copy-done.1
  14.7 1.2 %shard_map.71 = (bf16[28,2,32,128]{3,2,1,0:T(8,128)(2,1)S(1)}, bf16[28,2,32,128]{3,2,1,0:T(8,128)(2,1)S(1)}) custom-call(bf16[14,16,128]{2,1,0:T(8,128)(2,1)S(1)} %shard_map.69.refs_1_.after.refs_0_, bf16[32,4,48,128]{3,2,1,0:T(8,128)(2,1)S(1)} %copy-done.1), custom_call_target="tpu_custom_call" | custom-call | bytes 3145728 | tf_op jit(solution)/shard_map/pallas_call | solution.py:19
  15.9 2.6 %collective-permute-done.4.refs_2_.refs_1_ = bf16[14,16,128]{2,1,0:T(8,128)(2,1)S(1)} collective-permute-done((bf16[14,16,128]{2,1,0:T(8,128)(2,1)S(1)}, bf16[14,16,128]{2,1,0:T(8,128)(2,1)S(1)}, u32[]{:S(2)}, u32[]{:S(2)}) %collective-permute-start.4) | collective-permute-done | bytes 57376 | tf_op jit(solution)/shard_map/ppermute | solution.py:484
  18.6 0.0 collective-permute-done.3.refs_0_
  18.6 0.0 collective-permute-done.5.refs_1_.refs_2_.refs_17_
  18.6 3.5 %collective-permute-start.6 = (bf16[32,2,16,128]{3,2,1,0:T(8,128)(2,1)S(1)}, bf16[32,2,16,128]{3,2,1,0:T(8,128)(2,1)S(1)}, u32[]{:S(2)}, u32[]{:S(2)}) collective-permute-start(bf16[32,2,16,128]{3,2,1,0:T(8,128)(2,1)S(1)} %shard_map.73.refs_3_.refs_14_), channel_id=1, source_target_pairs={{2,0},{4,2},{6,4},{8,6},{10,8},{12,10},{14,12},{16,14},{18,16},{20... | collective-permute-start | bytes 786440 | tf_op jit(solution)/shard_map/ppermute | solution.py:490
  22.1 0.6 %shard_map.74 = (bf16[192,384]{1,0:T(8,128)(2,1)S(1)}, bf16[192,384]{1,0:T(8,128)(2,1)S(1)}, bf16[192,384]{1,0:T(8,128)(2,1)S(1)}, bf16[192,384]{1,0:T(8,128)(2,...) custom-call(bf16[14,16,128]{2,1,0:T(8,128)(2,1)S(1)} %shard_map.69.refs_1_.after.refs_0_, ...), custom_call_target="tpu_custom_call" | custom-call | bytes 589824 | tf_op jit(solution)/shard_map/pallas_call | solution.py:19
  22.7 0.0 collective-permute-done.refs_0_.refs_11_
  22.7 0.0 collective-permute-done.2.refs_1_.refs_12_
  22.7 2.6 %shard_map.75 = (bf16[30,2,32,128]{3,2,1,0:T(8,128)(2,1)S(1)}, bf16[30,2,32,128]{3,2,1,0:T(8,128)(2,1)S(1)}, bf16[30,2,32,128]{3,2,1,0:T(8,128)(2,1)S(1)}, bf16[...) custom-call(bf16[32,2,16,128]{3,2,1,0:T(8,128)(2,1)S(1)} %collective-permute-done.refs_0_.refs_11_, ...), custom_call_target="tpu_custom_call" | custom-call | flops 1019215872 | bytes 3145728 | tf_op jit(solution)/shard_map/pallas_call | solution.py:19
  25.3 1.6 %collective-permute-start.7 = (bf16[28,2,32,128]{3,2,1,0:T(8,128)(2,1)S(1)}, bf16[28,2,32,128]{3,2,1,0:T(8,128)(2,1)S(1)}, u32[]{:S(2)}, u32[]{:S(2)}) collective-permute-start(bf16[28,2,32,128]{3,2,1,0:T(8,128)(2,1)S(1)} %get-tuple-element.46.refs_3_), channel_id=1, source_target_pairs={{2,0},{4,2},{6,4},{8,6},{10,8},{12,10},{14,12},{16,14},{18,16},{20... | collective-permute-start | bytes 1376264 | tf_op jit(solution)/shard_map/ppermute | solution.py:490
  26.9 0.0 collective-permute-done.6.refs_3_.refs_18_
  26.9 1.8 %shard_map.76 = (bf16[30,2,32,128]{3,2,1,0:T(8,128)(2,1)S(1)}, bf16[30,2,32,128]{3,2,1,0:T(8,128)(2,1)S(1)}, bf16[28,2,32,128]{3,2,1,0:T(8,128)(2,1)S(1)}) custom-call(bf16[32,2,16,128]{3,2,1,0:T(8,128)(2,1)S(1)} %get-tuple-element.35.after.refs_4_.refs_0_.refs_15_, bf16[32,2,16,128]{3,2,1,0:T(8,128)(2,1)S(1)} %shard_map.70.refs_5_.refs_1_.refs_16_, ...), custom_call_target="tpu_custom_call" | custom-call | flops 679477248 | bytes 2359296 | tf_op jit(solution)/shard_map/pallas_call | solution.py:19
  28.7 0.2 collective-permute-start.9
  28.9 6.1 %shard_map.77 = (f32[2,7,16,128]{3,2,1,0:T(8,128)S(1)}, f32[2,7,16,128]{3,2,1,0:T(8,128)S(1)}, bf16[26,2,32,128]{3,2,1,0:T(8,128)(2,1)S(1)}) custom-call(bf16[30,2,32,128]{3,2,1,0:T(8,128)(2,1)S(1)} %get-tuple-element.42.refs_0_, bf16[30,2,32,128]{3,2,1,0:T(8,128)(2,1)S(1)} %get-tuple-element.43.refs_4_.refs_1_, ...), custom_call_target="tpu_custom_call" | custom-call | tf_op jit(solution)/shard_map/pallas_call | solution.py:19
  35.0 0.1 collective-permute-start.8
  35.1 0.0 collective-permute-done.7.below
  35.1 0.9 %shard_map.78.after.refs_6_ = bf16[26,2,32,128]{3,2,1,0:T(8,128)(2,1)S(1)} custom-call(f32[2,7,16,128]{3,2,1,0:T(8,128)S(1)} %get-tuple-element.54.after.one, bf16[192,384]{1,0:T(8,128)(2,1)S(1)} %get-tuple-element.48.refs_5_.weight.refs_0_, bf16[28,2,32,128]{3,2,1,0:T(8,128)(2,1)S(1)} %get-tuple-element.47.refs_4_.above, ...), custom_call_target="tpu_custom_call" | custom-call | flops 339738624 | bytes 786432 | tf_op jit(solution)/shard_map/pallas_call | solution.py:19
  36.0 0.4 collective-permute-done.8.two
  36.5 1.6 %collective-permute-start.10 = (f32[7,16,128]{2,1,0:T(8,128)S(1)}, f32[7,16,128]{2,1,0:T(8,128)S(1)}, u32[]{:S(2)}, u32[]{:S(2)}) collective-permute-start(f32[7,16,128]{2,1,0:T(8,128)S(1)} %get-tuple-element.60), channel_id=1, source_target_pairs={{0,1},{1,0},{2,3},{3,2},{4,5},{5,4},{6,7},{7,6},{8,9},{9,8},{10,11... | collective-permute-start | bytes 172040 | tf_op jit(solution)/shard_map/ppermute | solution.py:484
  38.0 0.2 collective-permute-start.12
  38.2 1.8 %collective-permute-start.11 = (f32[7,16,128]{2,1,0:T(8,128)S(1)}, f32[7,16,128]{2,1,0:T(8,128)S(1)}, u32[]{:S(2)}, u32[]{:S(2)}) collective-permute-start(f32[7,16,128]{2,1,0:T(8,128)S(1)} %get-tuple-element.56.after.refs_1_), channel_id=1, source_target_pairs={{0,4},{2,6},{4,0},{6,2},{8,12},{10,14},{12,8},{14,10},{16,20},{18,... | collective-permute-start | bytes 172040 | tf_op jit(solution)/shard_map/ppermute | solution.py:610
  40.0 0.0 collective-permute-done.9.refs_2_
  40.0 2.1 %shard_map.80 = (bf16[24,4,16,128]{3,2,1,0:T(8,128)(2,1)S(1)}, bf16[24,4,16,128]{3,2,1,0:T(8,128)(2,1)S(1)}) custom-call(f32[7,16,128]{2,1,0:T(8,128)S(1)} %get-tuple-element.56.after.refs_1_, bf16[192,384]{1,0:T(8,128)(2,1)S(1)} %get-tuple-element.48.refs_5_.weight.refs_0_, bf16[192,384]{1,0:T(8,128)(2,1)S(1)} %get-tuple-element.57.refs_1_, ...), custom_call_target="tpu_custom_call" | custom-call | flops 1358954496 | bytes 2359296 | tf_op jit(solution)/shard_map/pallas_call | solution.py:19
  42.2 0.0 collective-permute-done.10.refs_2_
  42.2 1.0 %collective-permute-done.11.refs_3_ = f32[7,16,128]{2,1,0:T(8,128)S(1)} collective-permute-done((f32[7,16,128]{2,1,0:T(8,128)S(1)}, f32[7,16,128]{2,1,0:T(8,128)S(1)}, u32[]{:S(2)}, u32[]{:S(2)}) %collective-permute-start.11) | collective-permute-done | bytes 57376 | tf_op jit(solution)/shard_map/ppermute | solution.py:610
  43.2 0.0 collective-permute-done.12.refs_4_
  43.2 1.2 %collective-permute-start.15 = (bf16[24,4,16,128]{3,2,1,0:T(8,128)(2,1)S(1)}, bf16[24,4,16,128]{3,2,1,0:T(8,128)(2,1)S(1)}, u32[]{:S(2)}, u32[]{:S(2)}) collective-permute-start(bf16[24,4,16,128]{3,2,1,0:T(8,128)(2,1)S(1)} %shard_map.84), channel_id=1, source_target_pairs={{0,1},{1,0},{2,3},{3,2},{4,5},{5,4},{6,7},{7,6},{8,9},{9,8},{10,11... | collective-permute-start | bytes 1179656 | tf_op jit(solution)/shard_map/ppermute | solution.py:484
  44.5 1.5 %collective-permute-start.13 = (f32[7,16,128]{2,1,0:T(8,128)S(1)}, f32[7,16,128]{2,1,0:T(8,128)S(1)}, u32[]{:S(2)}, u32[]{:S(2)}) collective-permute-start(f32[7,16,128]{2,1,0:T(8,128)S(1)} %shard_map.81.refs_0_.refs_1_), channel_id=1, source_target_pairs={{0,8},{2,10},{4,12},{6,14},{8,0},{10,2},{12,4},{14,6},{16,24},{18,... | collective-permute-start | bytes 172040 | tf_op jit(solution)/shard_map/ppermute | solution.py:610
  45.9 2.7 %collective-permute-done.13.refs_1_ = f32[7,16,128]{2,1,0:T(8,128)S(1)} collective-permute-done((f32[7,16,128]{2,1,0:T(8,128)S(1)}, f32[7,16,128]{2,1,0:T(8,128)S(1)}, u32[]{:S(2)}, u32[]{:S(2)}) %collective-permute-start.13) | collective-permute-done | bytes 57376 | tf_op jit(solution)/shard_map/ppermute | solution.py:610
  48.7 3.2 %collective-permute-start.14 = (f32[7,16,128]{2,1,0:T(8,128)S(1)}, f32[7,16,128]{2,1,0:T(8,128)S(1)}, u32[]{:S(2)}, u32[]{:S(2)}) collective-permute-start(f32[7,16,128]{2,1,0:T(8,128)S(1)} %shard_map.82.refs_0_), channel_id=1, source_target_pairs={{0,16},{2,18},{4,20},{6,22},{8,24},{10,26},{12,28},{14,30},{16,0},... | collective-permute-start | bytes 172040 | tf_op jit(solution)/shard_map/ppermute | solution.py:610
  51.8 2.2 %collective-permute-done.14.refs_1_ = f32[7,16,128]{2,1,0:T(8,128)S(1)} collective-permute-done((f32[7,16,128]{2,1,0:T(8,128)S(1)}, f32[7,16,128]{2,1,0:T(8,128)S(1)}, u32[]{:S(2)}, u32[]{:S(2)}) %collective-permute-start.14) | collective-permute-done | bytes 57376 | tf_op jit(solution)/shard_map/ppermute | solution.py:610
  54.0 0.1 collective-permute-start.16
  54.1 0.0 collective-permute-done.15.refs_1_
  54.1 1.8 %shard_map.85 = (bf16[16,4,48,128]{3,2,1,0:T(8,128)(2,1)}, f32[27,16,32]{2,1,0:T(8,128)}, f32[27,16,32]{2,1,0:T(8,128)}) custom-call(f32[7,16,128]{2,1,0:T(8,128)S(1)} %shard_map.83.mine, bf16[24,4,16,128]{3,2,1,0:T(8,128)(2,1)S(1)} %get-tuple-element.59.refs_0_, bf16[24,4,16,128]{3,2,1,0:T(8,128)(2,1)S(1)} %collective-permute-done.15.refs_1_), custom_call_target="tpu_custom_call" | custom-call | bytes 1572864 | tf_op jit(solution)/shard_map/pallas_call | solution.py:19
  55.9 0.0 collective-permute-done.16.other
  55.9 0.8 %shard_map.86 = (f32[27,16,32]{2,1,0:T(8,128)}, f32[27,16,32]{2,1,0:T(8,128)}) custom-call(f32[27,16,32]{2,1,0:T(8,128)} %get-tuple-element.63.first_in, f32[27,16,32]{2,1,0:T(8,128)} %get-tuple-element.64.second_in, f32[7,16,128]{2,1,0:T(8,128)S(1)} %collective-permute-done.16.other), custom_call_target="tpu_custom_call", output_to_operand_aliasing={{0}: (0, {}), {1}: (1, {})} | custom-call | tf_op jit(solution)/shard_map/pallas_call | solution.py:19
  (8 shorter events, 0.0 us)
Async XLA Ops:
  0.6 1.1 %copy-start = (bf16[16,4,48,128]{3,2,1,0:T(8,128)(2,1)S(1)}, bf16[16,4,48,128]{3,2,1,0:T(8,128)(2,1)}, u32[]{:S(2)}) copy-start(bf16[16,4,48,128]{3,2,1,0:T(8,128)(2,1)} %x_ref.4) | copy-start | bytes 2359300
  1.8 8.5 %copy-start.2 = (bf16[16,27,32]{2,0,1:T(8,128)(2,1)S(1)}, bf16[16,27,32]{2,0,1:T(8,128)(2,1)}, u32[]{:S(2)}) copy-start(bf16[16,27,32]{2,0,1:T(8,128)(2,1)} %param.6) | copy-start | bytes 82948
  1.8 8.5 %copy-start.3 = (bf16[16,27,32]{2,0,1:T(8,128)(2,1)S(1)}, bf16[16,27,32]{2,0,1:T(8,128)(2,1)}, u32[]{:S(2)}) copy-start(bf16[16,27,32]{2,0,1:T(8,128)(2,1)} %param.7) | copy-start | bytes 82948
  1.8 12.9 %copy-start.1 = (bf16[32,4,48,128]{3,2,1,0:T(8,128)(2,1)S(1)}, bf16[32,4,48,128]{3,2,1,0:T(8,128)(2,1)}, u32[]{:S(2)}) copy-start(bf16[32,4,48,128]{3,2,1,0:T(8,128)(2,1)} %x_ref.5) | copy-start | bytes 4718596
  2.5 10.1 %collective-permute-start.1 = (bf16[32,2,16,128]{3,2,1,0:T(8,128)(2,1)S(1)}, bf16[32,2,16,128]{3,2,1,0:T(8,128)(2,1)S(1)}, u32[]{:S(2)}, u32[]{:S(2)}) collective-permute-start(bf16[32,2,16,128]{3,2,1,0:T(8,128)(2,1)S(1)} %get-tuple-element.36), channel_id=1, source_target_pairs={{0,1},{1,0},{2,3},{3,2},{4,5},{5,4},{6,7},{7,6},{8,9},{9,8},{10,11... | collective-permute-start | bytes 786440 | tf_op jit(solution)/shard_map/ppermute | solution.py:484
  6.2 12.4 %collective-permute-start.3 = (bf16[32,2,16,128]{3,2,1,0:T(8,128)(2,1)S(1)}, bf16[32,2,16,128]{3,2,1,0:T(8,128)(2,1)S(1)}, u32[]{:S(2)}, u32[]{:S(2)}) collective-permute-start(bf16[32,2,16,128]{3,2,1,0:T(8,128)(2,1)S(1)} %get-tuple-element.38), channel_id=1, source_target_pairs={{0,1},{1,0},{2,3},{3,2},{4,5},{5,4},{6,7},{7,6},{8,9},{9,8},{10,11... | collective-permute-start | bytes 786440 | tf_op jit(solution)/shard_map/ppermute | solution.py:484
  6.3 12.3 %collective-permute-start.5 = (bf16[32,2,16,128]{3,2,1,0:T(8,128)(2,1)S(1)}, bf16[32,2,16,128]{3,2,1,0:T(8,128)(2,1)S(1)}, u32[]{:S(2)}, u32[]{:S(2)}) collective-permute-start(bf16[32,2,16,128]{3,2,1,0:T(8,128)(2,1)S(1)} %get-tuple-element.37.after.refs_2_.refs_13_), channel_id=1, source_target_pairs={{2,0},{4,2},{6,4},{8,6},{10,8},{12,10},{14,12},{16,14},{18,16},{20... | collective-permute-start | bytes 786440 | tf_op jit(solution)/shard_map/ppermute | solution.py:490
  10.2 12.5 %collective-permute-start = (bf16[32,2,16,128]{3,2,1,0:T(8,128)(2,1)S(1)}, bf16[32,2,16,128]{3,2,1,0:T(8,128)(2,1)S(1)}, u32[]{:S(2)}, u32[]{:S(2)}) collective-permute-start(bf16[32,2,16,128]{3,2,1,0:T(8,128)(2,1)S(1)} %get-tuple-element.35.after.refs_4_.refs_0_.refs_15_), channel_id=1, source_target_pairs={{0,2},{2,4},{4,6},{6,8},{8,10},{10,12},{12,14},{14,16},{16,18},{18... | collective-permute-start | bytes 786440 | tf_op jit(solution)/shard_map/ppermute | solution.py:487
  12.6 10.1 %collective-permute-start.2 = (bf16[32,2,16,128]{3,2,1,0:T(8,128)(2,1)S(1)}, bf16[32,2,16,128]{3,2,1,0:T(8,128)(2,1)S(1)}, u32[]{:S(2)}, u32[]{:S(2)}) collective-permute-start(bf16[32,2,16,128]{3,2,1,0:T(8,128)(2,1)S(1)} %shard_map.70.refs_5_.refs_1_.refs_16_), channel_id=1, source_target_pairs={{0,2},{2,4},{4,6},{6,8},{8,10},{10,12},{12,14},{14,16},{16,18},{18... | collective-permute-start | bytes 786440 | tf_op jit(solution)/shard_map/ppermute | solution.py:487
  12.6 5.9 %collective-permute-start.4 = (bf16[14,16,128]{2,1,0:T(8,128)(2,1)S(1)}, bf16[14,16,128]{2,1,0:T(8,128)(2,1)S(1)}, u32[]{:S(2)}, u32[]{:S(2)}) collective-permute-start(bf16[14,16,128]{2,1,0:T(8,128)(2,1)S(1)} %shard_map.69.refs_1_.after.refs_0_), channel_id=1, source_target_pairs={{0,1},{1,0},{2,3},{3,2},{4,5},{5,4},{6,7},{7,6},{8,9},{9,8},{10,11... | collective-permute-start | bytes 172040 | tf_op jit(solution)/shard_map/ppermute | solution.py:484
  18.6 8.3 %collective-permute-start.6 = (bf16[32,2,16,128]{3,2,1,0:T(8,128)(2,1)S(1)}, bf16[32,2,16,128]{3,2,1,0:T(8,128)(2,1)S(1)}, u32[]{:S(2)}, u32[]{:S(2)}) collective-permute-start(bf16[32,2,16,128]{3,2,1,0:T(8,128)(2,1)S(1)} %shard_map.73.refs_3_.refs_14_), channel_id=1, source_target_pairs={{2,0},{4,2},{6,4},{8,6},{10,8},{12,10},{14,12},{16,14},{18,16},{20... | collective-permute-start | bytes 786440 | tf_op jit(solution)/shard_map/ppermute | solution.py:490
  25.3 9.8 %collective-permute-start.7 = (bf16[28,2,32,128]{3,2,1,0:T(8,128)(2,1)S(1)}, bf16[28,2,32,128]{3,2,1,0:T(8,128)(2,1)S(1)}, u32[]{:S(2)}, u32[]{:S(2)}) collective-permute-start(bf16[28,2,32,128]{3,2,1,0:T(8,128)(2,1)S(1)} %get-tuple-element.46.refs_3_), channel_id=1, source_target_pairs={{2,0},{4,2},{6,4},{8,6},{10,8},{12,10},{14,12},{16,14},{18,16},{20... | collective-permute-start | bytes 1376264 | tf_op jit(solution)/shard_map/ppermute | solution.py:490
  28.7 11.3 %collective-permute-start.9 = (bf16[28,2,32,128]{3,2,1,0:T(8,128)(2,1)S(1)}, bf16[28,2,32,128]{3,2,1,0:T(8,128)(2,1)S(1)}, u32[]{:S(2)}, u32[]{:S(2)}) collective-permute-start(bf16[28,2,32,128]{3,2,1,0:T(8,128)(2,1)S(1)} %get-tuple-element.47.refs_4_.above), channel_id=1, source_target_pairs={{0,2},{2,4},{4,6},{6,8},{8,10},{10,12},{12,14},{14,16},{16,18},{18... | collective-permute-start | bytes 1376264 | tf_op jit(solution)/shard_map/ppermute | solution.py:487
  35.0 1.4 %collective-permute-start.8 = (f32[2,7,16,128]{3,2,1,0:T(8,128)S(1)}, f32[2,7,16,128]{3,2,1,0:T(8,128)S(1)}, u32[]{:S(2)}, u32[]{:S(2)}) collective-permute-start(f32[2,7,16,128]{3,2,1,0:T(8,128)S(1)} %get-tuple-element.55), channel_id=1, source_target_pairs={{0,2},{2,0},{4,6},{6,4},{8,10},{10,8},{12,14},{14,12},{16,18},{18,... | collective-permute-start | bytes 344072 | tf_op jit(solution)/shard_map/ppermute | solution.py:610
  36.5 5.7 %collective-permute-start.10 = (f32[7,16,128]{2,1,0:T(8,128)S(1)}, f32[7,16,128]{2,1,0:T(8,128)S(1)}, u32[]{:S(2)}, u32[]{:S(2)}) collective-permute-start(f32[7,16,128]{2,1,0:T(8,128)S(1)} %get-tuple-element.60), channel_id=1, source_target_pairs={{0,1},{1,0},{2,3},{3,2},{4,5},{5,4},{6,7},{7,6},{8,9},{9,8},{10,11... | collective-permute-start | bytes 172040 | tf_op jit(solution)/shard_map/ppermute | solution.py:484
  38.0 5.2 %collective-permute-start.12 = (f32[7,16,128]{2,1,0:T(8,128)S(1)}, f32[7,16,128]{2,1,0:T(8,128)S(1)}, u32[]{:S(2)}, u32[]{:S(2)}) collective-permute-start(f32[7,16,128]{2,1,0:T(8,128)S(1)} %get-tuple-element.60), channel_id=1, source_target_pairs={{0,5},{1,4},{2,7},{3,6},{4,1},{5,0},{6,3},{7,2},{8,13},{9,12},{10,... | collective-permute-start | bytes 172040 | tf_op jit(solution)/shard_map/ppermute | solution.py:616
  38.2 5.0 %collective-permute-start.11 = (f32[7,16,128]{2,1,0:T(8,128)S(1)}, f32[7,16,128]{2,1,0:T(8,128)S(1)}, u32[]{:S(2)}, u32[]{:S(2)}) collective-permute-start(f32[7,16,128]{2,1,0:T(8,128)S(1)} %get-tuple-element.56.after.refs_1_), channel_id=1, source_target_pairs={{0,4},{2,6},{4,0},{6,2},{8,12},{10,14},{12,8},{14,10},{16,20},{18,... | collective-permute-start | bytes 172040 | tf_op jit(solution)/shard_map/ppermute | solution.py:610
  43.2 10.8 %collective-permute-start.15 = (bf16[24,4,16,128]{3,2,1,0:T(8,128)(2,1)S(1)}, bf16[24,4,16,128]{3,2,1,0:T(8,128)(2,1)S(1)}, u32[]{:S(2)}, u32[]{:S(2)}) collective-permute-start(bf16[24,4,16,128]{3,2,1,0:T(8,128)(2,1)S(1)} %shard_map.84), channel_id=1, source_target_pairs={{0,1},{1,0},{2,3},{3,2},{4,5},{5,4},{6,7},{7,6},{8,9},{9,8},{10,11... | collective-permute-start | bytes 1179656 | tf_op jit(solution)/shard_map/ppermute | solution.py:484
  44.5 4.2 %collective-permute-start.13 = (f32[7,16,128]{2,1,0:T(8,128)S(1)}, f32[7,16,128]{2,1,0:T(8,128)S(1)}, u32[]{:S(2)}, u32[]{:S(2)}) collective-permute-start(f32[7,16,128]{2,1,0:T(8,128)S(1)} %shard_map.81.refs_0_.refs_1_), channel_id=1, source_target_pairs={{0,8},{2,10},{4,12},{6,14},{8,0},{10,2},{12,4},{14,6},{16,24},{18,... | collective-permute-start | bytes 172040 | tf_op jit(solution)/shard_map/ppermute | solution.py:610
  48.7 5.3 %collective-permute-start.14 = (f32[7,16,128]{2,1,0:T(8,128)S(1)}, f32[7,16,128]{2,1,0:T(8,128)S(1)}, u32[]{:S(2)}, u32[]{:S(2)}) collective-permute-start(f32[7,16,128]{2,1,0:T(8,128)S(1)} %shard_map.82.refs_0_), channel_id=1, source_target_pairs={{0,16},{2,18},{4,20},{6,22},{8,24},{10,26},{12,28},{14,30},{16,0},... | collective-permute-start | bytes 172040 | tf_op jit(solution)/shard_map/ppermute | solution.py:610
  54.0 1.9 %collective-permute-start.16 = (f32[7,16,128]{2,1,0:T(8,128)S(1)}, f32[7,16,128]{2,1,0:T(8,128)S(1)}, u32[]{:S(2)}, u32[]{:S(2)}) collective-permute-start(f32[7,16,128]{2,1,0:T(8,128)S(1)} %shard_map.83.mine), channel_id=1, source_target_pairs={{0,2},{2,0},{4,6},{6,4},{8,10},{10,8},{12,14},{14,12},{16,18},{18,... | collective-permute-start | bytes 172040 | tf_op jit(solution)/shard_map/ppermute | solution.py:610

commit v23 on v21

--- a/solution.py
+++ b/solution.py
@@ -249,7 +249,6 @@
                     wide = delta[delta_row + row + q, place]
                     depth = wide.shape[1]
                     rows += [pltpu.roll(wide, depth - 1, 1), wide, pltpu.roll(wide, 1, 1)]
-                    rows.append(jnp.zeros_like(wide))
                 right.append(jnp.concatenate(rows, axis=0))
                 rows = []
                 for refs, side in pieces[x : x + 3]:
@@ -565,7 +564,7 @@
 
     raw = jax.ShapeDtypeStruct((extent, 7, size, 4 * channels), F32)
     portion = jax.ShapeDtypeStruct(raw.shape[1:], F32)
-    total = pltpu.VMEM((12 * channels, 8 * channels), F32)
+    total = pltpu.VMEM((12 * channels, 6 * channels), F32)
 
     def room(rows_each):
         return pltpu.VMEM((rows_each, 2, channels, depth), BF16)

time: 56.9 us -> 57.2 us (level)
  no operation moved by 1% of the time
where the time goes in v23:
time: 57.2 us; the launch traced here: 57 us
  starting transfers between devices  23.9 us (42%)
  Pallas kernels  19.8 us (35%)
  waiting for transfers between devices  11.4 us (20%)
  local copies, waits for them, and re-layouts  1.14 us (2%)
  between operations  0.83 us (1%)
    pallas_call x20, Pallas kernels, call(): pl.pallas_call(kernel, out_shape=outs, in_specs=[still] * loose + [whole]...  19.8 us
    ppermute x3, starting transfers between devices, to_prev(): lax.ppermute(value, 'slab', [((i + 1) % slabs, i) for i in range(slabs)])  9.06 us
    ppermute x5, starting transfers between devices, to_chan(): lax.ppermute(value, 'chan', [(i, (i + shift) % extent) for i in range(ext...  7.92 us
    ppermute x5, starting transfers between devices, stepped(): return lax.ppermute(value, 'slab', [(i, i ^ stride) for i in range(slabs)])  6.49 us
    ppermute x5, waiting for transfers between devices, stepped(): return lax.ppermute(value, 'slab', [(i, i ^ stride) for i in range(slabs)])  6.45 us
    ppermute x5, waiting for transfers between devices, to_chan(): lax.ppermute(value, 'chan', [(i, (i + shift) % extent) for i in range(ext...  4.89 us
  transfers between devices with their start and end apart: 17, of which 6 were waited for; matrix products, arithmetic and copies ran while one was open for 0% of the time, Pallas kernels for 32%

profile of v23, /device:TPU:0, one launch (start us, length us, event | category | flops | bytes accessed | tf_op | source)
XLA Modules:
  0.0 57.0 jit_solution(13311582602091831339)
XLA Ops:
  0.6 0.0 copy-start
  0.6 1.1 %copy-done = bf16[16,4,48,128]{3,2,1,0:T(8,128)(2,1)S(1)} copy-done((bf16[16,4,48,128]{3,2,1,0:T(8,128)(2,1)S(1)}, bf16[16,4,48,128]{3,2,1,0:T(8,128)(2,1)}, u32[]{:S(2)}) %copy-start) | copy-done | bytes 786456
  1.8 0.0 copy-start.2
  1.8 0.0 copy-start.3
  1.8 0.0 copy-start.1
  1.8 0.7 %shard_map.67 = (bf16[32,2,16,128]{3,2,1,0:T(8,128)(2,1)S(1)}, bf16[32,2,16,128]{3,2,1,0:T(8,128)(2,1)S(1)}) custom-call(bf16[16,4,48,128]{3,2,1,0:T(8,128)(2,1)S(1)} %copy-done, bf16[16,4,48,128]{3,2,1,0:T(8,128)(2,1)S(1)} %copy-done), custom_call_target="tpu_custom_call" | custom-call | bytes 1179648 | tf_op jit(solution)/shard_map/pallas_call | solution.py:19
  2.5 3.0 %collective-permute-start.1 = (bf16[32,2,16,128]{3,2,1,0:T(8,128)(2,1)S(1)}, bf16[32,2,16,128]{3,2,1,0:T(8,128)(2,1)S(1)}, u32[]{:S(2)}, u32[]{:S(2)}) collective-permute-start(bf16[32,2,16,128]{3,2,1,0:T(8,128)(2,1)S(1)} %get-tuple-element.35), channel_id=1, source_target_pairs={{0,1},{1,0},{2,3},{3,2},{4,5},{5,4},{6,7},{7,6},{8,9},{9,8},{10,11... | collective-permute-start | bytes 786440 | tf_op jit(solution)/shard_map/ppermute | solution.py:461
  5.5 0.7 %shard_map.68 = (bf16[32,2,16,128]{3,2,1,0:T(8,128)(2,1)S(1)}, bf16[32,2,16,128]{3,2,1,0:T(8,128)(2,1)S(1)}) custom-call(bf16[32,2,16,128]{3,2,1,0:T(8,128)(2,1)S(1)} %get-tuple-element.34.after.refs_4_.refs_0_.refs_15_, bf16[16,4,48,128]{3,2,1,0:T(8,128)(2,1)S(1)} %copy-done), custom_call_target="tpu_custom_call" | custom-call | bytes 1179648 | tf_op jit(solution)/shard_map/pallas_call | solution.py:19
  6.2 0.1 collective-permute-start.3
  6.3 4.0 %collective-permute-start.5 = (bf16[32,2,16,128]{3,2,1,0:T(8,128)(2,1)S(1)}, bf16[32,2,16,128]{3,2,1,0:T(8,128)(2,1)S(1)}, u32[]{:S(2)}, u32[]{:S(2)}) collective-permute-start(bf16[32,2,16,128]{3,2,1,0:T(8,128)(2,1)S(1)} %get-tuple-element.36.after.refs_2_.refs_13_), channel_id=1, source_target_pairs={{2,0},{4,2},{6,4},{8,6},{10,8},{12,10},{14,12},{16,14},{18,16},{20... | collective-permute-start | bytes 786440 | tf_op jit(solution)/shard_map/ppermute | solution.py:467
  10.2 0.0 collective-permute-start
  10.2 0.0 copy-done.2
  10.2 0.0 copy-done.3
  10.2 0.1 shard_map.69.refs_1_.after.refs_0_
  10.4 2.3 %collective-permute-done.1.refs_0_ = bf16[32,2,16,128]{3,2,1,0:T(8,128)(2,1)S(1)} collective-permute-done((bf16[32,2,16,128]{3,2,1,0:T(8,128)(2,1)S(1)}, bf16[32,2,16,128]{3,2,1,0:T(8,128)(2,1)S(1)}, u32[]{:S(2)}, u32[]{:S(2)}) %collective-permute-start.1) | collective-permute-done | bytes 262176 | tf_op jit(solution)/shard_map/ppermute | solution.py:461
  12.6 0.0 collective-permute-start.2
  12.6 2.1 %collective-permute-start.4 = (bf16[14,16,128]{2,1,0:T(8,128)(2,1)S(1)}, bf16[14,16,128]{2,1,0:T(8,128)(2,1)S(1)}, u32[]{:S(2)}, u32[]{:S(2)}) collective-permute-start(bf16[14,16,128]{2,1,0:T(8,128)(2,1)S(1)} %shard_map.69.refs_1_.after.refs_0_), channel_id=1, source_target_pairs={{0,1},{1,0},{2,3},{3,2},{4,5},{5,4},{6,7},{7,6},{8,9},{9,8},{10,11... | collective-permute-start | bytes 172040 | tf_op jit(solution)/shard_map/ppermute | solution.py:461
  14.7 0.0 copy-done.1
  14.7 1.2 %shard_map.71 = (bf16[28,2,32,128]{3,2,1,0:T(8,128)(2,1)S(1)}, bf16[28,2,32,128]{3,2,1,0:T(8,128)(2,1)S(1)}) custom-call(bf16[14,16,128]{2,1,0:T(8,128)(2,1)S(1)} %shard_map.69.refs_1_.after.refs_0_, bf16[32,4,48,128]{3,2,1,0:T(8,128)(2,1)S(1)} %copy-done.1), custom_call_target="tpu_custom_call" | custom-call | bytes 3145728 | tf_op jit(solution)/shard_map/pallas_call | solution.py:19
  15.9 2.6 %collective-permute-done.4.refs_2_.refs_1_ = bf16[14,16,128]{2,1,0:T(8,128)(2,1)S(1)} collective-permute-done((bf16[14,16,128]{2,1,0:T(8,128)(2,1)S(1)}, bf16[14,16,128]{2,1,0:T(8,128)(2,1)S(1)}, u32[]{:S(2)}, u32[]{:S(2)}) %collective-permute-start.4) | collective-permute-done | bytes 57376 | tf_op jit(solution)/shard_map/ppermute | solution.py:461
  18.6 0.0 collective-permute-done.3.refs_0_
  18.6 0.0 collective-permute-done.5.refs_1_.refs_2_.refs_17_
  18.6 3.5 %collective-permute-start.6 = (bf16[32,2,16,128]{3,2,1,0:T(8,128)(2,1)S(1)}, bf16[32,2,16,128]{3,2,1,0:T(8,128)(2,1)S(1)}, u32[]{:S(2)}, u32[]{:S(2)}) collective-permute-start(bf16[32,2,16,128]{3,2,1,0:T(8,128)(2,1)S(1)} %shard_map.73.refs_3_.refs_14_), channel_id=1, source_target_pairs={{2,0},{4,2},{6,4},{8,6},{10,8},{12,10},{14,12},{16,14},{18,16},{20... | collective-permute-start | bytes 786440 | tf_op jit(solution)/shard_map/ppermute | solution.py:467
  22.1 0.6 %shard_map.74 = (bf16[192,384]{1,0:T(8,128)(2,1)S(1)}, bf16[192,384]{1,0:T(8,128)(2,1)S(1)}, bf16[192,384]{1,0:T(8,128)(2,1)S(1)}, bf16[192,384]{1,0:T(8,128)(2,...) custom-call(bf16[14,16,128]{2,1,0:T(8,128)(2,1)S(1)} %shard_map.69.refs_1_.after.refs_0_, ...), custom_call_target="tpu_custom_call" | custom-call | bytes 589824 | tf_op jit(solution)/shard_map/pallas_call | solution.py:19
  22.7 0.0 collective-permute-done.refs_0_.refs_11_
  22.7 0.0 collective-permute-done.2.refs_1_.refs_12_
  22.7 2.6 %shard_map.75 = (bf16[30,2,32,128]{3,2,1,0:T(8,128)(2,1)S(1)}, bf16[30,2,32,128]{3,2,1,0:T(8,128)(2,1)S(1)}, bf16[30,2,32,128]{3,2,1,0:T(8,128)(2,1)S(1)}, bf16[...) custom-call(bf16[32,2,16,128]{3,2,1,0:T(8,128)(2,1)S(1)} %collective-permute-done.refs_0_.refs_11_, ...), custom_call_target="tpu_custom_call" | custom-call | flops 1019215872 | bytes 3145728 | tf_op jit(solution)/shard_map/pallas_call | solution.py:19
  25.3 1.6 %collective-permute-start.7 = (bf16[28,2,32,128]{3,2,1,0:T(8,128)(2,1)S(1)}, bf16[28,2,32,128]{3,2,1,0:T(8,128)(2,1)S(1)}, u32[]{:S(2)}, u32[]{:S(2)}) collective-permute-start(bf16[28,2,32,128]{3,2,1,0:T(8,128)(2,1)S(1)} %get-tuple-element.45.refs_3_), channel_id=1, source_target_pairs={{2,0},{4,2},{6,4},{8,6},{10,8},{12,10},{14,12},{16,14},{18,16},{20... | collective-permute-start | bytes 1376264 | tf_op jit(solution)/shard_map/ppermute | solution.py:467
  26.9 0.0 collective-permute-done.6.refs_3_.refs_18_
  26.9 1.8 %shard_map.76 = (bf16[30,2,32,128]{3,2,1,0:T(8,128)(2,1)S(1)}, bf16[30,2,32,128]{3,2,1,0:T(8,128)(2,1)S(1)}, bf16[28,2,32,128]{3,2,1,0:T(8,128)(2,1)S(1)}) custom-call(bf16[32,2,16,128]{3,2,1,0:T(8,128)(2,1)S(1)} %get-tuple-element.34.after.refs_4_.refs_0_.refs_15_, bf16[32,2,16,128]{3,2,1,0:T(8,128)(2,1)S(1)} %shard_map.70.refs_5_.refs_1_.refs_16_, ...), custom_call_target="tpu_custom_call" | custom-call | flops 679477248 | bytes 2359296 | tf_op jit(solution)/shard_map/pallas_call | solution.py:19
  28.7 0.2 collective-permute-start.9
  28.9 6.4 %shard_map.77 = (f32[2,7,16,128]{3,2,1,0:T(8,128)S(1)}, f32[2,7,16,128]{3,2,1,0:T(8,128)S(1)}, bf16[26,2,32,128]{3,2,1,0:T(8,128)(2,1)S(1)}) custom-call(bf16[30,2,32,128]{3,2,1,0:T(8,128)(2,1)S(1)} %get-tuple-element.41.refs_0_, bf16[30,2,32,128]{3,2,1,0:T(8,128)(2,1)S(1)} %get-tuple-element.42.refs_4_.refs_1_, ...), custom_call_target="tpu_custom_call" | custom-call | tf_op jit(solution)/shard_map/pallas_call | solution.py:19
  35.3 0.1 collective-permute-start.8
  35.3 0.0 collective-permute-done.7.below
  35.4 0.9 %shard_map.78.after.refs_6_ = bf16[26,2,32,128]{3,2,1,0:T(8,128)(2,1)S(1)} custom-call(f32[2,7,16,128]{3,2,1,0:T(8,128)S(1)} %get-tuple-element.53.after.one, bf16[192,384]{1,0:T(8,128)(2,1)S(1)} %get-tuple-element.47.refs_5_.weight.refs_0_, bf16[28,2,32,128]{3,2,1,0:T(8,128)(2,1)S(1)} %get-tuple-element.46.refs_4_.above, ...), custom_call_target="tpu_custom_call" | custom-call | flops 339738624 | bytes 786432 | tf_op jit(solution)/shard_map/pallas_call | solution.py:19
  36.3 0.4 collective-permute-done.8.two
  36.7 1.6 %collective-permute-start.10 = (f32[7,16,128]{2,1,0:T(8,128)S(1)}, f32[7,16,128]{2,1,0:T(8,128)S(1)}, u32[]{:S(2)}, u32[]{:S(2)}) collective-permute-start(f32[7,16,128]{2,1,0:T(8,128)S(1)} %get-tuple-element.60), channel_id=1, source_target_pairs={{0,1},{1,0},{2,3},{3,2},{4,5},{5,4},{6,7},{7,6},{8,9},{9,8},{10,11... | collective-permute-start | bytes 172040 | tf_op jit(solution)/shard_map/ppermute | solution.py:461
  38.2 0.2 collective-permute-start.12
  38.4 1.8 %collective-permute-start.11 = (f32[7,16,128]{2,1,0:T(8,128)S(1)}, f32[7,16,128]{2,1,0:T(8,128)S(1)}, u32[]{:S(2)}, u32[]{:S(2)}) collective-permute-start(f32[7,16,128]{2,1,0:T(8,128)S(1)} %get-tuple-element.55.after.refs_1_), channel_id=1, source_target_pairs={{0,4},{2,6},{4,0},{6,2},{8,12},{10,14},{12,8},{14,10},{16,20},{18,... | collective-permute-start | bytes 172040 | tf_op jit(solution)/shard_map/ppermute | solution.py:587
  40.2 0.0 collective-permute-done.9.refs_2_
  40.2 2.1 %shard_map.80 = (bf16[24,4,16,128]{3,2,1,0:T(8,128)(2,1)S(1)}, bf16[24,4,16,128]{3,2,1,0:T(8,128)(2,1)S(1)}) custom-call(f32[7,16,128]{2,1,0:T(8,128)S(1)} %get-tuple-element.55.after.refs_1_, bf16[192,384]{1,0:T(8,128)(2,1)S(1)} %get-tuple-element.47.refs_5_.weight.refs_0_, bf16[192,384]{1,0:T(8,128)(2,1)S(1)} %get-tuple-element.56.refs_1_, ...), custom_call_target="tpu_custom_call" | custom-call | flops 1358954496 | bytes 2359296 | tf_op jit(solution)/shard_map/pallas_call | solution.py:19
  42.4 0.0 collective-permute-done.10.refs_2_
  42.4 1.1 %collective-permute-done.11.refs_3_ = f32[7,16,128]{2,1,0:T(8,128)S(1)} collective-permute-done((f32[7,16,128]{2,1,0:T(8,128)S(1)}, f32[7,16,128]{2,1,0:T(8,128)S(1)}, u32[]{:S(2)}, u32[]{:S(2)}) %collective-permute-start.11) | collective-permute-done | bytes 57376 | tf_op jit(solution)/shard_map/ppermute | solution.py:587
  43.5 0.0 collective-permute-done.12.refs_4_
  43.5 1.2 %collective-permute-start.13 = (bf16[24,4,16,128]{3,2,1,0:T(8,128)(2,1)S(1)}, bf16[24,4,16,128]{3,2,1,0:T(8,128)(2,1)S(1)}, u32[]{:S(2)}, u32[]{:S(2)}) collective-permute-start(bf16[24,4,16,128]{3,2,1,0:T(8,128)(2,1)S(1)} %shard_map.82), channel_id=1, source_target_pairs={{0,1},{1,0},{2,3},{3,2},{4,5},{5,4},{6,7},{7,6},{8,9},{9,8},{10,11... | collective-permute-start | bytes 1179656 | tf_op jit(solution)/shard_map/ppermute | solution.py:461
  44.7 1.3 %collective-permute-start.14 = (f32[7,16,128]{2,1,0:T(8,128)S(1)}, f32[7,16,128]{2,1,0:T(8,128)S(1)}, u32[]{:S(2)}, u32[]{:S(2)}) collective-permute-start(f32[7,16,128]{2,1,0:T(8,128)S(1)} %shard_map.81.refs_1_.refs_0_), channel_id=1, source_target_pairs={{0,8},{2,10},{4,12},{6,14},{8,0},{10,2},{12,4},{14,6},{16,24},{18,... | collective-permute-start | bytes 172040 | tf_op jit(solution)/shard_map/ppermute | solution.py:587
  46.0 2.8 %collective-permute-done.14.refs_1_ = f32[7,16,128]{2,1,0:T(8,128)S(1)} collective-permute-done((f32[7,16,128]{2,1,0:T(8,128)S(1)}, f32[7,16,128]{2,1,0:T(8,128)S(1)}, u32[]{:S(2)}, u32[]{:S(2)}) %collective-permute-start.14) | collective-permute-done | bytes 57376 | tf_op jit(solution)/shard_map/ppermute | solution.py:587
  48.9 3.2 %collective-permute-start.15 = (f32[7,16,128]{2,1,0:T(8,128)S(1)}, f32[7,16,128]{2,1,0:T(8,128)S(1)}, u32[]{:S(2)}, u32[]{:S(2)}) collective-permute-start(f32[7,16,128]{2,1,0:T(8,128)S(1)} %shard_map.84.refs_0_), channel_id=1, source_target_pairs={{0,16},{2,18},{4,20},{6,22},{8,24},{10,26},{12,28},{14,30},{16,0},... | collective-permute-start | bytes 172040 | tf_op jit(solution)/shard_map/ppermute | solution.py:587
  52.1 2.2 %collective-permute-done.15.refs_1_ = f32[7,16,128]{2,1,0:T(8,128)S(1)} collective-permute-done((f32[7,16,128]{2,1,0:T(8,128)S(1)}, f32[7,16,128]{2,1,0:T(8,128)S(1)}, u32[]{:S(2)}, u32[]{:S(2)}) %collective-permute-start.15) | collective-permute-done | bytes 57376 | tf_op jit(solution)/shard_map/ppermute | solution.py:587
  54.2 0.1 collective-permute-start.16
  54.3 0.0 collective-permute-done.13.refs_1_
  54.3 1.7 %shard_map.83 = (f32[8,128]{1,0:T(8,128)S(1)}, bf16[16,4,48,128]{3,2,1,0:T(8,128)(2,1)}) custom-call(bf16[24,4,16,128]{3,2,1,0:T(8,128)(2,1)S(1)} %get-tuple-element.58.refs_0_, bf16[24,4,16,128]{3,2,1,0:T(8,128)(2,1)S(1)} %collective-permute-done.13.refs_1_), custom_call_target="tpu_custom_call" | custom-call | bytes 1572864 | tf_op jit(solution)/shard_map/pallas_call | solution.py:19
  56.0 0.0 collective-permute-done.16.other
  56.1 0.9 %shard_map.86 = (f32[27,16,32]{2,1,0:T(8,128)}, f32[27,16,32]{2,1,0:T(8,128)}) custom-call(f32[8,128]{1,0:T(8,128)S(1)} %get-tuple-element.62.after, f32[7,16,128]{2,1,0:T(8,128)S(1)} %shard_map.85.mine, f32[7,16,128]{2,1,0:T(8,128)S(1)} %collective-permute-done.16.other), custom_call_target="tpu_custom_call" | custom-call | tf_op jit(solution)/shard_map/pallas_call | solution.py:19
  (8 shorter events, 0.0 us)
Async XLA Ops:
  0.6 1.1 %copy-start = (bf16[16,4,48,128]{3,2,1,0:T(8,128)(2,1)S(1)}, bf16[16,4,48,128]{3,2,1,0:T(8,128)(2,1)}, u32[]{:S(2)}) copy-start(bf16[16,4,48,128]{3,2,1,0:T(8,128)(2,1)} %x_ref.4) | copy-start | bytes 2359300
  1.8 8.5 %copy-start.2 = (bf16[16,27,32]{2,0,1:T(8,128)(2,1)S(1)}, bf16[16,27,32]{2,0,1:T(8,128)(2,1)}, u32[]{:S(2)}) copy-start(bf16[16,27,32]{2,0,1:T(8,128)(2,1)} %param.6) | copy-start | bytes 82948
  1.8 8.5 %copy-start.3 = (bf16[16,27,32]{2,0,1:T(8,128)(2,1)S(1)}, bf16[16,27,32]{2,0,1:T(8,128)(2,1)}, u32[]{:S(2)}) copy-start(bf16[16,27,32]{2,0,1:T(8,128)(2,1)} %param.7) | copy-start | bytes 82948
  1.8 12.9 %copy-start.1 = (bf16[32,4,48,128]{3,2,1,0:T(8,128)(2,1)S(1)}, bf16[32,4,48,128]{3,2,1,0:T(8,128)(2,1)}, u32[]{:S(2)}) copy-start(bf16[32,4,48,128]{3,2,1,0:T(8,128)(2,1)} %x_ref.5) | copy-start | bytes 4718596
  2.5 10.1 %collective-permute-start.1 = (bf16[32,2,16,128]{3,2,1,0:T(8,128)(2,1)S(1)}, bf16[32,2,16,128]{3,2,1,0:T(8,128)(2,1)S(1)}, u32[]{:S(2)}, u32[]{:S(2)}) collective-permute-start(bf16[32,2,16,128]{3,2,1,0:T(8,128)(2,1)S(1)} %get-tuple-element.35), channel_id=1, source_target_pairs={{0,1},{1,0},{2,3},{3,2},{4,5},{5,4},{6,7},{7,6},{8,9},{9,8},{10,11... | collective-permute-start | bytes 786440 | tf_op jit(solution)/shard_map/ppermute | solution.py:461
  6.2 12.4 %collective-permute-start.3 = (bf16[32,2,16,128]{3,2,1,0:T(8,128)(2,1)S(1)}, bf16[32,2,16,128]{3,2,1,0:T(8,128)(2,1)S(1)}, u32[]{:S(2)}, u32[]{:S(2)}) collective-permute-start(bf16[32,2,16,128]{3,2,1,0:T(8,128)(2,1)S(1)} %get-tuple-element.37), channel_id=1, source_target_pairs={{0,1},{1,0},{2,3},{3,2},{4,5},{5,4},{6,7},{7,6},{8,9},{9,8},{10,11... | collective-permute-start | bytes 786440 | tf_op jit(solution)/shard_map/ppermute | solution.py:461
  6.3 12.3 %collective-permute-start.5 = (bf16[32,2,16,128]{3,2,1,0:T(8,128)(2,1)S(1)}, bf16[32,2,16,128]{3,2,1,0:T(8,128)(2,1)S(1)}, u32[]{:S(2)}, u32[]{:S(2)}) collective-permute-start(bf16[32,2,16,128]{3,2,1,0:T(8,128)(2,1)S(1)} %get-tuple-element.36.after.refs_2_.refs_13_), channel_id=1, source_target_pairs={{2,0},{4,2},{6,4},{8,6},{10,8},{12,10},{14,12},{16,14},{18,16},{20... | collective-permute-start | bytes 786440 | tf_op jit(solution)/shard_map/ppermute | solution.py:467
  10.2 12.5 %collective-permute-start = (bf16[32,2,16,128]{3,2,1,0:T(8,128)(2,1)S(1)}, bf16[32,2,16,128]{3,2,1,0:T(8,128)(2,1)S(1)}, u32[]{:S(2)}, u32[]{:S(2)}) collective-permute-start(bf16[32,2,16,128]{3,2,1,0:T(8,128)(2,1)S(1)} %get-tuple-element.34.after.refs_4_.refs_0_.refs_15_), channel_id=1, source_target_pairs={{0,2},{2,4},{4,6},{6,8},{8,10},{10,12},{12,14},{14,16},{16,18},{18... | collective-permute-start | bytes 786440 | tf_op jit(solution)/shard_map/ppermute | solution.py:464
  12.6 10.1 %collective-permute-start.2 = (bf16[32,2,16,128]{3,2,1,0:T(8,128)(2,1)S(1)}, bf16[32,2,16,128]{3,2,1,0:T(8,128)(2,1)S(1)}, u32[]{:S(2)}, u32[]{:S(2)}) collective-permute-start(bf16[32,2,16,128]{3,2,1,0:T(8,128)(2,1)S(1)} %shard_map.70.refs_5_.refs_1_.refs_16_), channel_id=1, source_target_pairs={{0,2},{2,4},{4,6},{6,8},{8,10},{10,12},{12,14},{14,16},{16,18},{18... | collective-permute-start | bytes 786440 | tf_op jit(solution)/shard_map/ppermute | solution.py:464
  12.6 5.9 %collective-permute-start.4 = (bf16[14,16,128]{2,1,0:T(8,128)(2,1)S(1)}, bf16[14,16,128]{2,1,0:T(8,128)(2,1)S(1)}, u32[]{:S(2)}, u32[]{:S(2)}) collective-permute-start(bf16[14,16,128]{2,1,0:T(8,128)(2,1)S(1)} %shard_map.69.refs_1_.after.refs_0_), channel_id=1, source_target_pairs={{0,1},{1,0},{2,3},{3,2},{4,5},{5,4},{6,7},{7,6},{8,9},{9,8},{10,11... | collective-permute-start | bytes 172040 | tf_op jit(solution)/shard_map/ppermute | solution.py:461
  18.6 8.3 %collective-permute-start.6 = (bf16[32,2,16,128]{3,2,1,0:T(8,128)(2,1)S(1)}, bf16[32,2,16,128]{3,2,1,0:T(8,128)(2,1)S(1)}, u32[]{:S(2)}, u32[]{:S(2)}) collective-permute-start(bf16[32,2,16,128]{3,2,1,0:T(8,128)(2,1)S(1)} %shard_map.73.refs_3_.refs_14_), channel_id=1, source_target_pairs={{2,0},{4,2},{6,4},{8,6},{10,8},{12,10},{14,12},{16,14},{18,16},{20... | collective-permute-start | bytes 786440 | tf_op jit(solution)/shard_map/ppermute | solution.py:467
  25.3 10.1 %collective-permute-start.7 = (bf16[28,2,32,128]{3,2,1,0:T(8,128)(2,1)S(1)}, bf16[28,2,32,128]{3,2,1,0:T(8,128)(2,1)S(1)}, u32[]{:S(2)}, u32[]{:S(2)}) collective-permute-start(bf16[28,2,32,128]{3,2,1,0:T(8,128)(2,1)S(1)} %get-tuple-element.45.refs_3_), channel_id=1, source_target_pairs={{2,0},{4,2},{6,4},{8,6},{10,8},{12,10},{14,12},{16,14},{18,16},{20... | collective-permute-start | bytes 1376264 | tf_op jit(solution)/shard_map/ppermute | solution.py:467
  28.7 11.6 %collective-permute-start.9 = (bf16[28,2,32,128]{3,2,1,0:T(8,128)(2,1)S(1)}, bf16[28,2,32,128]{3,2,1,0:T(8,128)(2,1)S(1)}, u32[]{:S(2)}, u32[]{:S(2)}) collective-permute-start(bf16[28,2,32,128]{3,2,1,0:T(8,128)(2,1)S(1)} %get-tuple-element.46.refs_4_.above), channel_id=1, source_target_pairs={{0,2},{2,4},{4,6},{6,8},{8,10},{10,12},{12,14},{14,16},{16,18},{18... | collective-permute-start | bytes 1376264 | tf_op jit(solution)/shard_map/ppermute | solution.py:464
  35.3 1.4 %collective-permute-start.8 = (f32[2,7,16,128]{3,2,1,0:T(8,128)S(1)}, f32[2,7,16,128]{3,2,1,0:T(8,128)S(1)}, u32[]{:S(2)}, u32[]{:S(2)}) collective-permute-start(f32[2,7,16,128]{3,2,1,0:T(8,128)S(1)} %get-tuple-element.54), channel_id=1, source_target_pairs={{0,2},{2,0},{4,6},{6,4},{8,10},{10,8},{12,14},{14,12},{16,18},{18,... | collective-permute-start | bytes 344072 | tf_op jit(solution)/shard_map/ppermute | solution.py:587
  36.7 5.7 %collective-permute-start.10 = (f32[7,16,128]{2,1,0:T(8,128)S(1)}, f32[7,16,128]{2,1,0:T(8,128)S(1)}, u32[]{:S(2)}, u32[]{:S(2)}) collective-permute-start(f32[7,16,128]{2,1,0:T(8,128)S(1)} %get-tuple-element.60), channel_id=1, source_target_pairs={{0,1},{1,0},{2,3},{3,2},{4,5},{5,4},{6,7},{7,6},{8,9},{9,8},{10,11... | collective-permute-start | bytes 172040 | tf_op jit(solution)/shard_map/ppermute | solution.py:461
  38.2 5.2 %collective-permute-start.12 = (f32[7,16,128]{2,1,0:T(8,128)S(1)}, f32[7,16,128]{2,1,0:T(8,128)S(1)}, u32[]{:S(2)}, u32[]{:S(2)}) collective-permute-start(f32[7,16,128]{2,1,0:T(8,128)S(1)} %get-tuple-element.60), channel_id=1, source_target_pairs={{0,5},{1,4},{2,7},{3,6},{4,1},{5,0},{6,3},{7,2},{8,13},{9,12},{10,... | collective-permute-start | bytes 172040 | tf_op jit(solution)/shard_map/ppermute | solution.py:593
  38.4 5.0 %collective-permute-start.11 = (f32[7,16,128]{2,1,0:T(8,128)S(1)}, f32[7,16,128]{2,1,0:T(8,128)S(1)}, u32[]{:S(2)}, u32[]{:S(2)}) collective-permute-start(f32[7,16,128]{2,1,0:T(8,128)S(1)} %get-tuple-element.55.after.refs_1_), channel_id=1, source_target_pairs={{0,4},{2,6},{4,0},{6,2},{8,12},{10,14},{12,8},{14,10},{16,20},{18,... | collective-permute-start | bytes 172040 | tf_op jit(solution)/shard_map/ppermute | solution.py:587
  43.5 10.8 %collective-permute-start.13 = (bf16[24,4,16,128]{3,2,1,0:T(8,128)(2,1)S(1)}, bf16[24,4,16,128]{3,2,1,0:T(8,128)(2,1)S(1)}, u32[]{:S(2)}, u32[]{:S(2)}) collective-permute-start(bf16[24,4,16,128]{3,2,1,0:T(8,128)(2,1)S(1)} %shard_map.82), channel_id=1, source_target_pairs={{0,1},{1,0},{2,3},{3,2},{4,5},{5,4},{6,7},{7,6},{8,9},{9,8},{10,11... | collective-permute-start | bytes 1179656 | tf_op jit(solution)/shard_map/ppermute | solution.py:461
  44.7 4.2 %collective-permute-start.14 = (f32[7,16,128]{2,1,0:T(8,128)S(1)}, f32[7,16,128]{2,1,0:T(8,128)S(1)}, u32[]{:S(2)}, u32[]{:S(2)}) collective-permute-start(f32[7,16,128]{2,1,0:T(8,128)S(1)} %shard_map.81.refs_1_.refs_0_), channel_id=1, source_target_pairs={{0,8},{2,10},{4,12},{6,14},{8,0},{10,2},{12,4},{14,6},{16,24},{18,... | collective-permute-start | bytes 172040 | tf_op jit(solution)/shard_map/ppermute | solution.py:587
  48.9 5.3 %collective-permute-start.15 = (f32[7,16,128]{2,1,0:T(8,128)S(1)}, f32[7,16,128]{2,1,0:T(8,128)S(1)}, u32[]{:S(2)}, u32[]{:S(2)}) collective-permute-start(f32[7,16,128]{2,1,0:T(8,128)S(1)} %shard_map.84.refs_0_), channel_id=1, source_target_pairs={{0,16},{2,18},{4,20},{6,22},{8,24},{10,26},{12,28},{14,30},{16,0},... | collective-permute-start | bytes 172040 | tf_op jit(solution)/shard_map/ppermute | solution.py:587
  54.2 1.8 %collective-permute-start.16 = (f32[7,16,128]{2,1,0:T(8,128)S(1)}, f32[7,16,128]{2,1,0:T(8,128)S(1)}, u32[]{:S(2)}, u32[]{:S(2)}) collective-permute-start(f32[7,16,128]{2,1,0:T(8,128)S(1)} %shard_map.85.mine), channel_id=1, source_target_pairs={{0,2},{2,0},{4,6},{6,4},{8,10},{10,8},{12,14},{14,12},{16,18},{18,... | collective-permute-start | bytes 172040 | tf_op jit(solution)/shard_map/ppermute | solution.py:587
